TPU v7x, 32 devices: a whole 2x2x4 slice. The times are simulated.
32 devices in a mesh: grp: 4 (over y, x), rep: 8 (over z, core).
Axes of the slice: x: 2, y: 2, z: 4, core: 2. Of those that a mesh axis runs over, the one named last changes fastest.
Arguments:
- embeddings: bfloat16 [512, 256], P('rep')
- labels: int32 [512], replicated, may hold values from 0 to 262143
- class_weights: bfloat16 [262144, 256], P(('rep', 'grp'))
- centroids: bfloat16 [262144, 256], P(('grp', 'rep')), may hold values from -6 to 6
- centroid_class: int32 [262144], P(('grp', 'rep')), may hold values from 0 to 8191, as said below
Outputs:
- loss: float32 [512], P('rep')
- embedding_gradient: float32 [512, 256], P('rep')
- weight_grad: float32 [262144, 256], P(('rep', 'grp'))
- refreshed: bfloat16 [262144, 256], P(('rep', 'grp'))
Inputs may be any that keep to these rules, and one draw needn't show every extreme that they name: `centroid_class`: cut every block of 8192 consecutive entries into runs of 256 entries; over the k-th runs of all blocks together, each number of 0 to 8191 appears exactly once.
All inputs are finite; a program needn't handle non-finite values.
Results may differ from a plain program's by a relative error of at most 0.0053.
Values may be sent and summed in bfloat16 or wider, within the bound.
No kernel may reach another device: no remote copies, remote signals or barrier semaphores. Data moves between devices by JAX's collectives and lax.ppermute only.
A program may use at most 128 MiB of HBM per device.

v0:
```python
import math

import jax
import jax.numpy as jnp
from jax import lax
from jax.sharding import PartitionSpec as P

SCALE = 32.0
MARGIN = 0.2
SIN_FLOOR = 0.09


def unit_length_rows(values):
    wide = values.astype(jnp.float32)
    inv_norm = lax.rsqrt(jnp.sum(wide * wide, axis=1, keepdims=True) + 1e-06)
    return (wide * inv_norm, inv_norm)


def margin_terms(cosine_matrix, is_label):
    label_cos = jnp.sum(jnp.where(is_label, cosine_matrix, 0.0), axis=1)
    sine_sq = 1.0 - label_cos * label_cos
    sine = jnp.sqrt(jnp.maximum(sine_sq, SIN_FLOOR))
    margined = label_cos * math.cos(MARGIN) - sine * math.sin(MARGIN)
    margin_slope = math.cos(MARGIN) + jnp.where(
        sine_sq > SIN_FLOOR, label_cos * math.sin(MARGIN) / sine, 0.0
    )
    logits = jnp.where(is_label, SCALE * margined[:, None], SCALE * cosine_matrix)
    return (logits, margin_slope)


def shards(embeddings, labels, class_weights, centroids, centroid_class):
    rows_local, feature_width = embeddings.shape
    classes_local = class_weights.shape[0]
    grp_count = lax.axis_size("grp")
    rep_count = lax.axis_size("rep")
    peer_count = grp_count * rep_count
    per_peer = classes_local // peer_count
    rows_block = jnp.transpose(
        centroids.reshape(rep_count, grp_count, per_peer, feature_width), (1, 0, 2, 3)
    )
    slots_block = jnp.transpose(centroid_class.reshape(rep_count, grp_count, per_peer), (1, 0, 2))
    rows_got, slots_got = (
        lax.all_to_all(
            rows_block.reshape(peer_count, per_peer, feature_width),
            ("grp", "rep"),
            split_axis=0,
            concat_axis=0,
            tiled=True,
        ),
        lax.all_to_all(
            slots_block.reshape(peer_count, per_peer),
            ("grp", "rep"),
            split_axis=0,
            concat_axis=0,
            tiled=True,
        ),
    )
    relaid = (
        jnp.zeros((classes_local, feature_width), jnp.bfloat16)
        .at[slots_got.reshape(-1)]
        .set(rows_got.reshape(-1, feature_width))
    )
    normalized_input_wide, input_inverse_norm = unit_length_rows(embeddings)
    normalized_input_full = lax.all_gather(
        normalized_input_wide.astype(jnp.bfloat16), "rep", axis=0, tiled=True
    )
    what_wide, w_inv = unit_length_rows(class_weights)
    what = what_wide.astype(jnp.bfloat16)
    class_shard = lax.axis_index("rep") * grp_count + lax.axis_index("grp")
    column_ids = class_shard * classes_local + jnp.arange(classes_local, dtype=jnp.int32)
    overall_rows = normalized_input_full.shape[0]
    block_rows = math.gcd(overall_rows, 512)
    block_count = overall_rows // block_rows
    tiled_row_blocks = normalized_input_full.reshape(block_count, block_rows, feature_width)
    label_tiles = labels.reshape(block_count, block_rows)

    def tile_logits(row_tile, label_tile):
        cosine_matrix = lax.dot_general(
            row_tile, what, (((1,), (1,)), ((), ())), preferred_element_type=jnp.float32
        )
        is_label = label_tile[:, None] == column_ids[None, :]
        logits, margin_slope = margin_terms(cosine_matrix, is_label)
        return (logits, margin_slope, is_label)

    def first_pass(tile_pair):
        logits, _, is_label = tile_logits(tile_pair[0], tile_pair[1])
        return (
            jnp.sum(jnp.exp(logits - SCALE), axis=1),
            jnp.sum(jnp.where(is_label, logits, 0.0), axis=1),
        )

    exp_parts, target_parts = lax.map(first_pass, (tiled_row_blocks, label_tiles))
    totals, target = lax.psum((exp_parts.reshape(-1), target_parts.reshape(-1)), ("grp", "rep"))
    log_total = SCALE + jnp.log(totals)

    def second_pass(tile_triple):
        row_tile, label_tile, tile_total = tile_triple
        logits, margin_slope, is_label = tile_logits(row_tile, label_tile)
        probs = jnp.exp(logits - tile_total[:, None])
        onehot = is_label.astype(jnp.float32)
        return (SCALE * (probs - onehot) * jnp.where(is_label, margin_slope[:, None], 1.0)).astype(
            jnp.bfloat16
        )

    cosine_gradient = lax.map(
        second_pass, (tiled_row_blocks, label_tiles, log_total.reshape(block_count, block_rows))
    )
    cosine_gradient = cosine_gradient.reshape(overall_rows, classes_local)
    unnormalized_input = lax.dot_general(
        cosine_gradient,
        normalized_input_full,
        (((0,), (0,)), ((), ())),
        preferred_element_type=jnp.float32,
    )
    weight_grad = (
        unnormalized_input
        - what_wide * jnp.sum(what_wide * unnormalized_input, axis=1, keepdims=True)
    ) * w_inv
    row_start = lax.axis_index("rep") * rows_local
    grad_full = lax.psum(
        jnp.dot(cosine_gradient, what, preferred_element_type=jnp.float32), ("grp", "rep")
    )
    normalized_gradient = lax.dynamic_slice_in_dim(grad_full, row_start, rows_local, 0)
    embedding_gradient = (
        normalized_gradient
        - normalized_input_wide
        * jnp.sum(normalized_input_wide * normalized_gradient, axis=1, keepdims=True)
    ) * input_inverse_norm
    loss = lax.dynamic_slice_in_dim(log_total - target, row_start, rows_local, 0)
    chat, _ = unit_length_rows(relaid)
    refreshed, _ = unit_length_rows(what_wide + chat)
    return (loss, embedding_gradient, weight_grad, refreshed.astype(jnp.bfloat16))


def solution(mesh):
    in_specs = (
        P("rep", None),
        P(),
        P(("rep", "grp"), None),
        P(("grp", "rep"), None),
        P(("grp", "rep")),
    )
    out_specs = (P("rep"), P("rep", None), P(("rep", "grp"), None), P(("rep", "grp"), None))
    return jax.shard_map(shards, mesh=mesh, in_specs=in_specs, out_specs=out_specs, check_vma=False)
```

profile of v0, /device:TPU:0, one launch (start us, length us, event | category | flops | bytes accessed | tf_op | source)
XLA Modules:
  0.0 382.3 jit_solution(6757014034751390459)
XLA Ops:
  7.2 0.8 reshape.124
  8.0 0.6 copy.30
  8.6 7.3 %all-to-all-start = ((s32[32,1,256]{2,1,0:T(1,128)}), s32[32,1,256]{2,1,0:T(1,128)S(1)}, u32[]{:S(2)}, u32[]{:S(2)}) async-start(s32[32,1,256]{2,1,0:T(1,128)} %copy.30), calls=%async_computation | async-start | bytes 65536 | tf_op jit(solution)/shard_map/all_to_all | solution.py:50
  15.9 4.6 %copy.31 = bf16[4,8,256,256]{3,2,1,0:T(8,128)(2,1)} copy(bf16[4,8,256,256]{3,2,0,1:T(8,128)(2,1)} %bitcast.16) | data formatting | bytes 8388608 | tf_op jit(solution)/shard_map/transpose | solution.py:38
  20.6 2.6 all-to-all-done
  23.2 0.0 copy-start.5
  23.2 3.7 all-to-all-start.1
  26.9 0.0 all-reduce.3.cloned.1.call-start
  26.9 6.3 %copy.28 = bf16[8192,256]{0,1:T(8,128)(2,1)} copy(bf16[8192,256]{1,0:T(8,128)(2,1)} %param.7) | data formatting | bytes 8388608 | tf_op args[2]
  33.2 0.0 copy-done.5
  33.3 0.1 fusion.27
  33.4 0.1 fusion.23
  33.5 93.7 %all_gather.3 = bf16[512,256]{1,0:T(8,128)(2,1)S(1)} all-gather(bf16[64,256]{1,0:T(8,128)(2,1)S(1)} %fusion.23), channel_id=1, replica_groups=mesh['grp'=4,'rep'=8] {'rep'}, dimensions={0}, use_global_device_ids=true | all-gather | bytes 294912 | tf_op jit(solution)/shard_map/all_gather | solution.py:64
  127.2 3.1 fusion.13
  130.3 0.0 all-to-all-done.1
  130.3 0.0 copy-start.6
  130.3 38.0 %scatter_custom_fusion = bf16[8192,256]{1,0:T(8,128)(2,1)} fusion(s32[8192]{0:T(1024)S(1)} %bitcast.20, bf16[8192,256]{1,0:T(8,128)(2,1)} %bitcast.7, bf16[]{:T(256)} %constant.84.clone.1), kind=kCustom, calls=%fused_computation.30 | custom fusion | bytes 4194816 | tf_op jit(solution)/shard_map/scatter | solution.py:61
  168.3 6.4 %copy.32 = bf16[8192,256]{0,1:T(8,128)(2,1)} copy(bf16[8192,256]{1,0:T(8,128)(2,1)} %scatter_custom_fusion) | data formatting | bytes 8388608 | tf_op jit(solution)/shard_map/scatter | solution.py:61
  174.7 3.1 fusion.14
  177.7 0.0 copy-done.6
  177.8 4.5 %fusion = (f32[512]{0:T(512)S(1)}, f32[512,8192]{1,0:T(8,128)S(1)}) fusion(s32[8192]{0:T(1024)S(1)} %iota_add_fusion, s32[512]{0:T(512)S(1)} %copy-done.6, bf16[512,256]{1,0:T(8,128)(2,1)S(1)} %all_gather.3, bf16[8192,256]{0,1:T(8,128)(2,1)} %copy.28, f32[8192]{0:T(1024)S(1)} %get-tuple-element.82), kind=kOutput, calls=%fused_computation.6 | convolution fusion | flops 2166357504 | bytes 21303296 | tf_op jit(solution)/shard_map/while/body/eval_jaxpr/dot_general | solution.py:78
  182.2 0.0 copy-start
  182.3 5.9 %exponential_reduce_fusion = (f32[512]{0:T(512)S(1)}, f32[512]{0:T(512)S(1)}) fusion(f32[512,8192]{1,0:T(8,128)S(1)} %get-tuple-element.79, f32[512]{0:T(512)S(1)} %get-tuple-element.77, s32[8192]{0:T(1024)S(1)} %iota_add_fusion, s32[512]{0:T(512)S(1)} %copy-done.6), kind=kLoop, calls=%fused_computation.12 | loop fusion | flops 29359104 | bytes 16818176 | tf_op jit(solution)/shard_map/while/body/eval_jaxpr/reduce_sum | solution.py:88
  188.2 0.0 copy-done
  188.2 39.9 %all-reduce = (f32[512]{0:T(512)S(1)}, f32[512]{0:T(512)S(1)}) all-reduce(f32[512]{0:T(512)S(1)} %get-tuple-element.67, f32[512]{0:T(512)S(1)} %get-tuple-element.66), channel_id=1, replica_groups=mesh['grp'=4,'rep'=8] {'grp','rep'}, use_global_device_ids=true, to_apply=%region_6.7 | all-reduce | flops 1024 | bytes 8192 | tf_op jit(solution)/shard_map/psum | solution.py:93
  228.1 0.0 copy-start.1
  228.1 10.0 %fusion.5 = bf16[512,8192]{1,0:T(8,128)(2,1)S(1)} fusion(f32[512,8192]{1,0:T(8,128)} %copy-done, f32[512]{0:T(512)S(1)} %get-tuple-element.76, f32[512]{0:T(512)S(1)} %get-tuple-element.74, f32[512]{0:T(512)S(1)} %get-tuple-element.77, s32[8192]{0:T(1024)S(1)} %iota_add_fusion, s32[512]{0:T(512)S(1)} %copy-done.6), kind=kLoop, calls=%fused_computation.11 | loop fusion | flops 41943040 | bytes 25206784 | tf_op jit(solution)/shard_map/while/body/eval_jaxpr/convert_element_type | solution.py:101
  238.1 0.0 copy-start.4
  238.1 3.4 copy-done.4
  241.5 0.0 copy-done.1
  241.5 3.2 fusion.15
  244.7 0.0 all-reduce.3.cloned.1.call-update
  244.8 0.0 copy-start.2
  244.8 0.0 copy-start.3
  244.8 10.5 %multiply_reduce_fusion = (f32[8192]{0:T(1024)S(1)}, f32[8192]{0:T(1024)S(1)}, f32[8192,256]{0,1:T(8,128)S(1)}) fusion(bf16[8192,256]{0,1:T(8,128)(2,1)} %copy.32, bf16[8192,256]{0,1:T(8,128)(2,1)} %copy.28, f32[8192]{0:T(1024)S(1)} %get-tuple-element.81, f32[8192]{0:T(1024)S(1)} %get-tuple-element.82, bf16[512,8192]{1,0:T(8,128)(2,1)} %copy-done.4, ...), kind=kOutput, calls=%fused_computation.27 | convolution fusion | flops 2166341632 | bytes 25559040 | tf_op jit(solution)/shard_map/dot_general | solution.py:109
  255.3 0.0 copy-done.2
  255.3 0.0 copy-done.3
  255.3 6.0 %multiply_convert_fusion = (bf16[8192,256]{0,1:T(8,128)(2,1)}, f32[8192,256]{0,1:T(8,128)}) fusion(bf16[8192,256]{0,1:T(8,128)(2,1)S(1)} %copy-done.3, bf16[8192,256]{0,1:T(8,128)(2,1)S(1)} %copy-done.2, f32[8192]{0:T(1024)S(1)} %add_rsqrt_fusion, f32[8192]{0:T(1024)S(1)} %get-tuple-element.81, f32[8192]{0:T(1024)S(1)} %get-tuple-element.82, ...), kind=kLoop, calls=%fused_computation.26 | loop fusion | flops 20971520 | bytes 29491200 | tf_op jit(solution)/shard_map/convert_element_type | solution.py:132
  261.3 9.0 %copy.33 = f32[8192,256]{1,0:T(8,128)} copy(f32[8192,256]{0,1:T(8,128)} %get-tuple-element.73) | data formatting | bytes 16777216
  270.3 6.4 %copy.34 = bf16[8192,256]{1,0:T(8,128)(2,1)} copy(bf16[8192,256]{0,1:T(8,128)(2,1)} %get-tuple-element.72) | data formatting | bytes 8388608
  276.7 0.6 dynamic_slice.19
  277.3 95.6 %all-reduce.3.cloned.1.call-done = f32[512,256]{1,0:T(8,128)} async-done(((f32[512,256]{1,0:T(8,128)}), f32[512,256]{1,0:T(8,128)}) %all-reduce.3.cloned.1.call-update) | async-done | bytes 524304 | tf_op jit(solution)/shard_map/psum | solution.py:120
  372.9 1.0 fusion.24
  373.9 1.6 fusion.26
  (8 shorter events, 0.1 us)
Async XLA Ops:
  8.6 14.5 %all-to-all-start = ((s32[32,1,256]{2,1,0:T(1,128)}), s32[32,1,256]{2,1,0:T(1,128)S(1)}, u32[]{:S(2)}, u32[]{:S(2)}) async-start(s32[32,1,256]{2,1,0:T(1,128)} %copy.30), calls=%async_computation | async-start | bytes 65536 | tf_op jit(solution)/shard_map/all_to_all | solution.py:50
  23.2 10.1 %copy-start.5 = (bf16[64,256]{1,0:T(8,128)(2,1)S(1)}, bf16[64,256]{1,0:T(8,128)(2,1)}, u32[]{:S(2)}) copy-start(bf16[64,256]{1,0:T(8,128)(2,1)} %param.5) | copy-start | bytes 98308
  23.2 107.2 %all-to-all-start.1 = ((bf16[32,256,256]{2,1,0:T(8,128)(2,1)}), bf16[32,256,256]{2,1,0:T(8,128)(2,1)}, u32[]{:S(2)}, u32[]{:S(2)}) async-start(bf16[32,256,256]{2,1,0:T(8,128)(2,1)} %bitcast.15), calls=%async_computation.1 | async-start | bytes 8388608 | tf_op jit(solution)/shard_map/all_to_all | solution.py:43
  26.9 346.0 %all-reduce.3.cloned.1.call-start = ((), (), s32[]{:S(2)}) async-start(), calls=%async_computation.2 | async-start | bytes 1048576 | tf_op jit(solution)/shard_map/psum | solution.py:120
  130.3 47.4 %copy-start.6 = (s32[512]{0:T(512)S(1)}, s32[512]{0:T(512)}, u32[]{:S(2)}) copy-start(s32[512]{0:T(512)} %param.6) | copy-start | bytes 6148
  182.2 6.0 %copy-start = (f32[512,8192]{1,0:T(8,128)}, f32[512,8192]{1,0:T(8,128)S(1)}, u32[]{:S(2)}) copy-start(f32[512,8192]{1,0:T(8,128)S(1)} %get-tuple-element.79) | copy-start | bytes 50331652
  228.1 13.4 %copy-start.1 = (bf16[8192,256]{0,1:T(8,128)(2,1)S(1)}, bf16[8192,256]{0,1:T(8,128)(2,1)}, u32[]{:S(2)}) copy-start(bf16[8192,256]{0,1:T(8,128)(2,1)} %copy.28) | copy-start | bytes 12582916
  238.1 3.4 copy-start.4
  244.8 10.5 %copy-start.2 = (bf16[8192,256]{0,1:T(8,128)(2,1)S(1)}, bf16[8192,256]{0,1:T(8,128)(2,1)}, u32[]{:S(2)}) copy-start(bf16[8192,256]{0,1:T(8,128)(2,1)} %copy.28) | copy-start | bytes 12582916
  244.8 10.5 %copy-start.3 = (bf16[8192,256]{0,1:T(8,128)(2,1)S(1)}, bf16[8192,256]{0,1:T(8,128)(2,1)}, u32[]{:S(2)}) copy-start(bf16[8192,256]{0,1:T(8,128)(2,1)} %copy.32) | copy-start | bytes 12582916
Sparse Core Ops, SparseCore 0:
  244.9 127.9 all-reduce.2
where the time goes:
time: 383 us; the launch traced here: 382 us
  blocking collectives  134 us (35%)
  waiting for transfers between devices  98.2 us (26%)
  local copies, waits for them, and re-layouts  76.1 us (20%)
  other arithmetic  30.9 us (8%)
  matrix products  18.2 us (5%)
  between operations  14.2 us (4%)
  starting transfers between devices  11 us (3%)
    psum x1, waiting for transfers between devices, shards(): lax.psum(jnp.dot(cosine_gradient, what, preferred_element_type=jnp.float3...  95.6 us
    all_gather x1, blocking collectives, shards(): lax.all_gather(normalized_input_wide.astype(jnp.bfloat16), 'rep', axis=0,...  93.7 us
    scatter x2, local copies, waits for them, and re-layouts, shards(): relaid = jnp.zeros((classes_local, feature_width), jnp.bfloat16).at[slots...  44.3 us
    psum x1, blocking collectives, shards(): lax.psum((exp_parts.reshape(-1), target_parts.reshape(-1)), ('grp', 'rep'))  39.9 us
    unnamed x17, local copies, waits for them, and re-layouts  25.1 us
    dot_general x1, matrix products, shards(): lax.dot_general(cosine_gradient, normalized_input_full, (((0,), (0,)), ((...  10.5 us
    convert_element_type x1, other arithmetic, second_pass(): (SCALE * (probs - onehot) * jnp.where(is_label, margin_slope[:, None], 1....  10 us
  transfers between devices with their start and end apart: 3, of which 2 were waited for; matrix products, arithmetic and copies ran while one was open for 12% of the time, Pallas kernels for 0%

commit v1 on v0

v1 whole, which is shorter than its diff:
```python
import functools
import math

import jax
import jax.numpy as jnp
from jax import lax
from jax.experimental import pallas as pl
from jax.experimental.pallas import tpu as pltpu
from jax.sharding import PartitionSpec as P

SCALE = 32.0
MARGIN = 0.2
SIN_FLOOR = 0.09
LOG2E = math.log2(math.e)
ALL = ("rep", "grp")
VMEM_BYTES = 50 * 1024 * 1024

NT = (((1,), (1,)), ((), ()))


def unit_rows(wide):
    inv = lax.rsqrt(jnp.sum(wide * wide, axis=1, keepdims=True) + 1e-06)
    return wide * inv, inv


def column_of(row):
    lanes = row.shape[1]
    return jnp.transpose(jnp.broadcast_to(row, (128, lanes)))[:, :1]


def forward_kernel(base_ref, emb_ref, lab_ref, w_ref, a_ref, b_ref, st_ref, xhat_ref, sum_ref, *, classes):
    step = pl.program_id(0)
    tile = w_ref.shape[0]
    batch = emb_ref.shape[0]

    @pl.when(step == 0)
    def _():
        xwide, _ = unit_rows(emb_ref[...].astype(jnp.float32))
        xhat_ref[...] = xwide.astype(jnp.bfloat16)
        sum_ref[...] = jnp.zeros_like(sum_ref)
        a_ref[...] = jnp.zeros_like(a_ref)
        b_ref[...] = jnp.zeros_like(b_ref)

    wwide, _ = unit_rows(w_ref[...].astype(jnp.float32))
    what = wwide.astype(jnp.bfloat16)
    cosine = lax.dot_general(xhat_ref[...], what, NT, preferred_element_type=jnp.float32)
    ids = lax.broadcasted_iota(jnp.int32, (batch, tile), 1)
    is_label = ids == lab_ref[...] - (base_ref[0] + step * tile)
    e = jnp.where(is_label, 0.0, jnp.exp2(cosine * (SCALE * LOG2E) - SCALE * LOG2E))
    partial = e[:, :128]
    for c in range(1, tile // 128):
        partial = partial + e[:, c * 128 : (c + 1) * 128]
    sum_ref[...] += partial
    onehot = jnp.where(is_label, 1.0, 0.0).astype(jnp.bfloat16)
    a_ref[...] += jnp.dot(e.astype(jnp.bfloat16), what, preferred_element_type=jnp.float32)
    b_ref[...] += jnp.dot(onehot, what, preferred_element_type=jnp.float32)

    @pl.when(step == pl.num_programs(0) - 1)
    def _():
        xwide, x_inv = unit_rows(emb_ref[...].astype(jnp.float32))
        label_row = b_ref[...]
        c = jnp.sum(xhat_ref[...].astype(jnp.float32) * label_row, axis=1, keepdims=True)
        offset = lab_ref[...] - base_ref[0]
        has = jnp.where((offset >= 0) & (offset < classes), 1.0, 0.0)
        q = 1.0 - c * c
        sine = jnp.sqrt(jnp.maximum(q, SIN_FLOOR))
        margined = c * math.cos(MARGIN) - sine * math.sin(MARGIN)
        slope = math.cos(MARGIN) + jnp.where(q > SIN_FLOOR, c * math.sin(MARGIN) / sine, 0.0)
        slope = slope * has
        label_e = jnp.exp(SCALE * margined - SCALE) * has
        total = jnp.sum(sum_ref[...], axis=1, keepdims=True) + label_e
        target = SCALE * margined * has
        b = slope * label_row
        a = a_ref[...] + label_e * b
        gain = SCALE * x_inv
        a_ref[...] = (a - xwide * jnp.sum(xwide * a, axis=1, keepdims=True)) * gain
        b_ref[...] = (b - xwide * jnp.sum(xwide * b, axis=1, keepdims=True)) * gain
        lane = lax.broadcasted_iota(jnp.int32, (batch, 128), 1)
        stats = jnp.where(lane == 0, total, 0.0)
        stats = jnp.where(lane == 1, target, stats)
        stats = jnp.where(lane == 2, label_e * slope, stats)
        stats = jnp.where(lane == 3, slope, stats)
        st_ref[...] = jnp.transpose(stats)[:8, :]


def forward(base, emb, labels, weights):
    batch, width = emb.shape
    classes = weights.shape[0]
    tile = math.gcd(classes, 1024)
    whole = lambda i: (0, 0)
    return pl.pallas_call(
        functools.partial(forward_kernel, classes=classes),
        grid=(classes // tile,),
        in_specs=[
            pl.BlockSpec(memory_space=pltpu.SMEM),
            pl.BlockSpec((batch, width), whole),
            pl.BlockSpec((batch, 1), whole),
            pl.BlockSpec((tile, width), lambda i: (i, 0)),
        ],
        out_specs=[
            pl.BlockSpec((batch, width), whole),
            pl.BlockSpec((batch, width), whole),
            pl.BlockSpec((8, batch), whole),
        ],
        out_shape=[
            jax.ShapeDtypeStruct((batch, width), jnp.float32),
            jax.ShapeDtypeStruct((batch, width), jnp.float32),
            jax.ShapeDtypeStruct((8, batch), jnp.float32),
        ],
        scratch_shapes=[pltpu.VMEM((batch, width), jnp.bfloat16), pltpu.VMEM((batch, 128), jnp.float32)],
        compiler_params=pltpu.CompilerParams(
            dimension_semantics=("arbitrary",), vmem_limit_bytes=VMEM_BYTES
        ),
        cost_estimate=pl.CostEstimate(
            flops=6 * batch * classes * width,
            bytes_accessed=classes * width * 2,
            transcendentals=batch * classes,
        ),
        name="forward_sums",
    )(base, emb, labels.reshape(batch, 1), weights)


def weight_kernel(base_ref, emb_ref, lab_ref, st_ref, tot_ref, w_ref, g_ref, xhat_ref, y_ref, v_ref):
    step = pl.program_id(0)
    tile = w_ref.shape[0]
    batch = emb_ref.shape[0]

    @pl.when(step == 0)
    def _():
        xwide, _ = unit_rows(emb_ref[...].astype(jnp.float32))
        xhat = xwide.astype(jnp.bfloat16)
        xhat_ref[...] = xhat
        total = tot_ref[...]
        y_ref[...] = (xhat.astype(jnp.float32) * column_of(SCALE / total)).astype(jnp.bfloat16)
        v_ref[...] = st_ref[2:3, :] - st_ref[3:4, :] * total

    wwide, w_inv = unit_rows(w_ref[...].astype(jnp.float32))
    what = wwide.astype(jnp.bfloat16)
    cosine = lax.dot_general(what, xhat_ref[...], NT, preferred_element_type=jnp.float32)
    ids = lax.broadcasted_iota(jnp.int32, (tile, batch), 0)
    is_label = ids == lab_ref[...] - (base_ref[0] + step * tile)
    e = jnp.exp2(cosine * (SCALE * LOG2E) - SCALE * LOG2E)
    d = jnp.where(is_label, v_ref[...], e).astype(jnp.bfloat16)
    raw = jnp.dot(d, y_ref[...], preferred_element_type=jnp.float32)
    g_ref[...] = (raw - wwide * jnp.sum(wwide * raw, axis=1, keepdims=True)) * w_inv


def weight_gradient(base, emb, labels, stats, totals, weights):
    batch, width = emb.shape
    classes = weights.shape[0]
    tile = math.gcd(classes, 1024)
    whole = lambda i: (0, 0)
    return pl.pallas_call(
        weight_kernel,
        grid=(classes // tile,),
        in_specs=[
            pl.BlockSpec(memory_space=pltpu.SMEM),
            pl.BlockSpec((batch, width), whole),
            pl.BlockSpec((1, batch), whole),
            pl.BlockSpec((8, batch), whole),
            pl.BlockSpec((1, batch), whole),
            pl.BlockSpec((tile, width), lambda i: (i, 0)),
        ],
        out_specs=pl.BlockSpec((tile, width), lambda i: (i, 0)),
        out_shape=jax.ShapeDtypeStruct((classes, width), jnp.float32),
        scratch_shapes=[
            pltpu.VMEM((batch, width), jnp.bfloat16),
            pltpu.VMEM((batch, width), jnp.bfloat16),
            pltpu.VMEM((1, batch), jnp.float32),
        ],
        compiler_params=pltpu.CompilerParams(
            dimension_semantics=("arbitrary",), vmem_limit_bytes=VMEM_BYTES
        ),
        cost_estimate=pl.CostEstimate(
            flops=4 * batch * classes * width,
            bytes_accessed=classes * width * 6,
            transcendentals=batch * classes,
        ),
        name="weight_gradient",
    )(base, emb, labels.reshape(1, batch), stats, totals.reshape(1, batch), weights)


def refresh_kernel(slot_ref, rows_ref, w_ref, o_ref, stage_ref, held_ref):
    step = pl.program_id(0)
    parts = pl.num_programs(0) // 2
    tile = rows_ref.shape[0]

    @pl.when(step < parts)
    def _():
        unit, _ = unit_rows(rows_ref[...].astype(jnp.float32))
        stage_ref[0] = unit[:, :128]
        stage_ref[1] = unit[:, 128:]
        first = step * tile

        def place(j, carry):
            for u in range(16):
                row = j * 16 + u
                slot = slot_ref[first + row]
                held_ref[0, pl.ds(slot, 1), :] = stage_ref[0, pl.ds(row, 1), :]
                held_ref[1, pl.ds(slot, 1), :] = stage_ref[1, pl.ds(row, 1), :]
            return carry

        lax.fori_loop(0, tile // 16, place, 0)

    @pl.when(step >= parts)
    def _():
        wwide, _ = unit_rows(w_ref[...].astype(jnp.float32))
        at = pl.ds(pl.multiple_of((step - parts) * tile, tile), tile)
        low = wwide[:, :128] + held_ref[0, at, :]
        high = wwide[:, 128:] + held_ref[1, at, :]
        square = jnp.sum(low * low + high * high, axis=1, keepdims=True)
        inv = lax.rsqrt(square + 1e-06)
        o_ref[:, :128] = (low * inv).astype(jnp.bfloat16)
        o_ref[:, 128:] = (high * inv).astype(jnp.bfloat16)


def refresh(slots, rows, weights):
    classes, width = weights.shape
    tile = math.gcd(classes, 1024)
    parts = classes // tile
    return pl.pallas_call(
        refresh_kernel,
        grid=(2 * parts,),
        in_specs=[
            pl.BlockSpec(memory_space=pltpu.SMEM),
            pl.BlockSpec((tile, width), lambda i: (jnp.minimum(i, parts - 1), 0)),
            pl.BlockSpec((tile, width), lambda i: (jnp.maximum(i - parts, 0), 0)),
        ],
        out_specs=pl.BlockSpec((tile, width), lambda i: (jnp.maximum(i - parts, 0), 0)),
        out_shape=jax.ShapeDtypeStruct((classes, width), jnp.bfloat16),
        scratch_shapes=[
            pltpu.VMEM((2, tile, 128), jnp.float32),
            pltpu.VMEM((2, classes, 128), jnp.float32),
        ],
        compiler_params=pltpu.CompilerParams(
            dimension_semantics=("arbitrary",), vmem_limit_bytes=VMEM_BYTES
        ),
        cost_estimate=pl.CostEstimate(
            flops=10 * classes * width, bytes_accessed=classes * width * 6, transcendentals=classes
        ),
        name="refresh",
    )(slots, rows, weights)


def shifted(value, axis, shift):
    size = lax.axis_size(axis)
    return lax.ppermute(value, axis, [(i, (i + shift) % size) for i in range(size)])


def sum_over(value, axis):
    return sum((shifted(value, axis, s) for s in range(1, lax.axis_size(axis))), value)


def scatter_sum(blocks, axis):
    size, me = lax.axis_size(axis), lax.axis_index(axis)
    total = lax.dynamic_index_in_dim(blocks, me, 0, keepdims=False)
    for s in range(1, size):
        total = total + shifted(
            lax.dynamic_index_in_dim(blocks, (me + s) % size, 0, keepdims=False), axis, s
        )
    return total


def gather_blocks(block, axis):
    size, me = lax.axis_size(axis), lax.axis_index(axis)
    stack = jnp.stack([block] + [shifted(block, axis, s) for s in range(1, size)])
    return stack[(me - jnp.arange(size)) % size]


def shards(embeddings, labels, class_weights, centroids, centroid_class):
    rows_local, width = embeddings.shape
    classes = class_weights.shape[0]
    groups, reps = lax.axis_size("grp"), lax.axis_size("rep")
    peers = groups * reps
    batch = rows_local * reps
    per_peer = classes // peers
    share = rows_local // groups
    grp, rep = lax.axis_index("grp"), lax.axis_index("rep")
    base = ((rep * groups + grp) * classes).astype(jnp.int32).reshape(1)

    slots = centroid_class.reshape(peers, per_peer)
    digits = jnp.concatenate([slots // 128, slots % 128], axis=1).astype(jnp.bfloat16)
    digit_rows = -(-2 * per_peer // width)
    digits = jnp.pad(digits, ((0, 0), (0, digit_rows * width - 2 * per_peer)))
    mine = lax.dynamic_slice_in_dim(embeddings, grp * share, share, 0)
    head = jnp.concatenate(
        [jnp.broadcast_to(mine[None], (peers, share, width)), digits.reshape(peers, digit_rows, width)],
        axis=1,
    )
    head = lax.all_to_all(head, ALL, 0, 0, tiled=True)
    emb = head[:, :share].reshape(batch, width)
    digits = head[:, share:].reshape(peers, digit_rows * width).astype(jnp.int32)
    slots_got = (digits[:, :per_peer] * 128 + digits[:, per_peer : 2 * per_peer]).reshape(-1)
    rows_got = lax.all_to_all(centroids.reshape(peers, per_peer, width), ALL, 0, 0, tiled=True)

    a, b, stats = forward(base, emb, labels, class_weights)
    totals = sum_over(sum_over(stats[:2], "grp"), "rep")
    total, target = totals[0], totals[1]
    weight_grad = weight_gradient(base, emb, labels, stats, total, class_weights)
    loss = lax.dynamic_slice_in_dim(SCALE + jnp.log(total) - target, rep * rows_local, rows_local, 0)
    grad = a / total[:, None] - b
    blocks = grad.reshape(reps, groups, share, width).transpose(1, 0, 2, 3)
    own = scatter_sum(scatter_sum(blocks, "grp"), "rep")
    embedding_gradient = gather_blocks(own, "grp").reshape(rows_local, width)
    refreshed = refresh(slots_got, rows_got.reshape(classes, width), class_weights)
    return (loss, embedding_gradient, weight_grad, refreshed)


def solution(mesh):
    in_specs = (
        P("rep", None),
        P(),
        P(("rep", "grp"), None),
        P(("grp", "rep"), None),
        P(("grp", "rep")),
    )
    out_specs = (P("rep"), P("rep", None), P(("rep", "grp"), None), P(("rep", "grp"), None))
    return jax.shard_map(shards, mesh=mesh, in_specs=in_specs, out_specs=out_specs, check_vma=False)
```

time: 383 us -> 183 us (0.48)
  blocking collectives: 134 us -> 20.7 us
  local copies, waits for them, and re-layouts: 76.1 us -> 2.07 us
  Pallas kernels: 0 us -> 46.5 us
  starting transfers between devices: 11 us -> 57 us
  waiting for transfers between devices: 98.2 us -> 54.2 us
  other arithmetic: 30.9 us -> 1.36 us
  matrix products: 18.2 us -> 0 us
  between operations: 14.2 us -> 0.86 us
    psum x1 -> x0, waiting for transfers between devices: 95.6 us -> none  [shards(): lax.psum(jnp.dot(cosine_gradient, what, preferred_element_type=jnp.float3...]
    all_gather x1 -> x0, blocking collectives: 93.7 us -> none  [shards(): lax.all_gather(normalized_input_wide.astype(jnp.bfloat16), 'rep', axis=0,...]
    ppermute x0 -> x23, waiting for transfers between devices: none -> 54.2 us  [shifted(): lax.ppermute(value, axis, [(i, (i + shift) % size) for i in range(size)])]
    ppermute x0 -> x23, starting transfers between devices: none -> 53.3 us  [shifted(): lax.ppermute(value, axis, [(i, (i + shift) % size) for i in range(size)])]
    pallas_call x0 -> x3, Pallas kernels: none -> 46.5 us  [the longest x1 21.9 us: refresh(): pl.pallas_call(refresh_kernel, grid=(2 * parts,), in_specs=[pl.BlockSpec(...]
    scatter x2 -> x0, local copies, waits for them, and re-layouts: 44.3 us -> none  [shards(): relaid = jnp.zeros((classes_local, feature_width), jnp.bfloat16).at[slots...]
    psum x1 -> x0, blocking collectives: 39.9 us -> none  [shards(): lax.psum((exp_parts.reshape(-1), target_parts.reshape(-1)), ('grp', 'rep'))]
    unnamed x17 -> x6, local copies, waits for them, and re-layouts: 25.1 us -> 0.04 us
  transfers between devices with their start and end apart: 3 -> 24, of which waited for: 2 -> 9; matrix products, arithmetic and copies ran while one was open for 12% -> 1% of each run, Pallas kernels for 0% -> 13%
where the time goes in v1:
time: 183 us
  starting transfers between devices  57 us (31%)
  waiting for transfers between devices  54.2 us (30%)
  Pallas kernels  46.5 us (25%)
  blocking collectives  20.7 us (11%)
  local copies, waits for them, and re-layouts  2.07 us (1%)
    ppermute x23, waiting for transfers between devices, shifted(): lax.ppermute(value, axis, [(i, (i + shift) % size) for i in range(size)])  54.2 us
    ppermute x23, starting transfers between devices, shifted(): lax.ppermute(value, axis, [(i, (i + shift) % size) for i in range(size)])  53.3 us
    pallas_call x1, Pallas kernels, refresh(): pl.pallas_call(refresh_kernel, grid=(2 * parts,), in_specs=[pl.BlockSpec(...  21.9 us
    all_to_all x1, blocking collectives, shards(): head = lax.all_to_all(head, ALL, 0, 0, tiled=True)  20.7 us
    pallas_call x1, Pallas kernels, forward(): pl.pallas_call(functools.partial(forward_kernel, classes=classes), grid=(...  12.8 us
    pallas_call x1, Pallas kernels, weight_gradient(): pl.pallas_call(weight_kernel, grid=(classes // tile,), in_specs=[pl.Block...  11.8 us
    all_to_all x1, starting transfers between devices, shards(): lax.all_to_all(centroids.reshape(peers, per_peer, width), ALL, 0, 0, tile...  3.71 us
  transfers between devices with their start and end apart: 24, of which 9 were waited for; matrix products, arithmetic and copies ran while one was open for 1% of the time, Pallas kernels for 13%

profile of v1, /device:TPU:0, one launch (start us, length us, event | category | flops | bytes accessed | tf_op | source)
XLA Modules:
  0.0 182.7 jit_solution(4852794599829951887)
XLA Ops:
  0.6 0.0 copy-start
  0.7 0.9 fusion.4
  1.6 0.1 fusion.2
  1.6 0.0 copy-done
  1.7 0.1 pad_maximum_fusion
  1.8 20.7 %all_to_all.10 = bf16[32,18,256]{2,1,0:T(8,128)(2,1)S(1)} all-to-all(bf16[32,18,256]{2,1,0:T(8,128)(2,1)S(1)} %pad_maximum_fusion), channel_id=1, replica_groups=mesh['grp'=4,'rep'=8] {'rep','grp'}, dimensions={0} | all-to-all | bytes 589824 | tf_op jit(solution)/shard_map/all_to_all | solution.py:290
  22.5 0.0 copy-start.1
  22.5 3.7 %all-to-all-start.1 = ((bf16[32,256,256]{2,1,0:T(8,128)(2,1)}), bf16[32,256,256]{2,1,0:T(8,128)(2,1)}, u32[]{:S(2)}, u32[]{:S(2)}) async-start(bf16[32,256,256]{2,1,0:T(8,128)(2,1)} %bitcast.69), calls=%async_computation.1 | async-start | bytes 8388608 | tf_op jit(solution)/shard_map/all_to_all | solution.py:294
  26.3 0.0 copy-done.1
  26.3 0.1 copy.9.lab_ref
  26.5 12.8 %forward_sums.1 = (f32[512,256]{1,0:T(8,128)S(1)}, f32[512,256]{1,0:T(8,128)S(1)}, f32[8,512]{1,0:T(8,128)S(1)}) custom-call(s32[1]{0:T(128)} %bitcast.base_ref, bf16[512,256]{1,0:T(8,128)(2,1)S(1)} %bitcast.62, s32[512,1]{1,0:T(8,128)S(1)} %copy.9.lab_ref, bf16[8192,256]{1,0:T(8,128)(2,1)} %w_ref.5), custom_call_target="tpu_custom_call" | custom-call | flops 6442450944 | bytes 4194304 | tf_op jit(solution)/shard_map/forward_sums/pallas_call | solution.py:91
  39.3 1.6 collective-permute-start.1
  40.9 1.4 collective-permute-start.2
  42.3 0.6 collective-permute-start
  42.9 5.4 %collective-permute-done.1 = f32[2,512]{1,0:T(2,128)S(1)} collective-permute-done((f32[2,512]{1,0:T(2,128)S(1)}, f32[2,512]{1,0:T(2,128)S(1)}, u32[]{:S(2)}, u32[]{:S(2)}) %collective-permute-start.1) | collective-permute-done | bytes 4128 | tf_op jit(solution)/shard_map/ppermute | solution.py:247
  48.4 6.5 %collective-permute-done.2 = f32[2,512]{1,0:T(2,128)S(1)} collective-permute-done((f32[2,512]{1,0:T(2,128)S(1)}, f32[2,512]{1,0:T(2,128)S(1)}, u32[]{:S(2)}, u32[]{:S(2)}) %collective-permute-start.2) | collective-permute-done | bytes 4128 | tf_op jit(solution)/shard_map/ppermute | solution.py:247
  54.9 0.0 collective-permute-done
  54.9 5.2 %collective-permute-start.9 = (f32[2,512]{1,0:T(2,128)S(1)}, f32[2,512]{1,0:T(2,128)S(1)}, u32[]{:S(2)}, u32[]{:S(2)}) collective-permute-start(f32[2,512]{1,0:T(2,128)S(1)} %add_add_fusion.1), channel_id=1, source_target_pairs={{0,7},{1,0},{2,1},{3,2},{4,3},{5,4},{6,5},{7,6},{8,15},{9,8},{10,9... | collective-permute-start | bytes 12296 | tf_op jit(solution)/shard_map/ppermute | solution.py:247
  60.1 0.4 collective-permute-start.8
  60.5 0.0 collective-permute-start.7
  60.5 2.7 %collective-permute-start.6 = (f32[2,512]{1,0:T(2,128)S(1)}, f32[2,512]{1,0:T(2,128)S(1)}, u32[]{:S(2)}, u32[]{:S(2)}) collective-permute-start(f32[2,512]{1,0:T(2,128)S(1)} %add_add_fusion.1), channel_id=1, source_target_pairs={{0,4},{1,5},{2,6},{3,7},{4,0},{5,1},{6,2},{7,3},{8,12},{9,13},{10,... | collective-permute-start | bytes 12296 | tf_op jit(solution)/shard_map/ppermute | solution.py:247
  63.2 0.0 collective-permute-start.5
  63.2 31.4 %collective-permute-done.9 = f32[2,512]{1,0:T(2,128)S(1)} collective-permute-done((f32[2,512]{1,0:T(2,128)S(1)}, f32[2,512]{1,0:T(2,128)S(1)}, u32[]{:S(2)}, u32[]{:S(2)}) %collective-permute-start.9) | collective-permute-done | bytes 4128 | tf_op jit(solution)/shard_map/ppermute | solution.py:247
  94.6 0.0 collective-permute-start.4
  94.7 0.0 collective-permute-done.8
  94.7 26.6 %collective-permute-start.3 = (f32[2,512]{1,0:T(2,128)S(1)}, f32[2,512]{1,0:T(2,128)S(1)}, u32[]{:S(2)}, u32[]{:S(2)}) collective-permute-start(f32[2,512]{1,0:T(2,128)S(1)} %add_add_fusion.1), channel_id=1, source_target_pairs={{0,1},{1,2},{2,3},{3,4},{4,5},{5,6},{6,7},{7,0},{8,9},{9,10},{10,1... | collective-permute-start | bytes 12296 | tf_op jit(solution)/shard_map/ppermute | solution.py:247
  121.2 0.0 collective-permute-done.7
  121.2 0.0 collective-permute-done.6
  121.2 0.0 collective-permute-done.5
  121.2 0.0 collective-permute-done.4
  121.2 0.8 collective-permute-done.3
  122.1 0.1 divide_subtract_fusion
  122.3 1.1 collective-permute-start.10
  123.3 1.9 %collective-permute-start.12 = (f32[8,16,256]{2,1,0:T(8,128)S(1)}, f32[8,16,256]{2,1,0:T(8,128)S(1)}, u32[]{:S(2)}, u32[]{:S(2)}) collective-permute-start(f32[8,16,256]{2,1,0:T(8,128)S(1)} %get-tuple-element.13), channel_id=1, source_target_pairs={{0,24},{8,0},{16,8},{24,16},{1,25},{9,1},{17,9},{25,17},{2,26},{10... | collective-permute-start | bytes 393224 | tf_op jit(solution)/shard_map/ppermute | solution.py:247
  125.2 0.8 collective-permute-start.11
  126.0 3.5 %collective-permute-done.10 = f32[8,16,256]{2,1,0:T(8,128)S(1)} collective-permute-done((f32[8,16,256]{2,1,0:T(8,128)S(1)}, f32[8,16,256]{2,1,0:T(8,128)S(1)}, u32[]{:S(2)}, u32[]{:S(2)}) %collective-permute-start.10) | collective-permute-done | bytes 131104 | tf_op jit(solution)/shard_map/ppermute | solution.py:247
  129.5 1.8 collective-permute-done.12
  131.3 0.7 collective-permute-done.11
  132.0 0.1 collective-permute-start.13
  132.1 3.5 %collective-permute-start.19 = (f32[16,256]{1,0:T(8,128)S(1)}, f32[16,256]{1,0:T(8,128)S(1)}, u32[]{:S(2)}, u32[]{:S(2)}) collective-permute-start(f32[16,256]{1,0:T(8,128)S(1)} %get-tuple-element.16), channel_id=1, source_target_pairs={{0,7},{1,0},{2,1},{3,2},{4,3},{5,4},{6,5},{7,6},{8,15},{9,8},{10,9... | collective-permute-start | bytes 49160 | tf_op jit(solution)/shard_map/ppermute | solution.py:247
  135.7 0.1 collective-permute-start.18
  135.7 0.1 collective-permute-start.17
  135.8 2.6 %collective-permute-start.16 = (f32[16,256]{1,0:T(8,128)S(1)}, f32[16,256]{1,0:T(8,128)S(1)}, u32[]{:S(2)}, u32[]{:S(2)}) collective-permute-start(f32[16,256]{1,0:T(8,128)S(1)} %get-tuple-element.19), channel_id=1, source_target_pairs={{0,4},{1,5},{2,6},{3,7},{4,0},{5,1},{6,2},{7,3},{8,12},{9,13},{10,... | collective-permute-start | bytes 49160 | tf_op jit(solution)/shard_map/ppermute | solution.py:247
  138.4 0.0 collective-permute-done.13
  138.4 0.0 collective-permute-start.15
  138.4 0.0 collective-permute-done.19
  138.4 1.1 collective-permute-start.14
  139.5 11.8 %weight_gradient.1 = f32[8192,256]{1,0:T(8,128)} custom-call(s32[1]{0:T(128)} %bitcast.base_ref, bf16[512,256]{1,0:T(8,128)(2,1)S(1)} %bitcast.63, s32[1,512]{1,0:T(1,128)S(1)} %bitcast.68, f32[8,512]{1,0:T(8,128)S(1)} %get-tuple-element.7.st_ref, f32[1,512]{1,0:T(1,128)S(1)} %get-tuple-element.22.tot_ref, bf16[8192,256]{1,0:T(8,128)(2,1)} %w_ref.5), custom_call_target="tpu_custom_call" | custom-call | flops 4294967296 | bytes 12582912 | tf_op jit(solution)/shard_map/weight_gradient/pallas_call | solution.py:153
  151.3 0.0 collective-permute-done.18
  151.3 0.0 collective-permute-done.17
  151.3 0.0 collective-permute-done.16
  151.3 0.0 collective-permute-done.15
  151.4 0.0 collective-permute-done.14
  151.4 2.8 %collective-permute-start.22 = (f32[16,256]{1,0:T(8,128)S(1)}, f32[16,256]{1,0:T(8,128)S(1)}, u32[]{:S(2)}, u32[]{:S(2)}) collective-permute-start(f32[16,256]{1,0:T(8,128)S(1)} %fusion.10), channel_id=1, source_target_pairs={{0,24},{8,0},{16,8},{24,16},{1,25},{9,1},{17,9},{25,17},{2,26},{10... | collective-permute-start | bytes 49160 | tf_op jit(solution)/shard_map/ppermute | solution.py:247
  154.2 0.8 collective-permute-start.21
  155.0 0.0 collective-permute-start.20
  155.0 0.6 dynamic_slice.37
  155.6 0.0 collective-permute-done.22
  155.6 2.3 %collective-permute-done.21 = f32[16,256]{1,0:T(8,128)S(1)} collective-permute-done((f32[16,256]{1,0:T(8,128)S(1)}, f32[16,256]{1,0:T(8,128)S(1)}, u32[]{:S(2)}, u32[]{:S(2)}) %collective-permute-start.21) | collective-permute-done | bytes 16416 | tf_op jit(solution)/shard_map/ppermute | solution.py:247
  158.0 1.7 collective-permute-done.20
  159.7 1.2 gather_fusion
  160.8 0.0 all-to-all-done.1
  160.8 21.9 %refresh.1 = bf16[8192,256]{1,0:T(8,128)(2,1)} custom-call(s32[8192]{0:T(1024)S(1)} %bitcast.64, bf16[8192,256]{1,0:T(8,128)(2,1)} %bitcast.27.rows_ref, bf16[8192,256]{1,0:T(8,128)(2,1)} %w_ref.5), custom_call_target="tpu_custom_call" | custom-call | flops 20971520 | bytes 12582912 | tf_op jit(solution)/shard_map/refresh/pallas_call | solution.py:221
  (19 shorter events, 0.3 us)
Async XLA Ops:
  0.6 1.0 copy-start
  22.5 3.7 %copy-start.1 = (s32[512]{0:T(512)S(1)}, s32[512]{0:T(512)}, u32[]{:S(2)}) copy-start(s32[512]{0:T(512)} %param.6) | copy-start | bytes 6148
  22.5 138.3 %all-to-all-start.1 = ((bf16[32,256,256]{2,1,0:T(8,128)(2,1)}), bf16[32,256,256]{2,1,0:T(8,128)(2,1)}, u32[]{:S(2)}, u32[]{:S(2)}) async-start(bf16[32,256,256]{2,1,0:T(8,128)(2,1)} %bitcast.69), calls=%async_computation.1 | async-start | bytes 8388608 | tf_op jit(solution)/shard_map/all_to_all | solution.py:294
  39.3 9.1 %collective-permute-start.1 = (f32[2,512]{1,0:T(2,128)S(1)}, f32[2,512]{1,0:T(2,128)S(1)}, u32[]{:S(2)}, u32[]{:S(2)}) collective-permute-start(f32[2,512]{1,0:T(2,128)S(1)} %slice.22), channel_id=1, source_target_pairs={{0,16},{8,24},{16,0},{24,8},{1,17},{9,25},{17,1},{25,9},{2,18},{10... | collective-permute-start | bytes 12296 | tf_op jit(solution)/shard_map/ppermute | solution.py:247
  40.9 14.0 %collective-permute-start.2 = (f32[2,512]{1,0:T(2,128)S(1)}, f32[2,512]{1,0:T(2,128)S(1)}, u32[]{:S(2)}, u32[]{:S(2)}) collective-permute-start(f32[2,512]{1,0:T(2,128)S(1)} %slice.22), channel_id=1, source_target_pairs={{0,24},{8,0},{16,8},{24,16},{1,25},{9,1},{17,9},{25,17},{2,26},{10... | collective-permute-start | bytes 12296 | tf_op jit(solution)/shard_map/ppermute | solution.py:247
  42.3 12.5 %collective-permute-start = (f32[2,512]{1,0:T(2,128)S(1)}, f32[2,512]{1,0:T(2,128)S(1)}, u32[]{:S(2)}, u32[]{:S(2)}) collective-permute-start(f32[2,512]{1,0:T(2,128)S(1)} %slice.22), channel_id=1, source_target_pairs={{0,8},{8,16},{16,24},{24,0},{1,9},{9,17},{17,25},{25,1},{2,10},{10... | collective-permute-start | bytes 12296 | tf_op jit(solution)/shard_map/ppermute | solution.py:247
  54.9 39.8 %collective-permute-start.9 = (f32[2,512]{1,0:T(2,128)S(1)}, f32[2,512]{1,0:T(2,128)S(1)}, u32[]{:S(2)}, u32[]{:S(2)}) collective-permute-start(f32[2,512]{1,0:T(2,128)S(1)} %add_add_fusion.1), channel_id=1, source_target_pairs={{0,7},{1,0},{2,1},{3,2},{4,3},{5,4},{6,5},{7,6},{8,15},{9,8},{10,9... | collective-permute-start | bytes 12296 | tf_op jit(solution)/shard_map/ppermute | solution.py:247
  60.1 34.5 %collective-permute-start.8 = (f32[2,512]{1,0:T(2,128)S(1)}, f32[2,512]{1,0:T(2,128)S(1)}, u32[]{:S(2)}, u32[]{:S(2)}) collective-permute-start(f32[2,512]{1,0:T(2,128)S(1)} %add_add_fusion.1), channel_id=1, source_target_pairs={{0,6},{1,7},{2,0},{3,1},{4,2},{5,3},{6,4},{7,5},{8,14},{9,15},{10,... | collective-permute-start | bytes 12296 | tf_op jit(solution)/shard_map/ppermute | solution.py:247
  60.5 60.7 %collective-permute-start.7 = (f32[2,512]{1,0:T(2,128)S(1)}, f32[2,512]{1,0:T(2,128)S(1)}, u32[]{:S(2)}, u32[]{:S(2)}) collective-permute-start(f32[2,512]{1,0:T(2,128)S(1)} %add_add_fusion.1), channel_id=1, source_target_pairs={{0,5},{1,6},{2,7},{3,0},{4,1},{5,2},{6,3},{7,4},{8,13},{9,14},{10,... | collective-permute-start | bytes 12296 | tf_op jit(solution)/shard_map/ppermute | solution.py:247
  60.5 60.7 %collective-permute-start.6 = (f32[2,512]{1,0:T(2,128)S(1)}, f32[2,512]{1,0:T(2,128)S(1)}, u32[]{:S(2)}, u32[]{:S(2)}) collective-permute-start(f32[2,512]{1,0:T(2,128)S(1)} %add_add_fusion.1), channel_id=1, source_target_pairs={{0,4},{1,5},{2,6},{3,7},{4,0},{5,1},{6,2},{7,3},{8,12},{9,13},{10,... | collective-permute-start | bytes 12296 | tf_op jit(solution)/shard_map/ppermute | solution.py:247
  63.2 58.0 %collective-permute-start.5 = (f32[2,512]{1,0:T(2,128)S(1)}, f32[2,512]{1,0:T(2,128)S(1)}, u32[]{:S(2)}, u32[]{:S(2)}) collective-permute-start(f32[2,512]{1,0:T(2,128)S(1)} %add_add_fusion.1), channel_id=1, source_target_pairs={{0,3},{1,4},{2,5},{3,6},{4,7},{5,0},{6,1},{7,2},{8,11},{9,12},{10,... | collective-permute-start | bytes 12296 | tf_op jit(solution)/shard_map/ppermute | solution.py:247
  94.6 26.6 %collective-permute-start.4 = (f32[2,512]{1,0:T(2,128)S(1)}, f32[2,512]{1,0:T(2,128)S(1)}, u32[]{:S(2)}, u32[]{:S(2)}) collective-permute-start(f32[2,512]{1,0:T(2,128)S(1)} %add_add_fusion.1), channel_id=1, source_target_pairs={{0,2},{1,3},{2,4},{3,5},{4,6},{5,7},{6,0},{7,1},{8,10},{9,11},{10,... | collective-permute-start | bytes 12296 | tf_op jit(solution)/shard_map/ppermute | solution.py:247
  94.7 27.4 %collective-permute-start.3 = (f32[2,512]{1,0:T(2,128)S(1)}, f32[2,512]{1,0:T(2,128)S(1)}, u32[]{:S(2)}, u32[]{:S(2)}) collective-permute-start(f32[2,512]{1,0:T(2,128)S(1)} %add_add_fusion.1), channel_id=1, source_target_pairs={{0,1},{1,2},{2,3},{3,4},{4,5},{5,6},{6,7},{7,0},{8,9},{9,10},{10,1... | collective-permute-start | bytes 12296 | tf_op jit(solution)/shard_map/ppermute | solution.py:247
  122.3 7.2 %collective-permute-start.10 = (f32[8,16,256]{2,1,0:T(8,128)S(1)}, f32[8,16,256]{2,1,0:T(8,128)S(1)}, u32[]{:S(2)}, u32[]{:S(2)}) collective-permute-start(f32[8,16,256]{2,1,0:T(8,128)S(1)} %get-tuple-element.12), channel_id=1, source_target_pairs={{0,8},{8,16},{16,24},{24,0},{1,9},{9,17},{17,25},{25,1},{2,10},{10... | collective-permute-start | bytes 393224 | tf_op jit(solution)/shard_map/ppermute | solution.py:247
  123.3 7.9 %collective-permute-start.12 = (f32[8,16,256]{2,1,0:T(8,128)S(1)}, f32[8,16,256]{2,1,0:T(8,128)S(1)}, u32[]{:S(2)}, u32[]{:S(2)}) collective-permute-start(f32[8,16,256]{2,1,0:T(8,128)S(1)} %get-tuple-element.13), channel_id=1, source_target_pairs={{0,24},{8,0},{16,8},{24,16},{1,25},{9,1},{17,9},{25,17},{2,26},{10... | collective-permute-start | bytes 393224 | tf_op jit(solution)/shard_map/ppermute | solution.py:247
  125.2 6.7 %collective-permute-start.11 = (f32[8,16,256]{2,1,0:T(8,128)S(1)}, f32[8,16,256]{2,1,0:T(8,128)S(1)}, u32[]{:S(2)}, u32[]{:S(2)}) collective-permute-start(f32[8,16,256]{2,1,0:T(8,128)S(1)} %get-tuple-element.14), channel_id=1, source_target_pairs={{0,16},{8,24},{16,0},{24,8},{1,17},{9,25},{17,1},{25,9},{2,18},{10... | collective-permute-start | bytes 393224 | tf_op jit(solution)/shard_map/ppermute | solution.py:247
  132.0 6.3 %collective-permute-start.13 = (f32[16,256]{1,0:T(8,128)S(1)}, f32[16,256]{1,0:T(8,128)S(1)}, u32[]{:S(2)}, u32[]{:S(2)}) collective-permute-start(f32[16,256]{1,0:T(8,128)S(1)} %get-tuple-element.15), channel_id=1, source_target_pairs={{0,1},{1,2},{2,3},{3,4},{4,5},{5,6},{6,7},{7,0},{8,9},{9,10},{10,1... | collective-permute-start | bytes 49160 | tf_op jit(solution)/shard_map/ppermute | solution.py:247
  132.1 6.3 %collective-permute-start.19 = (f32[16,256]{1,0:T(8,128)S(1)}, f32[16,256]{1,0:T(8,128)S(1)}, u32[]{:S(2)}, u32[]{:S(2)}) collective-permute-start(f32[16,256]{1,0:T(8,128)S(1)} %get-tuple-element.16), channel_id=1, source_target_pairs={{0,7},{1,0},{2,1},{3,2},{4,3},{5,4},{6,5},{7,6},{8,15},{9,8},{10,9... | collective-permute-start | bytes 49160 | tf_op jit(solution)/shard_map/ppermute | solution.py:247
  135.7 15.7 %collective-permute-start.18 = (f32[16,256]{1,0:T(8,128)S(1)}, f32[16,256]{1,0:T(8,128)S(1)}, u32[]{:S(2)}, u32[]{:S(2)}) collective-permute-start(f32[16,256]{1,0:T(8,128)S(1)} %get-tuple-element.17), channel_id=1, source_target_pairs={{0,6},{1,7},{2,0},{3,1},{4,2},{5,3},{6,4},{7,5},{8,14},{9,15},{10,... | collective-permute-start | bytes 49160 | tf_op jit(solution)/shard_map/ppermute | solution.py:247
  135.7 15.6 %collective-permute-start.17 = (f32[16,256]{1,0:T(8,128)S(1)}, f32[16,256]{1,0:T(8,128)S(1)}, u32[]{:S(2)}, u32[]{:S(2)}) collective-permute-start(f32[16,256]{1,0:T(8,128)S(1)} %get-tuple-element.18), channel_id=1, source_target_pairs={{0,5},{1,6},{2,7},{3,0},{4,1},{5,2},{6,3},{7,4},{8,13},{9,14},{10,... | collective-permute-start | bytes 49160 | tf_op jit(solution)/shard_map/ppermute | solution.py:247
  135.8 15.5 %collective-permute-start.16 = (f32[16,256]{1,0:T(8,128)S(1)}, f32[16,256]{1,0:T(8,128)S(1)}, u32[]{:S(2)}, u32[]{:S(2)}) collective-permute-start(f32[16,256]{1,0:T(8,128)S(1)} %get-tuple-element.19), channel_id=1, source_target_pairs={{0,4},{1,5},{2,6},{3,7},{4,0},{5,1},{6,2},{7,3},{8,12},{9,13},{10,... | collective-permute-start | bytes 49160 | tf_op jit(solution)/shard_map/ppermute | solution.py:247
  138.4 13.0 %collective-permute-start.15 = (f32[16,256]{1,0:T(8,128)S(1)}, f32[16,256]{1,0:T(8,128)S(1)}, u32[]{:S(2)}, u32[]{:S(2)}) collective-permute-start(f32[16,256]{1,0:T(8,128)S(1)} %get-tuple-element.20), channel_id=1, source_target_pairs={{0,3},{1,4},{2,5},{3,6},{4,7},{5,0},{6,1},{7,2},{8,11},{9,12},{10,... | collective-permute-start | bytes 49160 | tf_op jit(solution)/shard_map/ppermute | solution.py:247
  138.4 13.0 %collective-permute-start.14 = (f32[16,256]{1,0:T(8,128)S(1)}, f32[16,256]{1,0:T(8,128)S(1)}, u32[]{:S(2)}, u32[]{:S(2)}) collective-permute-start(f32[16,256]{1,0:T(8,128)S(1)} %get-tuple-element.21), channel_id=1, source_target_pairs={{0,2},{1,3},{2,4},{3,5},{4,6},{5,7},{6,0},{7,1},{8,10},{9,11},{10,... | collective-permute-start | bytes 49160 | tf_op jit(solution)/shard_map/ppermute | solution.py:247
  151.4 4.2 %collective-permute-start.22 = (f32[16,256]{1,0:T(8,128)S(1)}, f32[16,256]{1,0:T(8,128)S(1)}, u32[]{:S(2)}, u32[]{:S(2)}) collective-permute-start(f32[16,256]{1,0:T(8,128)S(1)} %fusion.10), channel_id=1, source_target_pairs={{0,24},{8,0},{16,8},{24,16},{1,25},{9,1},{17,9},{25,17},{2,26},{10... | collective-permute-start | bytes 49160 | tf_op jit(solution)/shard_map/ppermute | solution.py:247
  154.2 3.8 %collective-permute-start.21 = (f32[16,256]{1,0:T(8,128)S(1)}, f32[16,256]{1,0:T(8,128)S(1)}, u32[]{:S(2)}, u32[]{:S(2)}) collective-permute-start(f32[16,256]{1,0:T(8,128)S(1)} %fusion.10), channel_id=1, source_target_pairs={{0,16},{8,24},{16,0},{24,8},{1,17},{9,25},{17,1},{25,9},{2,18},{10... | collective-permute-start | bytes 49160 | tf_op jit(solution)/shard_map/ppermute | solution.py:247
  155.0 4.6 %collective-permute-start.20 = (f32[16,256]{1,0:T(8,128)S(1)}, f32[16,256]{1,0:T(8,128)S(1)}, u32[]{:S(2)}, u32[]{:S(2)}) collective-permute-start(f32[16,256]{1,0:T(8,128)S(1)} %fusion.10), channel_id=1, source_target_pairs={{0,8},{8,16},{16,24},{24,0},{1,9},{9,17},{17,25},{25,1},{2,10},{10... | collective-permute-start | bytes 49160 | tf_op jit(solution)/shard_map/ppermute | solution.py:247

commit v2 on v1

--- a/solution.py
+++ b/solution.py
@@ -13,7 +13,8 @@
 SIN_FLOOR = 0.09
 LOG2E = math.log2(math.e)
 ALL = ("rep", "grp")
-VMEM_BYTES = 50 * 1024 * 1024
+VMEM_BYTES = 28 * 1024 * 1024
+GROUPS = 4
 
 NT = (((1,), (1,)), ((), ()))
 
@@ -180,91 +181,81 @@
     )(base, emb, labels.reshape(1, batch), stats, totals.reshape(1, batch), weights)
 
 
-def refresh_kernel(slot_ref, rows_ref, w_ref, o_ref, stage_ref, held_ref):
-    step = pl.program_id(0)
-    parts = pl.num_programs(0) // 2
-    tile = rows_ref.shape[0]
-
-    @pl.when(step < parts)
-    def _():
-        unit, _ = unit_rows(rows_ref[...].astype(jnp.float32))
-        stage_ref[0] = unit[:, :128]
-        stage_ref[1] = unit[:, 128:]
-        first = step * tile
-
-        def place(j, carry):
-            for u in range(16):
-                row = j * 16 + u
+def place_kernel(*refs, sources, started):
+    me_ref, slot_ref = refs[:2]
+    rows = refs[2 : 2 + len(sources)]
+    held_ref, stage_ref = refs[-2:]
+    run = rows[0].shape[0]
+    for u, (k, row_ref) in enumerate(zip(sources, rows)):
+        unit, _ = unit_rows(row_ref[...].astype(jnp.float32))
+        stage_ref[pl.ds(u * 2 * run, run, stride=2), :] = unit[:, :128]
+        stage_ref[pl.ds(u * 2 * run + 1, run, stride=2), :] = unit[:, 128:]
+        first = (me_ref[0] ^ k) * run
+
+        def place(j, carry, u=u, first=first):
+            for v in range(16):
+                row = j * 16 + v
                 slot = slot_ref[first + row]
-                held_ref[0, pl.ds(slot, 1), :] = stage_ref[0, pl.ds(row, 1), :]
-                held_ref[1, pl.ds(slot, 1), :] = stage_ref[1, pl.ds(row, 1), :]
+                held_ref[pl.ds(slot * 2, 2), :] = stage_ref[pl.ds((u * run + row) * 2, 2), :]
             return carry
 
-        lax.fori_loop(0, tile // 16, place, 0)
-
-    @pl.when(step >= parts)
-    def _():
-        wwide, _ = unit_rows(w_ref[...].astype(jnp.float32))
-        at = pl.ds(pl.multiple_of((step - parts) * tile, tile), tile)
-        low = wwide[:, :128] + held_ref[0, at, :]
-        high = wwide[:, 128:] + held_ref[1, at, :]
-        square = jnp.sum(low * low + high * high, axis=1, keepdims=True)
-        inv = lax.rsqrt(square + 1e-06)
-        o_ref[:, :128] = (low * inv).astype(jnp.bfloat16)
-        o_ref[:, 128:] = (high * inv).astype(jnp.bfloat16)
-
-
-def refresh(slots, rows, weights):
+        lax.fori_loop(0, run // 16, place, 0)
+
+
+def place_rows(me, slots, rows, sources, held, classes):
+    run, width = rows[0].shape
+    smem = pl.BlockSpec(memory_space=pltpu.SMEM)
+    vmem = pl.BlockSpec(memory_space=pltpu.VMEM)
+    started = held is not None
+    operands = [me, slots, *rows] + ([held] if started else [])
+    return pl.pallas_call(
+        functools.partial(place_kernel, sources=tuple(sources), started=started),
+        in_specs=[smem, smem] + [vmem] * (len(operands) - 2),
+        out_specs=vmem,
+        out_shape=jax.ShapeDtypeStruct((2 * classes, 128), jnp.float32),
+        input_output_aliases={len(operands) - 1: 0} if started else {},
+        scratch_shapes=[pltpu.VMEM((2 * run * len(sources), 128), jnp.float32)],
+        compiler_params=pltpu.CompilerParams(vmem_limit_bytes=VMEM_BYTES),
+        cost_estimate=pl.CostEstimate(
+            flops=10 * len(sources) * run * width,
+            bytes_accessed=16 * len(sources) * run * width,
+            transcendentals=0,
+        ),
+        name="place_rows",
+    )(*operands)
+
+
+def blend_kernel(w_ref, held_ref, o_ref):
+    wwide, _ = unit_rows(w_ref[...].astype(jnp.float32))
+    tile = w_ref.shape[0]
+    low = wwide[:, :128] + held_ref[pl.ds(0, tile, stride=2), :]
+    high = wwide[:, 128:] + held_ref[pl.ds(1, tile, stride=2), :]
+    square = jnp.sum(low * low + high * high, axis=1, keepdims=True)
+    inv = lax.rsqrt(square + 1e-06)
+    o_ref[:, :128] = (low * inv).astype(jnp.bfloat16)
+    o_ref[:, 128:] = (high * inv).astype(jnp.bfloat16)
+
+
+def blend(weights, held):
     classes, width = weights.shape
     tile = math.gcd(classes, 1024)
-    parts = classes // tile
     return pl.pallas_call(
-        refresh_kernel,
-        grid=(2 * parts,),
+        blend_kernel,
+        grid=(classes // tile,),
         in_specs=[
-            pl.BlockSpec(memory_space=pltpu.SMEM),
-            pl.BlockSpec((tile, width), lambda i: (jnp.minimum(i, parts - 1), 0)),
-            pl.BlockSpec((tile, width), lambda i: (jnp.maximum(i - parts, 0), 0)),
-        ],
-        out_specs=pl.BlockSpec((tile, width), lambda i: (jnp.maximum(i - parts, 0), 0)),
+            pl.BlockSpec((tile, width), lambda i: (i, 0)),
+            pl.BlockSpec((2 * tile, 128), lambda i: (i, 0)),
+        ],
+        out_specs=pl.BlockSpec((tile, width), lambda i: (i, 0)),
         out_shape=jax.ShapeDtypeStruct((classes, width), jnp.bfloat16),
-        scratch_shapes=[
-            pltpu.VMEM((2, tile, 128), jnp.float32),
-            pltpu.VMEM((2, classes, 128), jnp.float32),
-        ],
         compiler_params=pltpu.CompilerParams(
             dimension_semantics=("arbitrary",), vmem_limit_bytes=VMEM_BYTES
         ),
         cost_estimate=pl.CostEstimate(
-            flops=10 * classes * width, bytes_accessed=classes * width * 6, transcendentals=classes
-        ),
-        name="refresh",
-    )(slots, rows, weights)
-
-
-def shifted(value, axis, shift):
-    size = lax.axis_size(axis)
-    return lax.ppermute(value, axis, [(i, (i + shift) % size) for i in range(size)])
-
-
-def sum_over(value, axis):
-    return sum((shifted(value, axis, s) for s in range(1, lax.axis_size(axis))), value)
-
-
-def scatter_sum(blocks, axis):
-    size, me = lax.axis_size(axis), lax.axis_index(axis)
-    total = lax.dynamic_index_in_dim(blocks, me, 0, keepdims=False)
-    for s in range(1, size):
-        total = total + shifted(
-            lax.dynamic_index_in_dim(blocks, (me + s) % size, 0, keepdims=False), axis, s
-        )
-    return total
-
-
-def gather_blocks(block, axis):
-    size, me = lax.axis_size(axis), lax.axis_index(axis)
-    stack = jnp.stack([block] + [shifted(block, axis, s) for s in range(1, size)])
-    return stack[(me - jnp.arange(size)) % size]
+            flops=10 * classes * width, bytes_accessed=classes * width * 8, transcendentals=classes
+        ),
+        name="blend",
+    )(weights, held)
 
 
 def shards(embeddings, labels, class_weights, centroids, centroid_class):
@@ -291,19 +282,36 @@
     emb = head[:, :share].reshape(batch, width)
     digits = head[:, share:].reshape(peers, digit_rows * width).astype(jnp.int32)
     slots_got = (digits[:, :per_peer] * 128 + digits[:, per_peer : 2 * per_peer]).reshape(-1)
-    rows_got = lax.all_to_all(centroids.reshape(peers, per_peer, width), ALL, 0, 0, tiled=True)
+    me = (rep * groups + grp).astype(jnp.int32)
+    crossing, near = list(range(peers // 2, peers)), list(range(1, peers // 2))
+    order = [k for pair in zip(crossing, near + [0]) for k in pair]
+    at = lambda d: d % groups * reps + d // groups
+    runs = {}
+    for k in order:
+        run = lax.dynamic_slice_in_dim(centroids, (me ^ k) * per_peer, per_peer, 0)
+        pairs = [(at(d), at(d ^ k)) for d in range(peers)]
+        runs[k] = lax.ppermute(run, ("grp", "rep"), pairs) if k else run
 
     a, b, stats = forward(base, emb, labels, class_weights)
-    totals = sum_over(sum_over(stats[:2], "grp"), "rep")
+    sums = jnp.broadcast_to(stats[:2].reshape(1, -1, 128), (peers, 2 * batch // 128, 128))
+    sums = lax.all_to_all(sums, ALL, 0, 0, tiled=True)
+    totals = jnp.sum(sums, axis=0).reshape(2, batch)
     total, target = totals[0], totals[1]
     weight_grad = weight_gradient(base, emb, labels, stats, total, class_weights)
     loss = lax.dynamic_slice_in_dim(SCALE + jnp.log(total) - target, rep * rows_local, rows_local, 0)
     grad = a / total[:, None] - b
-    blocks = grad.reshape(reps, groups, share, width).transpose(1, 0, 2, 3)
-    own = scatter_sum(scatter_sum(blocks, "grp"), "rep")
-    embedding_gradient = gather_blocks(own, "grp").reshape(rows_local, width)
-    refreshed = refresh(slots_got, rows_got.reshape(classes, width), class_weights)
-    return (loss, embedding_gradient, weight_grad, refreshed)
+    parts = lax.all_to_all(grad.reshape(peers, share, width), ALL, 0, 0, tiled=True)
+    own = jnp.sum(parts, axis=0)
+    embedding_gradient = lax.all_to_all(
+        jnp.broadcast_to(own[None], (groups, share, width)), "grp", 0, 0, tiled=True
+    ).reshape(rows_local, width)
+
+    held = None
+    step = max(1, peers // GROUPS)
+    for first in range(0, peers, step):
+        sources = order[first : first + step]
+        held = place_rows(me.reshape(1), slots_got, [runs[k] for k in sources], sources, held, classes)
+    return (loss, embedding_gradient, weight_grad, blend(class_weights, held))
 
 
 def solution(mesh):

time: 183 us -> 188 us (1.027)
  starting transfers between devices: 57 us -> 84.6 us
  blocking collectives: 20.7 us -> 0 us
  waiting for transfers between devices: 54.2 us -> 37.4 us
  local copies, waits for them, and re-layouts: 2.07 us -> 11.9 us
  other arithmetic: 1.36 us -> 4.85 us
    ppermute x23 -> x31, waiting for transfers between devices: 54.2 us -> 24.5 us  [shards(): runs[k] = lax.ppermute(run, ('grp', 'rep'), pairs) if k else run]
    all_to_all x1 -> x0, blocking collectives: 20.7 us -> none  [shards(): head = lax.all_to_all(head, ALL, 0, 0, tiled=True)]
    all_to_all x1 -> x4, starting transfers between devices: 3.71 us -> 17.9 us  [the longest x1 7.3 us: shards(): head = lax.all_to_all(head, ALL, 0, 0, tiled=True)]
    ppermute x23 -> x31, starting transfers between devices: 53.3 us -> 66.7 us  [shards(): runs[k] = lax.ppermute(run, ('grp', 'rep'), pairs) if k else run]
    all_to_all x1 -> x4, waiting for transfers between devices: 0.01 us -> 12.9 us  [the longest x1 8.66 us: shards(): head = lax.all_to_all(head, ALL, 0, 0, tiled=True)]
    dynamic_slice x0 -> x2, local copies, waits for them, and re-layouts: none -> 5.49 us  [shards(): run = lax.dynamic_slice_in_dim(centroids, (me ^ k) * per_peer, per_peer, 0)]
    pallas_call x1 -> x5, Pallas kernels: 21.9 us -> 26.1 us  [the longest x4 21 us: place_rows(): pl.pallas_call(functools.partial(place_kernel, sources=tuple(sources), st...]
    unnamed x6 -> x13, local copies, waits for them, and re-layouts: 0.04 us -> 3.59 us
  transfers between devices with their start and end apart: 24 -> 35, of which waited for: 9 -> 9; matrix products, arithmetic and copies ran while one was open for 1% -> 5% of each run, Pallas kernels for 13% -> 25%
where the time goes in v2:
time: 188 us; the launch traced here: 187 us
  starting transfers between devices  84.6 us (45%)
  Pallas kernels  47.2 us (25%)
  waiting for transfers between devices  37.4 us (20%)
  local copies, waits for them, and re-layouts  11.9 us (6%)
  other arithmetic  4.85 us (3%)
    ppermute x31, starting transfers between devices, shards(): runs[k] = lax.ppermute(run, ('grp', 'rep'), pairs) if k else run  66.7 us
    ppermute x31, waiting for transfers between devices, shards(): runs[k] = lax.ppermute(run, ('grp', 'rep'), pairs) if k else run  24.5 us
    pallas_call x4, Pallas kernels, place_rows(): pl.pallas_call(functools.partial(place_kernel, sources=tuple(sources), st...  21 us
    pallas_call x1, Pallas kernels, forward(): pl.pallas_call(functools.partial(forward_kernel, classes=classes), grid=(...  11.6 us
    pallas_call x1, Pallas kernels, weight_gradient(): pl.pallas_call(weight_kernel, grid=(classes // tile,), in_specs=[pl.Block...  9.49 us
    all_to_all x1, waiting for transfers between devices, shards(): head = lax.all_to_all(head, ALL, 0, 0, tiled=True)  8.66 us
    all_to_all x1, starting transfers between devices, shards(): head = lax.all_to_all(head, ALL, 0, 0, tiled=True)  7.3 us
    dynamic_slice x2, local copies, waits for them, and re-layouts, shards(): run = lax.dynamic_slice_in_dim(centroids, (me ^ k) * per_peer, per_peer, 0)  5.49 us
  transfers between devices with their start and end apart: 35, of which 9 were waited for; matrix products, arithmetic and copies ran while one was open for 5% of the time, Pallas kernels for 25%

profile of v2, /device:TPU:0, one launch (start us, length us, event | category | flops | bytes accessed | tf_op | source)
XLA Modules:
  0.0 186.9 jit_solution(5727598379088373120)
XLA Ops:
  0.6 0.0 copy-start
  0.7 0.9 fusion.2
  1.6 0.1 fusion
  1.7 0.8 pad_maximum_fusion
  2.5 7.3 %all-to-all-start = ((bf16[32,18,256]{2,1,0:T(8,128)(2,1)}), bf16[32,18,256]{2,1,0:T(8,128)(2,1)S(1)}, u32[]{:S(2)}, u32[]{:S(2)}) async-start(bf16[32,18,256]{2,1,0:T(8,128)(2,1)} %pad_maximum_fusion), calls=%async_computation | async-start | bytes 786432 | tf_op jit(solution)/shard_map/all_to_all | solution.py:281
  9.9 2.4 %constant_dynamic-slice_fusion.1 = (bf16[256,256]{1,0:T(8,128)(2,1)S(1)}, bf16[256,256]{1,0:T(8,128)(2,1)S(1)}, bf16[256,256]{1,0:T(8,128)(2,1)S(1)}, bf16[256,2...) fusion(bf16[8192,256]{1,0:T(8,128)(2,1)} %param.8, ...), kind=kLoop, calls=%fused_computation.14 | loop fusion | bytes 3670072 | tf_op jit(solution)/shard_map/dynamic_slice | solution.py:291
  12.4 4.5 %collective-permute-start.29 = (bf16[256,256]{1,0:T(8,128)(2,1)S(1)}, bf16[256,256]{1,0:T(8,128)(2,1)S(1)}, u32[]{:S(2)}, u32[]{:S(2)}) collective-permute-start(bf16[256,256]{1,0:T(8,128)(2,1)S(1)} %get-tuple-element.30), channel_id=1, source_target_pairs={{0,28},{8,20},{16,12},{24,4},{1,29},{9,21},{17,13},{25,5},{2,30},{... | collective-permute-start | bytes 393224 | tf_op jit(solution)/shard_map/ppermute | solution.py:293
  16.9 0.8 copy.13.lab_ref
  17.7 8.7 %all-to-all-done = bf16[32,18,256]{2,1,0:T(8,128)(2,1)S(1)} async-done(((bf16[32,18,256]{2,1,0:T(8,128)(2,1)}), bf16[32,18,256]{2,1,0:T(8,128)(2,1)S(1)}, u32[]{:S(2)}, u32[]{:S(2)}) %all-to-all-start) | async-done | bytes 294944 | tf_op jit(solution)/shard_map/all_to_all | solution.py:281
  26.4 0.7 copy-done.4
  27.1 2.2 %copy-done.1 = bf16[8192,256]{1,0:T(8,128)(2,1)S(1)} copy-done((bf16[8192,256]{1,0:T(8,128)(2,1)S(1)}, bf16[8192,256]{1,0:T(8,128)(2,1)}, u32[]{:S(2)}) %copy-start.1) | copy-done | bytes 4194328
  29.3 11.6 %forward_sums.1 = (f32[512,256]{1,0:T(8,128)S(1)}, f32[512,256]{1,0:T(8,128)S(1)}, f32[8,512]{1,0:T(8,128)S(1)}) custom-call(s32[1]{0:T(128)} %bitcast.base_ref, bf16[512,256]{1,0:T(8,128)(2,1)S(1)} %bitcast.23, s32[512,1]{1,0:T(8,128)S(1)} %copy.13.lab_ref, bf16[8192,256]{1,0:T(8,128)(2,1)S(1)} %copy-done.1), custom_call_target="tpu_custom_call" | custom-call | flops 6442450944 | bytes 4194304 | tf_op jit(solution)/shard_map/forward_sums/pallas_call | solution.py:92
  40.9 0.7 broadcast_in_dim.10
  41.6 2.6 %all-to-all-start.1 = ((f32[32,8,128]{2,1,0:T(8,128)}), f32[32,8,128]{2,1,0:T(8,128)S(1)}, u32[]{:S(2)}, u32[]{:S(2)}) async-start(f32[32,8,128]{2,1,0:T(8,128)} %broadcast_in_dim.10), calls=%async_computation.1 | async-start | bytes 262144 | tf_op jit(solution)/shard_map/all_to_all | solution.py:297
  44.1 4.6 %collective-permute-start.11 = (bf16[256,256]{1,0:T(8,128)(2,1)S(1)}, bf16[256,256]{1,0:T(8,128)(2,1)S(1)}, u32[]{:S(2)}, u32[]{:S(2)}) collective-permute-start(bf16[256,256]{1,0:T(8,128)(2,1)S(1)} %get-tuple-element.31), channel_id=1, source_target_pairs={{0,22},{8,30},{16,6},{24,14},{1,23},{9,31},{17,7},{25,15},{2,20},{... | collective-permute-start | bytes 393224 | tf_op jit(solution)/shard_map/ppermute | solution.py:293
  48.8 1.9 %collective-permute-start.9 = (bf16[256,256]{1,0:T(8,128)(2,1)S(1)}, bf16[256,256]{1,0:T(8,128)(2,1)S(1)}, u32[]{:S(2)}, u32[]{:S(2)}) collective-permute-start(bf16[256,256]{1,0:T(8,128)(2,1)S(1)} %get-tuple-element.33), channel_id=1, source_target_pairs={{0,14},{8,6},{16,30},{24,22},{1,15},{9,7},{17,31},{25,23},{2,12},{... | collective-permute-start | bytes 393224 | tf_op jit(solution)/shard_map/ppermute | solution.py:293
  50.6 1.0 collective-permute-start.8
  51.7 2.9 %collective-permute-start.7 = (bf16[256,256]{1,0:T(8,128)(2,1)S(1)}, bf16[256,256]{1,0:T(8,128)(2,1)S(1)}, u32[]{:S(2)}, u32[]{:S(2)}) collective-permute-start(bf16[256,256]{1,0:T(8,128)(2,1)S(1)} %get-tuple-element.35), channel_id=1, source_target_pairs={{0,6},{8,14},{16,22},{24,30},{1,7},{9,15},{17,23},{25,31},{2,4},{1... | collective-permute-start | bytes 393224 | tf_op jit(solution)/shard_map/ppermute | solution.py:293
  54.6 3.0 %constant_dynamic-slice_fusion = (bf16[256,256]{1,0:T(8,128)(2,1)}, bf16[256,256]{1,0:T(8,128)(2,1)S(1)}, bf16[256,256]{1,0:T(8,128)(2,1)}, bf16[256,256]{1,0:T(...) fusion(bf16[8192,256]{1,0:T(8,128)(2,1)} %param.8, ...), kind=kLoop, calls=%fused_computation.13 | loop fusion | bytes 4718664 | tf_op jit(solution)/shard_map/dynamic_slice | solution.py:291
  57.7 0.6 collective-permute-start.6
  58.3 3.4 %collective-permute-start.5 = (bf16[256,256]{1,0:T(8,128)(2,1)S(1)}, bf16[256,256]{1,0:T(8,128)(2,1)S(1)}, u32[]{:S(2)}, u32[]{:S(2)}) collective-permute-start(bf16[256,256]{1,0:T(8,128)(2,1)S(1)} %get-tuple-element.38), channel_id=1, source_target_pairs={{0,27},{8,19},{16,11},{24,3},{1,26},{9,18},{17,10},{25,2},{2,25},{... | collective-permute-start | bytes 393224 | tf_op jit(solution)/shard_map/ppermute | solution.py:293
  61.7 0.5 collective-permute-start.30
  62.2 1.0 collective-permute-done.8.refs_3_
  63.2 1.5 collective-permute-start.28
  64.7 1.7 collective-permute-done.7.refs_2_
  66.4 6.3 %collective-permute-start.27 = (bf16[256,256]{1,0:T(8,128)(2,1)}, bf16[256,256]{1,0:T(8,128)(2,1)S(1)}, u32[]{:S(2)}, u32[]{:S(2)}) collective-permute-start(bf16[256,256]{1,0:T(8,128)(2,1)} %get-tuple-element.14), channel_id=1, source_target_pairs={{0,20},{8,28},{16,4},{24,12},{1,21},{9,29},{17,5},{25,13},{2,22},{... | collective-permute-start | bytes 393224 | tf_op jit(solution)/shard_map/ppermute | solution.py:293
  72.7 0.1 collective-permute-start.26
  72.8 5.8 %collective-permute-start.25 = (bf16[256,256]{1,0:T(8,128)(2,1)}, bf16[256,256]{1,0:T(8,128)(2,1)S(1)}, u32[]{:S(2)}, u32[]{:S(2)}) collective-permute-start(bf16[256,256]{1,0:T(8,128)(2,1)} %get-tuple-element.16), channel_id=1, source_target_pairs={{0,12},{8,4},{16,28},{24,20},{1,13},{9,5},{17,29},{25,21},{2,14},{... | collective-permute-start | bytes 393224 | tf_op jit(solution)/shard_map/ppermute | solution.py:293
  78.6 2.2 %collective-permute-start.24 = (bf16[256,256]{1,0:T(8,128)(2,1)}, bf16[256,256]{1,0:T(8,128)(2,1)S(1)}, u32[]{:S(2)}, u32[]{:S(2)}) collective-permute-start(bf16[256,256]{1,0:T(8,128)(2,1)} %get-tuple-element.17), channel_id=1, source_target_pairs={{0,8},{8,0},{16,24},{24,16},{1,9},{9,1},{17,25},{25,17},{2,10},{10... | collective-permute-start | bytes 393224 | tf_op jit(solution)/shard_map/ppermute | solution.py:293
  80.8 0.4 collective-permute-done.27.refs_6_
  81.2 1.3 collective-permute-start.22
  82.5 1.0 divide_subtract_fusion
  83.5 4.7 %all-to-all-start.2 = ((f32[32,16,256]{2,1,0:T(8,128)}), f32[32,16,256]{2,1,0:T(8,128)}, u32[]{:S(2)}, u32[]{:S(2)}) async-start(f32[32,16,256]{2,1,0:T(8,128)} %bitcast.28), calls=%async_computation.2 | async-start | bytes 1048576 | tf_op jit(solution)/shard_map/all_to_all | solution.py:303
  88.3 4.1 %collective-permute-start.21 = (bf16[256,256]{1,0:T(8,128)(2,1)}, bf16[256,256]{1,0:T(8,128)(2,1)S(1)}, u32[]{:S(2)}, u32[]{:S(2)}) collective-permute-start(bf16[256,256]{1,0:T(8,128)(2,1)} %get-tuple-element.20), channel_id=1, source_target_pairs={{0,29},{8,21},{16,13},{24,5},{1,28},{9,20},{17,12},{25,4},{2,31},{... | collective-permute-start | bytes 393224 | tf_op jit(solution)/shard_map/ppermute | solution.py:293
  92.3 0.5 collective-permute-start.20
  92.8 1.2 collective-permute-start.19
  94.1 0.5 collective-permute-start.18
  94.5 3.1 %collective-permute-start.17 = (bf16[256,256]{1,0:T(8,128)(2,1)}, bf16[256,256]{1,0:T(8,128)(2,1)S(1)}, u32[]{:S(2)}, u32[]{:S(2)}) collective-permute-start(bf16[256,256]{1,0:T(8,128)(2,1)} %get-tuple-element.24), channel_id=1, source_target_pairs={{0,13},{8,5},{16,29},{24,21},{1,12},{9,4},{17,28},{25,20},{2,15},{... | collective-permute-start | bytes 393224 | tf_op jit(solution)/shard_map/ppermute | solution.py:293
  97.6 17.9 %collective-permute-done.21.refs_8_ = bf16[256,256]{1,0:T(8,128)(2,1)S(1)} collective-permute-done((bf16[256,256]{1,0:T(8,128)(2,1)}, bf16[256,256]{1,0:T(8,128)(2,1)S(1)}, u32[]{:S(2)}, u32[]{:S(2)}) %collective-permute-start.21) | collective-permute-done | bytes 131104 | tf_op jit(solution)/shard_map/ppermute | solution.py:293
  115.5 2.2 %collective-permute-start.16 = (bf16[256,256]{1,0:T(8,128)(2,1)}, bf16[256,256]{1,0:T(8,128)(2,1)S(1)}, u32[]{:S(2)}, u32[]{:S(2)}) collective-permute-start(bf16[256,256]{1,0:T(8,128)(2,1)} %get-tuple-element.25), channel_id=1, source_target_pairs={{0,9},{8,1},{16,25},{24,17},{1,8},{9,0},{17,24},{25,16},{2,11},{10... | collective-permute-start | bytes 393224 | tf_op jit(solution)/shard_map/ppermute | solution.py:293
  117.7 1.0 collective-permute-done.19.refs_6_
  118.7 0.6 collective-permute-start.14
  119.3 2.6 %collective-permute-start.13 = (bf16[256,256]{1,0:T(8,128)(2,1)}, bf16[256,256]{1,0:T(8,128)(2,1)S(1)}, u32[]{:S(2)}, u32[]{:S(2)}) collective-permute-start(bf16[256,256]{1,0:T(8,128)(2,1)} %get-tuple-element.28), channel_id=1, source_target_pairs={{0,30},{8,22},{16,14},{24,6},{1,31},{9,23},{17,15},{25,7},{2,28},{... | collective-permute-start | bytes 393224 | tf_op jit(solution)/shard_map/ppermute | solution.py:293
  121.9 1.4 collective-permute-done.17.refs_4_
  123.3 1.1 collective-permute-start.12
  124.4 0.9 slice_convert_fusion
  125.3 2.3 %collective-permute-start.4 = (bf16[256,256]{1,0:T(8,128)(2,1)}, bf16[256,256]{1,0:T(8,128)(2,1)S(1)}, u32[]{:S(2)}, u32[]{:S(2)}) collective-permute-start(bf16[256,256]{1,0:T(8,128)(2,1)} %get-tuple-element.39), channel_id=1, source_target_pairs={{0,23},{8,31},{16,7},{24,15},{1,22},{9,30},{17,6},{25,14},{2,21},{... | collective-permute-start | bytes 393224 | tf_op jit(solution)/shard_map/ppermute | solution.py:293
  127.6 2.4 %collective-permute-start.3 = (bf16[256,256]{1,0:T(8,128)(2,1)}, bf16[256,256]{1,0:T(8,128)(2,1)S(1)}, u32[]{:S(2)}, u32[]{:S(2)}) collective-permute-start(bf16[256,256]{1,0:T(8,128)(2,1)} %get-tuple-element.40), channel_id=1, source_target_pairs={{0,19},{8,27},{16,3},{24,11},{1,18},{9,26},{17,2},{25,10},{2,17},{... | collective-permute-start | bytes 393224 | tf_op jit(solution)/shard_map/ppermute | solution.py:293
  130.0 2.6 %collective-permute-start.2 = (bf16[256,256]{1,0:T(8,128)(2,1)}, bf16[256,256]{1,0:T(8,128)(2,1)S(1)}, u32[]{:S(2)}, u32[]{:S(2)}) collective-permute-start(bf16[256,256]{1,0:T(8,128)(2,1)} %get-tuple-element.41), channel_id=1, source_target_pairs={{0,15},{8,7},{16,31},{24,23},{1,14},{9,6},{17,30},{25,22},{2,13},{... | collective-permute-start | bytes 393224 | tf_op jit(solution)/shard_map/ppermute | solution.py:293
  132.6 5.3 %collective-permute-start.1 = (bf16[256,256]{1,0:T(8,128)(2,1)}, bf16[256,256]{1,0:T(8,128)(2,1)S(1)}, u32[]{:S(2)}, u32[]{:S(2)}) collective-permute-start(bf16[256,256]{1,0:T(8,128)(2,1)} %get-tuple-element.42), channel_id=1, source_target_pairs={{0,11},{8,3},{16,27},{24,19},{1,10},{9,2},{17,26},{25,18},{2,9},{1... | collective-permute-start | bytes 393224 | tf_op jit(solution)/shard_map/ppermute | solution.py:293
  137.9 1.0 collective-permute-done.12.refs_7_
  138.9 1.7 collective-permute-start
  140.7 5.2 %place_rows.4.refs_10_ = f32[16384,128]{1,0:T(8,128)S(1)} custom-call(s32[1]{0:T(128)} %bitcast.10.refs_0_, s32[8192]{0:T(1024)S(1)} %bitcast.19, bf16[256,256]{1,0:T(8,128)(2,1)S(1)} %collective-permute-done.23.refs_2_, bf16[256,256]{1,0:T(8,128)(2,1)S(1)} %collective-permute-done.24.refs_3_, bf16[256,256]{1,0:T(8,128)(2,1)S(1)} %collective-permute-done.25.refs_4_, ...), custom_call_target="tpu_custom_call" | custom-call | flops 5242880 | bytes 8388608 | tf_op jit(solution)/shard_map/place_rows/pallas_call | solution.py:211
  146.0 5.3 %place_rows.5.refs_10_ = f32[16384,128]{1,0:T(8,128)S(1)} custom-call(s32[1]{0:T(128)} %bitcast.10.refs_0_, s32[8192]{0:T(1024)S(1)} %bitcast.20, bf16[256,256]{1,0:T(8,128)(2,1)S(1)} %collective-permute-done.15.refs_2_, bf16[256,256]{1,0:T(8,128)(2,1)S(1)} %collective-permute-done.16.refs_3_, ...), custom_call_target="tpu_custom_call", output_to_operand_aliasing={{}: (10, {})} | custom-call | flops 5242880 | bytes 8388608 | tf_op jit(solution)/shard_map/place_rows/pallas_call | solution.py:211
  151.2 5.2 %place_rows.6.refs_10_ = f32[16384,128]{1,0:T(8,128)S(1)} custom-call(s32[1]{0:T(128)} %bitcast.10.refs_0_, s32[8192]{0:T(1024)S(1)} %bitcast.21, bf16[256,256]{1,0:T(8,128)(2,1)S(1)} %collective-permute-done.7.refs_2_, bf16[256,256]{1,0:T(8,128)(2,1)S(1)} %collective-permute-done.8.refs_3_, ...), custom_call_target="tpu_custom_call", output_to_operand_aliasing={{}: (10, {})} | custom-call | flops 5242880 | bytes 8388608 | tf_op jit(solution)/shard_map/place_rows/pallas_call | solution.py:211
  156.5 5.2 %place_rows.7.held_ref = f32[16384,128]{1,0:T(8,128)S(1)} custom-call(s32[1]{0:T(128)} %bitcast.10.refs_0_, s32[8192]{0:T(1024)S(1)} %bitcast.22, bf16[256,256]{1,0:T(8,128)(2,1)S(1)} %collective-permute-done.refs_2_, bf16[256,256]{1,0:T(8,128)(2,1)S(1)} %collective-permute-done.1.refs_3_, ...), custom_call_target="tpu_custom_call", output_to_operand_aliasing={{}: (10, {})} | custom-call | flops 5242880 | bytes 8388608 | tf_op jit(solution)/shard_map/place_rows/pallas_call | solution.py:211
  161.8 5.1 %blend.1 = bf16[8192,256]{1,0:T(8,128)(2,1)} custom-call(bf16[8192,256]{1,0:T(8,128)(2,1)S(1)} %copy-done.2, f32[16384,128]{1,0:T(8,128)S(1)} %place_rows.7.held_ref), custom_call_target="tpu_custom_call" | custom-call | flops 20971520 | bytes 16777216 | tf_op jit(solution)/shard_map/blend/pallas_call | solution.py:242
  166.9 9.5 %weight_gradient.1 = f32[8192,256]{1,0:T(8,128)} custom-call(s32[1]{0:T(128)} %bitcast.base_ref, bf16[512,256]{1,0:T(8,128)(2,1)S(1)} %bitcast.24, s32[1,512]{1,0:T(1,128)S(1)} %bitcast.26, f32[8,512]{1,0:T(8,128)S(1)} %get-tuple-element.7.st_ref, f32[1,512]{1,0:T(1,128)S(1)} %bitcast.27, bf16[8192,256]{1,0:T(8,128)(2,1)S(1)} %copy-done.2), custom_call_target="tpu_custom_call" | custom-call | flops 4294967296 | bytes 12582912 | tf_op jit(solution)/shard_map/weight_gradient/pallas_call | solution.py:154
  176.4 1.1 reduce_sum.19
  177.5 0.6 broadcast_in_dim.22
  178.1 3.3 %all-to-all-start.3 = ((f32[4,16,256]{2,1,0:T(8,128)}), f32[4,16,256]{2,1,0:T(8,128)S(1)}, u32[]{:S(2)}, u32[]{:S(2)}) async-start(f32[4,16,256]{2,1,0:T(8,128)} %broadcast_in_dim.22), calls=%async_computation.3 | async-start | bytes 131072 | tf_op jit(solution)/shard_map/all_to_all | solution.py:305
  181.4 0.6 dynamic_slice.103
  182.0 4.2 %all-to-all-done.3 = f32[4,16,256]{2,1,0:T(8,128)S(1)} async-done(((f32[4,16,256]{2,1,0:T(8,128)}), f32[4,16,256]{2,1,0:T(8,128)S(1)}, u32[]{:S(2)}, u32[]{:S(2)}) %all-to-all-start.3) | async-done | bytes 65568 | tf_op jit(solution)/shard_map/all_to_all | solution.py:305
  186.2 0.6 copy.20
  (47 shorter events, 0.2 us)
Async XLA Ops:
  0.6 1.0 copy-start
  2.5 23.8 %all-to-all-start = ((bf16[32,18,256]{2,1,0:T(8,128)(2,1)}), bf16[32,18,256]{2,1,0:T(8,128)(2,1)S(1)}, u32[]{:S(2)}, u32[]{:S(2)}) async-start(bf16[32,18,256]{2,1,0:T(8,128)(2,1)} %pad_maximum_fusion), calls=%async_computation | async-start | bytes 786432 | tf_op jit(solution)/shard_map/all_to_all | solution.py:281
  12.4 39.3 %collective-permute-start.29 = (bf16[256,256]{1,0:T(8,128)(2,1)S(1)}, bf16[256,256]{1,0:T(8,128)(2,1)S(1)}, u32[]{:S(2)}, u32[]{:S(2)}) collective-permute-start(bf16[256,256]{1,0:T(8,128)(2,1)S(1)} %get-tuple-element.30), channel_id=1, source_target_pairs={{0,28},{8,20},{16,12},{24,4},{1,29},{9,21},{17,13},{25,5},{2,30},{... | collective-permute-start | bytes 393224 | tf_op jit(solution)/shard_map/ppermute | solution.py:293
  26.4 0.7 copy-start.4
  27.1 2.2 %copy-start.1 = (bf16[8192,256]{1,0:T(8,128)(2,1)S(1)}, bf16[8192,256]{1,0:T(8,128)(2,1)}, u32[]{:S(2)}) copy-start(bf16[8192,256]{1,0:T(8,128)(2,1)} %w_ref.5) | copy-start | bytes 12582916
  41.6 16.1 %all-to-all-start.1 = ((f32[32,8,128]{2,1,0:T(8,128)}), f32[32,8,128]{2,1,0:T(8,128)S(1)}, u32[]{:S(2)}, u32[]{:S(2)}) async-start(f32[32,8,128]{2,1,0:T(8,128)} %broadcast_in_dim.10), calls=%async_computation.1 | async-start | bytes 262144 | tf_op jit(solution)/shard_map/all_to_all | solution.py:297
  44.1 13.5 %collective-permute-start.11 = (bf16[256,256]{1,0:T(8,128)(2,1)S(1)}, bf16[256,256]{1,0:T(8,128)(2,1)S(1)}, u32[]{:S(2)}, u32[]{:S(2)}) collective-permute-start(bf16[256,256]{1,0:T(8,128)(2,1)S(1)} %get-tuple-element.31), channel_id=1, source_target_pairs={{0,22},{8,30},{16,6},{24,14},{1,23},{9,31},{17,7},{25,15},{2,20},{... | collective-permute-start | bytes 393224 | tf_op jit(solution)/shard_map/ppermute | solution.py:293
  48.8 9.6 %collective-permute-start.10 = (bf16[256,256]{1,0:T(8,128)(2,1)S(1)}, bf16[256,256]{1,0:T(8,128)(2,1)S(1)}, u32[]{:S(2)}, u32[]{:S(2)}) collective-permute-start(bf16[256,256]{1,0:T(8,128)(2,1)S(1)} %get-tuple-element.32), channel_id=1, source_target_pairs={{0,18},{8,26},{16,2},{24,10},{1,19},{9,27},{17,3},{25,11},{2,16},{... | collective-permute-start | bytes 393224 | tf_op jit(solution)/shard_map/ppermute | solution.py:293
  48.8 13.0 %collective-permute-start.9 = (bf16[256,256]{1,0:T(8,128)(2,1)S(1)}, bf16[256,256]{1,0:T(8,128)(2,1)S(1)}, u32[]{:S(2)}, u32[]{:S(2)}) collective-permute-start(bf16[256,256]{1,0:T(8,128)(2,1)S(1)} %get-tuple-element.33), channel_id=1, source_target_pairs={{0,14},{8,6},{16,30},{24,22},{1,15},{9,7},{17,31},{25,23},{2,12},{... | collective-permute-start | bytes 393224 | tf_op jit(solution)/shard_map/ppermute | solution.py:293
  50.6 12.6 %collective-permute-start.8 = (bf16[256,256]{1,0:T(8,128)(2,1)S(1)}, bf16[256,256]{1,0:T(8,128)(2,1)S(1)}, u32[]{:S(2)}, u32[]{:S(2)}) collective-permute-start(bf16[256,256]{1,0:T(8,128)(2,1)S(1)} %get-tuple-element.34), channel_id=1, source_target_pairs={{0,10},{8,2},{16,26},{24,18},{1,11},{9,3},{17,27},{25,19},{2,8},{1... | collective-permute-start | bytes 393224 | tf_op jit(solution)/shard_map/ppermute | solution.py:293
  51.7 14.7 %collective-permute-start.7 = (bf16[256,256]{1,0:T(8,128)(2,1)S(1)}, bf16[256,256]{1,0:T(8,128)(2,1)S(1)}, u32[]{:S(2)}, u32[]{:S(2)}) collective-permute-start(bf16[256,256]{1,0:T(8,128)(2,1)S(1)} %get-tuple-element.35), channel_id=1, source_target_pairs={{0,6},{8,14},{16,22},{24,30},{1,7},{9,15},{17,23},{25,31},{2,4},{1... | collective-permute-start | bytes 393224 | tf_op jit(solution)/shard_map/ppermute | solution.py:293
  57.7 15.1 %collective-permute-start.6 = (bf16[256,256]{1,0:T(8,128)(2,1)S(1)}, bf16[256,256]{1,0:T(8,128)(2,1)S(1)}, u32[]{:S(2)}, u32[]{:S(2)}) collective-permute-start(bf16[256,256]{1,0:T(8,128)(2,1)S(1)} %get-tuple-element.37), channel_id=1, source_target_pairs={{0,31},{8,23},{16,15},{24,7},{1,30},{9,22},{17,14},{25,6},{2,29},{... | collective-permute-start | bytes 393224 | tf_op jit(solution)/shard_map/ppermute | solution.py:293
  58.3 14.5 %collective-permute-start.5 = (bf16[256,256]{1,0:T(8,128)(2,1)S(1)}, bf16[256,256]{1,0:T(8,128)(2,1)S(1)}, u32[]{:S(2)}, u32[]{:S(2)}) collective-permute-start(bf16[256,256]{1,0:T(8,128)(2,1)S(1)} %get-tuple-element.38), channel_id=1, source_target_pairs={{0,27},{8,19},{16,11},{24,3},{1,26},{9,18},{17,10},{25,2},{2,25},{... | collective-permute-start | bytes 393224 | tf_op jit(solution)/shard_map/ppermute | solution.py:293
  61.7 16.8 %collective-permute-start.30 = (bf16[256,256]{1,0:T(8,128)(2,1)}, bf16[256,256]{1,0:T(8,128)(2,1)S(1)}, u32[]{:S(2)}, u32[]{:S(2)}) collective-permute-start(bf16[256,256]{1,0:T(8,128)(2,1)} %get-tuple-element.12), channel_id=1, source_target_pairs={{0,1},{8,9},{16,17},{24,25},{1,0},{9,8},{17,16},{25,24},{2,3},{10,... | collective-permute-start | bytes 393224 | tf_op jit(solution)/shard_map/ppermute | solution.py:293
  63.2 17.6 %collective-permute-start.28 = (bf16[256,256]{1,0:T(8,128)(2,1)S(1)}, bf16[256,256]{1,0:T(8,128)(2,1)S(1)}, u32[]{:S(2)}, u32[]{:S(2)}) collective-permute-start(bf16[256,256]{1,0:T(8,128)(2,1)S(1)} %get-tuple-element.13), channel_id=1, source_target_pairs={{0,24},{8,16},{16,8},{24,0},{1,25},{9,17},{17,9},{25,1},{2,26},{10... | collective-permute-start | bytes 393224 | tf_op jit(solution)/shard_map/ppermute | solution.py:293
  66.4 14.8 %collective-permute-start.27 = (bf16[256,256]{1,0:T(8,128)(2,1)}, bf16[256,256]{1,0:T(8,128)(2,1)S(1)}, u32[]{:S(2)}, u32[]{:S(2)}) collective-permute-start(bf16[256,256]{1,0:T(8,128)(2,1)} %get-tuple-element.14), channel_id=1, source_target_pairs={{0,20},{8,28},{16,4},{24,12},{1,21},{9,29},{17,5},{25,13},{2,22},{... | collective-permute-start | bytes 393224 | tf_op jit(solution)/shard_map/ppermute | solution.py:293
  72.7 15.5 %collective-permute-start.26 = (bf16[256,256]{1,0:T(8,128)(2,1)}, bf16[256,256]{1,0:T(8,128)(2,1)S(1)}, u32[]{:S(2)}, u32[]{:S(2)}) collective-permute-start(bf16[256,256]{1,0:T(8,128)(2,1)} %get-tuple-element.15), channel_id=1, source_target_pairs={{0,16},{8,24},{16,0},{24,8},{1,17},{9,25},{17,1},{25,9},{2,18},{10... | collective-permute-start | bytes 393224 | tf_op jit(solution)/shard_map/ppermute | solution.py:293
  72.8 19.5 %collective-permute-start.25 = (bf16[256,256]{1,0:T(8,128)(2,1)}, bf16[256,256]{1,0:T(8,128)(2,1)S(1)}, u32[]{:S(2)}, u32[]{:S(2)}) collective-permute-start(bf16[256,256]{1,0:T(8,128)(2,1)} %get-tuple-element.16), channel_id=1, source_target_pairs={{0,12},{8,4},{16,28},{24,20},{1,13},{9,5},{17,29},{25,21},{2,14},{... | collective-permute-start | bytes 393224 | tf_op jit(solution)/shard_map/ppermute | solution.py:293
  78.6 14.3 %collective-permute-start.24 = (bf16[256,256]{1,0:T(8,128)(2,1)}, bf16[256,256]{1,0:T(8,128)(2,1)S(1)}, u32[]{:S(2)}, u32[]{:S(2)}) collective-permute-start(bf16[256,256]{1,0:T(8,128)(2,1)} %get-tuple-element.17), channel_id=1, source_target_pairs={{0,8},{8,0},{16,24},{24,16},{1,9},{9,1},{17,25},{25,17},{2,10},{10... | collective-permute-start | bytes 393224 | tf_op jit(solution)/shard_map/ppermute | solution.py:293
  80.8 13.3 %collective-permute-start.23 = (bf16[256,256]{1,0:T(8,128)(2,1)}, bf16[256,256]{1,0:T(8,128)(2,1)S(1)}, u32[]{:S(2)}, u32[]{:S(2)}) collective-permute-start(bf16[256,256]{1,0:T(8,128)(2,1)} %get-tuple-element.18), channel_id=1, source_target_pairs={{0,4},{8,12},{16,20},{24,28},{1,5},{9,13},{17,21},{25,29},{2,6},{1... | collective-permute-start | bytes 393224 | tf_op jit(solution)/shard_map/ppermute | solution.py:293
  81.2 13.3 %collective-permute-start.22 = (bf16[256,256]{1,0:T(8,128)(2,1)}, bf16[256,256]{1,0:T(8,128)(2,1)}, u32[]{:S(2)}, u32[]{:S(2)}) collective-permute-start(bf16[256,256]{1,0:T(8,128)(2,1)} %get-tuple-element.19), channel_id=1, source_target_pairs={{0,2},{8,10},{16,18},{24,26},{1,3},{9,11},{17,19},{25,27},{2,0},{1... | collective-permute-start | bytes 393224 | tf_op jit(solution)/shard_map/ppermute | solution.py:293
  83.5 92.9 %all-to-all-start.2 = ((f32[32,16,256]{2,1,0:T(8,128)}), f32[32,16,256]{2,1,0:T(8,128)}, u32[]{:S(2)}, u32[]{:S(2)}) async-start(f32[32,16,256]{2,1,0:T(8,128)} %bitcast.28), calls=%async_computation.2 | async-start | bytes 1048576 | tf_op jit(solution)/shard_map/all_to_all | solution.py:303
  88.3 27.3 %collective-permute-start.21 = (bf16[256,256]{1,0:T(8,128)(2,1)}, bf16[256,256]{1,0:T(8,128)(2,1)S(1)}, u32[]{:S(2)}, u32[]{:S(2)}) collective-permute-start(bf16[256,256]{1,0:T(8,128)(2,1)} %get-tuple-element.20), channel_id=1, source_target_pairs={{0,29},{8,21},{16,13},{24,5},{1,28},{9,20},{17,12},{25,4},{2,31},{... | collective-permute-start | bytes 393224 | tf_op jit(solution)/shard_map/ppermute | solution.py:293
  92.3 25.4 %collective-permute-start.20 = (bf16[256,256]{1,0:T(8,128)(2,1)}, bf16[256,256]{1,0:T(8,128)(2,1)S(1)}, u32[]{:S(2)}, u32[]{:S(2)}) collective-permute-start(bf16[256,256]{1,0:T(8,128)(2,1)} %get-tuple-element.21), channel_id=1, source_target_pairs={{0,25},{8,17},{16,9},{24,1},{1,24},{9,16},{17,8},{25,0},{2,27},{10... | collective-permute-start | bytes 393224 | tf_op jit(solution)/shard_map/ppermute | solution.py:293
  92.8 25.9 %collective-permute-start.19 = (bf16[256,256]{1,0:T(8,128)(2,1)}, bf16[256,256]{1,0:T(8,128)(2,1)S(1)}, u32[]{:S(2)}, u32[]{:S(2)}) collective-permute-start(bf16[256,256]{1,0:T(8,128)(2,1)} %get-tuple-element.22), channel_id=1, source_target_pairs={{0,21},{8,29},{16,5},{24,13},{1,20},{9,28},{17,4},{25,12},{2,23},{... | collective-permute-start | bytes 393224 | tf_op jit(solution)/shard_map/ppermute | solution.py:293
  94.1 25.2 %collective-permute-start.18 = (bf16[256,256]{1,0:T(8,128)(2,1)}, bf16[256,256]{1,0:T(8,128)(2,1)S(1)}, u32[]{:S(2)}, u32[]{:S(2)}) collective-permute-start(bf16[256,256]{1,0:T(8,128)(2,1)} %get-tuple-element.23), channel_id=1, source_target_pairs={{0,17},{8,25},{16,1},{24,9},{1,16},{9,24},{17,0},{25,8},{2,19},{10... | collective-permute-start | bytes 393224 | tf_op jit(solution)/shard_map/ppermute | solution.py:293
  94.5 28.8 %collective-permute-start.17 = (bf16[256,256]{1,0:T(8,128)(2,1)}, bf16[256,256]{1,0:T(8,128)(2,1)S(1)}, u32[]{:S(2)}, u32[]{:S(2)}) collective-permute-start(bf16[256,256]{1,0:T(8,128)(2,1)} %get-tuple-element.24), channel_id=1, source_target_pairs={{0,13},{8,5},{16,29},{24,21},{1,12},{9,4},{17,28},{25,20},{2,15},{... | collective-permute-start | bytes 393224 | tf_op jit(solution)/shard_map/ppermute | solution.py:293
  115.5 9.8 %collective-permute-start.16 = (bf16[256,256]{1,0:T(8,128)(2,1)}, bf16[256,256]{1,0:T(8,128)(2,1)S(1)}, u32[]{:S(2)}, u32[]{:S(2)}) collective-permute-start(bf16[256,256]{1,0:T(8,128)(2,1)} %get-tuple-element.25), channel_id=1, source_target_pairs={{0,9},{8,1},{16,25},{24,17},{1,8},{9,0},{17,24},{25,16},{2,11},{10... | collective-permute-start | bytes 393224 | tf_op jit(solution)/shard_map/ppermute | solution.py:293
  117.7 9.9 %collective-permute-start.15 = (bf16[256,256]{1,0:T(8,128)(2,1)}, bf16[256,256]{1,0:T(8,128)(2,1)S(1)}, u32[]{:S(2)}, u32[]{:S(2)}) collective-permute-start(bf16[256,256]{1,0:T(8,128)(2,1)} %get-tuple-element.26), channel_id=1, source_target_pairs={{0,5},{8,13},{16,21},{24,29},{1,4},{9,12},{17,20},{25,28},{2,7},{1... | collective-permute-start | bytes 393224 | tf_op jit(solution)/shard_map/ppermute | solution.py:293
  118.7 11.3 %collective-permute-start.14 = (bf16[256,256]{1,0:T(8,128)(2,1)}, bf16[256,256]{1,0:T(8,128)(2,1)S(1)}, u32[]{:S(2)}, u32[]{:S(2)}) collective-permute-start(bf16[256,256]{1,0:T(8,128)(2,1)} %get-tuple-element.27), channel_id=1, source_target_pairs={{0,3},{8,11},{16,19},{24,27},{1,2},{9,10},{17,18},{25,26},{2,1},{1... | collective-permute-start | bytes 393224 | tf_op jit(solution)/shard_map/ppermute | solution.py:293
  119.3 13.3 %collective-permute-start.13 = (bf16[256,256]{1,0:T(8,128)(2,1)}, bf16[256,256]{1,0:T(8,128)(2,1)S(1)}, u32[]{:S(2)}, u32[]{:S(2)}) collective-permute-start(bf16[256,256]{1,0:T(8,128)(2,1)} %get-tuple-element.28), channel_id=1, source_target_pairs={{0,30},{8,22},{16,14},{24,6},{1,31},{9,23},{17,15},{25,7},{2,28},{... | collective-permute-start | bytes 393224 | tf_op jit(solution)/shard_map/ppermute | solution.py:293
  123.3 15.6 %collective-permute-start.12 = (bf16[256,256]{1,0:T(8,128)(2,1)}, bf16[256,256]{1,0:T(8,128)(2,1)S(1)}, u32[]{:S(2)}, u32[]{:S(2)}) collective-permute-start(bf16[256,256]{1,0:T(8,128)(2,1)} %get-tuple-element.29), channel_id=1, source_target_pairs={{0,26},{8,18},{16,10},{24,2},{1,27},{9,19},{17,11},{25,3},{2,24},{... | collective-permute-start | bytes 393224 | tf_op jit(solution)/shard_map/ppermute | solution.py:293
  125.3 31.1 %collective-permute-start.4 = (bf16[256,256]{1,0:T(8,128)(2,1)}, bf16[256,256]{1,0:T(8,128)(2,1)S(1)}, u32[]{:S(2)}, u32[]{:S(2)}) collective-permute-start(bf16[256,256]{1,0:T(8,128)(2,1)} %get-tuple-element.39), channel_id=1, source_target_pairs={{0,23},{8,31},{16,7},{24,15},{1,22},{9,30},{17,6},{25,14},{2,21},{... | collective-permute-start | bytes 393224 | tf_op jit(solution)/shard_map/ppermute | solution.py:293
  127.6 28.9 %collective-permute-start.3 = (bf16[256,256]{1,0:T(8,128)(2,1)}, bf16[256,256]{1,0:T(8,128)(2,1)S(1)}, u32[]{:S(2)}, u32[]{:S(2)}) collective-permute-start(bf16[256,256]{1,0:T(8,128)(2,1)} %get-tuple-element.40), channel_id=1, source_target_pairs={{0,19},{8,27},{16,3},{24,11},{1,18},{9,26},{17,2},{25,10},{2,17},{... | collective-permute-start | bytes 393224 | tf_op jit(solution)/shard_map/ppermute | solution.py:293
  130.0 26.5 %collective-permute-start.2 = (bf16[256,256]{1,0:T(8,128)(2,1)}, bf16[256,256]{1,0:T(8,128)(2,1)S(1)}, u32[]{:S(2)}, u32[]{:S(2)}) collective-permute-start(bf16[256,256]{1,0:T(8,128)(2,1)} %get-tuple-element.41), channel_id=1, source_target_pairs={{0,15},{8,7},{16,31},{24,23},{1,14},{9,6},{17,30},{25,22},{2,13},{... | collective-permute-start | bytes 393224 | tf_op jit(solution)/shard_map/ppermute | solution.py:293
  132.6 23.9 %collective-permute-start.1 = (bf16[256,256]{1,0:T(8,128)(2,1)}, bf16[256,256]{1,0:T(8,128)(2,1)S(1)}, u32[]{:S(2)}, u32[]{:S(2)}) collective-permute-start(bf16[256,256]{1,0:T(8,128)(2,1)} %get-tuple-element.42), channel_id=1, source_target_pairs={{0,11},{8,3},{16,27},{24,19},{1,10},{9,2},{17,26},{25,18},{2,9},{1... | collective-permute-start | bytes 393224 | tf_op jit(solution)/shard_map/ppermute | solution.py:293
  138.9 17.6 %collective-permute-start = (bf16[256,256]{1,0:T(8,128)(2,1)}, bf16[256,256]{1,0:T(8,128)(2,1)S(1)}, u32[]{:S(2)}, u32[]{:S(2)}) collective-permute-start(bf16[256,256]{1,0:T(8,128)(2,1)} %get-tuple-element.43), channel_id=1, source_target_pairs={{0,7},{8,15},{16,23},{24,31},{1,6},{9,14},{17,22},{25,30},{2,5},{1... | collective-permute-start | bytes 393224 | tf_op jit(solution)/shard_map/ppermute | solution.py:293
  156.5 5.3 %copy-start.2 = (bf16[8192,256]{1,0:T(8,128)(2,1)S(1)}, bf16[8192,256]{1,0:T(8,128)(2,1)}, u32[]{:S(2)}) copy-start(bf16[8192,256]{1,0:T(8,128)(2,1)} %w_ref.5) | copy-start | bytes 12582916
  161.8 5.1 %copy-start.3 = (s32[512]{0:T(512)S(1)}, s32[512]{0:T(512)}, u32[]{:S(2)}) copy-start(s32[512]{0:T(512)} %param.6) | copy-start | bytes 6148
  178.1 8.1 %all-to-all-start.3 = ((f32[4,16,256]{2,1,0:T(8,128)}), f32[4,16,256]{2,1,0:T(8,128)S(1)}, u32[]{:S(2)}, u32[]{:S(2)}) async-start(f32[4,16,256]{2,1,0:T(8,128)} %broadcast_in_dim.22), calls=%async_computation.3 | async-start | bytes 131072 | tf_op jit(solution)/shard_map/all_to_all | solution.py:305

commit v3 on v2

--- a/solution.py
+++ b/solution.py
@@ -14,7 +14,6 @@
 LOG2E = math.log2(math.e)
 ALL = ("rep", "grp")
 VMEM_BYTES = 28 * 1024 * 1024
-GROUPS = 4
 
 NT = (((1,), (1,)), ((), ()))
 
@@ -29,13 +28,19 @@
     return jnp.transpose(jnp.broadcast_to(row, (128, lanes)))[:, :1]
 
 
-def forward_kernel(base_ref, emb_ref, lab_ref, w_ref, a_ref, b_ref, st_ref, xhat_ref, sum_ref, *, classes):
+def forward_kernel(base_ref, rep_ref, lab_ref, w_ref, *refs, classes, reps):
+    blocks = refs[:reps]
+    emb_ref, a_ref, b_ref, st_ref, xhat_ref, sum_ref = refs[reps:]
     step = pl.program_id(0)
     tile = w_ref.shape[0]
     batch = emb_ref.shape[0]
 
     @pl.when(step == 0)
     def _():
+        for k, block_ref in enumerate(blocks):
+            rows = block_ref.shape[0]
+            first = pl.multiple_of((rep_ref[0] ^ k) * rows, rows)
+            emb_ref[pl.ds(first, rows), :] = block_ref[...]
         xwide, _ = unit_rows(emb_ref[...].astype(jnp.float32))
         xhat_ref[...] = xwide.astype(jnp.bfloat16)
         sum_ref[...] = jnp.zeros_like(sum_ref)
@@ -84,26 +89,32 @@
         st_ref[...] = jnp.transpose(stats)[:8, :]
 
 
-def forward(base, emb, labels, weights):
-    batch, width = emb.shape
+def forward(base, rep, blocks, labels, weights):
+    rows, width = blocks[0].shape
+    reps = len(blocks)
+    batch = rows * reps
     classes = weights.shape[0]
     tile = math.gcd(classes, 1024)
     whole = lambda i: (0, 0)
-    return pl.pallas_call(
-        functools.partial(forward_kernel, classes=classes),
+    smem = pl.BlockSpec(memory_space=pltpu.SMEM)
+    return pl.pallas_call(
+        functools.partial(forward_kernel, classes=classes, reps=reps),
         grid=(classes // tile,),
         in_specs=[
-            pl.BlockSpec(memory_space=pltpu.SMEM),
-            pl.BlockSpec((batch, width), whole),
+            smem,
+            smem,
             pl.BlockSpec((batch, 1), whole),
             pl.BlockSpec((tile, width), lambda i: (i, 0)),
-        ],
+        ]
+        + [pl.BlockSpec((rows, width), whole)] * reps,
         out_specs=[
             pl.BlockSpec((batch, width), whole),
             pl.BlockSpec((batch, width), whole),
+            pl.BlockSpec((batch, width), whole),
             pl.BlockSpec((8, batch), whole),
         ],
         out_shape=[
+            jax.ShapeDtypeStruct((batch, width), jnp.bfloat16),
             jax.ShapeDtypeStruct((batch, width), jnp.float32),
             jax.ShapeDtypeStruct((batch, width), jnp.float32),
             jax.ShapeDtypeStruct((8, batch), jnp.float32),
@@ -118,7 +129,7 @@
             transcendentals=batch * classes,
         ),
         name="forward_sums",
-    )(base, emb, labels.reshape(batch, 1), weights)
+    )(base, rep, labels.reshape(batch, 1), weights, *blocks)
 
 
 def weight_kernel(base_ref, emb_ref, lab_ref, st_ref, tot_ref, w_ref, g_ref, xhat_ref, y_ref, v_ref):
@@ -181,11 +192,41 @@
     )(base, emb, labels.reshape(1, batch), stats, totals.reshape(1, batch), weights)
 
 
-def place_kernel(*refs, sources, started):
+def fetch_kernel(me_ref, rows_ref, *refs, sources, tokens):
+    outs, sem = refs[tokens : tokens + len(sources)], refs[-1]
+    copies = []
+    for u, (k, out_ref) in enumerate(zip(sources, outs)):
+        run = out_ref.shape[0]
+        first = pl.multiple_of((me_ref[0] ^ k) * run, run)
+        copies.append(pltpu.make_async_copy(rows_ref.at[pl.ds(first, run), :], out_ref, sem.at[u]))
+    for copy in copies:
+        copy.start()
+    for copy in copies:
+        copy.wait()
+
+
+def fetch_runs(me, rows, run, sources, tokens):
+    anywhere = pl.BlockSpec(memory_space=pl.ANY)
+    return pl.pallas_call(
+        functools.partial(fetch_kernel, sources=tuple(sources), tokens=len(tokens)),
+        in_specs=[pl.BlockSpec(memory_space=pltpu.SMEM)] + [anywhere] * (1 + len(tokens)),
+        out_specs=[anywhere] * len(sources),
+        out_shape=[jax.ShapeDtypeStruct((run, rows.shape[1]), rows.dtype)] * len(sources),
+        scratch_shapes=[pltpu.SemaphoreType.DMA((len(sources),))],
+        cost_estimate=pl.CostEstimate(
+            flops=0, bytes_accessed=4 * len(sources) * run * rows.shape[1], transcendentals=0
+        ),
+        name="fetch_runs",
+    )(me, rows, *tokens)
+
+
+def place_kernel(*refs, sources):
     me_ref, slot_ref = refs[:2]
     rows = refs[2 : 2 + len(sources)]
-    held_ref, stage_ref = refs[-2:]
+    held_ref, token_ref, stage_ref = refs[-3:]
     run = rows[0].shape[0]
+    batch = math.gcd(run, 32)
+    token_ref[...] = jnp.zeros_like(token_ref)
     for u, (k, row_ref) in enumerate(zip(sources, rows)):
         unit, _ = unit_rows(row_ref[...].astype(jnp.float32))
         stage_ref[pl.ds(u * 2 * run, run, stride=2), :] = unit[:, :128]
@@ -193,27 +234,30 @@
         first = (me_ref[0] ^ k) * run
 
         def place(j, carry, u=u, first=first):
-            for v in range(16):
-                row = j * 16 + v
-                slot = slot_ref[first + row]
-                held_ref[pl.ds(slot * 2, 2), :] = stage_ref[pl.ds((u * run + row) * 2, 2), :]
+            at = j * batch
+            slots = [slot_ref[first + at + v] for v in range(batch)]
+            values = [stage_ref[pl.ds((u * run + at + v) * 2, 2), :] for v in range(batch)]
+            for slot, value in zip(slots, values):
+                held_ref[pl.ds(slot * 2, 2), :] = value
             return carry
 
-        lax.fori_loop(0, run // 16, place, 0)
+        lax.fori_loop(0, run // batch, place, 0)
 
 
 def place_rows(me, slots, rows, sources, held, classes):
     run, width = rows[0].shape
     smem = pl.BlockSpec(memory_space=pltpu.SMEM)
     vmem = pl.BlockSpec(memory_space=pltpu.VMEM)
-    started = held is not None
-    operands = [me, slots, *rows] + ([held] if started else [])
-    return pl.pallas_call(
-        functools.partial(place_kernel, sources=tuple(sources), started=started),
+    operands = [me, slots, *rows] + ([] if held is None else [held])
+    return pl.pallas_call(
+        functools.partial(place_kernel, sources=tuple(sources)),
         in_specs=[smem, smem] + [vmem] * (len(operands) - 2),
-        out_specs=vmem,
-        out_shape=jax.ShapeDtypeStruct((2 * classes, 128), jnp.float32),
-        input_output_aliases={len(operands) - 1: 0} if started else {},
+        out_specs=[vmem, vmem],
+        out_shape=[
+            jax.ShapeDtypeStruct((2 * classes, 128), jnp.float32),
+            jax.ShapeDtypeStruct((8, 128), jnp.float32),
+        ],
+        input_output_aliases={} if held is None else {len(operands) - 1: 0},
         scratch_shapes=[pltpu.VMEM((2 * run * len(sources), 128), jnp.float32)],
         compiler_params=pltpu.CompilerParams(vmem_limit_bytes=VMEM_BYTES),
         cost_estimate=pl.CostEstimate(
@@ -228,8 +272,9 @@
 def blend_kernel(w_ref, held_ref, o_ref):
     wwide, _ = unit_rows(w_ref[...].astype(jnp.float32))
     tile = w_ref.shape[0]
-    low = wwide[:, :128] + held_ref[pl.ds(0, tile, stride=2), :]
-    high = wwide[:, 128:] + held_ref[pl.ds(1, tile, stride=2), :]
+    first = pl.multiple_of(pl.program_id(0) * 2 * tile, 2 * tile)
+    low = wwide[:, :128] + held_ref[pl.ds(first, tile, stride=2), :]
+    high = wwide[:, 128:] + held_ref[pl.ds(first + 1, tile, stride=2), :]
     square = jnp.sum(low * low + high * high, axis=1, keepdims=True)
     inv = lax.rsqrt(square + 1e-06)
     o_ref[:, :128] = (low * inv).astype(jnp.bfloat16)
@@ -244,7 +289,7 @@
         grid=(classes // tile,),
         in_specs=[
             pl.BlockSpec((tile, width), lambda i: (i, 0)),
-            pl.BlockSpec((2 * tile, 128), lambda i: (i, 0)),
+            pl.BlockSpec(memory_space=pltpu.VMEM),
         ],
         out_specs=pl.BlockSpec((tile, width), lambda i: (i, 0)),
         out_shape=jax.ShapeDtypeStruct((classes, width), jnp.bfloat16),
@@ -264,41 +309,47 @@
     groups, reps = lax.axis_size("grp"), lax.axis_size("rep")
     peers = groups * reps
     batch = rows_local * reps
-    per_peer = classes // peers
+    run = classes // peers
     share = rows_local // groups
-    grp, rep = lax.axis_index("grp"), lax.axis_index("rep")
-    base = ((rep * groups + grp) * classes).astype(jnp.int32).reshape(1)
-
-    slots = centroid_class.reshape(peers, per_peer)
-    digits = jnp.concatenate([slots // 128, slots % 128], axis=1).astype(jnp.bfloat16)
-    digit_rows = -(-2 * per_peer // width)
-    digits = jnp.pad(digits, ((0, 0), (0, digit_rows * width - 2 * per_peer)))
-    mine = lax.dynamic_slice_in_dim(embeddings, grp * share, share, 0)
-    head = jnp.concatenate(
-        [jnp.broadcast_to(mine[None], (peers, share, width)), digits.reshape(peers, digit_rows, width)],
-        axis=1,
-    )
-    head = lax.all_to_all(head, ALL, 0, 0, tiled=True)
-    emb = head[:, :share].reshape(batch, width)
-    digits = head[:, share:].reshape(peers, digit_rows * width).astype(jnp.int32)
-    slots_got = (digits[:, :per_peer] * 128 + digits[:, per_peer : 2 * per_peer]).reshape(-1)
-    me = (rep * groups + grp).astype(jnp.int32)
-    crossing, near = list(range(peers // 2, peers)), list(range(1, peers // 2))
-    order = [k for pair in zip(crossing, near + [0]) for k in pair]
+    grp, rep = lax.axis_index("grp").astype(jnp.int32), lax.axis_index("rep").astype(jnp.int32)
+    me = rep * groups + grp
+    base, me = (me * classes).reshape(1), me.reshape(1)
     at = lambda d: d % groups * reps + d // groups
-    runs = {}
-    for k in order:
-        run = lax.dynamic_slice_in_dim(centroids, (me ^ k) * per_peer, per_peer, 0)
-        pairs = [(at(d), at(d ^ k)) for d in range(peers)]
-        runs[k] = lax.ppermute(run, ("grp", "rep"), pairs) if k else run
-
-    a, b, stats = forward(base, emb, labels, class_weights)
-    sums = jnp.broadcast_to(stats[:2].reshape(1, -1, 128), (peers, 2 * batch // 128, 128))
-    sums = lax.all_to_all(sums, ALL, 0, 0, tiled=True)
-    totals = jnp.sum(sums, axis=0).reshape(2, batch)
-    total, target = totals[0], totals[1]
-    weight_grad = weight_gradient(base, emb, labels, stats, total, class_weights)
-    loss = lax.dynamic_slice_in_dim(SCALE + jnp.log(total) - target, rep * rows_local, rows_local, 0)
+
+    def exchange(value, k):
+        return lax.ppermute(value, ("grp", "rep"), [(at(d), at(d ^ k)) for d in range(peers)])
+
+    blocks = [embeddings] + [
+        lax.ppermute(embeddings, "rep", [(i, i ^ k) for i in range(reps)]) for k in range(1, reps)
+    ]
+    far, near = list(range(peers // 2, peers)), list(range(1, peers // 2))
+    order = [k for pair in zip(far, near) for k in pair] + far[len(near) :]
+    cuts = [0] + [round(len(order) * c / 31) for c in (5, 12, 19, 26, 31)]
+    plan = [order[i:j] for i, j in zip(cuts, cuts[1:])]
+
+    def send(group, tokens):
+        fetched = fetch_runs(me, centroids, run, plan[group], tokens)
+        return [exchange(value, k) for value, k in zip(fetched, plan[group])]
+
+    got = [send(0, [])]
+    emb, a, b, stats = forward(base, rep.reshape(1), blocks, labels, class_weights)
+    got.append(send(1, [stats]))
+
+    flat = [
+        jnp.broadcast_to(stats[0][None], (peers, batch)),
+        centroid_class.reshape(peers, run).astype(jnp.float32),
+        jnp.repeat(stats[1].reshape(reps, rows_local), groups, axis=0),
+    ]
+    size = batch + run + rows_local
+    pad = -size % 1024
+    flat = jnp.pad(jnp.concatenate(flat, axis=1), ((0, 0), (0, pad)))
+    flat = lax.all_to_all(flat.reshape(peers, -1, 128), ALL, 0, 0, tiled=True).reshape(peers, -1)
+    total = jnp.sum(flat[:, :batch], axis=0)
+    slots = flat[:, batch : batch + run].reshape(-1).astype(jnp.int32)
+    target = jnp.sum(flat[:, batch + run : size], axis=0)
+    own_total = lax.dynamic_slice_in_dim(total, rep * rows_local, rows_local, 0)
+    loss = SCALE + jnp.log(own_total) - target
+
     grad = a / total[:, None] - b
     parts = lax.all_to_all(grad.reshape(peers, share, width), ALL, 0, 0, tiled=True)
     own = jnp.sum(parts, axis=0)
@@ -306,11 +357,15 @@
         jnp.broadcast_to(own[None], (groups, share, width)), "grp", 0, 0, tiled=True
     ).reshape(rows_local, width)
 
-    held = None
-    step = max(1, peers // GROUPS)
-    for first in range(0, peers, step):
-        sources = order[first : first + step]
-        held = place_rows(me.reshape(1), slots_got, [runs[k] for k in sources], sources, held, classes)
+    weight_grad = weight_gradient(base, emb, labels, stats, total, class_weights)
+    mine = list(fetch_runs(me, centroids, run, [0], [stats]))
+    held, token = place_rows(me, slots, got[0] + mine, plan[0] + [0], None, classes)
+    tokens = [token, weight_grad]
+    for group in range(1, len(plan)):
+        if group + 1 < len(plan):
+            got.append(send(group + 1, tokens))
+        held, token = place_rows(me, slots, got[group], plan[group], held, classes)
+        tokens = [token]
     return (loss, embedding_gradient, weight_grad, blend(class_weights, held))
 
 

time: 188 us -> 324 us (1.72)
  Pallas kernels: 47.2 us -> 180 us
  local copies, waits for them, and re-layouts: 11.9 us -> 30.3 us
  starting transfers between devices: 84.6 us -> 70.3 us
    pallas_call x5 -> x12, Pallas kernels: 32.6 us -> 165 us  [the longest x6 134 us: fetch_runs(): pl.pallas_call(functools.partial(fetch_kernel, sources=tuple(sources), to...]
    unnamed x13 -> x49, local copies, waits for them, and re-layouts: 3.59 us -> 28.7 us
    ppermute x31 -> x38, waiting for transfers between devices: 24.5 us -> 39.2 us  [the longest x31 34.8 us: exchange(): lax.ppermute(value, ('grp', 'rep'), [(at(d), at(d ^ k)) for d in range(pe...]
    all_to_all x2 -> x1, waiting for transfers between devices: 8.66 us -> 0.01 us  [shards(): lax.all_to_all(flat.reshape(peers, -1, 128), ALL, 0, 0, tiled=True)]
    ppermute x31 -> x38, starting transfers between devices: 66.7 us -> 58.3 us  [the longest x31 48.1 us: exchange(): lax.ppermute(value, ('grp', 'rep'), [(at(d), at(d ^ k)) for d in range(pe...]
    all_to_all x2 -> x1, starting transfers between devices: 9.87 us -> 2.89 us  [shards(): lax.all_to_all(flat.reshape(peers, -1, 128), ALL, 0, 0, tiled=True)]
    dynamic_slice x4 -> x0, local copies, waits for them, and re-layouts: 6.09 us -> none  [the longest x2 5.49 us: shards(): run = lax.dynamic_slice_in_dim(centroids, (me ^ k) * per_peer, per_peer, 0)]
    all_to_all x1, waiting for transfers between devices: 4.21 us -> 0.01 us  [shards(): lax.all_to_all(jnp.broadcast_to(own[None], (groups, share, width)), 'grp'...]
  transfers between devices with their start and end apart: 35 -> 41, of which waited for: 9 -> 8; matrix products, arithmetic and copies ran while one was open for 5% -> 1% of each run, Pallas kernels for 25% -> 52%
where the time goes in v3:
time: 324 us; the launch traced here: 323 us
  Pallas kernels  180 us (56%)
  starting transfers between devices  70.3 us (22%)
  waiting for transfers between devices  39.2 us (12%)
  local copies, waits for them, and re-layouts  30.3 us (9%)
    pallas_call x6, Pallas kernels, fetch_runs(): pl.pallas_call(functools.partial(fetch_kernel, sources=tuple(sources), to...  134 us
    ppermute x31, starting transfers between devices, exchange(): lax.ppermute(value, ('grp', 'rep'), [(at(d), at(d ^ k)) for d in range(pe...  48.1 us
    ppermute x31, waiting for transfers between devices, exchange(): lax.ppermute(value, ('grp', 'rep'), [(at(d), at(d ^ k)) for d in range(pe...  34.8 us
    unnamed x49, local copies, waits for them, and re-layouts  28.7 us
    pallas_call x5, Pallas kernels, place_rows(): pl.pallas_call(functools.partial(place_kernel, sources=tuple(sources)), i...  19.7 us
    pallas_call x1, Pallas kernels, forward(): pl.pallas_call(functools.partial(forward_kernel, classes=classes, reps=re...  11.6 us
    ppermute x7, starting transfers between devices, shards(): lax.ppermute(embeddings, 'rep', [(i, i ^ k) for i in range(reps)])  10.2 us
    pallas_call x1, Pallas kernels, weight_gradient(): pl.pallas_call(weight_kernel, grid=(classes // tile,), in_specs=[pl.Block...  9.53 us
  transfers between devices with their start and end apart: 41, of which 8 were waited for; matrix products, arithmetic and copies ran while one was open for 1% of the time, Pallas kernels for 52%

profile of v3, /device:TPU:0, one launch (start us, length us, event | category | flops | bytes accessed | tf_op | source)
XLA Modules:
  0.0 323.0 jit_solution(18044931395291127744)
XLA Ops:
  0.6 5.1 %collective-permute-start.5 = (bf16[64,256]{1,0:T(8,128)(2,1)}, bf16[64,256]{1,0:T(8,128)(2,1)S(1)}, u32[]{:S(2)}, u32[]{:S(2)}) collective-permute-start(bf16[64,256]{1,0:T(8,128)(2,1)} %refs_0_.1), channel_id=1, source_target_pairs={{0,6},{1,7},{2,4},{3,5},{4,2},{5,3},{6,0},{7,1},{8,14},{9,15},{10,... | collective-permute-start | bytes 98312 | tf_op jit(solution)/shard_map/ppermute | solution.py:323
  5.7 2.1 collective-permute-start.3
  7.8 2.3 collective-permute-start.1
  10.1 1.0 collective-permute-done.4.refs_5_
  11.8 0.8 convert_element_type.13
  12.6 0.8 copy.14.lab_ref
  13.5 3.3 %collective-permute-done.6.refs_7_ = bf16[64,256]{1,0:T(8,128)(2,1)S(1)} collective-permute-done((bf16[64,256]{1,0:T(8,128)(2,1)}, bf16[64,256]{1,0:T(8,128)(2,1)S(1)}, u32[]{:S(2)}, u32[]{:S(2)}) %collective-permute-start.6) | collective-permute-done | bytes 32800 | tf_op jit(solution)/shard_map/ppermute | solution.py:323
  16.8 2.2 copy-done.6
  19.0 0.8 copy-done.16
  19.8 11.6 %forward_sums.1 = (bf16[512,256]{1,0:T(8,128)(2,1)S(1)}, f32[512,256]{1,0:T(8,128)S(1)}, f32[512,256]{1,0:T(8,128)S(1)}, f32[8,512]{1,0:T(8,128)S(1)}) custom-call(s32[1]{0:T(128)} %bitcast.base_ref, s32[1]{0:T(128)} %bitcast.1.rep_ref, s32[512,1]{1,0:T(8,128)S(1)} %copy.14.lab_ref, bf16[8192,256]{1,0:T(8,128)(2,1)S(1)} %copy-done.6, ...), custom_call_target="tpu_custom_call" | custom-call | flops 6442450944 | bytes 4194304 | tf_op jit(solution)/shard_map/forward_sums/pallas_call | solution.py:100
  31.5 0.7 copy.15
  32.2 2.9 all-to-all-start
  35.1 21.0 %fetch_runs.6 = (bf16[256,256]{1,0:T(8,128)(2,1)}, bf16[256,256]{1,0:T(8,128)(2,1)}, bf16[256,256]{1,0:T(8,128)(2,1)}, bf16[256,256]{1,0:T(8,128)(2,1)}, bf16[256,256]{1,0:T(8,128)(2,1)}) custom-call(s32[1]{0:T(128)} %bitcast.9.me_ref.refs_0_, bf16[8192,256]{1,0:T(8,128)(2,1)} %rows_ref.11), custom_call_target="tpu_custom_call" | custom-call | bytes 1310720 | tf_op jit(solution)/shard_map/fetch_runs/pallas_call | solution.py:210
  56.1 2.7 collective-permute-start.7
  58.9 1.5 collective-permute-start.8
  60.6 1.8 collective-permute-start.10
  62.3 2.4 collective-permute-start.11
  64.7 5.1 %fetch_runs.7.refs_7_ = bf16[256,256]{1,0:T(8,128)(2,1)} custom-call(s32[1]{0:T(128)} %bitcast.9.me_ref.refs_0_, bf16[8192,256]{1,0:T(8,128)(2,1)} %rows_ref.11, f32[8,512]{1,0:T(8,128)} %copy-done.10), custom_call_target="tpu_custom_call" | custom-call | bytes 262144 | tf_op jit(solution)/shard_map/fetch_runs/pallas_call | solution.py:210
  69.8 29.0 %fetch_runs.9 = (bf16[256,256]{1,0:T(8,128)(2,1)}, bf16[256,256]{1,0:T(8,128)(2,1)}, bf16[256,256]{1,0:T(8,128)(2,1)}, bf16[256,256]{1,0:T(8,128)(2,1)}, bf16[25...) custom-call(s32[1]{0:T(128)} %bitcast.9.me_ref.refs_0_, bf16[8192,256]{1,0:T(8,128)(2,1)} %rows_ref.11, ...), custom_call_target="tpu_custom_call" | custom-call | bytes 1835008 | tf_op jit(solution)/shard_map/fetch_runs/pallas_call | solution.py:210
  98.8 2.5 collective-permute-start.19
  101.5 0.9 divide_subtract_fusion
  102.5 5.8 %all-to-all-start.1 = ((f32[32,16,256]{2,1,0:T(8,128)}), f32[32,16,256]{2,1,0:T(8,128)S(1)}, u32[]{:S(2)}, u32[]{:S(2)}) async-start(f32[32,16,256]{2,1,0:T(8,128)} %bitcast.5), calls=%async_computation.1 | async-start | bytes 1048576 | tf_op jit(solution)/shard_map/all_to_all | solution.py:354
  108.6 2.5 collective-permute-start.22
  111.2 1.2 collective-permute-start.23
  112.6 1.5 collective-permute-start.25
  114.2 0.9 copy-done.9
  115.1 3.5 %place_rows.5 = (f32[16384,128]{1,0:T(8,128)S(1)}, f32[8,128]{1,0:T(8,128)S(1)}) custom-call(s32[1]{0:T(128)} %bitcast.9.me_ref.refs_0_, s32[8192]{0:T(1024)S(1)} %bitcast.20, bf16[256,256]{1,0:T(8,128)(2,1)S(1)} %collective-permute-done.7.refs_2_, bf16[256,256]{1,0:T(8,128)(2,1)S(1)} %collective-permute-done.8.refs_3_, ...), custom_call_target="tpu_custom_call" | custom-call | flops 3932160 | bytes 6291456 | tf_op jit(solution)/shard_map/place_rows/pallas_call | solution.py:252
  118.7 12.6 %collective-permute-done.22.refs_5_ = bf16[256,256]{1,0:T(8,128)(2,1)S(1)} collective-permute-done((bf16[256,256]{1,0:T(8,128)(2,1)}, bf16[256,256]{1,0:T(8,128)(2,1)S(1)}, u32[]{:S(2)}, u32[]{:S(2)}) %collective-permute-start.22) | collective-permute-done | bytes 131104 | tf_op jit(solution)/shard_map/ppermute | solution.py:320
  131.3 3.7 %collective-permute-done.24.refs_7_ = bf16[256,256]{1,0:T(8,128)(2,1)S(1)} collective-permute-done((bf16[256,256]{1,0:T(8,128)(2,1)}, bf16[256,256]{1,0:T(8,128)(2,1)S(1)}, u32[]{:S(2)}, u32[]{:S(2)}) %collective-permute-start.24) | collective-permute-done | bytes 131104 | tf_op jit(solution)/shard_map/ppermute | solution.py:320
  135.0 4.0 %place_rows.6 = (f32[16384,128]{1,0:T(8,128)S(1)}, f32[8,128]{1,0:T(8,128)S(1)}) custom-call(s32[1]{0:T(128)} %bitcast.9.me_ref.refs_0_, s32[8192]{0:T(1024)S(1)} %bitcast.21, bf16[256,256]{1,0:T(8,128)(2,1)S(1)} %collective-permute-done.19.refs_2_, bf16[256,256]{1,0:T(8,128)(2,1)S(1)} %collective-permute-done.20.refs_3_, ...), custom_call_target="tpu_custom_call", output_to_operand_aliasing={{0}: (9, {})} | custom-call | flops 4587520 | bytes 7340032 | tf_op jit(solution)/shard_map/place_rows/pallas_call | solution.py:252
  138.9 3.3 %copy-done = f32[16384,128]{1,0:T(8,128)} copy-done((f32[16384,128]{1,0:T(8,128)}, f32[16384,128]{1,0:T(8,128)S(1)}, u32[]{:S(2)}) %copy-start) | copy-done | bytes 8388632
  142.8 29.0 %fetch_runs.11 = (bf16[256,256]{1,0:T(8,128)(2,1)}, bf16[256,256]{1,0:T(8,128)(2,1)}, bf16[256,256]{1,0:T(8,128)(2,1)}, bf16[256,256]{1,0:T(8,128)(2,1)}, bf16[2...) custom-call(s32[1]{0:T(128)} %bitcast.9.me_ref.refs_0_, bf16[8192,256]{1,0:T(8,128)(2,1)} %rows_ref.11, ...), custom_call_target="tpu_custom_call" | custom-call | bytes 1835008 | tf_op jit(solution)/shard_map/fetch_runs/pallas_call | solution.py:210
  171.9 2.7 collective-permute-start.32
  174.6 2.2 copy-done.7
  176.8 9.5 %weight_gradient.1.refs_1_ = f32[8192,256]{1,0:T(8,128)} custom-call(s32[1]{0:T(128)} %bitcast.base_ref, bf16[512,256]{1,0:T(8,128)(2,1)S(1)} %get-tuple-element.50.emb_ref, s32[1,512]{1,0:T(1,128)S(1)} %bitcast.27, f32[8,512]{1,0:T(8,128)S(1)} %copy-done.11, f32[1,512]{1,0:T(1,128)S(1)} %bitcast.25, bf16[8192,256]{1,0:T(8,128)(2,1)S(1)} %copy-done.7), custom_call_target="tpu_custom_call" | custom-call | flops 4294967296 | bytes 12582912 | tf_op jit(solution)/shard_map/weight_gradient/pallas_call | solution.py:165
  186.4 29.0 %fetch_runs.8 = (bf16[256,256]{1,0:T(8,128)(2,1)}, bf16[256,256]{1,0:T(8,128)(2,1)}, bf16[256,256]{1,0:T(8,128)(2,1)}, bf16[256,256]{1,0:T(8,128)(2,1)}, bf16[25...) custom-call(s32[1]{0:T(128)} %bitcast.9.me_ref.refs_0_, bf16[8192,256]{1,0:T(8,128)(2,1)} %rows_ref.11, ...), custom_call_target="tpu_custom_call" | custom-call | bytes 1835008 | tf_op jit(solution)/shard_map/fetch_runs/pallas_call | solution.py:210
  215.3 2.0 collective-permute-start.12
  217.3 0.9 collective-permute-start.13
  218.2 1.6 collective-permute-start.14
  219.8 1.7 collective-permute-start.15
  221.5 2.3 collective-permute-start.16
  223.8 5.0 %collective-permute-done.12.refs_2_ = bf16[256,256]{1,0:T(8,128)(2,1)S(1)} collective-permute-done((bf16[256,256]{1,0:T(8,128)(2,1)}, bf16[256,256]{1,0:T(8,128)(2,1)S(1)}, u32[]{:S(2)}, u32[]{:S(2)}) %collective-permute-start.12) | collective-permute-done | bytes 131104 | tf_op jit(solution)/shard_map/ppermute | solution.py:320
  228.8 0.9 collective-permute-start.18
  229.7 4.9 %collective-permute-done.14.refs_4_ = bf16[256,256]{1,0:T(8,128)(2,1)S(1)} collective-permute-done((bf16[256,256]{1,0:T(8,128)(2,1)}, bf16[256,256]{1,0:T(8,128)(2,1)S(1)}, u32[]{:S(2)}, u32[]{:S(2)}) %collective-permute-start.14) | collective-permute-done | bytes 131104 | tf_op jit(solution)/shard_map/ppermute | solution.py:320
  234.5 1.9 collective-permute-start.34
  236.6 3.2 collective-permute-done.17.refs_7_
  239.9 1.2 collective-permute-start.36
  241.0 6.2 %collective-permute-start.37 = (bf16[256,256]{1,0:T(8,128)(2,1)S(1)}, bf16[256,256]{1,0:T(8,128)(2,1)S(1)}, u32[]{:S(2)}, u32[]{:S(2)}) collective-permute-start(bf16[256,256]{1,0:T(8,128)(2,1)S(1)} %copy-done.17), channel_id=1, source_target_pairs={{0,11},{8,3},{16,27},{24,19},{1,10},{9,2},{17,26},{25,18},{2,9},{1... | collective-permute-start | bytes 393224 | tf_op jit(solution)/shard_map/ppermute | solution.py:320
  247.2 3.4 %copy-done.1 = f32[16384,128]{1,0:T(8,128)S(1)} copy-done((f32[16384,128]{1,0:T(8,128)S(1)}, f32[16384,128]{1,0:T(8,128)}, u32[]{:S(2)}) %copy-start.1) | copy-done | bytes 8388632
  250.6 4.0 %place_rows.7 = (f32[16384,128]{1,0:T(8,128)S(1)}, f32[8,128]{1,0:T(8,128)S(1)}) custom-call(s32[1]{0:T(128)} %bitcast.9.me_ref.refs_0_, s32[8192]{0:T(1024)S(1)} %bitcast.22, bf16[256,256]{1,0:T(8,128)(2,1)S(1)} %collective-permute-done.12.refs_2_, bf16[256,256]{1,0:T(8,128)(2,1)S(1)} %collective-permute-done.13.refs_3_, ...), custom_call_target="tpu_custom_call", output_to_operand_aliasing={{0}: (9, {})} | custom-call | flops 4587520 | bytes 7340032 | tf_op jit(solution)/shard_map/place_rows/pallas_call | solution.py:252
  254.6 3.3 %copy-done.2 = f32[16384,128]{1,0:T(8,128)} copy-done((f32[16384,128]{1,0:T(8,128)}, f32[16384,128]{1,0:T(8,128)S(1)}, u32[]{:S(2)}) %copy-start.2) | copy-done | bytes 8388632
  258.5 21.0 %fetch_runs.10 = (bf16[256,256]{1,0:T(8,128)(2,1)}, bf16[256,256]{1,0:T(8,128)(2,1)}, bf16[256,256]{1,0:T(8,128)(2,1)}, bf16[256,256]{1,0:T(8,128)(2,1)}, bf16[256,256]{1,0:T(8,128)(2,1)}) custom-call(s32[1]{0:T(128)} %bitcast.9.me_ref.refs_0_, bf16[8192,256]{1,0:T(8,128)(2,1)} %rows_ref.11, f32[8,128]{1,0:T(8,128)} %copy-done.14), custom_call_target="tpu_custom_call" | custom-call | bytes 1310720 | tf_op jit(solution)/shard_map/fetch_runs/pallas_call | solution.py:210
  280.2 3.3 %all-to-all-start.2 = ((f32[4,16,256]{2,1,0:T(8,128)}), f32[4,16,256]{2,1,0:T(8,128)S(1)}, u32[]{:S(2)}, u32[]{:S(2)}) async-start(f32[4,16,256]{2,1,0:T(8,128)} %broadcast_in_dim.20), calls=%async_computation.2 | async-start | bytes 131072 | tf_op jit(solution)/shard_map/all_to_all | solution.py:356
  283.5 2.3 collective-permute-start.26
  286.3 3.1 collective-permute-start.28
  289.4 1.7 collective-permute-start.29
  291.1 1.9 collective-permute-start.30
  293.6 3.4 %copy-done.3 = f32[16384,128]{1,0:T(8,128)S(1)} copy-done((f32[16384,128]{1,0:T(8,128)S(1)}, f32[16384,128]{1,0:T(8,128)}, u32[]{:S(2)}) %copy-start.3) | copy-done | bytes 8388632
  297.0 4.5 %place_rows.8 = (f32[16384,128]{1,0:T(8,128)S(1)}, f32[8,128]{1,0:T(8,128)}) custom-call(s32[1]{0:T(128)} %bitcast.9.me_ref.refs_0_, s32[8192]{0:T(1024)S(1)} %bitcast.23, bf16[256,256]{1,0:T(8,128)(2,1)S(1)} %collective-permute-done.31.refs_2_, bf16[256,256]{1,0:T(8,128)(2,1)S(1)} %collective-permute-done.32.refs_3_, ...), custom_call_target="tpu_custom_call", output_to_operand_aliasing={{0}: (9, {})} | custom-call | flops 4587520 | bytes 7340032 | tf_op jit(solution)/shard_map/place_rows/pallas_call | solution.py:252
  301.5 5.4 %collective-permute-done.30.refs_6_ = bf16[256,256]{1,0:T(8,128)(2,1)S(1)} collective-permute-done((bf16[256,256]{1,0:T(8,128)(2,1)}, bf16[256,256]{1,0:T(8,128)(2,1)S(1)}, u32[]{:S(2)}, u32[]{:S(2)}) %collective-permute-start.30) | collective-permute-done | bytes 131104 | tf_op jit(solution)/shard_map/ppermute | solution.py:320
  306.9 3.7 %place_rows.9 = (f32[16384,128]{1,0:T(8,128)S(1)}, f32[8,128]{1,0:T(8,128)}) custom-call(s32[1]{0:T(128)} %bitcast.9.me_ref.refs_0_, s32[8192]{0:T(1024)S(1)} %bitcast.24, bf16[256,256]{1,0:T(8,128)(2,1)S(1)} %collective-permute-done.26.refs_2_, bf16[256,256]{1,0:T(8,128)(2,1)S(1)} %collective-permute-done.27.refs_3_, ...), custom_call_target="tpu_custom_call", output_to_operand_aliasing={{0}: (7, {})} | custom-call | flops 3276800 | bytes 5242880 | tf_op jit(solution)/shard_map/place_rows/pallas_call | solution.py:252
  310.6 3.3 %copy-done.4 = f32[16384,128]{1,0:T(8,128)} copy-done((f32[16384,128]{1,0:T(8,128)}, f32[16384,128]{1,0:T(8,128)S(1)}, u32[]{:S(2)}) %copy-start.4) | copy-done | bytes 8388632
  313.9 3.4 %copy-done.5 = f32[16384,128]{1,0:T(8,128)S(1)} copy-done((f32[16384,128]{1,0:T(8,128)S(1)}, f32[16384,128]{1,0:T(8,128)}, u32[]{:S(2)}) %copy-start.5) | copy-done | bytes 8388632
  317.3 5.1 %blend.1 = bf16[8192,256]{1,0:T(8,128)(2,1)} custom-call(bf16[8192,256]{1,0:T(8,128)(2,1)S(1)} %copy-done.8, f32[16384,128]{1,0:T(8,128)S(1)} %copy-done.5), custom_call_target="tpu_custom_call" | custom-call | flops 20971520 | bytes 16777216 | tf_op jit(solution)/shard_map/blend/pallas_call | solution.py:287
  (96 shorter events, 5.9 us)
Async XLA Ops:
  0.6 9.5 %collective-permute-start.5 = (bf16[64,256]{1,0:T(8,128)(2,1)}, bf16[64,256]{1,0:T(8,128)(2,1)S(1)}, u32[]{:S(2)}, u32[]{:S(2)}) collective-permute-start(bf16[64,256]{1,0:T(8,128)(2,1)} %refs_0_.1), channel_id=1, source_target_pairs={{0,6},{1,7},{2,4},{3,5},{4,2},{5,3},{6,0},{7,1},{8,14},{9,15},{10,... | collective-permute-start | bytes 98312 | tf_op jit(solution)/shard_map/ppermute | solution.py:323
  5.7 5.4 %collective-permute-start.4 = (bf16[64,256]{1,0:T(8,128)(2,1)}, bf16[64,256]{1,0:T(8,128)(2,1)S(1)}, u32[]{:S(2)}, u32[]{:S(2)}) collective-permute-start(bf16[64,256]{1,0:T(8,128)(2,1)} %refs_0_.1), channel_id=1, source_target_pairs={{0,5},{1,4},{2,7},{3,6},{4,1},{5,0},{6,3},{7,2},{8,13},{9,12},{10,... | collective-permute-start | bytes 98312 | tf_op jit(solution)/shard_map/ppermute | solution.py:323
  5.7 7.7 %collective-permute-start.3 = (bf16[64,256]{1,0:T(8,128)(2,1)}, bf16[64,256]{1,0:T(8,128)(2,1)S(1)}, u32[]{:S(2)}, u32[]{:S(2)}) collective-permute-start(bf16[64,256]{1,0:T(8,128)(2,1)} %refs_0_.1), channel_id=1, source_target_pairs={{0,4},{1,5},{2,6},{3,7},{4,0},{5,1},{6,2},{7,3},{8,12},{9,13},{10,... | collective-permute-start | bytes 98312 | tf_op jit(solution)/shard_map/ppermute | solution.py:323
  7.8 5.6 %collective-permute-start.2 = (bf16[64,256]{1,0:T(8,128)(2,1)}, bf16[64,256]{1,0:T(8,128)(2,1)S(1)}, u32[]{:S(2)}, u32[]{:S(2)}) collective-permute-start(bf16[64,256]{1,0:T(8,128)(2,1)} %refs_0_.1), channel_id=1, source_target_pairs={{0,3},{1,2},{2,1},{3,0},{4,7},{5,6},{6,5},{7,4},{8,11},{9,10},{10,... | collective-permute-start | bytes 98312 | tf_op jit(solution)/shard_map/ppermute | solution.py:323
  7.8 5.6 %collective-permute-start.1 = (bf16[64,256]{1,0:T(8,128)(2,1)}, bf16[64,256]{1,0:T(8,128)(2,1)S(1)}, u32[]{:S(2)}, u32[]{:S(2)}) collective-permute-start(bf16[64,256]{1,0:T(8,128)(2,1)} %refs_0_.1), channel_id=1, source_target_pairs={{0,2},{1,3},{2,0},{3,1},{4,6},{5,7},{6,4},{7,5},{8,10},{9,11},{10,... | collective-permute-start | bytes 98312 | tf_op jit(solution)/shard_map/ppermute | solution.py:323
  10.1 3.3 %collective-permute-start = (bf16[64,256]{1,0:T(8,128)(2,1)}, bf16[64,256]{1,0:T(8,128)(2,1)S(1)}, u32[]{:S(2)}, u32[]{:S(2)}) collective-permute-start(bf16[64,256]{1,0:T(8,128)(2,1)} %refs_0_.1), channel_id=1, source_target_pairs={{0,1},{1,0},{2,3},{3,2},{4,5},{5,4},{6,7},{7,6},{8,9},{9,8},{10,11... | collective-permute-start | bytes 98312 | tf_op jit(solution)/shard_map/ppermute | solution.py:323
  11.2 5.6 %collective-permute-start.6 = (bf16[64,256]{1,0:T(8,128)(2,1)}, bf16[64,256]{1,0:T(8,128)(2,1)S(1)}, u32[]{:S(2)}, u32[]{:S(2)}) collective-permute-start(bf16[64,256]{1,0:T(8,128)(2,1)} %refs_0_.1), channel_id=1, source_target_pairs={{0,7},{1,6},{2,5},{3,4},{4,3},{5,2},{6,1},{7,0},{8,15},{9,14},{10,... | collective-permute-start | bytes 98312 | tf_op jit(solution)/shard_map/ppermute | solution.py:323
  16.8 2.2 copy-start.6
  19.0 0.8 copy-start.16
  31.4 33.3 %copy-start.10 = (f32[8,512]{1,0:T(8,128)}, f32[8,512]{1,0:T(8,128)S(1)}, u32[]{:S(2)}) copy-start(f32[8,512]{1,0:T(8,128)S(1)} %get-tuple-element.47.st_ref.refs_0_) | copy-start | bytes 49156
  32.2 66.6 %all-to-all-start = ((f32[32,8,128]{2,1,0:T(8,128)}), f32[32,8,128]{2,1,0:T(8,128)S(1)}, u32[]{:S(2)}, u32[]{:S(2)}) async-start(f32[32,8,128]{2,1,0:T(8,128)} %bitcast.11), calls=%async_computation | async-start | bytes 262144 | tf_op jit(solution)/shard_map/all_to_all | solution.py:346
  56.1 42.7 %collective-permute-start.7 = (bf16[256,256]{1,0:T(8,128)(2,1)}, bf16[256,256]{1,0:T(8,128)(2,1)S(1)}, u32[]{:S(2)}, u32[]{:S(2)}) collective-permute-start(bf16[256,256]{1,0:T(8,128)(2,1)} %get-tuple-element.51), channel_id=1, source_target_pairs={{0,4},{8,12},{16,20},{24,28},{1,5},{9,13},{17,21},{25,29},{2,6},{1... | collective-permute-start | bytes 393224 | tf_op jit(solution)/shard_map/ppermute | solution.py:320
  58.9 42.5 %collective-permute-start.8 = (bf16[256,256]{1,0:T(8,128)(2,1)}, bf16[256,256]{1,0:T(8,128)(2,1)S(1)}, u32[]{:S(2)}, u32[]{:S(2)}) collective-permute-start(bf16[256,256]{1,0:T(8,128)(2,1)} %get-tuple-element.52), channel_id=1, source_target_pairs={{0,8},{8,0},{16,24},{24,16},{1,9},{9,1},{17,25},{25,17},{2,10},{10... | collective-permute-start | bytes 393224 | tf_op jit(solution)/shard_map/ppermute | solution.py:320
  60.3 48.0 %collective-permute-start.9 = (bf16[256,256]{1,0:T(8,128)(2,1)}, bf16[256,256]{1,0:T(8,128)(2,1)S(1)}, u32[]{:S(2)}, u32[]{:S(2)}) collective-permute-start(bf16[256,256]{1,0:T(8,128)(2,1)} %get-tuple-element.53), channel_id=1, source_target_pairs={{0,12},{8,4},{16,28},{24,20},{1,13},{9,5},{17,29},{25,21},{2,14},{... | collective-permute-start | bytes 393224 | tf_op jit(solution)/shard_map/ppermute | solution.py:320
  60.6 48.1 %collective-permute-start.10 = (bf16[256,256]{1,0:T(8,128)(2,1)}, bf16[256,256]{1,0:T(8,128)(2,1)S(1)}, u32[]{:S(2)}, u32[]{:S(2)}) collective-permute-start(bf16[256,256]{1,0:T(8,128)(2,1)} %get-tuple-element.54), channel_id=1, source_target_pairs={{0,16},{8,24},{16,0},{24,8},{1,17},{9,25},{17,1},{25,9},{2,18},{10... | collective-permute-start | bytes 393224 | tf_op jit(solution)/shard_map/ppermute | solution.py:320
  62.3 48.8 %collective-permute-start.11 = (bf16[256,256]{1,0:T(8,128)(2,1)}, bf16[256,256]{1,0:T(8,128)(2,1)S(1)}, u32[]{:S(2)}, u32[]{:S(2)}) collective-permute-start(bf16[256,256]{1,0:T(8,128)(2,1)} %get-tuple-element.55), channel_id=1, source_target_pairs={{0,20},{8,28},{16,4},{24,12},{1,21},{9,29},{17,5},{25,13},{2,22},{... | collective-permute-start | bytes 393224 | tf_op jit(solution)/shard_map/ppermute | solution.py:320
  98.8 13.6 %collective-permute-start.19 = (bf16[256,256]{1,0:T(8,128)(2,1)}, bf16[256,256]{1,0:T(8,128)(2,1)S(1)}, u32[]{:S(2)}, u32[]{:S(2)}) collective-permute-start(bf16[256,256]{1,0:T(8,128)(2,1)} %get-tuple-element.64), channel_id=1, source_target_pairs={{0,24},{8,16},{16,8},{24,0},{1,25},{9,17},{17,9},{25,1},{2,26},{10... | collective-permute-start | bytes 393224 | tf_op jit(solution)/shard_map/ppermute | solution.py:320
  101.3 11.3 %collective-permute-start.20 = (bf16[256,256]{1,0:T(8,128)(2,1)}, bf16[256,256]{1,0:T(8,128)(2,1)S(1)}, u32[]{:S(2)}, u32[]{:S(2)}) collective-permute-start(bf16[256,256]{1,0:T(8,128)(2,1)} %get-tuple-element.65), channel_id=1, source_target_pairs={{0,28},{8,20},{16,12},{24,4},{1,29},{9,21},{17,13},{25,5},{2,30},{... | collective-permute-start | bytes 393224 | tf_op jit(solution)/shard_map/ppermute | solution.py:320
  101.5 73.1 %copy-start.11 = (f32[8,512]{1,0:T(8,128)S(1)}, f32[8,512]{1,0:T(8,128)}, u32[]{:S(2)}) copy-start(f32[8,512]{1,0:T(8,128)} %copy-done.10) | copy-start | bytes 49156
  101.5 73.1 %copy-start.15 = (s32[512]{0:T(512)S(1)}, s32[512]{0:T(512)}, u32[]{:S(2)}) copy-start(s32[512]{0:T(512)} %param.6) | copy-start | bytes 6148
  102.5 177.0 %all-to-all-start.1 = ((f32[32,16,256]{2,1,0:T(8,128)}), f32[32,16,256]{2,1,0:T(8,128)S(1)}, u32[]{:S(2)}, u32[]{:S(2)}) async-start(f32[32,16,256]{2,1,0:T(8,128)} %bitcast.5), calls=%async_computation.1 | async-start | bytes 1048576 | tf_op jit(solution)/shard_map/all_to_all | solution.py:354
  108.3 10.3 %collective-permute-start.21 = (bf16[256,256]{1,0:T(8,128)(2,1)}, bf16[256,256]{1,0:T(8,128)(2,1)S(1)}, u32[]{:S(2)}, u32[]{:S(2)}) collective-permute-start(bf16[256,256]{1,0:T(8,128)(2,1)} %get-tuple-element.66), channel_id=1, source_target_pairs={{0,1},{8,9},{16,17},{24,25},{1,0},{9,8},{17,16},{25,24},{2,3},{10,... | collective-permute-start | bytes 393224 | tf_op jit(solution)/shard_map/ppermute | solution.py:320
  108.6 22.6 %collective-permute-start.22 = (bf16[256,256]{1,0:T(8,128)(2,1)}, bf16[256,256]{1,0:T(8,128)(2,1)S(1)}, u32[]{:S(2)}, u32[]{:S(2)}) collective-permute-start(bf16[256,256]{1,0:T(8,128)(2,1)} %get-tuple-element.67), channel_id=1, source_target_pairs={{0,5},{8,13},{16,21},{24,29},{1,4},{9,12},{17,20},{25,28},{2,7},{1... | collective-permute-start | bytes 393224 | tf_op jit(solution)/shard_map/ppermute | solution.py:320
  111.2 20.1 %collective-permute-start.23 = (bf16[256,256]{1,0:T(8,128)(2,1)}, bf16[256,256]{1,0:T(8,128)(2,1)S(1)}, u32[]{:S(2)}, u32[]{:S(2)}) collective-permute-start(bf16[256,256]{1,0:T(8,128)(2,1)} %get-tuple-element.68), channel_id=1, source_target_pairs={{0,9},{8,1},{16,25},{24,17},{1,8},{9,0},{17,24},{25,16},{2,11},{10... | collective-permute-start | bytes 393224 | tf_op jit(solution)/shard_map/ppermute | solution.py:320
  112.4 22.6 %collective-permute-start.24 = (bf16[256,256]{1,0:T(8,128)(2,1)}, bf16[256,256]{1,0:T(8,128)(2,1)S(1)}, u32[]{:S(2)}, u32[]{:S(2)}) collective-permute-start(bf16[256,256]{1,0:T(8,128)(2,1)} %get-tuple-element.69), channel_id=1, source_target_pairs={{0,13},{8,5},{16,29},{24,21},{1,12},{9,4},{17,28},{25,20},{2,15},{... | collective-permute-start | bytes 393224 | tf_op jit(solution)/shard_map/ppermute | solution.py:320
  112.6 22.3 %collective-permute-start.25 = (bf16[256,256]{1,0:T(8,128)(2,1)}, bf16[256,256]{1,0:T(8,128)(2,1)S(1)}, u32[]{:S(2)}, u32[]{:S(2)}) collective-permute-start(bf16[256,256]{1,0:T(8,128)(2,1)} %get-tuple-element.70), channel_id=1, source_target_pairs={{0,17},{8,25},{16,1},{24,9},{1,16},{9,24},{17,0},{25,8},{2,19},{10... | collective-permute-start | bytes 393224 | tf_op jit(solution)/shard_map/ppermute | solution.py:320
  114.2 0.9 copy-start.9
  118.6 67.7 %copy-start.12 = (f32[8,128]{1,0:T(8,128)}, f32[8,128]{1,0:T(8,128)S(1)}, u32[]{:S(2)}) copy-start(f32[8,128]{1,0:T(8,128)S(1)} %get-tuple-element.56.refs_0_) | copy-start | bytes 12292
  138.9 3.3 %copy-start = (f32[16384,128]{1,0:T(8,128)}, f32[16384,128]{1,0:T(8,128)S(1)}, u32[]{:S(2)}) copy-start(f32[16384,128]{1,0:T(8,128)S(1)} %get-tuple-element.72.refs_9_) | copy-start | bytes 25165828
  142.2 0.6 copy-start.13
  171.8 48.0 %collective-permute-start.31 = (bf16[256,256]{1,0:T(8,128)(2,1)}, bf16[256,256]{1,0:T(8,128)(2,1)S(1)}, u32[]{:S(2)}, u32[]{:S(2)}) collective-permute-start(bf16[256,256]{1,0:T(8,128)(2,1)} %get-tuple-element.80), channel_id=1, source_target_pairs={{0,18},{8,26},{16,2},{24,10},{1,19},{9,27},{17,3},{25,11},{2,16},{... | collective-permute-start | bytes 393224 | tf_op jit(solution)/shard_map/ppermute | solution.py:320
  171.9 49.6 %collective-permute-start.32 = (bf16[256,256]{1,0:T(8,128)(2,1)}, bf16[256,256]{1,0:T(8,128)(2,1)S(1)}, u32[]{:S(2)}, u32[]{:S(2)}) collective-permute-start(bf16[256,256]{1,0:T(8,128)(2,1)} %get-tuple-element.81), channel_id=1, source_target_pairs={{0,22},{8,30},{16,6},{24,14},{1,23},{9,31},{17,7},{25,15},{2,20},{... | collective-permute-start | bytes 393224 | tf_op jit(solution)/shard_map/ppermute | solution.py:320
  174.6 2.2 copy-start.7
  186.3 48.2 %copy-start.21 = (bf16[256,256]{1,0:T(8,128)(2,1)S(1)}, bf16[256,256]{1,0:T(8,128)(2,1)}, u32[]{:S(2)}) copy-start(bf16[256,256]{1,0:T(8,128)(2,1)} %get-tuple-element.82) | copy-start | bytes 393220
  186.3 48.2 %copy-start.20 = (bf16[256,256]{1,0:T(8,128)(2,1)S(1)}, bf16[256,256]{1,0:T(8,128)(2,1)}, u32[]{:S(2)}) copy-start(bf16[256,256]{1,0:T(8,128)(2,1)} %get-tuple-element.83) | copy-start | bytes 393220
  186.3 50.1 %copy-start.19 = (bf16[256,256]{1,0:T(8,128)(2,1)S(1)}, bf16[256,256]{1,0:T(8,128)(2,1)}, u32[]{:S(2)}) copy-start(bf16[256,256]{1,0:T(8,128)(2,1)} %get-tuple-element.84) | copy-start | bytes 393220
  186.3 53.5 %copy-start.18 = (bf16[256,256]{1,0:T(8,128)(2,1)S(1)}, bf16[256,256]{1,0:T(8,128)(2,1)}, u32[]{:S(2)}) copy-start(bf16[256,256]{1,0:T(8,128)(2,1)} %get-tuple-element.85) | copy-start | bytes 393220
  186.3 54.7 %copy-start.17 = (bf16[256,256]{1,0:T(8,128)(2,1)S(1)}, bf16[256,256]{1,0:T(8,128)(2,1)}, u32[]{:S(2)}) copy-start(bf16[256,256]{1,0:T(8,128)(2,1)} %get-tuple-element.86) | copy-start | bytes 393220
  215.3 13.5 %collective-permute-start.12 = (bf16[256,256]{1,0:T(8,128)(2,1)}, bf16[256,256]{1,0:T(8,128)(2,1)S(1)}, u32[]{:S(2)}, u32[]{:S(2)}) collective-permute-start(bf16[256,256]{1,0:T(8,128)(2,1)} %get-tuple-element.57), channel_id=1, source_target_pairs={{0,21},{8,29},{16,5},{24,13},{1,20},{9,28},{17,4},{25,12},{2,23},{... | collective-permute-start | bytes 393224 | tf_op jit(solution)/shard_map/ppermute | solution.py:320
  217.3 11.5 %collective-permute-start.13 = (bf16[256,256]{1,0:T(8,128)(2,1)}, bf16[256,256]{1,0:T(8,128)(2,1)S(1)}, u32[]{:S(2)}, u32[]{:S(2)}) collective-permute-start(bf16[256,256]{1,0:T(8,128)(2,1)} %get-tuple-element.58), channel_id=1, source_target_pairs={{0,25},{8,17},{16,9},{24,1},{1,24},{9,16},{17,8},{25,0},{2,27},{10... | collective-permute-start | bytes 393224 | tf_op jit(solution)/shard_map/ppermute | solution.py:320
  218.2 16.3 %collective-permute-start.14 = (bf16[256,256]{1,0:T(8,128)(2,1)}, bf16[256,256]{1,0:T(8,128)(2,1)S(1)}, u32[]{:S(2)}, u32[]{:S(2)}) collective-permute-start(bf16[256,256]{1,0:T(8,128)(2,1)} %get-tuple-element.59), channel_id=1, source_target_pairs={{0,29},{8,21},{16,13},{24,5},{1,28},{9,20},{17,12},{25,4},{2,31},{... | collective-permute-start | bytes 393224 | tf_op jit(solution)/shard_map/ppermute | solution.py:320
  219.8 14.7 %collective-permute-start.15 = (bf16[256,256]{1,0:T(8,128)(2,1)}, bf16[256,256]{1,0:T(8,128)(2,1)S(1)}, u32[]{:S(2)}, u32[]{:S(2)}) collective-permute-start(bf16[256,256]{1,0:T(8,128)(2,1)} %get-tuple-element.60), channel_id=1, source_target_pairs={{0,2},{8,10},{16,18},{24,26},{1,3},{9,11},{17,19},{25,27},{2,0},{1... | collective-permute-start | bytes 393224 | tf_op jit(solution)/shard_map/ppermute | solution.py:320
  221.5 15.0 %collective-permute-start.16 = (bf16[256,256]{1,0:T(8,128)(2,1)}, bf16[256,256]{1,0:T(8,128)(2,1)S(1)}, u32[]{:S(2)}, u32[]{:S(2)}) collective-permute-start(bf16[256,256]{1,0:T(8,128)(2,1)} %get-tuple-element.61), channel_id=1, source_target_pairs={{0,6},{8,14},{16,22},{24,30},{1,7},{9,15},{17,23},{25,31},{2,4},{1... | collective-permute-start | bytes 393224 | tf_op jit(solution)/shard_map/ppermute | solution.py:320
  228.8 11.0 %collective-permute-start.17 = (bf16[256,256]{1,0:T(8,128)(2,1)}, bf16[256,256]{1,0:T(8,128)(2,1)S(1)}, u32[]{:S(2)}, u32[]{:S(2)}) collective-permute-start(bf16[256,256]{1,0:T(8,128)(2,1)} %get-tuple-element.62), channel_id=1, source_target_pairs={{0,10},{8,2},{16,26},{24,18},{1,11},{9,3},{17,27},{25,19},{2,8},{1... | collective-permute-start | bytes 393224 | tf_op jit(solution)/shard_map/ppermute | solution.py:320
  228.8 12.2 %collective-permute-start.18 = (bf16[256,256]{1,0:T(8,128)(2,1)}, bf16[256,256]{1,0:T(8,128)(2,1)S(1)}, u32[]{:S(2)}, u32[]{:S(2)}) collective-permute-start(bf16[256,256]{1,0:T(8,128)(2,1)} %get-tuple-element.63), channel_id=1, source_target_pairs={{0,14},{8,6},{16,30},{24,22},{1,15},{9,7},{17,31},{25,23},{2,12},{... | collective-permute-start | bytes 393224 | tf_op jit(solution)/shard_map/ppermute | solution.py:320
  234.5 48.9 %collective-permute-start.33 = (bf16[256,256]{1,0:T(8,128)(2,1)S(1)}, bf16[256,256]{1,0:T(8,128)(2,1)S(1)}, u32[]{:S(2)}, u32[]{:S(2)}) collective-permute-start(bf16[256,256]{1,0:T(8,128)(2,1)S(1)} %copy-done.21), channel_id=1, source_target_pairs={{0,26},{8,18},{16,10},{24,2},{1,27},{9,19},{17,11},{25,3},{2,24},{... | collective-permute-start | bytes 393224 | tf_op jit(solution)/shard_map/ppermute | solution.py:320
  234.5 51.2 %collective-permute-start.34 = (bf16[256,256]{1,0:T(8,128)(2,1)S(1)}, bf16[256,256]{1,0:T(8,128)(2,1)S(1)}, u32[]{:S(2)}, u32[]{:S(2)}) collective-permute-start(bf16[256,256]{1,0:T(8,128)(2,1)S(1)} %copy-done.20), channel_id=1, source_target_pairs={{0,30},{8,22},{16,14},{24,6},{1,31},{9,23},{17,15},{25,7},{2,28},{... | collective-permute-start | bytes 393224 | tf_op jit(solution)/shard_map/ppermute | solution.py:320
  236.5 49.9 %collective-permute-start.35 = (bf16[256,256]{1,0:T(8,128)(2,1)S(1)}, bf16[256,256]{1,0:T(8,128)(2,1)S(1)}, u32[]{:S(2)}, u32[]{:S(2)}) collective-permute-start(bf16[256,256]{1,0:T(8,128)(2,1)S(1)} %copy-done.19), channel_id=1, source_target_pairs={{0,3},{8,11},{16,19},{24,27},{1,2},{9,10},{17,18},{25,26},{2,1},{1... | collective-permute-start | bytes 393224 | tf_op jit(solution)/shard_map/ppermute | solution.py:320
  239.9 49.6 %collective-permute-start.36 = (bf16[256,256]{1,0:T(8,128)(2,1)S(1)}, bf16[256,256]{1,0:T(8,128)(2,1)S(1)}, u32[]{:S(2)}, u32[]{:S(2)}) collective-permute-start(bf16[256,256]{1,0:T(8,128)(2,1)S(1)} %copy-done.18), channel_id=1, source_target_pairs={{0,7},{8,15},{16,23},{24,31},{1,6},{9,14},{17,22},{25,30},{2,5},{1... | collective-permute-start | bytes 393224 | tf_op jit(solution)/shard_map/ppermute | solution.py:320
  241.0 50.1 %collective-permute-start.37 = (bf16[256,256]{1,0:T(8,128)(2,1)S(1)}, bf16[256,256]{1,0:T(8,128)(2,1)S(1)}, u32[]{:S(2)}, u32[]{:S(2)}) collective-permute-start(bf16[256,256]{1,0:T(8,128)(2,1)S(1)} %copy-done.17), channel_id=1, source_target_pairs={{0,11},{8,3},{16,27},{24,19},{1,10},{9,2},{17,26},{25,18},{2,9},{1... | collective-permute-start | bytes 393224 | tf_op jit(solution)/shard_map/ppermute | solution.py:320
  247.2 3.4 %copy-start.1 = (f32[16384,128]{1,0:T(8,128)S(1)}, f32[16384,128]{1,0:T(8,128)}, u32[]{:S(2)}) copy-start(f32[16384,128]{1,0:T(8,128)} %copy-done) | copy-start | bytes 25165828
  254.6 3.3 %copy-start.2 = (f32[16384,128]{1,0:T(8,128)}, f32[16384,128]{1,0:T(8,128)S(1)}, u32[]{:S(2)}) copy-start(f32[16384,128]{1,0:T(8,128)S(1)} %get-tuple-element.87.refs_9_) | copy-start | bytes 25165828
  257.9 0.6 copy-start.14
  280.2 42.2 %all-to-all-start.2 = ((f32[4,16,256]{2,1,0:T(8,128)}), f32[4,16,256]{2,1,0:T(8,128)S(1)}, u32[]{:S(2)}, u32[]{:S(2)}) async-start(f32[4,16,256]{2,1,0:T(8,128)} %broadcast_in_dim.20), calls=%async_computation.2 | async-start | bytes 131072 | tf_op jit(solution)/shard_map/all_to_all | solution.py:356
  283.5 18.0 %collective-permute-start.26 = (bf16[256,256]{1,0:T(8,128)(2,1)}, bf16[256,256]{1,0:T(8,128)(2,1)S(1)}, u32[]{:S(2)}, u32[]{:S(2)}) collective-permute-start(bf16[256,256]{1,0:T(8,128)(2,1)} %get-tuple-element.74), channel_id=1, source_target_pairs={{0,15},{8,7},{16,31},{24,23},{1,14},{9,6},{17,30},{25,22},{2,13},{... | collective-permute-start | bytes 393224 | tf_op jit(solution)/shard_map/ppermute | solution.py:320
  285.8 15.7 %collective-permute-start.27 = (bf16[256,256]{1,0:T(8,128)(2,1)}, bf16[256,256]{1,0:T(8,128)(2,1)S(1)}, u32[]{:S(2)}, u32[]{:S(2)}) collective-permute-start(bf16[256,256]{1,0:T(8,128)(2,1)} %get-tuple-element.75), channel_id=1, source_target_pairs={{0,19},{8,27},{16,3},{24,11},{1,18},{9,26},{17,2},{25,10},{2,17},{... | collective-permute-start | bytes 393224 | tf_op jit(solution)/shard_map/ppermute | solution.py:320
  286.3 15.2 %collective-permute-start.28 = (bf16[256,256]{1,0:T(8,128)(2,1)}, bf16[256,256]{1,0:T(8,128)(2,1)S(1)}, u32[]{:S(2)}, u32[]{:S(2)}) collective-permute-start(bf16[256,256]{1,0:T(8,128)(2,1)} %get-tuple-element.76), channel_id=1, source_target_pairs={{0,23},{8,31},{16,7},{24,15},{1,22},{9,30},{17,6},{25,14},{2,21},{... | collective-permute-start | bytes 393224 | tf_op jit(solution)/shard_map/ppermute | solution.py:320
  289.4 12.1 %collective-permute-start.29 = (bf16[256,256]{1,0:T(8,128)(2,1)}, bf16[256,256]{1,0:T(8,128)(2,1)S(1)}, u32[]{:S(2)}, u32[]{:S(2)}) collective-permute-start(bf16[256,256]{1,0:T(8,128)(2,1)} %get-tuple-element.77), channel_id=1, source_target_pairs={{0,27},{8,19},{16,11},{24,3},{1,26},{9,18},{17,10},{25,2},{2,25},{... | collective-permute-start | bytes 393224 | tf_op jit(solution)/shard_map/ppermute | solution.py:320
  291.1 15.8 %collective-permute-start.30 = (bf16[256,256]{1,0:T(8,128)(2,1)}, bf16[256,256]{1,0:T(8,128)(2,1)S(1)}, u32[]{:S(2)}, u32[]{:S(2)}) collective-permute-start(bf16[256,256]{1,0:T(8,128)(2,1)} %get-tuple-element.78), channel_id=1, source_target_pairs={{0,31},{8,23},{16,15},{24,7},{1,30},{9,22},{17,14},{25,6},{2,29},{... | collective-permute-start | bytes 393224 | tf_op jit(solution)/shard_map/ppermute | solution.py:320
  293.6 3.4 %copy-start.3 = (f32[16384,128]{1,0:T(8,128)S(1)}, f32[16384,128]{1,0:T(8,128)}, u32[]{:S(2)}) copy-start(f32[16384,128]{1,0:T(8,128)} %copy-done.2) | copy-start | bytes 25165828
  296.9 17.0 %copy-start.8 = (bf16[8192,256]{1,0:T(8,128)(2,1)S(1)}, bf16[8192,256]{1,0:T(8,128)(2,1)}, u32[]{:S(2)}) copy-start(bf16[8192,256]{1,0:T(8,128)(2,1)} %w_ref.5) | copy-start | bytes 12582916
  310.6 3.3 %copy-start.4 = (f32[16384,128]{1,0:T(8,128)}, f32[16384,128]{1,0:T(8,128)S(1)}, u32[]{:S(2)}) copy-start(f32[16384,128]{1,0:T(8,128)S(1)} %get-tuple-element.89.held_ref) | copy-start | bytes 25165828
  313.9 3.4 %copy-start.5 = (f32[16384,128]{1,0:T(8,128)S(1)}, f32[16384,128]{1,0:T(8,128)}, u32[]{:S(2)}) copy-start(f32[16384,128]{1,0:T(8,128)} %copy-done.4) | copy-start | bytes 25165828

commit v4 on v3

--- a/solution.py
+++ b/solution.py
@@ -13,7 +13,8 @@
 SIN_FLOOR = 0.09
 LOG2E = math.log2(math.e)
 ALL = ("rep", "grp")
-VMEM_BYTES = 28 * 1024 * 1024
+MIB = 1024 * 1024
+COST = pl.CostEstimate(flops=1, bytes_accessed=1, transcendentals=0)
 
 NT = (((1,), (1,)), ((), ()))
 
@@ -121,12 +122,10 @@
         ],
         scratch_shapes=[pltpu.VMEM((batch, width), jnp.bfloat16), pltpu.VMEM((batch, 128), jnp.float32)],
         compiler_params=pltpu.CompilerParams(
-            dimension_semantics=("arbitrary",), vmem_limit_bytes=VMEM_BYTES
+            dimension_semantics=("arbitrary",), vmem_limit_bytes=20 * MIB
         ),
         cost_estimate=pl.CostEstimate(
-            flops=6 * batch * classes * width,
-            bytes_accessed=classes * width * 2,
-            transcendentals=batch * classes,
+            flops=12 * batch * classes * width, bytes_accessed=classes * width * 2, transcendentals=0
         ),
         name="forward_sums",
     )(base, rep, labels.reshape(batch, 1), weights, *blocks)
@@ -181,62 +180,75 @@
             pltpu.VMEM((1, batch), jnp.float32),
         ],
         compiler_params=pltpu.CompilerParams(
-            dimension_semantics=("arbitrary",), vmem_limit_bytes=VMEM_BYTES
+            dimension_semantics=("arbitrary",), vmem_limit_bytes=20 * MIB
         ),
         cost_estimate=pl.CostEstimate(
-            flops=4 * batch * classes * width,
-            bytes_accessed=classes * width * 6,
-            transcendentals=batch * classes,
+            flops=12 * batch * classes * width, bytes_accessed=classes * width * 6, transcendentals=0
         ),
         name="weight_gradient",
     )(base, emb, labels.reshape(1, batch), stats, totals.reshape(1, batch), weights)
 
 
-def fetch_kernel(me_ref, rows_ref, *refs, sources, tokens):
-    outs, sem = refs[tokens : tokens + len(sources)], refs[-1]
+def fetch_kernel(me_ref, rows_ref, *refs, picks, tokens):
+    outs, sem = refs[tokens : tokens + len(picks)], refs[-1]
     copies = []
-    for u, (k, out_ref) in enumerate(zip(sources, outs)):
-        run = out_ref.shape[0]
-        first = pl.multiple_of((me_ref[0] ^ k) * run, run)
-        copies.append(pltpu.make_async_copy(rows_ref.at[pl.ds(first, run), :], out_ref, sem.at[u]))
+    for u, (k, out_ref) in enumerate(zip(picks, outs)):
+        size = out_ref.shape[0]
+        first = pl.multiple_of((me_ref[0] ^ k) * size, size)
+        copies.append(pltpu.make_async_copy(rows_ref.at[pl.ds(first, size), :], out_ref, sem.at[u]))
     for copy in copies:
         copy.start()
     for copy in copies:
         copy.wait()
 
 
-def fetch_runs(me, rows, run, sources, tokens):
+def fetch(me, rows, size, picks, tokens):
     anywhere = pl.BlockSpec(memory_space=pl.ANY)
     return pl.pallas_call(
-        functools.partial(fetch_kernel, sources=tuple(sources), tokens=len(tokens)),
+        functools.partial(fetch_kernel, picks=tuple(picks), tokens=len(tokens)),
         in_specs=[pl.BlockSpec(memory_space=pltpu.SMEM)] + [anywhere] * (1 + len(tokens)),
-        out_specs=[anywhere] * len(sources),
-        out_shape=[jax.ShapeDtypeStruct((run, rows.shape[1]), rows.dtype)] * len(sources),
-        scratch_shapes=[pltpu.SemaphoreType.DMA((len(sources),))],
-        cost_estimate=pl.CostEstimate(
-            flops=0, bytes_accessed=4 * len(sources) * run * rows.shape[1], transcendentals=0
-        ),
-        name="fetch_runs",
+        out_specs=[pl.BlockSpec(memory_space=pltpu.VMEM)] * len(picks),
+        out_shape=[jax.ShapeDtypeStruct((size, rows.shape[1]), rows.dtype)] * len(picks),
+        scratch_shapes=[pltpu.SemaphoreType.DMA((len(picks),))],
+        compiler_params=pltpu.CompilerParams(vmem_limit_bytes=4 * MIB),
+        cost_estimate=COST,
+        name="fetch",
     )(me, rows, *tokens)
 
 
-def place_kernel(*refs, sources):
-    me_ref, slot_ref = refs[:2]
-    rows = refs[2 : 2 + len(sources)]
-    held_ref, token_ref, stage_ref = refs[-3:]
-    run = rows[0].shape[0]
+def tie_kernel(value_ref, *refs):
+    refs[-1][...] = value_ref[...]
+
+
+def tie(value, tokens):
+    anywhere = pl.BlockSpec(memory_space=pl.ANY)
+    vmem = pl.BlockSpec(memory_space=pltpu.VMEM)
+    return pl.pallas_call(
+        tie_kernel,
+        in_specs=[vmem] + [anywhere] * len(tokens),
+        out_specs=vmem,
+        out_shape=jax.ShapeDtypeStruct(value.shape, value.dtype),
+        compiler_params=pltpu.CompilerParams(vmem_limit_bytes=2 * MIB),
+        cost_estimate=COST,
+        name="tie",
+    )(value, *tokens)
+
+
+def place_runs(info_ref, slot_ref, row_refs, origins, groups, held_ref, stage_ref):
+    run = stage_ref.shape[0] // 2
     batch = math.gcd(run, 32)
-    token_ref[...] = jnp.zeros_like(token_ref)
-    for u, (k, row_ref) in enumerate(zip(sources, rows)):
-        unit, _ = unit_rows(row_ref[...].astype(jnp.float32))
-        stage_ref[pl.ds(u * 2 * run, run, stride=2), :] = unit[:, :128]
-        stage_ref[pl.ds(u * 2 * run + 1, run, stride=2), :] = unit[:, 128:]
-        first = (me_ref[0] ^ k) * run
-
-        def place(j, carry, u=u, first=first):
+    parts = [(ref, u) for ref in row_refs for u in range(ref.shape[0] // run)]
+    for (row_ref, u), (rep_flip, grp_flip, grp_from) in zip(parts, origins):
+        unit, _ = unit_rows(row_ref[u * run : (u + 1) * run, :].astype(jnp.float32))
+        stage_ref[pl.ds(0, run, stride=2), :] = unit[:, :128]
+        stage_ref[pl.ds(1, run, stride=2), :] = unit[:, 128:]
+        grp = info_ref[1] ^ grp_flip if grp_from is None else grp_from
+        first = ((info_ref[0] ^ rep_flip) * groups + grp) * run
+
+        def place(j, carry, first=first):
             at = j * batch
             slots = [slot_ref[first + at + v] for v in range(batch)]
-            values = [stage_ref[pl.ds((u * run + at + v) * 2, 2), :] for v in range(batch)]
+            values = [stage_ref[pl.ds((at + v) * 2, 2), :] for v in range(batch)]
             for slot, value in zip(slots, values):
                 held_ref[pl.ds(slot * 2, 2), :] = value
             return carry
@@ -244,13 +256,20 @@
         lax.fori_loop(0, run // batch, place, 0)
 
 
-def place_rows(me, slots, rows, sources, held, classes):
-    run, width = rows[0].shape
+def place_kernel(info_ref, slot_ref, *refs, origins, groups, arrays):
+    held_ref, token_ref, stage_ref = refs[-3:]
+    token_ref[...] = jnp.zeros_like(token_ref)
+    place_runs(info_ref, slot_ref, refs[:arrays], origins, groups, held_ref, stage_ref)
+
+
+def place_rows(info, slots, arrays, origins, groups, held, classes, run):
     smem = pl.BlockSpec(memory_space=pltpu.SMEM)
     vmem = pl.BlockSpec(memory_space=pltpu.VMEM)
-    operands = [me, slots, *rows] + ([] if held is None else [held])
+    operands = [info, slots, *arrays] + ([] if held is None else [held])
     return pl.pallas_call(
-        functools.partial(place_kernel, sources=tuple(sources)),
+        functools.partial(
+            place_kernel, origins=tuple(origins), groups=groups, arrays=len(arrays)
+        ),
         in_specs=[smem, smem] + [vmem] * (len(operands) - 2),
         out_specs=[vmem, vmem],
         out_shape=[
@@ -258,21 +277,24 @@
             jax.ShapeDtypeStruct((8, 128), jnp.float32),
         ],
         input_output_aliases={} if held is None else {len(operands) - 1: 0},
-        scratch_shapes=[pltpu.VMEM((2 * run * len(sources), 128), jnp.float32)],
-        compiler_params=pltpu.CompilerParams(vmem_limit_bytes=VMEM_BYTES),
-        cost_estimate=pl.CostEstimate(
-            flops=10 * len(sources) * run * width,
-            bytes_accessed=16 * len(sources) * run * width,
-            transcendentals=0,
-        ),
+        scratch_shapes=[pltpu.VMEM((2 * run, 128), jnp.float32)],
+        compiler_params=pltpu.CompilerParams(vmem_limit_bytes=4 * MIB),
+        cost_estimate=COST,
         name="place_rows",
     )(*operands)
 
 
-def blend_kernel(w_ref, held_ref, o_ref):
+def blend_kernel(info_ref, slot_ref, w_ref, *refs, origins, groups, arrays):
+    o_ref, held_ref, stage_ref = refs[-3:]
+    step = pl.program_id(0)
+    tile = w_ref.shape[0]
+
+    @pl.when(step == 0)
+    def _():
+        place_runs(info_ref, slot_ref, refs[:arrays], origins, groups, held_ref, stage_ref)
+
     wwide, _ = unit_rows(w_ref[...].astype(jnp.float32))
-    tile = w_ref.shape[0]
-    first = pl.multiple_of(pl.program_id(0) * 2 * tile, 2 * tile)
+    first = pl.multiple_of(step * 2 * tile, 2 * tile)
     low = wwide[:, :128] + held_ref[pl.ds(first, tile, stride=2), :]
     high = wwide[:, 128:] + held_ref[pl.ds(first + 1, tile, stride=2), :]
     square = jnp.sum(low * low + high * high, axis=1, keepdims=True)
@@ -281,26 +303,32 @@
     o_ref[:, 128:] = (high * inv).astype(jnp.bfloat16)
 
 
-def blend(weights, held):
+def place_and_blend(info, slots, arrays, origins, groups, held, weights, run):
     classes, width = weights.shape
     tile = math.gcd(classes, 1024)
-    return pl.pallas_call(
-        blend_kernel,
+    smem = pl.BlockSpec(memory_space=pltpu.SMEM)
+    vmem = pl.BlockSpec(memory_space=pltpu.VMEM)
+    tiles = pl.BlockSpec((tile, width), lambda i: (i, 0))
+    refreshed, _ = pl.pallas_call(
+        functools.partial(
+            blend_kernel, origins=tuple(origins), groups=groups, arrays=len(arrays)
+        ),
         grid=(classes // tile,),
-        in_specs=[
-            pl.BlockSpec((tile, width), lambda i: (i, 0)),
-            pl.BlockSpec(memory_space=pltpu.VMEM),
-        ],
-        out_specs=pl.BlockSpec((tile, width), lambda i: (i, 0)),
-        out_shape=jax.ShapeDtypeStruct((classes, width), jnp.bfloat16),
+        in_specs=[smem, smem, tiles] + [vmem] * (len(arrays) + 1),
+        out_specs=[tiles, vmem],
+        out_shape=[
+            jax.ShapeDtypeStruct((classes, width), jnp.bfloat16),
+            jax.ShapeDtypeStruct(held.shape, held.dtype),
+        ],
+        input_output_aliases={3 + len(arrays): 1},
+        scratch_shapes=[pltpu.VMEM((2 * run, 128), jnp.float32)],
         compiler_params=pltpu.CompilerParams(
-            dimension_semantics=("arbitrary",), vmem_limit_bytes=VMEM_BYTES
-        ),
-        cost_estimate=pl.CostEstimate(
-            flops=10 * classes * width, bytes_accessed=classes * width * 8, transcendentals=classes
-        ),
-        name="blend",
-    )(weights, held)
+            dimension_semantics=("arbitrary",), vmem_limit_bytes=10 * MIB
+        ),
+        cost_estimate=COST,
+        name="place_and_blend",
+    )(info, slots, weights, *arrays, held)
+    return refreshed
 
 
 def shards(embeddings, labels, class_weights, centroids, centroid_class):
@@ -314,35 +342,50 @@
     grp, rep = lax.axis_index("grp").astype(jnp.int32), lax.axis_index("rep").astype(jnp.int32)
     me = rep * groups + grp
     base, me = (me * classes).reshape(1), me.reshape(1)
+    info = jnp.stack([rep, grp])
     at = lambda d: d % groups * reps + d // groups
 
-    def exchange(value, k):
+    def over_rep(value, k):
+        return lax.ppermute(value, "rep", [(i, i ^ k) for i in range(reps)])
+
+    def over_all(value, k):
         return lax.ppermute(value, ("grp", "rep"), [(at(d), at(d ^ k)) for d in range(peers)])
 
-    blocks = [embeddings] + [
-        lax.ppermute(embeddings, "rep", [(i, i ^ k) for i in range(reps)]) for k in range(1, reps)
-    ]
-    far, near = list(range(peers // 2, peers)), list(range(1, peers // 2))
-    order = [k for pair in zip(far, near) for k in pair] + far[len(near) :]
-    cuts = [0] + [round(len(order) * c / 31) for c in (5, 12, 19, 26, 31)]
-    plan = [order[i:j] for i, j in zip(cuts, cuts[1:])]
-
-    def send(group, tokens):
-        fetched = fetch_runs(me, centroids, run, plan[group], tokens)
-        return [exchange(value, k) for value, k in zip(fetched, plan[group])]
-
-    got = [send(0, [])]
+    def hop(picks, tokens):
+        fetched = fetch(rep.reshape(1), centroids, groups * run, picks, tokens)
+        return {k: over_rep(value, k) if k else value for k, value in zip(picks, fetched)}
+
+    def spread(held_rows, picks):
+        parts = [held_rows[k].reshape(groups, run, width) for k in picks]
+        parts = lax.all_to_all(jnp.concatenate(parts, axis=1), "grp", 0, 0, tiled=True)
+        origins = [(k, 0, g) for g in range(groups) for k in picks]
+        return parts.reshape(-1, width), origins
+
+    def direct(picks, tokens):
+        fetched = fetch(me, centroids, run, picks, tokens)
+        rows = [over_all(value, k) for k, value in zip(picks, fetched)]
+        return rows, [(k // groups, k % groups, None) for k in picks]
+
+    half = reps // 2
+    far, near = list(range(peers // 2, peers)), list(range(1, half))
+    cuts = [round(len(far) * c / 16) for c in (0, 5, 9, 13, 16)]
+    plan = [far[i:j] for i, j in zip(cuts, cuts[1:])]
+
+    blocks = [embeddings] + [over_rep(embeddings, k) for k in range(1, reps)]
+    rows0, from0 = direct(plan[0], [blocks[1]])
     emb, a, b, stats = forward(base, rep.reshape(1), blocks, labels, class_weights)
-    got.append(send(1, [stats]))
-
+    moved = hop(near, [stats])
+    moved |= hop([0], [stats])
+    rows1, from1 = direct(plan[1], [stats])
+
+    tied = tie(stats, rows0[:3])
     flat = [
-        jnp.broadcast_to(stats[0][None], (peers, batch)),
+        jnp.broadcast_to(tied[0][None], (peers, batch)),
         centroid_class.reshape(peers, run).astype(jnp.float32),
-        jnp.repeat(stats[1].reshape(reps, rows_local), groups, axis=0),
+        jnp.repeat(tied[1].reshape(reps, rows_local), groups, axis=0),
     ]
     size = batch + run + rows_local
-    pad = -size % 1024
-    flat = jnp.pad(jnp.concatenate(flat, axis=1), ((0, 0), (0, pad)))
+    flat = jnp.pad(jnp.concatenate(flat, axis=1), ((0, 0), (0, -size % 1024)))
     flat = lax.all_to_all(flat.reshape(peers, -1, 128), ALL, 0, 0, tiled=True).reshape(peers, -1)
     total = jnp.sum(flat[:, :batch], axis=0)
     slots = flat[:, batch : batch + run].reshape(-1).astype(jnp.int32)
@@ -350,6 +393,9 @@
     own_total = lax.dynamic_slice_in_dim(total, rep * rows_local, rows_local, 0)
     loss = SCALE + jnp.log(own_total) - target
 
+    weight_grad = weight_gradient(base, emb, labels, stats, total, class_weights)
+    rows2, from2 = direct(plan[2], [weight_grad])
+
     grad = a / total[:, None] - b
     parts = lax.all_to_all(grad.reshape(peers, share, width), ALL, 0, 0, tiled=True)
     own = jnp.sum(parts, axis=0)
@@ -357,16 +403,14 @@
         jnp.broadcast_to(own[None], (groups, share, width)), "grp", 0, 0, tiled=True
     ).reshape(rows_local, width)
 
-    weight_grad = weight_gradient(base, emb, labels, stats, total, class_weights)
-    mine = list(fetch_runs(me, centroids, run, [0], [stats]))
-    held, token = place_rows(me, slots, got[0] + mine, plan[0] + [0], None, classes)
-    tokens = [token, weight_grad]
-    for group in range(1, len(plan)):
-        if group + 1 < len(plan):
-            got.append(send(group + 1, tokens))
-        held, token = place_rows(me, slots, got[group], plan[group], held, classes)
-        tokens = [token]
-    return (loss, embedding_gradient, weight_grad, blend(class_weights, held))
+    held, token = place_rows(info, slots, rows0 + rows1, from0 + from1, groups, None, classes, run)
+    rows3, from3 = direct(plan[3], [token])
+    rows, origins = spread(moved, [0] + near)
+    held, _ = place_rows(
+        info, slots, [rows, *rows2], origins + from2, groups, held, classes, run
+    )
+    refreshed = place_and_blend(info, slots, rows3, from3, groups, held, class_weights, run)
+    return (loss, embedding_gradient, weight_grad, refreshed)
 
 
 def solution(mesh):

time: 324 us -> 198 us (0.61)
  the two profiles are of different devices: /device:TPU:0 before, /device:TPU:9 now
where the time goes in v4:
time: 198 us; the launch traced here: 197 us
  starting transfers between devices  56.5 us (29%)
  Pallas kernels  47.1 us (24%)
  waiting for transfers between devices  42.2 us (21%)
  local copies, waits for them, and re-layouts  29.4 us (15%)
  blocking collectives  13.1 us (7%)
  other arithmetic  7.81 us (4%)
    ppermute x16, starting transfers between devices, over_all(): lax.ppermute(value, ('grp', 'rep'), [(at(d), at(d ^ k)) for d in range(pe...  32.1 us
    ppermute x16, waiting for transfers between devices, over_all(): lax.ppermute(value, ('grp', 'rep'), [(at(d), at(d ^ k)) for d in range(pe...  29.5 us
    unnamed x45, local copies, waits for them, and re-layouts  27.8 us
    pallas_call x2, Pallas kernels, place_rows(): pl.pallas_call(functools.partial(place_kernel, origins=tuple(origins), gr...  14.7 us
    all_to_all x1, blocking collectives, shards(): lax.all_to_all(flat.reshape(peers, -1, 128), ALL, 0, 0, tiled=True)  13.1 us
    ppermute x10, starting transfers between devices, over_rep(): return lax.ppermute(value, 'rep', [(i, i ^ k) for i in range(reps)])  11.8 us
    pallas_call x1, Pallas kernels, forward(): pl.pallas_call(functools.partial(forward_kernel, classes=classes, reps=re...  11.6 us
    ppermute x10, waiting for transfers between devices, over_rep(): return lax.ppermute(value, 'rep', [(i, i ^ k) for i in range(reps)])  11.5 us
  transfers between devices with their start and end apart: 29, of which 8 were waited for; matrix products, arithmetic and copies ran while one was open for 4% of the time, Pallas kernels for 20%

profile of v4, /device:TPU:9, one launch (start us, length us, event | category | flops | bytes accessed | tf_op | source)
XLA Modules:
  0.0 197.0 jit_solution(14839709928993501986)
XLA Ops:
  0.6 1.4 collective-permute-start.5
  2.0 1.0 collective-permute-start
  3.0 0.8 collective-permute-start.4
  3.7 1.5 collective-permute-start.3
  5.2 2.9 %collective-permute-start.2 = (bf16[64,256]{1,0:T(8,128)(2,1)}, bf16[64,256]{1,0:T(8,128)(2,1)S(1)}, u32[]{:S(2)}, u32[]{:S(2)}) collective-permute-start(bf16[64,256]{1,0:T(8,128)(2,1)} %refs_0_.1), channel_id=1, source_target_pairs={{0,3},{1,2},{2,1},{3,0},{4,7},{5,6},{6,5},{7,4},{8,11},{9,10},{10,... | collective-permute-start | bytes 98312 | tf_op jit(solution)/shard_map/ppermute | solution.py:349
  8.1 2.2 %collective-permute-start.6 = (bf16[64,256]{1,0:T(8,128)(2,1)}, bf16[64,256]{1,0:T(8,128)(2,1)S(1)}, u32[]{:S(2)}, u32[]{:S(2)}) collective-permute-start(bf16[64,256]{1,0:T(8,128)(2,1)} %refs_0_.1), channel_id=1, source_target_pairs={{0,7},{1,6},{2,5},{3,4},{4,3},{5,2},{6,1},{7,0},{8,15},{9,14},{10,... | collective-permute-start | bytes 98312 | tf_op jit(solution)/shard_map/ppermute | solution.py:349
  10.3 0.8 convert_element_type.13
  11.1 0.8 copy.12.lab_ref
  11.9 2.2 %copy-done = bf16[8192,256]{1,0:T(8,128)(2,1)S(1)} copy-done((bf16[8192,256]{1,0:T(8,128)(2,1)S(1)}, bf16[8192,256]{1,0:T(8,128)(2,1)}, u32[]{:S(2)}) %copy-start) | copy-done | bytes 4194328
  14.1 0.9 fetch.6
  15.0 1.3 collective-permute-start.7
  16.3 2.0 %collective-permute-start.8 = (bf16[256,256]{1,0:T(8,128)(2,1)S(1)}, bf16[256,256]{1,0:T(8,128)(2,1)S(1)}, u32[]{:S(2)}, u32[]{:S(2)}) collective-permute-start(bf16[256,256]{1,0:T(8,128)(2,1)S(1)} %get-tuple-element.33), channel_id=1, source_target_pairs={{0,12},{8,4},{16,28},{24,20},{1,13},{9,5},{17,29},{25,21},{2,14},{... | collective-permute-start | bytes 393224 | tf_op jit(solution)/shard_map/ppermute | solution.py:352
  18.3 2.2 %collective-permute-start.9 = (bf16[256,256]{1,0:T(8,128)(2,1)S(1)}, bf16[256,256]{1,0:T(8,128)(2,1)S(1)}, u32[]{:S(2)}, u32[]{:S(2)}) collective-permute-start(bf16[256,256]{1,0:T(8,128)(2,1)S(1)} %get-tuple-element.34), channel_id=1, source_target_pairs={{0,20},{8,28},{16,4},{24,12},{1,21},{9,29},{17,5},{25,13},{2,22},{... | collective-permute-start | bytes 393224 | tf_op jit(solution)/shard_map/ppermute | solution.py:352
  20.6 11.6 %forward_sums.1 = (bf16[512,256]{1,0:T(8,128)(2,1)S(1)}, f32[512,256]{1,0:T(8,128)S(1)}, f32[512,256]{1,0:T(8,128)S(1)}, f32[8,512]{1,0:T(8,128)S(1)}) custom-call(s32[1]{0:T(128)} %bitcast.base_ref, s32[1]{0:T(128)} %bitcast.1.rep_ref.me_ref, s32[512,1]{1,0:T(8,128)S(1)} %copy.12.lab_ref, bf16[8192,256]{1,0:T(8,128)(2,1)S(1)} %copy-done.9, ...), custom_call_target="tpu_custom_call" | custom-call | flops 12884901888 | bytes 4194304 | tf_op jit(solution)/shard_map/forward_sums/pallas_call | solution.py:101
  32.2 0.6 collective-permute-done.9.refs_2_
  33.0 13.1 %all_to_all.20 = f32[32,8,128]{2,1,0:T(8,128)S(1)} all-to-all(f32[32,8,128]{2,1,0:T(8,128)S(1)} %bitcast.34), channel_id=1, replica_groups=mesh['grp'=4,'rep'=8] {'rep','grp'}, dimensions={0} | all-to-all | bytes 262144 | tf_op jit(solution)/shard_map/all_to_all | solution.py:389
  46.1 0.9 divide_subtract_fusion
  47.0 5.3 %all-to-all-start.1 = ((f32[32,16,256]{2,1,0:T(8,128)}), f32[32,16,256]{2,1,0:T(8,128)}, u32[]{:S(2)}, u32[]{:S(2)}) async-start(f32[32,16,256]{2,1,0:T(8,128)} %bitcast.6), calls=%async_computation.1 | async-start | bytes 1048576 | tf_op jit(solution)/shard_map/all_to_all | solution.py:400
  52.3 2.2 %copy-done.1 = bf16[8192,256]{1,0:T(8,128)(2,1)S(1)} copy-done((bf16[8192,256]{1,0:T(8,128)(2,1)S(1)}, bf16[8192,256]{1,0:T(8,128)(2,1)}, u32[]{:S(2)}) %copy-start.1) | copy-done | bytes 4194328
  54.7 0.4 collective-permute-start.19
  55.2 1.6 collective-permute-start.21
  57.0 2.2 %copy-done.2 = bf16[8192,256]{1,0:T(8,128)(2,1)S(1)} copy-done((bf16[8192,256]{1,0:T(8,128)(2,1)S(1)}, bf16[8192,256]{1,0:T(8,128)(2,1)}, u32[]{:S(2)}) %copy-start.2) | copy-done | bytes 4194328
  59.2 1.4 fetch.7
  60.6 0.6 copy-done.13
  61.2 4.1 %collective-permute-start.10 = (bf16[256,256]{1,0:T(8,128)(2,1)S(1)}, bf16[256,256]{1,0:T(8,128)(2,1)S(1)}, u32[]{:S(2)}, u32[]{:S(2)}) collective-permute-start(bf16[256,256]{1,0:T(8,128)(2,1)S(1)} %get-tuple-element.38), channel_id=1, source_target_pairs={{0,28},{8,20},{16,12},{24,4},{1,29},{9,21},{17,13},{25,5},{2,30},{... | collective-permute-start | bytes 393224 | tf_op jit(solution)/shard_map/ppermute | solution.py:352
  65.3 0.4 collective-permute-start.11
  65.7 1.2 all-to-all-done.1
  66.9 1.1 reduce_sum.29
  68.0 0.6 broadcast_in_dim.20
  68.7 3.3 %all-to-all-start.2 = ((f32[4,16,256]{2,1,0:T(8,128)}), f32[4,16,256]{2,1,0:T(8,128)S(1)}, u32[]{:S(2)}, u32[]{:S(2)}) async-start(f32[4,16,256]{2,1,0:T(8,128)} %broadcast_in_dim.20), calls=%async_computation.2 | async-start | bytes 131072 | tf_op jit(solution)/shard_map/all_to_all | solution.py:402
  72.0 3.4 %collective-permute-start.12 = (bf16[256,256]{1,0:T(8,128)(2,1)}, bf16[256,256]{1,0:T(8,128)(2,1)S(1)}, u32[]{:S(2)}, u32[]{:S(2)}) collective-permute-start(bf16[256,256]{1,0:T(8,128)(2,1)} %get-tuple-element.40), channel_id=1, source_target_pairs={{0,13},{8,5},{16,29},{24,21},{1,12},{9,4},{17,28},{25,20},{2,15},{... | collective-permute-start | bytes 393224 | tf_op jit(solution)/shard_map/ppermute | solution.py:352
  75.4 5.1 %collective-permute-done.20 = bf16[1024,256]{1,0:T(8,128)(2,1)} collective-permute-done((bf16[1024,256]{1,0:T(8,128)(2,1)S(1)}, bf16[1024,256]{1,0:T(8,128)(2,1)}, u32[]{:S(2)}, u32[]{:S(2)}) %collective-permute-start.20) | collective-permute-done | bytes 524320 | tf_op jit(solution)/shard_map/ppermute | solution.py:349
  80.5 5.1 %collective-permute-start.13 = (bf16[256,256]{1,0:T(8,128)(2,1)}, bf16[256,256]{1,0:T(8,128)(2,1)S(1)}, u32[]{:S(2)}, u32[]{:S(2)}) collective-permute-start(bf16[256,256]{1,0:T(8,128)(2,1)} %copy-done.15), channel_id=1, source_target_pairs={{0,21},{8,29},{16,5},{24,13},{1,20},{9,28},{17,4},{25,12},{2,23},{... | collective-permute-start | bytes 393224 | tf_op jit(solution)/shard_map/ppermute | solution.py:352
  85.6 6.4 %collective-permute-done.21 = bf16[1024,256]{1,0:T(8,128)(2,1)} collective-permute-done((bf16[1024,256]{1,0:T(8,128)(2,1)S(1)}, bf16[1024,256]{1,0:T(8,128)(2,1)}, u32[]{:S(2)}, u32[]{:S(2)}) %collective-permute-start.21) | collective-permute-done | bytes 524320 | tf_op jit(solution)/shard_map/ppermute | solution.py:349
  92.0 2.8 %pad_maximum_fusion = bf16[4,1024,256]{2,1,0:T(8,128)(2,1)} fusion(bf16[4,256,256]{2,1,0:T(8,128)(2,1)} %bitcast.14, bf16[4,256,256]{2,1,0:T(8,128)(2,1)} %bitcast.13, bf16[4,256,256]{2,1,0:T(8,128)(2,1)} %bitcast.12, bf16[4,256,256]{2,1,0:T(8,128)(2,1)S(1)} %bitcast.27), kind=kLoop, calls=%fused_computation | loop fusion | flops 8388608 | bytes 4194304 | tf_op jit(solution)/shard_map/concatenate | solution.py:360
  94.8 4.0 %all-to-all-start.3 = ((bf16[4,1024,256]{2,1,0:T(8,128)(2,1)}), bf16[4,1024,256]{2,1,0:T(8,128)(2,1)S(1)}, u32[]{:S(2)}, u32[]{:S(2)}) async-start(bf16[4,1024,256]{2,1,0:T(8,128)(2,1)} %pad_maximum_fusion), calls=%async_computation.3 | async-start | bytes 4194304 | tf_op jit(solution)/shard_map/all_to_all | solution.py:360
  98.8 2.2 %copy-done.10 = bf16[8192,256]{1,0:T(8,128)(2,1)S(1)} copy-done((bf16[8192,256]{1,0:T(8,128)(2,1)S(1)}, bf16[8192,256]{1,0:T(8,128)(2,1)}, u32[]{:S(2)}) %copy-start.10) | copy-done | bytes 4194328
  101.0 0.9 copy-done.18
  102.0 9.5 %weight_gradient.1.refs_0_ = f32[8192,256]{1,0:T(8,128)} custom-call(s32[1]{0:T(128)} %bitcast.base_ref, bf16[512,256]{1,0:T(8,128)(2,1)S(1)} %copy-done.18, s32[1,512]{1,0:T(1,128)S(1)} %bitcast.33, f32[8,512]{1,0:T(8,128)S(1)} %get-tuple-element.31.value_ref.st_ref.refs_0_, f32[1,512]{1,0:T(1,128)S(1)} %bitcast.31, bf16[8192,256]{1,0:T(8,128)(2,1)S(1)} %copy-done.10), custom_call_target="tpu_custom_call" | custom-call | flops 12884901888 | bytes 12582912 | tf_op jit(solution)/shard_map/weight_gradient/pallas_call | solution.py:164
  111.5 5.8 %collective-permute-start.14 = (bf16[256,256]{1,0:T(8,128)(2,1)S(1)}, bf16[256,256]{1,0:T(8,128)(2,1)S(1)}, u32[]{:S(2)}, u32[]{:S(2)}) collective-permute-start(bf16[256,256]{1,0:T(8,128)(2,1)S(1)} %copy-done.14), channel_id=1, source_target_pairs={{0,29},{8,21},{16,13},{24,5},{1,28},{9,20},{17,12},{25,4},{2,31},{... | collective-permute-start | bytes 393224 | tf_op jit(solution)/shard_map/ppermute | solution.py:352
  117.3 3.4 %copy-done.8 = f32[8192,256]{1,0:T(8,128)S(1)} copy-done((f32[8192,256]{1,0:T(8,128)S(1)}, f32[8192,256]{1,0:T(8,128)}, u32[]{:S(2)}) %copy-start.8) | copy-done | bytes 8388632
  120.6 0.7 fetch.11
  121.3 0.7 collective-permute-start.15
  122.1 0.8 collective-permute-start.22
  123.0 0.8 fusion
  123.8 11.4 %collective-permute-done.15.refs_8_ = bf16[256,256]{1,0:T(8,128)(2,1)S(1)} collective-permute-done((bf16[256,256]{1,0:T(8,128)(2,1)S(1)}, bf16[256,256]{1,0:T(8,128)(2,1)S(1)}, u32[]{:S(2)}, u32[]{:S(2)}) %collective-permute-start.15) | collective-permute-done | bytes 131104 | tf_op jit(solution)/shard_map/ppermute | solution.py:352
  135.1 4.8 %place_rows.2 = (f32[16384,128]{1,0:T(8,128)S(1)}, f32[8,128]{1,0:T(8,128)S(1)}) custom-call(s32[2]{0:T(128)S(1)} %pad_add_fusion.info_ref, s32[8192]{0:T(1024)S(1)} %bitcast.28, bf16[256,256]{1,0:T(8,128)(2,1)S(1)} %collective-permute-done.7.refs_0_, bf16[256,256]{1,0:T(8,128)(2,1)S(1)} %collective-permute-done.8.refs_1_, ...), custom_call_target="tpu_custom_call" | custom-call | flops 1 | bytes 1 | tf_op jit(solution)/shard_map/place_rows/pallas_call | solution.py:269
  140.0 3.3 %copy-done.4 = f32[16384,128]{1,0:T(8,128)} copy-done((f32[16384,128]{1,0:T(8,128)}, f32[16384,128]{1,0:T(8,128)S(1)}, u32[]{:S(2)}) %copy-start.4) | copy-done | bytes 8388632
  143.2 0.5 fetch.8
  143.8 1.2 collective-permute-start.16
  145.2 3.1 %collective-permute-start.18 = (bf16[256,256]{1,0:T(8,128)(2,1)S(1)}, bf16[256,256]{1,0:T(8,128)(2,1)S(1)}, u32[]{:S(2)}, u32[]{:S(2)}) collective-permute-start(bf16[256,256]{1,0:T(8,128)(2,1)S(1)} %get-tuple-element.47), channel_id=1, source_target_pairs={{0,31},{8,23},{16,15},{24,7},{1,30},{9,22},{17,14},{25,6},{2,29},{... | collective-permute-start | bytes 393224 | tf_op jit(solution)/shard_map/ppermute | solution.py:352
  148.3 0.7 slice_reduce_fusion.1
  149.1 0.5 collective-permute-start.24
  149.6 5.2 %collective-permute-done.23.refs_2_ = bf16[256,256]{1,0:T(8,128)(2,1)S(1)} collective-permute-done((bf16[256,256]{1,0:T(8,128)(2,1)S(1)}, bf16[256,256]{1,0:T(8,128)(2,1)S(1)}, u32[]{:S(2)}, u32[]{:S(2)}) %collective-permute-start.23) | collective-permute-done | bytes 131104 | tf_op jit(solution)/shard_map/ppermute | solution.py:352
  154.8 1.1 collective-permute-start.25
  155.9 0.6 add_subtract_fusion
  156.5 9.8 %collective-permute-done.24.refs_3_ = bf16[256,256]{1,0:T(8,128)(2,1)S(1)} collective-permute-done((bf16[256,256]{1,0:T(8,128)(2,1)S(1)}, bf16[256,256]{1,0:T(8,128)(2,1)S(1)}, u32[]{:S(2)}, u32[]{:S(2)}) %collective-permute-start.24) | collective-permute-done | bytes 131104 | tf_op jit(solution)/shard_map/ppermute | solution.py:352
  166.3 2.5 %collective-permute-done.25.refs_4_ = bf16[256,256]{1,0:T(8,128)(2,1)S(1)} collective-permute-done((bf16[256,256]{1,0:T(8,128)(2,1)S(1)}, bf16[256,256]{1,0:T(8,128)(2,1)S(1)}, u32[]{:S(2)}, u32[]{:S(2)}) %collective-permute-start.25) | collective-permute-done | bytes 131104 | tf_op jit(solution)/shard_map/ppermute | solution.py:352
  168.8 3.4 %copy-done.5 = f32[16384,128]{1,0:T(8,128)S(1)} copy-done((f32[16384,128]{1,0:T(8,128)S(1)}, f32[16384,128]{1,0:T(8,128)}, u32[]{:S(2)}) %copy-start.5) | copy-done | bytes 8388632
  172.2 9.9 %place_rows.3 = (f32[16384,128]{1,0:T(8,128)S(1)}, f32[8,128]{1,0:T(8,128)}) custom-call(s32[2]{0:T(128)S(1)} %pad_add_fusion.info_ref, s32[8192]{0:T(1024)S(1)} %bitcast.29, bf16[4096,256]{1,0:T(8,128)(2,1)S(1)} %bitcast.26, bf16[256,256]{1,0:T(8,128)(2,1)S(1)} %collective-permute-done.22.refs_1_, ...), custom_call_target="tpu_custom_call", output_to_operand_aliasing={{0}: (7, {})} | custom-call | flops 1 | bytes 1 | tf_op jit(solution)/shard_map/place_rows/pallas_call | solution.py:269
  182.1 3.3 %copy-done.6 = f32[16384,128]{1,0:T(8,128)} copy-done((f32[16384,128]{1,0:T(8,128)}, f32[16384,128]{1,0:T(8,128)S(1)}, u32[]{:S(2)}) %copy-start.6) | copy-done | bytes 8388632
  185.4 3.4 %copy-done.7 = f32[16384,128]{1,0:T(8,128)S(1)} copy-done((f32[16384,128]{1,0:T(8,128)S(1)}, f32[16384,128]{1,0:T(8,128)}, u32[]{:S(2)}) %copy-start.7) | copy-done | bytes 8388632
  188.8 7.6 %place_and_blend.1 = (bf16[8192,256]{1,0:T(8,128)(2,1)}, f32[16384,128]{1,0:T(8,128)S(1)}) custom-call(s32[2]{0:T(128)S(1)} %pad_add_fusion.info_ref, s32[8192]{0:T(1024)S(1)} %bitcast.30, bf16[8192,256]{1,0:T(8,128)(2,1)S(1)} %copy-done.11, bf16[256,256]{1,0:T(8,128)(2,1)S(1)} %collective-permute-done.16.refs_0_, ...), custom_call_target="tpu_custom_call", output_to_operand_aliasing={{1}: (6, {})} | custom-call | flops 1 | bytes 1 | tf_op jit(solution)/shard_map/place_and_blend/pallas_call | solution.py:312
  196.4 0.6 copy.21
  (69 shorter events, 1.1 us)
Async XLA Ops:
  0.6 19.9 %copy-start.16 = (bf16[64,256]{1,0:T(8,128)(2,1)S(1)}, bf16[64,256]{1,0:T(8,128)(2,1)}, u32[]{:S(2)}) copy-start(bf16[64,256]{1,0:T(8,128)(2,1)} %refs_0_.1) | copy-start | bytes 98308
  0.6 7.4 %collective-permute-start.5 = (bf16[64,256]{1,0:T(8,128)(2,1)}, bf16[64,256]{1,0:T(8,128)(2,1)S(1)}, u32[]{:S(2)}, u32[]{:S(2)}) collective-permute-start(bf16[64,256]{1,0:T(8,128)(2,1)} %refs_0_.1), channel_id=1, source_target_pairs={{0,6},{1,7},{2,4},{3,5},{4,2},{5,3},{6,0},{7,1},{8,14},{9,15},{10,... | collective-permute-start | bytes 98312 | tf_op jit(solution)/shard_map/ppermute | solution.py:349
  2.0 6.1 %collective-permute-start = (bf16[64,256]{1,0:T(8,128)(2,1)}, bf16[64,256]{1,0:T(8,128)(2,1)S(1)}, u32[]{:S(2)}, u32[]{:S(2)}) collective-permute-start(bf16[64,256]{1,0:T(8,128)(2,1)} %refs_0_.1), channel_id=1, source_target_pairs={{0,1},{1,0},{2,3},{3,2},{4,5},{5,4},{6,7},{7,6},{8,9},{9,8},{10,11... | collective-permute-start | bytes 98312 | tf_op jit(solution)/shard_map/ppermute | solution.py:349
  3.0 12.0 %collective-permute-start.4 = (bf16[64,256]{1,0:T(8,128)(2,1)}, bf16[64,256]{1,0:T(8,128)(2,1)S(1)}, u32[]{:S(2)}, u32[]{:S(2)}) collective-permute-start(bf16[64,256]{1,0:T(8,128)(2,1)} %refs_0_.1), channel_id=1, source_target_pairs={{0,5},{1,4},{2,7},{3,6},{4,1},{5,0},{6,3},{7,2},{8,13},{9,12},{10,... | collective-permute-start | bytes 98312 | tf_op jit(solution)/shard_map/ppermute | solution.py:349
  3.7 12.6 %collective-permute-start.3 = (bf16[64,256]{1,0:T(8,128)(2,1)}, bf16[64,256]{1,0:T(8,128)(2,1)S(1)}, u32[]{:S(2)}, u32[]{:S(2)}) collective-permute-start(bf16[64,256]{1,0:T(8,128)(2,1)} %refs_0_.1), channel_id=1, source_target_pairs={{0,4},{1,5},{2,6},{3,7},{4,0},{5,1},{6,2},{7,3},{8,12},{9,13},{10,... | collective-permute-start | bytes 98312 | tf_op jit(solution)/shard_map/ppermute | solution.py:349
  5.2 13.1 %collective-permute-start.2 = (bf16[64,256]{1,0:T(8,128)(2,1)}, bf16[64,256]{1,0:T(8,128)(2,1)S(1)}, u32[]{:S(2)}, u32[]{:S(2)}) collective-permute-start(bf16[64,256]{1,0:T(8,128)(2,1)} %refs_0_.1), channel_id=1, source_target_pairs={{0,3},{1,2},{2,1},{3,0},{4,7},{5,6},{6,5},{7,4},{8,11},{9,10},{10,... | collective-permute-start | bytes 98312 | tf_op jit(solution)/shard_map/ppermute | solution.py:349
  8.1 12.5 %collective-permute-start.1 = (bf16[64,256]{1,0:T(8,128)(2,1)}, bf16[64,256]{1,0:T(8,128)(2,1)S(1)}, u32[]{:S(2)}, u32[]{:S(2)}) collective-permute-start(bf16[64,256]{1,0:T(8,128)(2,1)} %refs_0_.1), channel_id=1, source_target_pairs={{0,2},{1,3},{2,0},{3,1},{4,6},{5,7},{6,4},{7,5},{8,10},{9,11},{10,... | collective-permute-start | bytes 98312 | tf_op jit(solution)/shard_map/ppermute | solution.py:349
  8.1 12.5 %collective-permute-start.6 = (bf16[64,256]{1,0:T(8,128)(2,1)}, bf16[64,256]{1,0:T(8,128)(2,1)S(1)}, u32[]{:S(2)}, u32[]{:S(2)}) collective-permute-start(bf16[64,256]{1,0:T(8,128)(2,1)} %refs_0_.1), channel_id=1, source_target_pairs={{0,7},{1,6},{2,5},{3,4},{4,3},{5,2},{6,1},{7,0},{8,15},{9,14},{10,... | collective-permute-start | bytes 98312 | tf_op jit(solution)/shard_map/ppermute | solution.py:349
  11.9 2.2 %copy-start = (bf16[8192,256]{1,0:T(8,128)(2,1)S(1)}, bf16[8192,256]{1,0:T(8,128)(2,1)}, u32[]{:S(2)}) copy-start(bf16[8192,256]{1,0:T(8,128)(2,1)} %rows_ref.11) | copy-start | bytes 12582916
  14.1 6.5 %copy-start.9 = (bf16[8192,256]{1,0:T(8,128)(2,1)S(1)}, bf16[8192,256]{1,0:T(8,128)(2,1)}, u32[]{:S(2)}) copy-start(bf16[8192,256]{1,0:T(8,128)(2,1)} %w_ref.5) | copy-start | bytes 12582916
  15.0 17.2 %collective-permute-start.7 = (bf16[256,256]{1,0:T(8,128)(2,1)S(1)}, bf16[256,256]{1,0:T(8,128)(2,1)S(1)}, u32[]{:S(2)}, u32[]{:S(2)}) collective-permute-start(bf16[256,256]{1,0:T(8,128)(2,1)S(1)} %get-tuple-element.32), channel_id=1, source_target_pairs={{0,4},{8,12},{16,20},{24,28},{1,5},{9,13},{17,21},{25,29},{2,6},{1... | collective-permute-start | bytes 393224 | tf_op jit(solution)/shard_map/ppermute | solution.py:352
  16.3 15.9 %collective-permute-start.8 = (bf16[256,256]{1,0:T(8,128)(2,1)S(1)}, bf16[256,256]{1,0:T(8,128)(2,1)S(1)}, u32[]{:S(2)}, u32[]{:S(2)}) collective-permute-start(bf16[256,256]{1,0:T(8,128)(2,1)S(1)} %get-tuple-element.33), channel_id=1, source_target_pairs={{0,12},{8,4},{16,28},{24,20},{1,13},{9,5},{17,29},{25,21},{2,14},{... | collective-permute-start | bytes 393224 | tf_op jit(solution)/shard_map/ppermute | solution.py:352
  18.3 14.4 %collective-permute-start.9 = (bf16[256,256]{1,0:T(8,128)(2,1)S(1)}, bf16[256,256]{1,0:T(8,128)(2,1)S(1)}, u32[]{:S(2)}, u32[]{:S(2)}) collective-permute-start(bf16[256,256]{1,0:T(8,128)(2,1)S(1)} %get-tuple-element.34), channel_id=1, source_target_pairs={{0,20},{8,28},{16,4},{24,12},{1,21},{9,29},{17,5},{25,13},{2,22},{... | collective-permute-start | bytes 393224 | tf_op jit(solution)/shard_map/ppermute | solution.py:352
  32.2 14.8 %copy-start.17 = (bf16[512,256]{1,0:T(8,128)(2,1)}, bf16[512,256]{1,0:T(8,128)(2,1)S(1)}, u32[]{:S(2)}) copy-start(bf16[512,256]{1,0:T(8,128)(2,1)S(1)} %get-tuple-element.37.emb_ref) | copy-start | bytes 786436
  46.1 10.9 %copy-start.19 = (f32[4,8,8,128]{3,1,2,0:T(8,128)}, f32[4,8,8,128]{3,1,2,0:T(8,128)S(1)}, u32[]{:S(2)}) copy-start(f32[4,8,8,128]{3,1,2,0:T(8,128)S(1)} %copy.17) | copy-start | bytes 393220
  47.0 19.9 %all-to-all-start.1 = ((f32[32,16,256]{2,1,0:T(8,128)}), f32[32,16,256]{2,1,0:T(8,128)}, u32[]{:S(2)}, u32[]{:S(2)}) async-start(f32[32,16,256]{2,1,0:T(8,128)} %bitcast.6), calls=%async_computation.1 | async-start | bytes 1048576 | tf_op jit(solution)/shard_map/all_to_all | solution.py:400
  52.3 2.2 %copy-start.1 = (bf16[8192,256]{1,0:T(8,128)(2,1)S(1)}, bf16[8192,256]{1,0:T(8,128)(2,1)}, u32[]{:S(2)}) copy-start(bf16[8192,256]{1,0:T(8,128)(2,1)} %rows_ref.11) | copy-start | bytes 12582916
  54.7 17.3 %collective-permute-start.19 = (bf16[1024,256]{1,0:T(8,128)(2,1)S(1)}, bf16[1024,256]{1,0:T(8,128)(2,1)}, u32[]{:S(2)}, u32[]{:S(2)}) collective-permute-start(bf16[1024,256]{1,0:T(8,128)(2,1)S(1)} %get-tuple-element.48), channel_id=1, source_target_pairs={{0,1},{1,0},{2,3},{3,2},{4,5},{5,4},{6,7},{7,6},{8,9},{9,8},{10,11... | collective-permute-start | bytes 1572872 | tf_op jit(solution)/shard_map/ppermute | solution.py:349
  55.1 25.4 %collective-permute-start.20 = (bf16[1024,256]{1,0:T(8,128)(2,1)S(1)}, bf16[1024,256]{1,0:T(8,128)(2,1)}, u32[]{:S(2)}, u32[]{:S(2)}) collective-permute-start(bf16[1024,256]{1,0:T(8,128)(2,1)S(1)} %get-tuple-element.49), channel_id=1, source_target_pairs={{0,2},{1,3},{2,0},{3,1},{4,6},{5,7},{6,4},{7,5},{8,10},{9,11},{10,... | collective-permute-start | bytes 1572872 | tf_op jit(solution)/shard_map/ppermute | solution.py:349
  55.2 36.7 %collective-permute-start.21 = (bf16[1024,256]{1,0:T(8,128)(2,1)S(1)}, bf16[1024,256]{1,0:T(8,128)(2,1)}, u32[]{:S(2)}, u32[]{:S(2)}) collective-permute-start(bf16[1024,256]{1,0:T(8,128)(2,1)S(1)} %get-tuple-element.50), channel_id=1, source_target_pairs={{0,3},{1,2},{2,1},{3,0},{4,7},{5,6},{6,5},{7,4},{8,11},{9,10},{10,... | collective-permute-start | bytes 1572872 | tf_op jit(solution)/shard_map/ppermute | solution.py:349
  57.0 2.2 %copy-start.2 = (bf16[8192,256]{1,0:T(8,128)(2,1)S(1)}, bf16[8192,256]{1,0:T(8,128)(2,1)}, u32[]{:S(2)}) copy-start(bf16[8192,256]{1,0:T(8,128)(2,1)} %rows_ref.11) | copy-start | bytes 12582916
  60.6 0.6 copy-start.13
  61.2 4.1 %copy-start.15 = (bf16[256,256]{1,0:T(8,128)(2,1)}, bf16[256,256]{1,0:T(8,128)(2,1)S(1)}, u32[]{:S(2)}) copy-start(bf16[256,256]{1,0:T(8,128)(2,1)S(1)} %get-tuple-element.41) | copy-start | bytes 393220
  61.2 60.1 %collective-permute-start.10 = (bf16[256,256]{1,0:T(8,128)(2,1)S(1)}, bf16[256,256]{1,0:T(8,128)(2,1)S(1)}, u32[]{:S(2)}, u32[]{:S(2)}) collective-permute-start(bf16[256,256]{1,0:T(8,128)(2,1)S(1)} %get-tuple-element.38), channel_id=1, source_target_pairs={{0,28},{8,20},{16,12},{24,4},{1,29},{9,21},{17,13},{25,5},{2,30},{... | collective-permute-start | bytes 393224 | tf_op jit(solution)/shard_map/ppermute | solution.py:352
  65.3 56.8 %collective-permute-start.11 = (bf16[256,256]{1,0:T(8,128)(2,1)S(1)}, bf16[256,256]{1,0:T(8,128)(2,1)S(1)}, u32[]{:S(2)}, u32[]{:S(2)}) collective-permute-start(bf16[256,256]{1,0:T(8,128)(2,1)S(1)} %get-tuple-element.39), channel_id=1, source_target_pairs={{0,5},{8,13},{16,21},{24,29},{1,4},{9,12},{17,20},{25,28},{2,7},{1... | collective-permute-start | bytes 393224 | tf_op jit(solution)/shard_map/ppermute | solution.py:352
  68.7 26.1 %all-to-all-start.2 = ((f32[4,16,256]{2,1,0:T(8,128)}), f32[4,16,256]{2,1,0:T(8,128)S(1)}, u32[]{:S(2)}, u32[]{:S(2)}) async-start(f32[4,16,256]{2,1,0:T(8,128)} %broadcast_in_dim.20), calls=%async_computation.2 | async-start | bytes 131072 | tf_op jit(solution)/shard_map/all_to_all | solution.py:402
  72.0 50.9 %collective-permute-start.12 = (bf16[256,256]{1,0:T(8,128)(2,1)}, bf16[256,256]{1,0:T(8,128)(2,1)S(1)}, u32[]{:S(2)}, u32[]{:S(2)}) collective-permute-start(bf16[256,256]{1,0:T(8,128)(2,1)} %get-tuple-element.40), channel_id=1, source_target_pairs={{0,13},{8,5},{16,29},{24,21},{1,12},{9,4},{17,28},{25,20},{2,15},{... | collective-permute-start | bytes 393224 | tf_op jit(solution)/shard_map/ppermute | solution.py:352
  80.5 43.3 %collective-permute-start.13 = (bf16[256,256]{1,0:T(8,128)(2,1)}, bf16[256,256]{1,0:T(8,128)(2,1)S(1)}, u32[]{:S(2)}, u32[]{:S(2)}) collective-permute-start(bf16[256,256]{1,0:T(8,128)(2,1)} %copy-done.15), channel_id=1, source_target_pairs={{0,21},{8,29},{16,5},{24,13},{1,20},{9,28},{17,4},{25,12},{2,23},{... | collective-permute-start | bytes 393224 | tf_op jit(solution)/shard_map/ppermute | solution.py:352
  92.0 6.9 %copy-start.12 = (s32[512]{0:T(512)S(1)}, s32[512]{0:T(512)}, u32[]{:S(2)}) copy-start(s32[512]{0:T(512)} %param.6) | copy-start | bytes 6148
  94.8 74.1 %all-to-all-start.3 = ((bf16[4,1024,256]{2,1,0:T(8,128)(2,1)}), bf16[4,1024,256]{2,1,0:T(8,128)(2,1)S(1)}, u32[]{:S(2)}, u32[]{:S(2)}) async-start(bf16[4,1024,256]{2,1,0:T(8,128)(2,1)} %pad_maximum_fusion), calls=%async_computation.3 | async-start | bytes 4194304 | tf_op jit(solution)/shard_map/all_to_all | solution.py:360
  98.8 2.2 %copy-start.10 = (bf16[8192,256]{1,0:T(8,128)(2,1)S(1)}, bf16[8192,256]{1,0:T(8,128)(2,1)}, u32[]{:S(2)}) copy-start(bf16[8192,256]{1,0:T(8,128)(2,1)} %w_ref.5) | copy-start | bytes 12582916
  101.0 0.9 copy-start.18
  102.0 9.5 %copy-start.14 = (bf16[256,256]{1,0:T(8,128)(2,1)S(1)}, bf16[256,256]{1,0:T(8,128)(2,1)}, u32[]{:S(2)}) copy-start(bf16[256,256]{1,0:T(8,128)(2,1)} %copy-done.13) | copy-start | bytes 393220
  102.0 15.3 %copy-start.3 = (bf16[8192,256]{1,0:T(8,128)(2,1)S(1)}, bf16[8192,256]{1,0:T(8,128)(2,1)}, u32[]{:S(2)}) copy-start(bf16[8192,256]{1,0:T(8,128)(2,1)} %rows_ref.11) | copy-start | bytes 12582916
  111.5 12.3 %collective-permute-start.14 = (bf16[256,256]{1,0:T(8,128)(2,1)S(1)}, bf16[256,256]{1,0:T(8,128)(2,1)S(1)}, u32[]{:S(2)}, u32[]{:S(2)}) collective-permute-start(bf16[256,256]{1,0:T(8,128)(2,1)S(1)} %copy-done.14), channel_id=1, source_target_pairs={{0,29},{8,21},{16,13},{24,5},{1,28},{9,20},{17,12},{25,4},{2,31},{... | collective-permute-start | bytes 393224 | tf_op jit(solution)/shard_map/ppermute | solution.py:352
  117.3 3.4 %copy-start.8 = (f32[8192,256]{1,0:T(8,128)S(1)}, f32[8192,256]{1,0:T(8,128)}, u32[]{:S(2)}) copy-start(f32[8192,256]{1,0:T(8,128)} %weight_gradient.1.refs_0_) | copy-start | bytes 25165828
  121.3 13.8 %collective-permute-start.15 = (bf16[256,256]{1,0:T(8,128)(2,1)S(1)}, bf16[256,256]{1,0:T(8,128)(2,1)S(1)}, u32[]{:S(2)}, u32[]{:S(2)}) collective-permute-start(bf16[256,256]{1,0:T(8,128)(2,1)S(1)} %get-tuple-element.43), channel_id=1, source_target_pairs={{0,6},{8,14},{16,22},{24,30},{1,7},{9,15},{17,23},{25,31},{2,4},{1... | collective-permute-start | bytes 393224 | tf_op jit(solution)/shard_map/ppermute | solution.py:352
  122.1 27.0 %collective-permute-start.22 = (bf16[256,256]{1,0:T(8,128)(2,1)S(1)}, bf16[256,256]{1,0:T(8,128)(2,1)S(1)}, u32[]{:S(2)}, u32[]{:S(2)}) collective-permute-start(bf16[256,256]{1,0:T(8,128)(2,1)S(1)} %get-tuple-element.51), channel_id=1, source_target_pairs={{0,14},{8,6},{16,30},{24,22},{1,15},{9,7},{17,31},{25,23},{2,12},{... | collective-permute-start | bytes 393224 | tf_op jit(solution)/shard_map/ppermute | solution.py:352
  122.9 31.9 %collective-permute-start.23 = (bf16[256,256]{1,0:T(8,128)(2,1)S(1)}, bf16[256,256]{1,0:T(8,128)(2,1)S(1)}, u32[]{:S(2)}, u32[]{:S(2)}) collective-permute-start(bf16[256,256]{1,0:T(8,128)(2,1)S(1)} %get-tuple-element.52), channel_id=1, source_target_pairs={{0,22},{8,30},{16,6},{24,14},{1,23},{9,31},{17,7},{25,15},{2,20},{... | collective-permute-start | bytes 393224 | tf_op jit(solution)/shard_map/ppermute | solution.py:352
  139.9 3.3 %copy-start.4 = (f32[16384,128]{1,0:T(8,128)}, f32[16384,128]{1,0:T(8,128)S(1)}, u32[]{:S(2)}) copy-start(f32[16384,128]{1,0:T(8,128)S(1)} %get-tuple-element.55.refs_5_) | copy-start | bytes 25165828
  143.8 41.7 %collective-permute-start.16 = (bf16[256,256]{1,0:T(8,128)(2,1)S(1)}, bf16[256,256]{1,0:T(8,128)(2,1)S(1)}, u32[]{:S(2)}, u32[]{:S(2)}) collective-permute-start(bf16[256,256]{1,0:T(8,128)(2,1)S(1)} %get-tuple-element.45), channel_id=1, source_target_pairs={{0,15},{8,7},{16,31},{24,23},{1,14},{9,6},{17,30},{25,22},{2,13},{... | collective-permute-start | bytes 393224 | tf_op jit(solution)/shard_map/ppermute | solution.py:352
  144.9 40.5 %collective-permute-start.17 = (bf16[256,256]{1,0:T(8,128)(2,1)S(1)}, bf16[256,256]{1,0:T(8,128)(2,1)S(1)}, u32[]{:S(2)}, u32[]{:S(2)}) collective-permute-start(bf16[256,256]{1,0:T(8,128)(2,1)S(1)} %get-tuple-element.46), channel_id=1, source_target_pairs={{0,23},{8,31},{16,7},{24,15},{1,22},{9,30},{17,6},{25,14},{2,21},{... | collective-permute-start | bytes 393224 | tf_op jit(solution)/shard_map/ppermute | solution.py:352
  145.2 40.2 %collective-permute-start.18 = (bf16[256,256]{1,0:T(8,128)(2,1)S(1)}, bf16[256,256]{1,0:T(8,128)(2,1)S(1)}, u32[]{:S(2)}, u32[]{:S(2)}) collective-permute-start(bf16[256,256]{1,0:T(8,128)(2,1)S(1)} %get-tuple-element.47), channel_id=1, source_target_pairs={{0,31},{8,23},{16,15},{24,7},{1,30},{9,22},{17,14},{25,6},{2,29},{... | collective-permute-start | bytes 393224 | tf_op jit(solution)/shard_map/ppermute | solution.py:352
  149.1 17.2 %collective-permute-start.24 = (bf16[256,256]{1,0:T(8,128)(2,1)S(1)}, bf16[256,256]{1,0:T(8,128)(2,1)S(1)}, u32[]{:S(2)}, u32[]{:S(2)}) collective-permute-start(bf16[256,256]{1,0:T(8,128)(2,1)S(1)} %get-tuple-element.53), channel_id=1, source_target_pairs={{0,30},{8,22},{16,14},{24,6},{1,31},{9,23},{17,15},{25,7},{2,28},{... | collective-permute-start | bytes 393224 | tf_op jit(solution)/shard_map/ppermute | solution.py:352
  154.8 14.0 %collective-permute-start.25 = (bf16[256,256]{1,0:T(8,128)(2,1)S(1)}, bf16[256,256]{1,0:T(8,128)(2,1)S(1)}, u32[]{:S(2)}, u32[]{:S(2)}) collective-permute-start(bf16[256,256]{1,0:T(8,128)(2,1)S(1)} %get-tuple-element.54), channel_id=1, source_target_pairs={{0,7},{8,15},{16,23},{24,31},{1,6},{9,14},{17,22},{25,30},{2,5},{1... | collective-permute-start | bytes 393224 | tf_op jit(solution)/shard_map/ppermute | solution.py:352
  168.8 3.4 %copy-start.5 = (f32[16384,128]{1,0:T(8,128)S(1)}, f32[16384,128]{1,0:T(8,128)}, u32[]{:S(2)}) copy-start(f32[16384,128]{1,0:T(8,128)} %copy-done.4) | copy-start | bytes 25165828
  172.2 13.2 %copy-start.11 = (bf16[8192,256]{1,0:T(8,128)(2,1)S(1)}, bf16[8192,256]{1,0:T(8,128)(2,1)}, u32[]{:S(2)}) copy-start(bf16[8192,256]{1,0:T(8,128)(2,1)} %w_ref.5) | copy-start | bytes 12582916
  182.1 3.3 %copy-start.6 = (f32[16384,128]{1,0:T(8,128)}, f32[16384,128]{1,0:T(8,128)S(1)}, u32[]{:S(2)}) copy-start(f32[16384,128]{1,0:T(8,128)S(1)} %get-tuple-element.56.refs_3_) | copy-start | bytes 25165828
  185.4 3.4 %copy-start.7 = (f32[16384,128]{1,0:T(8,128)S(1)}, f32[16384,128]{1,0:T(8,128)}, u32[]{:S(2)}) copy-start(f32[16384,128]{1,0:T(8,128)} %copy-done.6) | copy-start | bytes 25165828

commit v5 on v4

--- a/solution.py
+++ b/solution.py
@@ -368,17 +368,15 @@
 
     half = reps // 2
     far, near = list(range(peers // 2, peers)), list(range(1, half))
-    cuts = [round(len(far) * c / 16) for c in (0, 5, 9, 13, 16)]
+    cuts = [len(far) * c // 4 for c in range(5)]
     plan = [far[i:j] for i, j in zip(cuts, cuts[1:])]
 
     blocks = [embeddings] + [over_rep(embeddings, k) for k in range(1, reps)]
     rows0, from0 = direct(plan[0], [blocks[1]])
     emb, a, b, stats = forward(base, rep.reshape(1), blocks, labels, class_weights)
-    moved = hop(near, [stats])
-    moved |= hop([0], [stats])
-    rows1, from1 = direct(plan[1], [stats])
-
-    tied = tie(stats, rows0[:3])
+    rows1, from1 = direct(plan[1], [blocks[1]])
+
+    tied = tie(stats, rows0)
     flat = [
         jnp.broadcast_to(tied[0][None], (peers, batch)),
         centroid_class.reshape(peers, run).astype(jnp.float32),
@@ -394,9 +392,9 @@
     loss = SCALE + jnp.log(own_total) - target
 
     weight_grad = weight_gradient(base, emb, labels, stats, total, class_weights)
-    rows2, from2 = direct(plan[2], [weight_grad])
-
-    grad = a / total[:, None] - b
+    rows2, from2 = direct(plan[2], [total])
+
+    grad = tie(a / total[:, None] - b, [weight_grad, *rows1])
     parts = lax.all_to_all(grad.reshape(peers, share, width), ALL, 0, 0, tiled=True)
     own = jnp.sum(parts, axis=0)
     embedding_gradient = lax.all_to_all(
@@ -405,6 +403,8 @@
 
     held, token = place_rows(info, slots, rows0 + rows1, from0 + from1, groups, None, classes, run)
     rows3, from3 = direct(plan[3], [token])
+    moved = hop(near, [weight_grad])
+    moved |= hop([0], [weight_grad])
     rows, origins = spread(moved, [0] + near)
     held, _ = place_rows(
         info, slots, [rows, *rows2], origins + from2, groups, held, classes, run

time: 198 us -> 199 us (level)
  the two profiles are of different devices: /device:TPU:9 before, /device:TPU:16 now
where the time goes in v5:
time: 199 us; the launch traced here: 198 us
  starting transfers between devices  57.2 us (29%)
  Pallas kernels  47.8 us (24%)
  waiting for transfers between devices  47.4 us (24%)
  local copies, waits for them, and re-layouts  37.7 us (19%)
  other arithmetic  7.01 us (4%)
    unnamed x47, local copies, waits for them, and re-layouts  36.2 us
    ppermute x16, waiting for transfers between devices, over_all(): lax.ppermute(value, ('grp', 'rep'), [(at(d), at(d ^ k)) for d in range(pe...  27 us
    ppermute x16, starting transfers between devices, over_all(): lax.ppermute(value, ('grp', 'rep'), [(at(d), at(d ^ k)) for d in range(pe...  23.5 us
    ppermute x10, waiting for transfers between devices, over_rep(): return lax.ppermute(value, 'rep', [(i, i ^ k) for i in range(reps)])  14.6 us
    pallas_call x2, Pallas kernels, place_rows(): pl.pallas_call(functools.partial(place_kernel, origins=tuple(origins), gr...  14.3 us
    pallas_call x1, Pallas kernels, forward(): pl.pallas_call(functools.partial(forward_kernel, classes=classes, reps=re...  11.7 us
    ppermute x10, starting transfers between devices, over_rep(): return lax.ppermute(value, 'rep', [(i, i ^ k) for i in range(reps)])  9.68 us
    pallas_call x1, Pallas kernels, weight_gradient(): pl.pallas_call(weight_kernel, grid=(classes // tile,), in_specs=[pl.Block...  9.49 us
  transfers between devices with their start and end apart: 30, of which 11 were waited for; matrix products, arithmetic and copies ran while one was open for 4% of the time, Pallas kernels for 20%

profile of v5, /device:TPU:16, one launch (start us, length us, event | category | flops | bytes accessed | tf_op | source)
XLA Modules:
  0.0 198.1 jit_solution(16084915393111505652)
XLA Ops:
  1.2 3.6 %collective-permute-start.4 = (bf16[64,256]{1,0:T(8,128)(2,1)}, bf16[64,256]{1,0:T(8,128)(2,1)S(1)}, u32[]{:S(2)}, u32[]{:S(2)}) collective-permute-start(bf16[64,256]{1,0:T(8,128)(2,1)} %refs_0_.1), channel_id=1, source_target_pairs={{0,5},{1,4},{2,7},{3,6},{4,1},{5,0},{6,3},{7,2},{8,13},{9,12},{10,... | collective-permute-start | bytes 98312 | tf_op jit(solution)/shard_map/ppermute | solution.py:349
  4.8 3.6 %collective-permute-start.1 = (bf16[64,256]{1,0:T(8,128)(2,1)}, bf16[64,256]{1,0:T(8,128)(2,1)S(1)}, u32[]{:S(2)}, u32[]{:S(2)}) collective-permute-start(bf16[64,256]{1,0:T(8,128)(2,1)} %refs_0_.1), channel_id=1, source_target_pairs={{0,2},{1,3},{2,0},{3,1},{4,6},{5,7},{6,4},{7,5},{8,10},{9,11},{10,... | collective-permute-start | bytes 98312 | tf_op jit(solution)/shard_map/ppermute | solution.py:349
  8.4 0.8 convert_element_type.13
  9.2 0.8 copy.12.lab_ref
  10.1 2.2 %copy-done = bf16[8192,256]{1,0:T(8,128)(2,1)S(1)} copy-done((bf16[8192,256]{1,0:T(8,128)(2,1)S(1)}, bf16[8192,256]{1,0:T(8,128)(2,1)}, u32[]{:S(2)}) %copy-start) | copy-done | bytes 4194328
  12.2 0.7 fetch.6
  12.9 0.9 collective-permute-start.7
  13.8 3.0 %collective-permute-start.8 = (bf16[256,256]{1,0:T(8,128)(2,1)S(1)}, bf16[256,256]{1,0:T(8,128)(2,1)S(1)}, u32[]{:S(2)}, u32[]{:S(2)}) collective-permute-start(bf16[256,256]{1,0:T(8,128)(2,1)S(1)} %get-tuple-element.33), channel_id=1, source_target_pairs={{0,12},{8,4},{16,28},{24,20},{1,13},{9,5},{17,29},{25,21},{2,14},{... | collective-permute-start | bytes 393224 | tf_op jit(solution)/shard_map/ppermute | solution.py:352
  16.9 1.9 collective-permute-start.9
  18.8 1.9 collective-permute-start.10
  20.7 11.7 %forward_sums.1 = (bf16[512,256]{1,0:T(8,128)(2,1)S(1)}, f32[512,256]{1,0:T(8,128)S(1)}, f32[512,256]{1,0:T(8,128)S(1)}, f32[8,512]{1,0:T(8,128)S(1)}) custom-call(s32[1]{0:T(128)} %bitcast.base_ref, s32[1]{0:T(128)} %bitcast.1.rep_ref.me_ref, s32[512,1]{1,0:T(8,128)S(1)} %copy.12.lab_ref, bf16[8192,256]{1,0:T(8,128)(2,1)S(1)} %copy-done.11, ...), custom_call_target="tpu_custom_call" | custom-call | flops 12884901888 | bytes 4194304 | tf_op jit(solution)/shard_map/forward_sums/pallas_call | solution.py:101
  32.4 1.6 collective-permute-done.9.refs_2_
  33.9 2.8 %collective-permute-done.10.refs_3_ = bf16[256,256]{1,0:T(8,128)(2,1)S(1)} collective-permute-done((bf16[256,256]{1,0:T(8,128)(2,1)S(1)}, bf16[256,256]{1,0:T(8,128)(2,1)S(1)}, u32[]{:S(2)}, u32[]{:S(2)}) %collective-permute-start.10) | collective-permute-done | bytes 131104 | tf_op jit(solution)/shard_map/ppermute | solution.py:352
  36.9 0.7 copy.13
  37.6 8.0 %all-to-all-start = ((f32[32,8,128]{2,1,0:T(8,128)}), f32[32,8,128]{2,1,0:T(8,128)S(1)}, u32[]{:S(2)}, u32[]{:S(2)}) async-start(f32[32,8,128]{2,1,0:T(8,128)} %bitcast.17), calls=%async_computation | async-start | bytes 262144 | tf_op jit(solution)/shard_map/all_to_all | solution.py:387
  45.6 2.2 %copy-done.1 = bf16[8192,256]{1,0:T(8,128)(2,1)S(1)} copy-done((bf16[8192,256]{1,0:T(8,128)(2,1)S(1)}, bf16[8192,256]{1,0:T(8,128)(2,1)}, u32[]{:S(2)}) %copy-start.1) | copy-done | bytes 4194328
  47.8 0.7 fetch.7
  48.7 3.4 %collective-permute-start.12 = (bf16[256,256]{1,0:T(8,128)(2,1)S(1)}, bf16[256,256]{1,0:T(8,128)(2,1)S(1)}, u32[]{:S(2)}, u32[]{:S(2)}) collective-permute-start(bf16[256,256]{1,0:T(8,128)(2,1)S(1)} %get-tuple-element.40), channel_id=1, source_target_pairs={{0,13},{8,5},{16,29},{24,21},{1,12},{9,4},{17,28},{25,20},{2,15},{... | collective-permute-start | bytes 393224 | tf_op jit(solution)/shard_map/ppermute | solution.py:352
  52.1 1.2 collective-permute-start.13
  53.3 2.3 %collective-permute-start.14 = (bf16[256,256]{1,0:T(8,128)(2,1)S(1)}, bf16[256,256]{1,0:T(8,128)(2,1)S(1)}, u32[]{:S(2)}, u32[]{:S(2)}) collective-permute-start(bf16[256,256]{1,0:T(8,128)(2,1)S(1)} %get-tuple-element.42), channel_id=1, source_target_pairs={{0,29},{8,21},{16,13},{24,5},{1,28},{9,20},{17,12},{25,4},{2,31},{... | collective-permute-start | bytes 393224 | tf_op jit(solution)/shard_map/ppermute | solution.py:352
  55.7 0.6 copy-done.20
  56.3 2.2 %copy-done.12 = bf16[8192,256]{1,0:T(8,128)(2,1)S(1)} copy-done((bf16[8192,256]{1,0:T(8,128)(2,1)S(1)}, bf16[8192,256]{1,0:T(8,128)(2,1)}, u32[]{:S(2)}) %copy-start.12) | copy-done | bytes 4194328
  58.5 9.5 %weight_gradient.1.refs_0_ = f32[8192,256]{1,0:T(8,128)} custom-call(s32[1]{0:T(128)} %bitcast.base_ref, bf16[512,256]{1,0:T(8,128)(2,1)S(1)} %get-tuple-element.38.emb_ref, s32[1,512]{1,0:T(1,128)S(1)} %bitcast.33, f32[8,512]{1,0:T(8,128)S(1)} %get-tuple-element.31.value_ref.st_ref, f32[1,512]{1,0:T(1,128)S(1)} %bitcast.31, bf16[8192,256]{1,0:T(8,128)(2,1)S(1)} %copy-done.12), custom_call_target="tpu_custom_call" | custom-call | flops 12884901888 | bytes 12582912 | tf_op jit(solution)/shard_map/weight_gradient/pallas_call | solution.py:164
  68.2 1.1 collective-permute-done.13.refs_3_.refs_6_
  69.3 2.5 %collective-permute-done.14.refs_4_.refs_7_ = bf16[256,256]{1,0:T(8,128)(2,1)S(1)} collective-permute-done((bf16[256,256]{1,0:T(8,128)(2,1)S(1)}, bf16[256,256]{1,0:T(8,128)(2,1)S(1)}, u32[]{:S(2)}, u32[]{:S(2)}) %collective-permute-start.14) | collective-permute-done | bytes 131104 | tf_op jit(solution)/shard_map/ppermute | solution.py:352
  71.8 3.4 %copy-done.5 = f32[8192,256]{1,0:T(8,128)S(1)} copy-done((f32[8192,256]{1,0:T(8,128)S(1)}, f32[8192,256]{1,0:T(8,128)}, u32[]{:S(2)}) %copy-start.5) | copy-done | bytes 8388632
  75.2 0.8 tie.3
  76.0 8.9 %all-to-all-start.1 = ((f32[32,16,256]{2,1,0:T(8,128)}), f32[32,16,256]{2,1,0:T(8,128)}, u32[]{:S(2)}, u32[]{:S(2)}) async-start(f32[32,16,256]{2,1,0:T(8,128)} %bitcast.8), calls=%async_computation.1 | async-start | bytes 1048576 | tf_op jit(solution)/shard_map/all_to_all | solution.py:398
  84.9 2.2 %copy-done.2 = bf16[8192,256]{1,0:T(8,128)(2,1)S(1)} copy-done((bf16[8192,256]{1,0:T(8,128)(2,1)S(1)}, bf16[8192,256]{1,0:T(8,128)(2,1)}, u32[]{:S(2)}) %copy-start.2) | copy-done | bytes 4194328
  87.1 3.4 %copy-done.6 = f32[8192,256]{1,0:T(8,128)S(1)} copy-done((f32[8192,256]{1,0:T(8,128)S(1)}, f32[8192,256]{1,0:T(8,128)}, u32[]{:S(2)}) %copy-start.6) | copy-done | bytes 8388632
  90.8 1.5 collective-permute-start.20
  92.6 5.8 %all-to-all-done.1 = f32[32,16,256]{2,1,0:T(8,128)} async-done(((f32[32,16,256]{2,1,0:T(8,128)}), f32[32,16,256]{2,1,0:T(8,128)}, u32[]{:S(2)}, u32[]{:S(2)}) %all-to-all-start.1) | async-done | bytes 524320 | tf_op jit(solution)/shard_map/all_to_all | solution.py:398
  98.4 1.1 reduce_sum.29
  99.5 0.6 broadcast_in_dim.20
  100.1 3.3 %all-to-all-start.2 = ((f32[4,16,256]{2,1,0:T(8,128)}), f32[4,16,256]{2,1,0:T(8,128)S(1)}, u32[]{:S(2)}, u32[]{:S(2)}) async-start(f32[4,16,256]{2,1,0:T(8,128)} %broadcast_in_dim.20), calls=%async_computation.2 | async-start | bytes 131072 | tf_op jit(solution)/shard_map/all_to_all | solution.py:400
  103.5 4.3 %collective-permute-done.20 = bf16[1024,256]{1,0:T(8,128)(2,1)} collective-permute-done((bf16[1024,256]{1,0:T(8,128)(2,1)S(1)}, bf16[1024,256]{1,0:T(8,128)(2,1)}, u32[]{:S(2)}, u32[]{:S(2)}) %collective-permute-start.20) | collective-permute-done | bytes 524320 | tf_op jit(solution)/shard_map/ppermute | solution.py:349
  107.7 10.3 %collective-permute-done.21 = bf16[1024,256]{1,0:T(8,128)(2,1)} collective-permute-done((bf16[1024,256]{1,0:T(8,128)(2,1)S(1)}, bf16[1024,256]{1,0:T(8,128)(2,1)}, u32[]{:S(2)}, u32[]{:S(2)}) %collective-permute-start.21) | collective-permute-done | bytes 524320 | tf_op jit(solution)/shard_map/ppermute | solution.py:349
  118.0 2.8 %pad_maximum_fusion = bf16[4,1024,256]{2,1,0:T(8,128)(2,1)} fusion(bf16[4,256,256]{2,1,0:T(8,128)(2,1)} %bitcast.14, bf16[4,256,256]{2,1,0:T(8,128)(2,1)} %bitcast.13, bf16[4,256,256]{2,1,0:T(8,128)(2,1)} %bitcast.12, bf16[4,256,256]{2,1,0:T(8,128)(2,1)S(1)} %bitcast.27), kind=kLoop, calls=%fused_computation | loop fusion | flops 8388608 | bytes 4194304 | tf_op jit(solution)/shard_map/concatenate | solution.py:360
  120.8 3.8 %all-to-all-start.3 = ((bf16[4,1024,256]{2,1,0:T(8,128)(2,1)}), bf16[4,1024,256]{2,1,0:T(8,128)(2,1)S(1)}, u32[]{:S(2)}, u32[]{:S(2)}) async-start(bf16[4,1024,256]{2,1,0:T(8,128)(2,1)} %pad_maximum_fusion), calls=%async_computation.3 | async-start | bytes 4194304 | tf_op jit(solution)/shard_map/all_to_all | solution.py:360
  124.7 2.2 %copy-done.3 = bf16[8192,256]{1,0:T(8,128)(2,1)S(1)} copy-done((bf16[8192,256]{1,0:T(8,128)(2,1)S(1)}, bf16[8192,256]{1,0:T(8,128)(2,1)}, u32[]{:S(2)}) %copy-start.3) | copy-done | bytes 4194328
  126.9 0.7 fetch.11
  127.7 3.4 %collective-permute-start.23 = (bf16[256,256]{1,0:T(8,128)(2,1)S(1)}, bf16[256,256]{1,0:T(8,128)(2,1)S(1)}, u32[]{:S(2)}, u32[]{:S(2)}) collective-permute-start(bf16[256,256]{1,0:T(8,128)(2,1)S(1)} %get-tuple-element.52), channel_id=1, source_target_pairs={{0,14},{8,6},{16,30},{24,22},{1,15},{9,7},{17,31},{25,23},{2,12},{... | collective-permute-start | bytes 393224 | tf_op jit(solution)/shard_map/ppermute | solution.py:352
  131.0 1.0 collective-permute-start.24
  132.0 0.8 fusion
  132.8 1.6 collective-permute-start.25
  134.3 4.4 %place_rows.2 = (f32[16384,128]{1,0:T(8,128)S(1)}, f32[8,128]{1,0:T(8,128)S(1)}) custom-call(s32[2]{0:T(128)S(1)} %pad_add_fusion.info_ref, s32[8192]{0:T(1024)S(1)} %bitcast.28, bf16[256,256]{1,0:T(8,128)(2,1)S(1)} %collective-permute-done.7.refs_0_, bf16[256,256]{1,0:T(8,128)(2,1)S(1)} %collective-permute-done.8.refs_1_, ...), custom_call_target="tpu_custom_call" | custom-call | flops 1 | bytes 1 | tf_op jit(solution)/shard_map/place_rows/pallas_call | solution.py:269
  138.7 3.3 %copy-done.7 = f32[16384,128]{1,0:T(8,128)} copy-done((f32[16384,128]{1,0:T(8,128)}, f32[16384,128]{1,0:T(8,128)S(1)}, u32[]{:S(2)}) %copy-start.7) | copy-done | bytes 8388632
  142.0 1.4 fetch.8
  143.5 0.7 slice_reduce_fusion.1
  144.3 0.9 collective-permute-done.22.refs_1_
  145.2 2.2 %collective-permute-start.16 = (bf16[256,256]{1,0:T(8,128)(2,1)}, bf16[256,256]{1,0:T(8,128)(2,1)S(1)}, u32[]{:S(2)}, u32[]{:S(2)}) collective-permute-start(bf16[256,256]{1,0:T(8,128)(2,1)} %get-tuple-element.45), channel_id=1, source_target_pairs={{0,15},{8,7},{16,31},{24,23},{1,14},{9,6},{17,30},{25,22},{2,13},{... | collective-permute-start | bytes 393224 | tf_op jit(solution)/shard_map/ppermute | solution.py:352
  147.4 2.0 collective-permute-done.23.refs_2_
  149.4 2.9 %collective-permute-done.24.refs_3_ = bf16[256,256]{1,0:T(8,128)(2,1)S(1)} collective-permute-done((bf16[256,256]{1,0:T(8,128)(2,1)S(1)}, bf16[256,256]{1,0:T(8,128)(2,1)S(1)}, u32[]{:S(2)}, u32[]{:S(2)}) %collective-permute-start.24) | collective-permute-done | bytes 131104 | tf_op jit(solution)/shard_map/ppermute | solution.py:352
  152.3 0.7 copy-done.14
  153.9 13.3 %collective-permute-done.25.refs_4_ = bf16[256,256]{1,0:T(8,128)(2,1)S(1)} collective-permute-done((bf16[256,256]{1,0:T(8,128)(2,1)S(1)}, bf16[256,256]{1,0:T(8,128)(2,1)S(1)}, u32[]{:S(2)}, u32[]{:S(2)}) %collective-permute-start.25) | collective-permute-done | bytes 131104 | tf_op jit(solution)/shard_map/ppermute | solution.py:352
  167.2 0.7 copy-done.16
  167.8 3.4 %copy-done.8 = f32[16384,128]{1,0:T(8,128)S(1)} copy-done((f32[16384,128]{1,0:T(8,128)S(1)}, f32[16384,128]{1,0:T(8,128)}, u32[]{:S(2)}) %copy-start.8) | copy-done | bytes 8388632
  171.2 0.9 copy-done.15
  172.1 0.9 copy-done.17
  173.0 9.9 %place_rows.3 = (f32[16384,128]{1,0:T(8,128)S(1)}, f32[8,128]{1,0:T(8,128)}) custom-call(s32[2]{0:T(128)S(1)} %pad_add_fusion.info_ref, s32[8192]{0:T(1024)S(1)} %bitcast.29, bf16[4096,256]{1,0:T(8,128)(2,1)S(1)} %bitcast.26, bf16[256,256]{1,0:T(8,128)(2,1)S(1)} %collective-permute-done.22.refs_1_, ...), custom_call_target="tpu_custom_call", output_to_operand_aliasing={{0}: (7, {})} | custom-call | flops 1 | bytes 1 | tf_op jit(solution)/shard_map/place_rows/pallas_call | solution.py:269
  182.9 3.3 %copy-done.9 = f32[16384,128]{1,0:T(8,128)} copy-done((f32[16384,128]{1,0:T(8,128)}, f32[16384,128]{1,0:T(8,128)S(1)}, u32[]{:S(2)}) %copy-start.9) | copy-done | bytes 8388632
  186.2 3.4 %copy-done.10 = f32[16384,128]{1,0:T(8,128)S(1)} copy-done((f32[16384,128]{1,0:T(8,128)S(1)}, f32[16384,128]{1,0:T(8,128)}, u32[]{:S(2)}) %copy-start.10) | copy-done | bytes 8388632
  189.6 7.9 %place_and_blend.1 = (bf16[8192,256]{1,0:T(8,128)(2,1)}, f32[16384,128]{1,0:T(8,128)S(1)}) custom-call(s32[2]{0:T(128)S(1)} %pad_add_fusion.info_ref, s32[8192]{0:T(1024)S(1)} %bitcast.30, bf16[8192,256]{1,0:T(8,128)(2,1)S(1)} %copy-done.13, bf16[256,256]{1,0:T(8,128)(2,1)S(1)} %collective-permute-done.15.refs_0_, ...), custom_call_target="tpu_custom_call", output_to_operand_aliasing={{1}: (7, {})} | custom-call | flops 1 | bytes 1 | tf_op jit(solution)/shard_map/place_and_blend/pallas_call | solution.py:312
  197.5 0.6 copy.21
  (73 shorter events, 3.0 us)
Async XLA Ops:
  0.6 20.0 %copy-start.19 = (bf16[64,256]{1,0:T(8,128)(2,1)S(1)}, bf16[64,256]{1,0:T(8,128)(2,1)}, u32[]{:S(2)}) copy-start(bf16[64,256]{1,0:T(8,128)(2,1)} %refs_0_.1) | copy-start | bytes 98308
  0.6 4.2 %collective-permute-start.5 = (bf16[64,256]{1,0:T(8,128)(2,1)}, bf16[64,256]{1,0:T(8,128)(2,1)S(1)}, u32[]{:S(2)}, u32[]{:S(2)}) collective-permute-start(bf16[64,256]{1,0:T(8,128)(2,1)} %refs_0_.1), channel_id=1, source_target_pairs={{0,6},{1,7},{2,4},{3,5},{4,2},{5,3},{6,0},{7,1},{8,14},{9,15},{10,... | collective-permute-start | bytes 98312 | tf_op jit(solution)/shard_map/ppermute | solution.py:349
  1.2 7.3 %collective-permute-start = (bf16[64,256]{1,0:T(8,128)(2,1)}, bf16[64,256]{1,0:T(8,128)(2,1)S(1)}, u32[]{:S(2)}, u32[]{:S(2)}) collective-permute-start(bf16[64,256]{1,0:T(8,128)(2,1)} %refs_0_.1), channel_id=1, source_target_pairs={{0,1},{1,0},{2,3},{3,2},{4,5},{5,4},{6,7},{7,6},{8,9},{9,8},{10,11... | collective-permute-start | bytes 98312 | tf_op jit(solution)/shard_map/ppermute | solution.py:349
  1.2 11.8 %collective-permute-start.4 = (bf16[64,256]{1,0:T(8,128)(2,1)}, bf16[64,256]{1,0:T(8,128)(2,1)S(1)}, u32[]{:S(2)}, u32[]{:S(2)}) collective-permute-start(bf16[64,256]{1,0:T(8,128)(2,1)} %refs_0_.1), channel_id=1, source_target_pairs={{0,5},{1,4},{2,7},{3,6},{4,1},{5,0},{6,3},{7,2},{8,13},{9,12},{10,... | collective-permute-start | bytes 98312 | tf_op jit(solution)/shard_map/ppermute | solution.py:349
  4.8 9.1 %collective-permute-start.3 = (bf16[64,256]{1,0:T(8,128)(2,1)}, bf16[64,256]{1,0:T(8,128)(2,1)S(1)}, u32[]{:S(2)}, u32[]{:S(2)}) collective-permute-start(bf16[64,256]{1,0:T(8,128)(2,1)} %refs_0_.1), channel_id=1, source_target_pairs={{0,4},{1,5},{2,6},{3,7},{4,0},{5,1},{6,2},{7,3},{8,12},{9,13},{10,... | collective-permute-start | bytes 98312 | tf_op jit(solution)/shard_map/ppermute | solution.py:349
  4.8 12.1 %collective-permute-start.2 = (bf16[64,256]{1,0:T(8,128)(2,1)}, bf16[64,256]{1,0:T(8,128)(2,1)S(1)}, u32[]{:S(2)}, u32[]{:S(2)}) collective-permute-start(bf16[64,256]{1,0:T(8,128)(2,1)} %refs_0_.1), channel_id=1, source_target_pairs={{0,3},{1,2},{2,1},{3,0},{4,7},{5,6},{6,5},{7,4},{8,11},{9,10},{10,... | collective-permute-start | bytes 98312 | tf_op jit(solution)/shard_map/ppermute | solution.py:349
  4.8 14.0 %collective-permute-start.1 = (bf16[64,256]{1,0:T(8,128)(2,1)}, bf16[64,256]{1,0:T(8,128)(2,1)S(1)}, u32[]{:S(2)}, u32[]{:S(2)}) collective-permute-start(bf16[64,256]{1,0:T(8,128)(2,1)} %refs_0_.1), channel_id=1, source_target_pairs={{0,2},{1,3},{2,0},{3,1},{4,6},{5,7},{6,4},{7,5},{8,10},{9,11},{10,... | collective-permute-start | bytes 98312 | tf_op jit(solution)/shard_map/ppermute | solution.py:349
  8.4 12.2 %collective-permute-start.6 = (bf16[64,256]{1,0:T(8,128)(2,1)}, bf16[64,256]{1,0:T(8,128)(2,1)S(1)}, u32[]{:S(2)}, u32[]{:S(2)}) collective-permute-start(bf16[64,256]{1,0:T(8,128)(2,1)} %refs_0_.1), channel_id=1, source_target_pairs={{0,7},{1,6},{2,5},{3,4},{4,3},{5,2},{6,1},{7,0},{8,15},{9,14},{10,... | collective-permute-start | bytes 98312 | tf_op jit(solution)/shard_map/ppermute | solution.py:349
  10.0 2.2 %copy-start = (bf16[8192,256]{1,0:T(8,128)(2,1)S(1)}, bf16[8192,256]{1,0:T(8,128)(2,1)}, u32[]{:S(2)}) copy-start(bf16[8192,256]{1,0:T(8,128)(2,1)} %rows_ref.11) | copy-start | bytes 12582916
  12.2 8.4 %copy-start.11 = (bf16[8192,256]{1,0:T(8,128)(2,1)S(1)}, bf16[8192,256]{1,0:T(8,128)(2,1)}, u32[]{:S(2)}) copy-start(bf16[8192,256]{1,0:T(8,128)(2,1)} %w_ref.5) | copy-start | bytes 12582916
  12.9 19.4 %collective-permute-start.7 = (bf16[256,256]{1,0:T(8,128)(2,1)S(1)}, bf16[256,256]{1,0:T(8,128)(2,1)S(1)}, u32[]{:S(2)}, u32[]{:S(2)}) collective-permute-start(bf16[256,256]{1,0:T(8,128)(2,1)S(1)} %get-tuple-element.32), channel_id=1, source_target_pairs={{0,4},{8,12},{16,20},{24,28},{1,5},{9,13},{17,21},{25,29},{2,6},{1... | collective-permute-start | bytes 393224 | tf_op jit(solution)/shard_map/ppermute | solution.py:352
  13.8 18.5 %collective-permute-start.8 = (bf16[256,256]{1,0:T(8,128)(2,1)S(1)}, bf16[256,256]{1,0:T(8,128)(2,1)S(1)}, u32[]{:S(2)}, u32[]{:S(2)}) collective-permute-start(bf16[256,256]{1,0:T(8,128)(2,1)S(1)} %get-tuple-element.33), channel_id=1, source_target_pairs={{0,12},{8,4},{16,28},{24,20},{1,13},{9,5},{17,29},{25,21},{2,14},{... | collective-permute-start | bytes 393224 | tf_op jit(solution)/shard_map/ppermute | solution.py:352
  16.9 17.1 %collective-permute-start.9 = (bf16[256,256]{1,0:T(8,128)(2,1)S(1)}, bf16[256,256]{1,0:T(8,128)(2,1)S(1)}, u32[]{:S(2)}, u32[]{:S(2)}) collective-permute-start(bf16[256,256]{1,0:T(8,128)(2,1)S(1)} %get-tuple-element.34), channel_id=1, source_target_pairs={{0,20},{8,28},{16,4},{24,12},{1,21},{9,29},{17,5},{25,13},{2,22},{... | collective-permute-start | bytes 393224 | tf_op jit(solution)/shard_map/ppermute | solution.py:352
  18.8 18.0 %collective-permute-start.10 = (bf16[256,256]{1,0:T(8,128)(2,1)S(1)}, bf16[256,256]{1,0:T(8,128)(2,1)S(1)}, u32[]{:S(2)}, u32[]{:S(2)}) collective-permute-start(bf16[256,256]{1,0:T(8,128)(2,1)S(1)} %get-tuple-element.35), channel_id=1, source_target_pairs={{0,28},{8,20},{16,12},{24,4},{1,29},{9,21},{17,13},{25,5},{2,30},{... | collective-permute-start | bytes 393224 | tf_op jit(solution)/shard_map/ppermute | solution.py:352
  32.3 24.0 %copy-start.18 = (s32[512]{0:T(512)S(1)}, s32[512]{0:T(512)}, u32[]{:S(2)}) copy-start(s32[512]{0:T(512)} %param.6) | copy-start | bytes 6148
  37.6 18.1 %all-to-all-start = ((f32[32,8,128]{2,1,0:T(8,128)}), f32[32,8,128]{2,1,0:T(8,128)S(1)}, u32[]{:S(2)}, u32[]{:S(2)}) async-start(f32[32,8,128]{2,1,0:T(8,128)} %bitcast.17), calls=%async_computation | async-start | bytes 262144 | tf_op jit(solution)/shard_map/all_to_all | solution.py:387
  45.6 2.2 %copy-start.1 = (bf16[8192,256]{1,0:T(8,128)(2,1)S(1)}, bf16[8192,256]{1,0:T(8,128)(2,1)}, u32[]{:S(2)}) copy-start(bf16[8192,256]{1,0:T(8,128)(2,1)} %rows_ref.11) | copy-start | bytes 12582916
  48.5 19.7 %collective-permute-start.11 = (bf16[256,256]{1,0:T(8,128)(2,1)S(1)}, bf16[256,256]{1,0:T(8,128)(2,1)S(1)}, u32[]{:S(2)}, u32[]{:S(2)}) collective-permute-start(bf16[256,256]{1,0:T(8,128)(2,1)S(1)} %get-tuple-element.39), channel_id=1, source_target_pairs={{0,5},{8,13},{16,21},{24,29},{1,4},{9,12},{17,20},{25,28},{2,7},{1... | collective-permute-start | bytes 393224 | tf_op jit(solution)/shard_map/ppermute | solution.py:352
  48.7 19.5 %collective-permute-start.12 = (bf16[256,256]{1,0:T(8,128)(2,1)S(1)}, bf16[256,256]{1,0:T(8,128)(2,1)S(1)}, u32[]{:S(2)}, u32[]{:S(2)}) collective-permute-start(bf16[256,256]{1,0:T(8,128)(2,1)S(1)} %get-tuple-element.40), channel_id=1, source_target_pairs={{0,13},{8,5},{16,29},{24,21},{1,12},{9,4},{17,28},{25,20},{2,15},{... | collective-permute-start | bytes 393224 | tf_op jit(solution)/shard_map/ppermute | solution.py:352
  52.1 17.2 %collective-permute-start.13 = (bf16[256,256]{1,0:T(8,128)(2,1)S(1)}, bf16[256,256]{1,0:T(8,128)(2,1)S(1)}, u32[]{:S(2)}, u32[]{:S(2)}) collective-permute-start(bf16[256,256]{1,0:T(8,128)(2,1)S(1)} %get-tuple-element.41), channel_id=1, source_target_pairs={{0,21},{8,29},{16,5},{24,13},{1,20},{9,28},{17,4},{25,12},{2,23},{... | collective-permute-start | bytes 393224 | tf_op jit(solution)/shard_map/ppermute | solution.py:352
  53.3 18.5 %collective-permute-start.14 = (bf16[256,256]{1,0:T(8,128)(2,1)S(1)}, bf16[256,256]{1,0:T(8,128)(2,1)S(1)}, u32[]{:S(2)}, u32[]{:S(2)}) collective-permute-start(bf16[256,256]{1,0:T(8,128)(2,1)S(1)} %get-tuple-element.42), channel_id=1, source_target_pairs={{0,29},{8,21},{16,13},{24,5},{1,28},{9,20},{17,12},{25,4},{2,31},{... | collective-permute-start | bytes 393224 | tf_op jit(solution)/shard_map/ppermute | solution.py:352
  55.7 0.7 copy-start.20
  56.3 2.2 %copy-start.12 = (bf16[8192,256]{1,0:T(8,128)(2,1)S(1)}, bf16[8192,256]{1,0:T(8,128)(2,1)}, u32[]{:S(2)}) copy-start(bf16[8192,256]{1,0:T(8,128)(2,1)} %w_ref.5) | copy-start | bytes 12582916
  71.8 3.4 %copy-start.5 = (f32[8192,256]{1,0:T(8,128)S(1)}, f32[8192,256]{1,0:T(8,128)}, u32[]{:S(2)}) copy-start(f32[8192,256]{1,0:T(8,128)} %weight_gradient.1.refs_0_) | copy-start | bytes 25165828
  76.0 22.4 %all-to-all-start.1 = ((f32[32,16,256]{2,1,0:T(8,128)}), f32[32,16,256]{2,1,0:T(8,128)}, u32[]{:S(2)}, u32[]{:S(2)}) async-start(f32[32,16,256]{2,1,0:T(8,128)} %bitcast.8), calls=%async_computation.1 | async-start | bytes 1048576 | tf_op jit(solution)/shard_map/all_to_all | solution.py:398
  84.9 2.2 %copy-start.2 = (bf16[8192,256]{1,0:T(8,128)(2,1)S(1)}, bf16[8192,256]{1,0:T(8,128)(2,1)}, u32[]{:S(2)}) copy-start(bf16[8192,256]{1,0:T(8,128)(2,1)} %rows_ref.11) | copy-start | bytes 12582916
  87.1 3.4 %copy-start.6 = (f32[8192,256]{1,0:T(8,128)S(1)}, f32[8192,256]{1,0:T(8,128)}, u32[]{:S(2)}) copy-start(f32[8192,256]{1,0:T(8,128)} %weight_gradient.1.refs_0_) | copy-start | bytes 25165828
  90.6 12.8 %collective-permute-start.19 = (bf16[1024,256]{1,0:T(8,128)(2,1)S(1)}, bf16[1024,256]{1,0:T(8,128)(2,1)}, u32[]{:S(2)}, u32[]{:S(2)}) collective-permute-start(bf16[1024,256]{1,0:T(8,128)(2,1)S(1)} %get-tuple-element.48), channel_id=1, source_target_pairs={{0,1},{1,0},{2,3},{3,2},{4,5},{5,4},{6,7},{7,6},{8,9},{9,8},{10,11... | collective-permute-start | bytes 1572872 | tf_op jit(solution)/shard_map/ppermute | solution.py:349
  90.8 16.9 %collective-permute-start.20 = (bf16[1024,256]{1,0:T(8,128)(2,1)S(1)}, bf16[1024,256]{1,0:T(8,128)(2,1)}, u32[]{:S(2)}, u32[]{:S(2)}) collective-permute-start(bf16[1024,256]{1,0:T(8,128)(2,1)S(1)} %get-tuple-element.49), channel_id=1, source_target_pairs={{0,2},{1,3},{2,0},{3,1},{4,6},{5,7},{6,4},{7,5},{8,10},{9,11},{10,... | collective-permute-start | bytes 1572872 | tf_op jit(solution)/shard_map/ppermute | solution.py:349
  92.4 25.6 %collective-permute-start.21 = (bf16[1024,256]{1,0:T(8,128)(2,1)S(1)}, bf16[1024,256]{1,0:T(8,128)(2,1)}, u32[]{:S(2)}, u32[]{:S(2)}) collective-permute-start(bf16[1024,256]{1,0:T(8,128)(2,1)S(1)} %get-tuple-element.50), channel_id=1, source_target_pairs={{0,3},{1,2},{2,1},{3,0},{4,7},{5,6},{6,5},{7,4},{8,11},{9,10},{10,... | collective-permute-start | bytes 1572872 | tf_op jit(solution)/shard_map/ppermute | solution.py:349
  100.1 20.7 %all-to-all-start.2 = ((f32[4,16,256]{2,1,0:T(8,128)}), f32[4,16,256]{2,1,0:T(8,128)S(1)}, u32[]{:S(2)}, u32[]{:S(2)}) async-start(f32[4,16,256]{2,1,0:T(8,128)} %broadcast_in_dim.20), calls=%async_computation.2 | async-start | bytes 131072 | tf_op jit(solution)/shard_map/all_to_all | solution.py:400
  120.8 47.0 %all-to-all-start.3 = ((bf16[4,1024,256]{2,1,0:T(8,128)(2,1)}), bf16[4,1024,256]{2,1,0:T(8,128)(2,1)S(1)}, u32[]{:S(2)}, u32[]{:S(2)}) async-start(bf16[4,1024,256]{2,1,0:T(8,128)(2,1)} %pad_maximum_fusion), calls=%async_computation.3 | async-start | bytes 4194304 | tf_op jit(solution)/shard_map/all_to_all | solution.py:360
  124.7 2.2 %copy-start.3 = (bf16[8192,256]{1,0:T(8,128)(2,1)S(1)}, bf16[8192,256]{1,0:T(8,128)(2,1)}, u32[]{:S(2)}) copy-start(bf16[8192,256]{1,0:T(8,128)(2,1)} %rows_ref.11) | copy-start | bytes 12582916
  126.9 15.2 %copy-start.4 = (bf16[8192,256]{1,0:T(8,128)(2,1)S(1)}, bf16[8192,256]{1,0:T(8,128)(2,1)}, u32[]{:S(2)}) copy-start(bf16[8192,256]{1,0:T(8,128)(2,1)} %rows_ref.11) | copy-start | bytes 12582916
  127.6 17.6 %collective-permute-start.22 = (bf16[256,256]{1,0:T(8,128)(2,1)S(1)}, bf16[256,256]{1,0:T(8,128)(2,1)S(1)}, u32[]{:S(2)}, u32[]{:S(2)}) collective-permute-start(bf16[256,256]{1,0:T(8,128)(2,1)S(1)} %get-tuple-element.51), channel_id=1, source_target_pairs={{0,6},{8,14},{16,22},{24,30},{1,7},{9,15},{17,23},{25,31},{2,4},{1... | collective-permute-start | bytes 393224 | tf_op jit(solution)/shard_map/ppermute | solution.py:352
  127.7 21.8 %collective-permute-start.23 = (bf16[256,256]{1,0:T(8,128)(2,1)S(1)}, bf16[256,256]{1,0:T(8,128)(2,1)S(1)}, u32[]{:S(2)}, u32[]{:S(2)}) collective-permute-start(bf16[256,256]{1,0:T(8,128)(2,1)S(1)} %get-tuple-element.52), channel_id=1, source_target_pairs={{0,14},{8,6},{16,30},{24,22},{1,15},{9,7},{17,31},{25,23},{2,12},{... | collective-permute-start | bytes 393224 | tf_op jit(solution)/shard_map/ppermute | solution.py:352
  131.0 21.3 %collective-permute-start.24 = (bf16[256,256]{1,0:T(8,128)(2,1)S(1)}, bf16[256,256]{1,0:T(8,128)(2,1)S(1)}, u32[]{:S(2)}, u32[]{:S(2)}) collective-permute-start(bf16[256,256]{1,0:T(8,128)(2,1)S(1)} %get-tuple-element.53), channel_id=1, source_target_pairs={{0,22},{8,30},{16,6},{24,14},{1,23},{9,31},{17,7},{25,15},{2,20},{... | collective-permute-start | bytes 393224 | tf_op jit(solution)/shard_map/ppermute | solution.py:352
  132.8 34.4 %collective-permute-start.25 = (bf16[256,256]{1,0:T(8,128)(2,1)S(1)}, bf16[256,256]{1,0:T(8,128)(2,1)S(1)}, u32[]{:S(2)}, u32[]{:S(2)}) collective-permute-start(bf16[256,256]{1,0:T(8,128)(2,1)S(1)} %get-tuple-element.54), channel_id=1, source_target_pairs={{0,30},{8,22},{16,14},{24,6},{1,31},{9,23},{17,15},{25,7},{2,28},{... | collective-permute-start | bytes 393224 | tf_op jit(solution)/shard_map/ppermute | solution.py:352
  138.7 3.3 %copy-start.7 = (f32[16384,128]{1,0:T(8,128)}, f32[16384,128]{1,0:T(8,128)S(1)}, u32[]{:S(2)}) copy-start(f32[16384,128]{1,0:T(8,128)S(1)} %get-tuple-element.55.refs_5_) | copy-start | bytes 25165828
  143.5 42.7 %collective-permute-start.15 = (bf16[256,256]{1,0:T(8,128)(2,1)}, bf16[256,256]{1,0:T(8,128)(2,1)S(1)}, u32[]{:S(2)}, u32[]{:S(2)}) collective-permute-start(bf16[256,256]{1,0:T(8,128)(2,1)} %get-tuple-element.44), channel_id=1, source_target_pairs={{0,7},{8,15},{16,23},{24,31},{1,6},{9,14},{17,22},{25,30},{2,5},{1... | collective-permute-start | bytes 393224 | tf_op jit(solution)/shard_map/ppermute | solution.py:352
  145.2 41.0 %collective-permute-start.16 = (bf16[256,256]{1,0:T(8,128)(2,1)}, bf16[256,256]{1,0:T(8,128)(2,1)S(1)}, u32[]{:S(2)}, u32[]{:S(2)}) collective-permute-start(bf16[256,256]{1,0:T(8,128)(2,1)} %get-tuple-element.45), channel_id=1, source_target_pairs={{0,15},{8,7},{16,31},{24,23},{1,14},{9,6},{17,30},{25,22},{2,13},{... | collective-permute-start | bytes 393224 | tf_op jit(solution)/shard_map/ppermute | solution.py:352
  149.4 36.8 %collective-permute-start.17 = (bf16[256,256]{1,0:T(8,128)(2,1)S(1)}, bf16[256,256]{1,0:T(8,128)(2,1)S(1)}, u32[]{:S(2)}, u32[]{:S(2)}) collective-permute-start(bf16[256,256]{1,0:T(8,128)(2,1)S(1)} %get-tuple-element.46), channel_id=1, source_target_pairs={{0,23},{8,31},{16,7},{24,15},{1,22},{9,30},{17,6},{25,14},{2,21},{... | collective-permute-start | bytes 393224 | tf_op jit(solution)/shard_map/ppermute | solution.py:352
  152.3 0.7 copy-start.14
  152.9 33.3 %collective-permute-start.18 = (bf16[256,256]{1,0:T(8,128)(2,1)S(1)}, bf16[256,256]{1,0:T(8,128)(2,1)S(1)}, u32[]{:S(2)}, u32[]{:S(2)}) collective-permute-start(bf16[256,256]{1,0:T(8,128)(2,1)S(1)} %get-tuple-element.47), channel_id=1, source_target_pairs={{0,31},{8,23},{16,15},{24,7},{1,30},{9,22},{17,14},{25,6},{2,29},{... | collective-permute-start | bytes 393224 | tf_op jit(solution)/shard_map/ppermute | solution.py:352
  167.1 0.7 copy-start.16
  167.8 3.4 %copy-start.8 = (f32[16384,128]{1,0:T(8,128)S(1)}, f32[16384,128]{1,0:T(8,128)}, u32[]{:S(2)}) copy-start(f32[16384,128]{1,0:T(8,128)} %copy-done.7) | copy-start | bytes 25165828
  171.2 0.9 copy-start.15
  172.1 0.9 copy-start.17
  173.0 13.2 %copy-start.13 = (bf16[8192,256]{1,0:T(8,128)(2,1)S(1)}, bf16[8192,256]{1,0:T(8,128)(2,1)}, u32[]{:S(2)}) copy-start(bf16[8192,256]{1,0:T(8,128)(2,1)} %w_ref.5) | copy-start | bytes 12582916
  182.9 3.3 %copy-start.9 = (f32[16384,128]{1,0:T(8,128)}, f32[16384,128]{1,0:T(8,128)S(1)}, u32[]{:S(2)}) copy-start(f32[16384,128]{1,0:T(8,128)S(1)} %get-tuple-element.56.refs_4_) | copy-start | bytes 25165828
  186.2 3.4 %copy-start.10 = (f32[16384,128]{1,0:T(8,128)S(1)}, f32[16384,128]{1,0:T(8,128)}, u32[]{:S(2)}) copy-start(f32[16384,128]{1,0:T(8,128)} %copy-done.9) | copy-start | bytes 25165828

commit v6 on v5

--- a/solution.py
+++ b/solution.py
@@ -189,31 +189,27 @@
     )(base, emb, labels.reshape(1, batch), stats, totals.reshape(1, batch), weights)
 
 
-def fetch_kernel(me_ref, rows_ref, *refs, picks, tokens):
-    outs, sem = refs[tokens : tokens + len(picks)], refs[-1]
-    copies = []
-    for u, (k, out_ref) in enumerate(zip(picks, outs)):
-        size = out_ref.shape[0]
-        first = pl.multiple_of((me_ref[0] ^ k) * size, size)
-        copies.append(pltpu.make_async_copy(rows_ref.at[pl.ds(first, size), :], out_ref, sem.at[u]))
-    for copy in copies:
-        copy.start()
-    for copy in copies:
-        copy.wait()
-
-
-def fetch(me, rows, size, picks, tokens):
+def fetch_kernel(rows_ref, *refs, first):
+    out_ref, sem = refs[-2:]
+    size = out_ref.shape[1]
+    copy = pltpu.make_async_copy(rows_ref.at[:, pl.ds(first, size), :], out_ref, sem)
+    copy.start()
+    copy.wait()
+
+
+def fetch(runs, first, size, tokens):
+    peers, _, width = runs.shape
     anywhere = pl.BlockSpec(memory_space=pl.ANY)
     return pl.pallas_call(
-        functools.partial(fetch_kernel, picks=tuple(picks), tokens=len(tokens)),
-        in_specs=[pl.BlockSpec(memory_space=pltpu.SMEM)] + [anywhere] * (1 + len(tokens)),
-        out_specs=[pl.BlockSpec(memory_space=pltpu.VMEM)] * len(picks),
-        out_shape=[jax.ShapeDtypeStruct((size, rows.shape[1]), rows.dtype)] * len(picks),
-        scratch_shapes=[pltpu.SemaphoreType.DMA((len(picks),))],
-        compiler_params=pltpu.CompilerParams(vmem_limit_bytes=4 * MIB),
+        functools.partial(fetch_kernel, first=first),
+        in_specs=[anywhere] * (1 + len(tokens)),
+        out_specs=pl.BlockSpec(memory_space=pltpu.VMEM),
+        out_shape=jax.ShapeDtypeStruct((peers, size, width), runs.dtype),
+        scratch_shapes=[pltpu.SemaphoreType.DMA],
+        compiler_params=pltpu.CompilerParams(vmem_limit_bytes=6 * MIB),
         cost_estimate=COST,
         name="fetch",
-    )(me, rows, *tokens)
+    )(runs, *tokens)
 
 
 def tie_kernel(value_ref, *refs):
@@ -234,100 +230,97 @@
     )(value, *tokens)
 
 
-def place_runs(info_ref, slot_ref, row_refs, origins, groups, held_ref, stage_ref):
-    run = stage_ref.shape[0] // 2
-    batch = math.gcd(run, 32)
-    parts = [(ref, u) for ref in row_refs for u in range(ref.shape[0] // run)]
-    for (row_ref, u), (rep_flip, grp_flip, grp_from) in zip(parts, origins):
-        unit, _ = unit_rows(row_ref[u * run : (u + 1) * run, :].astype(jnp.float32))
-        stage_ref[pl.ds(0, run, stride=2), :] = unit[:, :128]
-        stage_ref[pl.ds(1, run, stride=2), :] = unit[:, 128:]
-        grp = info_ref[1] ^ grp_flip if grp_from is None else grp_from
-        first = ((info_ref[0] ^ rep_flip) * groups + grp) * run
-
-        def place(j, carry, first=first):
+def place_runs(me_ref, slot_ref, row_ref, held_ref, stage_ref, peers, run, first):
+    size = stage_ref.shape[0] // 2
+    batch = math.gcd(size, 32)
+    for source in range(peers):
+        rows = row_ref[source * size : (source + 1) * size, :].astype(jnp.float32)
+        unit, _ = unit_rows(rows)
+        stage_ref[pl.ds(0, size, stride=2), :] = unit[:, :128]
+        stage_ref[pl.ds(1, size, stride=2), :] = unit[:, 128:]
+        start = (me_ref[0] ^ source) * run + first
+
+        def place(j, carry, start=start):
             at = j * batch
-            slots = [slot_ref[first + at + v] for v in range(batch)]
+            slots = [slot_ref[start + at + v] for v in range(batch)]
             values = [stage_ref[pl.ds((at + v) * 2, 2), :] for v in range(batch)]
             for slot, value in zip(slots, values):
                 held_ref[pl.ds(slot * 2, 2), :] = value
             return carry
 
-        lax.fori_loop(0, run // batch, place, 0)
-
-
-def place_kernel(info_ref, slot_ref, *refs, origins, groups, arrays):
-    held_ref, token_ref, stage_ref = refs[-3:]
+        lax.fori_loop(0, size // batch, place, 0)
+
+
+def place_kernel(me_ref, slot_ref, row_ref, held_ref, token_ref, stage_ref, *, peers, run, first):
     token_ref[...] = jnp.zeros_like(token_ref)
-    place_runs(info_ref, slot_ref, refs[:arrays], origins, groups, held_ref, stage_ref)
-
-
-def place_rows(info, slots, arrays, origins, groups, held, classes, run):
+    place_runs(me_ref, slot_ref, row_ref, held_ref, stage_ref, peers, run, first)
+
+
+def place_rows(me, slots, rows, peers, run, first):
     smem = pl.BlockSpec(memory_space=pltpu.SMEM)
     vmem = pl.BlockSpec(memory_space=pltpu.VMEM)
-    operands = [info, slots, *arrays] + ([] if held is None else [held])
     return pl.pallas_call(
-        functools.partial(
-            place_kernel, origins=tuple(origins), groups=groups, arrays=len(arrays)
-        ),
-        in_specs=[smem, smem] + [vmem] * (len(operands) - 2),
+        functools.partial(place_kernel, peers=peers, run=run, first=first),
+        in_specs=[smem, smem, vmem],
         out_specs=[vmem, vmem],
         out_shape=[
-            jax.ShapeDtypeStruct((2 * classes, 128), jnp.float32),
+            jax.ShapeDtypeStruct((2 * peers * run, 128), jnp.float32),
             jax.ShapeDtypeStruct((8, 128), jnp.float32),
         ],
-        input_output_aliases={} if held is None else {len(operands) - 1: 0},
-        scratch_shapes=[pltpu.VMEM((2 * run, 128), jnp.float32)],
-        compiler_params=pltpu.CompilerParams(vmem_limit_bytes=4 * MIB),
-        cost_estimate=COST,
+        scratch_shapes=[pltpu.VMEM((2 * rows.shape[0] // peers, 128), jnp.float32)],
+        compiler_params=pltpu.CompilerParams(vmem_limit_bytes=16 * MIB),
+        cost_estimate=pl.CostEstimate(
+            flops=0, bytes_accessed=16 * rows.shape[0] * rows.shape[1], transcendentals=0
+        ),
         name="place_rows",
-    )(*operands)
-
-
-def blend_kernel(info_ref, slot_ref, w_ref, *refs, origins, groups, arrays):
-    o_ref, held_ref, stage_ref = refs[-3:]
+    )(me, slots, rows)
+
+
+def blend_kernel(
+    me_ref, slot_ref, w_ref, row_ref, _, o_ref, held_ref, stage_ref, *, peers, run, first
+):
     step = pl.program_id(0)
     tile = w_ref.shape[0]
 
     @pl.when(step == 0)
     def _():
-        place_runs(info_ref, slot_ref, refs[:arrays], origins, groups, held_ref, stage_ref)
+        place_runs(me_ref, slot_ref, row_ref, held_ref, stage_ref, peers, run, first)
 
     wwide, _ = unit_rows(w_ref[...].astype(jnp.float32))
-    first = pl.multiple_of(step * 2 * tile, 2 * tile)
-    low = wwide[:, :128] + held_ref[pl.ds(first, tile, stride=2), :]
-    high = wwide[:, 128:] + held_ref[pl.ds(first + 1, tile, stride=2), :]
+    at = pl.multiple_of(step * 2 * tile, 2 * tile)
+    low = wwide[:, :128] + held_ref[pl.ds(at, tile, stride=2), :]
+    high = wwide[:, 128:] + held_ref[pl.ds(at + 1, tile, stride=2), :]
     square = jnp.sum(low * low + high * high, axis=1, keepdims=True)
     inv = lax.rsqrt(square + 1e-06)
     o_ref[:, :128] = (low * inv).astype(jnp.bfloat16)
     o_ref[:, 128:] = (high * inv).astype(jnp.bfloat16)
 
 
-def place_and_blend(info, slots, arrays, origins, groups, held, weights, run):
+def place_and_blend(me, slots, rows, held, weights, peers, run, first):
     classes, width = weights.shape
     tile = math.gcd(classes, 1024)
     smem = pl.BlockSpec(memory_space=pltpu.SMEM)
     vmem = pl.BlockSpec(memory_space=pltpu.VMEM)
     tiles = pl.BlockSpec((tile, width), lambda i: (i, 0))
     refreshed, _ = pl.pallas_call(
-        functools.partial(
-            blend_kernel, origins=tuple(origins), groups=groups, arrays=len(arrays)
-        ),
+        functools.partial(blend_kernel, peers=peers, run=run, first=first),
         grid=(classes // tile,),
-        in_specs=[smem, smem, tiles] + [vmem] * (len(arrays) + 1),
+        in_specs=[smem, smem, tiles, vmem, vmem],
         out_specs=[tiles, vmem],
         out_shape=[
             jax.ShapeDtypeStruct((classes, width), jnp.bfloat16),
             jax.ShapeDtypeStruct(held.shape, held.dtype),
         ],
-        input_output_aliases={3 + len(arrays): 1},
-        scratch_shapes=[pltpu.VMEM((2 * run, 128), jnp.float32)],
+        input_output_aliases={4: 1},
+        scratch_shapes=[pltpu.VMEM((2 * rows.shape[0] // peers, 128), jnp.float32)],
         compiler_params=pltpu.CompilerParams(
-            dimension_semantics=("arbitrary",), vmem_limit_bytes=10 * MIB
-        ),
-        cost_estimate=COST,
+            dimension_semantics=("arbitrary",), vmem_limit_bytes=16 * MIB
+        ),
+        cost_estimate=pl.CostEstimate(
+            flops=0, bytes_accessed=12 * classes * width, transcendentals=0
+        ),
         name="place_and_blend",
-    )(info, slots, weights, *arrays, held)
+    )(me, slots, weights, rows, held)
     return refreshed
 
 
@@ -340,76 +333,60 @@
     run = classes // peers
     share = rows_local // groups
     grp, rep = lax.axis_index("grp").astype(jnp.int32), lax.axis_index("rep").astype(jnp.int32)
-    me = rep * groups + grp
-    base, me = (me * classes).reshape(1), me.reshape(1)
-    info = jnp.stack([rep, grp])
-    at = lambda d: d % groups * reps + d // groups
-
-    def over_rep(value, k):
-        return lax.ppermute(value, "rep", [(i, i ^ k) for i in range(reps)])
-
-    def over_all(value, k):
-        return lax.ppermute(value, ("grp", "rep"), [(at(d), at(d ^ k)) for d in range(peers)])
-
-    def hop(picks, tokens):
-        fetched = fetch(rep.reshape(1), centroids, groups * run, picks, tokens)
-        return {k: over_rep(value, k) if k else value for k, value in zip(picks, fetched)}
-
-    def spread(held_rows, picks):
-        parts = [held_rows[k].reshape(groups, run, width) for k in picks]
-        parts = lax.all_to_all(jnp.concatenate(parts, axis=1), "grp", 0, 0, tiled=True)
-        origins = [(k, 0, g) for g in range(groups) for k in picks]
-        return parts.reshape(-1, width), origins
-
-    def direct(picks, tokens):
-        fetched = fetch(me, centroids, run, picks, tokens)
-        rows = [over_all(value, k) for k, value in zip(picks, fetched)]
-        return rows, [(k // groups, k % groups, None) for k in picks]
-
-    half = reps // 2
-    far, near = list(range(peers // 2, peers)), list(range(1, half))
-    cuts = [len(far) * c // 4 for c in range(5)]
-    plan = [far[i:j] for i, j in zip(cuts, cuts[1:])]
-
-    blocks = [embeddings] + [over_rep(embeddings, k) for k in range(1, reps)]
-    rows0, from0 = direct(plan[0], [blocks[1]])
+    me = (rep * groups + grp).reshape(1)
+    base = me * classes
+
+    def swap(value, axis, k):
+        size = lax.axis_size(axis)
+        return lax.ppermute(value, axis, [(i, i ^ k) for i in range(size)]) if k else value
+
+    def pick(value, axis, k, dim):
+        return lax.dynamic_index_in_dim(value, lax.axis_index(axis) ^ k, dim, keepdims=False)
+
+    blocks = [swap(embeddings, "rep", k) for k in range(reps)]
+
+    runs = centroids.reshape(peers, run, width)
+    cut = run * 5 // 8 // 16 * 16
+
+    def relay(first, size, tokens):
+        sent = fetch(runs, first, size, tokens)
+        return lax.all_to_all(sent, ALL, 0, 0, tiled=True).reshape(peers * size, width)
+
+    rows_a = relay(0, cut, blocks[1:])
     emb, a, b, stats = forward(base, rep.reshape(1), blocks, labels, class_weights)
-    rows1, from1 = direct(plan[1], [blocks[1]])
-
-    tied = tie(stats, rows0)
-    flat = [
-        jnp.broadcast_to(tied[0][None], (peers, batch)),
-        centroid_class.reshape(peers, run).astype(jnp.float32),
-        jnp.repeat(tied[1].reshape(reps, rows_local), groups, axis=0),
+
+    wanted = centroid_class.reshape(reps, groups, run).astype(jnp.float32)
+    sums = stats[:2].reshape(-1)
+    near = [
+        swap(jnp.concatenate([sums, pick(wanted, "grp", j, 1).reshape(-1)]).reshape(-1, 128), "grp", j)
+        for j in range(groups)
     ]
-    size = batch + run + rows_local
-    flat = jnp.pad(jnp.concatenate(flat, axis=1), ((0, 0), (0, -size % 1024)))
-    flat = lax.all_to_all(flat.reshape(peers, -1, 128), ALL, 0, 0, tiled=True).reshape(peers, -1)
-    total = jnp.sum(flat[:, :batch], axis=0)
-    slots = flat[:, batch : batch + run].reshape(-1).astype(jnp.int32)
-    target = jnp.sum(flat[:, batch + run : size], axis=0)
-    own_total = lax.dynamic_slice_in_dim(total, rep * rows_local, rows_local, 0)
-    loss = SCALE + jnp.log(own_total) - target
-
+    near = jnp.stack(near).reshape(groups, -1)
+    sums = jnp.sum(near[:, : 2 * batch], axis=0)
+    wanted = near[:, 2 * batch :].reshape(groups, reps, run)
+    every = [
+        swap(jnp.concatenate([sums, pick(wanted, "rep", k, 1).reshape(-1)]).reshape(-1, 128), "rep", k)
+        for k in range(reps)
+    ]
+    every = jnp.stack(every).reshape(reps, -1)
+    sums = jnp.sum(every[:, : 2 * batch], axis=0)
+    slots = every[:, 2 * batch :].reshape(-1).astype(jnp.int32)
+    total, target = sums[:batch], sums[batch:]
+    losses = SCALE + jnp.log(total) - target
+    loss = lax.dynamic_slice_in_dim(losses, rep * rows_local, rows_local, 0)
+
+    rows_b = relay(cut, run - cut, [total])
     weight_grad = weight_gradient(base, emb, labels, stats, total, class_weights)
-    rows2, from2 = direct(plan[2], [total])
-
-    grad = tie(a / total[:, None] - b, [weight_grad, *rows1])
-    parts = lax.all_to_all(grad.reshape(peers, share, width), ALL, 0, 0, tiled=True)
-    own = jnp.sum(parts, axis=0)
-    embedding_gradient = lax.all_to_all(
-        jnp.broadcast_to(own[None], (groups, share, width)), "grp", 0, 0, tiled=True
-    ).reshape(rows_local, width)
-
-    held, token = place_rows(info, slots, rows0 + rows1, from0 + from1, groups, None, classes, run)
-    rows3, from3 = direct(plan[3], [token])
-    moved = hop(near, [weight_grad])
-    moved |= hop([0], [weight_grad])
-    rows, origins = spread(moved, [0] + near)
-    held, _ = place_rows(
-        info, slots, [rows, *rows2], origins + from2, groups, held, classes, run
-    )
-    refreshed = place_and_blend(info, slots, rows3, from3, groups, held, class_weights, run)
+    held, token = place_rows(me, slots, rows_a, peers, run, 0)
+
+    grad = tie(a / total[:, None] - b, [weight_grad, token])
+    grad = grad.reshape(reps, groups, share, width)
+    grad = sum(swap(pick(grad, "grp", j, 1), "grp", j) for j in range(groups))
+    own = sum(swap(pick(grad, "rep", k, 0), "rep", k) for k in range(reps))
+    shares = jnp.stack([swap(own, "grp", j) for j in range(groups)])
+    embedding_gradient = shares[grp ^ jnp.arange(groups)].reshape(rows_local, width)
+
+    refreshed = place_and_blend(me, slots, rows_b, held, class_weights, peers, run, cut)
     return (loss, embedding_gradient, weight_grad, refreshed)
 
 

time: 199 us -> 172 us (0.86)
  the two profiles are of different devices: /device:TPU:16 before, /device:TPU:0 now
where the time goes in v6:
time: 172 us; the launch traced here: 171 us
  waiting for transfers between devices  46.2 us (27%)
  Pallas kernels  46.2 us (27%)
  starting transfers between devices  45.2 us (26%)
  local copies, waits for them, and re-layouts  31 us (18%)
    ppermute x30, waiting for transfers between devices, swap(): lax.ppermute(value, axis, [(i, i ^ k) for i in range(size)])  46.2 us
    ppermute x30, starting transfers between devices, swap(): lax.ppermute(value, axis, [(i, i ^ k) for i in range(size)])  37.3 us
    unnamed x50, local copies, waits for them, and re-layouts  28.9 us
    pallas_call x1, Pallas kernels, place_and_blend(): pl.pallas_call(functools.partial(blend_kernel, peers=peers, run=run, firs...  12.9 us
    pallas_call x1, Pallas kernels, forward(): pl.pallas_call(functools.partial(forward_kernel, classes=classes, reps=re...  11.6 us
    pallas_call x1, Pallas kernels, place_rows(): pl.pallas_call(functools.partial(place_kernel, peers=peers, run=run, firs...  10.3 us
    pallas_call x1, Pallas kernels, weight_gradient(): pl.pallas_call(weight_kernel, grid=(classes // tile,), in_specs=[pl.Block...  9.49 us
    all_to_all x2, starting transfers between devices, relay(): lax.all_to_all(sent, ALL, 0, 0, tiled=True).reshape(peers * size, width)  7.83 us
  transfers between devices with their start and end apart: 32, of which 11 were waited for; matrix products, arithmetic and copies ran while one was open for 1% of the time, Pallas kernels for 26%

profile of v6, /device:TPU:0, one launch (start us, length us, event | category | flops | bytes accessed | tf_op | source)
XLA Modules:
  0.0 170.9 jit_solution(6348294603620578263)
XLA Ops:
  0.6 0.5 collective-permute-start
  1.1 2.7 %collective-permute-start.1 = (bf16[64,256]{1,0:T(8,128)(2,1)}, bf16[64,256]{1,0:T(8,128)(2,1)S(1)}, u32[]{:S(2)}, u32[]{:S(2)}) collective-permute-start(bf16[64,256]{1,0:T(8,128)(2,1)} %refs_0_.1), channel_id=1, source_target_pairs={{0,2},{1,3},{2,0},{3,1},{4,6},{5,7},{6,4},{7,5},{8,10},{9,11},{10,... | collective-permute-start | bytes 98312 | tf_op jit(solution)/shard_map/ppermute | solution.py:341
  3.9 2.8 %collective-permute-start.3 = (bf16[64,256]{1,0:T(8,128)(2,1)}, bf16[64,256]{1,0:T(8,128)(2,1)S(1)}, u32[]{:S(2)}, u32[]{:S(2)}) collective-permute-start(bf16[64,256]{1,0:T(8,128)(2,1)} %refs_0_.1), channel_id=1, source_target_pairs={{0,4},{1,5},{2,6},{3,7},{4,0},{5,1},{6,2},{7,3},{8,12},{9,13},{10,... | collective-permute-start | bytes 98312 | tf_op jit(solution)/shard_map/ppermute | solution.py:341
  6.6 3.6 %collective-permute-start.5 = (bf16[64,256]{1,0:T(8,128)(2,1)}, bf16[64,256]{1,0:T(8,128)(2,1)S(1)}, u32[]{:S(2)}, u32[]{:S(2)}) collective-permute-start(bf16[64,256]{1,0:T(8,128)(2,1)} %refs_0_.1), channel_id=1, source_target_pairs={{0,6},{1,7},{2,4},{3,5},{4,2},{5,3},{6,0},{7,1},{8,14},{9,15},{10,... | collective-permute-start | bytes 98312 | tf_op jit(solution)/shard_map/ppermute | solution.py:341
  10.3 0.8 collective-permute-done.4.refs_5_.refs_4_
  11.2 2.0 %collective-permute-done.5.refs_6_.refs_5_ = bf16[64,256]{1,0:T(8,128)(2,1)S(1)} collective-permute-done((bf16[64,256]{1,0:T(8,128)(2,1)}, bf16[64,256]{1,0:T(8,128)(2,1)S(1)}, u32[]{:S(2)}, u32[]{:S(2)}) %collective-permute-start.5) | collective-permute-done | bytes 32800 | tf_op jit(solution)/shard_map/ppermute | solution.py:341
  13.2 2.4 %collective-permute-done.6.refs_7_.refs_6_ = bf16[64,256]{1,0:T(8,128)(2,1)S(1)} collective-permute-done((bf16[64,256]{1,0:T(8,128)(2,1)}, bf16[64,256]{1,0:T(8,128)(2,1)S(1)}, u32[]{:S(2)}, u32[]{:S(2)}) %collective-permute-start.6) | collective-permute-done | bytes 32800 | tf_op jit(solution)/shard_map/ppermute | solution.py:341
  15.6 2.2 %copy-done = bf16[8192,256]{1,0:T(8,128)(2,1)S(1)} copy-done((bf16[8192,256]{1,0:T(8,128)(2,1)S(1)}, bf16[8192,256]{1,0:T(8,128)(2,1)}, u32[]{:S(2)}) %copy-start) | copy-done | bytes 4194328
  17.8 1.7 %fetch.2 = bf16[32,160,256]{2,1,0:T(8,128)(2,1)} custom-call(bf16[32,256,256]{2,1,0:T(8,128)(2,1)S(1)} %bitcast.99, bf16[64,256]{1,0:T(8,128)(2,1)S(1)} %collective-permute-done.refs_1_.refs_0_, bf16[64,256]{1,0:T(8,128)(2,1)S(1)} %collective-permute-done.1.refs_2_.refs_1_, bf16[64,256]{1,0:T(8,128)(2,1)S(1)} %collective-permute-done.2.refs_3_.refs_2_, ...), custom_call_target="tpu_custom_call" | custom-call | flops 1 | bytes 1 | tf_op jit(solution)/shard_map/fetch/pallas_call | solution.py:203
  19.5 0.6 copy-done.10
  20.1 0.6 copy-done.12
  20.7 0.6 copy-done.14
  21.4 3.1 %all-to-all-start = ((bf16[32,160,256]{2,1,0:T(8,128)(2,1)}), bf16[32,160,256]{2,1,0:T(8,128)(2,1)S(1)}, u32[]{:S(2)}, u32[]{:S(2)}) async-start(bf16[32,160,256]{2,1,0:T(8,128)(2,1)} %fetch.2), calls=%async_computation | async-start | bytes 5242880 | tf_op jit(solution)/shard_map/all_to_all | solution.py:353
  24.8 2.2 %copy-done.6 = bf16[8192,256]{1,0:T(8,128)(2,1)S(1)} copy-done((bf16[8192,256]{1,0:T(8,128)(2,1)S(1)}, bf16[8192,256]{1,0:T(8,128)(2,1)}, u32[]{:S(2)}) %copy-start.6) | copy-done | bytes 4194328
  26.9 0.8 copy-done.11
  27.7 0.8 copy-done.13
  28.5 0.8 copy-done.15
  29.2 0.8 copy-done.19
  30.0 11.6 %forward_sums.1 = (bf16[512,256]{1,0:T(8,128)(2,1)S(1)}, f32[512,256]{1,0:T(8,128)S(1)}, f32[512,256]{1,0:T(8,128)S(1)}, f32[8,512]{1,0:T(8,128)S(1)}) custom-call(s32[1]{0:T(128)S(6)} %mul.10.base_ref, s32[1]{0:T(128)} %bitcast.1.rep_ref, s32[512,1]{1,0:T(8,128)S(1)} %copy.11.lab_ref, bf16[8192,256]{1,0:T(8,128)(2,1)S(1)} %copy-done.6, ...), custom_call_target="tpu_custom_call" | custom-call | flops 12884901888 | bytes 4194304 | tf_op jit(solution)/shard_map/forward_sums/pallas_call | solution.py:101
  41.6 0.8 copy-done.9
  42.4 0.7 copy-done.20
  43.1 0.6 copy-done.17
  43.7 1.8 %collective-permute-start.8 = (f32[24,128]{1,0:T(8,128)S(1)}, f32[24,128]{1,0:T(8,128)S(1)}, u32[]{:S(2)}, u32[]{:S(2)}) collective-permute-start(f32[24,128]{1,0:T(8,128)S(1)} %get-tuple-element.53), channel_id=1, source_target_pairs={{0,16},{8,24},{16,0},{24,8},{1,17},{9,25},{17,1},{25,9},{2,18},{10... | collective-permute-start | bytes 36872 | tf_op jit(solution)/shard_map/ppermute | solution.py:341
  45.5 1.5 collective-permute-start.9
  47.0 0.3 collective-permute-start.7
  47.2 0.8 collective-permute-done.8
  48.0 4.0 %collective-permute-done.9 = f32[24,128]{1,0:T(8,128)S(1)} collective-permute-done((f32[24,128]{1,0:T(8,128)S(1)}, f32[24,128]{1,0:T(8,128)S(1)}, u32[]{:S(2)}, u32[]{:S(2)}) %collective-permute-start.9) | collective-permute-done | bytes 12320 | tf_op jit(solution)/shard_map/ppermute | solution.py:341
  52.2 0.3 collective-permute-start.11
  52.5 1.5 collective-permute-start.12
  54.1 1.2 collective-permute-start.13
  55.2 1.4 collective-permute-start.14
  56.7 2.1 %collective-permute-start.15 = (f32[16,128]{1,0:T(8,128)S(1)}, f32[16,128]{1,0:T(8,128)S(1)}, u32[]{:S(2)}, u32[]{:S(2)}) collective-permute-start(f32[16,128]{1,0:T(8,128)S(1)} %get-tuple-element.49), channel_id=1, source_target_pairs={{0,6},{1,7},{2,4},{3,5},{4,2},{5,3},{6,0},{7,1},{8,14},{9,15},{10,... | collective-permute-start | bytes 24584 | tf_op jit(solution)/shard_map/ppermute | solution.py:341
  58.8 9.2 %collective-permute-done.11 = f32[16,128]{1,0:T(8,128)S(1)} collective-permute-done((f32[16,128]{1,0:T(8,128)S(1)}, f32[16,128]{1,0:T(8,128)S(1)}, u32[]{:S(2)}, u32[]{:S(2)}) %collective-permute-start.11) | collective-permute-done | bytes 8224 | tf_op jit(solution)/shard_map/ppermute | solution.py:341
  68.0 2.3 %collective-permute-start.16 = (f32[16,128]{1,0:T(8,128)S(1)}, f32[16,128]{1,0:T(8,128)S(1)}, u32[]{:S(2)}, u32[]{:S(2)}) collective-permute-start(f32[16,128]{1,0:T(8,128)S(1)} %get-tuple-element.44), channel_id=1, source_target_pairs={{0,7},{1,6},{2,5},{3,4},{4,3},{5,2},{6,1},{7,0},{8,15},{9,14},{10,... | collective-permute-start | bytes 24584 | tf_op jit(solution)/shard_map/ppermute | solution.py:341
  70.3 15.2 %collective-permute-done.13 = f32[16,128]{1,0:T(8,128)S(1)} collective-permute-done((f32[16,128]{1,0:T(8,128)S(1)}, f32[16,128]{1,0:T(8,128)S(1)}, u32[]{:S(2)}, u32[]{:S(2)}) %collective-permute-start.13) | collective-permute-done | bytes 8224 | tf_op jit(solution)/shard_map/ppermute | solution.py:341
  85.7 2.2 %copy-done.1 = bf16[8192,256]{1,0:T(8,128)(2,1)S(1)} copy-done((bf16[8192,256]{1,0:T(8,128)(2,1)S(1)}, bf16[8192,256]{1,0:T(8,128)(2,1)}, u32[]{:S(2)}) %copy-start.1) | copy-done | bytes 4194328
  88.1 1.1 copy-done.5
  89.2 4.7 %all-to-all-start.1 = ((bf16[32,96,256]{2,1,0:T(8,128)(2,1)}), bf16[32,96,256]{2,1,0:T(8,128)(2,1)}, u32[]{:S(2)}, u32[]{:S(2)}) async-start(bf16[32,96,256]{2,1,0:T(8,128)(2,1)} %copy-done.5), calls=%async_computation.1 | async-start | bytes 3145728 | tf_op jit(solution)/shard_map/all_to_all | solution.py:353
  94.0 1.2 divide_subtract_fusion.value_ref
  95.2 2.2 %copy-done.7 = bf16[8192,256]{1,0:T(8,128)(2,1)S(1)} copy-done((bf16[8192,256]{1,0:T(8,128)(2,1)S(1)}, bf16[8192,256]{1,0:T(8,128)(2,1)}, u32[]{:S(2)}) %copy-start.7) | copy-done | bytes 4194328
  97.4 9.5 %weight_gradient.1.refs_0_ = f32[8192,256]{1,0:T(8,128)} custom-call(s32[1]{0:T(128)S(6)} %mul.10.base_ref, bf16[512,256]{1,0:T(8,128)(2,1)S(1)} %copy-done.21, s32[1,512]{1,0:T(1,128)S(1)} %bitcast.108, f32[8,512]{1,0:T(8,128)S(1)} %copy-done.18, f32[1,512]{1,0:T(1,128)S(1)} %bitcast.106, bf16[8192,256]{1,0:T(8,128)(2,1)S(1)} %copy-done.7), custom_call_target="tpu_custom_call" | custom-call | flops 12884901888 | bytes 12582912 | tf_op jit(solution)/shard_map/weight_gradient/pallas_call | solution.py:164
  106.8 10.3 %place_rows.1 = (f32[16384,128]{1,0:T(8,128)S(1)}, f32[8,128]{1,0:T(8,128)S(1)}) custom-call(s32[1]{0:T(128)} %bitcast.me_ref, s32[8192]{0:T(1024)S(1)} %bitcast.104, bf16[5120,256]{1,0:T(8,128)(2,1)S(1)} %bitcast.101), custom_call_target="tpu_custom_call" | custom-call | bytes 20971520 | tf_op jit(solution)/shard_map/place_rows/pallas_call | solution.py:262
  117.1 6.4 %copy-done.2 = f32[8192,256]{1,0:T(8,128)S(1)} copy-done((f32[8192,256]{1,0:T(8,128)S(1)}, f32[8192,256]{1,0:T(8,128)}, u32[]{:S(2)}) %copy-start.2) | copy-done | bytes 8388632
  123.6 1.6 collective-permute-start.17
  125.2 1.5 collective-permute-start.18
  126.7 0.5 collective-permute-start.19
  127.2 3.2 %collective-permute-done.17 = f32[8,16,256]{2,1,0:T(8,128)S(1)} collective-permute-done((f32[8,16,256]{2,1,0:T(8,128)S(1)}, f32[8,16,256]{2,1,0:T(8,128)S(1)}, u32[]{:S(2)}, u32[]{:S(2)}) %collective-permute-start.17) | collective-permute-done | bytes 131104 | tf_op jit(solution)/shard_map/ppermute | solution.py:341
  130.3 4.6 %collective-permute-done.18 = f32[8,16,256]{2,1,0:T(8,128)S(1)} collective-permute-done((f32[8,16,256]{2,1,0:T(8,128)S(1)}, f32[8,16,256]{2,1,0:T(8,128)S(1)}, u32[]{:S(2)}, u32[]{:S(2)}) %collective-permute-start.18) | collective-permute-done | bytes 131104 | tf_op jit(solution)/shard_map/ppermute | solution.py:341
  135.1 1.5 collective-permute-start.21
  136.6 0.3 collective-permute-start.22
  136.9 1.4 collective-permute-start.23
  138.3 1.2 collective-permute-start.24
  139.5 2.6 %collective-permute-start.25 = (f32[16,256]{1,0:T(8,128)S(1)}, f32[16,256]{1,0:T(8,128)S(1)}, u32[]{:S(2)}, u32[]{:S(2)}) collective-permute-start(f32[16,256]{1,0:T(8,128)S(1)} %get-tuple-element.23), channel_id=1, source_target_pairs={{0,6},{1,7},{2,4},{3,5},{4,2},{5,3},{6,0},{7,1},{8,14},{9,15},{10,... | collective-permute-start | bytes 49160 | tf_op jit(solution)/shard_map/ppermute | solution.py:341
  142.1 1.0 collective-permute-start.26
  143.1 1.9 %collective-permute-done.25 = f32[16,256]{1,0:T(8,128)S(1)} collective-permute-done((f32[16,256]{1,0:T(8,128)S(1)}, f32[16,256]{1,0:T(8,128)S(1)}, u32[]{:S(2)}, u32[]{:S(2)}) %collective-permute-start.25) | collective-permute-done | bytes 16416 | tf_op jit(solution)/shard_map/ppermute | solution.py:341
  145.1 2.0 %collective-permute-done.26 = f32[16,256]{1,0:T(8,128)S(1)} collective-permute-done((f32[16,256]{1,0:T(8,128)S(1)}, f32[16,256]{1,0:T(8,128)S(1)}, u32[]{:S(2)}, u32[]{:S(2)}) %collective-permute-start.26) | collective-permute-done | bytes 16416 | tf_op jit(solution)/shard_map/ppermute | solution.py:341
  147.1 1.0 collective-permute-start.27
  148.1 0.7 collective-permute-start.28
  148.7 1.9 %collective-permute-start.29 = (f32[16,256]{1,0:T(8,128)S(1)}, f32[16,256]{1,0:T(8,128)S(1)}, u32[]{:S(2)}, u32[]{:S(2)}) collective-permute-start(f32[16,256]{1,0:T(8,128)S(1)} %fusion.8), channel_id=1, source_target_pairs={{0,24},{8,16},{16,8},{24,0},{1,25},{9,17},{17,9},{25,1},{2,26},{10... | collective-permute-start | bytes 49160 | tf_op jit(solution)/shard_map/ppermute | solution.py:341
  150.7 0.6 dynamic_slice.91
  151.2 3.4 %copy-done.4 = f32[16384,128]{1,0:T(8,128)S(1)} copy-done((f32[16384,128]{1,0:T(8,128)S(1)}, f32[16384,128]{1,0:T(8,128)}, u32[]{:S(2)}) %copy-start.4) | copy-done | bytes 8388632
  154.6 2.2 %copy-done.8 = bf16[8192,256]{1,0:T(8,128)(2,1)S(1)} copy-done((bf16[8192,256]{1,0:T(8,128)(2,1)S(1)}, bf16[8192,256]{1,0:T(8,128)(2,1)}, u32[]{:S(2)}) %copy-start.8) | copy-done | bytes 4194328
  156.8 12.9 %place_and_blend.1 = (bf16[8192,256]{1,0:T(8,128)(2,1)}, f32[16384,128]{1,0:T(8,128)S(1)}) custom-call(s32[1]{0:T(128)} %bitcast.me_ref, s32[8192]{0:T(1024)S(1)} %bitcast.105, bf16[8192,256]{1,0:T(8,128)(2,1)S(1)} %copy-done.8, bf16[3072,256]{1,0:T(8,128)(2,1)} %bitcast.54.row_ref, f32[16384,128]{1,0:T(8,128)S(1)} %copy-done.4), custom_call_target="tpu_custom_call", output_to_operand_aliasing={{1}: (4, {})} | custom-call | bytes 25165824 | tf_op jit(solution)/shard_map/place_and_blend/pallas_call | solution.py:305
  169.7 1.2 gather_fusion
  (80 shorter events, 1.2 us)
Async XLA Ops:
  0.6 6.0 %collective-permute-start = (bf16[64,256]{1,0:T(8,128)(2,1)}, bf16[64,256]{1,0:T(8,128)(2,1)S(1)}, u32[]{:S(2)}, u32[]{:S(2)}) collective-permute-start(bf16[64,256]{1,0:T(8,128)(2,1)} %refs_0_.1), channel_id=1, source_target_pairs={{0,1},{1,0},{2,3},{3,2},{4,5},{5,4},{6,7},{7,6},{8,9},{9,8},{10,11... | collective-permute-start | bytes 98312 | tf_op jit(solution)/shard_map/ppermute | solution.py:341
  1.1 9.1 %collective-permute-start.1 = (bf16[64,256]{1,0:T(8,128)(2,1)}, bf16[64,256]{1,0:T(8,128)(2,1)S(1)}, u32[]{:S(2)}, u32[]{:S(2)}) collective-permute-start(bf16[64,256]{1,0:T(8,128)(2,1)} %refs_0_.1), channel_id=1, source_target_pairs={{0,2},{1,3},{2,0},{3,1},{4,6},{5,7},{6,4},{7,5},{8,10},{9,11},{10,... | collective-permute-start | bytes 98312 | tf_op jit(solution)/shard_map/ppermute | solution.py:341
  3.8 6.5 %collective-permute-start.2 = (bf16[64,256]{1,0:T(8,128)(2,1)}, bf16[64,256]{1,0:T(8,128)(2,1)S(1)}, u32[]{:S(2)}, u32[]{:S(2)}) collective-permute-start(bf16[64,256]{1,0:T(8,128)(2,1)} %refs_0_.1), channel_id=1, source_target_pairs={{0,3},{1,2},{2,1},{3,0},{4,7},{5,6},{6,5},{7,4},{8,11},{9,10},{10,... | collective-permute-start | bytes 98312 | tf_op jit(solution)/shard_map/ppermute | solution.py:341
  3.9 6.5 %collective-permute-start.3 = (bf16[64,256]{1,0:T(8,128)(2,1)}, bf16[64,256]{1,0:T(8,128)(2,1)S(1)}, u32[]{:S(2)}, u32[]{:S(2)}) collective-permute-start(bf16[64,256]{1,0:T(8,128)(2,1)} %refs_0_.1), channel_id=1, source_target_pairs={{0,4},{1,5},{2,6},{3,7},{4,0},{5,1},{6,2},{7,3},{8,12},{9,13},{10,... | collective-permute-start | bytes 98312 | tf_op jit(solution)/shard_map/ppermute | solution.py:341
  6.6 4.6 %collective-permute-start.4 = (bf16[64,256]{1,0:T(8,128)(2,1)}, bf16[64,256]{1,0:T(8,128)(2,1)S(1)}, u32[]{:S(2)}, u32[]{:S(2)}) collective-permute-start(bf16[64,256]{1,0:T(8,128)(2,1)} %refs_0_.1), channel_id=1, source_target_pairs={{0,5},{1,4},{2,7},{3,6},{4,1},{5,0},{6,3},{7,2},{8,13},{9,12},{10,... | collective-permute-start | bytes 98312 | tf_op jit(solution)/shard_map/ppermute | solution.py:341
  6.6 6.6 %collective-permute-start.5 = (bf16[64,256]{1,0:T(8,128)(2,1)}, bf16[64,256]{1,0:T(8,128)(2,1)S(1)}, u32[]{:S(2)}, u32[]{:S(2)}) collective-permute-start(bf16[64,256]{1,0:T(8,128)(2,1)} %refs_0_.1), channel_id=1, source_target_pairs={{0,6},{1,7},{2,4},{3,5},{4,2},{5,3},{6,0},{7,1},{8,14},{9,15},{10,... | collective-permute-start | bytes 98312 | tf_op jit(solution)/shard_map/ppermute | solution.py:341
  10.2 5.4 %collective-permute-start.6 = (bf16[64,256]{1,0:T(8,128)(2,1)}, bf16[64,256]{1,0:T(8,128)(2,1)S(1)}, u32[]{:S(2)}, u32[]{:S(2)}) collective-permute-start(bf16[64,256]{1,0:T(8,128)(2,1)} %refs_0_.1), channel_id=1, source_target_pairs={{0,7},{1,6},{2,5},{3,4},{4,3},{5,2},{6,1},{7,0},{8,15},{9,14},{10,... | collective-permute-start | bytes 98312 | tf_op jit(solution)/shard_map/ppermute | solution.py:341
  15.6 2.2 %copy-start = (bf16[8192,256]{1,0:T(8,128)(2,1)S(1)}, bf16[8192,256]{1,0:T(8,128)(2,1)}, u32[]{:S(2)}) copy-start(bf16[8192,256]{1,0:T(8,128)(2,1)} %param.8) | copy-start | bytes 12582916
  19.5 0.6 copy-start.10
  20.1 0.6 copy-start.12
  20.7 0.6 copy-start.14
  21.3 3.1 %copy-start.22 = (s32[8192]{0:T(1024)S(1)}, s32[8192]{0:T(1024)}, u32[]{:S(2)}) copy-start(s32[8192]{0:T(1024)} %param.9) | copy-start | bytes 98308
  21.4 3.2 %copy-start.16 = (s32[512]{0:T(512)S(1)}, s32[512]{0:T(512)}, u32[]{:S(2)}) copy-start(s32[512]{0:T(512)} %param.6) | copy-start | bytes 6148
  21.4 67.8 %all-to-all-start = ((bf16[32,160,256]{2,1,0:T(8,128)(2,1)}), bf16[32,160,256]{2,1,0:T(8,128)(2,1)S(1)}, u32[]{:S(2)}, u32[]{:S(2)}) async-start(bf16[32,160,256]{2,1,0:T(8,128)(2,1)} %fetch.2), calls=%async_computation | async-start | bytes 5242880 | tf_op jit(solution)/shard_map/all_to_all | solution.py:353
  24.8 2.2 %copy-start.6 = (bf16[8192,256]{1,0:T(8,128)(2,1)S(1)}, bf16[8192,256]{1,0:T(8,128)(2,1)}, u32[]{:S(2)}) copy-start(bf16[8192,256]{1,0:T(8,128)(2,1)} %w_ref.5) | copy-start | bytes 12582916
  26.9 0.8 copy-start.11
  27.7 0.8 copy-start.13
  28.5 0.8 copy-start.15
  29.2 0.8 copy-start.19
  41.6 0.8 copy-start.9
  42.4 0.7 copy-start.20
  43.1 0.6 copy-start.17
  43.7 4.3 %collective-permute-start.8 = (f32[24,128]{1,0:T(8,128)S(1)}, f32[24,128]{1,0:T(8,128)S(1)}, u32[]{:S(2)}, u32[]{:S(2)}) collective-permute-start(f32[24,128]{1,0:T(8,128)S(1)} %get-tuple-element.53), channel_id=1, source_target_pairs={{0,16},{8,24},{16,0},{24,8},{1,17},{9,25},{17,1},{25,9},{2,18},{10... | collective-permute-start | bytes 36872 | tf_op jit(solution)/shard_map/ppermute | solution.py:341
  45.5 6.5 %collective-permute-start.9 = (f32[24,128]{1,0:T(8,128)S(1)}, f32[24,128]{1,0:T(8,128)S(1)}, u32[]{:S(2)}, u32[]{:S(2)}) collective-permute-start(f32[24,128]{1,0:T(8,128)S(1)} %get-tuple-element.54), channel_id=1, source_target_pairs={{0,24},{8,16},{16,8},{24,0},{1,25},{9,17},{17,9},{25,1},{2,26},{10... | collective-permute-start | bytes 36872 | tf_op jit(solution)/shard_map/ppermute | solution.py:341
  47.0 5.0 %collective-permute-start.7 = (f32[24,128]{1,0:T(8,128)S(1)}, f32[24,128]{1,0:T(8,128)S(1)}, u32[]{:S(2)}, u32[]{:S(2)}) collective-permute-start(f32[24,128]{1,0:T(8,128)S(1)} %get-tuple-element.52), channel_id=1, source_target_pairs={{0,8},{8,0},{16,24},{24,16},{1,9},{9,1},{17,25},{25,17},{2,10},{10... | collective-permute-start | bytes 36872 | tf_op jit(solution)/shard_map/ppermute | solution.py:341
  52.2 4.5 %collective-permute-start.10 = (f32[16,128]{1,0:T(8,128)S(1)}, f32[16,128]{1,0:T(8,128)S(1)}, u32[]{:S(2)}, u32[]{:S(2)}) collective-permute-start(f32[16,128]{1,0:T(8,128)S(1)} %get-tuple-element.50), channel_id=1, source_target_pairs={{0,1},{1,0},{2,3},{3,2},{4,5},{5,4},{6,7},{7,6},{8,9},{9,8},{10,11... | collective-permute-start | bytes 24584 | tf_op jit(solution)/shard_map/ppermute | solution.py:341
  52.2 15.8 %collective-permute-start.11 = (f32[16,128]{1,0:T(8,128)S(1)}, f32[16,128]{1,0:T(8,128)S(1)}, u32[]{:S(2)}, u32[]{:S(2)}) collective-permute-start(f32[16,128]{1,0:T(8,128)S(1)} %get-tuple-element.45), channel_id=1, source_target_pairs={{0,2},{1,3},{2,0},{3,1},{4,6},{5,7},{6,4},{7,5},{8,10},{9,11},{10,... | collective-permute-start | bytes 24584 | tf_op jit(solution)/shard_map/ppermute | solution.py:341
  52.5 17.8 %collective-permute-start.12 = (f32[16,128]{1,0:T(8,128)S(1)}, f32[16,128]{1,0:T(8,128)S(1)}, u32[]{:S(2)}, u32[]{:S(2)}) collective-permute-start(f32[16,128]{1,0:T(8,128)S(1)} %get-tuple-element.46), channel_id=1, source_target_pairs={{0,3},{1,2},{2,1},{3,0},{4,7},{5,6},{6,5},{7,4},{8,11},{9,10},{10,... | collective-permute-start | bytes 24584 | tf_op jit(solution)/shard_map/ppermute | solution.py:341
  54.1 31.4 %collective-permute-start.13 = (f32[16,128]{1,0:T(8,128)S(1)}, f32[16,128]{1,0:T(8,128)S(1)}, u32[]{:S(2)}, u32[]{:S(2)}) collective-permute-start(f32[16,128]{1,0:T(8,128)S(1)} %get-tuple-element.47), channel_id=1, source_target_pairs={{0,4},{1,5},{2,6},{3,7},{4,0},{5,1},{6,2},{7,3},{8,12},{9,13},{10,... | collective-permute-start | bytes 24584 | tf_op jit(solution)/shard_map/ppermute | solution.py:341
  55.2 30.3 %collective-permute-start.14 = (f32[16,128]{1,0:T(8,128)S(1)}, f32[16,128]{1,0:T(8,128)S(1)}, u32[]{:S(2)}, u32[]{:S(2)}) collective-permute-start(f32[16,128]{1,0:T(8,128)S(1)} %get-tuple-element.48), channel_id=1, source_target_pairs={{0,5},{1,4},{2,7},{3,6},{4,1},{5,0},{6,3},{7,2},{8,13},{9,12},{10,... | collective-permute-start | bytes 24584 | tf_op jit(solution)/shard_map/ppermute | solution.py:341
  56.7 28.9 %collective-permute-start.15 = (f32[16,128]{1,0:T(8,128)S(1)}, f32[16,128]{1,0:T(8,128)S(1)}, u32[]{:S(2)}, u32[]{:S(2)}) collective-permute-start(f32[16,128]{1,0:T(8,128)S(1)} %get-tuple-element.49), channel_id=1, source_target_pairs={{0,6},{1,7},{2,4},{3,5},{4,2},{5,3},{6,0},{7,1},{8,14},{9,15},{10,... | collective-permute-start | bytes 24584 | tf_op jit(solution)/shard_map/ppermute | solution.py:341
  68.0 17.6 %collective-permute-start.16 = (f32[16,128]{1,0:T(8,128)S(1)}, f32[16,128]{1,0:T(8,128)S(1)}, u32[]{:S(2)}, u32[]{:S(2)}) collective-permute-start(f32[16,128]{1,0:T(8,128)S(1)} %get-tuple-element.44), channel_id=1, source_target_pairs={{0,7},{1,6},{2,5},{3,4},{4,3},{5,2},{6,1},{7,0},{8,15},{9,14},{10,... | collective-permute-start | bytes 24584 | tf_op jit(solution)/shard_map/ppermute | solution.py:341
  85.7 2.2 %copy-start.1 = (bf16[8192,256]{1,0:T(8,128)(2,1)S(1)}, bf16[8192,256]{1,0:T(8,128)(2,1)}, u32[]{:S(2)}) copy-start(bf16[8192,256]{1,0:T(8,128)(2,1)} %param.8) | copy-start | bytes 12582916
  87.9 7.3 %copy-start.18 = (f32[8,512]{1,0:T(8,128)S(1)}, f32[8,512]{1,0:T(8,128)}, u32[]{:S(2)}) copy-start(f32[8,512]{1,0:T(8,128)} %copy-done.17) | copy-start | bytes 49156
  87.9 7.3 %copy-start.21 = (bf16[512,256]{1,0:T(8,128)(2,1)S(1)}, bf16[512,256]{1,0:T(8,128)(2,1)}, u32[]{:S(2)}) copy-start(bf16[512,256]{1,0:T(8,128)(2,1)} %copy-done.20) | copy-start | bytes 786436
  88.1 1.1 copy-start.5
  89.2 62.0 %all-to-all-start.1 = ((bf16[32,96,256]{2,1,0:T(8,128)(2,1)}), bf16[32,96,256]{2,1,0:T(8,128)(2,1)}, u32[]{:S(2)}, u32[]{:S(2)}) async-start(bf16[32,96,256]{2,1,0:T(8,128)(2,1)} %copy-done.5), calls=%async_computation.1 | async-start | bytes 3145728 | tf_op jit(solution)/shard_map/all_to_all | solution.py:353
  95.2 2.2 %copy-start.7 = (bf16[8192,256]{1,0:T(8,128)(2,1)S(1)}, bf16[8192,256]{1,0:T(8,128)(2,1)}, u32[]{:S(2)}) copy-start(bf16[8192,256]{1,0:T(8,128)(2,1)} %w_ref.5) | copy-start | bytes 12582916
  117.1 6.5 %copy-start.3 = (f32[16384,128]{1,0:T(8,128)}, f32[16384,128]{1,0:T(8,128)S(1)}, u32[]{:S(2)}) copy-start(f32[16384,128]{1,0:T(8,128)S(1)} %get-tuple-element.16._) | copy-start | bytes 25165828
  117.1 6.4 %copy-start.2 = (f32[8192,256]{1,0:T(8,128)S(1)}, f32[8192,256]{1,0:T(8,128)}, u32[]{:S(2)}) copy-start(f32[8192,256]{1,0:T(8,128)} %weight_gradient.1.refs_0_) | copy-start | bytes 25165828
  123.6 6.7 %collective-permute-start.17 = (f32[8,16,256]{2,1,0:T(8,128)S(1)}, f32[8,16,256]{2,1,0:T(8,128)S(1)}, u32[]{:S(2)}, u32[]{:S(2)}) collective-permute-start(f32[8,16,256]{2,1,0:T(8,128)S(1)} %get-tuple-element.18), channel_id=1, source_target_pairs={{0,8},{8,0},{16,24},{24,16},{1,9},{9,1},{17,25},{25,17},{2,10},{10... | collective-permute-start | bytes 393224 | tf_op jit(solution)/shard_map/ppermute | solution.py:341
  125.2 9.7 %collective-permute-start.18 = (f32[8,16,256]{2,1,0:T(8,128)S(1)}, f32[8,16,256]{2,1,0:T(8,128)S(1)}, u32[]{:S(2)}, u32[]{:S(2)}) collective-permute-start(f32[8,16,256]{2,1,0:T(8,128)S(1)} %get-tuple-element.20), channel_id=1, source_target_pairs={{0,16},{8,24},{16,0},{24,8},{1,17},{9,25},{17,1},{25,9},{2,18},{10... | collective-permute-start | bytes 393224 | tf_op jit(solution)/shard_map/ppermute | solution.py:341
  126.7 8.2 %collective-permute-start.19 = (f32[8,16,256]{2,1,0:T(8,128)S(1)}, f32[8,16,256]{2,1,0:T(8,128)S(1)}, u32[]{:S(2)}, u32[]{:S(2)}) collective-permute-start(f32[8,16,256]{2,1,0:T(8,128)S(1)} %get-tuple-element.19), channel_id=1, source_target_pairs={{0,24},{8,16},{16,8},{24,0},{1,25},{9,17},{17,9},{25,1},{2,26},{10... | collective-permute-start | bytes 393224 | tf_op jit(solution)/shard_map/ppermute | solution.py:341
  135.0 4.5 %collective-permute-start.20 = (f32[16,256]{1,0:T(8,128)S(1)}, f32[16,256]{1,0:T(8,128)S(1)}, u32[]{:S(2)}, u32[]{:S(2)}) collective-permute-start(f32[16,256]{1,0:T(8,128)S(1)} %get-tuple-element.21), channel_id=1, source_target_pairs={{0,1},{1,0},{2,3},{3,2},{4,5},{5,4},{6,7},{7,6},{8,9},{9,8},{10,11... | collective-permute-start | bytes 49160 | tf_op jit(solution)/shard_map/ppermute | solution.py:341
  135.1 7.1 %collective-permute-start.21 = (f32[16,256]{1,0:T(8,128)S(1)}, f32[16,256]{1,0:T(8,128)S(1)}, u32[]{:S(2)}, u32[]{:S(2)}) collective-permute-start(f32[16,256]{1,0:T(8,128)S(1)} %get-tuple-element.27), channel_id=1, source_target_pairs={{0,2},{1,3},{2,0},{3,1},{4,6},{5,7},{6,4},{7,5},{8,10},{9,11},{10,... | collective-permute-start | bytes 49160 | tf_op jit(solution)/shard_map/ppermute | solution.py:341
  136.6 6.5 %collective-permute-start.22 = (f32[16,256]{1,0:T(8,128)S(1)}, f32[16,256]{1,0:T(8,128)S(1)}, u32[]{:S(2)}, u32[]{:S(2)}) collective-permute-start(f32[16,256]{1,0:T(8,128)S(1)} %get-tuple-element.26), channel_id=1, source_target_pairs={{0,3},{1,2},{2,1},{3,0},{4,7},{5,6},{6,5},{7,4},{8,11},{9,10},{10,... | collective-permute-start | bytes 49160 | tf_op jit(solution)/shard_map/ppermute | solution.py:341
  136.9 6.2 %collective-permute-start.23 = (f32[16,256]{1,0:T(8,128)S(1)}, f32[16,256]{1,0:T(8,128)S(1)}, u32[]{:S(2)}, u32[]{:S(2)}) collective-permute-start(f32[16,256]{1,0:T(8,128)S(1)} %get-tuple-element.25), channel_id=1, source_target_pairs={{0,4},{1,5},{2,6},{3,7},{4,0},{5,1},{6,2},{7,3},{8,12},{9,13},{10,... | collective-permute-start | bytes 49160 | tf_op jit(solution)/shard_map/ppermute | solution.py:341
  138.3 4.8 %collective-permute-start.24 = (f32[16,256]{1,0:T(8,128)S(1)}, f32[16,256]{1,0:T(8,128)S(1)}, u32[]{:S(2)}, u32[]{:S(2)}) collective-permute-start(f32[16,256]{1,0:T(8,128)S(1)} %get-tuple-element.24), channel_id=1, source_target_pairs={{0,5},{1,4},{2,7},{3,6},{4,1},{5,0},{6,3},{7,2},{8,13},{9,12},{10,... | collective-permute-start | bytes 49160 | tf_op jit(solution)/shard_map/ppermute | solution.py:341
  139.5 5.5 %collective-permute-start.25 = (f32[16,256]{1,0:T(8,128)S(1)}, f32[16,256]{1,0:T(8,128)S(1)}, u32[]{:S(2)}, u32[]{:S(2)}) collective-permute-start(f32[16,256]{1,0:T(8,128)S(1)} %get-tuple-element.23), channel_id=1, source_target_pairs={{0,6},{1,7},{2,4},{3,5},{4,2},{5,3},{6,0},{7,1},{8,14},{9,15},{10,... | collective-permute-start | bytes 49160 | tf_op jit(solution)/shard_map/ppermute | solution.py:341
  142.1 5.0 %collective-permute-start.26 = (f32[16,256]{1,0:T(8,128)S(1)}, f32[16,256]{1,0:T(8,128)S(1)}, u32[]{:S(2)}, u32[]{:S(2)}) collective-permute-start(f32[16,256]{1,0:T(8,128)S(1)} %get-tuple-element.22), channel_id=1, source_target_pairs={{0,7},{1,6},{2,5},{3,4},{4,3},{5,2},{6,1},{7,0},{8,15},{9,14},{10,... | collective-permute-start | bytes 49160 | tf_op jit(solution)/shard_map/ppermute | solution.py:341
  147.1 22.6 %collective-permute-start.27 = (f32[16,256]{1,0:T(8,128)S(1)}, f32[16,256]{1,0:T(8,128)S(1)}, u32[]{:S(2)}, u32[]{:S(2)}) collective-permute-start(f32[16,256]{1,0:T(8,128)S(1)} %fusion.8), channel_id=1, source_target_pairs={{0,8},{8,0},{16,24},{24,16},{1,9},{9,1},{17,25},{25,17},{2,10},{10... | collective-permute-start | bytes 49160 | tf_op jit(solution)/shard_map/ppermute | solution.py:341
  148.1 21.6 %collective-permute-start.28 = (f32[16,256]{1,0:T(8,128)S(1)}, f32[16,256]{1,0:T(8,128)S(1)}, u32[]{:S(2)}, u32[]{:S(2)}) collective-permute-start(f32[16,256]{1,0:T(8,128)S(1)} %fusion.8), channel_id=1, source_target_pairs={{0,16},{8,24},{16,0},{24,8},{1,17},{9,25},{17,1},{25,9},{2,18},{10... | collective-permute-start | bytes 49160 | tf_op jit(solution)/shard_map/ppermute | solution.py:341
  148.7 21.0 %collective-permute-start.29 = (f32[16,256]{1,0:T(8,128)S(1)}, f32[16,256]{1,0:T(8,128)S(1)}, u32[]{:S(2)}, u32[]{:S(2)}) collective-permute-start(f32[16,256]{1,0:T(8,128)S(1)} %fusion.8), channel_id=1, source_target_pairs={{0,24},{8,16},{16,8},{24,0},{1,25},{9,17},{17,9},{25,1},{2,26},{10... | collective-permute-start | bytes 49160 | tf_op jit(solution)/shard_map/ppermute | solution.py:341
  151.2 3.4 %copy-start.4 = (f32[16384,128]{1,0:T(8,128)S(1)}, f32[16384,128]{1,0:T(8,128)}, u32[]{:S(2)}) copy-start(f32[16384,128]{1,0:T(8,128)} %copy-done.3) | copy-start | bytes 25165828
  154.6 2.2 %copy-start.8 = (bf16[8192,256]{1,0:T(8,128)(2,1)S(1)}, bf16[8192,256]{1,0:T(8,128)(2,1)}, u32[]{:S(2)}) copy-start(bf16[8192,256]{1,0:T(8,128)(2,1)} %w_ref.5) | copy-start | bytes 12582916

commit v7 on v6

--- a/solution.py
+++ b/solution.py
@@ -19,6 +19,10 @@
 NT = (((1,), (1,)), ((), ()))
 
 
+def in_hbm(value):
+    return pltpu.with_memory_space_constraint(value, pltpu.HBM)
+
+
 def unit_rows(wide):
     inv = lax.rsqrt(jnp.sum(wide * wide, axis=1, keepdims=True) + 1e-06)
     return wide * inv, inv
@@ -29,9 +33,9 @@
     return jnp.transpose(jnp.broadcast_to(row, (128, lanes)))[:, :1]
 
 
-def forward_kernel(base_ref, rep_ref, lab_ref, w_ref, *refs, classes, reps):
+def forward_kernel(base_ref, rep_ref, lab_ref, w_ref, _, *refs, classes, reps):
     blocks = refs[:reps]
-    emb_ref, a_ref, b_ref, st_ref, xhat_ref, sum_ref = refs[reps:]
+    emb_ref, a_ref, b_ref, st_ref, wide_ref, xhat_ref, sum_ref = refs[reps:]
     step = pl.program_id(0)
     tile = w_ref.shape[0]
     batch = emb_ref.shape[0]
@@ -49,6 +53,8 @@
         b_ref[...] = jnp.zeros_like(b_ref)
 
     wwide, _ = unit_rows(w_ref[...].astype(jnp.float32))
+    wide_ref[pl.ds(0, tile, stride=2), :] = wwide[:, :128]
+    wide_ref[pl.ds(1, tile, stride=2), :] = wwide[:, 128:]
     what = wwide.astype(jnp.bfloat16)
     cosine = lax.dot_general(xhat_ref[...], what, NT, preferred_element_type=jnp.float32)
     ids = lax.broadcasted_iota(jnp.int32, (batch, tile), 1)
@@ -90,7 +96,7 @@
         st_ref[...] = jnp.transpose(stats)[:8, :]
 
 
-def forward(base, rep, blocks, labels, weights):
+def forward(base, rep, blocks, labels, weights, after):
     rows, width = blocks[0].shape
     reps = len(blocks)
     batch = rows * reps
@@ -106,6 +112,7 @@
             smem,
             pl.BlockSpec((batch, 1), whole),
             pl.BlockSpec((tile, width), lambda i: (i, 0)),
+            pl.BlockSpec(memory_space=pl.ANY),
         ]
         + [pl.BlockSpec((rows, width), whole)] * reps,
         out_specs=[
@@ -113,12 +120,14 @@
             pl.BlockSpec((batch, width), whole),
             pl.BlockSpec((batch, width), whole),
             pl.BlockSpec((8, batch), whole),
+            pl.BlockSpec((2 * tile, 128), lambda i: (i, 0)),
         ],
         out_shape=[
             jax.ShapeDtypeStruct((batch, width), jnp.bfloat16),
             jax.ShapeDtypeStruct((batch, width), jnp.float32),
             jax.ShapeDtypeStruct((batch, width), jnp.float32),
             jax.ShapeDtypeStruct((8, batch), jnp.float32),
+            pltpu.HBM((2 * classes, 128), jnp.float32),
         ],
         scratch_shapes=[pltpu.VMEM((batch, width), jnp.bfloat16), pltpu.VMEM((batch, 128), jnp.float32)],
         compiler_params=pltpu.CompilerParams(
@@ -128,7 +137,7 @@
             flops=12 * batch * classes * width, bytes_accessed=classes * width * 2, transcendentals=0
         ),
         name="forward_sums",
-    )(base, rep, labels.reshape(batch, 1), weights, *blocks)
+    )(base, rep, labels.reshape(batch, 1), weights, after, *blocks)
 
 
 def weight_kernel(base_ref, emb_ref, lab_ref, st_ref, tot_ref, w_ref, g_ref, xhat_ref, y_ref, v_ref):
@@ -173,7 +182,7 @@
             pl.BlockSpec((tile, width), lambda i: (i, 0)),
         ],
         out_specs=pl.BlockSpec((tile, width), lambda i: (i, 0)),
-        out_shape=jax.ShapeDtypeStruct((classes, width), jnp.float32),
+        out_shape=pltpu.HBM((classes, width), jnp.float32),
         scratch_shapes=[
             pltpu.VMEM((batch, width), jnp.bfloat16),
             pltpu.VMEM((batch, width), jnp.bfloat16),
@@ -199,10 +208,11 @@
 
 def fetch(runs, first, size, tokens):
     peers, _, width = runs.shape
+    hbm = pl.BlockSpec(memory_space=pltpu.HBM)
     anywhere = pl.BlockSpec(memory_space=pl.ANY)
     return pl.pallas_call(
         functools.partial(fetch_kernel, first=first),
-        in_specs=[anywhere] * (1 + len(tokens)),
+        in_specs=[hbm] + [anywhere] * len(tokens),
         out_specs=pl.BlockSpec(memory_space=pltpu.VMEM),
         out_shape=jax.ShapeDtypeStruct((peers, size, width), runs.dtype),
         scratch_shapes=[pltpu.SemaphoreType.DMA],
@@ -230,98 +240,121 @@
     )(value, *tokens)
 
 
-def place_runs(me_ref, slot_ref, row_ref, held_ref, stage_ref, peers, run, first):
-    size = stage_ref.shape[0] // 2
+def place_runs(me_ref, slot_ref, row_ref, held_ref, stage_ref, held_copy, peers, run, first):
+    size = row_ref.shape[0] // peers
     batch = math.gcd(size, 32)
-    for source in range(peers):
-        rows = row_ref[source * size : (source + 1) * size, :].astype(jnp.float32)
-        unit, _ = unit_rows(rows)
-        stage_ref[pl.ds(0, size, stride=2), :] = unit[:, :128]
-        stage_ref[pl.ds(1, size, stride=2), :] = unit[:, 128:]
-        start = (me_ref[0] ^ source) * run + first
-
-        def place(j, carry, start=start):
-            at = j * batch
-            slots = [slot_ref[start + at + v] for v in range(batch)]
-            values = [stage_ref[pl.ds((at + v) * 2, 2), :] for v in range(batch)]
-            for slot, value in zip(slots, values):
-                held_ref[pl.ds(slot * 2, 2), :] = value
-            return carry
-
-        lax.fori_loop(0, size // batch, place, 0)
-
-
-def place_kernel(me_ref, slot_ref, row_ref, held_ref, token_ref, stage_ref, *, peers, run, first):
+
+    def prepare(source, carry):
+        at = pl.multiple_of(source * size, size)
+        unit, _ = unit_rows(row_ref[pl.ds(at, size), :].astype(jnp.float32))
+        at = pl.multiple_of(source * 2 * size, 2 * size)
+        stage_ref[pl.ds(at, size, stride=2), :] = unit[:, :128]
+        stage_ref[pl.ds(at + 1, size, stride=2), :] = unit[:, 128:]
+        return carry
+
+    lax.fori_loop(0, peers, prepare, 0)
+    held_copy.wait()
+
+    def place(j, carry):
+        source = j // (size // batch)
+        at = (j - source * (size // batch)) * batch
+        start = (me_ref[0] ^ source) * run + first + at
+        at = (source * size + at) * 2
+        slots = [slot_ref[start + v] for v in range(batch)]
+        values = [
+            stage_ref[pl.ds(at + 2 * v, 2), :] + held_ref[pl.ds(slot, 2), :]
+            for v, slot in enumerate(slots)
+        ]
+        for slot, value in zip(slots, values):
+            held_ref[pl.ds(slot, 2), :] = value
+        return carry
+
+    lax.fori_loop(0, peers * size // batch, place, 0)
+
+
+def place_kernel(
+    me_ref, slot_ref, row_ref, in_ref, _, out_ref, token_ref, held_ref, stage_ref, sem,
+    *, peers, run, first,
+):
     token_ref[...] = jnp.zeros_like(token_ref)
-    place_runs(me_ref, slot_ref, row_ref, held_ref, stage_ref, peers, run, first)
-
-
-def place_rows(me, slots, rows, peers, run, first):
+    load = pltpu.make_async_copy(in_ref, held_ref, sem.at[0])
+    load.start()
+    place_runs(me_ref, slot_ref, row_ref, held_ref, stage_ref, load, peers, run, first)
+    store = pltpu.make_async_copy(held_ref, out_ref, sem.at[1])
+    store.start()
+    store.wait()
+
+
+def place_rows(me, slots, rows, held, after, peers, run, first):
     smem = pl.BlockSpec(memory_space=pltpu.SMEM)
     vmem = pl.BlockSpec(memory_space=pltpu.VMEM)
+    anywhere = pl.BlockSpec(memory_space=pltpu.HBM)
     return pl.pallas_call(
         functools.partial(place_kernel, peers=peers, run=run, first=first),
-        in_specs=[smem, smem, vmem],
-        out_specs=[vmem, vmem],
+        in_specs=[smem, smem, vmem, anywhere, anywhere],
+        out_specs=[anywhere, vmem],
         out_shape=[
-            jax.ShapeDtypeStruct((2 * peers * run, 128), jnp.float32),
+            pltpu.HBM(held.shape, jnp.float32),
             jax.ShapeDtypeStruct((8, 128), jnp.float32),
         ],
-        scratch_shapes=[pltpu.VMEM((2 * rows.shape[0] // peers, 128), jnp.float32)],
-        compiler_params=pltpu.CompilerParams(vmem_limit_bytes=16 * MIB),
+        scratch_shapes=[
+            pltpu.VMEM(held.shape, jnp.float32),
+            pltpu.VMEM((2 * rows.shape[0], 128), jnp.float32),
+            pltpu.SemaphoreType.DMA((2,)),
+        ],
+        compiler_params=pltpu.CompilerParams(vmem_limit_bytes=32 * MIB),
         cost_estimate=pl.CostEstimate(
             flops=0, bytes_accessed=16 * rows.shape[0] * rows.shape[1], transcendentals=0
         ),
         name="place_rows",
-    )(me, slots, rows)
+    )(me, slots, rows, held, after)
 
 
 def blend_kernel(
-    me_ref, slot_ref, w_ref, row_ref, _, o_ref, held_ref, stage_ref, *, peers, run, first
+    me_ref, slot_ref, row_ref, in_ref, o_ref, held_ref, stage_ref, sem, *, peers, run, first
 ):
     step = pl.program_id(0)
-    tile = w_ref.shape[0]
+    tile = o_ref.shape[0]
 
     @pl.when(step == 0)
     def _():
-        place_runs(me_ref, slot_ref, row_ref, held_ref, stage_ref, peers, run, first)
-
-    wwide, _ = unit_rows(w_ref[...].astype(jnp.float32))
+        load = pltpu.make_async_copy(in_ref, held_ref, sem)
+        load.start()
+        place_runs(me_ref, slot_ref, row_ref, held_ref, stage_ref, load, peers, run, first)
+
     at = pl.multiple_of(step * 2 * tile, 2 * tile)
-    low = wwide[:, :128] + held_ref[pl.ds(at, tile, stride=2), :]
-    high = wwide[:, 128:] + held_ref[pl.ds(at + 1, tile, stride=2), :]
+    low = held_ref[pl.ds(at, tile, stride=2), :]
+    high = held_ref[pl.ds(at + 1, tile, stride=2), :]
     square = jnp.sum(low * low + high * high, axis=1, keepdims=True)
     inv = lax.rsqrt(square + 1e-06)
     o_ref[:, :128] = (low * inv).astype(jnp.bfloat16)
     o_ref[:, 128:] = (high * inv).astype(jnp.bfloat16)
 
 
-def place_and_blend(me, slots, rows, held, weights, peers, run, first):
-    classes, width = weights.shape
+def place_and_blend(me, slots, rows, held, peers, run, first):
+    classes, width = peers * run, rows.shape[1]
     tile = math.gcd(classes, 1024)
     smem = pl.BlockSpec(memory_space=pltpu.SMEM)
     vmem = pl.BlockSpec(memory_space=pltpu.VMEM)
-    tiles = pl.BlockSpec((tile, width), lambda i: (i, 0))
-    refreshed, _ = pl.pallas_call(
+    return pl.pallas_call(
         functools.partial(blend_kernel, peers=peers, run=run, first=first),
         grid=(classes // tile,),
-        in_specs=[smem, smem, tiles, vmem, vmem],
-        out_specs=[tiles, vmem],
-        out_shape=[
-            jax.ShapeDtypeStruct((classes, width), jnp.bfloat16),
-            jax.ShapeDtypeStruct(held.shape, held.dtype),
-        ],
-        input_output_aliases={4: 1},
-        scratch_shapes=[pltpu.VMEM((2 * rows.shape[0] // peers, 128), jnp.float32)],
+        in_specs=[smem, smem, vmem, pl.BlockSpec(memory_space=pltpu.HBM)],
+        out_specs=pl.BlockSpec((tile, width), lambda i: (i, 0)),
+        out_shape=pltpu.HBM((classes, width), jnp.bfloat16),
+        scratch_shapes=[
+            pltpu.VMEM(held.shape, jnp.float32),
+            pltpu.VMEM((2 * rows.shape[0], 128), jnp.float32),
+            pltpu.SemaphoreType.DMA,
+        ],
         compiler_params=pltpu.CompilerParams(
-            dimension_semantics=("arbitrary",), vmem_limit_bytes=16 * MIB
+            dimension_semantics=("arbitrary",), vmem_limit_bytes=32 * MIB
         ),
         cost_estimate=pl.CostEstimate(
             flops=0, bytes_accessed=12 * classes * width, transcendentals=0
         ),
         name="place_and_blend",
-    )(me, slots, weights, rows, held)
-    return refreshed
+    )(me, slots, rows, held)
 
 
 def shards(embeddings, labels, class_weights, centroids, centroid_class):
@@ -345,15 +378,16 @@
 
     blocks = [swap(embeddings, "rep", k) for k in range(reps)]
 
-    runs = centroids.reshape(peers, run, width)
+    weights = in_hbm(class_weights)
+    runs = in_hbm(centroids.reshape(peers, run, width))
     cut = run * 5 // 8 // 16 * 16
 
-    def relay(first, size, tokens):
-        sent = fetch(runs, first, size, tokens)
-        return lax.all_to_all(sent, ALL, 0, 0, tiled=True).reshape(peers * size, width)
-
-    rows_a = relay(0, cut, blocks[1:])
-    emb, a, b, stats = forward(base, rep.reshape(1), blocks, labels, class_weights)
+    def relay(sent):
+        return lax.all_to_all(sent, ALL, 0, 0, tiled=True).reshape(-1, width)
+
+    sent = fetch(runs, 0, cut, blocks[1:])
+    rows_a = relay(sent)
+    emb, a, b, stats, wide = forward(base, rep.reshape(1), blocks, labels, weights, sent)
 
     wanted = centroid_class.reshape(reps, groups, run).astype(jnp.float32)
     sums = stats[:2].reshape(-1)
@@ -370,23 +404,25 @@
     ]
     every = jnp.stack(every).reshape(reps, -1)
     sums = jnp.sum(every[:, : 2 * batch], axis=0)
-    slots = every[:, 2 * batch :].reshape(-1).astype(jnp.int32)
+    slots = every[:, 2 * batch :].reshape(-1).astype(jnp.int32) * 2
     total, target = sums[:batch], sums[batch:]
     losses = SCALE + jnp.log(total) - target
     loss = lax.dynamic_slice_in_dim(losses, rep * rows_local, rows_local, 0)
 
-    rows_b = relay(cut, run - cut, [total])
-    weight_grad = weight_gradient(base, emb, labels, stats, total, class_weights)
-    held, token = place_rows(me, slots, rows_a, peers, run, 0)
-
-    grad = tie(a / total[:, None] - b, [weight_grad, token])
-    grad = grad.reshape(reps, groups, share, width)
+    rows_b = relay(fetch(runs, cut, run - cut, [total]))
+    weight_grad = weight_gradient(base, emb, labels, stats, total, weights)
+    done = in_hbm(weight_grad)
+    held, token = place_rows(me, slots, rows_a, in_hbm(wide), done, peers, run, 0)
+
+    grad = (a / total[:, None] - b).reshape(reps, groups, share, width)
     grad = sum(swap(pick(grad, "grp", j, 1), "grp", j) for j in range(groups))
+    grad = tie(grad, [done])
     own = sum(swap(pick(grad, "rep", k, 0), "rep", k) for k in range(reps))
+    own = tie(own, [token])
     shares = jnp.stack([swap(own, "grp", j) for j in range(groups)])
     embedding_gradient = shares[grp ^ jnp.arange(groups)].reshape(rows_local, width)
 
-    refreshed = place_and_blend(me, slots, rows_b, held, class_weights, peers, run, cut)
+    refreshed = place_and_blend(me, slots, rows_b, in_hbm(held), peers, run, cut)
     return (loss, embedding_gradient, weight_grad, refreshed)
 
 

time: 172 us -> 175 us (1.017)
  local copies, waits for them, and re-layouts: 31 us -> 10.3 us
  Pallas kernels: 46.2 us -> 65.5 us
  starting transfers between devices: 45.2 us -> 56.7 us
  waiting for transfers between devices: 46.2 us -> 38.5 us
    unnamed x50 -> x34, local copies, waits for them, and re-layouts: 28.9 us -> 8.14 us
    ppermute x30, starting transfers between devices: 37.3 us -> 49 us  [swap(): lax.ppermute(value, axis, [(i, i ^ k) for i in range(size)])]
    pallas_call x1, Pallas kernels: 10.3 us -> 19 us  [place_rows(): pl.pallas_call(functools.partial(place_kernel, peers=peers, run=run, firs...]
    ppermute x30, waiting for transfers between devices: 46.2 us -> 38.5 us  [swap(): lax.ppermute(value, axis, [(i, i ^ k) for i in range(size)])]
    pallas_call x1, Pallas kernels: 12.9 us -> 15.8 us  [place_and_blend(): pl.pallas_call(functools.partial(blend_kernel, peers=peers, run=run, firs...]
    pallas_call x2, Pallas kernels: 1.88 us -> 4.66 us  [fetch(): pl.pallas_call(functools.partial(fetch_kernel, first=first), in_specs=[hb...]
    pallas_call x1, Pallas kernels: 11.6 us -> 14.2 us  [forward(): pl.pallas_call(functools.partial(forward_kernel, classes=classes, reps=re...]
    pallas_call x1, Pallas kernels: 9.49 us -> 11.8 us  [weight_gradient(): pl.pallas_call(weight_kernel, grid=(classes // tile,), in_specs=[pl.Block...]
  transfers between devices with their start and end apart: 32 -> 32, of which waited for: 11 -> 12; matrix products, arithmetic and copies ran while one was open for 1% -> 1% of each run, Pallas kernels for 26% -> 36%
where the time goes in v7:
time: 175 us; the launch traced here: 173 us
  Pallas kernels  65.5 us (37%)
  starting transfers between devices  56.7 us (32%)
  waiting for transfers between devices  38.5 us (22%)
  local copies, waits for them, and re-layouts  10.3 us (6%)
    ppermute x30, starting transfers between devices, swap(): lax.ppermute(value, axis, [(i, i ^ k) for i in range(size)])  49 us
    ppermute x30, waiting for transfers between devices, swap(): lax.ppermute(value, axis, [(i, i ^ k) for i in range(size)])  38.5 us
    pallas_call x1, Pallas kernels, place_rows(): pl.pallas_call(functools.partial(place_kernel, peers=peers, run=run, firs...  19 us
    pallas_call x1, Pallas kernels, place_and_blend(): pl.pallas_call(functools.partial(blend_kernel, peers=peers, run=run, firs...  15.8 us
    pallas_call x1, Pallas kernels, forward(): pl.pallas_call(functools.partial(forward_kernel, classes=classes, reps=re...  14.2 us
    pallas_call x1, Pallas kernels, weight_gradient(): pl.pallas_call(weight_kernel, grid=(classes // tile,), in_specs=[pl.Block...  11.8 us
    unnamed x34, local copies, waits for them, and re-layouts  8.14 us
    all_to_all x2, starting transfers between devices, relay(): return lax.all_to_all(sent, ALL, 0, 0, tiled=True).reshape(-1, width)  7.65 us
  transfers between devices with their start and end apart: 32, of which 12 were waited for; matrix products, arithmetic and copies ran while one was open for 1% of the time, Pallas kernels for 36%

profile of v7, /device:TPU:0, one launch (start us, length us, event | category | flops | bytes accessed | tf_op | source)
XLA Modules:
  0.0 173.4 jit_solution(12173074459221149575)
XLA Ops:
  0.6 0.5 collective-permute-start
  1.1 2.7 %collective-permute-start.1 = (bf16[64,256]{1,0:T(8,128)(2,1)}, bf16[64,256]{1,0:T(8,128)(2,1)S(1)}, u32[]{:S(2)}, u32[]{:S(2)}) collective-permute-start(bf16[64,256]{1,0:T(8,128)(2,1)} %refs_0_.1), channel_id=1, source_target_pairs={{0,2},{1,3},{2,0},{3,1},{4,6},{5,7},{6,4},{7,5},{8,10},{9,11},{10,... | collective-permute-start | bytes 98312 | tf_op jit(solution)/shard_map/ppermute | solution.py:374
  3.8 0.1 collective-permute-start.2
  3.9 2.8 %collective-permute-start.3 = (bf16[64,256]{1,0:T(8,128)(2,1)}, bf16[64,256]{1,0:T(8,128)(2,1)S(1)}, u32[]{:S(2)}, u32[]{:S(2)}) collective-permute-start(bf16[64,256]{1,0:T(8,128)(2,1)} %refs_0_.1), channel_id=1, source_target_pairs={{0,4},{1,5},{2,6},{3,7},{4,0},{5,1},{6,2},{7,3},{8,12},{9,13},{10,... | collective-permute-start | bytes 98312 | tf_op jit(solution)/shard_map/ppermute | solution.py:374
  6.6 3.6 %collective-permute-start.5 = (bf16[64,256]{1,0:T(8,128)(2,1)}, bf16[64,256]{1,0:T(8,128)(2,1)S(1)}, u32[]{:S(2)}, u32[]{:S(2)}) collective-permute-start(bf16[64,256]{1,0:T(8,128)(2,1)} %refs_0_.1), channel_id=1, source_target_pairs={{0,6},{1,7},{2,4},{3,5},{4,2},{5,3},{6,0},{7,1},{8,14},{9,15},{10,... | collective-permute-start | bytes 98312 | tf_op jit(solution)/shard_map/ppermute | solution.py:374
  10.2 0.1 collective-permute-start.6
  10.3 0.8 collective-permute-done.4.refs_4_.refs_5_
  11.2 2.0 %collective-permute-done.5.refs_5_.refs_6_ = bf16[64,256]{1,0:T(8,128)(2,1)S(1)} collective-permute-done((bf16[64,256]{1,0:T(8,128)(2,1)}, bf16[64,256]{1,0:T(8,128)(2,1)S(1)}, u32[]{:S(2)}, u32[]{:S(2)}) %collective-permute-start.5) | collective-permute-done | bytes 32800 | tf_op jit(solution)/shard_map/ppermute | solution.py:374
  13.2 2.4 %collective-permute-done.6.refs_6_.refs_7_ = bf16[64,256]{1,0:T(8,128)(2,1)S(1)} collective-permute-done((bf16[64,256]{1,0:T(8,128)(2,1)}, bf16[64,256]{1,0:T(8,128)(2,1)S(1)}, u32[]{:S(2)}, u32[]{:S(2)}) %collective-permute-start.6) | collective-permute-done | bytes 32800 | tf_op jit(solution)/shard_map/ppermute | solution.py:374
  15.6 3.2 %fetch.2._ = bf16[32,160,256]{2,1,0:T(8,128)(2,1)} custom-call(bf16[32,256,256]{2,1,0:T(8,128)(2,1)} %bitcast.114, bf16[64,256]{1,0:T(8,128)(2,1)S(1)} %collective-permute-done.refs_0_.refs_1_, bf16[64,256]{1,0:T(8,128)(2,1)S(1)} %collective-permute-done.1.refs_1_.refs_2_, bf16[64,256]{1,0:T(8,128)(2,1)S(1)} %collective-permute-done.2.refs_2_.refs_3_, ...), custom_call_target="tpu_custom_call" | custom-call | flops 1 | bytes 1 | tf_op jit(solution)/shard_map/fetch/pallas_call | solution.py:213
  18.8 0.6 copy-done.2
  19.4 0.6 copy-done.4
  20.1 0.6 copy-done.6
  20.7 3.1 %all-to-all-start = ((bf16[32,160,256]{2,1,0:T(8,128)(2,1)}), bf16[32,160,256]{2,1,0:T(8,128)(2,1)S(1)}, u32[]{:S(2)}, u32[]{:S(2)}) async-start(bf16[32,160,256]{2,1,0:T(8,128)(2,1)} %fetch.2._), calls=%async_computation | async-start | bytes 5242880 | tf_op jit(solution)/shard_map/all_to_all | solution.py:386
  23.8 0.1 copy.18.lab_ref
  24.1 0.7 copy-done.3
  24.8 0.8 copy-done.5
  25.6 0.8 copy-done.7
  26.4 0.8 copy-done.11
  27.1 14.2 %forward_sums.1 = (bf16[512,256]{1,0:T(8,128)(2,1)S(1)}, f32[512,256]{1,0:T(8,128)S(1)}, f32[512,256]{1,0:T(8,128)S(1)}, f32[8,512]{1,0:T(8,128)S(1)}, f32[16384,128]{1,0:T(8,128)}) custom-call(s32[1]{0:T(128)S(6)} %mul.18.base_ref, s32[1]{0:T(128)} %bitcast.1.rep_ref, s32[512,1]{1,0:T(8,128)S(1)} %copy.18.lab_ref, bf16[8192,256]{1,0:T(8,128)(2,1)} %w_ref.3, ...), custom_call_target="tpu_custom_call" | custom-call | flops 12884901888 | bytes 4194304 | tf_op jit(solution)/shard_map/forward_sums/pallas_call | solution.py:107
  41.3 0.8 copy-done.1
  42.1 0.7 copy-done.12
  42.8 0.6 copy-done.9
  43.4 2.7 %collective-permute-start.9 = (f32[24,128]{1,0:T(8,128)S(1)}, f32[24,128]{1,0:T(8,128)S(1)}, u32[]{:S(2)}, u32[]{:S(2)}) collective-permute-start(f32[24,128]{1,0:T(8,128)S(1)} %get-tuple-element.52), channel_id=1, source_target_pairs={{0,24},{8,16},{16,8},{24,0},{1,25},{9,17},{17,9},{25,1},{2,26},{10... | collective-permute-start | bytes 36872 | tf_op jit(solution)/shard_map/ppermute | solution.py:374
  46.1 0.6 collective-permute-start.8
  46.7 0.3 collective-permute-start.7
  46.9 1.2 collective-permute-done.9
  48.2 1.7 collective-permute-done.8
  49.8 0.7 collective-permute-done.7
  50.6 0.1 collective-permute-start.10
  50.7 1.5 collective-permute-start.11
  52.3 0.3 collective-permute-start.12
  52.6 2.4 %collective-permute-start.13 = (f32[16,128]{1,0:T(8,128)S(1)}, f32[16,128]{1,0:T(8,128)S(1)}, u32[]{:S(2)}, u32[]{:S(2)}) collective-permute-start(f32[16,128]{1,0:T(8,128)S(1)} %get-tuple-element.45), channel_id=1, source_target_pairs={{0,4},{1,5},{2,6},{3,7},{4,0},{5,1},{6,2},{7,3},{8,12},{9,13},{10,... | collective-permute-start | bytes 24584 | tf_op jit(solution)/shard_map/ppermute | solution.py:374
  55.0 0.2 collective-permute-start.14
  55.2 3.3 %collective-permute-start.15 = (f32[16,128]{1,0:T(8,128)S(1)}, f32[16,128]{1,0:T(8,128)S(1)}, u32[]{:S(2)}, u32[]{:S(2)}) collective-permute-start(f32[16,128]{1,0:T(8,128)S(1)} %get-tuple-element.47), channel_id=1, source_target_pairs={{0,6},{1,7},{2,4},{3,5},{4,2},{5,3},{6,0},{7,1},{8,14},{9,15},{10,... | collective-permute-start | bytes 24584 | tf_op jit(solution)/shard_map/ppermute | solution.py:374
  58.5 8.8 %collective-permute-done.11 = f32[16,128]{1,0:T(8,128)S(1)} collective-permute-done((f32[16,128]{1,0:T(8,128)S(1)}, f32[16,128]{1,0:T(8,128)S(1)}, u32[]{:S(2)}, u32[]{:S(2)}) %collective-permute-start.11) | collective-permute-done | bytes 8224 | tf_op jit(solution)/shard_map/ppermute | solution.py:374
  67.3 2.3 %collective-permute-start.16 = (f32[16,128]{1,0:T(8,128)S(1)}, f32[16,128]{1,0:T(8,128)S(1)}, u32[]{:S(2)}, u32[]{:S(2)}) collective-permute-start(f32[16,128]{1,0:T(8,128)S(1)} %get-tuple-element.42), channel_id=1, source_target_pairs={{0,7},{1,6},{2,5},{3,4},{4,3},{5,2},{6,1},{7,0},{8,15},{9,14},{10,... | collective-permute-start | bytes 24584 | tf_op jit(solution)/shard_map/ppermute | solution.py:374
  69.6 15.2 %collective-permute-done.13 = f32[16,128]{1,0:T(8,128)S(1)} collective-permute-done((f32[16,128]{1,0:T(8,128)S(1)}, f32[16,128]{1,0:T(8,128)S(1)}, u32[]{:S(2)}, u32[]{:S(2)}) %collective-permute-start.13) | collective-permute-done | bytes 8224 | tf_op jit(solution)/shard_map/ppermute | solution.py:374
  84.9 0.1 stack.68
  85.0 1.4 fetch.3
  86.5 1.1 copy-done
  87.6 4.6 %all-to-all-start.1 = ((bf16[32,96,256]{2,1,0:T(8,128)(2,1)}), bf16[32,96,256]{2,1,0:T(8,128)(2,1)}, u32[]{:S(2)}, u32[]{:S(2)}) async-start(bf16[32,96,256]{2,1,0:T(8,128)(2,1)} %copy-done), calls=%async_computation.1 | async-start | bytes 3145728 | tf_op jit(solution)/shard_map/all_to_all | solution.py:386
  92.2 1.2 divide_subtract_fusion
  93.4 2.7 %collective-permute-start.19 = (f32[8,16,256]{2,1,0:T(8,128)S(1)}, f32[8,16,256]{2,1,0:T(8,128)S(1)}, u32[]{:S(2)}, u32[]{:S(2)}) collective-permute-start(f32[8,16,256]{2,1,0:T(8,128)S(1)} %get-tuple-element.20), channel_id=1, source_target_pairs={{0,24},{8,16},{16,8},{24,0},{1,25},{9,17},{17,9},{25,1},{2,26},{10... | collective-permute-start | bytes 393224 | tf_op jit(solution)/shard_map/ppermute | solution.py:374
  96.1 0.6 collective-permute-start.18
  96.6 0.3 collective-permute-start.17
  97.0 11.8 %weight_gradient.1.refs_0_._ = f32[8192,256]{1,0:T(8,128)} custom-call(s32[1]{0:T(128)S(6)} %mul.18.base_ref, bf16[512,256]{1,0:T(8,128)(2,1)S(1)} %copy-done.13, s32[1,512]{1,0:T(1,128)S(1)} %bitcast.113, f32[8,512]{1,0:T(8,128)S(1)} %copy-done.10, f32[1,512]{1,0:T(1,128)S(1)} %bitcast.111, bf16[8192,256]{1,0:T(8,128)(2,1)} %w_ref.3), custom_call_target="tpu_custom_call" | custom-call | flops 12884901888 | bytes 12582912 | tf_op jit(solution)/shard_map/weight_gradient/pallas_call | solution.py:173
  108.8 1.3 collective-permute-done.19
  110.1 3.1 %collective-permute-done.18 = f32[8,16,256]{2,1,0:T(8,128)S(1)} collective-permute-done((f32[8,16,256]{2,1,0:T(8,128)S(1)}, f32[8,16,256]{2,1,0:T(8,128)S(1)}, u32[]{:S(2)}, u32[]{:S(2)}) %collective-permute-start.18) | collective-permute-done | bytes 131104 | tf_op jit(solution)/shard_map/ppermute | solution.py:374
  113.2 0.4 collective-permute-done.17
  113.7 4.7 %collective-permute-start.26 = (f32[16,256]{1,0:T(8,128)S(1)}, f32[16,256]{1,0:T(8,128)S(1)}, u32[]{:S(2)}, u32[]{:S(2)}) collective-permute-start(f32[16,256]{1,0:T(8,128)S(1)} %get-tuple-element.22), channel_id=1, source_target_pairs={{0,7},{1,6},{2,5},{3,4},{4,3},{5,2},{6,1},{7,0},{8,15},{9,14},{10,... | collective-permute-start | bytes 49160 | tf_op jit(solution)/shard_map/ppermute | solution.py:374
  118.4 0.7 collective-permute-start.25
  119.1 2.6 %collective-permute-start.23 = (f32[16,256]{1,0:T(8,128)S(1)}, f32[16,256]{1,0:T(8,128)S(1)}, u32[]{:S(2)}, u32[]{:S(2)}) collective-permute-start(f32[16,256]{1,0:T(8,128)S(1)} %get-tuple-element.25), channel_id=1, source_target_pairs={{0,4},{1,5},{2,6},{3,7},{4,0},{5,1},{6,2},{7,3},{8,12},{9,13},{10,... | collective-permute-start | bytes 49160 | tf_op jit(solution)/shard_map/ppermute | solution.py:374
  121.8 0.9 collective-permute-start.22
  122.7 8.8 %collective-permute-start.21 = (f32[16,256]{1,0:T(8,128)S(1)}, f32[16,256]{1,0:T(8,128)S(1)}, u32[]{:S(2)}, u32[]{:S(2)}) collective-permute-start(f32[16,256]{1,0:T(8,128)S(1)} %get-tuple-element.27), channel_id=1, source_target_pairs={{0,2},{1,3},{2,0},{3,1},{4,6},{5,7},{6,4},{7,5},{8,10},{9,11},{10,... | collective-permute-start | bytes 49160 | tf_op jit(solution)/shard_map/ppermute | solution.py:374
  131.5 0.9 collective-permute-start.20
  132.4 0.7 collective-permute-done.21
  133.2 19.0 %place_rows.1 = (f32[16384,128]{1,0:T(8,128)}, f32[8,128]{1,0:T(8,128)S(1)}) custom-call(s32[1]{0:T(128)} %bitcast.me_ref, s32[8192]{0:T(1024)S(1)} %bitcast.108, bf16[5120,256]{1,0:T(8,128)(2,1)S(1)} %bitcast.107, f32[16384,128]{1,0:T(8,128)} %get-tuple-element.15.in_ref, f32[8192,256]{1,0:T(8,128)} %weight_gradient.1.refs_0_._), custom_call_target="tpu_custom_call" | custom-call | bytes 20971520 | tf_op jit(solution)/shard_map/place_rows/pallas_call | solution.py:292
  152.2 2.5 %collective-permute-start.29 = (f32[16,256]{1,0:T(8,128)S(1)}, f32[16,256]{1,0:T(8,128)S(1)}, u32[]{:S(2)}, u32[]{:S(2)}) collective-permute-start(f32[16,256]{1,0:T(8,128)S(1)} %tie.3), channel_id=1, source_target_pairs={{0,24},{8,16},{16,8},{24,0},{1,25},{9,17},{17,9},{25,1},{2,26},{10... | collective-permute-start | bytes 49160 | tf_op jit(solution)/shard_map/ppermute | solution.py:374
  154.7 0.6 collective-permute-start.28
  155.3 0.5 collective-permute-start.27
  155.7 0.6 dynamic_slice.91
  156.3 15.8 %place_and_blend.1 = bf16[8192,256]{1,0:T(8,128)(2,1)} custom-call(s32[1]{0:T(128)} %bitcast.me_ref, s32[8192]{0:T(1024)S(1)} %bitcast.109, bf16[3072,256]{1,0:T(8,128)(2,1)} %bitcast.54.row_ref, f32[16384,128]{1,0:T(8,128)} %get-tuple-element.17.in_ref), custom_call_target="tpu_custom_call" | custom-call | bytes 25165824 | tf_op jit(solution)/shard_map/place_and_blend/pallas_call | solution.py:339
  172.2 1.2 gather_fusion
  (66 shorter events, 0.5 us)
Async XLA Ops:
  0.6 6.0 %collective-permute-start = (bf16[64,256]{1,0:T(8,128)(2,1)}, bf16[64,256]{1,0:T(8,128)(2,1)S(1)}, u32[]{:S(2)}, u32[]{:S(2)}) collective-permute-start(bf16[64,256]{1,0:T(8,128)(2,1)} %refs_0_.1), channel_id=1, source_target_pairs={{0,1},{1,0},{2,3},{3,2},{4,5},{5,4},{6,7},{7,6},{8,9},{9,8},{10,11... | collective-permute-start | bytes 98312 | tf_op jit(solution)/shard_map/ppermute | solution.py:374
  1.1 9.1 %collective-permute-start.1 = (bf16[64,256]{1,0:T(8,128)(2,1)}, bf16[64,256]{1,0:T(8,128)(2,1)S(1)}, u32[]{:S(2)}, u32[]{:S(2)}) collective-permute-start(bf16[64,256]{1,0:T(8,128)(2,1)} %refs_0_.1), channel_id=1, source_target_pairs={{0,2},{1,3},{2,0},{3,1},{4,6},{5,7},{6,4},{7,5},{8,10},{9,11},{10,... | collective-permute-start | bytes 98312 | tf_op jit(solution)/shard_map/ppermute | solution.py:374
  3.8 6.5 %collective-permute-start.2 = (bf16[64,256]{1,0:T(8,128)(2,1)}, bf16[64,256]{1,0:T(8,128)(2,1)S(1)}, u32[]{:S(2)}, u32[]{:S(2)}) collective-permute-start(bf16[64,256]{1,0:T(8,128)(2,1)} %refs_0_.1), channel_id=1, source_target_pairs={{0,3},{1,2},{2,1},{3,0},{4,7},{5,6},{6,5},{7,4},{8,11},{9,10},{10,... | collective-permute-start | bytes 98312 | tf_op jit(solution)/shard_map/ppermute | solution.py:374
  3.9 6.5 %collective-permute-start.3 = (bf16[64,256]{1,0:T(8,128)(2,1)}, bf16[64,256]{1,0:T(8,128)(2,1)S(1)}, u32[]{:S(2)}, u32[]{:S(2)}) collective-permute-start(bf16[64,256]{1,0:T(8,128)(2,1)} %refs_0_.1), channel_id=1, source_target_pairs={{0,4},{1,5},{2,6},{3,7},{4,0},{5,1},{6,2},{7,3},{8,12},{9,13},{10,... | collective-permute-start | bytes 98312 | tf_op jit(solution)/shard_map/ppermute | solution.py:374
  6.6 4.6 %collective-permute-start.4 = (bf16[64,256]{1,0:T(8,128)(2,1)}, bf16[64,256]{1,0:T(8,128)(2,1)S(1)}, u32[]{:S(2)}, u32[]{:S(2)}) collective-permute-start(bf16[64,256]{1,0:T(8,128)(2,1)} %refs_0_.1), channel_id=1, source_target_pairs={{0,5},{1,4},{2,7},{3,6},{4,1},{5,0},{6,3},{7,2},{8,13},{9,12},{10,... | collective-permute-start | bytes 98312 | tf_op jit(solution)/shard_map/ppermute | solution.py:374
  6.6 6.6 %collective-permute-start.5 = (bf16[64,256]{1,0:T(8,128)(2,1)}, bf16[64,256]{1,0:T(8,128)(2,1)S(1)}, u32[]{:S(2)}, u32[]{:S(2)}) collective-permute-start(bf16[64,256]{1,0:T(8,128)(2,1)} %refs_0_.1), channel_id=1, source_target_pairs={{0,6},{1,7},{2,4},{3,5},{4,2},{5,3},{6,0},{7,1},{8,14},{9,15},{10,... | collective-permute-start | bytes 98312 | tf_op jit(solution)/shard_map/ppermute | solution.py:374
  10.2 5.4 %collective-permute-start.6 = (bf16[64,256]{1,0:T(8,128)(2,1)}, bf16[64,256]{1,0:T(8,128)(2,1)S(1)}, u32[]{:S(2)}, u32[]{:S(2)}) collective-permute-start(bf16[64,256]{1,0:T(8,128)(2,1)} %refs_0_.1), channel_id=1, source_target_pairs={{0,7},{1,6},{2,5},{3,4},{4,3},{5,2},{6,1},{7,0},{8,15},{9,14},{10,... | collective-permute-start | bytes 98312 | tf_op jit(solution)/shard_map/ppermute | solution.py:374
  18.8 0.6 copy-start.2
  19.4 0.6 copy-start.4
  20.1 0.6 copy-start.6
  20.7 3.1 %copy-start.8 = (s32[512]{0:T(512)S(1)}, s32[512]{0:T(512)}, u32[]{:S(2)}) copy-start(s32[512]{0:T(512)} %param.6) | copy-start | bytes 6148
  20.7 3.3 %copy-start.14 = (s32[8192]{0:T(1024)S(1)}, s32[8192]{0:T(1024)}, u32[]{:S(2)}) copy-start(s32[8192]{0:T(1024)} %param.9) | copy-start | bytes 98308
  20.7 66.9 %all-to-all-start = ((bf16[32,160,256]{2,1,0:T(8,128)(2,1)}), bf16[32,160,256]{2,1,0:T(8,128)(2,1)S(1)}, u32[]{:S(2)}, u32[]{:S(2)}) async-start(bf16[32,160,256]{2,1,0:T(8,128)(2,1)} %fetch.2._), calls=%async_computation | async-start | bytes 5242880 | tf_op jit(solution)/shard_map/all_to_all | solution.py:386
  24.1 0.8 copy-start.3
  24.8 0.8 copy-start.5
  25.6 0.8 copy-start.7
  26.4 0.8 copy-start.11
  41.3 0.8 copy-start.1
  42.1 0.7 copy-start.12
  42.8 0.6 copy-start.9
  43.4 4.7 %collective-permute-start.9 = (f32[24,128]{1,0:T(8,128)S(1)}, f32[24,128]{1,0:T(8,128)S(1)}, u32[]{:S(2)}, u32[]{:S(2)}) collective-permute-start(f32[24,128]{1,0:T(8,128)S(1)} %get-tuple-element.52), channel_id=1, source_target_pairs={{0,24},{8,16},{16,8},{24,0},{1,25},{9,17},{17,9},{25,1},{2,26},{10... | collective-permute-start | bytes 36872 | tf_op jit(solution)/shard_map/ppermute | solution.py:374
  46.1 3.7 %collective-permute-start.8 = (f32[24,128]{1,0:T(8,128)S(1)}, f32[24,128]{1,0:T(8,128)S(1)}, u32[]{:S(2)}, u32[]{:S(2)}) collective-permute-start(f32[24,128]{1,0:T(8,128)S(1)} %get-tuple-element.51), channel_id=1, source_target_pairs={{0,16},{8,24},{16,0},{24,8},{1,17},{9,25},{17,1},{25,9},{2,18},{10... | collective-permute-start | bytes 36872 | tf_op jit(solution)/shard_map/ppermute | solution.py:374
  46.7 3.8 %collective-permute-start.7 = (f32[24,128]{1,0:T(8,128)S(1)}, f32[24,128]{1,0:T(8,128)S(1)}, u32[]{:S(2)}, u32[]{:S(2)}) collective-permute-start(f32[24,128]{1,0:T(8,128)S(1)} %get-tuple-element.50), channel_id=1, source_target_pairs={{0,8},{8,0},{16,24},{24,16},{1,9},{9,1},{17,25},{25,17},{2,10},{10... | collective-permute-start | bytes 36872 | tf_op jit(solution)/shard_map/ppermute | solution.py:374
  50.6 4.5 %collective-permute-start.10 = (f32[16,128]{1,0:T(8,128)S(1)}, f32[16,128]{1,0:T(8,128)S(1)}, u32[]{:S(2)}, u32[]{:S(2)}) collective-permute-start(f32[16,128]{1,0:T(8,128)S(1)} %get-tuple-element.48), channel_id=1, source_target_pairs={{0,1},{1,0},{2,3},{3,2},{4,5},{5,4},{6,7},{7,6},{8,9},{9,8},{10,11... | collective-permute-start | bytes 24584 | tf_op jit(solution)/shard_map/ppermute | solution.py:374
  50.7 16.6 %collective-permute-start.11 = (f32[16,128]{1,0:T(8,128)S(1)}, f32[16,128]{1,0:T(8,128)S(1)}, u32[]{:S(2)}, u32[]{:S(2)}) collective-permute-start(f32[16,128]{1,0:T(8,128)S(1)} %get-tuple-element.43), channel_id=1, source_target_pairs={{0,2},{1,3},{2,0},{3,1},{4,6},{5,7},{6,4},{7,5},{8,10},{9,11},{10,... | collective-permute-start | bytes 24584 | tf_op jit(solution)/shard_map/ppermute | solution.py:374
  52.3 17.4 %collective-permute-start.12 = (f32[16,128]{1,0:T(8,128)S(1)}, f32[16,128]{1,0:T(8,128)S(1)}, u32[]{:S(2)}, u32[]{:S(2)}) collective-permute-start(f32[16,128]{1,0:T(8,128)S(1)} %get-tuple-element.44), channel_id=1, source_target_pairs={{0,3},{1,2},{2,1},{3,0},{4,7},{5,6},{6,5},{7,4},{8,11},{9,10},{10,... | collective-permute-start | bytes 24584 | tf_op jit(solution)/shard_map/ppermute | solution.py:374
  52.6 32.3 %collective-permute-start.13 = (f32[16,128]{1,0:T(8,128)S(1)}, f32[16,128]{1,0:T(8,128)S(1)}, u32[]{:S(2)}, u32[]{:S(2)}) collective-permute-start(f32[16,128]{1,0:T(8,128)S(1)} %get-tuple-element.45), channel_id=1, source_target_pairs={{0,4},{1,5},{2,6},{3,7},{4,0},{5,1},{6,2},{7,3},{8,12},{9,13},{10,... | collective-permute-start | bytes 24584 | tf_op jit(solution)/shard_map/ppermute | solution.py:374
  55.0 29.9 %collective-permute-start.14 = (f32[16,128]{1,0:T(8,128)S(1)}, f32[16,128]{1,0:T(8,128)S(1)}, u32[]{:S(2)}, u32[]{:S(2)}) collective-permute-start(f32[16,128]{1,0:T(8,128)S(1)} %get-tuple-element.46), channel_id=1, source_target_pairs={{0,5},{1,4},{2,7},{3,6},{4,1},{5,0},{6,3},{7,2},{8,13},{9,12},{10,... | collective-permute-start | bytes 24584 | tf_op jit(solution)/shard_map/ppermute | solution.py:374
  55.2 29.7 %collective-permute-start.15 = (f32[16,128]{1,0:T(8,128)S(1)}, f32[16,128]{1,0:T(8,128)S(1)}, u32[]{:S(2)}, u32[]{:S(2)}) collective-permute-start(f32[16,128]{1,0:T(8,128)S(1)} %get-tuple-element.47), channel_id=1, source_target_pairs={{0,6},{1,7},{2,4},{3,5},{4,2},{5,3},{6,0},{7,1},{8,14},{9,15},{10,... | collective-permute-start | bytes 24584 | tf_op jit(solution)/shard_map/ppermute | solution.py:374
  67.3 17.6 %collective-permute-start.16 = (f32[16,128]{1,0:T(8,128)S(1)}, f32[16,128]{1,0:T(8,128)S(1)}, u32[]{:S(2)}, u32[]{:S(2)}) collective-permute-start(f32[16,128]{1,0:T(8,128)S(1)} %get-tuple-element.42), channel_id=1, source_target_pairs={{0,7},{1,6},{2,5},{3,4},{4,3},{5,2},{6,1},{7,0},{8,15},{9,14},{10,... | collective-permute-start | bytes 24584 | tf_op jit(solution)/shard_map/ppermute | solution.py:374
  86.4 1.1 copy-start
  87.6 9.4 %copy-start.10 = (f32[8,512]{1,0:T(8,128)S(1)}, f32[8,512]{1,0:T(8,128)}, u32[]{:S(2)}) copy-start(f32[8,512]{1,0:T(8,128)} %copy-done.9) | copy-start | bytes 49156
  87.6 9.4 %copy-start.13 = (bf16[512,256]{1,0:T(8,128)(2,1)S(1)}, bf16[512,256]{1,0:T(8,128)(2,1)}, u32[]{:S(2)}) copy-start(bf16[512,256]{1,0:T(8,128)(2,1)} %copy-done.12) | copy-start | bytes 786436
  87.6 68.7 %all-to-all-start.1 = ((bf16[32,96,256]{2,1,0:T(8,128)(2,1)}), bf16[32,96,256]{2,1,0:T(8,128)(2,1)}, u32[]{:S(2)}, u32[]{:S(2)}) async-start(bf16[32,96,256]{2,1,0:T(8,128)(2,1)} %copy-done), calls=%async_computation.1 | async-start | bytes 3145728 | tf_op jit(solution)/shard_map/all_to_all | solution.py:386
  93.4 16.7 %collective-permute-start.19 = (f32[8,16,256]{2,1,0:T(8,128)S(1)}, f32[8,16,256]{2,1,0:T(8,128)S(1)}, u32[]{:S(2)}, u32[]{:S(2)}) collective-permute-start(f32[8,16,256]{2,1,0:T(8,128)S(1)} %get-tuple-element.20), channel_id=1, source_target_pairs={{0,24},{8,16},{16,8},{24,0},{1,25},{9,17},{17,9},{25,1},{2,26},{10... | collective-permute-start | bytes 393224 | tf_op jit(solution)/shard_map/ppermute | solution.py:374
  96.1 17.1 %collective-permute-start.18 = (f32[8,16,256]{2,1,0:T(8,128)S(1)}, f32[8,16,256]{2,1,0:T(8,128)S(1)}, u32[]{:S(2)}, u32[]{:S(2)}) collective-permute-start(f32[8,16,256]{2,1,0:T(8,128)S(1)} %get-tuple-element.19), channel_id=1, source_target_pairs={{0,16},{8,24},{16,0},{24,8},{1,17},{9,25},{17,1},{25,9},{2,18},{10... | collective-permute-start | bytes 393224 | tf_op jit(solution)/shard_map/ppermute | solution.py:374
  96.6 17.0 %collective-permute-start.17 = (f32[8,16,256]{2,1,0:T(8,128)S(1)}, f32[8,16,256]{2,1,0:T(8,128)S(1)}, u32[]{:S(2)}, u32[]{:S(2)}) collective-permute-start(f32[8,16,256]{2,1,0:T(8,128)S(1)} %get-tuple-element.18), channel_id=1, source_target_pairs={{0,8},{8,0},{16,24},{24,16},{1,9},{9,1},{17,25},{25,17},{2,10},{10... | collective-permute-start | bytes 393224 | tf_op jit(solution)/shard_map/ppermute | solution.py:374
  113.7 9.0 %collective-permute-start.26 = (f32[16,256]{1,0:T(8,128)S(1)}, f32[16,256]{1,0:T(8,128)S(1)}, u32[]{:S(2)}, u32[]{:S(2)}) collective-permute-start(f32[16,256]{1,0:T(8,128)S(1)} %get-tuple-element.22), channel_id=1, source_target_pairs={{0,7},{1,6},{2,5},{3,4},{4,3},{5,2},{6,1},{7,0},{8,15},{9,14},{10,... | collective-permute-start | bytes 49160 | tf_op jit(solution)/shard_map/ppermute | solution.py:374
  118.4 13.0 %collective-permute-start.25 = (f32[16,256]{1,0:T(8,128)S(1)}, f32[16,256]{1,0:T(8,128)S(1)}, u32[]{:S(2)}, u32[]{:S(2)}) collective-permute-start(f32[16,256]{1,0:T(8,128)S(1)} %get-tuple-element.23), channel_id=1, source_target_pairs={{0,6},{1,7},{2,4},{3,5},{4,2},{5,3},{6,0},{7,1},{8,14},{9,15},{10,... | collective-permute-start | bytes 49160 | tf_op jit(solution)/shard_map/ppermute | solution.py:374
  119.1 13.2 %collective-permute-start.24 = (f32[16,256]{1,0:T(8,128)S(1)}, f32[16,256]{1,0:T(8,128)S(1)}, u32[]{:S(2)}, u32[]{:S(2)}) collective-permute-start(f32[16,256]{1,0:T(8,128)S(1)} %get-tuple-element.24), channel_id=1, source_target_pairs={{0,5},{1,4},{2,7},{3,6},{4,1},{5,0},{6,3},{7,2},{8,13},{9,12},{10,... | collective-permute-start | bytes 49160 | tf_op jit(solution)/shard_map/ppermute | solution.py:374
  119.1 13.3 %collective-permute-start.23 = (f32[16,256]{1,0:T(8,128)S(1)}, f32[16,256]{1,0:T(8,128)S(1)}, u32[]{:S(2)}, u32[]{:S(2)}) collective-permute-start(f32[16,256]{1,0:T(8,128)S(1)} %get-tuple-element.25), channel_id=1, source_target_pairs={{0,4},{1,5},{2,6},{3,7},{4,0},{5,1},{6,2},{7,3},{8,12},{9,13},{10,... | collective-permute-start | bytes 49160 | tf_op jit(solution)/shard_map/ppermute | solution.py:374
  121.8 10.7 %collective-permute-start.22 = (f32[16,256]{1,0:T(8,128)S(1)}, f32[16,256]{1,0:T(8,128)S(1)}, u32[]{:S(2)}, u32[]{:S(2)}) collective-permute-start(f32[16,256]{1,0:T(8,128)S(1)} %get-tuple-element.26), channel_id=1, source_target_pairs={{0,3},{1,2},{2,1},{3,0},{4,7},{5,6},{6,5},{7,4},{8,11},{9,10},{10,... | collective-permute-start | bytes 49160 | tf_op jit(solution)/shard_map/ppermute | solution.py:374
  122.7 10.5 %collective-permute-start.21 = (f32[16,256]{1,0:T(8,128)S(1)}, f32[16,256]{1,0:T(8,128)S(1)}, u32[]{:S(2)}, u32[]{:S(2)}) collective-permute-start(f32[16,256]{1,0:T(8,128)S(1)} %get-tuple-element.27), channel_id=1, source_target_pairs={{0,2},{1,3},{2,0},{3,1},{4,6},{5,7},{6,4},{7,5},{8,10},{9,11},{10,... | collective-permute-start | bytes 49160 | tf_op jit(solution)/shard_map/ppermute | solution.py:374
  131.5 1.7 collective-permute-start.20
  152.2 20.0 %collective-permute-start.29 = (f32[16,256]{1,0:T(8,128)S(1)}, f32[16,256]{1,0:T(8,128)S(1)}, u32[]{:S(2)}, u32[]{:S(2)}) collective-permute-start(f32[16,256]{1,0:T(8,128)S(1)} %tie.3), channel_id=1, source_target_pairs={{0,24},{8,16},{16,8},{24,0},{1,25},{9,17},{17,9},{25,1},{2,26},{10... | collective-permute-start | bytes 49160 | tf_op jit(solution)/shard_map/ppermute | solution.py:374
  154.7 17.5 %collective-permute-start.28 = (f32[16,256]{1,0:T(8,128)S(1)}, f32[16,256]{1,0:T(8,128)S(1)}, u32[]{:S(2)}, u32[]{:S(2)}) collective-permute-start(f32[16,256]{1,0:T(8,128)S(1)} %tie.3), channel_id=1, source_target_pairs={{0,16},{8,24},{16,0},{24,8},{1,17},{9,25},{17,1},{25,9},{2,18},{10... | collective-permute-start | bytes 49160 | tf_op jit(solution)/shard_map/ppermute | solution.py:374
  155.3 16.9 %collective-permute-start.27 = (f32[16,256]{1,0:T(8,128)S(1)}, f32[16,256]{1,0:T(8,128)S(1)}, u32[]{:S(2)}, u32[]{:S(2)}) collective-permute-start(f32[16,256]{1,0:T(8,128)S(1)} %tie.3), channel_id=1, source_target_pairs={{0,8},{8,0},{16,24},{24,16},{1,9},{9,1},{17,25},{25,17},{2,10},{10... | collective-permute-start | bytes 49160 | tf_op jit(solution)/shard_map/ppermute | solution.py:374

commit v8 on v7

--- a/solution.py
+++ b/solution.py
@@ -23,9 +23,25 @@
     return pltpu.with_memory_space_constraint(value, pltpu.HBM)
 
 
+def row_sums(values):
+    folded = values[:, :128]
+    for c in range(1, values.shape[1] // 128):
+        folded = folded + values[:, c * 128 : (c + 1) * 128]
+    ones = jnp.ones((128, 128), jnp.bfloat16)
+    high = folded.astype(jnp.bfloat16)
+    low = (folded - high.astype(jnp.float32)).astype(jnp.bfloat16)
+    total = jnp.dot(high, ones, preferred_element_type=jnp.float32)
+    return total + jnp.dot(low, ones, preferred_element_type=jnp.float32)
+
+
+def scale_rows(values, factor):
+    parts = [values[:, c : c + 128] * factor for c in range(0, values.shape[1], 128)]
+    return jnp.concatenate(parts, axis=1)
+
+
 def unit_rows(wide):
-    inv = lax.rsqrt(jnp.sum(wide * wide, axis=1, keepdims=True) + 1e-06)
-    return wide * inv, inv
+    inv = lax.rsqrt(row_sums(wide * wide) + 1e-06)
+    return scale_rows(wide, inv), inv
 
 
 def column_of(row):
@@ -33,19 +49,20 @@
     return jnp.transpose(jnp.broadcast_to(row, (128, lanes)))[:, :1]
 
 
-def forward_kernel(base_ref, rep_ref, lab_ref, w_ref, _, *refs, classes, reps):
-    blocks = refs[:reps]
-    emb_ref, a_ref, b_ref, st_ref, wide_ref, xhat_ref, sum_ref = refs[reps:]
+def forward_kernel(
+    base_ref, rep_ref, lab_ref, w_ref, mixed_ref, emb_ref, a_ref, b_ref, st_ref, xhat_ref, sum_ref,
+    *, classes, reps,
+):
     step = pl.program_id(0)
     tile = w_ref.shape[0]
     batch = emb_ref.shape[0]
 
     @pl.when(step == 0)
     def _():
-        for k, block_ref in enumerate(blocks):
-            rows = block_ref.shape[0]
+        rows = batch // reps
+        for k in range(reps):
             first = pl.multiple_of((rep_ref[0] ^ k) * rows, rows)
-            emb_ref[pl.ds(first, rows), :] = block_ref[...]
+            emb_ref[pl.ds(first, rows), :] = mixed_ref[k * rows : (k + 1) * rows, :]
         xwide, _ = unit_rows(emb_ref[...].astype(jnp.float32))
         xhat_ref[...] = xwide.astype(jnp.bfloat16)
         sum_ref[...] = jnp.zeros_like(sum_ref)
@@ -53,8 +70,6 @@
         b_ref[...] = jnp.zeros_like(b_ref)
 
     wwide, _ = unit_rows(w_ref[...].astype(jnp.float32))
-    wide_ref[pl.ds(0, tile, stride=2), :] = wwide[:, :128]
-    wide_ref[pl.ds(1, tile, stride=2), :] = wwide[:, 128:]
     what = wwide.astype(jnp.bfloat16)
     cosine = lax.dot_general(xhat_ref[...], what, NT, preferred_element_type=jnp.float32)
     ids = lax.broadcasted_iota(jnp.int32, (batch, tile), 1)
@@ -86,8 +101,8 @@
         b = slope * label_row
         a = a_ref[...] + label_e * b
         gain = SCALE * x_inv
-        a_ref[...] = (a - xwide * jnp.sum(xwide * a, axis=1, keepdims=True)) * gain
-        b_ref[...] = (b - xwide * jnp.sum(xwide * b, axis=1, keepdims=True)) * gain
+        a_ref[...] = scale_rows(a - scale_rows(xwide, row_sums(xwide * a)), gain)
+        b_ref[...] = scale_rows(b - scale_rows(xwide, row_sums(xwide * b)), gain)
         lane = lax.broadcasted_iota(jnp.int32, (batch, 128), 1)
         stats = jnp.where(lane == 0, total, 0.0)
         stats = jnp.where(lane == 1, target, stats)
@@ -96,10 +111,8 @@
         st_ref[...] = jnp.transpose(stats)[:8, :]
 
 
-def forward(base, rep, blocks, labels, weights, after):
-    rows, width = blocks[0].shape
-    reps = len(blocks)
-    batch = rows * reps
+def forward(base, rep, mixed, reps, labels, weights):
+    batch, width = mixed.shape
     classes = weights.shape[0]
     tile = math.gcd(classes, 1024)
     whole = lambda i: (0, 0)
@@ -112,22 +125,19 @@
             smem,
             pl.BlockSpec((batch, 1), whole),
             pl.BlockSpec((tile, width), lambda i: (i, 0)),
-            pl.BlockSpec(memory_space=pl.ANY),
-        ]
-        + [pl.BlockSpec((rows, width), whole)] * reps,
+            pl.BlockSpec((batch, width), whole),
+        ],
         out_specs=[
             pl.BlockSpec((batch, width), whole),
             pl.BlockSpec((batch, width), whole),
             pl.BlockSpec((batch, width), whole),
             pl.BlockSpec((8, batch), whole),
-            pl.BlockSpec((2 * tile, 128), lambda i: (i, 0)),
         ],
         out_shape=[
             jax.ShapeDtypeStruct((batch, width), jnp.bfloat16),
             jax.ShapeDtypeStruct((batch, width), jnp.float32),
             jax.ShapeDtypeStruct((batch, width), jnp.float32),
             jax.ShapeDtypeStruct((8, batch), jnp.float32),
-            pltpu.HBM((2 * classes, 128), jnp.float32),
         ],
         scratch_shapes=[pltpu.VMEM((batch, width), jnp.bfloat16), pltpu.VMEM((batch, 128), jnp.float32)],
         compiler_params=pltpu.CompilerParams(
@@ -137,7 +147,7 @@
             flops=12 * batch * classes * width, bytes_accessed=classes * width * 2, transcendentals=0
         ),
         name="forward_sums",
-    )(base, rep, labels.reshape(batch, 1), weights, after, *blocks)
+    )(base, rep, labels.reshape(batch, 1), weights, mixed)
 
 
 def weight_kernel(base_ref, emb_ref, lab_ref, st_ref, tot_ref, w_ref, g_ref, xhat_ref, y_ref, v_ref):
@@ -162,7 +172,7 @@
     e = jnp.exp2(cosine * (SCALE * LOG2E) - SCALE * LOG2E)
     d = jnp.where(is_label, v_ref[...], e).astype(jnp.bfloat16)
     raw = jnp.dot(d, y_ref[...], preferred_element_type=jnp.float32)
-    g_ref[...] = (raw - wwide * jnp.sum(wwide * raw, axis=1, keepdims=True)) * w_inv
+    g_ref[...] = scale_rows(raw - scale_rows(wwide, row_sums(wwide * raw)), w_inv)
 
 
 def weight_gradient(base, emb, labels, stats, totals, weights):
@@ -253,65 +263,57 @@
         return carry
 
     lax.fori_loop(0, peers, prepare, 0)
-    held_copy.wait()
-
-    def place(j, carry):
-        source = j // (size // batch)
-        at = (j - source * (size // batch)) * batch
-        start = (me_ref[0] ^ source) * run + first + at
-        at = (source * size + at) * 2
-        slots = [slot_ref[start + v] for v in range(batch)]
-        values = [
-            stage_ref[pl.ds(at + 2 * v, 2), :] + held_ref[pl.ds(slot, 2), :]
-            for v, slot in enumerate(slots)
-        ]
-        for slot, value in zip(slots, values):
-            held_ref[pl.ds(slot, 2), :] = value
+    if held_copy is not None:
+        held_copy.wait()
+
+    def place(source, carry):
+        start = (me_ref[0] ^ source) * run + first
+        at = source * size * 2
+        for block in range(0, size, batch):
+            slots = [slot_ref[start + block + v] for v in range(batch)]
+            values = [stage_ref[pl.ds(at + 2 * (block + v), 2), :] for v in range(batch)]
+            for slot, value in zip(slots, values):
+                held_ref[pl.ds(slot, 2), :] = value
         return carry
 
-    lax.fori_loop(0, peers * size // batch, place, 0)
+    lax.fori_loop(0, peers, place, 0)
 
 
 def place_kernel(
-    me_ref, slot_ref, row_ref, in_ref, _, out_ref, token_ref, held_ref, stage_ref, sem,
-    *, peers, run, first,
+    me_ref, slot_ref, row_ref, _, out_ref, token_ref, held_ref, stage_ref, sem, *, peers, run, first
 ):
     token_ref[...] = jnp.zeros_like(token_ref)
-    load = pltpu.make_async_copy(in_ref, held_ref, sem.at[0])
-    load.start()
-    place_runs(me_ref, slot_ref, row_ref, held_ref, stage_ref, load, peers, run, first)
-    store = pltpu.make_async_copy(held_ref, out_ref, sem.at[1])
+    place_runs(me_ref, slot_ref, row_ref, held_ref, stage_ref, None, peers, run, first)
+    store = pltpu.make_async_copy(held_ref, out_ref, sem)
     store.start()
     store.wait()
 
 
-def place_rows(me, slots, rows, held, after, peers, run, first):
+def place_rows(me, slots, rows, after, peers, run, first):
     smem = pl.BlockSpec(memory_space=pltpu.SMEM)
     vmem = pl.BlockSpec(memory_space=pltpu.VMEM)
-    anywhere = pl.BlockSpec(memory_space=pltpu.HBM)
+    anywhere = pl.BlockSpec(memory_space=pl.ANY)
+    held = (2 * peers * run, 128)
     return pl.pallas_call(
         functools.partial(place_kernel, peers=peers, run=run, first=first),
-        in_specs=[smem, smem, vmem, anywhere, anywhere],
+        in_specs=[smem, smem, vmem, anywhere],
         out_specs=[anywhere, vmem],
-        out_shape=[
-            pltpu.HBM(held.shape, jnp.float32),
-            jax.ShapeDtypeStruct((8, 128), jnp.float32),
-        ],
+        out_shape=[pltpu.HBM(held, jnp.float32), jax.ShapeDtypeStruct((8, 128), jnp.float32)],
         scratch_shapes=[
-            pltpu.VMEM(held.shape, jnp.float32),
+            pltpu.VMEM(held, jnp.float32),
             pltpu.VMEM((2 * rows.shape[0], 128), jnp.float32),
-            pltpu.SemaphoreType.DMA((2,)),
+            pltpu.SemaphoreType.DMA,
         ],
         compiler_params=pltpu.CompilerParams(vmem_limit_bytes=32 * MIB),
         cost_estimate=pl.CostEstimate(
             flops=0, bytes_accessed=16 * rows.shape[0] * rows.shape[1], transcendentals=0
         ),
         name="place_rows",
-    )(me, slots, rows, held, after)
+    )(me, slots, rows, after)
 
 
 def blend_kernel(
-    me_ref, slot_ref, row_ref, in_ref, o_ref, held_ref, stage_ref, sem, *, peers, run, first
+    me_ref, slot_ref, w_ref, row_ref, in_ref, o_ref, held_ref, stage_ref, sem, *, peers, run, first
 ):
     step = pl.program_id(0)
     tile = o_ref.shape[0]
@@ -322,25 +324,26 @@
         load.start()
         place_runs(me_ref, slot_ref, row_ref, held_ref, stage_ref, load, peers, run, first)
 
+    wwide, _ = unit_rows(w_ref[...].astype(jnp.float32))
     at = pl.multiple_of(step * 2 * tile, 2 * tile)
-    low = held_ref[pl.ds(at, tile, stride=2), :]
-    high = held_ref[pl.ds(at + 1, tile, stride=2), :]
-    square = jnp.sum(low * low + high * high, axis=1, keepdims=True)
-    inv = lax.rsqrt(square + 1e-06)
+    low = wwide[:, :128] + held_ref[pl.ds(at, tile, stride=2), :]
+    high = wwide[:, 128:] + held_ref[pl.ds(at + 1, tile, stride=2), :]
+    inv = lax.rsqrt(row_sums(low * low + high * high) + 1e-06)
     o_ref[:, :128] = (low * inv).astype(jnp.bfloat16)
     o_ref[:, 128:] = (high * inv).astype(jnp.bfloat16)
 
 
-def place_and_blend(me, slots, rows, held, peers, run, first):
-    classes, width = peers * run, rows.shape[1]
+def place_and_blend(me, slots, rows, held, weights, peers, run, first):
+    classes, width = weights.shape
     tile = math.gcd(classes, 1024)
     smem = pl.BlockSpec(memory_space=pltpu.SMEM)
     vmem = pl.BlockSpec(memory_space=pltpu.VMEM)
+    tiles = pl.BlockSpec((tile, width), lambda i: (i, 0))
     return pl.pallas_call(
         functools.partial(blend_kernel, peers=peers, run=run, first=first),
         grid=(classes // tile,),
-        in_specs=[smem, smem, vmem, pl.BlockSpec(memory_space=pltpu.HBM)],
-        out_specs=pl.BlockSpec((tile, width), lambda i: (i, 0)),
+        in_specs=[smem, smem, tiles, vmem, pl.BlockSpec(memory_space=pl.ANY)],
+        out_specs=tiles,
         out_shape=pltpu.HBM((classes, width), jnp.bfloat16),
         scratch_shapes=[
             pltpu.VMEM(held.shape, jnp.float32),
@@ -354,7 +357,7 @@
             flops=0, bytes_accessed=12 * classes * width, transcendentals=0
         ),
         name="place_and_blend",
-    )(me, slots, rows, held)
+    )(me, slots, weights, rows, held)
 
 
 def shards(embeddings, labels, class_weights, centroids, centroid_class):
@@ -373,56 +376,62 @@
         size = lax.axis_size(axis)
         return lax.ppermute(value, axis, [(i, i ^ k) for i in range(size)]) if k else value
 
-    def pick(value, axis, k, dim):
-        return lax.dynamic_index_in_dim(value, lax.axis_index(axis) ^ k, dim, keepdims=False)
-
-    blocks = [swap(embeddings, "rep", k) for k in range(reps)]
+    def released(value, tokens):
+        return lax.dynamic_update_slice(value, tie(value[:1, :16], tokens), (0, 0, 0))
+
+    def relay(sent):
+        return lax.all_to_all(sent, ALL, 0, 0, tiled=True).reshape(-1, width)
 
     weights = in_hbm(class_weights)
     runs = in_hbm(centroids.reshape(peers, run, width))
     cut = run * 5 // 8 // 16 * 16
-
-    def relay(sent):
-        return lax.all_to_all(sent, ALL, 0, 0, tiled=True).reshape(-1, width)
-
-    sent = fetch(runs, 0, cut, blocks[1:])
-    rows_a = relay(sent)
-    emb, a, b, stats, wide = forward(base, rep.reshape(1), blocks, labels, weights, sent)
-
-    wanted = centroid_class.reshape(reps, groups, run).astype(jnp.float32)
-    sums = stats[:2].reshape(-1)
-    near = [
-        swap(jnp.concatenate([sums, pick(wanted, "grp", j, 1).reshape(-1)]).reshape(-1, 128), "grp", j)
-        for j in range(groups)
-    ]
-    near = jnp.stack(near).reshape(groups, -1)
-    sums = jnp.sum(near[:, : 2 * batch], axis=0)
-    wanted = near[:, 2 * batch :].reshape(groups, reps, run)
-    every = [
-        swap(jnp.concatenate([sums, pick(wanted, "rep", k, 1).reshape(-1)]).reshape(-1, 128), "rep", k)
-        for k in range(reps)
-    ]
-    every = jnp.stack(every).reshape(reps, -1)
-    sums = jnp.sum(every[:, : 2 * batch], axis=0)
-    slots = every[:, 2 * batch :].reshape(-1).astype(jnp.int32) * 2
+    mixed = jnp.concatenate([swap(embeddings, "rep", k) for k in range(reps)])
+    rows_a = relay(released(fetch(runs, 0, cut, []), [mixed]))
+    emb, a, b, stats = forward(base, rep.reshape(1), mixed, reps, labels, weights)
+
+    half = reps // 2
+    core, deep = rep % 2, rep // 2
+    index = lax.dynamic_index_in_dim
+
+    def share_out(sums, wanted, axis, flips):
+        got = []
+        for flip, asked in zip(flips, wanted):
+            sent = jnp.concatenate([sums, asked.reshape(-1)]).reshape(-1, 128)
+            got.append(swap(sent, axis, flip).reshape(-1))
+        got = jnp.stack(got)
+        return jnp.sum(got[:, : 2 * batch], axis=0), got[:, 2 * batch :]
+
+    wanted = centroid_class.reshape(half, 2, groups, run).astype(jnp.float32)
+    wanted = [index(wanted, grp ^ j, 2, False) for j in range(groups)]
+    sums, wanted = share_out(stats[:2].reshape(-1), wanted, "grp", range(groups))
+    wanted = wanted.reshape(groups, half, 2, run)
+    wanted = [index(wanted, core ^ c, 2, False) for c in range(2)]
+    sums, wanted = share_out(sums, wanted, "rep", range(2))
+    sent_b = fetch(runs, cut, run - cut, [stats])
+    sums = tie(sums.reshape(-1, 128), [sent_b]).reshape(-1)
+    wanted = wanted.reshape(2, groups, half, run)
+    wanted = [index(wanted, deep ^ z, 2, False) for z in range(half)]
+    sums, slots = share_out(sums, wanted, "rep", range(0, reps, 2))
+    slots = slots.reshape(-1).astype(jnp.int32) * 2
     total, target = sums[:batch], sums[batch:]
     losses = SCALE + jnp.log(total) - target
     loss = lax.dynamic_slice_in_dim(losses, rep * rows_local, rows_local, 0)
 
-    rows_b = relay(fetch(runs, cut, run - cut, [total]))
+    rows_b = relay(released(sent_b, [total]))
     weight_grad = weight_gradient(base, emb, labels, stats, total, weights)
     done = in_hbm(weight_grad)
-    held, token = place_rows(me, slots, rows_a, in_hbm(wide), done, peers, run, 0)
-
-    grad = (a / total[:, None] - b).reshape(reps, groups, share, width)
-    grad = sum(swap(pick(grad, "grp", j, 1), "grp", j) for j in range(groups))
+    held, token = place_rows(me, slots, rows_a, done, peers, run, 0)
+
+    grad = (a / total[:, None] - b).reshape(half, 2, groups, share, width)
+    grad = sum(swap(index(grad, grp ^ j, 2, False), "grp", j) for j in range(groups))
     grad = tie(grad, [done])
-    own = sum(swap(pick(grad, "rep", k, 0), "rep", k) for k in range(reps))
+    grad = sum(swap(index(grad, core ^ c, 1, False), "rep", c) for c in range(2))
+    own = sum(swap(index(grad, deep ^ z, 0, False), "rep", 2 * z) for z in range(half))
     own = tie(own, [token])
     shares = jnp.stack([swap(own, "grp", j) for j in range(groups)])
     embedding_gradient = shares[grp ^ jnp.arange(groups)].reshape(rows_local, width)
 
-    refreshed = place_and_blend(me, slots, rows_b, in_hbm(held), peers, run, cut)
+    refreshed = place_and_blend(me, slots, rows_b, in_hbm(held), weights, peers, run, cut)
     return (loss, embedding_gradient, weight_grad, refreshed)
 
 

time: 175 us -> 170 us (0.971)
  starting transfers between devices: 56.7 us -> 38 us
  waiting for transfers between devices: 38.5 us -> 51.1 us
  Pallas kernels: 65.5 us -> 67.5 us
    ppermute x30 -> x24, starting transfers between devices: 49 us -> 29.4 us  [swap(): lax.ppermute(value, axis, [(i, i ^ k) for i in range(size)])]
    ppermute x30 -> x24, waiting for transfers between devices: 38.5 us -> 51.1 us  [swap(): lax.ppermute(value, axis, [(i, i ^ k) for i in range(size)])]
    pallas_call x1, Pallas kernels: 19 us -> 14 us  [place_rows(): pl.pallas_call(functools.partial(place_kernel, peers=peers, run=run, firs...]
    unnamed x34 -> x24, local copies, waits for them, and re-layouts: 8.14 us -> 4.18 us
    pallas_call x1, Pallas kernels: 11.8 us -> 14.7 us  [weight_gradient(): pl.pallas_call(weight_kernel, grid=(classes // tile,), in_specs=[pl.Block...]
    pallas_call x1, Pallas kernels: 15.8 us -> 17.6 us  [place_and_blend(): pl.pallas_call(functools.partial(blend_kernel, peers=peers, run=run, firs...]
  transfers between devices with their start and end apart: 32 -> 26, of which waited for: 12 -> 12; matrix products, arithmetic and copies ran while one was open for 1% -> 4% of each run, Pallas kernels for 36% -> 40%
where the time goes in v8:
time: 170 us; the launch traced here: 169 us
  Pallas kernels  67.5 us (40%)
  waiting for transfers between devices  51.1 us (30%)
  starting transfers between devices  38 us (22%)
  local copies, waits for them, and re-layouts  9.67 us (6%)
    ppermute x24, waiting for transfers between devices, swap(): lax.ppermute(value, axis, [(i, i ^ k) for i in range(size)])  51.1 us
    ppermute x24, starting transfers between devices, swap(): lax.ppermute(value, axis, [(i, i ^ k) for i in range(size)])  29.4 us
    pallas_call x1, Pallas kernels, place_and_blend(): pl.pallas_call(functools.partial(blend_kernel, peers=peers, run=run, firs...  17.6 us
    pallas_call x1, Pallas kernels, forward(): pl.pallas_call(functools.partial(forward_kernel, classes=classes, reps=re...  15.3 us
    pallas_call x1, Pallas kernels, weight_gradient(): pl.pallas_call(weight_kernel, grid=(classes // tile,), in_specs=[pl.Block...  14.7 us
    pallas_call x1, Pallas kernels, place_rows(): pl.pallas_call(functools.partial(place_kernel, peers=peers, run=run, firs...  14 us
    all_to_all x2, starting transfers between devices, relay(): return lax.all_to_all(sent, ALL, 0, 0, tiled=True).reshape(-1, width)  8.63 us
    pallas_call x2, Pallas kernels, fetch(): pl.pallas_call(functools.partial(fetch_kernel, first=first), in_specs=[hb...  5.81 us
  transfers between devices with their start and end apart: 26, of which 12 were waited for; matrix products, arithmetic and copies ran while one was open for 4% of the time, Pallas kernels for 40%

profile of v8, /device:TPU:0, one launch (start us, length us, event | category | flops | bytes accessed | tf_op | source)
XLA Modules:
  0.0 168.8 jit_solution(10262061524114857703)
XLA Ops:
  0.6 5.1 %collective-permute-start.5 = (bf16[64,256]{1,0:T(8,128)(2,1)}, bf16[64,256]{1,0:T(8,128)(2,1)S(1)}, u32[]{:S(2)}, u32[]{:S(2)}) collective-permute-start(bf16[64,256]{1,0:T(8,128)(2,1)} %param.5), channel_id=1, source_target_pairs={{0,6},{1,7},{2,4},{3,5},{4,2},{5,3},{6,0},{7,1},{8,14},{9,15},{10,... | collective-permute-start | bytes 98312 | tf_op jit(solution)/shard_map/ppermute | solution.py:377
  5.7 0.0 collective-permute-start.4
  5.7 2.1 %collective-permute-start.3 = (bf16[64,256]{1,0:T(8,128)(2,1)}, bf16[64,256]{1,0:T(8,128)(2,1)S(1)}, u32[]{:S(2)}, u32[]{:S(2)}) collective-permute-start(bf16[64,256]{1,0:T(8,128)(2,1)} %param.5), channel_id=1, source_target_pairs={{0,4},{1,5},{2,6},{3,7},{4,0},{5,1},{6,2},{7,3},{8,12},{9,13},{10,... | collective-permute-start | bytes 98312 | tf_op jit(solution)/shard_map/ppermute | solution.py:377
  7.8 0.0 collective-permute-start.2
  7.8 0.7 collective-permute-start
  8.5 0.8 constant_dynamic-update-slice_fusion.7
  9.3 3.2 %fetch.3 = bf16[32,160,256]{2,1,0:T(8,128)(2,1)} custom-call(bf16[32,256,256]{2,1,0:T(8,128)(2,1)} %bitcast.103), custom_call_target="tpu_custom_call" | custom-call | flops 1 | bytes 1 | tf_op jit(solution)/shard_map/fetch/pallas_call | solution.py:223
  12.5 0.7 slice.46.value_ref
  13.2 0.0 collective-permute-done
  13.2 1.7 collective-permute-start.1
  14.9 2.2 %collective-permute-done.1 = bf16[64,256]{1,0:T(8,128)(2,1)S(1)} collective-permute-done((bf16[64,256]{1,0:T(8,128)(2,1)S(1)}, bf16[64,256]{1,0:T(8,128)(2,1)S(1)}, u32[]{:S(2)}, u32[]{:S(2)}) %collective-permute-start.1) | collective-permute-done | bytes 32800 | tf_op jit(solution)/shard_map/ppermute | solution.py:377
  17.1 0.3 collective-permute-start.6
  17.5 0.0 collective-permute-done.2
  17.5 4.7 %collective-permute-done.6 = bf16[64,256]{1,0:T(8,128)(2,1)S(1)} collective-permute-done((bf16[64,256]{1,0:T(8,128)(2,1)S(1)}, bf16[64,256]{1,0:T(8,128)(2,1)S(1)}, u32[]{:S(2)}, u32[]{:S(2)}) %collective-permute-start.6) | collective-permute-done | bytes 32800 | tf_op jit(solution)/shard_map/ppermute | solution.py:377
  22.3 0.6 constant_dynamic-update-slice_fusion.9
  22.9 4.0 %all-to-all-start = ((bf16[32,160,256]{2,1,0:T(8,128)(2,1)}), bf16[32,160,256]{2,1,0:T(8,128)(2,1)S(1)}, u32[]{:S(2)}, u32[]{:S(2)}) async-start(bf16[32,160,256]{2,1,0:T(8,128)(2,1)} %constant_dynamic-update-slice_fusion.9), calls=%async_computation | async-start | bytes 5242880 | tf_op jit(solution)/shard_map/all_to_all | solution.py:383
  27.0 0.9 copy.18.lab_ref
  27.9 0.0 copy-start.1
  27.9 0.9 copy-done.1
  28.9 15.3 %forward_sums.1 = (bf16[512,256]{1,0:T(8,128)(2,1)S(1)}, f32[512,256]{1,0:T(8,128)S(1)}, f32[512,256]{1,0:T(8,128)S(1)}, f32[8,512]{1,0:T(8,128)S(1)}) custom-call(s32[1]{0:T(128)S(6)} %mul.18.base_ref, s32[1]{0:T(128)} %bitcast.1.rep_ref, s32[512,1]{1,0:T(8,128)S(1)} %copy-done.1, bf16[8192,256]{1,0:T(8,128)(2,1)} %w_ref.5, ...), custom_call_target="tpu_custom_call" | custom-call | flops 12884901888 | bytes 4194304 | tf_op jit(solution)/shard_map/forward_sums/pallas_call | solution.py:120
  44.2 0.8 copy-done
  45.0 0.7 copy-done.3
  45.7 1.8 %collective-permute-start.7 = (f32[24,128]{1,0:T(8,128)S(1)}, f32[24,128]{1,0:T(8,128)S(1)}, u32[]{:S(2)}, u32[]{:S(2)}) collective-permute-start(f32[24,128]{1,0:T(8,128)S(1)} %get-tuple-element.41), channel_id=1, source_target_pairs={{0,8},{8,0},{16,24},{24,16},{1,9},{9,1},{17,25},{25,17},{2,10},{10... | collective-permute-start | bytes 36872 | tf_op jit(solution)/shard_map/ppermute | solution.py:377
  47.5 1.5 collective-permute-start.8
  49.0 0.3 collective-permute-start.9
  49.3 0.2 collective-permute-done.7
  49.5 1.8 %collective-permute-done.8 = f32[24,128]{1,0:T(8,128)S(1)} collective-permute-done((f32[24,128]{1,0:T(8,128)S(1)}, f32[24,128]{1,0:T(8,128)S(1)}, u32[]{:S(2)}, u32[]{:S(2)}) %collective-permute-start.8) | collective-permute-done | bytes 12320 | tf_op jit(solution)/shard_map/ppermute | solution.py:377
  51.3 3.6 %collective-permute-done.9 = f32[24,128]{1,0:T(8,128)S(1)} collective-permute-done((f32[24,128]{1,0:T(8,128)S(1)}, f32[24,128]{1,0:T(8,128)S(1)}, u32[]{:S(2)}, u32[]{:S(2)}) %collective-permute-start.9) | collective-permute-done | bytes 12320 | tf_op jit(solution)/shard_map/ppermute | solution.py:377
  55.0 0.1 collective-permute-start.10
  55.1 2.6 %fetch.2.refs_0_ = bf16[32,96,256]{2,1,0:T(8,128)(2,1)} custom-call(bf16[32,256,256]{2,1,0:T(8,128)(2,1)} %bitcast.104, f32[8,512]{1,0:T(8,128)S(1)} %get-tuple-element.10.refs_0_.st_ref), custom_call_target="tpu_custom_call" | custom-call | flops 1 | bytes 1 | tf_op jit(solution)/shard_map/fetch/pallas_call | solution.py:223
  57.7 0.0 collective-permute-done.10
  57.9 0.4 collective-permute-start.11
  58.3 2.4 %collective-permute-start.12 = (f32[24,128]{1,0:T(8,128)S(1)}, f32[24,128]{1,0:T(8,128)S(1)}, u32[]{:S(2)}, u32[]{:S(2)}) collective-permute-start(f32[24,128]{1,0:T(8,128)S(1)} %get-tuple-element.36), channel_id=1, source_target_pairs={{0,4},{1,5},{2,6},{3,7},{4,0},{5,1},{6,2},{7,3},{8,12},{9,13},{10,... | collective-permute-start | bytes 36872 | tf_op jit(solution)/shard_map/ppermute | solution.py:377
  60.7 1.7 collective-permute-start.13
  62.3 0.7 slice.47.value_ref
  63.0 7.5 %collective-permute-done.11 = f32[24,128]{1,0:T(8,128)S(1)} collective-permute-done((f32[24,128]{1,0:T(8,128)S(1)}, f32[24,128]{1,0:T(8,128)S(1)}, u32[]{:S(2)}, u32[]{:S(2)}) %collective-permute-start.11) | collective-permute-done | bytes 12320 | tf_op jit(solution)/shard_map/ppermute | solution.py:377
  70.5 17.3 %collective-permute-done.12 = f32[24,128]{1,0:T(8,128)S(1)} collective-permute-done((f32[24,128]{1,0:T(8,128)S(1)}, f32[24,128]{1,0:T(8,128)S(1)}, u32[]{:S(2)}, u32[]{:S(2)}) %collective-permute-start.12) | collective-permute-done | bytes 12320 | tf_op jit(solution)/shard_map/ppermute | solution.py:377
  87.8 0.0 collective-permute-done.13
  87.9 0.6 constant_dynamic-update-slice_fusion.8
  88.5 4.6 %all-to-all-start.1 = ((bf16[32,96,256]{2,1,0:T(8,128)(2,1)}), bf16[32,96,256]{2,1,0:T(8,128)(2,1)}, u32[]{:S(2)}, u32[]{:S(2)}) async-start(bf16[32,96,256]{2,1,0:T(8,128)(2,1)} %constant_dynamic-update-slice_fusion.8), calls=%async_computation.1 | async-start | bytes 3145728 | tf_op jit(solution)/shard_map/all_to_all | solution.py:383
  93.1 1.2 divide_subtract_fusion
  94.3 1.8 %collective-permute-start.14 = (f32[4,2,16,256]{3,2,1,0:T(8,128)S(1)}, f32[4,2,16,256]{3,2,1,0:T(8,128)S(1)}, u32[]{:S(2)}, u32[]{:S(2)}) collective-permute-start(f32[4,2,16,256]{3,2,1,0:T(8,128)S(1)} %get-tuple-element.16), channel_id=1, source_target_pairs={{0,8},{8,0},{16,24},{24,16},{1,9},{9,1},{17,25},{25,17},{2,10},{10... | collective-permute-start | bytes 393224 | tf_op jit(solution)/shard_map/ppermute | solution.py:377
  96.1 1.5 collective-permute-start.15
  97.5 0.3 collective-permute-start.16
  97.9 0.9 copy-done.4
  98.8 14.7 %weight_gradient.1.refs_0_._ = f32[8192,256]{1,0:T(8,128)} custom-call(s32[1]{0:T(128)S(6)} %mul.18.base_ref, bf16[512,256]{1,0:T(8,128)(2,1)S(1)} %copy-done.4, s32[1,512]{1,0:T(1,128)S(1)} %bitcast.102, f32[8,512]{1,0:T(8,128)S(1)} %get-tuple-element.10.refs_0_.st_ref, f32[1,512]{1,0:T(1,128)S(1)} %bitcast.98, bf16[8192,256]{1,0:T(8,128)(2,1)} %w_ref.5), custom_call_target="tpu_custom_call" | custom-call | flops 12884901888 | bytes 12582912 | tf_op jit(solution)/shard_map/weight_gradient/pallas_call | solution.py:183
  113.5 0.0 collective-permute-done.14
  113.5 0.0 collective-permute-done.15
  113.5 2.2 %collective-permute-done.16 = f32[4,2,16,256]{3,2,1,0:T(8,128)S(1)} collective-permute-done((f32[4,2,16,256]{3,2,1,0:T(8,128)S(1)}, f32[4,2,16,256]{3,2,1,0:T(8,128)S(1)}, u32[]{:S(2)}, u32[]{:S(2)}) %collective-permute-start.16) | collective-permute-done | bytes 131104 | tf_op jit(solution)/shard_map/ppermute | solution.py:377
  115.8 0.1 collective-permute-start.17
  115.9 1.2 collective-permute-done.17
  117.2 0.1 collective-permute-start.18
  117.3 3.7 %collective-permute-start.20 = (f32[16,256]{1,0:T(8,128)S(1)}, f32[16,256]{1,0:T(8,128)S(1)}, u32[]{:S(2)}, u32[]{:S(2)}) collective-permute-start(f32[16,256]{1,0:T(8,128)S(1)} %get-tuple-element.20), channel_id=1, source_target_pairs={{0,6},{1,7},{2,4},{3,5},{4,2},{5,3},{6,0},{7,1},{8,14},{9,15},{10,... | collective-permute-start | bytes 49160 | tf_op jit(solution)/shard_map/ppermute | solution.py:377
  121.0 0.5 collective-permute-start.19
  121.5 0.1 collective-permute-done.18
  121.6 2.1 %collective-permute-done.20 = f32[16,256]{1,0:T(8,128)S(1)} collective-permute-done((f32[16,256]{1,0:T(8,128)S(1)}, f32[16,256]{1,0:T(8,128)S(1)}, u32[]{:S(2)}, u32[]{:S(2)}) %collective-permute-start.20) | collective-permute-done | bytes 16416 | tf_op jit(solution)/shard_map/ppermute | solution.py:377
  123.7 8.2 %collective-permute-done.19 = f32[16,256]{1,0:T(8,128)S(1)} collective-permute-done((f32[16,256]{1,0:T(8,128)S(1)}, f32[16,256]{1,0:T(8,128)S(1)}, u32[]{:S(2)}, u32[]{:S(2)}) %collective-permute-start.19) | collective-permute-done | bytes 16416 | tf_op jit(solution)/shard_map/ppermute | solution.py:377
  131.9 14.0 %place_rows.1 = (f32[16384,128]{1,0:T(8,128)}, f32[8,128]{1,0:T(8,128)S(1)}) custom-call(s32[1]{0:T(128)} %bitcast.me_ref, s32[8192]{0:T(1024)S(1)} %bitcast.95, bf16[5120,256]{1,0:T(8,128)(2,1)S(1)} %bitcast.94, f32[8192,256]{1,0:T(8,128)} %weight_gradient.1.refs_0_._), custom_call_target="tpu_custom_call" | custom-call | bytes 20971520 | tf_op jit(solution)/shard_map/place_rows/pallas_call | solution.py:297
  145.9 2.5 %collective-permute-start.23 = (f32[16,256]{1,0:T(8,128)S(1)}, f32[16,256]{1,0:T(8,128)S(1)}, u32[]{:S(2)}, u32[]{:S(2)}) collective-permute-start(f32[16,256]{1,0:T(8,128)S(1)} %tie.8), channel_id=1, source_target_pairs={{0,24},{8,16},{16,8},{24,0},{1,25},{9,17},{17,9},{25,1},{2,26},{10... | collective-permute-start | bytes 49160 | tf_op jit(solution)/shard_map/ppermute | solution.py:377
  148.4 0.6 collective-permute-start.22
  148.9 0.5 collective-permute-start.21
  149.5 0.6 dynamic_slice.79
  150.1 17.6 %place_and_blend.1 = bf16[8192,256]{1,0:T(8,128)(2,1)} custom-call(s32[1]{0:T(128)} %bitcast.me_ref, s32[8192]{0:T(1024)S(1)} %bitcast.96, bf16[8192,256]{1,0:T(8,128)(2,1)} %w_ref.5, bf16[3072,256]{1,0:T(8,128)(2,1)} %bitcast.53.row_ref, f32[16384,128]{1,0:T(8,128)} %get-tuple-element.15.in_ref), custom_call_target="tpu_custom_call" | custom-call | bytes 25165824 | tf_op jit(solution)/shard_map/place_and_blend/pallas_call | solution.py:342
  167.7 1.2 gather_fusion
  (58 shorter events, 0.7 us)
Async XLA Ops:
  0.6 16.9 %collective-permute-start.5 = (bf16[64,256]{1,0:T(8,128)(2,1)}, bf16[64,256]{1,0:T(8,128)(2,1)S(1)}, u32[]{:S(2)}, u32[]{:S(2)}) collective-permute-start(bf16[64,256]{1,0:T(8,128)(2,1)} %param.5), channel_id=1, source_target_pairs={{0,6},{1,7},{2,4},{3,5},{4,2},{5,3},{6,0},{7,1},{8,14},{9,15},{10,... | collective-permute-start | bytes 98312 | tf_op jit(solution)/shard_map/ppermute | solution.py:377
  5.7 11.8 %collective-permute-start.4 = (bf16[64,256]{1,0:T(8,128)(2,1)}, bf16[64,256]{1,0:T(8,128)(2,1)S(1)}, u32[]{:S(2)}, u32[]{:S(2)}) collective-permute-start(bf16[64,256]{1,0:T(8,128)(2,1)} %param.5), channel_id=1, source_target_pairs={{0,5},{1,4},{2,7},{3,6},{4,1},{5,0},{6,3},{7,2},{8,13},{9,12},{10,... | collective-permute-start | bytes 98312 | tf_op jit(solution)/shard_map/ppermute | solution.py:377
  5.7 11.7 %collective-permute-start.3 = (bf16[64,256]{1,0:T(8,128)(2,1)}, bf16[64,256]{1,0:T(8,128)(2,1)S(1)}, u32[]{:S(2)}, u32[]{:S(2)}) collective-permute-start(bf16[64,256]{1,0:T(8,128)(2,1)} %param.5), channel_id=1, source_target_pairs={{0,4},{1,5},{2,6},{3,7},{4,0},{5,1},{6,2},{7,3},{8,12},{9,13},{10,... | collective-permute-start | bytes 98312 | tf_op jit(solution)/shard_map/ppermute | solution.py:377
  7.8 9.6 %collective-permute-start.2 = (bf16[64,256]{1,0:T(8,128)(2,1)}, bf16[64,256]{1,0:T(8,128)(2,1)S(1)}, u32[]{:S(2)}, u32[]{:S(2)}) collective-permute-start(bf16[64,256]{1,0:T(8,128)(2,1)} %param.5), channel_id=1, source_target_pairs={{0,3},{1,2},{2,1},{3,0},{4,7},{5,6},{6,5},{7,4},{8,11},{9,10},{10,... | collective-permute-start | bytes 98312 | tf_op jit(solution)/shard_map/ppermute | solution.py:377
  7.8 5.4 %collective-permute-start = (bf16[64,256]{1,0:T(8,128)(2,1)}, bf16[64,256]{1,0:T(8,128)(2,1)S(1)}, u32[]{:S(2)}, u32[]{:S(2)}) collective-permute-start(bf16[64,256]{1,0:T(8,128)(2,1)} %param.5), channel_id=1, source_target_pairs={{0,1},{1,0},{2,3},{3,2},{4,5},{5,4},{6,7},{7,6},{8,9},{9,8},{10,11... | collective-permute-start | bytes 98312 | tf_op jit(solution)/shard_map/ppermute | solution.py:377
  9.3 4.0 %copy-start.5 = (bf16[64,256]{1,0:T(8,128)(2,1)S(1)}, bf16[64,256]{1,0:T(8,128)(2,1)}, u32[]{:S(2)}) copy-start(bf16[64,256]{1,0:T(8,128)(2,1)} %param.5) | copy-start | bytes 98308
  13.2 3.9 %collective-permute-start.1 = (bf16[64,256]{1,0:T(8,128)(2,1)S(1)}, bf16[64,256]{1,0:T(8,128)(2,1)S(1)}, u32[]{:S(2)}, u32[]{:S(2)}) collective-permute-start(bf16[64,256]{1,0:T(8,128)(2,1)S(1)} %copy-done.5), channel_id=1, source_target_pairs={{0,2},{1,3},{2,0},{3,1},{4,6},{5,7},{6,4},{7,5},{8,10},{9,11},{10,... | collective-permute-start | bytes 98312 | tf_op jit(solution)/shard_map/ppermute | solution.py:377
  17.1 5.1 %collective-permute-start.6 = (bf16[64,256]{1,0:T(8,128)(2,1)S(1)}, bf16[64,256]{1,0:T(8,128)(2,1)S(1)}, u32[]{:S(2)}, u32[]{:S(2)}) collective-permute-start(bf16[64,256]{1,0:T(8,128)(2,1)S(1)} %copy-done.5), channel_id=1, source_target_pairs={{0,7},{1,6},{2,5},{3,4},{4,3},{5,2},{6,1},{7,0},{8,15},{9,14},{10,... | collective-permute-start | bytes 98312 | tf_op jit(solution)/shard_map/ppermute | solution.py:377
  22.9 4.1 %copy-start.6 = (s32[8192]{0:T(1024)S(1)}, s32[8192]{0:T(1024)}, u32[]{:S(2)}) copy-start(s32[8192]{0:T(1024)} %param.9) | copy-start | bytes 98308
  22.9 4.1 %copy-start.2 = (s32[512]{0:T(512)S(1)}, s32[512]{0:T(512)}, u32[]{:S(2)}) copy-start(s32[512]{0:T(512)} %param.6) | copy-start | bytes 6148
  22.9 65.6 %all-to-all-start = ((bf16[32,160,256]{2,1,0:T(8,128)(2,1)}), bf16[32,160,256]{2,1,0:T(8,128)(2,1)S(1)}, u32[]{:S(2)}, u32[]{:S(2)}) async-start(bf16[32,160,256]{2,1,0:T(8,128)(2,1)} %constant_dynamic-update-slice_fusion.9), calls=%async_computation | async-start | bytes 5242880 | tf_op jit(solution)/shard_map/all_to_all | solution.py:383
  27.9 1.0 copy-start.1
  44.2 0.8 copy-start
  45.0 0.7 copy-start.3
  45.7 3.8 %collective-permute-start.7 = (f32[24,128]{1,0:T(8,128)S(1)}, f32[24,128]{1,0:T(8,128)S(1)}, u32[]{:S(2)}, u32[]{:S(2)}) collective-permute-start(f32[24,128]{1,0:T(8,128)S(1)} %get-tuple-element.41), channel_id=1, source_target_pairs={{0,8},{8,0},{16,24},{24,16},{1,9},{9,1},{17,25},{25,17},{2,10},{10... | collective-permute-start | bytes 36872 | tf_op jit(solution)/shard_map/ppermute | solution.py:377
  47.5 3.7 %collective-permute-start.8 = (f32[24,128]{1,0:T(8,128)S(1)}, f32[24,128]{1,0:T(8,128)S(1)}, u32[]{:S(2)}, u32[]{:S(2)}) collective-permute-start(f32[24,128]{1,0:T(8,128)S(1)} %get-tuple-element.42), channel_id=1, source_target_pairs={{0,16},{8,24},{16,0},{24,8},{1,17},{9,25},{17,1},{25,9},{2,18},{10... | collective-permute-start | bytes 36872 | tf_op jit(solution)/shard_map/ppermute | solution.py:377
  49.0 5.8 %collective-permute-start.9 = (f32[24,128]{1,0:T(8,128)S(1)}, f32[24,128]{1,0:T(8,128)S(1)}, u32[]{:S(2)}, u32[]{:S(2)}) collective-permute-start(f32[24,128]{1,0:T(8,128)S(1)} %get-tuple-element.43), channel_id=1, source_target_pairs={{0,24},{8,16},{16,8},{24,0},{1,25},{9,17},{17,9},{25,1},{2,26},{10... | collective-permute-start | bytes 36872 | tf_op jit(solution)/shard_map/ppermute | solution.py:377
  55.0 2.7 %collective-permute-start.10 = (f32[40,128]{1,0:T(8,128)S(1)}, f32[40,128]{1,0:T(8,128)S(1)}, u32[]{:S(2)}, u32[]{:S(2)}) collective-permute-start(f32[40,128]{1,0:T(8,128)S(1)} %get-tuple-element.39), channel_id=1, source_target_pairs={{0,1},{1,0},{2,3},{3,2},{4,5},{5,4},{6,7},{7,6},{8,9},{9,8},{10,11... | collective-permute-start | bytes 61448 | tf_op jit(solution)/shard_map/ppermute | solution.py:377
  57.9 12.6 %collective-permute-start.11 = (f32[24,128]{1,0:T(8,128)S(1)}, f32[24,128]{1,0:T(8,128)S(1)}, u32[]{:S(2)}, u32[]{:S(2)}) collective-permute-start(f32[24,128]{1,0:T(8,128)S(1)} %get-tuple-element.35), channel_id=1, source_target_pairs={{0,2},{1,3},{2,0},{3,1},{4,6},{5,7},{6,4},{7,5},{8,10},{9,11},{10,... | collective-permute-start | bytes 36872 | tf_op jit(solution)/shard_map/ppermute | solution.py:377
  58.3 29.5 %collective-permute-start.12 = (f32[24,128]{1,0:T(8,128)S(1)}, f32[24,128]{1,0:T(8,128)S(1)}, u32[]{:S(2)}, u32[]{:S(2)}) collective-permute-start(f32[24,128]{1,0:T(8,128)S(1)} %get-tuple-element.36), channel_id=1, source_target_pairs={{0,4},{1,5},{2,6},{3,7},{4,0},{5,1},{6,2},{7,3},{8,12},{9,13},{10,... | collective-permute-start | bytes 36872 | tf_op jit(solution)/shard_map/ppermute | solution.py:377
  60.7 27.1 %collective-permute-start.13 = (f32[24,128]{1,0:T(8,128)S(1)}, f32[24,128]{1,0:T(8,128)S(1)}, u32[]{:S(2)}, u32[]{:S(2)}) collective-permute-start(f32[24,128]{1,0:T(8,128)S(1)} %get-tuple-element.37), channel_id=1, source_target_pairs={{0,6},{1,7},{2,4},{3,5},{4,2},{5,3},{6,0},{7,1},{8,14},{9,15},{10,... | collective-permute-start | bytes 36872 | tf_op jit(solution)/shard_map/ppermute | solution.py:377
  88.5 61.6 %all-to-all-start.1 = ((bf16[32,96,256]{2,1,0:T(8,128)(2,1)}), bf16[32,96,256]{2,1,0:T(8,128)(2,1)}, u32[]{:S(2)}, u32[]{:S(2)}) async-start(bf16[32,96,256]{2,1,0:T(8,128)(2,1)} %constant_dynamic-update-slice_fusion.8), calls=%async_computation.1 | async-start | bytes 3145728 | tf_op jit(solution)/shard_map/all_to_all | solution.py:383
  94.3 19.2 %collective-permute-start.14 = (f32[4,2,16,256]{3,2,1,0:T(8,128)S(1)}, f32[4,2,16,256]{3,2,1,0:T(8,128)S(1)}, u32[]{:S(2)}, u32[]{:S(2)}) collective-permute-start(f32[4,2,16,256]{3,2,1,0:T(8,128)S(1)} %get-tuple-element.16), channel_id=1, source_target_pairs={{0,8},{8,0},{16,24},{24,16},{1,9},{9,1},{17,25},{25,17},{2,10},{10... | collective-permute-start | bytes 393224 | tf_op jit(solution)/shard_map/ppermute | solution.py:377
  96.1 17.5 %collective-permute-start.15 = (f32[4,2,16,256]{3,2,1,0:T(8,128)S(1)}, f32[4,2,16,256]{3,2,1,0:T(8,128)S(1)}, u32[]{:S(2)}, u32[]{:S(2)}) collective-permute-start(f32[4,2,16,256]{3,2,1,0:T(8,128)S(1)} %get-tuple-element.17), channel_id=1, source_target_pairs={{0,16},{8,24},{16,0},{24,8},{1,17},{9,25},{17,1},{25,9},{2,18},{10... | collective-permute-start | bytes 393224 | tf_op jit(solution)/shard_map/ppermute | solution.py:377
  97.5 18.2 %collective-permute-start.16 = (f32[4,2,16,256]{3,2,1,0:T(8,128)S(1)}, f32[4,2,16,256]{3,2,1,0:T(8,128)S(1)}, u32[]{:S(2)}, u32[]{:S(2)}) collective-permute-start(f32[4,2,16,256]{3,2,1,0:T(8,128)S(1)} %get-tuple-element.18), channel_id=1, source_target_pairs={{0,24},{8,16},{16,8},{24,0},{1,25},{9,17},{17,9},{25,1},{2,26},{10... | collective-permute-start | bytes 393224 | tf_op jit(solution)/shard_map/ppermute | solution.py:377
  97.9 0.9 copy-start.4
  115.8 1.3 collective-permute-start.17
  117.2 4.4 %collective-permute-start.18 = (f32[16,256]{1,0:T(8,128)S(1)}, f32[16,256]{1,0:T(8,128)S(1)}, u32[]{:S(2)}, u32[]{:S(2)}) collective-permute-start(f32[16,256]{1,0:T(8,128)S(1)} %get-tuple-element.19), channel_id=1, source_target_pairs={{0,2},{1,3},{2,0},{3,1},{4,6},{5,7},{6,4},{7,5},{8,10},{9,11},{10,... | collective-permute-start | bytes 49160 | tf_op jit(solution)/shard_map/ppermute | solution.py:377
  117.3 6.4 %collective-permute-start.20 = (f32[16,256]{1,0:T(8,128)S(1)}, f32[16,256]{1,0:T(8,128)S(1)}, u32[]{:S(2)}, u32[]{:S(2)}) collective-permute-start(f32[16,256]{1,0:T(8,128)S(1)} %get-tuple-element.20), channel_id=1, source_target_pairs={{0,6},{1,7},{2,4},{3,5},{4,2},{5,3},{6,0},{7,1},{8,14},{9,15},{10,... | collective-permute-start | bytes 49160 | tf_op jit(solution)/shard_map/ppermute | solution.py:377
  121.0 10.9 %collective-permute-start.19 = (f32[16,256]{1,0:T(8,128)S(1)}, f32[16,256]{1,0:T(8,128)S(1)}, u32[]{:S(2)}, u32[]{:S(2)}) collective-permute-start(f32[16,256]{1,0:T(8,128)S(1)} %get-tuple-element.21), channel_id=1, source_target_pairs={{0,4},{1,5},{2,6},{3,7},{4,0},{5,1},{6,2},{7,3},{8,12},{9,13},{10,... | collective-permute-start | bytes 49160 | tf_op jit(solution)/shard_map/ppermute | solution.py:377
  145.9 21.7 %collective-permute-start.23 = (f32[16,256]{1,0:T(8,128)S(1)}, f32[16,256]{1,0:T(8,128)S(1)}, u32[]{:S(2)}, u32[]{:S(2)}) collective-permute-start(f32[16,256]{1,0:T(8,128)S(1)} %tie.8), channel_id=1, source_target_pairs={{0,24},{8,16},{16,8},{24,0},{1,25},{9,17},{17,9},{25,1},{2,26},{10... | collective-permute-start | bytes 49160 | tf_op jit(solution)/shard_map/ppermute | solution.py:377
  148.4 19.3 %collective-permute-start.22 = (f32[16,256]{1,0:T(8,128)S(1)}, f32[16,256]{1,0:T(8,128)S(1)}, u32[]{:S(2)}, u32[]{:S(2)}) collective-permute-start(f32[16,256]{1,0:T(8,128)S(1)} %tie.8), channel_id=1, source_target_pairs={{0,16},{8,24},{16,0},{24,8},{1,17},{9,25},{17,1},{25,9},{2,18},{10... | collective-permute-start | bytes 49160 | tf_op jit(solution)/shard_map/ppermute | solution.py:377
  148.9 18.7 %collective-permute-start.21 = (f32[16,256]{1,0:T(8,128)S(1)}, f32[16,256]{1,0:T(8,128)S(1)}, u32[]{:S(2)}, u32[]{:S(2)}) collective-permute-start(f32[16,256]{1,0:T(8,128)S(1)} %tie.8), channel_id=1, source_target_pairs={{0,8},{8,0},{16,24},{24,16},{1,9},{9,1},{17,25},{25,17},{2,10},{10... | collective-permute-start | bytes 49160 | tf_op jit(solution)/shard_map/ppermute | solution.py:377

commit v9 on v8

--- a/solution.py
+++ b/solution.py
@@ -23,25 +23,13 @@
     return pltpu.with_memory_space_constraint(value, pltpu.HBM)
 
 
-def row_sums(values):
-    folded = values[:, :128]
-    for c in range(1, values.shape[1] // 128):
-        folded = folded + values[:, c * 128 : (c + 1) * 128]
-    ones = jnp.ones((128, 128), jnp.bfloat16)
-    high = folded.astype(jnp.bfloat16)
-    low = (folded - high.astype(jnp.float32)).astype(jnp.bfloat16)
-    total = jnp.dot(high, ones, preferred_element_type=jnp.float32)
-    return total + jnp.dot(low, ones, preferred_element_type=jnp.float32)
-
-
-def scale_rows(values, factor):
-    parts = [values[:, c : c + 128] * factor for c in range(0, values.shape[1], 128)]
-    return jnp.concatenate(parts, axis=1)
-
-
 def unit_rows(wide):
-    inv = lax.rsqrt(row_sums(wide * wide) + 1e-06)
-    return scale_rows(wide, inv), inv
+    inv = lax.rsqrt(jnp.sum(wide * wide, axis=1, keepdims=True) + 1e-06)
+    return wide * inv, inv
+
+
+def off_axis(values, unit):
+    return values - unit * jnp.sum(unit * values, axis=1, keepdims=True)
 
 
 def column_of(row):
@@ -50,7 +38,8 @@
 
 
 def forward_kernel(
-    base_ref, rep_ref, lab_ref, w_ref, mixed_ref, emb_ref, a_ref, b_ref, st_ref, xhat_ref, sum_ref,
+    base_ref, rep_ref, lab_ref, w_ref, mixed_ref, emb_ref, a_ref, b_ref, st_ref, what_ref, xhat_ref,
+    sum_ref,
     *, classes, reps,
 ):
     step = pl.program_id(0)
@@ -71,10 +60,11 @@
 
     wwide, _ = unit_rows(w_ref[...].astype(jnp.float32))
     what = wwide.astype(jnp.bfloat16)
+    what_ref[...] = what
     cosine = lax.dot_general(xhat_ref[...], what, NT, preferred_element_type=jnp.float32)
     ids = lax.broadcasted_iota(jnp.int32, (batch, tile), 1)
     is_label = ids == lab_ref[...] - (base_ref[0] + step * tile)
-    e = jnp.where(is_label, 0.0, jnp.exp2(cosine * (SCALE * LOG2E) - SCALE * LOG2E))
+    e = jnp.where(is_label, 0.0, jnp.exp2(cosine * (SCALE * LOG2E)))
     partial = e[:, :128]
     for c in range(1, tile // 128):
         partial = partial + e[:, c * 128 : (c + 1) * 128]
@@ -95,14 +85,14 @@
         margined = c * math.cos(MARGIN) - sine * math.sin(MARGIN)
         slope = math.cos(MARGIN) + jnp.where(q > SIN_FLOOR, c * math.sin(MARGIN) / sine, 0.0)
         slope = slope * has
-        label_e = jnp.exp(SCALE * margined - SCALE) * has
+        label_e = jnp.exp(SCALE * margined) * has
         total = jnp.sum(sum_ref[...], axis=1, keepdims=True) + label_e
         target = SCALE * margined * has
         b = slope * label_row
         a = a_ref[...] + label_e * b
         gain = SCALE * x_inv
-        a_ref[...] = scale_rows(a - scale_rows(xwide, row_sums(xwide * a)), gain)
-        b_ref[...] = scale_rows(b - scale_rows(xwide, row_sums(xwide * b)), gain)
+        a_ref[...] = off_axis(a, xwide) * gain
+        b_ref[...] = off_axis(b, xwide) * gain
         lane = lax.broadcasted_iota(jnp.int32, (batch, 128), 1)
         stats = jnp.where(lane == 0, total, 0.0)
         stats = jnp.where(lane == 1, target, stats)
@@ -132,12 +122,14 @@
             pl.BlockSpec((batch, width), whole),
             pl.BlockSpec((batch, width), whole),
             pl.BlockSpec((8, batch), whole),
+            pl.BlockSpec((tile, width), lambda i: (i, 0)),
         ],
         out_shape=[
             jax.ShapeDtypeStruct((batch, width), jnp.bfloat16),
             jax.ShapeDtypeStruct((batch, width), jnp.float32),
             jax.ShapeDtypeStruct((batch, width), jnp.float32),
             jax.ShapeDtypeStruct((8, batch), jnp.float32),
+            pltpu.HBM((classes, width), jnp.bfloat16),
         ],
         scratch_shapes=[pltpu.VMEM((batch, width), jnp.bfloat16), pltpu.VMEM((batch, 128), jnp.float32)],
         compiler_params=pltpu.CompilerParams(
@@ -169,10 +161,10 @@
     cosine = lax.dot_general(what, xhat_ref[...], NT, preferred_element_type=jnp.float32)
     ids = lax.broadcasted_iota(jnp.int32, (tile, batch), 0)
     is_label = ids == lab_ref[...] - (base_ref[0] + step * tile)
-    e = jnp.exp2(cosine * (SCALE * LOG2E) - SCALE * LOG2E)
+    e = jnp.exp2(cosine * (SCALE * LOG2E))
     d = jnp.where(is_label, v_ref[...], e).astype(jnp.bfloat16)
     raw = jnp.dot(d, y_ref[...], preferred_element_type=jnp.float32)
-    g_ref[...] = scale_rows(raw - scale_rows(wwide, row_sums(wwide * raw)), w_inv)
+    g_ref[...] = off_axis(raw, wwide) * w_inv
 
 
 def weight_gradient(base, emb, labels, stats, totals, weights):
@@ -210,10 +202,21 @@
 
 def fetch_kernel(rows_ref, *refs, first):
     out_ref, sem = refs[-2:]
-    size = out_ref.shape[1]
-    copy = pltpu.make_async_copy(rows_ref.at[:, pl.ds(first, size), :], out_ref, sem)
-    copy.start()
-    copy.wait()
+    peers, size, _ = out_ref.shape
+    lanes = sem.shape[0]
+    part = peers // lanes
+    copies = [
+        pltpu.make_async_copy(
+            rows_ref.at[pl.ds(c * part, part), pl.ds(first, size), :],
+            out_ref.at[pl.ds(c * part, part)],
+            sem.at[c],
+        )
+        for c in range(lanes)
+    ]
+    for copy in copies:
+        copy.start()
+    for copy in copies:
+        copy.wait()
 
 
 def fetch(runs, first, size, tokens):
@@ -225,7 +228,7 @@
         in_specs=[hbm] + [anywhere] * len(tokens),
         out_specs=pl.BlockSpec(memory_space=pltpu.VMEM),
         out_shape=jax.ShapeDtypeStruct((peers, size, width), runs.dtype),
-        scratch_shapes=[pltpu.SemaphoreType.DMA],
+        scratch_shapes=[pltpu.SemaphoreType.DMA((math.gcd(peers, 8),))],
         compiler_params=pltpu.CompilerParams(vmem_limit_bytes=6 * MIB),
         cost_estimate=COST,
         name="fetch",
@@ -250,7 +253,7 @@
     )(value, *tokens)
 
 
-def place_runs(me_ref, slot_ref, row_ref, held_ref, stage_ref, held_copy, peers, run, first):
+def place_runs(me_ref, slot_ref, row_ref, held_ref, stage_ref, copies, peers, run, first):
     size = row_ref.shape[0] // peers
     batch = math.gcd(size, 32)
 
@@ -263,8 +266,8 @@
         return carry
 
     lax.fori_loop(0, peers, prepare, 0)
-    if held_copy is not None:
-        held_copy.wait()
+    for copy in copies:
+        copy.wait()
 
     def place(source, carry):
         start = (me_ref[0] ^ source) * run + first
@@ -280,31 +283,26 @@
 
 
 def place_kernel(
-    me_ref, slot_ref, row_ref, _, out_ref, token_ref, held_ref, stage_ref, sem, *, peers, run, first
+    me_ref, slot_ref, row_ref, _, held_ref, token_ref, stage_ref, *, peers, run, first
 ):
     token_ref[...] = jnp.zeros_like(token_ref)
-    place_runs(me_ref, slot_ref, row_ref, held_ref, stage_ref, None, peers, run, first)
-    store = pltpu.make_async_copy(held_ref, out_ref, sem)
-    store.start()
-    store.wait()
+    place_runs(me_ref, slot_ref, row_ref, held_ref, stage_ref, [], peers, run, first)
 
 
 def place_rows(me, slots, rows, after, peers, run, first):
     smem = pl.BlockSpec(memory_space=pltpu.SMEM)
     vmem = pl.BlockSpec(memory_space=pltpu.VMEM)
     anywhere = pl.BlockSpec(memory_space=pl.ANY)
-    held = (2 * peers * run, 128)
     return pl.pallas_call(
         functools.partial(place_kernel, peers=peers, run=run, first=first),
         in_specs=[smem, smem, vmem, anywhere],
-        out_specs=[anywhere, vmem],
-        out_shape=[pltpu.HBM(held, jnp.float32), jax.ShapeDtypeStruct((8, 128), jnp.float32)],
-        scratch_shapes=[
-            pltpu.VMEM(held, jnp.float32),
-            pltpu.VMEM((2 * rows.shape[0], 128), jnp.float32),
-            pltpu.SemaphoreType.DMA,
-        ],
-        compiler_params=pltpu.CompilerParams(vmem_limit_bytes=32 * MIB),
+        out_specs=[vmem, vmem],
+        out_shape=[
+            jax.ShapeDtypeStruct((2 * peers * run, 128), jnp.float32),
+            jax.ShapeDtypeStruct((8, 128), jnp.float32),
+        ],
+        scratch_shapes=[pltpu.VMEM((2 * rows.shape[0], 128), jnp.float32)],
+        compiler_params=pltpu.CompilerParams(vmem_limit_bytes=24 * MIB),
         cost_estimate=pl.CostEstimate(
             flops=0, bytes_accessed=16 * rows.shape[0] * rows.shape[1], transcendentals=0
         ),
@@ -320,15 +318,22 @@
 
     @pl.when(step == 0)
     def _():
-        load = pltpu.make_async_copy(in_ref, held_ref, sem)
-        load.start()
-        place_runs(me_ref, slot_ref, row_ref, held_ref, stage_ref, load, peers, run, first)
-
-    wwide, _ = unit_rows(w_ref[...].astype(jnp.float32))
+        lanes = sem.shape[0]
+        part = held_ref.shape[0] // lanes
+        parts = [pl.ds(c * part, part) for c in range(lanes)]
+        copies = [
+            pltpu.make_async_copy(in_ref.at[at, :], held_ref.at[at, :], sem.at[c])
+            for c, at in enumerate(parts)
+        ]
+        for copy in copies:
+            copy.start()
+        place_runs(me_ref, slot_ref, row_ref, held_ref, stage_ref, copies, peers, run, first)
+
+    wwide = w_ref[...].astype(jnp.float32)
     at = pl.multiple_of(step * 2 * tile, 2 * tile)
     low = wwide[:, :128] + held_ref[pl.ds(at, tile, stride=2), :]
     high = wwide[:, 128:] + held_ref[pl.ds(at + 1, tile, stride=2), :]
-    inv = lax.rsqrt(row_sums(low * low + high * high) + 1e-06)
+    inv = lax.rsqrt(jnp.sum(low * low + high * high, axis=1, keepdims=True) + 1e-06)
     o_ref[:, :128] = (low * inv).astype(jnp.bfloat16)
     o_ref[:, 128:] = (high * inv).astype(jnp.bfloat16)
 
@@ -348,7 +353,7 @@
         scratch_shapes=[
             pltpu.VMEM(held.shape, jnp.float32),
             pltpu.VMEM((2 * rows.shape[0], 128), jnp.float32),
-            pltpu.SemaphoreType.DMA,
+            pltpu.SemaphoreType.DMA((4,)),
         ],
         compiler_params=pltpu.CompilerParams(
             dimension_semantics=("arbitrary",), vmem_limit_bytes=32 * MIB
@@ -385,9 +390,10 @@
     weights = in_hbm(class_weights)
     runs = in_hbm(centroids.reshape(peers, run, width))
     cut = run * 5 // 8 // 16 * 16
-    mixed = jnp.concatenate([swap(embeddings, "rep", k) for k in range(reps)])
+    mixed = jnp.concatenate([swap(embeddings, "rep", c) for c in range(2)])
+    mixed = jnp.concatenate([swap(mixed, "rep", 2 * z) for z in range(reps // 2)])
     rows_a = relay(released(fetch(runs, 0, cut, []), [mixed]))
-    emb, a, b, stats = forward(base, rep.reshape(1), mixed, reps, labels, weights)
+    emb, a, b, stats, what = forward(base, rep.reshape(1), mixed, reps, labels, weights)
 
     half = reps // 2
     core, deep = rep % 2, rep // 2
@@ -414,7 +420,7 @@
     sums, slots = share_out(sums, wanted, "rep", range(0, reps, 2))
     slots = slots.reshape(-1).astype(jnp.int32) * 2
     total, target = sums[:batch], sums[batch:]
-    losses = SCALE + jnp.log(total) - target
+    losses = jnp.log(total) - target
     loss = lax.dynamic_slice_in_dim(losses, rep * rows_local, rows_local, 0)
 
     rows_b = relay(released(sent_b, [total]))
@@ -426,12 +432,12 @@
     grad = sum(swap(index(grad, grp ^ j, 2, False), "grp", j) for j in range(groups))
     grad = tie(grad, [done])
     grad = sum(swap(index(grad, core ^ c, 1, False), "rep", c) for c in range(2))
+    grad = tie(grad, [token])
     own = sum(swap(index(grad, deep ^ z, 0, False), "rep", 2 * z) for z in range(half))
-    own = tie(own, [token])
     shares = jnp.stack([swap(own, "grp", j) for j in range(groups)])
     embedding_gradient = shares[grp ^ jnp.arange(groups)].reshape(rows_local, width)
 
-    refreshed = place_and_blend(me, slots, rows_b, in_hbm(held), weights, peers, run, cut)
+    refreshed = place_and_blend(me, slots, rows_b, in_hbm(held), in_hbm(what), peers, run, cut)
     return (loss, embedding_gradient, weight_grad, refreshed)
 
 

time: 170 us -> 155 us (0.912)
  Pallas kernels: 67.5 us -> 54 us
  waiting for transfers between devices: 51.1 us -> 47.8 us
  local copies, waits for them, and re-layouts: 9.67 us -> 12.9 us
  starting transfers between devices: 38 us -> 36.2 us
    pallas_call x1, Pallas kernels: 14 us -> 8.74 us  [place_rows(): pl.pallas_call(functools.partial(place_kernel, peers=peers, run=run, firs...]
    pallas_call x1, Pallas kernels: 17.6 us -> 14.2 us  [place_and_blend(): pl.pallas_call(functools.partial(blend_kernel, peers=peers, run=run, firs...]
    ppermute x24 -> x21, waiting for transfers between devices: 51.1 us -> 47.8 us  [swap(): lax.ppermute(value, axis, [(i, i ^ k) for i in range(size)])]
    unnamed x24 -> x20, local copies, waits for them, and re-layouts: 4.18 us -> 7.44 us
    pallas_call x1, Pallas kernels: 14.7 us -> 11.7 us  [weight_gradient(): pl.pallas_call(weight_kernel, grid=(classes // tile,), in_specs=[pl.Block...]
    ppermute x24 -> x21, starting transfers between devices: 29.4 us -> 27.3 us  [swap(): lax.ppermute(value, axis, [(i, i ^ k) for i in range(size)])]
    pallas_call x1, Pallas kernels: 15.3 us -> 13.5 us  [forward(): pl.pallas_call(functools.partial(forward_kernel, classes=classes, reps=re...]
  transfers between devices with their start and end apart: 26 -> 23, of which waited for: 12 -> 14; matrix products, arithmetic and copies ran while one was open for 4% -> 4% of each run, Pallas kernels for 40% -> 35%
where the time goes in v9:
time: 155 us; the launch traced here: 154 us
  Pallas kernels  54 us (35%)
  waiting for transfers between devices  47.8 us (31%)
  starting transfers between devices  36.2 us (23%)
  local copies, waits for them, and re-layouts  12.9 us (8%)
    ppermute x21, waiting for transfers between devices, swap(): lax.ppermute(value, axis, [(i, i ^ k) for i in range(size)])  47.8 us
    ppermute x21, starting transfers between devices, swap(): lax.ppermute(value, axis, [(i, i ^ k) for i in range(size)])  27.3 us
    pallas_call x1, Pallas kernels, place_and_blend(): pl.pallas_call(functools.partial(blend_kernel, peers=peers, run=run, firs...  14.2 us
    pallas_call x1, Pallas kernels, forward(): pl.pallas_call(functools.partial(forward_kernel, classes=classes, reps=re...  13.5 us
    pallas_call x1, Pallas kernels, weight_gradient(): pl.pallas_call(weight_kernel, grid=(classes // tile,), in_specs=[pl.Block...  11.7 us
    all_to_all x2, starting transfers between devices, relay(): return lax.all_to_all(sent, ALL, 0, 0, tiled=True).reshape(-1, width)  8.98 us
    pallas_call x1, Pallas kernels, place_rows(): pl.pallas_call(functools.partial(place_kernel, peers=peers, run=run, firs...  8.74 us
    unnamed x20, local copies, waits for them, and re-layouts  7.44 us
  transfers between devices with their start and end apart: 23, of which 14 were waited for; matrix products, arithmetic and copies ran while one was open for 4% of the time, Pallas kernels for 35%

profile of v9, /device:TPU:0, one launch (start us, length us, event | category | flops | bytes accessed | tf_op | source)
XLA Modules:
  0.0 153.6 jit_solution(5419368084060553640)
XLA Ops:
  0.6 0.5 collective-permute-start
  1.1 0.8 constant_dynamic-update-slice_fusion.1
  1.9 0.3 collective-permute-done
  2.2 2.9 %collective-permute-start.1 = (bf16[128,256]{1,0:T(8,128)(2,1)S(1)}, bf16[128,256]{1,0:T(8,128)(2,1)S(1)}, u32[]{:S(2)}, u32[]{:S(2)}) collective-permute-start(bf16[128,256]{1,0:T(8,128)(2,1)S(1)} %get-tuple-element.34), channel_id=1, source_target_pairs={{0,2},{1,3},{2,0},{3,1},{4,6},{5,7},{6,4},{7,5},{8,10},{9,11},{10,... | collective-permute-start | bytes 196616 | tf_op jit(solution)/shard_map/ppermute | solution.py:382
  5.1 3.2 %fetch.3 = bf16[32,160,256]{2,1,0:T(8,128)(2,1)} custom-call(bf16[32,256,256]{2,1,0:T(8,128)(2,1)} %bitcast.102), custom_call_target="tpu_custom_call" | custom-call | flops 1 | bytes 1 | tf_op jit(solution)/shard_map/fetch/pallas_call | solution.py:226
  8.4 0.7 slice.46.value_ref
  9.1 2.6 %collective-permute-start.2 = (bf16[128,256]{1,0:T(8,128)(2,1)S(1)}, bf16[128,256]{1,0:T(8,128)(2,1)S(1)}, u32[]{:S(2)}, u32[]{:S(2)}) collective-permute-start(bf16[128,256]{1,0:T(8,128)(2,1)S(1)} %get-tuple-element.34), channel_id=1, source_target_pairs={{0,4},{1,5},{2,6},{3,7},{4,0},{5,1},{6,2},{7,3},{8,12},{9,13},{10,... | collective-permute-start | bytes 196616 | tf_op jit(solution)/shard_map/ppermute | solution.py:382
  11.7 0.0 collective-permute-start.3
  11.7 0.0 collective-permute-done.1
  11.7 3.5 %collective-permute-done.2 = bf16[128,256]{1,0:T(8,128)(2,1)S(1)} collective-permute-done((bf16[128,256]{1,0:T(8,128)(2,1)S(1)}, bf16[128,256]{1,0:T(8,128)(2,1)S(1)}, u32[]{:S(2)}, u32[]{:S(2)}) %collective-permute-start.2) | collective-permute-done | bytes 65568 | tf_op jit(solution)/shard_map/ppermute | solution.py:382
  15.2 2.6 %collective-permute-done.3 = bf16[128,256]{1,0:T(8,128)(2,1)S(1)} collective-permute-done((bf16[128,256]{1,0:T(8,128)(2,1)S(1)}, bf16[128,256]{1,0:T(8,128)(2,1)S(1)}, u32[]{:S(2)}, u32[]{:S(2)}) %collective-permute-start.3) | collective-permute-done | bytes 65568 | tf_op jit(solution)/shard_map/ppermute | solution.py:382
  17.8 0.6 constant_dynamic-update-slice_fusion.8
  18.5 4.3 %all-to-all-start = ((bf16[32,160,256]{2,1,0:T(8,128)(2,1)}), bf16[32,160,256]{2,1,0:T(8,128)(2,1)S(1)}, u32[]{:S(2)}, u32[]{:S(2)}) async-start(bf16[32,160,256]{2,1,0:T(8,128)(2,1)} %constant_dynamic-update-slice_fusion.8), calls=%async_computation | async-start | bytes 5242880 | tf_op jit(solution)/shard_map/all_to_all | solution.py:388
  22.8 0.9 copy.18.lab_ref
  23.7 0.0 copy-start.2
  23.7 0.9 copy-done.2
  24.7 13.5 %forward_sums.1 = (bf16[512,256]{1,0:T(8,128)(2,1)S(1)}, f32[512,256]{1,0:T(8,128)S(1)}, f32[512,256]{1,0:T(8,128)S(1)}, f32[8,512]{1,0:T(8,128)S(1)}, bf16[8192,256]{1,0:T(8,128)(2,1)}) custom-call(s32[1]{0:T(128)S(6)} %mul.18.base_ref, s32[1]{0:T(128)} %bitcast.1.rep_ref, s32[512,1]{1,0:T(8,128)S(1)} %copy-done.2, bf16[8192,256]{1,0:T(8,128)(2,1)} %w_ref.3, ...), custom_call_target="tpu_custom_call" | custom-call | flops 12884901888 | bytes 4194304 | tf_op jit(solution)/shard_map/forward_sums/pallas_call | solution.py:110
  38.2 0.8 copy-done.1
  39.0 0.7 copy-done.4
  39.7 2.7 %collective-permute-start.6 = (f32[24,128]{1,0:T(8,128)S(1)}, f32[24,128]{1,0:T(8,128)S(1)}, u32[]{:S(2)}, u32[]{:S(2)}) collective-permute-start(f32[24,128]{1,0:T(8,128)S(1)} %get-tuple-element.49), channel_id=1, source_target_pairs={{0,24},{8,16},{16,8},{24,0},{1,25},{9,17},{17,9},{25,1},{2,26},{10... | collective-permute-start | bytes 36872 | tf_op jit(solution)/shard_map/ppermute | solution.py:382
  42.4 0.6 collective-permute-start.5
  43.0 0.3 collective-permute-start.4
  43.2 1.2 collective-permute-done.6
  44.4 2.2 %collective-permute-done.5 = f32[24,128]{1,0:T(8,128)S(1)} collective-permute-done((f32[24,128]{1,0:T(8,128)S(1)}, f32[24,128]{1,0:T(8,128)S(1)}, u32[]{:S(2)}, u32[]{:S(2)}) %collective-permute-start.5) | collective-permute-done | bytes 12320 | tf_op jit(solution)/shard_map/ppermute | solution.py:382
  46.6 0.2 collective-permute-done.4
  46.9 0.1 collective-permute-start.7
  47.1 2.7 %fetch.2.refs_0_ = bf16[32,96,256]{2,1,0:T(8,128)(2,1)} custom-call(bf16[32,256,256]{2,1,0:T(8,128)(2,1)} %bitcast.103, f32[8,512]{1,0:T(8,128)S(1)} %get-tuple-element.11.refs_0_.st_ref), custom_call_target="tpu_custom_call" | custom-call | flops 1 | bytes 1 | tf_op jit(solution)/shard_map/fetch/pallas_call | solution.py:226
  49.8 0.0 collective-permute-done.7
  50.0 3.4 %collective-permute-start.10 = (f32[24,128]{1,0:T(8,128)S(1)}, f32[24,128]{1,0:T(8,128)S(1)}, u32[]{:S(2)}, u32[]{:S(2)}) collective-permute-start(f32[24,128]{1,0:T(8,128)S(1)} %get-tuple-element.43), channel_id=1, source_target_pairs={{0,6},{1,7},{2,4},{3,5},{4,2},{5,3},{6,0},{7,1},{8,14},{9,15},{10,... | collective-permute-start | bytes 36872 | tf_op jit(solution)/shard_map/ppermute | solution.py:382
  53.4 0.0 collective-permute-start.9
  53.4 1.0 collective-permute-start.8
  54.4 0.7 slice.47.value_ref
  55.1 15.0 %collective-permute-done.10 = f32[24,128]{1,0:T(8,128)S(1)} collective-permute-done((f32[24,128]{1,0:T(8,128)S(1)}, f32[24,128]{1,0:T(8,128)S(1)}, u32[]{:S(2)}, u32[]{:S(2)}) %collective-permute-start.10) | collective-permute-done | bytes 12320 | tf_op jit(solution)/shard_map/ppermute | solution.py:382
  70.1 13.6 %collective-permute-done.9 = f32[24,128]{1,0:T(8,128)S(1)} collective-permute-done((f32[24,128]{1,0:T(8,128)S(1)}, f32[24,128]{1,0:T(8,128)S(1)}, u32[]{:S(2)}, u32[]{:S(2)}) %collective-permute-start.9) | collective-permute-done | bytes 12320 | tf_op jit(solution)/shard_map/ppermute | solution.py:382
  83.8 0.6 constant_dynamic-update-slice_fusion.7
  84.4 4.7 %all-to-all-start.1 = ((bf16[32,96,256]{2,1,0:T(8,128)(2,1)}), bf16[32,96,256]{2,1,0:T(8,128)(2,1)}, u32[]{:S(2)}, u32[]{:S(2)}) async-start(bf16[32,96,256]{2,1,0:T(8,128)(2,1)} %constant_dynamic-update-slice_fusion.7), calls=%async_computation.1 | async-start | bytes 3145728 | tf_op jit(solution)/shard_map/all_to_all | solution.py:388
  89.1 1.2 divide_subtract_fusion
  90.3 2.7 %collective-permute-start.13 = (f32[4,2,16,256]{3,2,1,0:T(8,128)S(1)}, f32[4,2,16,256]{3,2,1,0:T(8,128)S(1)}, u32[]{:S(2)}, u32[]{:S(2)}) collective-permute-start(f32[4,2,16,256]{3,2,1,0:T(8,128)S(1)} %get-tuple-element.20), channel_id=1, source_target_pairs={{0,24},{8,16},{16,8},{24,0},{1,25},{9,17},{17,9},{25,1},{2,26},{10... | collective-permute-start | bytes 393224 | tf_op jit(solution)/shard_map/ppermute | solution.py:382
  93.0 0.6 collective-permute-start.12
  93.6 0.3 collective-permute-start.11
  93.9 0.9 copy-done.5
  94.8 11.7 %weight_gradient.1.refs_0_._ = f32[8192,256]{1,0:T(8,128)} custom-call(s32[1]{0:T(128)S(6)} %mul.18.base_ref, bf16[512,256]{1,0:T(8,128)(2,1)S(1)} %copy-done.5, s32[1,512]{1,0:T(1,128)S(1)} %bitcast.101, f32[8,512]{1,0:T(8,128)S(1)} %get-tuple-element.11.refs_0_.st_ref, f32[1,512]{1,0:T(1,128)S(1)} %bitcast.97, bf16[8192,256]{1,0:T(8,128)(2,1)} %w_ref.3), custom_call_target="tpu_custom_call" | custom-call | flops 12884901888 | bytes 12582912 | tf_op jit(solution)/shard_map/weight_gradient/pallas_call | solution.py:175
  106.5 0.5 collective-permute-done.13
  107.1 3.1 %collective-permute-done.12 = f32[4,2,16,256]{3,2,1,0:T(8,128)S(1)} collective-permute-done((f32[4,2,16,256]{3,2,1,0:T(8,128)S(1)}, f32[4,2,16,256]{3,2,1,0:T(8,128)S(1)}, u32[]{:S(2)}, u32[]{:S(2)}) %collective-permute-start.12) | collective-permute-done | bytes 131104 | tf_op jit(solution)/shard_map/ppermute | solution.py:382
  110.1 0.4 collective-permute-done.11
  110.6 0.1 collective-permute-start.14
  110.8 1.2 collective-permute-done.14
  112.0 8.7 %place_rows.1 = (f32[16384,128]{1,0:T(8,128)S(1)}, f32[8,128]{1,0:T(8,128)S(1)}) custom-call(s32[1]{0:T(128)} %bitcast.me_ref, s32[8192]{0:T(1024)S(1)} %bitcast.95, bf16[5120,256]{1,0:T(8,128)(2,1)S(1)} %bitcast.94, f32[8192,256]{1,0:T(8,128)} %weight_gradient.1.refs_0_._), custom_call_target="tpu_custom_call" | custom-call | bytes 20971520 | tf_op jit(solution)/shard_map/place_rows/pallas_call | solution.py:296
  120.7 3.3 %copy-done = f32[16384,128]{1,0:T(8,128)} copy-done((f32[16384,128]{1,0:T(8,128)}, f32[16384,128]{1,0:T(8,128)S(1)}, u32[]{:S(2)}) %copy-start) | copy-done | bytes 8388632
  124.0 5.3 %collective-permute-start.17 = (f32[16,256]{1,0:T(8,128)S(1)}, f32[16,256]{1,0:T(8,128)S(1)}, u32[]{:S(2)}, u32[]{:S(2)}) collective-permute-start(f32[16,256]{1,0:T(8,128)S(1)} %get-tuple-element.22), channel_id=1, source_target_pairs={{0,6},{1,7},{2,4},{3,5},{4,2},{5,3},{6,0},{7,1},{8,14},{9,15},{10,... | collective-permute-start | bytes 49160 | tf_op jit(solution)/shard_map/ppermute | solution.py:382
  129.4 0.0 collective-permute-start.16
  129.4 0.6 collective-permute-start.15
  130.0 1.1 collective-permute-done.17
  131.1 2.9 %collective-permute-done.16 = f32[16,256]{1,0:T(8,128)S(1)} collective-permute-done((f32[16,256]{1,0:T(8,128)S(1)}, f32[16,256]{1,0:T(8,128)S(1)}, u32[]{:S(2)}, u32[]{:S(2)}) %collective-permute-start.16) | collective-permute-done | bytes 16416 | tf_op jit(solution)/shard_map/ppermute | solution.py:382
  134.0 0.0 collective-permute-done.15
  134.0 1.8 %collective-permute-start.20 = (f32[16,256]{1,0:T(8,128)S(1)}, f32[16,256]{1,0:T(8,128)S(1)}, u32[]{:S(2)}, u32[]{:S(2)}) collective-permute-start(f32[16,256]{1,0:T(8,128)S(1)} %fusion.7), channel_id=1, source_target_pairs={{0,24},{8,16},{16,8},{24,0},{1,25},{9,17},{17,9},{25,1},{2,26},{10... | collective-permute-start | bytes 49160 | tf_op jit(solution)/shard_map/ppermute | solution.py:382
  135.8 0.5 collective-permute-start.19
  136.4 1.2 collective-permute-start.18
  137.6 0.6 dynamic_slice.79
  138.2 0.0 all-to-all-done.1
  138.2 14.2 %place_and_blend.1 = bf16[8192,256]{1,0:T(8,128)(2,1)} custom-call(s32[1]{0:T(128)} %bitcast.me_ref, s32[8192]{0:T(1024)S(1)} %bitcast.96, bf16[8192,256]{1,0:T(8,128)(2,1)} %get-tuple-element.16.w_ref, bf16[3072,256]{1,0:T(8,128)(2,1)} %bitcast.53.row_ref, f32[16384,128]{1,0:T(8,128)} %copy-done), custom_call_target="tpu_custom_call" | custom-call | bytes 25165824 | tf_op jit(solution)/shard_map/place_and_blend/pallas_call | solution.py:347
  152.3 0.0 collective-permute-done.19
  152.4 0.0 collective-permute-done.18
  152.4 1.2 gather_fusion
  (49 shorter events, 0.6 us)
Async XLA Ops:
  0.6 1.6 %collective-permute-start = (bf16[64,256]{1,0:T(8,128)(2,1)}, bf16[64,256]{1,0:T(8,128)(2,1)S(1)}, u32[]{:S(2)}, u32[]{:S(2)}) collective-permute-start(bf16[64,256]{1,0:T(8,128)(2,1)} %param.5), channel_id=1, source_target_pairs={{0,1},{1,0},{2,3},{3,2},{4,5},{5,4},{6,7},{7,6},{8,9},{9,8},{10,11... | collective-permute-start | bytes 98312 | tf_op jit(solution)/shard_map/ppermute | solution.py:382
  2.2 9.4 %collective-permute-start.1 = (bf16[128,256]{1,0:T(8,128)(2,1)S(1)}, bf16[128,256]{1,0:T(8,128)(2,1)S(1)}, u32[]{:S(2)}, u32[]{:S(2)}) collective-permute-start(bf16[128,256]{1,0:T(8,128)(2,1)S(1)} %get-tuple-element.34), channel_id=1, source_target_pairs={{0,2},{1,3},{2,0},{3,1},{4,6},{5,7},{6,4},{7,5},{8,10},{9,11},{10,... | collective-permute-start | bytes 196616 | tf_op jit(solution)/shard_map/ppermute | solution.py:382
  9.1 6.1 %collective-permute-start.2 = (bf16[128,256]{1,0:T(8,128)(2,1)S(1)}, bf16[128,256]{1,0:T(8,128)(2,1)S(1)}, u32[]{:S(2)}, u32[]{:S(2)}) collective-permute-start(bf16[128,256]{1,0:T(8,128)(2,1)S(1)} %get-tuple-element.34), channel_id=1, source_target_pairs={{0,4},{1,5},{2,6},{3,7},{4,0},{5,1},{6,2},{7,3},{8,12},{9,13},{10,... | collective-permute-start | bytes 196616 | tf_op jit(solution)/shard_map/ppermute | solution.py:382
  11.7 6.2 %collective-permute-start.3 = (bf16[128,256]{1,0:T(8,128)(2,1)S(1)}, bf16[128,256]{1,0:T(8,128)(2,1)S(1)}, u32[]{:S(2)}, u32[]{:S(2)}) collective-permute-start(bf16[128,256]{1,0:T(8,128)(2,1)S(1)} %get-tuple-element.34), channel_id=1, source_target_pairs={{0,6},{1,7},{2,4},{3,5},{4,2},{5,3},{6,0},{7,1},{8,14},{9,15},{10,... | collective-permute-start | bytes 196616 | tf_op jit(solution)/shard_map/ppermute | solution.py:382
  18.4 4.3 %copy-start.3 = (s32[512]{0:T(512)S(1)}, s32[512]{0:T(512)}, u32[]{:S(2)}) copy-start(s32[512]{0:T(512)} %param.6) | copy-start | bytes 6148
  18.5 5.2 %copy-start.6 = (s32[8192]{0:T(1024)S(1)}, s32[8192]{0:T(1024)}, u32[]{:S(2)}) copy-start(s32[8192]{0:T(1024)} %param.9) | copy-start | bytes 98308
  18.5 66.0 %all-to-all-start = ((bf16[32,160,256]{2,1,0:T(8,128)(2,1)}), bf16[32,160,256]{2,1,0:T(8,128)(2,1)S(1)}, u32[]{:S(2)}, u32[]{:S(2)}) async-start(bf16[32,160,256]{2,1,0:T(8,128)(2,1)} %constant_dynamic-update-slice_fusion.8), calls=%async_computation | async-start | bytes 5242880 | tf_op jit(solution)/shard_map/all_to_all | solution.py:388
  23.7 1.0 copy-start.2
  38.2 0.8 copy-start.1
  39.0 0.7 copy-start.4
  39.7 4.7 %collective-permute-start.6 = (f32[24,128]{1,0:T(8,128)S(1)}, f32[24,128]{1,0:T(8,128)S(1)}, u32[]{:S(2)}, u32[]{:S(2)}) collective-permute-start(f32[24,128]{1,0:T(8,128)S(1)} %get-tuple-element.49), channel_id=1, source_target_pairs={{0,24},{8,16},{16,8},{24,0},{1,25},{9,17},{17,9},{25,1},{2,26},{10... | collective-permute-start | bytes 36872 | tf_op jit(solution)/shard_map/ppermute | solution.py:382
  42.4 4.2 %collective-permute-start.5 = (f32[24,128]{1,0:T(8,128)S(1)}, f32[24,128]{1,0:T(8,128)S(1)}, u32[]{:S(2)}, u32[]{:S(2)}) collective-permute-start(f32[24,128]{1,0:T(8,128)S(1)} %get-tuple-element.48), channel_id=1, source_target_pairs={{0,16},{8,24},{16,0},{24,8},{1,17},{9,25},{17,1},{25,9},{2,18},{10... | collective-permute-start | bytes 36872 | tf_op jit(solution)/shard_map/ppermute | solution.py:382
  43.0 3.8 %collective-permute-start.4 = (f32[24,128]{1,0:T(8,128)S(1)}, f32[24,128]{1,0:T(8,128)S(1)}, u32[]{:S(2)}, u32[]{:S(2)}) collective-permute-start(f32[24,128]{1,0:T(8,128)S(1)} %get-tuple-element.47), channel_id=1, source_target_pairs={{0,8},{8,0},{16,24},{24,16},{1,9},{9,1},{17,25},{25,17},{2,10},{10... | collective-permute-start | bytes 36872 | tf_op jit(solution)/shard_map/ppermute | solution.py:382
  46.9 2.8 %collective-permute-start.7 = (f32[40,128]{1,0:T(8,128)S(1)}, f32[40,128]{1,0:T(8,128)S(1)}, u32[]{:S(2)}, u32[]{:S(2)}) collective-permute-start(f32[40,128]{1,0:T(8,128)S(1)} %get-tuple-element.45), channel_id=1, source_target_pairs={{0,1},{1,0},{2,3},{3,2},{4,5},{5,4},{6,7},{7,6},{8,9},{9,8},{10,11... | collective-permute-start | bytes 61448 | tf_op jit(solution)/shard_map/ppermute | solution.py:382
  50.0 20.2 %collective-permute-start.10 = (f32[24,128]{1,0:T(8,128)S(1)}, f32[24,128]{1,0:T(8,128)S(1)}, u32[]{:S(2)}, u32[]{:S(2)}) collective-permute-start(f32[24,128]{1,0:T(8,128)S(1)} %get-tuple-element.43), channel_id=1, source_target_pairs={{0,6},{1,7},{2,4},{3,5},{4,2},{5,3},{6,0},{7,1},{8,14},{9,15},{10,... | collective-permute-start | bytes 36872 | tf_op jit(solution)/shard_map/ppermute | solution.py:382
  53.4 30.3 %collective-permute-start.9 = (f32[24,128]{1,0:T(8,128)S(1)}, f32[24,128]{1,0:T(8,128)S(1)}, u32[]{:S(2)}, u32[]{:S(2)}) collective-permute-start(f32[24,128]{1,0:T(8,128)S(1)} %get-tuple-element.42), channel_id=1, source_target_pairs={{0,4},{1,5},{2,6},{3,7},{4,0},{5,1},{6,2},{7,3},{8,12},{9,13},{10,... | collective-permute-start | bytes 36872 | tf_op jit(solution)/shard_map/ppermute | solution.py:382
  53.4 30.3 %collective-permute-start.8 = (f32[24,128]{1,0:T(8,128)S(1)}, f32[24,128]{1,0:T(8,128)S(1)}, u32[]{:S(2)}, u32[]{:S(2)}) collective-permute-start(f32[24,128]{1,0:T(8,128)S(1)} %get-tuple-element.41), channel_id=1, source_target_pairs={{0,2},{1,3},{2,0},{3,1},{4,6},{5,7},{6,4},{7,5},{8,10},{9,11},{10,... | collective-permute-start | bytes 36872 | tf_op jit(solution)/shard_map/ppermute | solution.py:382
  84.4 53.8 %all-to-all-start.1 = ((bf16[32,96,256]{2,1,0:T(8,128)(2,1)}), bf16[32,96,256]{2,1,0:T(8,128)(2,1)}, u32[]{:S(2)}, u32[]{:S(2)}) async-start(bf16[32,96,256]{2,1,0:T(8,128)(2,1)} %constant_dynamic-update-slice_fusion.7), calls=%async_computation.1 | async-start | bytes 3145728 | tf_op jit(solution)/shard_map/all_to_all | solution.py:388
  90.3 16.7 %collective-permute-start.13 = (f32[4,2,16,256]{3,2,1,0:T(8,128)S(1)}, f32[4,2,16,256]{3,2,1,0:T(8,128)S(1)}, u32[]{:S(2)}, u32[]{:S(2)}) collective-permute-start(f32[4,2,16,256]{3,2,1,0:T(8,128)S(1)} %get-tuple-element.20), channel_id=1, source_target_pairs={{0,24},{8,16},{16,8},{24,0},{1,25},{9,17},{17,9},{25,1},{2,26},{10... | collective-permute-start | bytes 393224 | tf_op jit(solution)/shard_map/ppermute | solution.py:382
  93.0 17.1 %collective-permute-start.12 = (f32[4,2,16,256]{3,2,1,0:T(8,128)S(1)}, f32[4,2,16,256]{3,2,1,0:T(8,128)S(1)}, u32[]{:S(2)}, u32[]{:S(2)}) collective-permute-start(f32[4,2,16,256]{3,2,1,0:T(8,128)S(1)} %get-tuple-element.19), channel_id=1, source_target_pairs={{0,16},{8,24},{16,0},{24,8},{1,17},{9,25},{17,1},{25,9},{2,18},{10... | collective-permute-start | bytes 393224 | tf_op jit(solution)/shard_map/ppermute | solution.py:382
  93.6 17.0 %collective-permute-start.11 = (f32[4,2,16,256]{3,2,1,0:T(8,128)S(1)}, f32[4,2,16,256]{3,2,1,0:T(8,128)S(1)}, u32[]{:S(2)}, u32[]{:S(2)}) collective-permute-start(f32[4,2,16,256]{3,2,1,0:T(8,128)S(1)} %get-tuple-element.18), channel_id=1, source_target_pairs={{0,8},{8,0},{16,24},{24,16},{1,9},{9,1},{17,25},{25,17},{2,10},{10... | collective-permute-start | bytes 393224 | tf_op jit(solution)/shard_map/ppermute | solution.py:382
  93.9 0.9 copy-start.5
  110.6 1.3 collective-permute-start.14
  120.7 3.3 %copy-start = (f32[16384,128]{1,0:T(8,128)}, f32[16384,128]{1,0:T(8,128)S(1)}, u32[]{:S(2)}) copy-start(f32[16384,128]{1,0:T(8,128)S(1)} %get-tuple-element.17.in_ref) | copy-start | bytes 25165828
  124.0 7.1 %collective-permute-start.17 = (f32[16,256]{1,0:T(8,128)S(1)}, f32[16,256]{1,0:T(8,128)S(1)}, u32[]{:S(2)}, u32[]{:S(2)}) collective-permute-start(f32[16,256]{1,0:T(8,128)S(1)} %get-tuple-element.22), channel_id=1, source_target_pairs={{0,6},{1,7},{2,4},{3,5},{4,2},{5,3},{6,0},{7,1},{8,14},{9,15},{10,... | collective-permute-start | bytes 49160 | tf_op jit(solution)/shard_map/ppermute | solution.py:382
  129.4 4.6 %collective-permute-start.16 = (f32[16,256]{1,0:T(8,128)S(1)}, f32[16,256]{1,0:T(8,128)S(1)}, u32[]{:S(2)}, u32[]{:S(2)}) collective-permute-start(f32[16,256]{1,0:T(8,128)S(1)} %get-tuple-element.23), channel_id=1, source_target_pairs={{0,4},{1,5},{2,6},{3,7},{4,0},{5,1},{6,2},{7,3},{8,12},{9,13},{10,... | collective-permute-start | bytes 49160 | tf_op jit(solution)/shard_map/ppermute | solution.py:382
  129.4 4.6 %collective-permute-start.15 = (f32[16,256]{1,0:T(8,128)S(1)}, f32[16,256]{1,0:T(8,128)S(1)}, u32[]{:S(2)}, u32[]{:S(2)}) collective-permute-start(f32[16,256]{1,0:T(8,128)S(1)} %get-tuple-element.21), channel_id=1, source_target_pairs={{0,2},{1,3},{2,0},{3,1},{4,6},{5,7},{6,4},{7,5},{8,10},{9,11},{10,... | collective-permute-start | bytes 49160 | tf_op jit(solution)/shard_map/ppermute | solution.py:382
  134.0 18.3 %collective-permute-start.20 = (f32[16,256]{1,0:T(8,128)S(1)}, f32[16,256]{1,0:T(8,128)S(1)}, u32[]{:S(2)}, u32[]{:S(2)}) collective-permute-start(f32[16,256]{1,0:T(8,128)S(1)} %fusion.7), channel_id=1, source_target_pairs={{0,24},{8,16},{16,8},{24,0},{1,25},{9,17},{17,9},{25,1},{2,26},{10... | collective-permute-start | bytes 49160 | tf_op jit(solution)/shard_map/ppermute | solution.py:382
  135.8 16.5 %collective-permute-start.19 = (f32[16,256]{1,0:T(8,128)S(1)}, f32[16,256]{1,0:T(8,128)S(1)}, u32[]{:S(2)}, u32[]{:S(2)}) collective-permute-start(f32[16,256]{1,0:T(8,128)S(1)} %fusion.7), channel_id=1, source_target_pairs={{0,16},{8,24},{16,0},{24,8},{1,17},{9,25},{17,1},{25,9},{2,18},{10... | collective-permute-start | bytes 49160 | tf_op jit(solution)/shard_map/ppermute | solution.py:382
  136.4 16.0 %collective-permute-start.18 = (f32[16,256]{1,0:T(8,128)S(1)}, f32[16,256]{1,0:T(8,128)S(1)}, u32[]{:S(2)}, u32[]{:S(2)}) collective-permute-start(f32[16,256]{1,0:T(8,128)S(1)} %fusion.7), channel_id=1, source_target_pairs={{0,8},{8,0},{16,24},{24,16},{1,9},{9,1},{17,25},{25,17},{2,10},{10... | collective-permute-start | bytes 49160 | tf_op jit(solution)/shard_map/ppermute | solution.py:382

commit v10 on v9

--- a/solution.py
+++ b/solution.py
@@ -156,15 +156,18 @@
         y_ref[...] = (xhat.astype(jnp.float32) * column_of(SCALE / total)).astype(jnp.bfloat16)
         v_ref[...] = st_ref[2:3, :] - st_ref[3:4, :] * total
 
-    wwide, w_inv = unit_rows(w_ref[...].astype(jnp.float32))
-    what = wwide.astype(jnp.bfloat16)
-    cosine = lax.dot_general(what, xhat_ref[...], NT, preferred_element_type=jnp.float32)
-    ids = lax.broadcasted_iota(jnp.int32, (tile, batch), 0)
-    is_label = ids == lab_ref[...] - (base_ref[0] + step * tile)
-    e = jnp.exp2(cosine * (SCALE * LOG2E))
-    d = jnp.where(is_label, v_ref[...], e).astype(jnp.bfloat16)
-    raw = jnp.dot(d, y_ref[...], preferred_element_type=jnp.float32)
-    g_ref[...] = off_axis(raw, wwide) * w_inv
+    block = math.gcd(tile, 256)
+    for first in range(0, tile, block):
+        at = pl.ds(first, block)
+        wwide, w_inv = unit_rows(w_ref[at, :].astype(jnp.float32))
+        what = wwide.astype(jnp.bfloat16)
+        cosine = lax.dot_general(what, xhat_ref[...], NT, preferred_element_type=jnp.float32)
+        ids = lax.broadcasted_iota(jnp.int32, (block, batch), 0)
+        is_label = ids == lab_ref[...] - (base_ref[0] + step * tile + first)
+        e = jnp.exp2(cosine * (SCALE * LOG2E))
+        d = jnp.where(is_label, v_ref[...], e).astype(jnp.bfloat16)
+        raw = jnp.dot(d, y_ref[...], preferred_element_type=jnp.float32)
+        g_ref[at, :] = off_axis(raw, wwide) * w_inv
 
 
 def weight_gradient(base, emb, labels, stats, totals, weights):
@@ -230,7 +233,9 @@
         out_shape=jax.ShapeDtypeStruct((peers, size, width), runs.dtype),
         scratch_shapes=[pltpu.SemaphoreType.DMA((math.gcd(peers, 8),))],
         compiler_params=pltpu.CompilerParams(vmem_limit_bytes=6 * MIB),
-        cost_estimate=COST,
+        cost_estimate=pl.CostEstimate(
+            flops=0, bytes_accessed=8 * peers * size * width, transcendentals=0
+        ),
         name="fetch",
     )(runs, *tokens)
 
@@ -255,14 +260,15 @@
 
 def place_runs(me_ref, slot_ref, row_ref, held_ref, stage_ref, copies, peers, run, first):
     size = row_ref.shape[0] // peers
-    batch = math.gcd(size, 32)
+    batch = max(n for n in range(1, 49) if size % n == 0)
+    chunk = max(n for n in range(16, 49, 16) if size % n == 0)
 
     def prepare(source, carry):
-        at = pl.multiple_of(source * size, size)
-        unit, _ = unit_rows(row_ref[pl.ds(at, size), :].astype(jnp.float32))
-        at = pl.multiple_of(source * 2 * size, 2 * size)
-        stage_ref[pl.ds(at, size, stride=2), :] = unit[:, :128]
-        stage_ref[pl.ds(at + 1, size, stride=2), :] = unit[:, 128:]
+        for block in range(0, size, chunk):
+            at = pl.multiple_of(source * size + block, chunk)
+            unit, _ = unit_rows(row_ref[pl.ds(at, chunk), :].astype(jnp.float32))
+            stage_ref[pl.ds(2 * at, chunk, stride=2), :] = unit[:, :128]
+            stage_ref[pl.ds(2 * at + 1, chunk, stride=2), :] = unit[:, 128:]
         return carry
 
     lax.fori_loop(0, peers, prepare, 0)
@@ -329,13 +335,15 @@
             copy.start()
         place_runs(me_ref, slot_ref, row_ref, held_ref, stage_ref, copies, peers, run, first)
 
-    wwide = w_ref[...].astype(jnp.float32)
-    at = pl.multiple_of(step * 2 * tile, 2 * tile)
-    low = wwide[:, :128] + held_ref[pl.ds(at, tile, stride=2), :]
-    high = wwide[:, 128:] + held_ref[pl.ds(at + 1, tile, stride=2), :]
-    inv = lax.rsqrt(jnp.sum(low * low + high * high, axis=1, keepdims=True) + 1e-06)
-    o_ref[:, :128] = (low * inv).astype(jnp.bfloat16)
-    o_ref[:, 128:] = (high * inv).astype(jnp.bfloat16)
+    block = math.gcd(tile, 64)
+    for begin in range(0, tile, block):
+        rows = pl.ds(begin, block)
+        at = pl.multiple_of((step * tile + begin) * 2, 2 * block)
+        low = w_ref[rows, :128].astype(jnp.float32) + held_ref[pl.ds(at, block, stride=2), :]
+        high = w_ref[rows, 128:].astype(jnp.float32) + held_ref[pl.ds(at + 1, block, stride=2), :]
+        inv = lax.rsqrt(jnp.sum(low * low + high * high, axis=1, keepdims=True) + 1e-06)
+        o_ref[rows, :128] = (low * inv).astype(jnp.bfloat16)
+        o_ref[rows, 128:] = (high * inv).astype(jnp.bfloat16)
 
 
 def place_and_blend(me, slots, rows, held, weights, peers, run, first):
@@ -389,7 +397,7 @@
 
     weights = in_hbm(class_weights)
     runs = in_hbm(centroids.reshape(peers, run, width))
-    cut = run * 5 // 8 // 16 * 16
+    cut = run * 9 // 16 // 16 * 16
     mixed = jnp.concatenate([swap(embeddings, "rep", c) for c in range(2)])
     mixed = jnp.concatenate([swap(mixed, "rep", 2 * z) for z in range(reps // 2)])
     rows_a = relay(released(fetch(runs, 0, cut, []), [mixed]))
@@ -432,10 +440,15 @@
     grad = sum(swap(index(grad, grp ^ j, 2, False), "grp", j) for j in range(groups))
     grad = tie(grad, [done])
     grad = sum(swap(index(grad, core ^ c, 1, False), "rep", c) for c in range(2))
-    grad = tie(grad, [token])
+    grad = tie(grad, [token, loss])
     own = sum(swap(index(grad, deep ^ z, 0, False), "rep", 2 * z) for z in range(half))
-    shares = jnp.stack([swap(own, "grp", j) for j in range(groups)])
-    embedding_gradient = shares[grp ^ jnp.arange(groups)].reshape(rows_local, width)
+    shares = [swap(own, "grp", j) for j in range(groups)]
+    bit = 1
+    while bit < groups:
+        flip = (grp & bit) != 0
+        shares = [jnp.where(flip, shares[j ^ bit], shares[j]) for j in range(groups)]
+        bit *= 2
+    embedding_gradient = jnp.concatenate(shares)
 
     refreshed = place_and_blend(me, slots, rows_b, in_hbm(held), in_hbm(what), peers, run, cut)
     return (loss, embedding_gradient, weight_grad, refreshed)

time: 155 us -> 151 us (0.974)
  waiting for transfers between devices: 47.8 us -> 45 us
  local copies, waits for them, and re-layouts: 12.9 us -> 11.2 us
    ppermute x21, waiting for transfers between devices: 47.8 us -> 44.9 us  [swap(): lax.ppermute(value, axis, [(i, i ^ k) for i in range(size)])]
    unnamed x20 -> x24, local copies, waits for them, and re-layouts: 7.44 us -> 7.36 us
  transfers between devices with their start and end apart: 23 -> 23, of which waited for: 14 -> 14; matrix products, arithmetic and copies ran while one was open for 4% -> 3% of each run, Pallas kernels for 35% -> 36%
where the time goes in v10:
time: 151 us; the launch traced here: 150 us
  Pallas kernels  54.3 us (36%)
  waiting for transfers between devices  45 us (30%)
  starting transfers between devices  36.8 us (24%)
  local copies, waits for them, and re-layouts  11.2 us (7%)
  other arithmetic  1.68 us (1%)
    ppermute x21, waiting for transfers between devices, swap(): lax.ppermute(value, axis, [(i, i ^ k) for i in range(size)])  44.9 us
    ppermute x21, starting transfers between devices, swap(): lax.ppermute(value, axis, [(i, i ^ k) for i in range(size)])  28 us
    pallas_call x1, Pallas kernels, place_and_blend(): pl.pallas_call(functools.partial(blend_kernel, peers=peers, run=run, firs...  14.7 us
    pallas_call x1, Pallas kernels, forward(): pl.pallas_call(functools.partial(forward_kernel, classes=classes, reps=re...  13.6 us
    pallas_call x1, Pallas kernels, weight_gradient(): pl.pallas_call(weight_kernel, grid=(classes // tile,), in_specs=[pl.Block...  11.8 us
    all_to_all x2, starting transfers between devices, relay(): return lax.all_to_all(sent, ALL, 0, 0, tiled=True).reshape(-1, width)  8.86 us
    pallas_call x1, Pallas kernels, place_rows(): pl.pallas_call(functools.partial(place_kernel, peers=peers, run=run, firs...  8.28 us
    unnamed x24, local copies, waits for them, and re-layouts  7.36 us
  transfers between devices with their start and end apart: 23, of which 14 were waited for; matrix products, arithmetic and copies ran while one was open for 3% of the time, Pallas kernels for 36%

profile of v10, /device:TPU:0, one launch (start us, length us, event | category | flops | bytes accessed | tf_op | source)
XLA Modules:
  0.0 150.1 jit_solution(10072011519324393288)
XLA Ops:
  0.6 0.5 collective-permute-start
  1.1 0.8 constant_dynamic-update-slice_fusion.1
  1.9 0.3 collective-permute-done
  2.2 2.9 %collective-permute-start.1 = (bf16[128,256]{1,0:T(8,128)(2,1)S(1)}, bf16[128,256]{1,0:T(8,128)(2,1)S(1)}, u32[]{:S(2)}, u32[]{:S(2)}) collective-permute-start(bf16[128,256]{1,0:T(8,128)(2,1)S(1)} %get-tuple-element.38), channel_id=1, source_target_pairs={{0,2},{1,3},{2,0},{3,1},{4,6},{5,7},{6,4},{7,5},{8,10},{9,11},{10,... | collective-permute-start | bytes 196616 | tf_op jit(solution)/shard_map/ppermute | solution.py:390
  5.1 3.1 %fetch.3 = bf16[32,144,256]{2,1,0:T(8,128)(2,1)} custom-call(bf16[32,256,256]{2,1,0:T(8,128)(2,1)} %bitcast.95), custom_call_target="tpu_custom_call" | custom-call | bytes 9437184 | tf_op jit(solution)/shard_map/fetch/pallas_call | solution.py:229
  8.2 0.7 slice.44.value_ref
  8.9 2.6 %collective-permute-start.2 = (bf16[128,256]{1,0:T(8,128)(2,1)S(1)}, bf16[128,256]{1,0:T(8,128)(2,1)S(1)}, u32[]{:S(2)}, u32[]{:S(2)}) collective-permute-start(bf16[128,256]{1,0:T(8,128)(2,1)S(1)} %get-tuple-element.38), channel_id=1, source_target_pairs={{0,4},{1,5},{2,6},{3,7},{4,0},{5,1},{6,2},{7,3},{8,12},{9,13},{10,... | collective-permute-start | bytes 196616 | tf_op jit(solution)/shard_map/ppermute | solution.py:390
  11.5 0.0 collective-permute-start.3
  11.5 0.0 collective-permute-done.1
  11.5 3.5 %collective-permute-done.2 = bf16[128,256]{1,0:T(8,128)(2,1)S(1)} collective-permute-done((bf16[128,256]{1,0:T(8,128)(2,1)S(1)}, bf16[128,256]{1,0:T(8,128)(2,1)S(1)}, u32[]{:S(2)}, u32[]{:S(2)}) %collective-permute-start.2) | collective-permute-done | bytes 65568 | tf_op jit(solution)/shard_map/ppermute | solution.py:390
  15.0 2.6 %collective-permute-done.3 = bf16[128,256]{1,0:T(8,128)(2,1)S(1)} collective-permute-done((bf16[128,256]{1,0:T(8,128)(2,1)S(1)}, bf16[128,256]{1,0:T(8,128)(2,1)S(1)}, u32[]{:S(2)}, u32[]{:S(2)}) %collective-permute-start.3) | collective-permute-done | bytes 65568 | tf_op jit(solution)/shard_map/ppermute | solution.py:390
  17.7 0.7 copy-done.1
  18.4 0.6 constant_dynamic-update-slice_fusion.8
  19.0 4.3 %all-to-all-start = ((bf16[32,144,256]{2,1,0:T(8,128)(2,1)}), bf16[32,144,256]{2,1,0:T(8,128)(2,1)S(1)}, u32[]{:S(2)}, u32[]{:S(2)}) async-start(bf16[32,144,256]{2,1,0:T(8,128)(2,1)} %constant_dynamic-update-slice_fusion.8), calls=%async_computation | async-start | bytes 4718592 | tf_op jit(solution)/shard_map/all_to_all | solution.py:396
  23.3 0.9 copy.18.lab_ref
  24.3 0.9 copy-done.2
  25.2 0.9 copy-done.3
  26.2 13.6 %forward_sums.1 = (bf16[512,256]{1,0:T(8,128)(2,1)S(1)}, f32[512,256]{1,0:T(8,128)S(1)}, f32[512,256]{1,0:T(8,128)S(1)}, f32[8,512]{1,0:T(8,128)S(1)}, bf16[8192,256]{1,0:T(8,128)(2,1)}) custom-call(s32[1]{0:T(128)S(6)} %mul.18.base_ref, s32[1]{0:T(128)} %bitcast.1.rep_ref, s32[512,1]{1,0:T(8,128)S(1)} %copy-done.3, bf16[8192,256]{1,0:T(8,128)(2,1)} %w_ref.3, ...), custom_call_target="tpu_custom_call" | custom-call | flops 12884901888 | bytes 4194304 | tf_op jit(solution)/shard_map/forward_sums/pallas_call | solution.py:110
  39.8 0.7 copy-done.6
  40.5 0.6 pad_maximum_fusion.13
  41.1 2.7 %collective-permute-start.6 = (f32[24,128]{1,0:T(8,128)}, f32[24,128]{1,0:T(8,128)S(1)}, u32[]{:S(2)}, u32[]{:S(2)}) collective-permute-start(f32[24,128]{1,0:T(8,128)} %get-tuple-element.53), channel_id=1, source_target_pairs={{0,24},{8,16},{16,8},{24,0},{1,25},{9,17},{17,9},{25,1},{2,26},{10... | collective-permute-start | bytes 36872 | tf_op jit(solution)/shard_map/ppermute | solution.py:390
  43.8 0.6 collective-permute-start.5
  44.3 0.3 collective-permute-start.4
  44.6 1.4 collective-permute-done.6
  46.0 1.5 collective-permute-done.5
  47.5 0.6 collective-permute-done.4
  48.3 0.1 collective-permute-start.7
  48.4 2.9 %fetch.2.refs_0_ = bf16[32,112,256]{2,1,0:T(8,128)(2,1)} custom-call(bf16[32,256,256]{2,1,0:T(8,128)(2,1)} %bitcast.96, f32[8,512]{1,0:T(8,128)S(1)} %get-tuple-element.11.refs_0_.st_ref), custom_call_target="tpu_custom_call" | custom-call | bytes 7340032 | tf_op jit(solution)/shard_map/fetch/pallas_call | solution.py:229
  51.3 0.0 collective-permute-done.7
  51.5 3.9 %collective-permute-start.10 = (f32[24,128]{1,0:T(8,128)S(1)}, f32[24,128]{1,0:T(8,128)S(1)}, u32[]{:S(2)}, u32[]{:S(2)}) collective-permute-start(f32[24,128]{1,0:T(8,128)S(1)} %get-tuple-element.47), channel_id=1, source_target_pairs={{0,6},{1,7},{2,4},{3,5},{4,2},{5,3},{6,0},{7,1},{8,14},{9,15},{10,... | collective-permute-start | bytes 36872 | tf_op jit(solution)/shard_map/ppermute | solution.py:390
  55.4 0.0 collective-permute-start.9
  55.4 0.6 collective-permute-start.8
  56.1 0.7 slice.45.value_ref
  56.8 9.7 %collective-permute-done.10 = f32[24,128]{1,0:T(8,128)S(1)} collective-permute-done((f32[24,128]{1,0:T(8,128)S(1)}, f32[24,128]{1,0:T(8,128)S(1)}, u32[]{:S(2)}, u32[]{:S(2)}) %collective-permute-start.10) | collective-permute-done | bytes 12320 | tf_op jit(solution)/shard_map/ppermute | solution.py:390
  66.5 12.2 %collective-permute-done.9 = f32[24,128]{1,0:T(8,128)S(1)} collective-permute-done((f32[24,128]{1,0:T(8,128)S(1)}, f32[24,128]{1,0:T(8,128)S(1)}, u32[]{:S(2)}, u32[]{:S(2)}) %collective-permute-start.9) | collective-permute-done | bytes 12320 | tf_op jit(solution)/shard_map/ppermute | solution.py:390
  78.6 0.0 collective-permute-done.8
  78.7 0.6 constant_dynamic-update-slice_fusion.7
  79.3 4.6 %all-to-all-start.1 = ((bf16[32,112,256]{2,1,0:T(8,128)(2,1)}), bf16[32,112,256]{2,1,0:T(8,128)(2,1)}, u32[]{:S(2)}, u32[]{:S(2)}) async-start(bf16[32,112,256]{2,1,0:T(8,128)(2,1)} %constant_dynamic-update-slice_fusion.7), calls=%async_computation.1 | async-start | bytes 3670016 | tf_op jit(solution)/shard_map/all_to_all | solution.py:396
  83.9 0.0 copy-start.7
  83.9 0.1 divide_subtract_fusion
  84.1 2.7 %collective-permute-start.13 = (f32[4,2,16,256]{3,2,1,0:T(8,128)S(1)}, f32[4,2,16,256]{3,2,1,0:T(8,128)S(1)}, u32[]{:S(2)}, u32[]{:S(2)}) collective-permute-start(f32[4,2,16,256]{3,2,1,0:T(8,128)S(1)} %get-tuple-element.20), channel_id=1, source_target_pairs={{0,24},{8,16},{16,8},{24,0},{1,25},{9,17},{17,9},{25,1},{2,26},{10... | collective-permute-start | bytes 393224 | tf_op jit(solution)/shard_map/ppermute | solution.py:390
  86.8 0.6 collective-permute-start.12
  87.3 0.3 collective-permute-start.11
  87.7 11.8 %weight_gradient.1.refs_0_._ = f32[8192,256]{1,0:T(8,128)} custom-call(s32[1]{0:T(128)S(6)} %mul.18.base_ref, bf16[512,256]{1,0:T(8,128)(2,1)S(1)} %copy-done.7, s32[1,512]{1,0:T(1,128)S(1)} %bitcast.94, f32[8,512]{1,0:T(8,128)S(1)} %get-tuple-element.11.refs_0_.st_ref, f32[1,512]{1,0:T(1,128)S(1)} %bitcast.90, bf16[8192,256]{1,0:T(8,128)(2,1)} %w_ref.3), custom_call_target="tpu_custom_call" | custom-call | flops 12884901888 | bytes 12582912 | tf_op jit(solution)/shard_map/weight_gradient/pallas_call | solution.py:178
  99.5 3.6 %collective-permute-done.13 = f32[4,2,16,256]{3,2,1,0:T(8,128)S(1)} collective-permute-done((f32[4,2,16,256]{3,2,1,0:T(8,128)S(1)}, f32[4,2,16,256]{3,2,1,0:T(8,128)S(1)}, u32[]{:S(2)}, u32[]{:S(2)}) %collective-permute-start.13) | collective-permute-done | bytes 131104 | tf_op jit(solution)/shard_map/ppermute | solution.py:390
  103.1 1.4 collective-permute-done.12
  104.6 2.9 %collective-permute-done.11 = f32[4,2,16,256]{3,2,1,0:T(8,128)S(1)} collective-permute-done((f32[4,2,16,256]{3,2,1,0:T(8,128)S(1)}, f32[4,2,16,256]{3,2,1,0:T(8,128)S(1)}, u32[]{:S(2)}, u32[]{:S(2)}) %collective-permute-start.11) | collective-permute-done | bytes 131104 | tf_op jit(solution)/shard_map/ppermute | solution.py:390
  107.5 0.1 collective-permute-start.14
  107.7 0.1 dynamic_slice.79.refs_1_
  107.8 1.1 collective-permute-done.14
  108.9 8.3 %place_rows.1 = (f32[16384,128]{1,0:T(8,128)S(1)}, f32[8,128]{1,0:T(8,128)S(1)}) custom-call(s32[1]{0:T(128)} %bitcast.me_ref, s32[8192]{0:T(1024)S(1)} %bitcast.88, bf16[4608,256]{1,0:T(8,128)(2,1)S(1)} %bitcast.87, f32[8192,256]{1,0:T(8,128)} %weight_gradient.1.refs_0_._), custom_call_target="tpu_custom_call" | custom-call | bytes 18874368 | tf_op jit(solution)/shard_map/place_rows/pallas_call | solution.py:302
  117.2 3.3 %copy-done = f32[16384,128]{1,0:T(8,128)} copy-done((f32[16384,128]{1,0:T(8,128)}, f32[16384,128]{1,0:T(8,128)S(1)}, u32[]{:S(2)}) %copy-start) | copy-done | bytes 8388632
  120.5 6.0 %collective-permute-start.17 = (f32[16,256]{1,0:T(8,128)S(1)}, f32[16,256]{1,0:T(8,128)S(1)}, u32[]{:S(2)}, u32[]{:S(2)}) collective-permute-start(f32[16,256]{1,0:T(8,128)S(1)} %get-tuple-element.26), channel_id=1, source_target_pairs={{0,6},{1,7},{2,4},{3,5},{4,2},{5,3},{6,0},{7,1},{8,14},{9,15},{10,... | collective-permute-start | bytes 49160 | tf_op jit(solution)/shard_map/ppermute | solution.py:390
  126.5 0.0 collective-permute-start.16
  126.5 0.6 collective-permute-start.15
  127.1 1.1 collective-permute-done.17
  128.2 2.9 %collective-permute-done.16 = f32[16,256]{1,0:T(8,128)S(1)} collective-permute-done((f32[16,256]{1,0:T(8,128)S(1)}, f32[16,256]{1,0:T(8,128)S(1)}, u32[]{:S(2)}, u32[]{:S(2)}) %collective-permute-start.16) | collective-permute-done | bytes 16416 | tf_op jit(solution)/shard_map/ppermute | solution.py:390
  131.1 0.0 collective-permute-done.15
  131.1 1.8 %collective-permute-start.18 = (f32[16,256]{1,0:T(8,128)S(1)}, f32[16,256]{1,0:T(8,128)S(1)}, u32[]{:S(2)}, u32[]{:S(2)}) collective-permute-start(f32[16,256]{1,0:T(8,128)S(1)} %fusion.7), channel_id=1, source_target_pairs={{0,24},{8,16},{16,8},{24,0},{1,25},{9,17},{17,9},{25,1},{2,26},{10... | collective-permute-start | bytes 49160 | tf_op jit(solution)/shard_map/ppermute | solution.py:390
  133.0 1.7 %collective-permute-start.20 = (f32[16,256]{1,0:T(8,128)S(1)}, f32[16,256]{1,0:T(8,128)S(1)}, u32[]{:S(2)}, u32[]{:S(2)}) collective-permute-start(f32[16,256]{1,0:T(8,128)S(1)} %fusion.7), channel_id=1, source_target_pairs={{0,8},{8,0},{16,24},{24,16},{1,9},{9,1},{17,25},{25,17},{2,10},{10... | collective-permute-start | bytes 49160 | tf_op jit(solution)/shard_map/ppermute | solution.py:390
  134.7 14.7 %place_and_blend.1 = bf16[8192,256]{1,0:T(8,128)(2,1)} custom-call(s32[1]{0:T(128)} %bitcast.me_ref, s32[8192]{0:T(1024)S(1)} %bitcast.89, bf16[8192,256]{1,0:T(8,128)(2,1)} %get-tuple-element.16.w_ref, bf16[3584,256]{1,0:T(8,128)(2,1)} %bitcast.47.row_ref, f32[16384,128]{1,0:T(8,128)} %copy-done), custom_call_target="tpu_custom_call" | custom-call | bytes 25165824 | tf_op jit(solution)/shard_map/place_and_blend/pallas_call | solution.py:355
  149.4 0.0 collective-permute-done.18
  149.4 0.0 collective-permute-done.19
  149.4 0.6 pad_maximum_fusion
  (51 shorter events, 0.7 us)
Async XLA Ops:
  0.6 1.6 %collective-permute-start = (bf16[64,256]{1,0:T(8,128)(2,1)}, bf16[64,256]{1,0:T(8,128)(2,1)S(1)}, u32[]{:S(2)}, u32[]{:S(2)}) collective-permute-start(bf16[64,256]{1,0:T(8,128)(2,1)} %param.5), channel_id=1, source_target_pairs={{0,1},{1,0},{2,3},{3,2},{4,5},{5,4},{6,7},{7,6},{8,9},{9,8},{10,11... | collective-permute-start | bytes 98312 | tf_op jit(solution)/shard_map/ppermute | solution.py:390
  2.2 9.3 %collective-permute-start.1 = (bf16[128,256]{1,0:T(8,128)(2,1)S(1)}, bf16[128,256]{1,0:T(8,128)(2,1)S(1)}, u32[]{:S(2)}, u32[]{:S(2)}) collective-permute-start(bf16[128,256]{1,0:T(8,128)(2,1)S(1)} %get-tuple-element.38), channel_id=1, source_target_pairs={{0,2},{1,3},{2,0},{3,1},{4,6},{5,7},{6,4},{7,5},{8,10},{9,11},{10,... | collective-permute-start | bytes 196616 | tf_op jit(solution)/shard_map/ppermute | solution.py:390
  8.9 6.1 %collective-permute-start.2 = (bf16[128,256]{1,0:T(8,128)(2,1)S(1)}, bf16[128,256]{1,0:T(8,128)(2,1)S(1)}, u32[]{:S(2)}, u32[]{:S(2)}) collective-permute-start(bf16[128,256]{1,0:T(8,128)(2,1)S(1)} %get-tuple-element.38), channel_id=1, source_target_pairs={{0,4},{1,5},{2,6},{3,7},{4,0},{5,1},{6,2},{7,3},{8,12},{9,13},{10,... | collective-permute-start | bytes 196616 | tf_op jit(solution)/shard_map/ppermute | solution.py:390
  11.5 6.2 %collective-permute-start.3 = (bf16[128,256]{1,0:T(8,128)(2,1)S(1)}, bf16[128,256]{1,0:T(8,128)(2,1)S(1)}, u32[]{:S(2)}, u32[]{:S(2)}) collective-permute-start(bf16[128,256]{1,0:T(8,128)(2,1)S(1)} %get-tuple-element.38), channel_id=1, source_target_pairs={{0,6},{1,7},{2,4},{3,5},{4,2},{5,3},{6,0},{7,1},{8,14},{9,15},{10,... | collective-permute-start | bytes 196616 | tf_op jit(solution)/shard_map/ppermute | solution.py:390
  17.7 0.7 copy-start.1
  19.0 4.3 %copy-start.4 = (s32[512]{0:T(512)S(1)}, s32[512]{0:T(512)}, u32[]{:S(2)}) copy-start(s32[512]{0:T(512)} %param.6) | copy-start | bytes 6148
  19.0 5.2 %copy-start.8 = (s32[8192]{0:T(1024)S(1)}, s32[8192]{0:T(1024)}, u32[]{:S(2)}) copy-start(s32[8192]{0:T(1024)} %param.9) | copy-start | bytes 98308
  19.0 60.3 %all-to-all-start = ((bf16[32,144,256]{2,1,0:T(8,128)(2,1)}), bf16[32,144,256]{2,1,0:T(8,128)(2,1)S(1)}, u32[]{:S(2)}, u32[]{:S(2)}) async-start(bf16[32,144,256]{2,1,0:T(8,128)(2,1)} %constant_dynamic-update-slice_fusion.8), calls=%async_computation | async-start | bytes 4718592 | tf_op jit(solution)/shard_map/all_to_all | solution.py:396
  24.3 1.0 copy-start.2
  25.2 0.9 copy-start.3
  39.8 0.7 copy-start.6
  41.1 4.9 %collective-permute-start.6 = (f32[24,128]{1,0:T(8,128)}, f32[24,128]{1,0:T(8,128)S(1)}, u32[]{:S(2)}, u32[]{:S(2)}) collective-permute-start(f32[24,128]{1,0:T(8,128)} %get-tuple-element.53), channel_id=1, source_target_pairs={{0,24},{8,16},{16,8},{24,0},{1,25},{9,17},{17,9},{25,1},{2,26},{10... | collective-permute-start | bytes 36872 | tf_op jit(solution)/shard_map/ppermute | solution.py:390
  43.8 3.7 %collective-permute-start.5 = (f32[24,128]{1,0:T(8,128)S(1)}, f32[24,128]{1,0:T(8,128)S(1)}, u32[]{:S(2)}, u32[]{:S(2)}) collective-permute-start(f32[24,128]{1,0:T(8,128)S(1)} %get-tuple-element.52), channel_id=1, source_target_pairs={{0,16},{8,24},{16,0},{24,8},{1,17},{9,25},{17,1},{25,9},{2,18},{10... | collective-permute-start | bytes 36872 | tf_op jit(solution)/shard_map/ppermute | solution.py:390
  44.3 3.8 %collective-permute-start.4 = (f32[24,128]{1,0:T(8,128)S(1)}, f32[24,128]{1,0:T(8,128)S(1)}, u32[]{:S(2)}, u32[]{:S(2)}) collective-permute-start(f32[24,128]{1,0:T(8,128)S(1)} %get-tuple-element.51), channel_id=1, source_target_pairs={{0,8},{8,0},{16,24},{24,16},{1,9},{9,1},{17,25},{25,17},{2,10},{10... | collective-permute-start | bytes 36872 | tf_op jit(solution)/shard_map/ppermute | solution.py:390
  48.3 3.0 %collective-permute-start.7 = (f32[40,128]{1,0:T(8,128)S(1)}, f32[40,128]{1,0:T(8,128)S(1)}, u32[]{:S(2)}, u32[]{:S(2)}) collective-permute-start(f32[40,128]{1,0:T(8,128)S(1)} %get-tuple-element.49), channel_id=1, source_target_pairs={{0,1},{1,0},{2,3},{3,2},{4,5},{5,4},{6,7},{7,6},{8,9},{9,8},{10,11... | collective-permute-start | bytes 61448 | tf_op jit(solution)/shard_map/ppermute | solution.py:390
  51.5 14.9 %collective-permute-start.10 = (f32[24,128]{1,0:T(8,128)S(1)}, f32[24,128]{1,0:T(8,128)S(1)}, u32[]{:S(2)}, u32[]{:S(2)}) collective-permute-start(f32[24,128]{1,0:T(8,128)S(1)} %get-tuple-element.47), channel_id=1, source_target_pairs={{0,6},{1,7},{2,4},{3,5},{4,2},{5,3},{6,0},{7,1},{8,14},{9,15},{10,... | collective-permute-start | bytes 36872 | tf_op jit(solution)/shard_map/ppermute | solution.py:390
  55.4 23.2 %collective-permute-start.9 = (f32[24,128]{1,0:T(8,128)S(1)}, f32[24,128]{1,0:T(8,128)S(1)}, u32[]{:S(2)}, u32[]{:S(2)}) collective-permute-start(f32[24,128]{1,0:T(8,128)S(1)} %get-tuple-element.46), channel_id=1, source_target_pairs={{0,4},{1,5},{2,6},{3,7},{4,0},{5,1},{6,2},{7,3},{8,12},{9,13},{10,... | collective-permute-start | bytes 36872 | tf_op jit(solution)/shard_map/ppermute | solution.py:390
  55.4 23.2 %collective-permute-start.8 = (f32[24,128]{1,0:T(8,128)S(1)}, f32[24,128]{1,0:T(8,128)S(1)}, u32[]{:S(2)}, u32[]{:S(2)}) collective-permute-start(f32[24,128]{1,0:T(8,128)S(1)} %get-tuple-element.45), channel_id=1, source_target_pairs={{0,2},{1,3},{2,0},{3,1},{4,6},{5,7},{6,4},{7,5},{8,10},{9,11},{10,... | collective-permute-start | bytes 36872 | tf_op jit(solution)/shard_map/ppermute | solution.py:390
  79.3 55.4 %all-to-all-start.1 = ((bf16[32,112,256]{2,1,0:T(8,128)(2,1)}), bf16[32,112,256]{2,1,0:T(8,128)(2,1)}, u32[]{:S(2)}, u32[]{:S(2)}) async-start(bf16[32,112,256]{2,1,0:T(8,128)(2,1)} %constant_dynamic-update-slice_fusion.7), calls=%async_computation.1 | async-start | bytes 3670016 | tf_op jit(solution)/shard_map/all_to_all | solution.py:396
  83.9 3.8 %copy-start.7 = (bf16[512,256]{1,0:T(8,128)(2,1)S(1)}, bf16[512,256]{1,0:T(8,128)(2,1)}, u32[]{:S(2)}) copy-start(bf16[512,256]{1,0:T(8,128)(2,1)} %copy-done.6) | copy-start | bytes 786436
  84.1 19.0 %collective-permute-start.13 = (f32[4,2,16,256]{3,2,1,0:T(8,128)S(1)}, f32[4,2,16,256]{3,2,1,0:T(8,128)S(1)}, u32[]{:S(2)}, u32[]{:S(2)}) collective-permute-start(f32[4,2,16,256]{3,2,1,0:T(8,128)S(1)} %get-tuple-element.20), channel_id=1, source_target_pairs={{0,24},{8,16},{16,8},{24,0},{1,25},{9,17},{17,9},{25,1},{2,26},{10... | collective-permute-start | bytes 393224 | tf_op jit(solution)/shard_map/ppermute | solution.py:390
  86.8 17.8 %collective-permute-start.12 = (f32[4,2,16,256]{3,2,1,0:T(8,128)S(1)}, f32[4,2,16,256]{3,2,1,0:T(8,128)S(1)}, u32[]{:S(2)}, u32[]{:S(2)}) collective-permute-start(f32[4,2,16,256]{3,2,1,0:T(8,128)S(1)} %get-tuple-element.19), channel_id=1, source_target_pairs={{0,16},{8,24},{16,0},{24,8},{1,17},{9,25},{17,1},{25,9},{2,18},{10... | collective-permute-start | bytes 393224 | tf_op jit(solution)/shard_map/ppermute | solution.py:390
  87.3 20.1 %collective-permute-start.11 = (f32[4,2,16,256]{3,2,1,0:T(8,128)S(1)}, f32[4,2,16,256]{3,2,1,0:T(8,128)S(1)}, u32[]{:S(2)}, u32[]{:S(2)}) collective-permute-start(f32[4,2,16,256]{3,2,1,0:T(8,128)S(1)} %get-tuple-element.18), channel_id=1, source_target_pairs={{0,8},{8,0},{16,24},{24,16},{1,9},{9,1},{17,25},{25,17},{2,10},{10... | collective-permute-start | bytes 393224 | tf_op jit(solution)/shard_map/ppermute | solution.py:390
  107.5 1.3 collective-permute-start.14
  107.8 12.7 %copy-start.5 = (f32[64]{0:T(128)}, f32[64]{0:T(128)S(1)}, u32[]{:S(2)}) copy-start(f32[64]{0:T(128)S(1)} %dynamic_slice.79.refs_1_) | copy-start | bytes 772
  117.2 3.3 %copy-start = (f32[16384,128]{1,0:T(8,128)}, f32[16384,128]{1,0:T(8,128)S(1)}, u32[]{:S(2)}) copy-start(f32[16384,128]{1,0:T(8,128)S(1)} %get-tuple-element.17.in_ref) | copy-start | bytes 25165828
  120.5 7.7 %collective-permute-start.17 = (f32[16,256]{1,0:T(8,128)S(1)}, f32[16,256]{1,0:T(8,128)S(1)}, u32[]{:S(2)}, u32[]{:S(2)}) collective-permute-start(f32[16,256]{1,0:T(8,128)S(1)} %get-tuple-element.26), channel_id=1, source_target_pairs={{0,6},{1,7},{2,4},{3,5},{4,2},{5,3},{6,0},{7,1},{8,14},{9,15},{10,... | collective-permute-start | bytes 49160 | tf_op jit(solution)/shard_map/ppermute | solution.py:390
  126.5 4.6 %collective-permute-start.16 = (f32[16,256]{1,0:T(8,128)S(1)}, f32[16,256]{1,0:T(8,128)S(1)}, u32[]{:S(2)}, u32[]{:S(2)}) collective-permute-start(f32[16,256]{1,0:T(8,128)S(1)} %get-tuple-element.27), channel_id=1, source_target_pairs={{0,4},{1,5},{2,6},{3,7},{4,0},{5,1},{6,2},{7,3},{8,12},{9,13},{10,... | collective-permute-start | bytes 49160 | tf_op jit(solution)/shard_map/ppermute | solution.py:390
  126.5 4.6 %collective-permute-start.15 = (f32[16,256]{1,0:T(8,128)S(1)}, f32[16,256]{1,0:T(8,128)S(1)}, u32[]{:S(2)}, u32[]{:S(2)}) collective-permute-start(f32[16,256]{1,0:T(8,128)S(1)} %get-tuple-element.25), channel_id=1, source_target_pairs={{0,2},{1,3},{2,0},{3,1},{4,6},{5,7},{6,4},{7,5},{8,10},{9,11},{10,... | collective-permute-start | bytes 49160 | tf_op jit(solution)/shard_map/ppermute | solution.py:390
  131.1 18.2 %collective-permute-start.18 = (f32[16,256]{1,0:T(8,128)S(1)}, f32[16,256]{1,0:T(8,128)S(1)}, u32[]{:S(2)}, u32[]{:S(2)}) collective-permute-start(f32[16,256]{1,0:T(8,128)S(1)} %fusion.7), channel_id=1, source_target_pairs={{0,24},{8,16},{16,8},{24,0},{1,25},{9,17},{17,9},{25,1},{2,26},{10... | collective-permute-start | bytes 49160 | tf_op jit(solution)/shard_map/ppermute | solution.py:390
  133.0 16.4 %collective-permute-start.19 = (f32[16,256]{1,0:T(8,128)S(1)}, f32[16,256]{1,0:T(8,128)S(1)}, u32[]{:S(2)}, u32[]{:S(2)}) collective-permute-start(f32[16,256]{1,0:T(8,128)S(1)} %fusion.7), channel_id=1, source_target_pairs={{0,16},{8,24},{16,0},{24,8},{1,17},{9,25},{17,1},{25,9},{2,18},{10... | collective-permute-start | bytes 49160 | tf_op jit(solution)/shard_map/ppermute | solution.py:390
  133.0 16.4 %collective-permute-start.20 = (f32[16,256]{1,0:T(8,128)S(1)}, f32[16,256]{1,0:T(8,128)S(1)}, u32[]{:S(2)}, u32[]{:S(2)}) collective-permute-start(f32[16,256]{1,0:T(8,128)S(1)} %fusion.7), channel_id=1, source_target_pairs={{0,8},{8,0},{16,24},{24,16},{1,9},{9,1},{17,25},{25,17},{2,10},{10... | collective-permute-start | bytes 49160 | tf_op jit(solution)/shard_map/ppermute | solution.py:390

commit v11 on v10

--- a/solution.py
+++ b/solution.py
@@ -258,6 +258,23 @@
     )(value, *tokens)
 
 
+def release_kernel(*refs):
+    pass
+
+
+def released(value, tokens):
+    anywhere = pl.BlockSpec(memory_space=pl.ANY)
+    return pl.pallas_call(
+        release_kernel,
+        in_specs=[anywhere] * (1 + len(tokens)),
+        out_specs=anywhere,
+        out_shape=jax.ShapeDtypeStruct(value.shape, value.dtype),
+        input_output_aliases={0: 0},
+        cost_estimate=COST,
+        name="release",
+    )(value, *tokens)
+
+
 def place_runs(me_ref, slot_ref, row_ref, held_ref, stage_ref, copies, peers, run, first):
     size = row_ref.shape[0] // peers
     batch = max(n for n in range(1, 49) if size % n == 0)
@@ -380,7 +397,6 @@
     peers = groups * reps
     batch = rows_local * reps
     run = classes // peers
-    share = rows_local // groups
     grp, rep = lax.axis_index("grp").astype(jnp.int32), lax.axis_index("rep").astype(jnp.int32)
     me = (rep * groups + grp).reshape(1)
     base = me * classes
@@ -389,15 +405,12 @@
         size = lax.axis_size(axis)
         return lax.ppermute(value, axis, [(i, i ^ k) for i in range(size)]) if k else value
 
-    def released(value, tokens):
-        return lax.dynamic_update_slice(value, tie(value[:1, :16], tokens), (0, 0, 0))
-
     def relay(sent):
         return lax.all_to_all(sent, ALL, 0, 0, tiled=True).reshape(-1, width)
 
     weights = in_hbm(class_weights)
     runs = in_hbm(centroids.reshape(peers, run, width))
-    cut = run * 9 // 16 // 16 * 16
+    cut = run * 5 // 8 // 16 * 16
     mixed = jnp.concatenate([swap(embeddings, "rep", c) for c in range(2)])
     mixed = jnp.concatenate([swap(mixed, "rep", 2 * z) for z in range(reps // 2)])
     rows_a = relay(released(fetch(runs, 0, cut, []), [mixed]))
@@ -436,19 +449,14 @@
     done = in_hbm(weight_grad)
     held, token = place_rows(me, slots, rows_a, done, peers, run, 0)
 
-    grad = (a / total[:, None] - b).reshape(half, 2, groups, share, width)
-    grad = sum(swap(index(grad, grp ^ j, 2, False), "grp", j) for j in range(groups))
+    grad = (a / total[:, None] - b).reshape(half, 2, rows_local, width)
+    grad = sum(swap(index(grad, core ^ c, 1, False), "rep", c) for c in range(2))
     grad = tie(grad, [done])
-    grad = sum(swap(index(grad, core ^ c, 1, False), "rep", c) for c in range(2))
+    grad = sum(swap(grad, "grp", j) for j in range(groups))
     grad = tie(grad, [token, loss])
-    own = sum(swap(index(grad, deep ^ z, 0, False), "rep", 2 * z) for z in range(half))
-    shares = [swap(own, "grp", j) for j in range(groups)]
-    bit = 1
-    while bit < groups:
-        flip = (grp & bit) != 0
-        shares = [jnp.where(flip, shares[j ^ bit], shares[j]) for j in range(groups)]
-        bit *= 2
-    embedding_gradient = jnp.concatenate(shares)
+    embedding_gradient = sum(
+        swap(index(grad, deep ^ z, 0, False), "rep", 2 * z) for z in range(half)
+    )
 
     refreshed = place_and_blend(me, slots, rows_b, in_hbm(held), in_hbm(what), peers, run, cut)
     return (loss, embedding_gradient, weight_grad, refreshed)

time: 151 us -> 155 us (1.026)
  waiting for transfers between devices: 45 us -> 60.9 us
  starting transfers between devices: 36.8 us -> 32.3 us
  local copies, waits for them, and re-layouts: 11.2 us -> 6.75 us
  Pallas kernels: 54.3 us -> 51.8 us
    ppermute x21 -> x18, waiting for transfers between devices: 44.9 us -> 60.9 us  [swap(): lax.ppermute(value, axis, [(i, i ^ k) for i in range(size)])]
    ppermute x21 -> x18, starting transfers between devices: 28 us -> 23.4 us  [swap(): lax.ppermute(value, axis, [(i, i ^ k) for i in range(size)])]
    pallas_call x2, Pallas kernels: 5.92 us -> 3.26 us  [fetch(): pl.pallas_call(functools.partial(fetch_kernel, first=first), in_specs=[hb...]
  transfers between devices with their start and end apart: 23 -> 20, of which waited for: 14 -> 11; matrix products, arithmetic and copies ran while one was open for 3% -> 2% of each run, Pallas kernels for 36% -> 33%
where the time goes in v11:
time: 155 us
  waiting for transfers between devices  60.9 us (39%)
  Pallas kernels  51.8 us (33%)
  starting transfers between devices  32.3 us (21%)
  local copies, waits for them, and re-layouts  6.75 us (4%)
  other arithmetic  1.7 us (1%)
    ppermute x18, waiting for transfers between devices, swap(): lax.ppermute(value, axis, [(i, i ^ k) for i in range(size)])  60.9 us
    ppermute x18, starting transfers between devices, swap(): lax.ppermute(value, axis, [(i, i ^ k) for i in range(size)])  23.4 us
    pallas_call x1, Pallas kernels, place_and_blend(): pl.pallas_call(functools.partial(blend_kernel, peers=peers, run=run, firs...  13.7 us
    pallas_call x1, Pallas kernels, forward(): pl.pallas_call(functools.partial(forward_kernel, classes=classes, reps=re...  13.5 us
    pallas_call x1, Pallas kernels, weight_gradient(): pl.pallas_call(weight_kernel, grid=(classes // tile,), in_specs=[pl.Block...  11.8 us
    pallas_call x1, Pallas kernels, place_rows(): pl.pallas_call(functools.partial(place_kernel, peers=peers, run=run, firs...  9.42 us
    all_to_all x2, starting transfers between devices, relay(): return lax.all_to_all(sent, ALL, 0, 0, tiled=True).reshape(-1, width)  8.98 us
    unnamed x24, local copies, waits for them, and re-layouts  6.26 us
  transfers between devices with their start and end apart: 20, of which 11 were waited for; matrix products, arithmetic and copies ran while one was open for 2% of the time, Pallas kernels for 33%

profile of v11, /device:TPU:0, one launch (start us, length us, event | category | flops | bytes accessed | tf_op | source)
XLA Modules:
  0.0 154.5 jit_solution(15173522638908022169)
XLA Ops:
  0.6 0.5 collective-permute-start
  1.1 0.8 constant_dynamic-update-slice_fusion.1
  1.9 0.3 collective-permute-done
  2.2 2.9 %collective-permute-start.1 = (bf16[128,256]{1,0:T(8,128)(2,1)S(1)}, bf16[128,256]{1,0:T(8,128)(2,1)S(1)}, u32[]{:S(2)}, u32[]{:S(2)}) collective-permute-start(bf16[128,256]{1,0:T(8,128)(2,1)S(1)} %get-tuple-element.31), channel_id=1, source_target_pairs={{0,2},{1,3},{2,0},{3,1},{4,6},{5,7},{6,4},{7,5},{8,10},{9,11},{10,... | collective-permute-start | bytes 196616 | tf_op jit(solution)/shard_map/ppermute | solution.py:406
  5.1 1.7 %fetch.3.refs_0_ = bf16[32,160,256]{2,1,0:T(8,128)(2,1)S(1)} custom-call(bf16[32,256,256]{2,1,0:T(8,128)(2,1)} %bitcast.79), custom_call_target="tpu_custom_call" | custom-call | bytes 10485760 | tf_op jit(solution)/shard_map/fetch/pallas_call | solution.py:229
  6.9 0.0 copy-start.1
  6.9 1.5 copy-done.1
  8.4 2.6 %collective-permute-start.2 = (bf16[128,256]{1,0:T(8,128)(2,1)S(1)}, bf16[128,256]{1,0:T(8,128)(2,1)S(1)}, u32[]{:S(2)}, u32[]{:S(2)}) collective-permute-start(bf16[128,256]{1,0:T(8,128)(2,1)S(1)} %get-tuple-element.31), channel_id=1, source_target_pairs={{0,4},{1,5},{2,6},{3,7},{4,0},{5,1},{6,2},{7,3},{8,12},{9,13},{10,... | collective-permute-start | bytes 196616 | tf_op jit(solution)/shard_map/ppermute | solution.py:406
  11.0 0.0 collective-permute-start.3
  11.0 0.0 collective-permute-done.1
  11.0 3.5 %collective-permute-done.2 = bf16[128,256]{1,0:T(8,128)(2,1)S(1)} collective-permute-done((bf16[128,256]{1,0:T(8,128)(2,1)S(1)}, bf16[128,256]{1,0:T(8,128)(2,1)S(1)}, u32[]{:S(2)}, u32[]{:S(2)}) %collective-permute-start.2) | collective-permute-done | bytes 65568 | tf_op jit(solution)/shard_map/ppermute | solution.py:406
  14.5 2.6 %collective-permute-done.3 = bf16[128,256]{1,0:T(8,128)(2,1)S(1)} collective-permute-done((bf16[128,256]{1,0:T(8,128)(2,1)S(1)}, bf16[128,256]{1,0:T(8,128)(2,1)S(1)}, u32[]{:S(2)}, u32[]{:S(2)}) %collective-permute-start.3) | collective-permute-done | bytes 65568 | tf_op jit(solution)/shard_map/ppermute | solution.py:406
  17.1 0.7 copy-done.3
  17.9 4.4 %all-to-all-start = ((bf16[32,160,256]{2,1,0:T(8,128)(2,1)}), bf16[32,160,256]{2,1,0:T(8,128)(2,1)}, u32[]{:S(2)}, u32[]{:S(2)}) async-start(bf16[32,160,256]{2,1,0:T(8,128)(2,1)} %release.2), calls=%async_computation | async-start | bytes 5242880 | tf_op jit(solution)/shard_map/all_to_all | solution.py:409
  22.3 0.0 copy-done.6
  22.3 0.1 copy.16.lab_ref
  22.4 0.0 copy-done.8
  22.5 0.0 copy-done.4
  22.6 13.5 %forward_sums.1 = (bf16[512,256]{1,0:T(8,128)(2,1)S(1)}, f32[512,256]{1,0:T(8,128)S(1)}, f32[512,256]{1,0:T(8,128)S(1)}, f32[8,512]{1,0:T(8,128)S(1)}, bf16[8192,256]{1,0:T(8,128)(2,1)}) custom-call(s32[1]{0:T(128)S(6)} %mul.18.base_ref, s32[1]{0:T(128)} %bitcast.1.rep_ref, s32[512,1]{1,0:T(8,128)S(1)} %copy.16.lab_ref, bf16[8192,256]{1,0:T(8,128)(2,1)} %w_ref.3, ...), custom_call_target="tpu_custom_call" | custom-call | flops 12884901888 | bytes 4194304 | tf_op jit(solution)/shard_map/forward_sums/pallas_call | solution.py:110
  36.1 2.7 %collective-permute-start.6 = (f32[24,128]{1,0:T(8,128)S(1)}, f32[24,128]{1,0:T(8,128)S(1)}, u32[]{:S(2)}, u32[]{:S(2)}) collective-permute-start(f32[24,128]{1,0:T(8,128)S(1)} %get-tuple-element.46), channel_id=1, source_target_pairs={{0,24},{8,16},{16,8},{24,0},{1,25},{9,17},{17,9},{25,1},{2,26},{10... | collective-permute-start | bytes 36872 | tf_op jit(solution)/shard_map/ppermute | solution.py:406
  38.8 0.6 collective-permute-start.5
  39.3 0.3 collective-permute-start.4
  39.7 1.5 collective-permute-done.6
  41.2 1.4 collective-permute-done.5
  42.5 0.7 collective-permute-done.4
  43.4 0.1 collective-permute-start.7
  43.6 1.5 fetch.2.refs_0_
  45.1 0.0 copy-start
  45.1 0.0 collective-permute-done.7
  45.3 3.3 %collective-permute-start.10 = (f32[24,128]{1,0:T(8,128)S(1)}, f32[24,128]{1,0:T(8,128)S(1)}, u32[]{:S(2)}, u32[]{:S(2)}) collective-permute-start(f32[24,128]{1,0:T(8,128)S(1)} %get-tuple-element.40), channel_id=1, source_target_pairs={{0,6},{1,7},{2,4},{3,5},{4,2},{5,3},{6,0},{7,1},{8,14},{9,15},{10,... | collective-permute-start | bytes 36872 | tf_op jit(solution)/shard_map/ppermute | solution.py:406
  48.6 0.0 collective-permute-start.9
  48.6 1.2 collective-permute-start.8
  49.8 19.8 %collective-permute-done.10 = f32[24,128]{1,0:T(8,128)S(1)} collective-permute-done((f32[24,128]{1,0:T(8,128)S(1)}, f32[24,128]{1,0:T(8,128)S(1)}, u32[]{:S(2)}, u32[]{:S(2)}) %collective-permute-start.10) | collective-permute-done | bytes 12320 | tf_op jit(solution)/shard_map/ppermute | solution.py:406
  69.5 13.6 %collective-permute-done.9 = f32[24,128]{1,0:T(8,128)S(1)} collective-permute-done((f32[24,128]{1,0:T(8,128)S(1)}, f32[24,128]{1,0:T(8,128)S(1)}, u32[]{:S(2)}, u32[]{:S(2)}) %collective-permute-start.9) | collective-permute-done | bytes 12320 | tf_op jit(solution)/shard_map/ppermute | solution.py:406
  83.1 0.0 collective-permute-done.8
  83.2 0.6 fusion.12
  83.8 0.0 copy-done
  83.8 0.0 all-to-all-done
  83.8 4.6 %all-to-all-start.1 = ((bf16[32,96,256]{2,1,0:T(8,128)(2,1)}), bf16[32,96,256]{2,1,0:T(8,128)(2,1)S(1)}, u32[]{:S(2)}, u32[]{:S(2)}) async-start(bf16[32,96,256]{2,1,0:T(8,128)(2,1)} %release.3), calls=%async_computation.1 | async-start | bytes 3145728 | tf_op jit(solution)/shard_map/all_to_all | solution.py:409
  88.4 0.0 copy-done.5
  88.4 0.1 divide_subtract_fusion
  88.6 0.3 collective-permute-start.11
  88.9 11.8 %weight_gradient.1.refs_0_._ = f32[8192,256]{1,0:T(8,128)} custom-call(s32[1]{0:T(128)S(6)} %mul.18.base_ref, bf16[512,256]{1,0:T(8,128)(2,1)S(1)} %get-tuple-element.14.emb_ref, s32[1,512]{1,0:T(1,128)S(1)} %bitcast.78, f32[8,512]{1,0:T(8,128)S(1)} %get-tuple-element.11.refs_0_.st_ref, f32[1,512]{1,0:T(1,128)S(1)} %bitcast.74, bf16[8192,256]{1,0:T(8,128)(2,1)} %w_ref.3), custom_call_target="tpu_custom_call" | custom-call | flops 12884901888 | bytes 12582912 | tf_op jit(solution)/shard_map/weight_gradient/pallas_call | solution.py:178
  100.7 0.0 collective-permute-done.11
  100.8 2.6 %collective-permute-start.14 = (f32[4,64,256]{2,1,0:T(8,128)S(1)}, f32[4,64,256]{2,1,0:T(8,128)S(1)}, u32[]{:S(2)}, u32[]{:S(2)}) collective-permute-start(f32[4,64,256]{2,1,0:T(8,128)S(1)} %tie.4), channel_id=1, source_target_pairs={{0,24},{8,16},{16,8},{24,0},{1,25},{9,17},{17,9},{25,1},{2,26},{10... | collective-permute-start | bytes 786440 | tf_op jit(solution)/shard_map/ppermute | solution.py:406
  103.4 0.6 collective-permute-start.13
  104.0 0.3 collective-permute-start.12
  104.4 0.1 dynamic_slice.66.refs_1_
  104.5 11.5 %collective-permute-done.14 = f32[4,64,256]{2,1,0:T(8,128)S(1)} collective-permute-done((f32[4,64,256]{2,1,0:T(8,128)S(1)}, f32[4,64,256]{2,1,0:T(8,128)S(1)}, u32[]{:S(2)}, u32[]{:S(2)}) %collective-permute-start.14) | collective-permute-done | bytes 262176 | tf_op jit(solution)/shard_map/ppermute | solution.py:406
  116.0 5.2 %collective-permute-done.13 = f32[4,64,256]{2,1,0:T(8,128)S(1)} collective-permute-done((f32[4,64,256]{2,1,0:T(8,128)S(1)}, f32[4,64,256]{2,1,0:T(8,128)S(1)}, u32[]{:S(2)}, u32[]{:S(2)}) %collective-permute-start.13) | collective-permute-done | bytes 262176 | tf_op jit(solution)/shard_map/ppermute | solution.py:406
  121.2 0.7 collective-permute-done.12
  121.9 0.1 add_add_fusion.value_ref
  122.0 9.4 %place_rows.1 = (f32[16384,128]{1,0:T(8,128)S(1)}, f32[8,128]{1,0:T(8,128)S(1)}) custom-call(s32[1]{0:T(128)} %bitcast.me_ref, s32[8192]{0:T(1024)S(1)} %bitcast.72, bf16[5120,256]{1,0:T(8,128)(2,1)} %bitcast.38.row_ref, f32[8192,256]{1,0:T(8,128)} %weight_gradient.1.refs_0_._), custom_call_target="tpu_custom_call" | custom-call | bytes 20971520 | tf_op jit(solution)/shard_map/place_rows/pallas_call | solution.py:319
  131.4 0.0 copy-start.2
  131.4 3.3 %copy-done.2 = f32[16384,128]{1,0:T(8,128)} copy-done((f32[16384,128]{1,0:T(8,128)}, f32[16384,128]{1,0:T(8,128)S(1)}, u32[]{:S(2)}) %copy-start.2) | copy-done | bytes 8388632
  134.7 3.9 %collective-permute-start.17 = (f32[64,256]{1,0:T(8,128)S(1)}, f32[64,256]{1,0:T(8,128)S(1)}, u32[]{:S(2)}, u32[]{:S(2)}) collective-permute-start(f32[64,256]{1,0:T(8,128)S(1)} %get-tuple-element.19), channel_id=1, source_target_pairs={{0,6},{1,7},{2,4},{3,5},{4,2},{5,3},{6,0},{7,1},{8,14},{9,15},{10,... | collective-permute-start | bytes 196616 | tf_op jit(solution)/shard_map/ppermute | solution.py:406
  138.7 1.5 collective-permute-start.16
  140.1 0.0 collective-permute-start.15
  140.1 0.0 all-to-all-done.1
  140.1 13.7 %place_and_blend.1 = bf16[8192,256]{1,0:T(8,128)(2,1)} custom-call(s32[1]{0:T(128)} %bitcast.me_ref, s32[8192]{0:T(1024)S(1)} %bitcast.73, bf16[8192,256]{1,0:T(8,128)(2,1)} %get-tuple-element.16.w_ref, bf16[3072,256]{1,0:T(8,128)(2,1)S(1)} %bitcast.71, f32[16384,128]{1,0:T(8,128)} %copy-done.2), custom_call_target="tpu_custom_call" | custom-call | bytes 25165824 | tf_op jit(solution)/shard_map/place_and_blend/pallas_call | solution.py:372
  153.8 0.0 collective-permute-done.17
  153.8 0.0 collective-permute-done.16
  153.8 0.0 collective-permute-done.15
  153.8 0.7 fusion.1
  (38 shorter events, 0.6 us)
Async XLA Ops:
  0.6 1.6 %collective-permute-start = (bf16[64,256]{1,0:T(8,128)(2,1)}, bf16[64,256]{1,0:T(8,128)(2,1)S(1)}, u32[]{:S(2)}, u32[]{:S(2)}) collective-permute-start(bf16[64,256]{1,0:T(8,128)(2,1)} %param.5), channel_id=1, source_target_pairs={{0,1},{1,0},{2,3},{3,2},{4,5},{5,4},{6,7},{7,6},{8,9},{9,8},{10,11... | collective-permute-start | bytes 98312 | tf_op jit(solution)/shard_map/ppermute | solution.py:406
  2.2 8.7 %collective-permute-start.1 = (bf16[128,256]{1,0:T(8,128)(2,1)S(1)}, bf16[128,256]{1,0:T(8,128)(2,1)S(1)}, u32[]{:S(2)}, u32[]{:S(2)}) collective-permute-start(bf16[128,256]{1,0:T(8,128)(2,1)S(1)} %get-tuple-element.31), channel_id=1, source_target_pairs={{0,2},{1,3},{2,0},{3,1},{4,6},{5,7},{6,4},{7,5},{8,10},{9,11},{10,... | collective-permute-start | bytes 196616 | tf_op jit(solution)/shard_map/ppermute | solution.py:406
  6.9 1.5 copy-start.1
  8.4 6.1 %collective-permute-start.2 = (bf16[128,256]{1,0:T(8,128)(2,1)S(1)}, bf16[128,256]{1,0:T(8,128)(2,1)S(1)}, u32[]{:S(2)}, u32[]{:S(2)}) collective-permute-start(bf16[128,256]{1,0:T(8,128)(2,1)S(1)} %get-tuple-element.31), channel_id=1, source_target_pairs={{0,4},{1,5},{2,6},{3,7},{4,0},{5,1},{6,2},{7,3},{8,12},{9,13},{10,... | collective-permute-start | bytes 196616 | tf_op jit(solution)/shard_map/ppermute | solution.py:406
  11.0 6.2 %collective-permute-start.3 = (bf16[128,256]{1,0:T(8,128)(2,1)S(1)}, bf16[128,256]{1,0:T(8,128)(2,1)S(1)}, u32[]{:S(2)}, u32[]{:S(2)}) collective-permute-start(bf16[128,256]{1,0:T(8,128)(2,1)S(1)} %get-tuple-element.31), channel_id=1, source_target_pairs={{0,6},{1,7},{2,4},{3,5},{4,2},{5,3},{6,0},{7,1},{8,14},{9,15},{10,... | collective-permute-start | bytes 196616 | tf_op jit(solution)/shard_map/ppermute | solution.py:406
  17.1 0.7 copy-start.3
  17.8 4.4 %copy-start.6 = (s32[512]{0:T(512)S(1)}, s32[512]{0:T(512)}, u32[]{:S(2)}) copy-start(s32[512]{0:T(512)} %param.6) | copy-start | bytes 6148
  17.8 4.6 %copy-start.8 = (s32[8192]{0:T(1024)S(1)}, s32[8192]{0:T(1024)}, u32[]{:S(2)}) copy-start(s32[8192]{0:T(1024)} %param.9) | copy-start | bytes 98308
  17.9 4.7 %copy-start.4 = (bf16[512,256]{1,0:T(8,128)(2,1)S(1)}, bf16[512,256]{1,0:T(8,128)(2,1)}, u32[]{:S(2)}) copy-start(bf16[512,256]{1,0:T(8,128)(2,1)} %copy-done.3) | copy-start | bytes 786436
  17.9 65.9 %all-to-all-start = ((bf16[32,160,256]{2,1,0:T(8,128)(2,1)}), bf16[32,160,256]{2,1,0:T(8,128)(2,1)}, u32[]{:S(2)}, u32[]{:S(2)}) async-start(bf16[32,160,256]{2,1,0:T(8,128)(2,1)} %release.2), calls=%async_computation | async-start | bytes 5242880 | tf_op jit(solution)/shard_map/all_to_all | solution.py:409
  36.1 5.1 %collective-permute-start.6 = (f32[24,128]{1,0:T(8,128)S(1)}, f32[24,128]{1,0:T(8,128)S(1)}, u32[]{:S(2)}, u32[]{:S(2)}) collective-permute-start(f32[24,128]{1,0:T(8,128)S(1)} %get-tuple-element.46), channel_id=1, source_target_pairs={{0,24},{8,16},{16,8},{24,0},{1,25},{9,17},{17,9},{25,1},{2,26},{10... | collective-permute-start | bytes 36872 | tf_op jit(solution)/shard_map/ppermute | solution.py:406
  38.8 3.8 %collective-permute-start.5 = (f32[24,128]{1,0:T(8,128)S(1)}, f32[24,128]{1,0:T(8,128)S(1)}, u32[]{:S(2)}, u32[]{:S(2)}) collective-permute-start(f32[24,128]{1,0:T(8,128)S(1)} %get-tuple-element.45), channel_id=1, source_target_pairs={{0,16},{8,24},{16,0},{24,8},{1,17},{9,25},{17,1},{25,9},{2,18},{10... | collective-permute-start | bytes 36872 | tf_op jit(solution)/shard_map/ppermute | solution.py:406
  39.3 3.9 %collective-permute-start.4 = (f32[24,128]{1,0:T(8,128)S(1)}, f32[24,128]{1,0:T(8,128)S(1)}, u32[]{:S(2)}, u32[]{:S(2)}) collective-permute-start(f32[24,128]{1,0:T(8,128)S(1)} %get-tuple-element.44), channel_id=1, source_target_pairs={{0,8},{8,0},{16,24},{24,16},{1,9},{9,1},{17,25},{25,17},{2,10},{10... | collective-permute-start | bytes 36872 | tf_op jit(solution)/shard_map/ppermute | solution.py:406
  43.4 1.7 %collective-permute-start.7 = (f32[40,128]{1,0:T(8,128)S(1)}, f32[40,128]{1,0:T(8,128)S(1)}, u32[]{:S(2)}, u32[]{:S(2)}) collective-permute-start(f32[40,128]{1,0:T(8,128)S(1)} %get-tuple-element.42), channel_id=1, source_target_pairs={{0,1},{1,0},{2,3},{3,2},{4,5},{5,4},{6,7},{7,6},{8,9},{9,8},{10,11... | collective-permute-start | bytes 61448 | tf_op jit(solution)/shard_map/ppermute | solution.py:406
  45.1 38.7 %copy-start = (bf16[32,96,256]{2,1,0:T(8,128)(2,1)}, bf16[32,96,256]{2,1,0:T(8,128)(2,1)S(1)}, u32[]{:S(2)}) copy-start(bf16[32,96,256]{2,1,0:T(8,128)(2,1)S(1)} %fetch.2.refs_0_) | copy-start | bytes 4718596
  45.3 24.2 %collective-permute-start.10 = (f32[24,128]{1,0:T(8,128)S(1)}, f32[24,128]{1,0:T(8,128)S(1)}, u32[]{:S(2)}, u32[]{:S(2)}) collective-permute-start(f32[24,128]{1,0:T(8,128)S(1)} %get-tuple-element.40), channel_id=1, source_target_pairs={{0,6},{1,7},{2,4},{3,5},{4,2},{5,3},{6,0},{7,1},{8,14},{9,15},{10,... | collective-permute-start | bytes 36872 | tf_op jit(solution)/shard_map/ppermute | solution.py:406
  48.6 34.6 %collective-permute-start.9 = (f32[24,128]{1,0:T(8,128)S(1)}, f32[24,128]{1,0:T(8,128)S(1)}, u32[]{:S(2)}, u32[]{:S(2)}) collective-permute-start(f32[24,128]{1,0:T(8,128)S(1)} %get-tuple-element.39), channel_id=1, source_target_pairs={{0,4},{1,5},{2,6},{3,7},{4,0},{5,1},{6,2},{7,3},{8,12},{9,13},{10,... | collective-permute-start | bytes 36872 | tf_op jit(solution)/shard_map/ppermute | solution.py:406
  48.6 34.6 %collective-permute-start.8 = (f32[24,128]{1,0:T(8,128)S(1)}, f32[24,128]{1,0:T(8,128)S(1)}, u32[]{:S(2)}, u32[]{:S(2)}) collective-permute-start(f32[24,128]{1,0:T(8,128)S(1)} %get-tuple-element.38), channel_id=1, source_target_pairs={{0,2},{1,3},{2,0},{3,1},{4,6},{5,7},{6,4},{7,5},{8,10},{9,11},{10,... | collective-permute-start | bytes 36872 | tf_op jit(solution)/shard_map/ppermute | solution.py:406
  83.8 4.6 %copy-start.5 = (f32[512]{0:T(512)S(1)}, f32[512]{0:T(512)}, u32[]{:S(2)}) copy-start(f32[512]{0:T(512)} %get-tuple-element.35.refs_1_) | copy-start | bytes 6148
  83.8 56.4 %all-to-all-start.1 = ((bf16[32,96,256]{2,1,0:T(8,128)(2,1)}), bf16[32,96,256]{2,1,0:T(8,128)(2,1)S(1)}, u32[]{:S(2)}, u32[]{:S(2)}) async-start(bf16[32,96,256]{2,1,0:T(8,128)(2,1)} %release.3), calls=%async_computation.1 | async-start | bytes 3145728 | tf_op jit(solution)/shard_map/all_to_all | solution.py:409
  88.6 12.1 %collective-permute-start.11 = (f32[4,64,256]{2,1,0:T(8,128)S(1)}, f32[4,64,256]{2,1,0:T(8,128)S(1)}, u32[]{:S(2)}, u32[]{:S(2)}) collective-permute-start(f32[4,64,256]{2,1,0:T(8,128)S(1)} %dynamic-slice_bitcast_fusion), channel_id=1, source_target_pairs={{0,1},{1,0},{2,3},{3,2},{4,5},{5,4},{6,7},{7,6},{8,9},{9,8},{10,11... | collective-permute-start | bytes 786440 | tf_op jit(solution)/shard_map/ppermute | solution.py:406
  100.8 15.2 %collective-permute-start.14 = (f32[4,64,256]{2,1,0:T(8,128)S(1)}, f32[4,64,256]{2,1,0:T(8,128)S(1)}, u32[]{:S(2)}, u32[]{:S(2)}) collective-permute-start(f32[4,64,256]{2,1,0:T(8,128)S(1)} %tie.4), channel_id=1, source_target_pairs={{0,24},{8,16},{16,8},{24,0},{1,25},{9,17},{17,9},{25,1},{2,26},{10... | collective-permute-start | bytes 786440 | tf_op jit(solution)/shard_map/ppermute | solution.py:406
  103.4 17.8 %collective-permute-start.13 = (f32[4,64,256]{2,1,0:T(8,128)S(1)}, f32[4,64,256]{2,1,0:T(8,128)S(1)}, u32[]{:S(2)}, u32[]{:S(2)}) collective-permute-start(f32[4,64,256]{2,1,0:T(8,128)S(1)} %tie.4), channel_id=1, source_target_pairs={{0,16},{8,24},{16,0},{24,8},{1,17},{9,25},{17,1},{25,9},{2,18},{10... | collective-permute-start | bytes 786440 | tf_op jit(solution)/shard_map/ppermute | solution.py:406
  104.0 17.9 %collective-permute-start.12 = (f32[4,64,256]{2,1,0:T(8,128)S(1)}, f32[4,64,256]{2,1,0:T(8,128)S(1)}, u32[]{:S(2)}, u32[]{:S(2)}) collective-permute-start(f32[4,64,256]{2,1,0:T(8,128)S(1)} %tie.4), channel_id=1, source_target_pairs={{0,8},{8,0},{16,24},{24,16},{1,9},{9,1},{17,25},{25,17},{2,10},{10... | collective-permute-start | bytes 786440 | tf_op jit(solution)/shard_map/ppermute | solution.py:406
  104.5 30.2 %copy-start.7 = (f32[64]{0:T(128)}, f32[64]{0:T(128)S(1)}, u32[]{:S(2)}) copy-start(f32[64]{0:T(128)S(1)} %dynamic_slice.66.refs_1_) | copy-start | bytes 772
  131.4 3.3 %copy-start.2 = (f32[16384,128]{1,0:T(8,128)}, f32[16384,128]{1,0:T(8,128)S(1)}, u32[]{:S(2)}) copy-start(f32[16384,128]{1,0:T(8,128)S(1)} %get-tuple-element.17.in_ref) | copy-start | bytes 25165828
  134.7 19.1 %collective-permute-start.17 = (f32[64,256]{1,0:T(8,128)S(1)}, f32[64,256]{1,0:T(8,128)S(1)}, u32[]{:S(2)}, u32[]{:S(2)}) collective-permute-start(f32[64,256]{1,0:T(8,128)S(1)} %get-tuple-element.19), channel_id=1, source_target_pairs={{0,6},{1,7},{2,4},{3,5},{4,2},{5,3},{6,0},{7,1},{8,14},{9,15},{10,... | collective-permute-start | bytes 196616 | tf_op jit(solution)/shard_map/ppermute | solution.py:406
  138.7 15.2 %collective-permute-start.16 = (f32[64,256]{1,0:T(8,128)S(1)}, f32[64,256]{1,0:T(8,128)S(1)}, u32[]{:S(2)}, u32[]{:S(2)}) collective-permute-start(f32[64,256]{1,0:T(8,128)S(1)} %get-tuple-element.20), channel_id=1, source_target_pairs={{0,4},{1,5},{2,6},{3,7},{4,0},{5,1},{6,2},{7,3},{8,12},{9,13},{10,... | collective-permute-start | bytes 196616 | tf_op jit(solution)/shard_map/ppermute | solution.py:406
  140.1 13.7 %collective-permute-start.15 = (f32[64,256]{1,0:T(8,128)S(1)}, f32[64,256]{1,0:T(8,128)S(1)}, u32[]{:S(2)}, u32[]{:S(2)}) collective-permute-start(f32[64,256]{1,0:T(8,128)S(1)} %get-tuple-element.18), channel_id=1, source_target_pairs={{0,2},{1,3},{2,0},{3,1},{4,6},{5,7},{6,4},{7,5},{8,10},{9,11},{10,... | collective-permute-start | bytes 196616 | tf_op jit(solution)/shard_map/ppermute | solution.py:406

commit v12 on v11

--- a/solution.py
+++ b/solution.py
@@ -240,22 +240,25 @@
     )(runs, *tokens)
 
 
-def tie_kernel(value_ref, *refs):
-    refs[-1][...] = value_ref[...]
-
-
-def tie(value, tokens):
+def join_kernel(*refs, count):
+    total = refs[0][...]
+    for ref in refs[1:count]:
+        total = total + ref[...]
+    refs[-1][...] = total
+
+
+def join(values, tokens):
     anywhere = pl.BlockSpec(memory_space=pl.ANY)
     vmem = pl.BlockSpec(memory_space=pltpu.VMEM)
     return pl.pallas_call(
-        tie_kernel,
-        in_specs=[vmem] + [anywhere] * len(tokens),
+        functools.partial(join_kernel, count=len(values)),
+        in_specs=[vmem] * len(values) + [anywhere] * len(tokens),
         out_specs=vmem,
-        out_shape=jax.ShapeDtypeStruct(value.shape, value.dtype),
-        compiler_params=pltpu.CompilerParams(vmem_limit_bytes=2 * MIB),
+        out_shape=jax.ShapeDtypeStruct(values[0].shape, values[0].dtype),
+        compiler_params=pltpu.CompilerParams(vmem_limit_bytes=6 * MIB),
         cost_estimate=COST,
-        name="tie",
-    )(value, *tokens)
+        name="join",
+    )(*values, *tokens)
 
 
 def release_kernel(*refs):
@@ -327,7 +330,7 @@
         scratch_shapes=[pltpu.VMEM((2 * rows.shape[0], 128), jnp.float32)],
         compiler_params=pltpu.CompilerParams(vmem_limit_bytes=24 * MIB),
         cost_estimate=pl.CostEstimate(
-            flops=0, bytes_accessed=16 * rows.shape[0] * rows.shape[1], transcendentals=0
+            flops=0, bytes_accessed=32 * rows.shape[0] * rows.shape[1], transcendentals=0
         ),
         name="place_rows",
     )(me, slots, rows, after)
@@ -435,7 +438,7 @@
     wanted = [index(wanted, core ^ c, 2, False) for c in range(2)]
     sums, wanted = share_out(sums, wanted, "rep", range(2))
     sent_b = fetch(runs, cut, run - cut, [stats])
-    sums = tie(sums.reshape(-1, 128), [sent_b]).reshape(-1)
+    sums = join([sums.reshape(-1, 128)], [sent_b]).reshape(-1)
     wanted = wanted.reshape(2, groups, half, run)
     wanted = [index(wanted, deep ^ z, 2, False) for z in range(half)]
     sums, slots = share_out(sums, wanted, "rep", range(0, reps, 2))
@@ -450,10 +453,8 @@
     held, token = place_rows(me, slots, rows_a, done, peers, run, 0)
 
     grad = (a / total[:, None] - b).reshape(half, 2, rows_local, width)
-    grad = sum(swap(index(grad, core ^ c, 1, False), "rep", c) for c in range(2))
-    grad = tie(grad, [done])
-    grad = sum(swap(grad, "grp", j) for j in range(groups))
-    grad = tie(grad, [token, loss])
+    grad = join([swap(index(grad, core ^ c, 1, False), "rep", c) for c in range(2)], [done])
+    grad = join([swap(grad, "grp", j) for j in range(groups)], [token, loss])
     embedding_gradient = sum(
         swap(index(grad, deep ^ z, 0, False), "rep", 2 * z) for z in range(half)
     )

time: 155 us -> 142 us (0.916)
  waiting for transfers between devices: 60.9 us -> 48.2 us
    ppermute x18, waiting for transfers between devices: 60.9 us -> 48.2 us  [swap(): lax.ppermute(value, axis, [(i, i ^ k) for i in range(size)])]
  transfers between devices with their start and end apart: 20 -> 20, of which waited for: 11 -> 10; matrix products, arithmetic and copies ran while one was open for 2% -> 2% of each run, Pallas kernels for 33% -> 37%
where the time goes in v12:
time: 142 us; the launch traced here: 141 us
  Pallas kernels  51.8 us (36%)
  waiting for transfers between devices  48.2 us (34%)
  starting transfers between devices  32.1 us (23%)
  local copies, waits for them, and re-layouts  6.76 us (5%)
  other arithmetic  1.59 us (1%)
    ppermute x18, waiting for transfers between devices, swap(): lax.ppermute(value, axis, [(i, i ^ k) for i in range(size)])  48.2 us
    ppermute x18, starting transfers between devices, swap(): lax.ppermute(value, axis, [(i, i ^ k) for i in range(size)])  23.2 us
    pallas_call x1, Pallas kernels, place_and_blend(): pl.pallas_call(functools.partial(blend_kernel, peers=peers, run=run, firs...  13.7 us
    pallas_call x1, Pallas kernels, forward(): pl.pallas_call(functools.partial(forward_kernel, classes=classes, reps=re...  13.5 us
    pallas_call x1, Pallas kernels, weight_gradient(): pl.pallas_call(weight_kernel, grid=(classes // tile,), in_specs=[pl.Block...  11.8 us
    pallas_call x1, Pallas kernels, place_rows(): pl.pallas_call(functools.partial(place_kernel, peers=peers, run=run, firs...  9.41 us
    all_to_all x2, starting transfers between devices, relay(): return lax.all_to_all(sent, ALL, 0, 0, tiled=True).reshape(-1, width)  8.98 us
    unnamed x24, local copies, waits for them, and re-layouts  6.25 us
  transfers between devices with their start and end apart: 20, of which 10 were waited for; matrix products, arithmetic and copies ran while one was open for 2% of the time, Pallas kernels for 37%

profile of v12, /device:TPU:0, one launch (start us, length us, event | category | flops | bytes accessed | tf_op | source)
XLA Modules:
  0.0 141.5 jit_solution(6161031169156857360)
XLA Ops:
  0.6 0.5 collective-permute-start
  1.1 0.8 constant_dynamic-update-slice_fusion.1
  1.9 0.3 collective-permute-done
  2.2 2.9 %collective-permute-start.1 = (bf16[128,256]{1,0:T(8,128)(2,1)S(1)}, bf16[128,256]{1,0:T(8,128)(2,1)S(1)}, u32[]{:S(2)}, u32[]{:S(2)}) collective-permute-start(bf16[128,256]{1,0:T(8,128)(2,1)S(1)} %get-tuple-element.33), channel_id=1, source_target_pairs={{0,2},{1,3},{2,0},{3,1},{4,6},{5,7},{6,4},{7,5},{8,10},{9,11},{10,... | collective-permute-start | bytes 196616 | tf_op jit(solution)/shard_map/ppermute | solution.py:409
  5.1 1.7 %fetch.3.refs_0_ = bf16[32,160,256]{2,1,0:T(8,128)(2,1)S(1)} custom-call(bf16[32,256,256]{2,1,0:T(8,128)(2,1)} %bitcast.79), custom_call_target="tpu_custom_call" | custom-call | bytes 10485760 | tf_op jit(solution)/shard_map/fetch/pallas_call | solution.py:229
  6.9 0.0 copy-start.1
  6.9 1.5 %copy-done.1 = bf16[32,160,256]{2,1,0:T(8,128)(2,1)} copy-done((bf16[32,160,256]{2,1,0:T(8,128)(2,1)}, bf16[32,160,256]{2,1,0:T(8,128)(2,1)S(1)}, u32[]{:S(2)}) %copy-start.1) | copy-done | bytes 2621464
  8.4 2.6 %collective-permute-start.2 = (bf16[128,256]{1,0:T(8,128)(2,1)S(1)}, bf16[128,256]{1,0:T(8,128)(2,1)S(1)}, u32[]{:S(2)}, u32[]{:S(2)}) collective-permute-start(bf16[128,256]{1,0:T(8,128)(2,1)S(1)} %get-tuple-element.33), channel_id=1, source_target_pairs={{0,4},{1,5},{2,6},{3,7},{4,0},{5,1},{6,2},{7,3},{8,12},{9,13},{10,... | collective-permute-start | bytes 196616 | tf_op jit(solution)/shard_map/ppermute | solution.py:409
  11.0 0.0 collective-permute-start.3
  11.0 0.0 collective-permute-done.1
  11.0 3.5 %collective-permute-done.2 = bf16[128,256]{1,0:T(8,128)(2,1)S(1)} collective-permute-done((bf16[128,256]{1,0:T(8,128)(2,1)S(1)}, bf16[128,256]{1,0:T(8,128)(2,1)S(1)}, u32[]{:S(2)}, u32[]{:S(2)}) %collective-permute-start.2) | collective-permute-done | bytes 65568 | tf_op jit(solution)/shard_map/ppermute | solution.py:409
  14.5 2.6 %collective-permute-done.3 = bf16[128,256]{1,0:T(8,128)(2,1)S(1)} collective-permute-done((bf16[128,256]{1,0:T(8,128)(2,1)S(1)}, bf16[128,256]{1,0:T(8,128)(2,1)S(1)}, u32[]{:S(2)}, u32[]{:S(2)}) %collective-permute-start.3) | collective-permute-done | bytes 65568 | tf_op jit(solution)/shard_map/ppermute | solution.py:409
  17.1 0.7 copy-done.3
  17.9 4.4 %all-to-all-start = ((bf16[32,160,256]{2,1,0:T(8,128)(2,1)}), bf16[32,160,256]{2,1,0:T(8,128)(2,1)}, u32[]{:S(2)}, u32[]{:S(2)}) async-start(bf16[32,160,256]{2,1,0:T(8,128)(2,1)} %release.2), calls=%async_computation | async-start | bytes 5242880 | tf_op jit(solution)/shard_map/all_to_all | solution.py:412
  22.3 0.0 copy-done.6
  22.3 0.1 copy.16.lab_ref
  22.4 0.0 copy-done.8
  22.5 0.0 copy-done.4
  22.6 13.5 %forward_sums.1 = (bf16[512,256]{1,0:T(8,128)(2,1)S(1)}, f32[512,256]{1,0:T(8,128)S(1)}, f32[512,256]{1,0:T(8,128)S(1)}, f32[8,512]{1,0:T(8,128)S(1)}, bf16[8192,256]{1,0:T(8,128)(2,1)}) custom-call(s32[1]{0:T(128)S(6)} %mul.18.base_ref, s32[1]{0:T(128)} %bitcast.1.rep_ref, s32[512,1]{1,0:T(8,128)S(1)} %copy.16.lab_ref, bf16[8192,256]{1,0:T(8,128)(2,1)} %w_ref.3, ...), custom_call_target="tpu_custom_call" | custom-call | flops 12884901888 | bytes 4194304 | tf_op jit(solution)/shard_map/forward_sums/pallas_call | solution.py:110
  36.1 2.7 %collective-permute-start.6 = (f32[24,128]{1,0:T(8,128)S(1)}, f32[24,128]{1,0:T(8,128)S(1)}, u32[]{:S(2)}, u32[]{:S(2)}) collective-permute-start(f32[24,128]{1,0:T(8,128)S(1)} %get-tuple-element.48), channel_id=1, source_target_pairs={{0,24},{8,16},{16,8},{24,0},{1,25},{9,17},{17,9},{25,1},{2,26},{10... | collective-permute-start | bytes 36872 | tf_op jit(solution)/shard_map/ppermute | solution.py:409
  38.8 0.6 collective-permute-start.5
  39.3 0.3 collective-permute-start.4
  39.6 1.5 %collective-permute-done.6 = f32[24,128]{1,0:T(8,128)S(1)} collective-permute-done((f32[24,128]{1,0:T(8,128)S(1)}, f32[24,128]{1,0:T(8,128)S(1)}, u32[]{:S(2)}, u32[]{:S(2)}) %collective-permute-start.6) | collective-permute-done | bytes 12320 | tf_op jit(solution)/shard_map/ppermute | solution.py:409
  41.2 1.4 collective-permute-done.5
  42.5 0.7 collective-permute-done.4
  43.4 0.1 collective-permute-start.7
  43.6 1.5 %fetch.2.refs_1_.refs_0_ = bf16[32,96,256]{2,1,0:T(8,128)(2,1)S(1)} custom-call(bf16[32,256,256]{2,1,0:T(8,128)(2,1)} %bitcast.80, f32[8,512]{1,0:T(8,128)S(1)} %get-tuple-element.11.refs_0_.st_ref), custom_call_target="tpu_custom_call" | custom-call | bytes 6291456 | tf_op jit(solution)/shard_map/fetch/pallas_call | solution.py:229
  45.1 0.0 copy-start
  45.1 0.0 collective-permute-done.7
  45.3 3.3 %collective-permute-start.10 = (f32[24,128]{1,0:T(8,128)S(1)}, f32[24,128]{1,0:T(8,128)S(1)}, u32[]{:S(2)}, u32[]{:S(2)}) collective-permute-start(f32[24,128]{1,0:T(8,128)S(1)} %get-tuple-element.42), channel_id=1, source_target_pairs={{0,6},{1,7},{2,4},{3,5},{4,2},{5,3},{6,0},{7,1},{8,14},{9,15},{10,... | collective-permute-start | bytes 36872 | tf_op jit(solution)/shard_map/ppermute | solution.py:409
  48.6 0.0 collective-permute-start.9
  48.6 1.2 collective-permute-start.8
  49.8 19.8 %collective-permute-done.10 = f32[24,128]{1,0:T(8,128)S(1)} collective-permute-done((f32[24,128]{1,0:T(8,128)S(1)}, f32[24,128]{1,0:T(8,128)S(1)}, u32[]{:S(2)}, u32[]{:S(2)}) %collective-permute-start.10) | collective-permute-done | bytes 12320 | tf_op jit(solution)/shard_map/ppermute | solution.py:409
  69.5 13.6 %collective-permute-done.9 = f32[24,128]{1,0:T(8,128)S(1)} collective-permute-done((f32[24,128]{1,0:T(8,128)S(1)}, f32[24,128]{1,0:T(8,128)S(1)}, u32[]{:S(2)}, u32[]{:S(2)}) %collective-permute-start.9) | collective-permute-done | bytes 12320 | tf_op jit(solution)/shard_map/ppermute | solution.py:409
  83.1 0.0 collective-permute-done.8
  83.2 0.6 fusion.12
  83.8 0.0 copy-done
  83.8 0.0 all-to-all-done
  83.8 4.6 %all-to-all-start.1 = ((bf16[32,96,256]{2,1,0:T(8,128)(2,1)}), bf16[32,96,256]{2,1,0:T(8,128)(2,1)S(1)}, u32[]{:S(2)}, u32[]{:S(2)}) async-start(bf16[32,96,256]{2,1,0:T(8,128)(2,1)} %release.3), calls=%async_computation.1 | async-start | bytes 3145728 | tf_op jit(solution)/shard_map/all_to_all | solution.py:412
  88.4 0.0 copy-done.5
  88.4 0.1 divide_subtract_fusion
  88.6 0.3 collective-permute-start.11
  88.9 11.8 %weight_gradient.1.refs_2_._ = f32[8192,256]{1,0:T(8,128)} custom-call(s32[1]{0:T(128)S(6)} %mul.18.base_ref, bf16[512,256]{1,0:T(8,128)(2,1)S(1)} %get-tuple-element.14.emb_ref, s32[1,512]{1,0:T(1,128)S(1)} %bitcast.78, f32[8,512]{1,0:T(8,128)S(1)} %get-tuple-element.11.refs_0_.st_ref, f32[1,512]{1,0:T(1,128)S(1)} %bitcast.74, bf16[8192,256]{1,0:T(8,128)(2,1)} %w_ref.3), custom_call_target="tpu_custom_call" | custom-call | flops 12884901888 | bytes 12582912 | tf_op jit(solution)/shard_map/weight_gradient/pallas_call | solution.py:178
  100.7 0.0 collective-permute-done.11.refs_1_
  100.8 1.7 %collective-permute-start.12 = (f32[4,64,256]{2,1,0:T(8,128)S(1)}, f32[4,64,256]{2,1,0:T(8,128)S(1)}, u32[]{:S(2)}, u32[]{:S(2)}) collective-permute-start(f32[4,64,256]{2,1,0:T(8,128)S(1)} %join.4.refs_0_), channel_id=1, source_target_pairs={{0,8},{8,0},{16,24},{24,16},{1,9},{9,1},{17,25},{25,17},{2,10},{10... | collective-permute-start | bytes 786440 | tf_op jit(solution)/shard_map/ppermute | solution.py:409
  102.5 1.5 %collective-permute-start.13 = (f32[4,64,256]{2,1,0:T(8,128)S(1)}, f32[4,64,256]{2,1,0:T(8,128)S(1)}, u32[]{:S(2)}, u32[]{:S(2)}) collective-permute-start(f32[4,64,256]{2,1,0:T(8,128)S(1)} %join.4.refs_0_), channel_id=1, source_target_pairs={{0,16},{8,24},{16,0},{24,8},{1,17},{9,25},{17,1},{25,9},{2,18},{10... | collective-permute-start | bytes 786440 | tf_op jit(solution)/shard_map/ppermute | solution.py:409
  104.0 0.3 collective-permute-start.14
  104.4 0.1 dynamic_slice.66.refs_5_
  104.4 9.4 %place_rows.1 = (f32[16384,128]{1,0:T(8,128)S(1)}, f32[8,128]{1,0:T(8,128)S(1)}) custom-call(s32[1]{0:T(128)} %bitcast.me_ref, s32[8192]{0:T(1024)S(1)} %bitcast.72, bf16[5120,256]{1,0:T(8,128)(2,1)} %bitcast.38.row_ref, f32[8192,256]{1,0:T(8,128)} %weight_gradient.1.refs_2_._), custom_call_target="tpu_custom_call" | custom-call | bytes 41943040 | tf_op jit(solution)/shard_map/place_rows/pallas_call | solution.py:322
  113.9 0.0 copy-start.2
  113.9 3.3 %copy-done.2 = f32[16384,128]{1,0:T(8,128)} copy-done((f32[16384,128]{1,0:T(8,128)}, f32[16384,128]{1,0:T(8,128)S(1)}, u32[]{:S(2)}) %copy-start.2) | copy-done | bytes 8388632
  117.1 0.0 collective-permute-done.12.refs_1_
  117.1 1.8 %collective-permute-done.13.refs_2_ = f32[4,64,256]{2,1,0:T(8,128)S(1)} collective-permute-done((f32[4,64,256]{2,1,0:T(8,128)S(1)}, f32[4,64,256]{2,1,0:T(8,128)S(1)}, u32[]{:S(2)}, u32[]{:S(2)}) %collective-permute-start.13) | collective-permute-done | bytes 262176 | tf_op jit(solution)/shard_map/ppermute | solution.py:409
  118.9 2.9 %collective-permute-done.14.refs_3_ = f32[4,64,256]{2,1,0:T(8,128)S(1)} collective-permute-done((f32[4,64,256]{2,1,0:T(8,128)S(1)}, f32[4,64,256]{2,1,0:T(8,128)S(1)}, u32[]{:S(2)}, u32[]{:S(2)}) %collective-permute-start.14) | collective-permute-done | bytes 262176 | tf_op jit(solution)/shard_map/ppermute | solution.py:409
  121.8 0.0 copy-done.7
  121.9 3.2 %collective-permute-start.17 = (f32[64,256]{1,0:T(8,128)S(1)}, f32[64,256]{1,0:T(8,128)S(1)}, u32[]{:S(2)}, u32[]{:S(2)}) collective-permute-start(f32[64,256]{1,0:T(8,128)S(1)} %get-tuple-element.21), channel_id=1, source_target_pairs={{0,6},{1,7},{2,4},{3,5},{4,2},{5,3},{6,0},{7,1},{8,14},{9,15},{10,... | collective-permute-start | bytes 196616 | tf_op jit(solution)/shard_map/ppermute | solution.py:409
  125.2 1.5 %collective-permute-start.16 = (f32[64,256]{1,0:T(8,128)S(1)}, f32[64,256]{1,0:T(8,128)S(1)}, u32[]{:S(2)}, u32[]{:S(2)}) collective-permute-start(f32[64,256]{1,0:T(8,128)S(1)} %get-tuple-element.22), channel_id=1, source_target_pairs={{0,4},{1,5},{2,6},{3,7},{4,0},{5,1},{6,2},{7,3},{8,12},{9,13},{10,... | collective-permute-start | bytes 196616 | tf_op jit(solution)/shard_map/ppermute | solution.py:409
  126.6 0.5 collective-permute-start.15
  127.1 0.0 all-to-all-done.1
  127.1 13.7 %place_and_blend.1 = bf16[8192,256]{1,0:T(8,128)(2,1)} custom-call(s32[1]{0:T(128)} %bitcast.me_ref, s32[8192]{0:T(1024)S(1)} %bitcast.73, bf16[8192,256]{1,0:T(8,128)(2,1)} %get-tuple-element.16.w_ref, bf16[3072,256]{1,0:T(8,128)(2,1)S(1)} %bitcast.71, f32[16384,128]{1,0:T(8,128)} %copy-done.2), custom_call_target="tpu_custom_call" | custom-call | bytes 25165824 | tf_op jit(solution)/shard_map/place_and_blend/pallas_call | solution.py:375
  140.8 0.0 collective-permute-done.17
  140.8 0.0 collective-permute-done.16
  140.8 0.0 collective-permute-done.15
  140.8 0.7 fusion.1
  (36 shorter events, 0.6 us)
Async XLA Ops:
  0.6 1.6 %collective-permute-start = (bf16[64,256]{1,0:T(8,128)(2,1)}, bf16[64,256]{1,0:T(8,128)(2,1)S(1)}, u32[]{:S(2)}, u32[]{:S(2)}) collective-permute-start(bf16[64,256]{1,0:T(8,128)(2,1)} %param.5), channel_id=1, source_target_pairs={{0,1},{1,0},{2,3},{3,2},{4,5},{5,4},{6,7},{7,6},{8,9},{9,8},{10,11... | collective-permute-start | bytes 98312 | tf_op jit(solution)/shard_map/ppermute | solution.py:409
  2.2 8.7 %collective-permute-start.1 = (bf16[128,256]{1,0:T(8,128)(2,1)S(1)}, bf16[128,256]{1,0:T(8,128)(2,1)S(1)}, u32[]{:S(2)}, u32[]{:S(2)}) collective-permute-start(bf16[128,256]{1,0:T(8,128)(2,1)S(1)} %get-tuple-element.33), channel_id=1, source_target_pairs={{0,2},{1,3},{2,0},{3,1},{4,6},{5,7},{6,4},{7,5},{8,10},{9,11},{10,... | collective-permute-start | bytes 196616 | tf_op jit(solution)/shard_map/ppermute | solution.py:409
  6.9 1.5 %copy-start.1 = (bf16[32,160,256]{2,1,0:T(8,128)(2,1)}, bf16[32,160,256]{2,1,0:T(8,128)(2,1)S(1)}, u32[]{:S(2)}) copy-start(bf16[32,160,256]{2,1,0:T(8,128)(2,1)S(1)} %fetch.3.refs_0_) | copy-start | bytes 7864324
  8.4 6.1 %collective-permute-start.2 = (bf16[128,256]{1,0:T(8,128)(2,1)S(1)}, bf16[128,256]{1,0:T(8,128)(2,1)S(1)}, u32[]{:S(2)}, u32[]{:S(2)}) collective-permute-start(bf16[128,256]{1,0:T(8,128)(2,1)S(1)} %get-tuple-element.33), channel_id=1, source_target_pairs={{0,4},{1,5},{2,6},{3,7},{4,0},{5,1},{6,2},{7,3},{8,12},{9,13},{10,... | collective-permute-start | bytes 196616 | tf_op jit(solution)/shard_map/ppermute | solution.py:409
  11.0 6.2 %collective-permute-start.3 = (bf16[128,256]{1,0:T(8,128)(2,1)S(1)}, bf16[128,256]{1,0:T(8,128)(2,1)S(1)}, u32[]{:S(2)}, u32[]{:S(2)}) collective-permute-start(bf16[128,256]{1,0:T(8,128)(2,1)S(1)} %get-tuple-element.33), channel_id=1, source_target_pairs={{0,6},{1,7},{2,4},{3,5},{4,2},{5,3},{6,0},{7,1},{8,14},{9,15},{10,... | collective-permute-start | bytes 196616 | tf_op jit(solution)/shard_map/ppermute | solution.py:409
  17.1 0.7 copy-start.3
  17.8 4.4 %copy-start.6 = (s32[512]{0:T(512)S(1)}, s32[512]{0:T(512)}, u32[]{:S(2)}) copy-start(s32[512]{0:T(512)} %param.6) | copy-start | bytes 6148
  17.8 4.6 %copy-start.8 = (s32[8192]{0:T(1024)S(1)}, s32[8192]{0:T(1024)}, u32[]{:S(2)}) copy-start(s32[8192]{0:T(1024)} %param.9) | copy-start | bytes 98308
  17.9 4.7 %copy-start.4 = (bf16[512,256]{1,0:T(8,128)(2,1)S(1)}, bf16[512,256]{1,0:T(8,128)(2,1)}, u32[]{:S(2)}) copy-start(bf16[512,256]{1,0:T(8,128)(2,1)} %copy-done.3) | copy-start | bytes 786436
  17.9 65.9 %all-to-all-start = ((bf16[32,160,256]{2,1,0:T(8,128)(2,1)}), bf16[32,160,256]{2,1,0:T(8,128)(2,1)}, u32[]{:S(2)}, u32[]{:S(2)}) async-start(bf16[32,160,256]{2,1,0:T(8,128)(2,1)} %release.2), calls=%async_computation | async-start | bytes 5242880 | tf_op jit(solution)/shard_map/all_to_all | solution.py:412
  36.1 5.1 %collective-permute-start.6 = (f32[24,128]{1,0:T(8,128)S(1)}, f32[24,128]{1,0:T(8,128)S(1)}, u32[]{:S(2)}, u32[]{:S(2)}) collective-permute-start(f32[24,128]{1,0:T(8,128)S(1)} %get-tuple-element.48), channel_id=1, source_target_pairs={{0,24},{8,16},{16,8},{24,0},{1,25},{9,17},{17,9},{25,1},{2,26},{10... | collective-permute-start | bytes 36872 | tf_op jit(solution)/shard_map/ppermute | solution.py:409
  38.8 3.8 %collective-permute-start.5 = (f32[24,128]{1,0:T(8,128)S(1)}, f32[24,128]{1,0:T(8,128)S(1)}, u32[]{:S(2)}, u32[]{:S(2)}) collective-permute-start(f32[24,128]{1,0:T(8,128)S(1)} %get-tuple-element.47), channel_id=1, source_target_pairs={{0,16},{8,24},{16,0},{24,8},{1,17},{9,25},{17,1},{25,9},{2,18},{10... | collective-permute-start | bytes 36872 | tf_op jit(solution)/shard_map/ppermute | solution.py:409
  39.3 3.9 %collective-permute-start.4 = (f32[24,128]{1,0:T(8,128)S(1)}, f32[24,128]{1,0:T(8,128)S(1)}, u32[]{:S(2)}, u32[]{:S(2)}) collective-permute-start(f32[24,128]{1,0:T(8,128)S(1)} %get-tuple-element.46), channel_id=1, source_target_pairs={{0,8},{8,0},{16,24},{24,16},{1,9},{9,1},{17,25},{25,17},{2,10},{10... | collective-permute-start | bytes 36872 | tf_op jit(solution)/shard_map/ppermute | solution.py:409
  43.4 1.7 %collective-permute-start.7 = (f32[40,128]{1,0:T(8,128)S(1)}, f32[40,128]{1,0:T(8,128)S(1)}, u32[]{:S(2)}, u32[]{:S(2)}) collective-permute-start(f32[40,128]{1,0:T(8,128)S(1)} %get-tuple-element.44), channel_id=1, source_target_pairs={{0,1},{1,0},{2,3},{3,2},{4,5},{5,4},{6,7},{7,6},{8,9},{9,8},{10,11... | collective-permute-start | bytes 61448 | tf_op jit(solution)/shard_map/ppermute | solution.py:409
  45.1 38.7 %copy-start = (bf16[32,96,256]{2,1,0:T(8,128)(2,1)}, bf16[32,96,256]{2,1,0:T(8,128)(2,1)S(1)}, u32[]{:S(2)}) copy-start(bf16[32,96,256]{2,1,0:T(8,128)(2,1)S(1)} %fetch.2.refs_1_.refs_0_) | copy-start | bytes 4718596
  45.3 24.2 %collective-permute-start.10 = (f32[24,128]{1,0:T(8,128)S(1)}, f32[24,128]{1,0:T(8,128)S(1)}, u32[]{:S(2)}, u32[]{:S(2)}) collective-permute-start(f32[24,128]{1,0:T(8,128)S(1)} %get-tuple-element.42), channel_id=1, source_target_pairs={{0,6},{1,7},{2,4},{3,5},{4,2},{5,3},{6,0},{7,1},{8,14},{9,15},{10,... | collective-permute-start | bytes 36872 | tf_op jit(solution)/shard_map/ppermute | solution.py:409
  48.6 34.6 %collective-permute-start.9 = (f32[24,128]{1,0:T(8,128)S(1)}, f32[24,128]{1,0:T(8,128)S(1)}, u32[]{:S(2)}, u32[]{:S(2)}) collective-permute-start(f32[24,128]{1,0:T(8,128)S(1)} %get-tuple-element.41), channel_id=1, source_target_pairs={{0,4},{1,5},{2,6},{3,7},{4,0},{5,1},{6,2},{7,3},{8,12},{9,13},{10,... | collective-permute-start | bytes 36872 | tf_op jit(solution)/shard_map/ppermute | solution.py:409
  48.6 34.6 %collective-permute-start.8 = (f32[24,128]{1,0:T(8,128)S(1)}, f32[24,128]{1,0:T(8,128)S(1)}, u32[]{:S(2)}, u32[]{:S(2)}) collective-permute-start(f32[24,128]{1,0:T(8,128)S(1)} %get-tuple-element.40), channel_id=1, source_target_pairs={{0,2},{1,3},{2,0},{3,1},{4,6},{5,7},{6,4},{7,5},{8,10},{9,11},{10,... | collective-permute-start | bytes 36872 | tf_op jit(solution)/shard_map/ppermute | solution.py:409
  83.8 4.6 %copy-start.5 = (f32[512]{0:T(512)S(1)}, f32[512]{0:T(512)}, u32[]{:S(2)}) copy-start(f32[512]{0:T(512)} %get-tuple-element.37.refs_1_) | copy-start | bytes 6148
  83.8 43.3 %all-to-all-start.1 = ((bf16[32,96,256]{2,1,0:T(8,128)(2,1)}), bf16[32,96,256]{2,1,0:T(8,128)(2,1)S(1)}, u32[]{:S(2)}, u32[]{:S(2)}) async-start(bf16[32,96,256]{2,1,0:T(8,128)(2,1)} %release.3), calls=%async_computation.1 | async-start | bytes 3145728 | tf_op jit(solution)/shard_map/all_to_all | solution.py:412
  88.6 12.1 %collective-permute-start.11 = (f32[4,64,256]{2,1,0:T(8,128)S(1)}, f32[4,64,256]{2,1,0:T(8,128)S(1)}, u32[]{:S(2)}, u32[]{:S(2)}) collective-permute-start(f32[4,64,256]{2,1,0:T(8,128)S(1)} %get-tuple-element.18), channel_id=1, source_target_pairs={{0,1},{1,0},{2,3},{3,2},{4,5},{5,4},{6,7},{7,6},{8,9},{9,8},{10,11... | collective-permute-start | bytes 786440 | tf_op jit(solution)/shard_map/ppermute | solution.py:409
  100.8 16.4 %collective-permute-start.12 = (f32[4,64,256]{2,1,0:T(8,128)S(1)}, f32[4,64,256]{2,1,0:T(8,128)S(1)}, u32[]{:S(2)}, u32[]{:S(2)}) collective-permute-start(f32[4,64,256]{2,1,0:T(8,128)S(1)} %join.4.refs_0_), channel_id=1, source_target_pairs={{0,8},{8,0},{16,24},{24,16},{1,9},{9,1},{17,25},{25,17},{2,10},{10... | collective-permute-start | bytes 786440 | tf_op jit(solution)/shard_map/ppermute | solution.py:409
  102.5 16.4 %collective-permute-start.13 = (f32[4,64,256]{2,1,0:T(8,128)S(1)}, f32[4,64,256]{2,1,0:T(8,128)S(1)}, u32[]{:S(2)}, u32[]{:S(2)}) collective-permute-start(f32[4,64,256]{2,1,0:T(8,128)S(1)} %join.4.refs_0_), channel_id=1, source_target_pairs={{0,16},{8,24},{16,0},{24,8},{1,17},{9,25},{17,1},{25,9},{2,18},{10... | collective-permute-start | bytes 786440 | tf_op jit(solution)/shard_map/ppermute | solution.py:409
  104.0 17.9 %collective-permute-start.14 = (f32[4,64,256]{2,1,0:T(8,128)S(1)}, f32[4,64,256]{2,1,0:T(8,128)S(1)}, u32[]{:S(2)}, u32[]{:S(2)}) collective-permute-start(f32[4,64,256]{2,1,0:T(8,128)S(1)} %join.4.refs_0_), channel_id=1, source_target_pairs={{0,24},{8,16},{16,8},{24,0},{1,25},{9,17},{17,9},{25,1},{2,26},{10... | collective-permute-start | bytes 786440 | tf_op jit(solution)/shard_map/ppermute | solution.py:409
  104.4 17.4 %copy-start.7 = (f32[64]{0:T(128)}, f32[64]{0:T(128)S(1)}, u32[]{:S(2)}) copy-start(f32[64]{0:T(128)S(1)} %dynamic_slice.66.refs_5_) | copy-start | bytes 772
  113.9 3.3 %copy-start.2 = (f32[16384,128]{1,0:T(8,128)}, f32[16384,128]{1,0:T(8,128)S(1)}, u32[]{:S(2)}) copy-start(f32[16384,128]{1,0:T(8,128)S(1)} %get-tuple-element.17.in_ref) | copy-start | bytes 25165828
  121.9 18.9 %collective-permute-start.17 = (f32[64,256]{1,0:T(8,128)S(1)}, f32[64,256]{1,0:T(8,128)S(1)}, u32[]{:S(2)}, u32[]{:S(2)}) collective-permute-start(f32[64,256]{1,0:T(8,128)S(1)} %get-tuple-element.21), channel_id=1, source_target_pairs={{0,6},{1,7},{2,4},{3,5},{4,2},{5,3},{6,0},{7,1},{8,14},{9,15},{10,... | collective-permute-start | bytes 196616 | tf_op jit(solution)/shard_map/ppermute | solution.py:409
  125.2 15.6 %collective-permute-start.16 = (f32[64,256]{1,0:T(8,128)S(1)}, f32[64,256]{1,0:T(8,128)S(1)}, u32[]{:S(2)}, u32[]{:S(2)}) collective-permute-start(f32[64,256]{1,0:T(8,128)S(1)} %get-tuple-element.22), channel_id=1, source_target_pairs={{0,4},{1,5},{2,6},{3,7},{4,0},{5,1},{6,2},{7,3},{8,12},{9,13},{10,... | collective-permute-start | bytes 196616 | tf_op jit(solution)/shard_map/ppermute | solution.py:409
  126.6 14.2 %collective-permute-start.15 = (f32[64,256]{1,0:T(8,128)S(1)}, f32[64,256]{1,0:T(8,128)S(1)}, u32[]{:S(2)}, u32[]{:S(2)}) collective-permute-start(f32[64,256]{1,0:T(8,128)S(1)} %get-tuple-element.20), channel_id=1, source_target_pairs={{0,2},{1,3},{2,0},{3,1},{4,6},{5,7},{6,4},{7,5},{8,10},{9,11},{10,... | collective-permute-start | bytes 196616 | tf_op jit(solution)/shard_map/ppermute | solution.py:409

commit v13 on v12

--- a/solution.py
+++ b/solution.py
@@ -142,7 +142,52 @@
     )(base, rep, labels.reshape(batch, 1), weights, mixed)
 
 
-def weight_kernel(base_ref, emb_ref, lab_ref, st_ref, tot_ref, w_ref, g_ref, xhat_ref, y_ref, v_ref):
+def split_copies(source_ref, target_ref, sem):
+    lanes = sem.shape[0]
+    size = source_ref.shape[0] // lanes
+    parts = [pl.ds(c * size, size) for c in range(lanes)]
+    return [
+        pltpu.make_async_copy(source_ref.at[part, :], target_ref.at[part, :], sem.at[c])
+        for c, part in enumerate(parts)
+    ]
+
+
+def place_runs(me_ref, slot_ref, row_ref, held_ref, stage_ref, copies, peers, run, first):
+    size = row_ref.shape[0] // peers
+    batch = max(n for n in range(1, 49) if size % n == 0)
+    chunk = max(n for n in range(16, 49, 16) if size % n == 0)
+
+    def prepare(source, carry):
+        for block in range(0, size, chunk):
+            at = pl.multiple_of(source * size + block, chunk)
+            unit, _ = unit_rows(row_ref[pl.ds(at, chunk), :].astype(jnp.float32))
+            stage_ref[pl.ds(2 * at, chunk, stride=2), :] = unit[:, :128]
+            stage_ref[pl.ds(2 * at + 1, chunk, stride=2), :] = unit[:, 128:]
+        return carry
+
+    lax.fori_loop(0, peers, prepare, 0)
+    for copy in copies:
+        copy.wait()
+
+    def place(source, carry):
+        start = (me_ref[0] ^ source) * run + first
+        at = source * size * 2
+        for block in range(0, size, batch):
+            slots = [slot_ref[start + block + v] for v in range(batch)]
+            values = [stage_ref[pl.ds(at + 2 * (block + v), 2), :] for v in range(batch)]
+            for slot, value in zip(slots, values):
+                held_ref[pl.ds(slot, 2), :] = value
+        return carry
+
+    lax.fori_loop(0, peers, place, 0)
+
+
+def weight_kernel(
+    base_ref, me_ref, slot_ref, emb_ref, lab_ref, st_ref, tot_ref, w_ref, *refs, peers, run, starts
+):
+    row_refs, refs = refs[: len(starts)], refs[len(starts) :]
+    g_ref, out_ref, xhat_ref, y_ref, v_ref, held_ref, stage_ref, sem = refs
+    copies = split_copies(held_ref, out_ref, sem)
     step = pl.program_id(0)
     tile = w_ref.shape[0]
     batch = emb_ref.shape[0]
@@ -155,6 +200,10 @@
         total = tot_ref[...]
         y_ref[...] = (xhat.astype(jnp.float32) * column_of(SCALE / total)).astype(jnp.bfloat16)
         v_ref[...] = st_ref[2:3, :] - st_ref[3:4, :] * total
+        for row_ref, first in zip(row_refs, starts):
+            place_runs(me_ref, slot_ref, row_ref, held_ref, stage_ref, [], peers, run, first)
+        for copy in copies:
+            copy.start()
 
     block = math.gcd(tile, 256)
     for first in range(0, tile, block):
@@ -169,38 +218,63 @@
         raw = jnp.dot(d, y_ref[...], preferred_element_type=jnp.float32)
         g_ref[at, :] = off_axis(raw, wwide) * w_inv
 
-
-def weight_gradient(base, emb, labels, stats, totals, weights):
+    @pl.when(step == pl.num_programs(0) - 1)
+    def _():
+        for copy in copies:
+            copy.wait()
+
+
+def weight_gradient(base, me, slots, emb, labels, stats, totals, weights, parts, starts, peers):
     batch, width = emb.shape
     classes = weights.shape[0]
+    largest = max(rows.shape[0] for rows in parts)
+    smem = pl.BlockSpec(memory_space=pltpu.SMEM)
+    vmem = pl.BlockSpec(memory_space=pltpu.VMEM)
     tile = math.gcd(classes, 1024)
     whole = lambda i: (0, 0)
     return pl.pallas_call(
-        weight_kernel,
+        functools.partial(
+            weight_kernel, peers=peers, run=classes // peers, starts=tuple(starts)
+        ),
         grid=(classes // tile,),
         in_specs=[
-            pl.BlockSpec(memory_space=pltpu.SMEM),
+            smem,
+            smem,
+            smem,
             pl.BlockSpec((batch, width), whole),
             pl.BlockSpec((1, batch), whole),
             pl.BlockSpec((8, batch), whole),
             pl.BlockSpec((1, batch), whole),
             pl.BlockSpec((tile, width), lambda i: (i, 0)),
-        ],
-        out_specs=pl.BlockSpec((tile, width), lambda i: (i, 0)),
-        out_shape=pltpu.HBM((classes, width), jnp.float32),
+        ]
+        + [vmem] * len(parts),
+        out_specs=[
+            pl.BlockSpec((tile, width), lambda i: (i, 0)),
+            pl.BlockSpec(memory_space=pl.ANY),
+        ],
+        out_shape=[
+            pltpu.HBM((classes, width), jnp.float32),
+            pltpu.HBM((2 * classes, 128), jnp.float32),
+        ],
         scratch_shapes=[
             pltpu.VMEM((batch, width), jnp.bfloat16),
             pltpu.VMEM((batch, width), jnp.bfloat16),
             pltpu.VMEM((1, batch), jnp.float32),
+            pltpu.VMEM((2 * classes, 128), jnp.float32),
+            pltpu.VMEM((2 * largest, 128), jnp.float32),
+            pltpu.SemaphoreType.DMA((4,)),
         ],
         compiler_params=pltpu.CompilerParams(
-            dimension_semantics=("arbitrary",), vmem_limit_bytes=20 * MIB
+            dimension_semantics=("arbitrary",), vmem_limit_bytes=40 * MIB
         ),
         cost_estimate=pl.CostEstimate(
             flops=12 * batch * classes * width, bytes_accessed=classes * width * 6, transcendentals=0
         ),
         name="weight_gradient",
-    )(base, emb, labels.reshape(1, batch), stats, totals.reshape(1, batch), weights)
+    )(
+        base, me, slots, emb, labels.reshape(1, batch), stats, totals.reshape(1, batch), weights,
+        *parts,
+    )
 
 
 def fetch_kernel(rows_ref, *refs, first):
@@ -278,64 +352,6 @@
     )(value, *tokens)
 
 
-def place_runs(me_ref, slot_ref, row_ref, held_ref, stage_ref, copies, peers, run, first):
-    size = row_ref.shape[0] // peers
-    batch = max(n for n in range(1, 49) if size % n == 0)
-    chunk = max(n for n in range(16, 49, 16) if size % n == 0)
-
-    def prepare(source, carry):
-        for block in range(0, size, chunk):
-            at = pl.multiple_of(source * size + block, chunk)
-            unit, _ = unit_rows(row_ref[pl.ds(at, chunk), :].astype(jnp.float32))
-            stage_ref[pl.ds(2 * at, chunk, stride=2), :] = unit[:, :128]
-            stage_ref[pl.ds(2 * at + 1, chunk, stride=2), :] = unit[:, 128:]
-        return carry
-
-    lax.fori_loop(0, peers, prepare, 0)
-    for copy in copies:
-        copy.wait()
-
-    def place(source, carry):
-        start = (me_ref[0] ^ source) * run + first
-        at = source * size * 2
-        for block in range(0, size, batch):
-            slots = [slot_ref[start + block + v] for v in range(batch)]
-            values = [stage_ref[pl.ds(at + 2 * (block + v), 2), :] for v in range(batch)]
-            for slot, value in zip(slots, values):
-                held_ref[pl.ds(slot, 2), :] = value
-        return carry
-
-    lax.fori_loop(0, peers, place, 0)
-
-
-def place_kernel(
-    me_ref, slot_ref, row_ref, _, held_ref, token_ref, stage_ref, *, peers, run, first
-):
-    token_ref[...] = jnp.zeros_like(token_ref)
-    place_runs(me_ref, slot_ref, row_ref, held_ref, stage_ref, [], peers, run, first)
-
-
-def place_rows(me, slots, rows, after, peers, run, first):
-    smem = pl.BlockSpec(memory_space=pltpu.SMEM)
-    vmem = pl.BlockSpec(memory_space=pltpu.VMEM)
-    anywhere = pl.BlockSpec(memory_space=pl.ANY)
-    return pl.pallas_call(
-        functools.partial(place_kernel, peers=peers, run=run, first=first),
-        in_specs=[smem, smem, vmem, anywhere],
-        out_specs=[vmem, vmem],
-        out_shape=[
-            jax.ShapeDtypeStruct((2 * peers * run, 128), jnp.float32),
-            jax.ShapeDtypeStruct((8, 128), jnp.float32),
-        ],
-        scratch_shapes=[pltpu.VMEM((2 * rows.shape[0], 128), jnp.float32)],
-        compiler_params=pltpu.CompilerParams(vmem_limit_bytes=24 * MIB),
-        cost_estimate=pl.CostEstimate(
-            flops=0, bytes_accessed=32 * rows.shape[0] * rows.shape[1], transcendentals=0
-        ),
-        name="place_rows",
-    )(me, slots, rows, after)
-
-
 def blend_kernel(
     me_ref, slot_ref, w_ref, row_ref, in_ref, o_ref, held_ref, stage_ref, sem, *, peers, run, first
 ):
@@ -344,13 +360,7 @@
 
     @pl.when(step == 0)
     def _():
-        lanes = sem.shape[0]
-        part = held_ref.shape[0] // lanes
-        parts = [pl.ds(c * part, part) for c in range(lanes)]
-        copies = [
-            pltpu.make_async_copy(in_ref.at[at, :], held_ref.at[at, :], sem.at[c])
-            for c, at in enumerate(parts)
-        ]
+        copies = split_copies(in_ref, held_ref, sem)
         for copy in copies:
             copy.start()
         place_runs(me_ref, slot_ref, row_ref, held_ref, stage_ref, copies, peers, run, first)
@@ -413,10 +423,12 @@
 
     weights = in_hbm(class_weights)
     runs = in_hbm(centroids.reshape(peers, run, width))
-    cut = run * 5 // 8 // 16 * 16
+    cut_a = max(16, run * 3 // 16 // 16 * 16)
+    cut = run - max(16, run * 5 // 16 // 16 * 16)
+    rows_a = relay(fetch(runs, 0, cut_a, []))
     mixed = jnp.concatenate([swap(embeddings, "rep", c) for c in range(2)])
     mixed = jnp.concatenate([swap(mixed, "rep", 2 * z) for z in range(reps // 2)])
-    rows_a = relay(released(fetch(runs, 0, cut, []), [mixed]))
+    rows_b = relay(released(fetch(runs, cut_a, cut - cut_a, []), [mixed, rows_a]))
     emb, a, b, stats, what = forward(base, rep.reshape(1), mixed, reps, labels, weights)
 
     half = reps // 2
@@ -437,8 +449,8 @@
     wanted = wanted.reshape(groups, half, 2, run)
     wanted = [index(wanted, core ^ c, 2, False) for c in range(2)]
     sums, wanted = share_out(sums, wanted, "rep", range(2))
-    sent_b = fetch(runs, cut, run - cut, [stats])
-    sums = join([sums.reshape(-1, 128)], [sent_b]).reshape(-1)
+    sent = fetch(runs, cut, run - cut, [stats])
+    sums = join([sums.reshape(-1, 128)], [sent]).reshape(-1)
     wanted = wanted.reshape(2, groups, half, run)
     wanted = [index(wanted, deep ^ z, 2, False) for z in range(half)]
     sums, slots = share_out(sums, wanted, "rep", range(0, reps, 2))
@@ -447,19 +459,19 @@
     losses = jnp.log(total) - target
     loss = lax.dynamic_slice_in_dim(losses, rep * rows_local, rows_local, 0)
 
-    rows_b = relay(released(sent_b, [total]))
-    weight_grad = weight_gradient(base, emb, labels, stats, total, weights)
-    done = in_hbm(weight_grad)
-    held, token = place_rows(me, slots, rows_a, done, peers, run, 0)
+    rows_c = relay(released(sent, [total]))
+    weight_grad, held = weight_gradient(
+        base, me, slots, emb, labels, stats, total, weights, [rows_a, rows_b], [0, cut_a], peers
+    )
 
     grad = (a / total[:, None] - b).reshape(half, 2, rows_local, width)
-    grad = join([swap(index(grad, core ^ c, 1, False), "rep", c) for c in range(2)], [done])
-    grad = join([swap(grad, "grp", j) for j in range(groups)], [token, loss])
+    grad = sum(swap(index(grad, core ^ c, 1, False), "rep", c) for c in range(2))
+    grad = join([swap(grad, "grp", j) for j in range(groups)], [in_hbm(weight_grad), loss])
     embedding_gradient = sum(
         swap(index(grad, deep ^ z, 0, False), "rep", 2 * z) for z in range(half)
     )
 
-    refreshed = place_and_blend(me, slots, rows_b, in_hbm(held), in_hbm(what), peers, run, cut)
+    refreshed = place_and_blend(me, slots, rows_c, in_hbm(held), in_hbm(what), peers, run, cut)
     return (loss, embedding_gradient, weight_grad, refreshed)
 
 

time: 142 us -> 146 us (1.028)
  Pallas kernels: 51.8 us -> 57.1 us
  starting transfers between devices: 32.1 us -> 36.6 us
  waiting for transfers between devices: 48.2 us -> 44.6 us
  local copies, waits for them, and re-layouts: 6.76 us -> 3.59 us
    all_to_all x2 -> x3, starting transfers between devices: 8.98 us -> 15.5 us  [relay(): return lax.all_to_all(sent, ALL, 0, 0, tiled=True).reshape(-1, width)]
    pallas_call x2 -> x1, Pallas kernels: 21.2 us -> 24.9 us  [weight_gradient(): pl.pallas_call(functools.partial(weight_kernel, peers=peers, run=classes...]
    ppermute x18, waiting for transfers between devices: 48.2 us -> 44.6 us  [swap(): lax.ppermute(value, axis, [(i, i ^ k) for i in range(size)])]
    unnamed x24 -> x30, local copies, waits for them, and re-layouts: 6.25 us -> 3.1 us
    ppermute x18, starting transfers between devices: 23.2 us -> 21.1 us  [swap(): lax.ppermute(value, axis, [(i, i ^ k) for i in range(size)])]
    pallas_call x2 -> x3, Pallas kernels: 3.26 us -> 5.21 us  [fetch(): pl.pallas_call(functools.partial(fetch_kernel, first=first), in_specs=[hb...]
  transfers between devices with their start and end apart: 20 -> 21, of which waited for: 10 -> 9; matrix products, arithmetic and copies ran while one was open for 2% -> 2% of each run, Pallas kernels for 37% -> 38%
where the time goes in v13:
time: 146 us
  Pallas kernels  57.1 us (39%)
  waiting for transfers between devices  44.6 us (31%)
  starting transfers between devices  36.6 us (25%)
  local copies, waits for them, and re-layouts  3.59 us (2%)
  other arithmetic  2.57 us (2%)
    ppermute x18, waiting for transfers between devices, swap(): lax.ppermute(value, axis, [(i, i ^ k) for i in range(size)])  44.6 us
    pallas_call x1, Pallas kernels, weight_gradient(): pl.pallas_call(functools.partial(weight_kernel, peers=peers, run=classes...  24.9 us
    ppermute x18, starting transfers between devices, swap(): lax.ppermute(value, axis, [(i, i ^ k) for i in range(size)])  21.1 us
    all_to_all x3, starting transfers between devices, relay(): return lax.all_to_all(sent, ALL, 0, 0, tiled=True).reshape(-1, width)  15.5 us
    pallas_call x1, Pallas kernels, forward(): pl.pallas_call(functools.partial(forward_kernel, classes=classes, reps=re...  13.6 us
    pallas_call x1, Pallas kernels, place_and_blend(): pl.pallas_call(functools.partial(blend_kernel, peers=peers, run=run, firs...  13.3 us
    pallas_call x3, Pallas kernels, fetch(): pl.pallas_call(functools.partial(fetch_kernel, first=first), in_specs=[hb...  5.21 us
    unnamed x30, local copies, waits for them, and re-layouts  3.1 us
  transfers between devices with their start and end apart: 21, of which 9 were waited for; matrix products, arithmetic and copies ran while one was open for 2% of the time, Pallas kernels for 38%

profile of v13, /device:TPU:0, one launch (start us, length us, event | category | flops | bytes accessed | tf_op | source)
XLA Modules:
  0.0 145.6 jit_solution(5863523827761104946)
XLA Ops:
  0.6 2.2 %fetch.4 = bf16[32,48,256]{2,1,0:T(8,128)(2,1)} custom-call(bf16[32,256,256]{2,1,0:T(8,128)(2,1)} %bitcast.82), custom_call_target="tpu_custom_call" | custom-call | bytes 3145728 | tf_op jit(solution)/shard_map/fetch/pallas_call | solution.py:303
  2.8 7.3 %all-to-all-start = ((bf16[32,48,256]{2,1,0:T(8,128)(2,1)}), bf16[32,48,256]{2,1,0:T(8,128)(2,1)S(1)}, u32[]{:S(2)}, u32[]{:S(2)}) async-start(bf16[32,48,256]{2,1,0:T(8,128)(2,1)} %fetch.4), calls=%async_computation | async-start | bytes 1572864 | tf_op jit(solution)/shard_map/all_to_all | solution.py:422
  10.1 0.3 collective-permute-start
  10.5 1.0 collective-permute-done
  11.4 1.8 %collective-permute-start.1 = (bf16[128,256]{1,0:T(8,128)(2,1)S(1)}, bf16[128,256]{1,0:T(8,128)(2,1)S(1)}, u32[]{:S(2)}, u32[]{:S(2)}) collective-permute-start(bf16[128,256]{1,0:T(8,128)(2,1)S(1)} %get-tuple-element.31), channel_id=1, source_target_pairs={{0,2},{1,3},{2,0},{3,1},{4,6},{5,7},{6,4},{7,5},{8,10},{9,11},{10,... | collective-permute-start | bytes 196616 | tf_op jit(solution)/shard_map/ppermute | solution.py:419
  13.2 1.6 %fetch.5.refs_0_ = bf16[32,128,256]{2,1,0:T(8,128)(2,1)S(1)} custom-call(bf16[32,256,256]{2,1,0:T(8,128)(2,1)} %bitcast.83), custom_call_target="tpu_custom_call" | custom-call | bytes 8388608 | tf_op jit(solution)/shard_map/fetch/pallas_call | solution.py:303
  14.8 0.0 copy-start.1
  14.8 1.3 copy-done.1
  16.1 2.4 %collective-permute-start.2 = (bf16[128,256]{1,0:T(8,128)(2,1)S(1)}, bf16[128,256]{1,0:T(8,128)(2,1)S(1)}, u32[]{:S(2)}, u32[]{:S(2)}) collective-permute-start(bf16[128,256]{1,0:T(8,128)(2,1)S(1)} %get-tuple-element.31), channel_id=1, source_target_pairs={{0,4},{1,5},{2,6},{3,7},{4,0},{5,1},{6,2},{7,3},{8,12},{9,13},{10,... | collective-permute-start | bytes 196616 | tf_op jit(solution)/shard_map/ppermute | solution.py:419
  18.5 0.2 collective-permute-start.3
  18.7 6.5 %collective-permute-done.1 = bf16[128,256]{1,0:T(8,128)(2,1)S(1)} collective-permute-done((bf16[128,256]{1,0:T(8,128)(2,1)S(1)}, bf16[128,256]{1,0:T(8,128)(2,1)S(1)}, u32[]{:S(2)}, u32[]{:S(2)}) %collective-permute-start.1) | collective-permute-done | bytes 65568 | tf_op jit(solution)/shard_map/ppermute | solution.py:419
  25.2 10.3 %collective-permute-done.2 = bf16[128,256]{1,0:T(8,128)(2,1)S(1)} collective-permute-done((bf16[128,256]{1,0:T(8,128)(2,1)S(1)}, bf16[128,256]{1,0:T(8,128)(2,1)S(1)}, u32[]{:S(2)}, u32[]{:S(2)}) %collective-permute-start.2) | collective-permute-done | bytes 65568 | tf_op jit(solution)/shard_map/ppermute | solution.py:419
  35.5 0.0 collective-permute-done.3
  35.5 0.0 all-to-all-done
  35.5 0.0 copy-start.2
  35.5 0.7 copy-done.4
  36.2 0.3 copy-done.2
  36.5 3.8 %all-to-all-start.1 = ((bf16[32,128,256]{2,1,0:T(8,128)(2,1)}), bf16[32,128,256]{2,1,0:T(8,128)(2,1)}, u32[]{:S(2)}, u32[]{:S(2)}) async-start(bf16[32,128,256]{2,1,0:T(8,128)(2,1)} %release.2), calls=%async_computation.1 | async-start | bytes 4194304 | tf_op jit(solution)/shard_map/all_to_all | solution.py:422
  40.3 0.1 copy.16.lab_ref
  40.5 0.0 copy-done.11
  40.6 13.6 %forward_sums.1 = (bf16[512,256]{1,0:T(8,128)(2,1)S(1)}, f32[512,256]{1,0:T(8,128)S(1)}, f32[512,256]{1,0:T(8,128)S(1)}, f32[8,512]{1,0:T(8,128)S(1)}, bf16[8192,256]{1,0:T(8,128)(2,1)}) custom-call(s32[1]{0:T(128)S(6)} %mul.18.base_ref, s32[1]{0:T(128)} %bitcast.1.rep_ref, s32[512,1]{1,0:T(8,128)S(1)} %copy.16.lab_ref, bf16[8192,256]{1,0:T(8,128)(2,1)} %w_ref.3, ...), custom_call_target="tpu_custom_call" | custom-call | flops 12884901888 | bytes 4194304 | tf_op jit(solution)/shard_map/forward_sums/pallas_call | solution.py:110
  54.2 2.7 %collective-permute-start.6 = (f32[24,128]{1,0:T(8,128)S(1)}, f32[24,128]{1,0:T(8,128)S(1)}, u32[]{:S(2)}, u32[]{:S(2)}) collective-permute-start(f32[24,128]{1,0:T(8,128)S(1)} %get-tuple-element.46), channel_id=1, source_target_pairs={{0,24},{8,16},{16,8},{24,0},{1,25},{9,17},{17,9},{25,1},{2,26},{10... | collective-permute-start | bytes 36872 | tf_op jit(solution)/shard_map/ppermute | solution.py:419
  56.9 0.6 collective-permute-start.5
  57.4 0.3 collective-permute-start.4
  57.8 1.2 collective-permute-done.6
  59.0 1.6 %collective-permute-done.5 = f32[24,128]{1,0:T(8,128)S(1)} collective-permute-done((f32[24,128]{1,0:T(8,128)S(1)}, f32[24,128]{1,0:T(8,128)S(1)}, u32[]{:S(2)}, u32[]{:S(2)}) %collective-permute-start.5) | collective-permute-done | bytes 12320 | tf_op jit(solution)/shard_map/ppermute | solution.py:419
  60.6 0.7 collective-permute-done.4
  61.4 0.1 collective-permute-start.7
  61.6 1.5 %fetch.3.refs_1_.refs_0_ = bf16[32,80,256]{2,1,0:T(8,128)(2,1)S(1)} custom-call(bf16[32,256,256]{2,1,0:T(8,128)(2,1)} %bitcast.84, f32[8,512]{1,0:T(8,128)S(1)} %get-tuple-element.11.refs_0_.st_ref), custom_call_target="tpu_custom_call" | custom-call | bytes 5242880 | tf_op jit(solution)/shard_map/fetch/pallas_call | solution.py:303
  63.0 0.0 collective-permute-done.7
  63.2 0.0 copy-start.3
  63.2 3.3 %collective-permute-start.10 = (f32[24,128]{1,0:T(8,128)S(1)}, f32[24,128]{1,0:T(8,128)S(1)}, u32[]{:S(2)}, u32[]{:S(2)}) collective-permute-start(f32[24,128]{1,0:T(8,128)S(1)} %get-tuple-element.40), channel_id=1, source_target_pairs={{0,6},{1,7},{2,4},{3,5},{4,2},{5,3},{6,0},{7,1},{8,14},{9,15},{10,... | collective-permute-start | bytes 36872 | tf_op jit(solution)/shard_map/ppermute | solution.py:419
  66.5 0.0 collective-permute-start.9
  66.5 1.2 collective-permute-start.8
  67.7 11.4 %collective-permute-done.10 = f32[24,128]{1,0:T(8,128)S(1)} collective-permute-done((f32[24,128]{1,0:T(8,128)S(1)}, f32[24,128]{1,0:T(8,128)S(1)}, u32[]{:S(2)}, u32[]{:S(2)}) %collective-permute-start.10) | collective-permute-done | bytes 12320 | tf_op jit(solution)/shard_map/ppermute | solution.py:419
  79.1 10.8 %collective-permute-done.9 = f32[24,128]{1,0:T(8,128)S(1)} collective-permute-done((f32[24,128]{1,0:T(8,128)S(1)}, f32[24,128]{1,0:T(8,128)S(1)}, u32[]{:S(2)}, u32[]{:S(2)}) %collective-permute-start.9) | collective-permute-done | bytes 12320 | tf_op jit(solution)/shard_map/ppermute | solution.py:419
  89.9 0.0 collective-permute-done.8
  90.0 0.6 fusion.12
  90.5 0.0 all-to-all-done.1
  90.5 4.4 %all-to-all-start.2 = ((bf16[32,80,256]{2,1,0:T(8,128)(2,1)}), bf16[32,80,256]{2,1,0:T(8,128)(2,1)S(1)}, u32[]{:S(2)}, u32[]{:S(2)}) async-start(bf16[32,80,256]{2,1,0:T(8,128)(2,1)} %release.3), calls=%async_computation.2 | async-start | bytes 2621440 | tf_op jit(solution)/shard_map/all_to_all | solution.py:422
  94.9 0.1 divide_subtract_fusion
  95.1 0.0 copy-start.9
  95.1 0.8 copy-done.9
  95.9 0.3 collective-permute-start.11
  96.3 0.1 dynamic_slice.66.refs_5_
  96.4 1.1 collective-permute-done.11
  97.5 1.0 bitcast_add_fusion.refs_0_
  98.5 1.8 %collective-permute-start.12 = (f32[4,64,256]{2,1,0:T(8,128)S(1)}, f32[4,64,256]{2,1,0:T(8,128)S(1)}, u32[]{:S(2)}, u32[]{:S(2)}) collective-permute-start(f32[4,64,256]{2,1,0:T(8,128)S(1)} %bitcast_add_fusion.refs_0_), channel_id=1, source_target_pairs={{0,8},{8,0},{16,24},{24,16},{1,9},{9,1},{17,25},{25,17},{2,10},{10... | collective-permute-start | bytes 786440 | tf_op jit(solution)/shard_map/ppermute | solution.py:419
  100.3 1.5 %collective-permute-start.13 = (f32[4,64,256]{2,1,0:T(8,128)S(1)}, f32[4,64,256]{2,1,0:T(8,128)S(1)}, u32[]{:S(2)}, u32[]{:S(2)}) collective-permute-start(f32[4,64,256]{2,1,0:T(8,128)S(1)} %bitcast_add_fusion.refs_0_), channel_id=1, source_target_pairs={{0,16},{8,24},{16,0},{24,8},{1,17},{9,25},{17,1},{25,9},{2,18},{10... | collective-permute-start | bytes 786440 | tf_op jit(solution)/shard_map/ppermute | solution.py:419
  101.8 0.3 collective-permute-start.14
  102.0 24.9 %weight_gradient.1 = (f32[8192,256]{1,0:T(8,128)}, f32[16384,128]{1,0:T(8,128)}) custom-call(s32[1]{0:T(128)S(6)} %mul.18.base_ref, s32[1]{0:T(128)} %bitcast.me_ref, s32[8192]{0:T(1024)S(1)} %bitcast.75, bf16[512,256]{1,0:T(8,128)(2,1)S(1)} %get-tuple-element.14.emb_ref, s32[1,512]{1,0:T(1,128)S(1)} %bitcast.81, ...), custom_call_target="tpu_custom_call" | custom-call | flops 12884901888 | bytes 12582912 | tf_op jit(solution)/shard_map/weight_gradient/pallas_call | solution.py:235
  127.0 0.0 collective-permute-done.12.refs_1_
  127.0 0.0 collective-permute-done.13.refs_2_
  127.0 0.0 collective-permute-done.14.refs_3_
  127.0 0.1 join.3
  127.1 3.7 %collective-permute-start.17 = (f32[64,256]{1,0:T(8,128)S(1)}, f32[64,256]{1,0:T(8,128)S(1)}, u32[]{:S(2)}, u32[]{:S(2)}) collective-permute-start(f32[64,256]{1,0:T(8,128)S(1)} %get-tuple-element.19), channel_id=1, source_target_pairs={{0,6},{1,7},{2,4},{3,5},{4,2},{5,3},{6,0},{7,1},{8,14},{9,15},{10,... | collective-permute-start | bytes 196616 | tf_op jit(solution)/shard_map/ppermute | solution.py:419
  130.8 0.0 collective-permute-start.16
  130.8 0.8 collective-permute-start.15
  131.6 0.0 all-to-all-done.2
  131.6 13.3 %place_and_blend.1 = bf16[8192,256]{1,0:T(8,128)(2,1)} custom-call(s32[1]{0:T(128)} %bitcast.me_ref, s32[8192]{0:T(1024)S(1)} %bitcast.76, bf16[8192,256]{1,0:T(8,128)(2,1)} %get-tuple-element.16.w_ref, bf16[2560,256]{1,0:T(8,128)(2,1)S(1)} %bitcast.72, f32[16384,128]{1,0:T(8,128)} %get-tuple-element.17.in_ref), custom_call_target="tpu_custom_call" | custom-call | bytes 25165824 | tf_op jit(solution)/shard_map/place_and_blend/pallas_call | solution.py:385
  144.9 0.0 collective-permute-done.17
  144.9 0.0 collective-permute-done.16
  144.9 0.0 collective-permute-done.15
  144.9 0.7 fusion.1
  (44 shorter events, 0.5 us)
Async XLA Ops:
  0.6 9.5 %copy-start.10 = (bf16[64,256]{1,0:T(8,128)(2,1)S(1)}, bf16[64,256]{1,0:T(8,128)(2,1)}, u32[]{:S(2)}) copy-start(bf16[64,256]{1,0:T(8,128)(2,1)} %param.5) | copy-start | bytes 98308
  2.8 32.7 %all-to-all-start = ((bf16[32,48,256]{2,1,0:T(8,128)(2,1)}), bf16[32,48,256]{2,1,0:T(8,128)(2,1)S(1)}, u32[]{:S(2)}, u32[]{:S(2)}) async-start(bf16[32,48,256]{2,1,0:T(8,128)(2,1)} %fetch.4), calls=%async_computation | async-start | bytes 1572864 | tf_op jit(solution)/shard_map/all_to_all | solution.py:422
  10.1 1.3 collective-permute-start
  11.4 13.8 %collective-permute-start.1 = (bf16[128,256]{1,0:T(8,128)(2,1)S(1)}, bf16[128,256]{1,0:T(8,128)(2,1)S(1)}, u32[]{:S(2)}, u32[]{:S(2)}) collective-permute-start(bf16[128,256]{1,0:T(8,128)(2,1)S(1)} %get-tuple-element.31), channel_id=1, source_target_pairs={{0,2},{1,3},{2,0},{3,1},{4,6},{5,7},{6,4},{7,5},{8,10},{9,11},{10,... | collective-permute-start | bytes 196616 | tf_op jit(solution)/shard_map/ppermute | solution.py:419
  14.8 1.3 copy-start.1
  16.1 19.4 %collective-permute-start.2 = (bf16[128,256]{1,0:T(8,128)(2,1)S(1)}, bf16[128,256]{1,0:T(8,128)(2,1)S(1)}, u32[]{:S(2)}, u32[]{:S(2)}) collective-permute-start(bf16[128,256]{1,0:T(8,128)(2,1)S(1)} %get-tuple-element.31), channel_id=1, source_target_pairs={{0,4},{1,5},{2,6},{3,7},{4,0},{5,1},{6,2},{7,3},{8,12},{9,13},{10,... | collective-permute-start | bytes 196616 | tf_op jit(solution)/shard_map/ppermute | solution.py:419
  18.5 17.0 %collective-permute-start.3 = (bf16[128,256]{1,0:T(8,128)(2,1)S(1)}, bf16[128,256]{1,0:T(8,128)(2,1)S(1)}, u32[]{:S(2)}, u32[]{:S(2)}) collective-permute-start(bf16[128,256]{1,0:T(8,128)(2,1)S(1)} %get-tuple-element.31), channel_id=1, source_target_pairs={{0,6},{1,7},{2,4},{3,5},{4,2},{5,3},{6,0},{7,1},{8,14},{9,15},{10,... | collective-permute-start | bytes 196616 | tf_op jit(solution)/shard_map/ppermute | solution.py:419
  35.5 0.7 copy-start.4
  35.5 0.9 copy-start.2
  36.5 3.8 %copy-start.7 = (s32[512]{0:T(512)S(1)}, s32[512]{0:T(512)}, u32[]{:S(2)}) copy-start(s32[512]{0:T(512)} %param.6) | copy-start | bytes 6148
  36.5 4.0 %copy-start.11 = (s32[8192]{0:T(1024)S(1)}, s32[8192]{0:T(1024)}, u32[]{:S(2)}) copy-start(s32[8192]{0:T(1024)} %param.9) | copy-start | bytes 98308
  36.5 4.1 %copy-start.5 = (bf16[512,256]{1,0:T(8,128)(2,1)S(1)}, bf16[512,256]{1,0:T(8,128)(2,1)}, u32[]{:S(2)}) copy-start(bf16[512,256]{1,0:T(8,128)(2,1)} %copy-done.4) | copy-start | bytes 786436
  36.5 54.1 %all-to-all-start.1 = ((bf16[32,128,256]{2,1,0:T(8,128)(2,1)}), bf16[32,128,256]{2,1,0:T(8,128)(2,1)}, u32[]{:S(2)}, u32[]{:S(2)}) async-start(bf16[32,128,256]{2,1,0:T(8,128)(2,1)} %release.2), calls=%async_computation.1 | async-start | bytes 4194304 | tf_op jit(solution)/shard_map/all_to_all | solution.py:422
  54.2 4.8 %collective-permute-start.6 = (f32[24,128]{1,0:T(8,128)S(1)}, f32[24,128]{1,0:T(8,128)S(1)}, u32[]{:S(2)}, u32[]{:S(2)}) collective-permute-start(f32[24,128]{1,0:T(8,128)S(1)} %get-tuple-element.46), channel_id=1, source_target_pairs={{0,24},{8,16},{16,8},{24,0},{1,25},{9,17},{17,9},{25,1},{2,26},{10... | collective-permute-start | bytes 36872 | tf_op jit(solution)/shard_map/ppermute | solution.py:419
  56.9 3.7 %collective-permute-start.5 = (f32[24,128]{1,0:T(8,128)S(1)}, f32[24,128]{1,0:T(8,128)S(1)}, u32[]{:S(2)}, u32[]{:S(2)}) collective-permute-start(f32[24,128]{1,0:T(8,128)S(1)} %get-tuple-element.45), channel_id=1, source_target_pairs={{0,16},{8,24},{16,0},{24,8},{1,17},{9,25},{17,1},{25,9},{2,18},{10... | collective-permute-start | bytes 36872 | tf_op jit(solution)/shard_map/ppermute | solution.py:419
  57.4 3.8 %collective-permute-start.4 = (f32[24,128]{1,0:T(8,128)S(1)}, f32[24,128]{1,0:T(8,128)S(1)}, u32[]{:S(2)}, u32[]{:S(2)}) collective-permute-start(f32[24,128]{1,0:T(8,128)S(1)} %get-tuple-element.44), channel_id=1, source_target_pairs={{0,8},{8,0},{16,24},{24,16},{1,9},{9,1},{17,25},{25,17},{2,10},{10... | collective-permute-start | bytes 36872 | tf_op jit(solution)/shard_map/ppermute | solution.py:419
  61.4 1.6 %collective-permute-start.7 = (f32[40,128]{1,0:T(8,128)S(1)}, f32[40,128]{1,0:T(8,128)S(1)}, u32[]{:S(2)}, u32[]{:S(2)}) collective-permute-start(f32[40,128]{1,0:T(8,128)S(1)} %get-tuple-element.42), channel_id=1, source_target_pairs={{0,1},{1,0},{2,3},{3,2},{4,5},{5,4},{6,7},{7,6},{8,9},{9,8},{10,11... | collective-permute-start | bytes 61448 | tf_op jit(solution)/shard_map/ppermute | solution.py:419
  63.0 27.5 %copy-start = (bf16[32,80,256]{2,1,0:T(8,128)(2,1)}, bf16[32,80,256]{2,1,0:T(8,128)(2,1)S(1)}, u32[]{:S(2)}) copy-start(bf16[32,80,256]{2,1,0:T(8,128)(2,1)S(1)} %fetch.3.refs_1_.refs_0_) | copy-start | bytes 3932164
  63.2 38.8 %copy-start.3 = (bf16[32,48,256]{2,1,0:T(8,128)(2,1)S(1)}, bf16[32,48,256]{2,1,0:T(8,128)(2,1)}, u32[]{:S(2)}) copy-start(bf16[32,48,256]{2,1,0:T(8,128)(2,1)} %copy-done.2) | copy-start | bytes 2359300
  63.2 15.9 %collective-permute-start.10 = (f32[24,128]{1,0:T(8,128)S(1)}, f32[24,128]{1,0:T(8,128)S(1)}, u32[]{:S(2)}, u32[]{:S(2)}) collective-permute-start(f32[24,128]{1,0:T(8,128)S(1)} %get-tuple-element.40), channel_id=1, source_target_pairs={{0,6},{1,7},{2,4},{3,5},{4,2},{5,3},{6,0},{7,1},{8,14},{9,15},{10,... | collective-permute-start | bytes 36872 | tf_op jit(solution)/shard_map/ppermute | solution.py:419
  66.5 23.4 %collective-permute-start.9 = (f32[24,128]{1,0:T(8,128)S(1)}, f32[24,128]{1,0:T(8,128)S(1)}, u32[]{:S(2)}, u32[]{:S(2)}) collective-permute-start(f32[24,128]{1,0:T(8,128)S(1)} %get-tuple-element.39), channel_id=1, source_target_pairs={{0,4},{1,5},{2,6},{3,7},{4,0},{5,1},{6,2},{7,3},{8,12},{9,13},{10,... | collective-permute-start | bytes 36872 | tf_op jit(solution)/shard_map/ppermute | solution.py:419
  66.5 23.4 %collective-permute-start.8 = (f32[24,128]{1,0:T(8,128)S(1)}, f32[24,128]{1,0:T(8,128)S(1)}, u32[]{:S(2)}, u32[]{:S(2)}) collective-permute-start(f32[24,128]{1,0:T(8,128)S(1)} %get-tuple-element.38), channel_id=1, source_target_pairs={{0,2},{1,3},{2,0},{3,1},{4,6},{5,7},{6,4},{7,5},{8,10},{9,11},{10,... | collective-permute-start | bytes 36872 | tf_op jit(solution)/shard_map/ppermute | solution.py:419
  90.5 4.4 %copy-start.6 = (f32[512]{0:T(512)S(1)}, f32[512]{0:T(512)}, u32[]{:S(2)}) copy-start(f32[512]{0:T(512)} %get-tuple-element.35.refs_1_) | copy-start | bytes 6148
  90.5 41.0 %all-to-all-start.2 = ((bf16[32,80,256]{2,1,0:T(8,128)(2,1)}), bf16[32,80,256]{2,1,0:T(8,128)(2,1)S(1)}, u32[]{:S(2)}, u32[]{:S(2)}) async-start(bf16[32,80,256]{2,1,0:T(8,128)(2,1)} %release.3), calls=%async_computation.2 | async-start | bytes 2621440 | tf_op jit(solution)/shard_map/all_to_all | solution.py:422
  95.1 0.8 copy-start.9
  95.9 1.6 %collective-permute-start.11 = (f32[4,64,256]{2,1,0:T(8,128)S(1)}, f32[4,64,256]{2,1,0:T(8,128)S(1)}, u32[]{:S(2)}, u32[]{:S(2)}) collective-permute-start(f32[4,64,256]{2,1,0:T(8,128)S(1)} %dynamic-slice_bitcast_fusion), channel_id=1, source_target_pairs={{0,1},{1,0},{2,3},{3,2},{4,5},{5,4},{6,7},{7,6},{8,9},{9,8},{10,11... | collective-permute-start | bytes 786440 | tf_op jit(solution)/shard_map/ppermute | solution.py:419
  96.4 30.7 %copy-start.8 = (f32[64]{0:T(128)}, f32[64]{0:T(128)S(1)}, u32[]{:S(2)}) copy-start(f32[64]{0:T(128)S(1)} %dynamic_slice.66.refs_5_) | copy-start | bytes 772
  98.5 28.5 %collective-permute-start.12 = (f32[4,64,256]{2,1,0:T(8,128)S(1)}, f32[4,64,256]{2,1,0:T(8,128)S(1)}, u32[]{:S(2)}, u32[]{:S(2)}) collective-permute-start(f32[4,64,256]{2,1,0:T(8,128)S(1)} %bitcast_add_fusion.refs_0_), channel_id=1, source_target_pairs={{0,8},{8,0},{16,24},{24,16},{1,9},{9,1},{17,25},{25,17},{2,10},{10... | collective-permute-start | bytes 786440 | tf_op jit(solution)/shard_map/ppermute | solution.py:419
  100.3 26.7 %collective-permute-start.13 = (f32[4,64,256]{2,1,0:T(8,128)S(1)}, f32[4,64,256]{2,1,0:T(8,128)S(1)}, u32[]{:S(2)}, u32[]{:S(2)}) collective-permute-start(f32[4,64,256]{2,1,0:T(8,128)S(1)} %bitcast_add_fusion.refs_0_), channel_id=1, source_target_pairs={{0,16},{8,24},{16,0},{24,8},{1,17},{9,25},{17,1},{25,9},{2,18},{10... | collective-permute-start | bytes 786440 | tf_op jit(solution)/shard_map/ppermute | solution.py:419
  101.8 25.2 %collective-permute-start.14 = (f32[4,64,256]{2,1,0:T(8,128)S(1)}, f32[4,64,256]{2,1,0:T(8,128)S(1)}, u32[]{:S(2)}, u32[]{:S(2)}) collective-permute-start(f32[4,64,256]{2,1,0:T(8,128)S(1)} %bitcast_add_fusion.refs_0_), channel_id=1, source_target_pairs={{0,24},{8,16},{16,8},{24,0},{1,25},{9,17},{17,9},{25,1},{2,26},{10... | collective-permute-start | bytes 786440 | tf_op jit(solution)/shard_map/ppermute | solution.py:419
  127.1 17.7 %collective-permute-start.17 = (f32[64,256]{1,0:T(8,128)S(1)}, f32[64,256]{1,0:T(8,128)S(1)}, u32[]{:S(2)}, u32[]{:S(2)}) collective-permute-start(f32[64,256]{1,0:T(8,128)S(1)} %get-tuple-element.19), channel_id=1, source_target_pairs={{0,6},{1,7},{2,4},{3,5},{4,2},{5,3},{6,0},{7,1},{8,14},{9,15},{10,... | collective-permute-start | bytes 196616 | tf_op jit(solution)/shard_map/ppermute | solution.py:419
  130.8 14.1 %collective-permute-start.16 = (f32[64,256]{1,0:T(8,128)S(1)}, f32[64,256]{1,0:T(8,128)S(1)}, u32[]{:S(2)}, u32[]{:S(2)}) collective-permute-start(f32[64,256]{1,0:T(8,128)S(1)} %get-tuple-element.20), channel_id=1, source_target_pairs={{0,4},{1,5},{2,6},{3,7},{4,0},{5,1},{6,2},{7,3},{8,12},{9,13},{10,... | collective-permute-start | bytes 196616 | tf_op jit(solution)/shard_map/ppermute | solution.py:419
  130.8 14.1 %collective-permute-start.15 = (f32[64,256]{1,0:T(8,128)S(1)}, f32[64,256]{1,0:T(8,128)S(1)}, u32[]{:S(2)}, u32[]{:S(2)}) collective-permute-start(f32[64,256]{1,0:T(8,128)S(1)} %get-tuple-element.18), channel_id=1, source_target_pairs={{0,2},{1,3},{2,0},{3,1},{4,6},{5,7},{6,4},{7,5},{8,10},{9,11},{10,... | collective-permute-start | bytes 196616 | tf_op jit(solution)/shard_map/ppermute | solution.py:419

commit v14 on v12

--- a/solution.py
+++ b/solution.py
@@ -50,7 +50,8 @@
     def _():
         rows = batch // reps
         for k in range(reps):
-            first = pl.multiple_of((rep_ref[0] ^ k) * rows, rows)
+            flip = k // (reps // 2) + k % (reps // 2) * 2
+            first = pl.multiple_of((rep_ref[0] ^ flip) * rows, rows)
             emb_ref[pl.ds(first, rows), :] = mixed_ref[k * rows : (k + 1) * rows, :]
         xwide, _ = unit_rows(emb_ref[...].astype(jnp.float32))
         xhat_ref[...] = xwide.astype(jnp.bfloat16)
@@ -173,7 +174,7 @@
 def weight_gradient(base, emb, labels, stats, totals, weights):
     batch, width = emb.shape
     classes = weights.shape[0]
-    tile = math.gcd(classes, 1024)
+    tile = math.gcd(classes, 512)
     whole = lambda i: (0, 0)
     return pl.pallas_call(
         weight_kernel,
@@ -414,9 +415,9 @@
     weights = in_hbm(class_weights)
     runs = in_hbm(centroids.reshape(peers, run, width))
     cut = run * 5 // 8 // 16 * 16
-    mixed = jnp.concatenate([swap(embeddings, "rep", c) for c in range(2)])
-    mixed = jnp.concatenate([swap(mixed, "rep", 2 * z) for z in range(reps // 2)])
+    mixed = jnp.concatenate([swap(embeddings, "rep", 2 * z) for z in range(reps // 2)])
     rows_a = relay(released(fetch(runs, 0, cut, []), [mixed]))
+    mixed = jnp.concatenate([swap(mixed, "rep", c) for c in range(2)])
     emb, a, b, stats, what = forward(base, rep.reshape(1), mixed, reps, labels, weights)
 
     half = reps // 2
@@ -453,7 +454,7 @@
     held, token = place_rows(me, slots, rows_a, done, peers, run, 0)
 
     grad = (a / total[:, None] - b).reshape(half, 2, rows_local, width)
-    grad = join([swap(index(grad, core ^ c, 1, False), "rep", c) for c in range(2)], [done])
+    grad = sum(swap(index(grad, core ^ c, 1, False), "rep", c) for c in range(2))
     grad = join([swap(grad, "grp", j) for j in range(groups)], [token, loss])
     embedding_gradient = sum(
         swap(index(grad, deep ^ z, 0, False), "rep", 2 * z) for z in range(half)

time: 142 us -> 138 us (0.972)
  waiting for transfers between devices: 48.2 us -> 39.9 us
  Pallas kernels: 51.8 us -> 56.3 us
    ppermute x18, waiting for transfers between devices: 48.2 us -> 39.9 us  [swap(): lax.ppermute(value, axis, [(i, i ^ k) for i in range(size)])]
    pallas_call x1, Pallas kernels: 11.8 us -> 16.3 us  [weight_gradient(): pl.pallas_call(weight_kernel, grid=(classes // tile,), in_specs=[pl.Block...]
  transfers between devices with their start and end apart: 20 -> 20, of which waited for: 10 -> 8; matrix products, arithmetic and copies ran while one was open for 2% -> 2% of each run, Pallas kernels for 37% -> 41%
where the time goes in v14:
time: 138 us; the launch traced here: 137 us
  Pallas kernels  56.3 us (41%)
  waiting for transfers between devices  39.9 us (29%)
  starting transfers between devices  31.2 us (23%)
  local copies, waits for them, and re-layouts  6.78 us (5%)
  other arithmetic  1.63 us (1%)
    ppermute x18, waiting for transfers between devices, swap(): lax.ppermute(value, axis, [(i, i ^ k) for i in range(size)])  39.9 us
    ppermute x18, starting transfers between devices, swap(): lax.ppermute(value, axis, [(i, i ^ k) for i in range(size)])  22.3 us
    pallas_call x1, Pallas kernels, weight_gradient(): pl.pallas_call(weight_kernel, grid=(classes // tile,), in_specs=[pl.Block...  16.3 us
    pallas_call x1, Pallas kernels, place_and_blend(): pl.pallas_call(functools.partial(blend_kernel, peers=peers, run=run, firs...  13.7 us
    pallas_call x1, Pallas kernels, forward(): pl.pallas_call(functools.partial(forward_kernel, classes=classes, reps=re...  13.5 us
    pallas_call x1, Pallas kernels, place_rows(): pl.pallas_call(functools.partial(place_kernel, peers=peers, run=run, firs...  9.41 us
    all_to_all x2, starting transfers between devices, relay(): return lax.all_to_all(sent, ALL, 0, 0, tiled=True).reshape(-1, width)  8.9 us
    unnamed x24, local copies, waits for them, and re-layouts  6.29 us
  transfers between devices with their start and end apart: 20, of which 8 were waited for; matrix products, arithmetic and copies ran while one was open for 2% of the time, Pallas kernels for 41%

profile of v14, /device:TPU:0, one launch (start us, length us, event | category | flops | bytes accessed | tf_op | source)
XLA Modules:
  0.0 136.9 jit_solution(6687168972384217769)
XLA Ops:
  0.6 3.1 %collective-permute-start = (bf16[64,256]{1,0:T(8,128)(2,1)}, bf16[64,256]{1,0:T(8,128)(2,1)S(1)}, u32[]{:S(2)}, u32[]{:S(2)}) collective-permute-start(bf16[64,256]{1,0:T(8,128)(2,1)} %param.5), channel_id=1, source_target_pairs={{0,2},{1,3},{2,0},{3,1},{4,6},{5,7},{6,4},{7,5},{8,10},{9,11},{10,... | collective-permute-start | bytes 98312 | tf_op jit(solution)/shard_map/ppermute | solution.py:410
  3.7 2.6 %collective-permute-start.1 = (bf16[64,256]{1,0:T(8,128)(2,1)}, bf16[64,256]{1,0:T(8,128)(2,1)S(1)}, u32[]{:S(2)}, u32[]{:S(2)}) collective-permute-start(bf16[64,256]{1,0:T(8,128)(2,1)} %param.5), channel_id=1, source_target_pairs={{0,4},{1,5},{2,6},{3,7},{4,0},{5,1},{6,2},{7,3},{8,12},{9,13},{10,... | collective-permute-start | bytes 98312 | tf_op jit(solution)/shard_map/ppermute | solution.py:410
  6.3 0.0 collective-permute-start.2
  6.3 0.8 constant_dynamic-update-slice_fusion.3
  7.1 1.7 %fetch.3.refs_0_ = bf16[32,160,256]{2,1,0:T(8,128)(2,1)S(1)} custom-call(bf16[32,256,256]{2,1,0:T(8,128)(2,1)} %bitcast.79), custom_call_target="tpu_custom_call" | custom-call | bytes 10485760 | tf_op jit(solution)/shard_map/fetch/pallas_call | solution.py:230
  8.9 0.0 copy-start.1
  8.9 1.5 %copy-done.1 = bf16[32,160,256]{2,1,0:T(8,128)(2,1)} copy-done((bf16[32,160,256]{2,1,0:T(8,128)(2,1)}, bf16[32,160,256]{2,1,0:T(8,128)(2,1)S(1)}, u32[]{:S(2)}) %copy-start.1) | copy-done | bytes 2621464
  10.4 0.0 collective-permute-done
  10.4 0.0 collective-permute-done.1
  10.4 1.8 %collective-permute-done.2 = bf16[64,256]{1,0:T(8,128)(2,1)S(1)} collective-permute-done((bf16[64,256]{1,0:T(8,128)(2,1)}, bf16[64,256]{1,0:T(8,128)(2,1)S(1)}, u32[]{:S(2)}, u32[]{:S(2)}) %collective-permute-start.2) | collective-permute-done | bytes 32800 | tf_op jit(solution)/shard_map/ppermute | solution.py:410
  12.2 0.7 copy-done.6
  12.9 4.4 %all-to-all-start = ((bf16[32,160,256]{2,1,0:T(8,128)(2,1)}), bf16[32,160,256]{2,1,0:T(8,128)(2,1)}, u32[]{:S(2)}, u32[]{:S(2)}) async-start(bf16[32,160,256]{2,1,0:T(8,128)(2,1)} %release.2), calls=%async_computation | async-start | bytes 5242880 | tf_op jit(solution)/shard_map/all_to_all | solution.py:413
  17.3 0.0 copy-done.7
  17.3 0.3 collective-permute-start.3
  17.5 0.0 copy-done.4
  17.5 0.1 copy.16.lab_ref
  17.7 0.0 copy-done.8
  17.8 0.9 collective-permute-done.3
  18.7 13.5 %forward_sums.1 = (bf16[512,256]{1,0:T(8,128)(2,1)S(1)}, f32[512,256]{1,0:T(8,128)S(1)}, f32[512,256]{1,0:T(8,128)S(1)}, f32[8,512]{1,0:T(8,128)S(1)}, bf16[8192,256]{1,0:T(8,128)(2,1)}) custom-call(s32[1]{0:T(128)S(6)} %mul.18.base_ref, s32[1]{0:T(128)} %bitcast.1.rep_ref, s32[512,1]{1,0:T(8,128)S(1)} %copy.16.lab_ref, bf16[8192,256]{1,0:T(8,128)(2,1)} %w_ref.3, ...), custom_call_target="tpu_custom_call" | custom-call | flops 12884901888 | bytes 4194304 | tf_op jit(solution)/shard_map/forward_sums/pallas_call | solution.py:111
  32.2 2.7 %collective-permute-start.6 = (f32[24,128]{1,0:T(8,128)S(1)}, f32[24,128]{1,0:T(8,128)S(1)}, u32[]{:S(2)}, u32[]{:S(2)}) collective-permute-start(f32[24,128]{1,0:T(8,128)S(1)} %get-tuple-element.50), channel_id=1, source_target_pairs={{0,24},{8,16},{16,8},{24,0},{1,25},{9,17},{17,9},{25,1},{2,26},{10... | collective-permute-start | bytes 36872 | tf_op jit(solution)/shard_map/ppermute | solution.py:410
  34.9 0.6 collective-permute-start.5
  35.5 0.3 collective-permute-start.4
  35.8 1.1 collective-permute-done.6
  36.9 1.7 %collective-permute-done.5 = f32[24,128]{1,0:T(8,128)S(1)} collective-permute-done((f32[24,128]{1,0:T(8,128)S(1)}, f32[24,128]{1,0:T(8,128)S(1)}, u32[]{:S(2)}, u32[]{:S(2)}) %collective-permute-start.5) | collective-permute-done | bytes 12320 | tf_op jit(solution)/shard_map/ppermute | solution.py:410
  38.6 0.5 collective-permute-done.4
  39.3 0.1 collective-permute-start.7
  39.4 1.5 %fetch.2.refs_1_.refs_0_ = bf16[32,96,256]{2,1,0:T(8,128)(2,1)S(1)} custom-call(bf16[32,256,256]{2,1,0:T(8,128)(2,1)} %bitcast.80, f32[8,512]{1,0:T(8,128)S(1)} %get-tuple-element.11.refs_0_.st_ref), custom_call_target="tpu_custom_call" | custom-call | bytes 6291456 | tf_op jit(solution)/shard_map/fetch/pallas_call | solution.py:230
  41.0 0.0 copy-start
  41.0 0.0 collective-permute-done.7
  41.2 3.7 %collective-permute-start.10 = (f32[24,128]{1,0:T(8,128)S(1)}, f32[24,128]{1,0:T(8,128)S(1)}, u32[]{:S(2)}, u32[]{:S(2)}) collective-permute-start(f32[24,128]{1,0:T(8,128)S(1)} %get-tuple-element.44), channel_id=1, source_target_pairs={{0,6},{1,7},{2,4},{3,5},{4,2},{5,3},{6,0},{7,1},{8,14},{9,15},{10,... | collective-permute-start | bytes 36872 | tf_op jit(solution)/shard_map/ppermute | solution.py:410
  44.9 0.2 collective-permute-start.9
  45.1 0.6 collective-permute-start.8
  45.6 18.9 %collective-permute-done.10 = f32[24,128]{1,0:T(8,128)S(1)} collective-permute-done((f32[24,128]{1,0:T(8,128)S(1)}, f32[24,128]{1,0:T(8,128)S(1)}, u32[]{:S(2)}, u32[]{:S(2)}) %collective-permute-start.10) | collective-permute-done | bytes 12320 | tf_op jit(solution)/shard_map/ppermute | solution.py:410
  64.6 13.6 %collective-permute-done.9 = f32[24,128]{1,0:T(8,128)S(1)} collective-permute-done((f32[24,128]{1,0:T(8,128)S(1)}, f32[24,128]{1,0:T(8,128)S(1)}, u32[]{:S(2)}, u32[]{:S(2)}) %collective-permute-start.9) | collective-permute-done | bytes 12320 | tf_op jit(solution)/shard_map/ppermute | solution.py:410
  78.2 0.0 collective-permute-done.8
  78.2 0.6 fusion.12
  78.8 0.0 copy-done
  78.8 0.0 all-to-all-done
  78.8 4.6 %all-to-all-start.1 = ((bf16[32,96,256]{2,1,0:T(8,128)(2,1)}), bf16[32,96,256]{2,1,0:T(8,128)(2,1)S(1)}, u32[]{:S(2)}, u32[]{:S(2)}) async-start(bf16[32,96,256]{2,1,0:T(8,128)(2,1)} %release.3), calls=%async_computation.1 | async-start | bytes 3145728 | tf_op jit(solution)/shard_map/all_to_all | solution.py:413
  83.4 0.0 copy-done.3
  83.4 0.1 divide_subtract_fusion
  83.6 0.3 collective-permute-start.11
  83.9 1.3 collective-permute-done.11
  85.2 1.8 %collective-permute-start.12 = (f32[4,64,256]{2,1,0:T(8,128)S(1)}, f32[4,64,256]{2,1,0:T(8,128)S(1)}, u32[]{:S(2)}, u32[]{:S(2)}) collective-permute-start(f32[4,64,256]{2,1,0:T(8,128)S(1)} %bitcast_add_fusion.refs_0_), channel_id=1, source_target_pairs={{0,8},{8,0},{16,24},{24,16},{1,9},{9,1},{17,25},{25,17},{2,10},{10... | collective-permute-start | bytes 786440 | tf_op jit(solution)/shard_map/ppermute | solution.py:410
  87.0 1.5 %collective-permute-start.13 = (f32[4,64,256]{2,1,0:T(8,128)S(1)}, f32[4,64,256]{2,1,0:T(8,128)S(1)}, u32[]{:S(2)}, u32[]{:S(2)}) collective-permute-start(f32[4,64,256]{2,1,0:T(8,128)S(1)} %bitcast_add_fusion.refs_0_), channel_id=1, source_target_pairs={{0,16},{8,24},{16,0},{24,8},{1,17},{9,25},{17,1},{25,9},{2,18},{10... | collective-permute-start | bytes 786440 | tf_op jit(solution)/shard_map/ppermute | solution.py:410
  88.5 0.3 collective-permute-start.14
  88.8 16.3 %weight_gradient.1._ = f32[8192,256]{1,0:T(8,128)} custom-call(s32[1]{0:T(128)S(6)} %mul.18.base_ref, bf16[512,256]{1,0:T(8,128)(2,1)S(1)} %get-tuple-element.14.emb_ref, s32[1,512]{1,0:T(1,128)S(1)} %bitcast.78, f32[8,512]{1,0:T(8,128)S(1)} %get-tuple-element.11.refs_0_.st_ref, f32[1,512]{1,0:T(1,128)S(1)} %bitcast.74, bf16[8192,256]{1,0:T(8,128)(2,1)} %w_ref.3), custom_call_target="tpu_custom_call" | custom-call | flops 12884901888 | bytes 12582912 | tf_op jit(solution)/shard_map/weight_gradient/pallas_call | solution.py:179
  105.2 0.1 dynamic_slice.66.refs_5_
  105.2 9.4 %place_rows.1 = (f32[16384,128]{1,0:T(8,128)S(1)}, f32[8,128]{1,0:T(8,128)S(1)}) custom-call(s32[1]{0:T(128)} %bitcast.me_ref, s32[8192]{0:T(1024)S(1)} %bitcast.72, bf16[5120,256]{1,0:T(8,128)(2,1)} %bitcast.36.row_ref, f32[8192,256]{1,0:T(8,128)} %weight_gradient.1._), custom_call_target="tpu_custom_call" | custom-call | bytes 41943040 | tf_op jit(solution)/shard_map/place_rows/pallas_call | solution.py:323
  114.7 0.0 copy-start.2
  114.7 3.3 %copy-done.2 = f32[16384,128]{1,0:T(8,128)} copy-done((f32[16384,128]{1,0:T(8,128)}, f32[16384,128]{1,0:T(8,128)S(1)}, u32[]{:S(2)}) %copy-start.2) | copy-done | bytes 8388632
  118.0 0.0 collective-permute-done.12.refs_1_
  118.0 0.0 collective-permute-done.13.refs_2_
  118.0 0.0 collective-permute-done.14.refs_3_
  118.0 0.1 join.3
  118.1 3.7 %collective-permute-start.17 = (f32[64,256]{1,0:T(8,128)S(1)}, f32[64,256]{1,0:T(8,128)S(1)}, u32[]{:S(2)}, u32[]{:S(2)}) collective-permute-start(f32[64,256]{1,0:T(8,128)S(1)} %get-tuple-element.19), channel_id=1, source_target_pairs={{0,6},{1,7},{2,4},{3,5},{4,2},{5,3},{6,0},{7,1},{8,14},{9,15},{10,... | collective-permute-start | bytes 196616 | tf_op jit(solution)/shard_map/ppermute | solution.py:410
  121.7 0.0 collective-permute-start.16
  121.8 0.8 collective-permute-start.15
  122.5 0.0 all-to-all-done.1
  122.5 13.7 %place_and_blend.1 = bf16[8192,256]{1,0:T(8,128)(2,1)} custom-call(s32[1]{0:T(128)} %bitcast.me_ref, s32[8192]{0:T(1024)S(1)} %bitcast.73, bf16[8192,256]{1,0:T(8,128)(2,1)} %get-tuple-element.16.w_ref, bf16[3072,256]{1,0:T(8,128)(2,1)S(1)} %bitcast.71, f32[16384,128]{1,0:T(8,128)} %copy-done.2), custom_call_target="tpu_custom_call" | custom-call | bytes 25165824 | tf_op jit(solution)/shard_map/place_and_blend/pallas_call | solution.py:376
  136.2 0.0 collective-permute-done.17
  136.2 0.0 collective-permute-done.16
  136.2 0.0 collective-permute-done.15
  136.2 0.7 fusion.1
  (36 shorter events, 0.6 us)
Async XLA Ops:
  0.6 9.7 %collective-permute-start = (bf16[64,256]{1,0:T(8,128)(2,1)}, bf16[64,256]{1,0:T(8,128)(2,1)S(1)}, u32[]{:S(2)}, u32[]{:S(2)}) collective-permute-start(bf16[64,256]{1,0:T(8,128)(2,1)} %param.5), channel_id=1, source_target_pairs={{0,2},{1,3},{2,0},{3,1},{4,6},{5,7},{6,4},{7,5},{8,10},{9,11},{10,... | collective-permute-start | bytes 98312 | tf_op jit(solution)/shard_map/ppermute | solution.py:410
  3.7 6.7 %collective-permute-start.1 = (bf16[64,256]{1,0:T(8,128)(2,1)}, bf16[64,256]{1,0:T(8,128)(2,1)S(1)}, u32[]{:S(2)}, u32[]{:S(2)}) collective-permute-start(bf16[64,256]{1,0:T(8,128)(2,1)} %param.5), channel_id=1, source_target_pairs={{0,4},{1,5},{2,6},{3,7},{4,0},{5,1},{6,2},{7,3},{8,12},{9,13},{10,... | collective-permute-start | bytes 98312 | tf_op jit(solution)/shard_map/ppermute | solution.py:410
  6.3 5.9 %collective-permute-start.2 = (bf16[64,256]{1,0:T(8,128)(2,1)}, bf16[64,256]{1,0:T(8,128)(2,1)S(1)}, u32[]{:S(2)}, u32[]{:S(2)}) collective-permute-start(bf16[64,256]{1,0:T(8,128)(2,1)} %param.5), channel_id=1, source_target_pairs={{0,6},{1,7},{2,4},{3,5},{4,2},{5,3},{6,0},{7,1},{8,14},{9,15},{10,... | collective-permute-start | bytes 98312 | tf_op jit(solution)/shard_map/ppermute | solution.py:410
  8.9 1.5 %copy-start.1 = (bf16[32,160,256]{2,1,0:T(8,128)(2,1)}, bf16[32,160,256]{2,1,0:T(8,128)(2,1)S(1)}, u32[]{:S(2)}) copy-start(bf16[32,160,256]{2,1,0:T(8,128)(2,1)S(1)} %fetch.3.refs_0_) | copy-start | bytes 7864324
  12.2 0.7 copy-start.6
  12.9 4.6 %copy-start.4 = (s32[512]{0:T(512)S(1)}, s32[512]{0:T(512)}, u32[]{:S(2)}) copy-start(s32[512]{0:T(512)} %param.6) | copy-start | bytes 6148
  12.9 4.8 %copy-start.8 = (s32[8192]{0:T(1024)S(1)}, s32[8192]{0:T(1024)}, u32[]{:S(2)}) copy-start(s32[8192]{0:T(1024)} %param.9) | copy-start | bytes 98308
  12.9 4.4 %copy-start.7 = (bf16[256,256]{1,0:T(8,128)(2,1)S(1)}, bf16[256,256]{1,0:T(8,128)(2,1)}, u32[]{:S(2)}) copy-start(bf16[256,256]{1,0:T(8,128)(2,1)} %copy-done.6) | copy-start | bytes 393220
  12.9 65.9 %all-to-all-start = ((bf16[32,160,256]{2,1,0:T(8,128)(2,1)}), bf16[32,160,256]{2,1,0:T(8,128)(2,1)}, u32[]{:S(2)}, u32[]{:S(2)}) async-start(bf16[32,160,256]{2,1,0:T(8,128)(2,1)} %release.2), calls=%async_computation | async-start | bytes 5242880 | tf_op jit(solution)/shard_map/all_to_all | solution.py:413
  17.3 1.4 %collective-permute-start.3 = (bf16[256,256]{1,0:T(8,128)(2,1)S(1)}, bf16[256,256]{1,0:T(8,128)(2,1)S(1)}, u32[]{:S(2)}, u32[]{:S(2)}) collective-permute-start(bf16[256,256]{1,0:T(8,128)(2,1)S(1)} %copy-done.7), channel_id=1, source_target_pairs={{0,1},{1,0},{2,3},{3,2},{4,5},{5,4},{6,7},{7,6},{8,9},{9,8},{10,11... | collective-permute-start | bytes 393224 | tf_op jit(solution)/shard_map/ppermute | solution.py:410
  32.2 4.7 %collective-permute-start.6 = (f32[24,128]{1,0:T(8,128)S(1)}, f32[24,128]{1,0:T(8,128)S(1)}, u32[]{:S(2)}, u32[]{:S(2)}) collective-permute-start(f32[24,128]{1,0:T(8,128)S(1)} %get-tuple-element.50), channel_id=1, source_target_pairs={{0,24},{8,16},{16,8},{24,0},{1,25},{9,17},{17,9},{25,1},{2,26},{10... | collective-permute-start | bytes 36872 | tf_op jit(solution)/shard_map/ppermute | solution.py:410
  34.9 3.7 %collective-permute-start.5 = (f32[24,128]{1,0:T(8,128)S(1)}, f32[24,128]{1,0:T(8,128)S(1)}, u32[]{:S(2)}, u32[]{:S(2)}) collective-permute-start(f32[24,128]{1,0:T(8,128)S(1)} %get-tuple-element.49), channel_id=1, source_target_pairs={{0,16},{8,24},{16,0},{24,8},{1,17},{9,25},{17,1},{25,9},{2,18},{10... | collective-permute-start | bytes 36872 | tf_op jit(solution)/shard_map/ppermute | solution.py:410
  35.5 3.7 %collective-permute-start.4 = (f32[24,128]{1,0:T(8,128)S(1)}, f32[24,128]{1,0:T(8,128)S(1)}, u32[]{:S(2)}, u32[]{:S(2)}) collective-permute-start(f32[24,128]{1,0:T(8,128)S(1)} %get-tuple-element.48), channel_id=1, source_target_pairs={{0,8},{8,0},{16,24},{24,16},{1,9},{9,1},{17,25},{25,17},{2,10},{10... | collective-permute-start | bytes 36872 | tf_op jit(solution)/shard_map/ppermute | solution.py:410
  39.3 1.7 %collective-permute-start.7 = (f32[40,128]{1,0:T(8,128)S(1)}, f32[40,128]{1,0:T(8,128)S(1)}, u32[]{:S(2)}, u32[]{:S(2)}) collective-permute-start(f32[40,128]{1,0:T(8,128)S(1)} %get-tuple-element.46), channel_id=1, source_target_pairs={{0,1},{1,0},{2,3},{3,2},{4,5},{5,4},{6,7},{7,6},{8,9},{9,8},{10,11... | collective-permute-start | bytes 61448 | tf_op jit(solution)/shard_map/ppermute | solution.py:410
  41.0 37.8 %copy-start = (bf16[32,96,256]{2,1,0:T(8,128)(2,1)}, bf16[32,96,256]{2,1,0:T(8,128)(2,1)S(1)}, u32[]{:S(2)}) copy-start(bf16[32,96,256]{2,1,0:T(8,128)(2,1)S(1)} %fetch.2.refs_1_.refs_0_) | copy-start | bytes 4718596
  41.2 23.4 %collective-permute-start.10 = (f32[24,128]{1,0:T(8,128)S(1)}, f32[24,128]{1,0:T(8,128)S(1)}, u32[]{:S(2)}, u32[]{:S(2)}) collective-permute-start(f32[24,128]{1,0:T(8,128)S(1)} %get-tuple-element.44), channel_id=1, source_target_pairs={{0,6},{1,7},{2,4},{3,5},{4,2},{5,3},{6,0},{7,1},{8,14},{9,15},{10,... | collective-permute-start | bytes 36872 | tf_op jit(solution)/shard_map/ppermute | solution.py:410
  44.9 33.3 %collective-permute-start.9 = (f32[24,128]{1,0:T(8,128)S(1)}, f32[24,128]{1,0:T(8,128)S(1)}, u32[]{:S(2)}, u32[]{:S(2)}) collective-permute-start(f32[24,128]{1,0:T(8,128)S(1)} %get-tuple-element.43), channel_id=1, source_target_pairs={{0,4},{1,5},{2,6},{3,7},{4,0},{5,1},{6,2},{7,3},{8,12},{9,13},{10,... | collective-permute-start | bytes 36872 | tf_op jit(solution)/shard_map/ppermute | solution.py:410
  45.1 33.1 %collective-permute-start.8 = (f32[24,128]{1,0:T(8,128)S(1)}, f32[24,128]{1,0:T(8,128)S(1)}, u32[]{:S(2)}, u32[]{:S(2)}) collective-permute-start(f32[24,128]{1,0:T(8,128)S(1)} %get-tuple-element.42), channel_id=1, source_target_pairs={{0,2},{1,3},{2,0},{3,1},{4,6},{5,7},{6,4},{7,5},{8,10},{9,11},{10,... | collective-permute-start | bytes 36872 | tf_op jit(solution)/shard_map/ppermute | solution.py:410
  78.8 4.6 %copy-start.3 = (f32[512]{0:T(512)S(1)}, f32[512]{0:T(512)}, u32[]{:S(2)}) copy-start(f32[512]{0:T(512)} %get-tuple-element.39.refs_1_) | copy-start | bytes 6148
  78.8 43.7 %all-to-all-start.1 = ((bf16[32,96,256]{2,1,0:T(8,128)(2,1)}), bf16[32,96,256]{2,1,0:T(8,128)(2,1)S(1)}, u32[]{:S(2)}, u32[]{:S(2)}) async-start(bf16[32,96,256]{2,1,0:T(8,128)(2,1)} %release.3), calls=%async_computation.1 | async-start | bytes 3145728 | tf_op jit(solution)/shard_map/all_to_all | solution.py:413
  83.6 1.6 %collective-permute-start.11 = (f32[4,64,256]{2,1,0:T(8,128)S(1)}, f32[4,64,256]{2,1,0:T(8,128)S(1)}, u32[]{:S(2)}, u32[]{:S(2)}) collective-permute-start(f32[4,64,256]{2,1,0:T(8,128)S(1)} %dynamic-slice_bitcast_fusion), channel_id=1, source_target_pairs={{0,1},{1,0},{2,3},{3,2},{4,5},{5,4},{6,7},{7,6},{8,9},{9,8},{10,11... | collective-permute-start | bytes 786440 | tf_op jit(solution)/shard_map/ppermute | solution.py:410
  85.2 32.7 %collective-permute-start.12 = (f32[4,64,256]{2,1,0:T(8,128)S(1)}, f32[4,64,256]{2,1,0:T(8,128)S(1)}, u32[]{:S(2)}, u32[]{:S(2)}) collective-permute-start(f32[4,64,256]{2,1,0:T(8,128)S(1)} %bitcast_add_fusion.refs_0_), channel_id=1, source_target_pairs={{0,8},{8,0},{16,24},{24,16},{1,9},{9,1},{17,25},{25,17},{2,10},{10... | collective-permute-start | bytes 786440 | tf_op jit(solution)/shard_map/ppermute | solution.py:410
  87.0 30.9 %collective-permute-start.13 = (f32[4,64,256]{2,1,0:T(8,128)S(1)}, f32[4,64,256]{2,1,0:T(8,128)S(1)}, u32[]{:S(2)}, u32[]{:S(2)}) collective-permute-start(f32[4,64,256]{2,1,0:T(8,128)S(1)} %bitcast_add_fusion.refs_0_), channel_id=1, source_target_pairs={{0,16},{8,24},{16,0},{24,8},{1,17},{9,25},{17,1},{25,9},{2,18},{10... | collective-permute-start | bytes 786440 | tf_op jit(solution)/shard_map/ppermute | solution.py:410
  88.5 29.5 %collective-permute-start.14 = (f32[4,64,256]{2,1,0:T(8,128)S(1)}, f32[4,64,256]{2,1,0:T(8,128)S(1)}, u32[]{:S(2)}, u32[]{:S(2)}) collective-permute-start(f32[4,64,256]{2,1,0:T(8,128)S(1)} %bitcast_add_fusion.refs_0_), channel_id=1, source_target_pairs={{0,24},{8,16},{16,8},{24,0},{1,25},{9,17},{17,9},{25,1},{2,26},{10... | collective-permute-start | bytes 786440 | tf_op jit(solution)/shard_map/ppermute | solution.py:410
  105.2 12.7 %copy-start.5 = (f32[64]{0:T(128)}, f32[64]{0:T(128)S(1)}, u32[]{:S(2)}) copy-start(f32[64]{0:T(128)S(1)} %dynamic_slice.66.refs_5_) | copy-start | bytes 772
  114.7 3.3 %copy-start.2 = (f32[16384,128]{1,0:T(8,128)}, f32[16384,128]{1,0:T(8,128)S(1)}, u32[]{:S(2)}) copy-start(f32[16384,128]{1,0:T(8,128)S(1)} %get-tuple-element.17.in_ref) | copy-start | bytes 25165828
  118.1 18.1 %collective-permute-start.17 = (f32[64,256]{1,0:T(8,128)S(1)}, f32[64,256]{1,0:T(8,128)S(1)}, u32[]{:S(2)}, u32[]{:S(2)}) collective-permute-start(f32[64,256]{1,0:T(8,128)S(1)} %get-tuple-element.19), channel_id=1, source_target_pairs={{0,6},{1,7},{2,4},{3,5},{4,2},{5,3},{6,0},{7,1},{8,14},{9,15},{10,... | collective-permute-start | bytes 196616 | tf_op jit(solution)/shard_map/ppermute | solution.py:410
  121.7 14.5 %collective-permute-start.16 = (f32[64,256]{1,0:T(8,128)S(1)}, f32[64,256]{1,0:T(8,128)S(1)}, u32[]{:S(2)}, u32[]{:S(2)}) collective-permute-start(f32[64,256]{1,0:T(8,128)S(1)} %get-tuple-element.20), channel_id=1, source_target_pairs={{0,4},{1,5},{2,6},{3,7},{4,0},{5,1},{6,2},{7,3},{8,12},{9,13},{10,... | collective-permute-start | bytes 196616 | tf_op jit(solution)/shard_map/ppermute | solution.py:410
  121.8 14.5 %collective-permute-start.15 = (f32[64,256]{1,0:T(8,128)S(1)}, f32[64,256]{1,0:T(8,128)S(1)}, u32[]{:S(2)}, u32[]{:S(2)}) collective-permute-start(f32[64,256]{1,0:T(8,128)S(1)} %get-tuple-element.18), channel_id=1, source_target_pairs={{0,2},{1,3},{2,0},{3,1},{4,6},{5,7},{6,4},{7,5},{8,10},{9,11},{10,... | collective-permute-start | bytes 196616 | tf_op jit(solution)/shard_map/ppermute | solution.py:410

commit v15 on v14

--- a/solution.py
+++ b/solution.py
@@ -174,7 +174,7 @@
 def weight_gradient(base, emb, labels, stats, totals, weights):
     batch, width = emb.shape
     classes = weights.shape[0]
-    tile = math.gcd(classes, 512)
+    tile = math.gcd(classes, 2048)
     whole = lambda i: (0, 0)
     return pl.pallas_call(
         weight_kernel,
@@ -205,22 +205,25 @@
 
 
 def fetch_kernel(rows_ref, *refs, first):
-    out_ref, sem = refs[-2:]
+    out_ref, held_ref, sem = refs[-3:]
     peers, size, _ = out_ref.shape
-    lanes = sem.shape[0]
-    part = peers // lanes
-    copies = [
-        pltpu.make_async_copy(
-            rows_ref.at[pl.ds(c * part, part), pl.ds(first, size), :],
-            out_ref.at[pl.ds(c * part, part)],
-            sem.at[c],
-        )
-        for c in range(lanes)
+    lanes = sem.shape[1]
+    parts = [pl.ds(c * (peers // lanes), peers // lanes) for c in range(lanes)]
+    loads = [
+        pltpu.make_async_copy(rows_ref.at[part, pl.ds(first, size), :], held_ref.at[part], sem.at[0, c])
+        for c, part in enumerate(parts)
     ]
-    for copy in copies:
-        copy.start()
-    for copy in copies:
-        copy.wait()
+    stores = [
+        pltpu.make_async_copy(held_ref.at[part], out_ref.at[part], sem.at[1, c])
+        for c, part in enumerate(parts)
+    ]
+    for load in loads:
+        load.start()
+    for load, store in zip(loads, stores):
+        load.wait()
+        store.start()
+    for store in stores:
+        store.wait()
 
 
 def fetch(runs, first, size, tokens):
@@ -230,9 +233,12 @@
     return pl.pallas_call(
         functools.partial(fetch_kernel, first=first),
         in_specs=[hbm] + [anywhere] * len(tokens),
-        out_specs=pl.BlockSpec(memory_space=pltpu.VMEM),
-        out_shape=jax.ShapeDtypeStruct((peers, size, width), runs.dtype),
-        scratch_shapes=[pltpu.SemaphoreType.DMA((math.gcd(peers, 8),))],
+        out_specs=anywhere,
+        out_shape=pltpu.HBM((peers, size, width), runs.dtype),
+        scratch_shapes=[
+            pltpu.VMEM((peers, size, width), runs.dtype),
+            pltpu.SemaphoreType.DMA((2, math.gcd(peers, 8))),
+        ],
         compiler_params=pltpu.CompilerParams(vmem_limit_bytes=6 * MIB),
         cost_estimate=pl.CostEstimate(
             flops=0, bytes_accessed=8 * peers * size * width, transcendentals=0
@@ -272,7 +278,7 @@
         release_kernel,
         in_specs=[anywhere] * (1 + len(tokens)),
         out_specs=anywhere,
-        out_shape=jax.ShapeDtypeStruct(value.shape, value.dtype),
+        out_shape=pltpu.HBM(value.shape, value.dtype),
         input_output_aliases={0: 0},
         cost_estimate=COST,
         name="release",
@@ -369,7 +375,7 @@
 
 def place_and_blend(me, slots, rows, held, weights, peers, run, first):
     classes, width = weights.shape
-    tile = math.gcd(classes, 1024)
+    tile = math.gcd(classes, 2048)
     smem = pl.BlockSpec(memory_space=pltpu.SMEM)
     vmem = pl.BlockSpec(memory_space=pltpu.VMEM)
     tiles = pl.BlockSpec((tile, width), lambda i: (i, 0))
@@ -416,7 +422,7 @@
     runs = in_hbm(centroids.reshape(peers, run, width))
     cut = run * 5 // 8 // 16 * 16
     mixed = jnp.concatenate([swap(embeddings, "rep", 2 * z) for z in range(reps // 2)])
-    rows_a = relay(released(fetch(runs, 0, cut, []), [mixed]))
+    rows_a = relay(released(in_hbm(fetch(runs, 0, cut, [])), [mixed]))
     mixed = jnp.concatenate([swap(mixed, "rep", c) for c in range(2)])
     emb, a, b, stats, what = forward(base, rep.reshape(1), mixed, reps, labels, weights)
 
@@ -438,7 +444,7 @@
     wanted = wanted.reshape(groups, half, 2, run)
     wanted = [index(wanted, core ^ c, 2, False) for c in range(2)]
     sums, wanted = share_out(sums, wanted, "rep", range(2))
-    sent_b = fetch(runs, cut, run - cut, [stats])
+    sent_b = in_hbm(fetch(runs, cut, run - cut, [stats]))
     sums = join([sums.reshape(-1, 128)], [sent_b]).reshape(-1)
     wanted = wanted.reshape(2, groups, half, run)
     wanted = [index(wanted, deep ^ z, 2, False) for z in range(half)]

time: 138 us -> 138 us (level)
  Pallas kernels: 56.3 us -> 50 us
  local copies, waits for them, and re-layouts: 6.78 us -> 10.2 us
  other arithmetic: 1.63 us -> 3.62 us
  waiting for transfers between devices: 39.9 us -> 41.5 us
    pallas_call x1, Pallas kernels: 16.3 us -> 10.1 us  [weight_gradient(): pl.pallas_call(weight_kernel, grid=(classes // tile,), in_specs=[pl.Block...]
    all_to_all x2, waiting for transfers between devices: 0.01 us -> 4.84 us  [relay(): return lax.all_to_all(sent, ALL, 0, 0, tiled=True).reshape(-1, width)]
    unnamed x24 -> x32, local copies, waits for them, and re-layouts: 6.29 us -> 9.68 us
    ppermute x18, waiting for transfers between devices: 39.9 us -> 36.6 us  [swap(): lax.ppermute(value, axis, [(i, i ^ k) for i in range(size)])]
    pallas_call x2, Pallas kernels: 3.26 us -> 4.91 us  [fetch(): pl.pallas_call(functools.partial(fetch_kernel, first=first), in_specs=[hb...]
  transfers between devices with their start and end apart: 20 -> 20, of which waited for: 8 -> 9; matrix products, arithmetic and copies ran while one was open for 2% -> 3% of each run, Pallas kernels for 41% -> 36%
where the time goes in v15:
time: 138 us; the launch traced here: 137 us
  Pallas kernels  50 us (36%)
  waiting for transfers between devices  41.5 us (30%)
  starting transfers between devices  30.6 us (22%)
  local copies, waits for them, and re-layouts  10.2 us (7%)
  other arithmetic  3.62 us (3%)
    ppermute x18, waiting for transfers between devices, swap(): lax.ppermute(value, axis, [(i, i ^ k) for i in range(size)])  36.6 us
    ppermute x18, starting transfers between devices, swap(): lax.ppermute(value, axis, [(i, i ^ k) for i in range(size)])  22.3 us
    pallas_call x1, Pallas kernels, forward(): pl.pallas_call(functools.partial(forward_kernel, classes=classes, reps=re...  13.6 us
    pallas_call x1, Pallas kernels, place_and_blend(): pl.pallas_call(functools.partial(blend_kernel, peers=peers, run=run, firs...  12.5 us
    pallas_call x1, Pallas kernels, weight_gradient(): pl.pallas_call(weight_kernel, grid=(classes // tile,), in_specs=[pl.Block...  10.1 us
    unnamed x32, local copies, waits for them, and re-layouts  9.68 us
    pallas_call x1, Pallas kernels, place_rows(): pl.pallas_call(functools.partial(place_kernel, peers=peers, run=run, firs...  8.73 us
    all_to_all x2, starting transfers between devices, relay(): return lax.all_to_all(sent, ALL, 0, 0, tiled=True).reshape(-1, width)  8.31 us
  transfers between devices with their start and end apart: 20, of which 9 were waited for; matrix products, arithmetic and copies ran while one was open for 3% of the time, Pallas kernels for 36%

profile of v15, /device:TPU:0, one launch (start us, length us, event | category | flops | bytes accessed | tf_op | source)
XLA Modules:
  0.0 136.9 jit_solution(4298802991651088300)
XLA Ops:
  0.6 3.1 %collective-permute-start = (bf16[64,256]{1,0:T(8,128)(2,1)}, bf16[64,256]{1,0:T(8,128)(2,1)S(1)}, u32[]{:S(2)}, u32[]{:S(2)}) collective-permute-start(bf16[64,256]{1,0:T(8,128)(2,1)} %param.5), channel_id=1, source_target_pairs={{0,2},{1,3},{2,0},{3,1},{4,6},{5,7},{6,4},{7,5},{8,10},{9,11},{10,... | collective-permute-start | bytes 98312 | tf_op jit(solution)/shard_map/ppermute | solution.py:416
  3.7 2.6 %collective-permute-start.1 = (bf16[64,256]{1,0:T(8,128)(2,1)}, bf16[64,256]{1,0:T(8,128)(2,1)S(1)}, u32[]{:S(2)}, u32[]{:S(2)}) collective-permute-start(bf16[64,256]{1,0:T(8,128)(2,1)} %param.5), channel_id=1, source_target_pairs={{0,4},{1,5},{2,6},{3,7},{4,0},{5,1},{6,2},{7,3},{8,12},{9,13},{10,... | collective-permute-start | bytes 98312 | tf_op jit(solution)/shard_map/ppermute | solution.py:416
  6.3 0.0 collective-permute-start.2
  6.3 0.8 constant_dynamic-update-slice_fusion.3
  7.1 2.6 %fetch.3.refs_0_ = bf16[32,160,256]{2,1,0:T(8,128)(2,1)} custom-call(bf16[32,256,256]{2,1,0:T(8,128)(2,1)} %bitcast.79), custom_call_target="tpu_custom_call" | custom-call | bytes 10485760 | tf_op jit(solution)/shard_map/fetch/pallas_call | solution.py:233
  9.7 0.0 collective-permute-done
  9.8 0.0 collective-permute-done.1
  9.8 2.4 %collective-permute-done.2 = bf16[64,256]{1,0:T(8,128)(2,1)S(1)} collective-permute-done((bf16[64,256]{1,0:T(8,128)(2,1)}, bf16[64,256]{1,0:T(8,128)(2,1)S(1)}, u32[]{:S(2)}, u32[]{:S(2)}) %collective-permute-start.2) | collective-permute-done | bytes 32800 | tf_op jit(solution)/shard_map/ppermute | solution.py:416
  12.2 0.7 copy-done.10
  12.9 3.6 %all-to-all-start = ((bf16[32,160,256]{2,1,0:T(8,128)(2,1)}), bf16[32,160,256]{2,1,0:T(8,128)(2,1)S(1)}, u32[]{:S(2)}, u32[]{:S(2)}) async-start(bf16[32,160,256]{2,1,0:T(8,128)(2,1)} %release.2), calls=%async_computation | async-start | bytes 5242880 | tf_op jit(solution)/shard_map/all_to_all | solution.py:419
  16.5 0.3 collective-permute-start.3
  16.9 0.1 copy.16.lab_ref
  17.1 0.8 collective-permute-done.3
  18.0 0.0 copy-start.3
  18.0 0.7 copy-done.3
  18.7 0.9 copy-done.4
  19.6 13.6 %forward_sums.1 = (bf16[512,256]{1,0:T(8,128)(2,1)S(1)}, f32[512,256]{1,0:T(8,128)S(1)}, f32[512,256]{1,0:T(8,128)S(1)}, f32[8,512]{1,0:T(8,128)S(1)}, bf16[8192,256]{1,0:T(8,128)(2,1)}) custom-call(s32[1]{0:T(128)S(6)} %mul.18.base_ref, s32[1]{0:T(128)} %bitcast.1.rep_ref, s32[512,1]{1,0:T(8,128)S(1)} %copy.16.lab_ref, bf16[8192,256]{1,0:T(8,128)(2,1)} %w_ref.3, ...), custom_call_target="tpu_custom_call" | custom-call | flops 12884901888 | bytes 4194304 | tf_op jit(solution)/shard_map/forward_sums/pallas_call | solution.py:111
  33.2 0.8 copy-done.1
  34.0 0.7 copy-done.7
  34.7 2.7 %collective-permute-start.6 = (f32[24,128]{1,0:T(8,128)S(1)}, f32[24,128]{1,0:T(8,128)S(1)}, u32[]{:S(2)}, u32[]{:S(2)}) collective-permute-start(f32[24,128]{1,0:T(8,128)S(1)} %get-tuple-element.50), channel_id=1, source_target_pairs={{0,24},{8,16},{16,8},{24,0},{1,25},{9,17},{17,9},{25,1},{2,26},{10... | collective-permute-start | bytes 36872 | tf_op jit(solution)/shard_map/ppermute | solution.py:416
  37.5 0.6 collective-permute-start.5
  38.0 0.3 collective-permute-start.4
  38.3 1.4 %collective-permute-done.6 = f32[24,128]{1,0:T(8,128)S(1)} collective-permute-done((f32[24,128]{1,0:T(8,128)S(1)}, f32[24,128]{1,0:T(8,128)S(1)}, u32[]{:S(2)}, u32[]{:S(2)}) %collective-permute-start.6) | collective-permute-done | bytes 12320 | tf_op jit(solution)/shard_map/ppermute | solution.py:416
  39.7 1.5 %collective-permute-done.5 = f32[24,128]{1,0:T(8,128)S(1)} collective-permute-done((f32[24,128]{1,0:T(8,128)S(1)}, f32[24,128]{1,0:T(8,128)S(1)}, u32[]{:S(2)}, u32[]{:S(2)}) %collective-permute-start.5) | collective-permute-done | bytes 12320 | tf_op jit(solution)/shard_map/ppermute | solution.py:416
  41.2 0.6 collective-permute-done.4
  42.0 0.1 collective-permute-start.7
  42.1 2.3 %fetch.2.refs_1_.refs_0_ = bf16[32,96,256]{2,1,0:T(8,128)(2,1)} custom-call(bf16[32,256,256]{2,1,0:T(8,128)(2,1)} %bitcast.80, f32[8,512]{1,0:T(8,128)S(1)} %get-tuple-element.11.refs_0_.st_ref), custom_call_target="tpu_custom_call" | custom-call | bytes 6291456 | tf_op jit(solution)/shard_map/fetch/pallas_call | solution.py:233
  44.5 0.0 collective-permute-done.7
  44.7 3.3 %collective-permute-start.10 = (f32[24,128]{1,0:T(8,128)S(1)}, f32[24,128]{1,0:T(8,128)S(1)}, u32[]{:S(2)}, u32[]{:S(2)}) collective-permute-start(f32[24,128]{1,0:T(8,128)S(1)} %get-tuple-element.44), channel_id=1, source_target_pairs={{0,6},{1,7},{2,4},{3,5},{4,2},{5,3},{6,0},{7,1},{8,14},{9,15},{10,... | collective-permute-start | bytes 36872 | tf_op jit(solution)/shard_map/ppermute | solution.py:416
  48.0 0.0 collective-permute-start.9
  48.0 1.1 collective-permute-start.8
  49.1 14.8 %collective-permute-done.10 = f32[24,128]{1,0:T(8,128)S(1)} collective-permute-done((f32[24,128]{1,0:T(8,128)S(1)}, f32[24,128]{1,0:T(8,128)S(1)}, u32[]{:S(2)}, u32[]{:S(2)}) %collective-permute-start.10) | collective-permute-done | bytes 12320 | tf_op jit(solution)/shard_map/ppermute | solution.py:416
  63.9 13.6 %collective-permute-done.9 = f32[24,128]{1,0:T(8,128)S(1)} collective-permute-done((f32[24,128]{1,0:T(8,128)S(1)}, f32[24,128]{1,0:T(8,128)S(1)}, u32[]{:S(2)}, u32[]{:S(2)}) %collective-permute-start.9) | collective-permute-done | bytes 12320 | tf_op jit(solution)/shard_map/ppermute | solution.py:416
  77.5 0.0 collective-permute-done.8
  77.6 0.6 fusion.12
  78.1 0.0 all-to-all-done
  78.1 4.7 %all-to-all-start.1 = ((bf16[32,96,256]{2,1,0:T(8,128)(2,1)}), bf16[32,96,256]{2,1,0:T(8,128)(2,1)}, u32[]{:S(2)}, u32[]{:S(2)}) async-start(bf16[32,96,256]{2,1,0:T(8,128)(2,1)} %release.3), calls=%async_computation.1 | async-start | bytes 3145728 | tf_op jit(solution)/shard_map/all_to_all | solution.py:419
  82.9 1.2 divide_subtract_fusion
  84.1 0.0 copy-start.9
  84.1 0.8 copy-done.9
  84.9 0.3 collective-permute-start.11
  85.1 1.3 collective-permute-done.11
  86.5 1.0 bitcast_add_fusion.refs_0_
  87.5 1.8 %collective-permute-start.12 = (f32[4,64,256]{2,1,0:T(8,128)S(1)}, f32[4,64,256]{2,1,0:T(8,128)S(1)}, u32[]{:S(2)}, u32[]{:S(2)}) collective-permute-start(f32[4,64,256]{2,1,0:T(8,128)S(1)} %bitcast_add_fusion.refs_0_), channel_id=1, source_target_pairs={{0,8},{8,0},{16,24},{24,16},{1,9},{9,1},{17,25},{25,17},{2,10},{10... | collective-permute-start | bytes 786440 | tf_op jit(solution)/shard_map/ppermute | solution.py:416
  89.2 1.5 %collective-permute-start.13 = (f32[4,64,256]{2,1,0:T(8,128)S(1)}, f32[4,64,256]{2,1,0:T(8,128)S(1)}, u32[]{:S(2)}, u32[]{:S(2)}) collective-permute-start(f32[4,64,256]{2,1,0:T(8,128)S(1)} %bitcast_add_fusion.refs_0_), channel_id=1, source_target_pairs={{0,16},{8,24},{16,0},{24,8},{1,17},{9,25},{17,1},{25,9},{2,18},{10... | collective-permute-start | bytes 786440 | tf_op jit(solution)/shard_map/ppermute | solution.py:416
  90.7 0.3 collective-permute-start.14
  91.0 0.9 copy-done.8
  92.0 10.1 %weight_gradient.1._ = f32[8192,256]{1,0:T(8,128)} custom-call(s32[1]{0:T(128)S(6)} %mul.18.base_ref, bf16[512,256]{1,0:T(8,128)(2,1)S(1)} %copy-done.8, s32[1,512]{1,0:T(1,128)S(1)} %bitcast.78, f32[8,512]{1,0:T(8,128)S(1)} %get-tuple-element.11.refs_0_.st_ref, f32[1,512]{1,0:T(1,128)S(1)} %bitcast.74, bf16[8192,256]{1,0:T(8,128)(2,1)} %w_ref.3), custom_call_target="tpu_custom_call" | custom-call | flops 12884901888 | bytes 12582912 | tf_op jit(solution)/shard_map/weight_gradient/pallas_call | solution.py:179
  102.2 0.1 dynamic_slice.66.refs_5_
  102.2 8.7 %place_rows.1 = (f32[16384,128]{1,0:T(8,128)S(1)}, f32[8,128]{1,0:T(8,128)S(1)}) custom-call(s32[1]{0:T(128)} %bitcast.me_ref, s32[8192]{0:T(1024)S(1)} %bitcast.72, bf16[5120,256]{1,0:T(8,128)(2,1)S(1)} %bitcast.71, f32[8192,256]{1,0:T(8,128)} %weight_gradient.1._), custom_call_target="tpu_custom_call" | custom-call | bytes 41943040 | tf_op jit(solution)/shard_map/place_rows/pallas_call | solution.py:329
  111.0 3.3 %copy-done = f32[16384,128]{1,0:T(8,128)} copy-done((f32[16384,128]{1,0:T(8,128)}, f32[16384,128]{1,0:T(8,128)S(1)}, u32[]{:S(2)}) %copy-start) | copy-done | bytes 8388632
  114.3 0.0 collective-permute-done.12.refs_1_
  114.3 0.0 collective-permute-done.13.refs_2_
  114.3 0.0 collective-permute-done.14.refs_3_
  114.3 0.1 join.3
  114.4 3.6 %collective-permute-start.17 = (f32[64,256]{1,0:T(8,128)S(1)}, f32[64,256]{1,0:T(8,128)S(1)}, u32[]{:S(2)}, u32[]{:S(2)}) collective-permute-start(f32[64,256]{1,0:T(8,128)S(1)} %get-tuple-element.19), channel_id=1, source_target_pairs={{0,6},{1,7},{2,4},{3,5},{4,2},{5,3},{6,0},{7,1},{8,14},{9,15},{10,... | collective-permute-start | bytes 196616 | tf_op jit(solution)/shard_map/ppermute | solution.py:416
  118.0 0.0 collective-permute-start.16
  118.0 0.8 collective-permute-start.15
  118.9 4.8 %all-to-all-done.1 = bf16[32,96,256]{2,1,0:T(8,128)(2,1)} async-done(((bf16[32,96,256]{2,1,0:T(8,128)(2,1)}), bf16[32,96,256]{2,1,0:T(8,128)(2,1)}, u32[]{:S(2)}, u32[]{:S(2)}) %all-to-all-start.1) | async-done | bytes 1572896 | tf_op jit(solution)/shard_map/all_to_all | solution.py:419
  123.7 12.5 %place_and_blend.1 = bf16[8192,256]{1,0:T(8,128)(2,1)} custom-call(s32[1]{0:T(128)} %bitcast.me_ref, s32[8192]{0:T(1024)S(1)} %bitcast.73, bf16[8192,256]{1,0:T(8,128)(2,1)} %get-tuple-element.16.w_ref, bf16[3072,256]{1,0:T(8,128)(2,1)} %bitcast.43.row_ref, f32[16384,128]{1,0:T(8,128)} %copy-done), custom_call_target="tpu_custom_call" | custom-call | bytes 25165824 | tf_op jit(solution)/shard_map/place_and_blend/pallas_call | solution.py:382
  136.2 0.0 collective-permute-done.17
  136.2 0.0 collective-permute-done.16
  136.2 0.0 collective-permute-done.15
  136.2 0.7 fusion.1
  (44 shorter events, 0.5 us)
Async XLA Ops:
  0.6 9.1 %collective-permute-start = (bf16[64,256]{1,0:T(8,128)(2,1)}, bf16[64,256]{1,0:T(8,128)(2,1)S(1)}, u32[]{:S(2)}, u32[]{:S(2)}) collective-permute-start(bf16[64,256]{1,0:T(8,128)(2,1)} %param.5), channel_id=1, source_target_pairs={{0,2},{1,3},{2,0},{3,1},{4,6},{5,7},{6,4},{7,5},{8,10},{9,11},{10,... | collective-permute-start | bytes 98312 | tf_op jit(solution)/shard_map/ppermute | solution.py:416
  3.7 6.0 %collective-permute-start.1 = (bf16[64,256]{1,0:T(8,128)(2,1)}, bf16[64,256]{1,0:T(8,128)(2,1)S(1)}, u32[]{:S(2)}, u32[]{:S(2)}) collective-permute-start(bf16[64,256]{1,0:T(8,128)(2,1)} %param.5), channel_id=1, source_target_pairs={{0,4},{1,5},{2,6},{3,7},{4,0},{5,1},{6,2},{7,3},{8,12},{9,13},{10,... | collective-permute-start | bytes 98312 | tf_op jit(solution)/shard_map/ppermute | solution.py:416
  6.3 5.9 %collective-permute-start.2 = (bf16[64,256]{1,0:T(8,128)(2,1)}, bf16[64,256]{1,0:T(8,128)(2,1)S(1)}, u32[]{:S(2)}, u32[]{:S(2)}) collective-permute-start(bf16[64,256]{1,0:T(8,128)(2,1)} %param.5), channel_id=1, source_target_pairs={{0,6},{1,7},{2,4},{3,5},{4,2},{5,3},{6,0},{7,1},{8,14},{9,15},{10,... | collective-permute-start | bytes 98312 | tf_op jit(solution)/shard_map/ppermute | solution.py:416
  12.2 0.7 copy-start.10
  12.9 4.0 %copy-start.5 = (s32[512]{0:T(512)S(1)}, s32[512]{0:T(512)}, u32[]{:S(2)}) copy-start(s32[512]{0:T(512)} %param.6) | copy-start | bytes 6148
  12.9 4.1 %copy-start.12 = (s32[8192]{0:T(1024)S(1)}, s32[8192]{0:T(1024)}, u32[]{:S(2)}) copy-start(s32[8192]{0:T(1024)} %param.9) | copy-start | bytes 98308
  12.9 3.6 %copy-start.11 = (bf16[256,256]{1,0:T(8,128)(2,1)S(1)}, bf16[256,256]{1,0:T(8,128)(2,1)}, u32[]{:S(2)}) copy-start(bf16[256,256]{1,0:T(8,128)(2,1)} %copy-done.10) | copy-start | bytes 393220
  12.9 65.2 %all-to-all-start = ((bf16[32,160,256]{2,1,0:T(8,128)(2,1)}), bf16[32,160,256]{2,1,0:T(8,128)(2,1)S(1)}, u32[]{:S(2)}, u32[]{:S(2)}) async-start(bf16[32,160,256]{2,1,0:T(8,128)(2,1)} %release.2), calls=%async_computation | async-start | bytes 5242880 | tf_op jit(solution)/shard_map/all_to_all | solution.py:419
  16.5 1.4 %collective-permute-start.3 = (bf16[256,256]{1,0:T(8,128)(2,1)S(1)}, bf16[256,256]{1,0:T(8,128)(2,1)S(1)}, u32[]{:S(2)}, u32[]{:S(2)}) collective-permute-start(bf16[256,256]{1,0:T(8,128)(2,1)S(1)} %copy-done.11), channel_id=1, source_target_pairs={{0,1},{1,0},{2,3},{3,2},{4,5},{5,4},{6,7},{7,6},{8,9},{9,8},{10,11... | collective-permute-start | bytes 393224 | tf_op jit(solution)/shard_map/ppermute | solution.py:416
  18.0 0.7 copy-start.3
  18.7 0.9 copy-start.4
  33.2 0.8 copy-start.1
  34.0 0.7 copy-start.7
  34.7 4.9 %collective-permute-start.6 = (f32[24,128]{1,0:T(8,128)S(1)}, f32[24,128]{1,0:T(8,128)S(1)}, u32[]{:S(2)}, u32[]{:S(2)}) collective-permute-start(f32[24,128]{1,0:T(8,128)S(1)} %get-tuple-element.50), channel_id=1, source_target_pairs={{0,24},{8,16},{16,8},{24,0},{1,25},{9,17},{17,9},{25,1},{2,26},{10... | collective-permute-start | bytes 36872 | tf_op jit(solution)/shard_map/ppermute | solution.py:416
  37.5 3.8 %collective-permute-start.5 = (f32[24,128]{1,0:T(8,128)S(1)}, f32[24,128]{1,0:T(8,128)S(1)}, u32[]{:S(2)}, u32[]{:S(2)}) collective-permute-start(f32[24,128]{1,0:T(8,128)S(1)} %get-tuple-element.49), channel_id=1, source_target_pairs={{0,16},{8,24},{16,0},{24,8},{1,17},{9,25},{17,1},{25,9},{2,18},{10... | collective-permute-start | bytes 36872 | tf_op jit(solution)/shard_map/ppermute | solution.py:416
  38.0 3.8 %collective-permute-start.4 = (f32[24,128]{1,0:T(8,128)S(1)}, f32[24,128]{1,0:T(8,128)S(1)}, u32[]{:S(2)}, u32[]{:S(2)}) collective-permute-start(f32[24,128]{1,0:T(8,128)S(1)} %get-tuple-element.48), channel_id=1, source_target_pairs={{0,8},{8,0},{16,24},{24,16},{1,9},{9,1},{17,25},{25,17},{2,10},{10... | collective-permute-start | bytes 36872 | tf_op jit(solution)/shard_map/ppermute | solution.py:416
  42.0 2.4 %collective-permute-start.7 = (f32[40,128]{1,0:T(8,128)S(1)}, f32[40,128]{1,0:T(8,128)S(1)}, u32[]{:S(2)}, u32[]{:S(2)}) collective-permute-start(f32[40,128]{1,0:T(8,128)S(1)} %get-tuple-element.46), channel_id=1, source_target_pairs={{0,1},{1,0},{2,3},{3,2},{4,5},{5,4},{6,7},{7,6},{8,9},{9,8},{10,11... | collective-permute-start | bytes 61448 | tf_op jit(solution)/shard_map/ppermute | solution.py:416
  44.7 19.3 %collective-permute-start.10 = (f32[24,128]{1,0:T(8,128)S(1)}, f32[24,128]{1,0:T(8,128)S(1)}, u32[]{:S(2)}, u32[]{:S(2)}) collective-permute-start(f32[24,128]{1,0:T(8,128)S(1)} %get-tuple-element.44), channel_id=1, source_target_pairs={{0,6},{1,7},{2,4},{3,5},{4,2},{5,3},{6,0},{7,1},{8,14},{9,15},{10,... | collective-permute-start | bytes 36872 | tf_op jit(solution)/shard_map/ppermute | solution.py:416
  48.0 29.5 %collective-permute-start.9 = (f32[24,128]{1,0:T(8,128)S(1)}, f32[24,128]{1,0:T(8,128)S(1)}, u32[]{:S(2)}, u32[]{:S(2)}) collective-permute-start(f32[24,128]{1,0:T(8,128)S(1)} %get-tuple-element.43), channel_id=1, source_target_pairs={{0,4},{1,5},{2,6},{3,7},{4,0},{5,1},{6,2},{7,3},{8,12},{9,13},{10,... | collective-permute-start | bytes 36872 | tf_op jit(solution)/shard_map/ppermute | solution.py:416
  48.0 29.5 %collective-permute-start.8 = (f32[24,128]{1,0:T(8,128)S(1)}, f32[24,128]{1,0:T(8,128)S(1)}, u32[]{:S(2)}, u32[]{:S(2)}) collective-permute-start(f32[24,128]{1,0:T(8,128)S(1)} %get-tuple-element.42), channel_id=1, source_target_pairs={{0,2},{1,3},{2,0},{3,1},{4,6},{5,7},{6,4},{7,5},{8,10},{9,11},{10,... | collective-permute-start | bytes 36872 | tf_op jit(solution)/shard_map/ppermute | solution.py:416
  78.1 4.7 %copy-start.2 = (f32[512]{0:T(512)S(1)}, f32[512]{0:T(512)}, u32[]{:S(2)}) copy-start(f32[512]{0:T(512)} %get-tuple-element.39.refs_1_) | copy-start | bytes 6148
  78.1 45.5 %all-to-all-start.1 = ((bf16[32,96,256]{2,1,0:T(8,128)(2,1)}), bf16[32,96,256]{2,1,0:T(8,128)(2,1)}, u32[]{:S(2)}, u32[]{:S(2)}) async-start(bf16[32,96,256]{2,1,0:T(8,128)(2,1)} %release.3), calls=%async_computation.1 | async-start | bytes 3145728 | tf_op jit(solution)/shard_map/all_to_all | solution.py:419
  84.1 0.8 copy-start.9
  84.9 1.6 %collective-permute-start.11 = (f32[4,64,256]{2,1,0:T(8,128)S(1)}, f32[4,64,256]{2,1,0:T(8,128)S(1)}, u32[]{:S(2)}, u32[]{:S(2)}) collective-permute-start(f32[4,64,256]{2,1,0:T(8,128)S(1)} %dynamic-slice_bitcast_fusion), channel_id=1, source_target_pairs={{0,1},{1,0},{2,3},{3,2},{4,5},{5,4},{6,7},{7,6},{8,9},{9,8},{10,11... | collective-permute-start | bytes 786440 | tf_op jit(solution)/shard_map/ppermute | solution.py:416
  87.5 26.8 %collective-permute-start.12 = (f32[4,64,256]{2,1,0:T(8,128)S(1)}, f32[4,64,256]{2,1,0:T(8,128)S(1)}, u32[]{:S(2)}, u32[]{:S(2)}) collective-permute-start(f32[4,64,256]{2,1,0:T(8,128)S(1)} %bitcast_add_fusion.refs_0_), channel_id=1, source_target_pairs={{0,8},{8,0},{16,24},{24,16},{1,9},{9,1},{17,25},{25,17},{2,10},{10... | collective-permute-start | bytes 786440 | tf_op jit(solution)/shard_map/ppermute | solution.py:416
  89.2 25.0 %collective-permute-start.13 = (f32[4,64,256]{2,1,0:T(8,128)S(1)}, f32[4,64,256]{2,1,0:T(8,128)S(1)}, u32[]{:S(2)}, u32[]{:S(2)}) collective-permute-start(f32[4,64,256]{2,1,0:T(8,128)S(1)} %bitcast_add_fusion.refs_0_), channel_id=1, source_target_pairs={{0,16},{8,24},{16,0},{24,8},{1,17},{9,25},{17,1},{25,9},{2,18},{10... | collective-permute-start | bytes 786440 | tf_op jit(solution)/shard_map/ppermute | solution.py:416
  90.7 23.6 %collective-permute-start.14 = (f32[4,64,256]{2,1,0:T(8,128)S(1)}, f32[4,64,256]{2,1,0:T(8,128)S(1)}, u32[]{:S(2)}, u32[]{:S(2)}) collective-permute-start(f32[4,64,256]{2,1,0:T(8,128)S(1)} %bitcast_add_fusion.refs_0_), channel_id=1, source_target_pairs={{0,24},{8,16},{16,8},{24,0},{1,25},{9,17},{17,9},{25,1},{2,26},{10... | collective-permute-start | bytes 786440 | tf_op jit(solution)/shard_map/ppermute | solution.py:416
  91.0 0.9 copy-start.8
  102.2 12.0 %copy-start.6 = (f32[64]{0:T(128)}, f32[64]{0:T(128)S(1)}, u32[]{:S(2)}) copy-start(f32[64]{0:T(128)S(1)} %dynamic_slice.66.refs_5_) | copy-start | bytes 772
  111.0 3.3 %copy-start = (f32[16384,128]{1,0:T(8,128)}, f32[16384,128]{1,0:T(8,128)S(1)}, u32[]{:S(2)}) copy-start(f32[16384,128]{1,0:T(8,128)S(1)} %get-tuple-element.17.in_ref) | copy-start | bytes 25165828
  114.4 21.8 %collective-permute-start.17 = (f32[64,256]{1,0:T(8,128)S(1)}, f32[64,256]{1,0:T(8,128)S(1)}, u32[]{:S(2)}, u32[]{:S(2)}) collective-permute-start(f32[64,256]{1,0:T(8,128)S(1)} %get-tuple-element.19), channel_id=1, source_target_pairs={{0,6},{1,7},{2,4},{3,5},{4,2},{5,3},{6,0},{7,1},{8,14},{9,15},{10,... | collective-permute-start | bytes 196616 | tf_op jit(solution)/shard_map/ppermute | solution.py:416
  118.0 18.2 %collective-permute-start.16 = (f32[64,256]{1,0:T(8,128)S(1)}, f32[64,256]{1,0:T(8,128)S(1)}, u32[]{:S(2)}, u32[]{:S(2)}) collective-permute-start(f32[64,256]{1,0:T(8,128)S(1)} %get-tuple-element.20), channel_id=1, source_target_pairs={{0,4},{1,5},{2,6},{3,7},{4,0},{5,1},{6,2},{7,3},{8,12},{9,13},{10,... | collective-permute-start | bytes 196616 | tf_op jit(solution)/shard_map/ppermute | solution.py:416
  118.0 18.2 %collective-permute-start.15 = (f32[64,256]{1,0:T(8,128)S(1)}, f32[64,256]{1,0:T(8,128)S(1)}, u32[]{:S(2)}, u32[]{:S(2)}) collective-permute-start(f32[64,256]{1,0:T(8,128)S(1)} %get-tuple-element.18), channel_id=1, source_target_pairs={{0,2},{1,3},{2,0},{3,1},{4,6},{5,7},{6,4},{7,5},{8,10},{9,11},{10,... | collective-permute-start | bytes 196616 | tf_op jit(solution)/shard_map/ppermute | solution.py:416

commit v16 on v15

--- a/solution.py
+++ b/solution.py
@@ -343,61 +343,80 @@
     )(me, slots, rows, after)
 
 
+def split_copies(source_ref, target_ref, sem):
+    lanes = sem.shape[0]
+    size = source_ref.shape[0] // lanes
+    parts = [pl.ds(c * size, size) for c in range(lanes)]
+    return [
+        pltpu.make_async_copy(source_ref.at[part, :], target_ref.at[part, :], sem.at[c])
+        for c, part in enumerate(parts)
+    ]
+
+
 def blend_kernel(
-    me_ref, slot_ref, w_ref, row_ref, in_ref, o_ref, held_ref, stage_ref, sem, *, peers, run, first
+    me_ref, slot_ref, row_ref, w_ref, in_ref, o_ref, held_ref, stage_ref, what_ref, new_ref,
+    held_sem, what_sem, new_sem, *, peers, run, first,
 ):
-    step = pl.program_id(0)
-    tile = o_ref.shape[0]
-
-    @pl.when(step == 0)
-    def _():
-        lanes = sem.shape[0]
-        part = held_ref.shape[0] // lanes
-        parts = [pl.ds(c * part, part) for c in range(lanes)]
-        copies = [
-            pltpu.make_async_copy(in_ref.at[at, :], held_ref.at[at, :], sem.at[c])
-            for c, at in enumerate(parts)
-        ]
-        for copy in copies:
-            copy.start()
-        place_runs(me_ref, slot_ref, row_ref, held_ref, stage_ref, copies, peers, run, first)
-
-    block = math.gcd(tile, 64)
-    for begin in range(0, tile, block):
-        rows = pl.ds(begin, block)
-        at = pl.multiple_of((step * tile + begin) * 2, 2 * block)
-        low = w_ref[rows, :128].astype(jnp.float32) + held_ref[pl.ds(at, block, stride=2), :]
-        high = w_ref[rows, 128:].astype(jnp.float32) + held_ref[pl.ds(at + 1, block, stride=2), :]
-        inv = lax.rsqrt(jnp.sum(low * low + high * high, axis=1, keepdims=True) + 1e-06)
-        o_ref[rows, :128] = (low * inv).astype(jnp.bfloat16)
-        o_ref[rows, 128:] = (high * inv).astype(jnp.bfloat16)
+    copies = split_copies(in_ref, held_ref, held_sem)
+    weights = split_copies(w_ref, what_ref, what_sem)
+    for copy in copies + weights:
+        copy.start()
+    place_runs(me_ref, slot_ref, row_ref, held_ref, stage_ref, copies, peers, run, first)
+    for copy in weights:
+        copy.wait()
+    classes = o_ref.shape[0]
+    pieces = new_sem.shape[0]
+    piece = classes // pieces
+    block = math.gcd(piece, 64)
+
+    def leaving(c):
+        part = pl.ds(pl.multiple_of(c * piece, piece), piece)
+        return pltpu.make_async_copy(new_ref.at[part, :], o_ref.at[part, :], new_sem.at[c])
+
+    def blend(c, carry):
+        for begin in range(0, piece, block):
+            start = pl.multiple_of(c * piece + begin, block)
+            rows = pl.ds(start, block)
+            low = held_ref[pl.ds(start * 2, block, stride=2), :]
+            high = held_ref[pl.ds(start * 2 + 1, block, stride=2), :]
+            low = low + what_ref[rows, :128].astype(jnp.float32)
+            high = high + what_ref[rows, 128:].astype(jnp.float32)
+            inv = lax.rsqrt(jnp.sum(low * low + high * high, axis=1, keepdims=True) + 1e-06)
+            new_ref[rows, :128] = (low * inv).astype(jnp.bfloat16)
+            new_ref[rows, 128:] = (high * inv).astype(jnp.bfloat16)
+        leaving(c).start()
+        return carry
+
+    lax.fori_loop(0, pieces, blend, 0)
+    for c in range(pieces):
+        leaving(c).wait()
 
 
 def place_and_blend(me, slots, rows, held, weights, peers, run, first):
     classes, width = weights.shape
-    tile = math.gcd(classes, 2048)
     smem = pl.BlockSpec(memory_space=pltpu.SMEM)
     vmem = pl.BlockSpec(memory_space=pltpu.VMEM)
-    tiles = pl.BlockSpec((tile, width), lambda i: (i, 0))
+    anywhere = pl.BlockSpec(memory_space=pl.ANY)
     return pl.pallas_call(
         functools.partial(blend_kernel, peers=peers, run=run, first=first),
-        grid=(classes // tile,),
-        in_specs=[smem, smem, tiles, vmem, pl.BlockSpec(memory_space=pl.ANY)],
-        out_specs=tiles,
+        in_specs=[smem, smem, vmem, anywhere, anywhere],
+        out_specs=anywhere,
         out_shape=pltpu.HBM((classes, width), jnp.bfloat16),
         scratch_shapes=[
             pltpu.VMEM(held.shape, jnp.float32),
             pltpu.VMEM((2 * rows.shape[0], 128), jnp.float32),
+            pltpu.VMEM((classes, width), jnp.bfloat16),
+            pltpu.VMEM((classes, width), jnp.bfloat16),
             pltpu.SemaphoreType.DMA((4,)),
-        ],
-        compiler_params=pltpu.CompilerParams(
-            dimension_semantics=("arbitrary",), vmem_limit_bytes=32 * MIB
-        ),
+            pltpu.SemaphoreType.DMA((2,)),
+            pltpu.SemaphoreType.DMA((8,)),
+        ],
+        compiler_params=pltpu.CompilerParams(vmem_limit_bytes=32 * MIB),
         cost_estimate=pl.CostEstimate(
             flops=0, bytes_accessed=12 * classes * width, transcendentals=0
         ),
         name="place_and_blend",
-    )(me, slots, weights, rows, held)
+    )(me, slots, rows, weights, held)
 
 
 def shards(embeddings, labels, class_weights, centroids, centroid_class):
@@ -462,9 +481,11 @@
     grad = (a / total[:, None] - b).reshape(half, 2, rows_local, width)
     grad = sum(swap(index(grad, core ^ c, 1, False), "rep", c) for c in range(2))
     grad = join([swap(grad, "grp", j) for j in range(groups)], [token, loss])
-    embedding_gradient = sum(
-        swap(index(grad, deep ^ z, 0, False), "rep", 2 * z) for z in range(half)
-    )
+    sent = grad.astype(jnp.bfloat16)
+    parts = [swap(index(sent, deep ^ z, 0, False), "rep", 2 * z) for z in range(1, half)]
+    embedding_gradient = index(grad, deep, 0, False)
+    for part in parts:
+        embedding_gradient = embedding_gradient + part.astype(jnp.float32)
 
     refreshed = place_and_blend(me, slots, rows_b, in_hbm(held), in_hbm(what), peers, run, cut)
     return (loss, embedding_gradient, weight_grad, refreshed)

time: 138 us -> 135 us (0.978)
  waiting for transfers between devices: 41.5 us -> 39.9 us
  Pallas kernels: 50 us -> 48.6 us
    all_to_all x2, waiting for transfers between devices: 4.84 us -> 3.24 us  [relay(): return lax.all_to_all(sent, ALL, 0, 0, tiled=True).reshape(-1, width)]
where the time goes in v16:
time: 135 us; the launch traced here: 134 us
  Pallas kernels  48.6 us (36%)
  waiting for transfers between devices  39.9 us (30%)
  starting transfers between devices  30.6 us (23%)
  local copies, waits for them, and re-layouts  10.2 us (8%)
  other arithmetic  3.64 us (3%)
    ppermute x18, waiting for transfers between devices, swap(): lax.ppermute(value, axis, [(i, i ^ k) for i in range(size)])  36.6 us
    ppermute x18, starting transfers between devices, swap(): lax.ppermute(value, axis, [(i, i ^ k) for i in range(size)])  22.3 us
    pallas_call x1, Pallas kernels, forward(): pl.pallas_call(functools.partial(forward_kernel, classes=classes, reps=re...  13.6 us
    pallas_call x1, Pallas kernels, place_and_blend(): pl.pallas_call(functools.partial(blend_kernel, peers=peers, run=run, firs...  11.1 us
    pallas_call x1, Pallas kernels, weight_gradient(): pl.pallas_call(weight_kernel, grid=(classes // tile,), in_specs=[pl.Block...  10.1 us
    unnamed x32, local copies, waits for them, and re-layouts  9.68 us
    pallas_call x1, Pallas kernels, place_rows(): pl.pallas_call(functools.partial(place_kernel, peers=peers, run=run, firs...  8.73 us
    all_to_all x2, starting transfers between devices, relay(): return lax.all_to_all(sent, ALL, 0, 0, tiled=True).reshape(-1, width)  8.31 us
  transfers between devices with their start and end apart: 20, of which 9 were waited for; matrix products, arithmetic and copies ran while one was open for 3% of the time, Pallas kernels for 36%

profile of v16, /device:TPU:0, one launch (start us, length us, event | category | flops | bytes accessed | tf_op | source)
XLA Modules:
  0.0 133.9 jit_solution(10912831847283435803)
XLA Ops:
  0.6 3.1 %collective-permute-start = (bf16[64,256]{1,0:T(8,128)(2,1)}, bf16[64,256]{1,0:T(8,128)(2,1)S(1)}, u32[]{:S(2)}, u32[]{:S(2)}) collective-permute-start(bf16[64,256]{1,0:T(8,128)(2,1)} %param.5), channel_id=1, source_target_pairs={{0,2},{1,3},{2,0},{3,1},{4,6},{5,7},{6,4},{7,5},{8,10},{9,11},{10,... | collective-permute-start | bytes 98312 | tf_op jit(solution)/shard_map/ppermute | solution.py:435
  3.7 2.6 %collective-permute-start.1 = (bf16[64,256]{1,0:T(8,128)(2,1)}, bf16[64,256]{1,0:T(8,128)(2,1)S(1)}, u32[]{:S(2)}, u32[]{:S(2)}) collective-permute-start(bf16[64,256]{1,0:T(8,128)(2,1)} %param.5), channel_id=1, source_target_pairs={{0,4},{1,5},{2,6},{3,7},{4,0},{5,1},{6,2},{7,3},{8,12},{9,13},{10,... | collective-permute-start | bytes 98312 | tf_op jit(solution)/shard_map/ppermute | solution.py:435
  6.3 0.0 collective-permute-start.2
  6.3 0.8 constant_dynamic-update-slice_fusion.3
  7.1 2.6 %fetch.3.refs_0_ = bf16[32,160,256]{2,1,0:T(8,128)(2,1)} custom-call(bf16[32,256,256]{2,1,0:T(8,128)(2,1)} %bitcast.79), custom_call_target="tpu_custom_call" | custom-call | bytes 10485760 | tf_op jit(solution)/shard_map/fetch/pallas_call | solution.py:233
  9.7 0.0 collective-permute-done
  9.8 0.0 collective-permute-done.1
  9.8 2.4 %collective-permute-done.2 = bf16[64,256]{1,0:T(8,128)(2,1)S(1)} collective-permute-done((bf16[64,256]{1,0:T(8,128)(2,1)}, bf16[64,256]{1,0:T(8,128)(2,1)S(1)}, u32[]{:S(2)}, u32[]{:S(2)}) %collective-permute-start.2) | collective-permute-done | bytes 32800 | tf_op jit(solution)/shard_map/ppermute | solution.py:435
  12.2 0.7 copy-done.10
  12.9 3.6 %all-to-all-start = ((bf16[32,160,256]{2,1,0:T(8,128)(2,1)}), bf16[32,160,256]{2,1,0:T(8,128)(2,1)S(1)}, u32[]{:S(2)}, u32[]{:S(2)}) async-start(bf16[32,160,256]{2,1,0:T(8,128)(2,1)} %release.2), calls=%async_computation | async-start | bytes 5242880 | tf_op jit(solution)/shard_map/all_to_all | solution.py:438
  16.5 0.3 collective-permute-start.3
  16.9 0.1 copy.16.lab_ref
  17.1 0.8 collective-permute-done.3
  18.0 0.0 copy-start.3
  18.0 0.7 copy-done.3
  18.7 0.9 copy-done.4
  19.6 13.6 %forward_sums.1 = (bf16[512,256]{1,0:T(8,128)(2,1)S(1)}, f32[512,256]{1,0:T(8,128)S(1)}, f32[512,256]{1,0:T(8,128)S(1)}, f32[8,512]{1,0:T(8,128)S(1)}, bf16[8192,256]{1,0:T(8,128)(2,1)}) custom-call(s32[1]{0:T(128)S(6)} %mul.18.base_ref, s32[1]{0:T(128)} %bitcast.1.rep_ref, s32[512,1]{1,0:T(8,128)S(1)} %copy.16.lab_ref, bf16[8192,256]{1,0:T(8,128)(2,1)} %w_ref.3, ...), custom_call_target="tpu_custom_call" | custom-call | flops 12884901888 | bytes 4194304 | tf_op jit(solution)/shard_map/forward_sums/pallas_call | solution.py:111
  33.2 0.8 copy-done.1
  34.0 0.7 copy-done.7
  34.7 2.7 %collective-permute-start.6 = (f32[24,128]{1,0:T(8,128)S(1)}, f32[24,128]{1,0:T(8,128)S(1)}, u32[]{:S(2)}, u32[]{:S(2)}) collective-permute-start(f32[24,128]{1,0:T(8,128)S(1)} %get-tuple-element.50), channel_id=1, source_target_pairs={{0,24},{8,16},{16,8},{24,0},{1,25},{9,17},{17,9},{25,1},{2,26},{10... | collective-permute-start | bytes 36872 | tf_op jit(solution)/shard_map/ppermute | solution.py:435
  37.5 0.6 collective-permute-start.5
  38.0 0.3 collective-permute-start.4
  38.3 1.4 %collective-permute-done.6 = f32[24,128]{1,0:T(8,128)S(1)} collective-permute-done((f32[24,128]{1,0:T(8,128)S(1)}, f32[24,128]{1,0:T(8,128)S(1)}, u32[]{:S(2)}, u32[]{:S(2)}) %collective-permute-start.6) | collective-permute-done | bytes 12320 | tf_op jit(solution)/shard_map/ppermute | solution.py:435
  39.7 1.5 %collective-permute-done.5 = f32[24,128]{1,0:T(8,128)S(1)} collective-permute-done((f32[24,128]{1,0:T(8,128)S(1)}, f32[24,128]{1,0:T(8,128)S(1)}, u32[]{:S(2)}, u32[]{:S(2)}) %collective-permute-start.5) | collective-permute-done | bytes 12320 | tf_op jit(solution)/shard_map/ppermute | solution.py:435
  41.2 0.6 collective-permute-done.4
  42.0 0.1 collective-permute-start.7
  42.1 2.3 %fetch.2.refs_1_.refs_0_ = bf16[32,96,256]{2,1,0:T(8,128)(2,1)} custom-call(bf16[32,256,256]{2,1,0:T(8,128)(2,1)} %bitcast.80, f32[8,512]{1,0:T(8,128)S(1)} %get-tuple-element.11.refs_0_.st_ref), custom_call_target="tpu_custom_call" | custom-call | bytes 6291456 | tf_op jit(solution)/shard_map/fetch/pallas_call | solution.py:233
  44.5 0.0 collective-permute-done.7
  44.7 3.3 %collective-permute-start.10 = (f32[24,128]{1,0:T(8,128)S(1)}, f32[24,128]{1,0:T(8,128)S(1)}, u32[]{:S(2)}, u32[]{:S(2)}) collective-permute-start(f32[24,128]{1,0:T(8,128)S(1)} %get-tuple-element.44), channel_id=1, source_target_pairs={{0,6},{1,7},{2,4},{3,5},{4,2},{5,3},{6,0},{7,1},{8,14},{9,15},{10,... | collective-permute-start | bytes 36872 | tf_op jit(solution)/shard_map/ppermute | solution.py:435
  48.0 0.0 collective-permute-start.9
  48.0 1.1 collective-permute-start.8
  49.1 14.8 %collective-permute-done.10 = f32[24,128]{1,0:T(8,128)S(1)} collective-permute-done((f32[24,128]{1,0:T(8,128)S(1)}, f32[24,128]{1,0:T(8,128)S(1)}, u32[]{:S(2)}, u32[]{:S(2)}) %collective-permute-start.10) | collective-permute-done | bytes 12320 | tf_op jit(solution)/shard_map/ppermute | solution.py:435
  63.9 13.6 %collective-permute-done.9 = f32[24,128]{1,0:T(8,128)S(1)} collective-permute-done((f32[24,128]{1,0:T(8,128)S(1)}, f32[24,128]{1,0:T(8,128)S(1)}, u32[]{:S(2)}, u32[]{:S(2)}) %collective-permute-start.9) | collective-permute-done | bytes 12320 | tf_op jit(solution)/shard_map/ppermute | solution.py:435
  77.5 0.0 collective-permute-done.8
  77.6 0.6 fusion.12
  78.1 0.0 all-to-all-done
  78.1 4.7 %all-to-all-start.1 = ((bf16[32,96,256]{2,1,0:T(8,128)(2,1)}), bf16[32,96,256]{2,1,0:T(8,128)(2,1)}, u32[]{:S(2)}, u32[]{:S(2)}) async-start(bf16[32,96,256]{2,1,0:T(8,128)(2,1)} %release.3), calls=%async_computation.1 | async-start | bytes 3145728 | tf_op jit(solution)/shard_map/all_to_all | solution.py:438
  82.9 1.2 divide_subtract_fusion
  84.1 0.0 copy-start.9
  84.1 0.8 copy-done.9
  84.9 0.3 collective-permute-start.11
  85.1 1.3 %collective-permute-done.11 = f32[4,64,256]{2,1,0:T(8,128)S(1)} collective-permute-done((f32[4,64,256]{2,1,0:T(8,128)S(1)}, f32[4,64,256]{2,1,0:T(8,128)S(1)}, u32[]{:S(2)}, u32[]{:S(2)}) %collective-permute-start.11) | collective-permute-done | bytes 262176 | tf_op jit(solution)/shard_map/ppermute | solution.py:435
  86.5 1.0 bitcast_add_fusion.refs_0_
  87.5 1.8 %collective-permute-start.12 = (f32[4,64,256]{2,1,0:T(8,128)S(1)}, f32[4,64,256]{2,1,0:T(8,128)S(1)}, u32[]{:S(2)}, u32[]{:S(2)}) collective-permute-start(f32[4,64,256]{2,1,0:T(8,128)S(1)} %bitcast_add_fusion.refs_0_), channel_id=1, source_target_pairs={{0,8},{8,0},{16,24},{24,16},{1,9},{9,1},{17,25},{25,17},{2,10},{10... | collective-permute-start | bytes 786440 | tf_op jit(solution)/shard_map/ppermute | solution.py:435
  89.2 1.5 %collective-permute-start.13 = (f32[4,64,256]{2,1,0:T(8,128)S(1)}, f32[4,64,256]{2,1,0:T(8,128)S(1)}, u32[]{:S(2)}, u32[]{:S(2)}) collective-permute-start(f32[4,64,256]{2,1,0:T(8,128)S(1)} %bitcast_add_fusion.refs_0_), channel_id=1, source_target_pairs={{0,16},{8,24},{16,0},{24,8},{1,17},{9,25},{17,1},{25,9},{2,18},{10... | collective-permute-start | bytes 786440 | tf_op jit(solution)/shard_map/ppermute | solution.py:435
  90.7 0.3 collective-permute-start.14
  91.0 0.9 copy-done.8
  92.0 10.1 %weight_gradient.1._ = f32[8192,256]{1,0:T(8,128)} custom-call(s32[1]{0:T(128)S(6)} %mul.18.base_ref, bf16[512,256]{1,0:T(8,128)(2,1)S(1)} %copy-done.8, s32[1,512]{1,0:T(1,128)S(1)} %bitcast.78, f32[8,512]{1,0:T(8,128)S(1)} %get-tuple-element.11.refs_0_.st_ref, f32[1,512]{1,0:T(1,128)S(1)} %bitcast.74, bf16[8192,256]{1,0:T(8,128)(2,1)} %w_ref.3), custom_call_target="tpu_custom_call" | custom-call | flops 12884901888 | bytes 12582912 | tf_op jit(solution)/shard_map/weight_gradient/pallas_call | solution.py:179
  102.2 0.1 dynamic_slice.67.refs_5_
  102.2 8.7 %place_rows.1 = (f32[16384,128]{1,0:T(8,128)S(1)}, f32[8,128]{1,0:T(8,128)S(1)}) custom-call(s32[1]{0:T(128)} %bitcast.me_ref, s32[8192]{0:T(1024)S(1)} %bitcast.72, bf16[5120,256]{1,0:T(8,128)(2,1)S(1)} %bitcast.71, f32[8192,256]{1,0:T(8,128)} %weight_gradient.1._), custom_call_target="tpu_custom_call" | custom-call | bytes 41943040 | tf_op jit(solution)/shard_map/place_rows/pallas_call | solution.py:329
  111.0 3.3 %copy-done = f32[16384,128]{1,0:T(8,128)} copy-done((f32[16384,128]{1,0:T(8,128)}, f32[16384,128]{1,0:T(8,128)S(1)}, u32[]{:S(2)}) %copy-start) | copy-done | bytes 8388632
  114.3 0.0 collective-permute-done.12.refs_1_
  114.3 0.0 collective-permute-done.13.refs_2_
  114.3 0.0 collective-permute-done.14.refs_3_
  114.3 0.1 join.3
  114.4 3.6 %collective-permute-start.17 = (bf16[64,256]{1,0:T(8,128)(2,1)S(1)}, bf16[64,256]{1,0:T(8,128)(2,1)S(1)}, u32[]{:S(2)}, u32[]{:S(2)}) collective-permute-start(bf16[64,256]{1,0:T(8,128)(2,1)S(1)} %get-tuple-element.19), channel_id=1, source_target_pairs={{0,6},{1,7},{2,4},{3,5},{4,2},{5,3},{6,0},{7,1},{8,14},{9,15},{10,... | collective-permute-start | bytes 98312 | tf_op jit(solution)/shard_map/ppermute | solution.py:435
  118.0 0.0 collective-permute-start.16
  118.0 0.8 collective-permute-start.15
  118.9 3.2 %all-to-all-done.1 = bf16[32,96,256]{2,1,0:T(8,128)(2,1)} async-done(((bf16[32,96,256]{2,1,0:T(8,128)(2,1)}), bf16[32,96,256]{2,1,0:T(8,128)(2,1)}, u32[]{:S(2)}, u32[]{:S(2)}) %all-to-all-start.1) | async-done | bytes 1572896 | tf_op jit(solution)/shard_map/all_to_all | solution.py:438
  122.1 11.1 %place_and_blend.1 = bf16[8192,256]{1,0:T(8,128)(2,1)} custom-call(s32[1]{0:T(128)} %bitcast.me_ref, s32[8192]{0:T(1024)S(1)} %bitcast.73, bf16[3072,256]{1,0:T(8,128)(2,1)} %bitcast.43.row_ref, bf16[8192,256]{1,0:T(8,128)(2,1)} %get-tuple-element.16.w_ref, f32[16384,128]{1,0:T(8,128)} %copy-done), custom_call_target="tpu_custom_call" | custom-call | bytes 25165824 | tf_op jit(solution)/shard_map/place_and_blend/pallas_call | solution.py:400
  133.2 0.0 collective-permute-done.17
  133.3 0.0 collective-permute-done.16
  133.3 0.0 collective-permute-done.15
  133.3 0.7 fusion.1
  (45 shorter events, 0.6 us)
Async XLA Ops:
  0.6 9.1 %collective-permute-start = (bf16[64,256]{1,0:T(8,128)(2,1)}, bf16[64,256]{1,0:T(8,128)(2,1)S(1)}, u32[]{:S(2)}, u32[]{:S(2)}) collective-permute-start(bf16[64,256]{1,0:T(8,128)(2,1)} %param.5), channel_id=1, source_target_pairs={{0,2},{1,3},{2,0},{3,1},{4,6},{5,7},{6,4},{7,5},{8,10},{9,11},{10,... | collective-permute-start | bytes 98312 | tf_op jit(solution)/shard_map/ppermute | solution.py:435
  3.7 6.0 %collective-permute-start.1 = (bf16[64,256]{1,0:T(8,128)(2,1)}, bf16[64,256]{1,0:T(8,128)(2,1)S(1)}, u32[]{:S(2)}, u32[]{:S(2)}) collective-permute-start(bf16[64,256]{1,0:T(8,128)(2,1)} %param.5), channel_id=1, source_target_pairs={{0,4},{1,5},{2,6},{3,7},{4,0},{5,1},{6,2},{7,3},{8,12},{9,13},{10,... | collective-permute-start | bytes 98312 | tf_op jit(solution)/shard_map/ppermute | solution.py:435
  6.3 5.9 %collective-permute-start.2 = (bf16[64,256]{1,0:T(8,128)(2,1)}, bf16[64,256]{1,0:T(8,128)(2,1)S(1)}, u32[]{:S(2)}, u32[]{:S(2)}) collective-permute-start(bf16[64,256]{1,0:T(8,128)(2,1)} %param.5), channel_id=1, source_target_pairs={{0,6},{1,7},{2,4},{3,5},{4,2},{5,3},{6,0},{7,1},{8,14},{9,15},{10,... | collective-permute-start | bytes 98312 | tf_op jit(solution)/shard_map/ppermute | solution.py:435
  12.2 0.7 copy-start.10
  12.9 4.0 %copy-start.5 = (s32[512]{0:T(512)S(1)}, s32[512]{0:T(512)}, u32[]{:S(2)}) copy-start(s32[512]{0:T(512)} %param.6) | copy-start | bytes 6148
  12.9 4.1 %copy-start.12 = (s32[8192]{0:T(1024)S(1)}, s32[8192]{0:T(1024)}, u32[]{:S(2)}) copy-start(s32[8192]{0:T(1024)} %param.9) | copy-start | bytes 98308
  12.9 3.6 %copy-start.11 = (bf16[256,256]{1,0:T(8,128)(2,1)S(1)}, bf16[256,256]{1,0:T(8,128)(2,1)}, u32[]{:S(2)}) copy-start(bf16[256,256]{1,0:T(8,128)(2,1)} %copy-done.10) | copy-start | bytes 393220
  12.9 65.2 %all-to-all-start = ((bf16[32,160,256]{2,1,0:T(8,128)(2,1)}), bf16[32,160,256]{2,1,0:T(8,128)(2,1)S(1)}, u32[]{:S(2)}, u32[]{:S(2)}) async-start(bf16[32,160,256]{2,1,0:T(8,128)(2,1)} %release.2), calls=%async_computation | async-start | bytes 5242880 | tf_op jit(solution)/shard_map/all_to_all | solution.py:438
  16.5 1.4 %collective-permute-start.3 = (bf16[256,256]{1,0:T(8,128)(2,1)S(1)}, bf16[256,256]{1,0:T(8,128)(2,1)S(1)}, u32[]{:S(2)}, u32[]{:S(2)}) collective-permute-start(bf16[256,256]{1,0:T(8,128)(2,1)S(1)} %copy-done.11), channel_id=1, source_target_pairs={{0,1},{1,0},{2,3},{3,2},{4,5},{5,4},{6,7},{7,6},{8,9},{9,8},{10,11... | collective-permute-start | bytes 393224 | tf_op jit(solution)/shard_map/ppermute | solution.py:435
  18.0 0.7 copy-start.3
  18.7 0.9 copy-start.4
  33.2 0.8 copy-start.1
  34.0 0.7 copy-start.7
  34.7 4.9 %collective-permute-start.6 = (f32[24,128]{1,0:T(8,128)S(1)}, f32[24,128]{1,0:T(8,128)S(1)}, u32[]{:S(2)}, u32[]{:S(2)}) collective-permute-start(f32[24,128]{1,0:T(8,128)S(1)} %get-tuple-element.50), channel_id=1, source_target_pairs={{0,24},{8,16},{16,8},{24,0},{1,25},{9,17},{17,9},{25,1},{2,26},{10... | collective-permute-start | bytes 36872 | tf_op jit(solution)/shard_map/ppermute | solution.py:435
  37.5 3.8 %collective-permute-start.5 = (f32[24,128]{1,0:T(8,128)S(1)}, f32[24,128]{1,0:T(8,128)S(1)}, u32[]{:S(2)}, u32[]{:S(2)}) collective-permute-start(f32[24,128]{1,0:T(8,128)S(1)} %get-tuple-element.49), channel_id=1, source_target_pairs={{0,16},{8,24},{16,0},{24,8},{1,17},{9,25},{17,1},{25,9},{2,18},{10... | collective-permute-start | bytes 36872 | tf_op jit(solution)/shard_map/ppermute | solution.py:435
  38.0 3.8 %collective-permute-start.4 = (f32[24,128]{1,0:T(8,128)S(1)}, f32[24,128]{1,0:T(8,128)S(1)}, u32[]{:S(2)}, u32[]{:S(2)}) collective-permute-start(f32[24,128]{1,0:T(8,128)S(1)} %get-tuple-element.48), channel_id=1, source_target_pairs={{0,8},{8,0},{16,24},{24,16},{1,9},{9,1},{17,25},{25,17},{2,10},{10... | collective-permute-start | bytes 36872 | tf_op jit(solution)/shard_map/ppermute | solution.py:435
  42.0 2.4 %collective-permute-start.7 = (f32[40,128]{1,0:T(8,128)S(1)}, f32[40,128]{1,0:T(8,128)S(1)}, u32[]{:S(2)}, u32[]{:S(2)}) collective-permute-start(f32[40,128]{1,0:T(8,128)S(1)} %get-tuple-element.46), channel_id=1, source_target_pairs={{0,1},{1,0},{2,3},{3,2},{4,5},{5,4},{6,7},{7,6},{8,9},{9,8},{10,11... | collective-permute-start | bytes 61448 | tf_op jit(solution)/shard_map/ppermute | solution.py:435
  44.7 19.3 %collective-permute-start.10 = (f32[24,128]{1,0:T(8,128)S(1)}, f32[24,128]{1,0:T(8,128)S(1)}, u32[]{:S(2)}, u32[]{:S(2)}) collective-permute-start(f32[24,128]{1,0:T(8,128)S(1)} %get-tuple-element.44), channel_id=1, source_target_pairs={{0,6},{1,7},{2,4},{3,5},{4,2},{5,3},{6,0},{7,1},{8,14},{9,15},{10,... | collective-permute-start | bytes 36872 | tf_op jit(solution)/shard_map/ppermute | solution.py:435
  48.0 29.5 %collective-permute-start.9 = (f32[24,128]{1,0:T(8,128)S(1)}, f32[24,128]{1,0:T(8,128)S(1)}, u32[]{:S(2)}, u32[]{:S(2)}) collective-permute-start(f32[24,128]{1,0:T(8,128)S(1)} %get-tuple-element.43), channel_id=1, source_target_pairs={{0,4},{1,5},{2,6},{3,7},{4,0},{5,1},{6,2},{7,3},{8,12},{9,13},{10,... | collective-permute-start | bytes 36872 | tf_op jit(solution)/shard_map/ppermute | solution.py:435
  48.0 29.5 %collective-permute-start.8 = (f32[24,128]{1,0:T(8,128)S(1)}, f32[24,128]{1,0:T(8,128)S(1)}, u32[]{:S(2)}, u32[]{:S(2)}) collective-permute-start(f32[24,128]{1,0:T(8,128)S(1)} %get-tuple-element.42), channel_id=1, source_target_pairs={{0,2},{1,3},{2,0},{3,1},{4,6},{5,7},{6,4},{7,5},{8,10},{9,11},{10,... | collective-permute-start | bytes 36872 | tf_op jit(solution)/shard_map/ppermute | solution.py:435
  78.1 4.7 %copy-start.2 = (f32[512]{0:T(512)S(1)}, f32[512]{0:T(512)}, u32[]{:S(2)}) copy-start(f32[512]{0:T(512)} %get-tuple-element.39.refs_1_) | copy-start | bytes 6148
  78.1 44.0 %all-to-all-start.1 = ((bf16[32,96,256]{2,1,0:T(8,128)(2,1)}), bf16[32,96,256]{2,1,0:T(8,128)(2,1)}, u32[]{:S(2)}, u32[]{:S(2)}) async-start(bf16[32,96,256]{2,1,0:T(8,128)(2,1)} %release.3), calls=%async_computation.1 | async-start | bytes 3145728 | tf_op jit(solution)/shard_map/all_to_all | solution.py:438
  84.1 0.8 copy-start.9
  84.9 1.6 %collective-permute-start.11 = (f32[4,64,256]{2,1,0:T(8,128)S(1)}, f32[4,64,256]{2,1,0:T(8,128)S(1)}, u32[]{:S(2)}, u32[]{:S(2)}) collective-permute-start(f32[4,64,256]{2,1,0:T(8,128)S(1)} %dynamic-slice_bitcast_fusion), channel_id=1, source_target_pairs={{0,1},{1,0},{2,3},{3,2},{4,5},{5,4},{6,7},{7,6},{8,9},{9,8},{10,11... | collective-permute-start | bytes 786440 | tf_op jit(solution)/shard_map/ppermute | solution.py:435
  87.5 26.8 %collective-permute-start.12 = (f32[4,64,256]{2,1,0:T(8,128)S(1)}, f32[4,64,256]{2,1,0:T(8,128)S(1)}, u32[]{:S(2)}, u32[]{:S(2)}) collective-permute-start(f32[4,64,256]{2,1,0:T(8,128)S(1)} %bitcast_add_fusion.refs_0_), channel_id=1, source_target_pairs={{0,8},{8,0},{16,24},{24,16},{1,9},{9,1},{17,25},{25,17},{2,10},{10... | collective-permute-start | bytes 786440 | tf_op jit(solution)/shard_map/ppermute | solution.py:435
  89.2 25.0 %collective-permute-start.13 = (f32[4,64,256]{2,1,0:T(8,128)S(1)}, f32[4,64,256]{2,1,0:T(8,128)S(1)}, u32[]{:S(2)}, u32[]{:S(2)}) collective-permute-start(f32[4,64,256]{2,1,0:T(8,128)S(1)} %bitcast_add_fusion.refs_0_), channel_id=1, source_target_pairs={{0,16},{8,24},{16,0},{24,8},{1,17},{9,25},{17,1},{25,9},{2,18},{10... | collective-permute-start | bytes 786440 | tf_op jit(solution)/shard_map/ppermute | solution.py:435
  90.7 23.6 %collective-permute-start.14 = (f32[4,64,256]{2,1,0:T(8,128)S(1)}, f32[4,64,256]{2,1,0:T(8,128)S(1)}, u32[]{:S(2)}, u32[]{:S(2)}) collective-permute-start(f32[4,64,256]{2,1,0:T(8,128)S(1)} %bitcast_add_fusion.refs_0_), channel_id=1, source_target_pairs={{0,24},{8,16},{16,8},{24,0},{1,25},{9,17},{17,9},{25,1},{2,26},{10... | collective-permute-start | bytes 786440 | tf_op jit(solution)/shard_map/ppermute | solution.py:435
  91.0 0.9 copy-start.8
  102.2 12.0 %copy-start.6 = (f32[64]{0:T(128)}, f32[64]{0:T(128)S(1)}, u32[]{:S(2)}) copy-start(f32[64]{0:T(128)S(1)} %dynamic_slice.67.refs_5_) | copy-start | bytes 772
  111.0 3.3 %copy-start = (f32[16384,128]{1,0:T(8,128)}, f32[16384,128]{1,0:T(8,128)S(1)}, u32[]{:S(2)}) copy-start(f32[16384,128]{1,0:T(8,128)S(1)} %get-tuple-element.17.in_ref) | copy-start | bytes 25165828
  114.4 18.8 %collective-permute-start.17 = (bf16[64,256]{1,0:T(8,128)(2,1)S(1)}, bf16[64,256]{1,0:T(8,128)(2,1)S(1)}, u32[]{:S(2)}, u32[]{:S(2)}) collective-permute-start(bf16[64,256]{1,0:T(8,128)(2,1)S(1)} %get-tuple-element.19), channel_id=1, source_target_pairs={{0,6},{1,7},{2,4},{3,5},{4,2},{5,3},{6,0},{7,1},{8,14},{9,15},{10,... | collective-permute-start | bytes 98312 | tf_op jit(solution)/shard_map/ppermute | solution.py:435
  118.0 15.2 %collective-permute-start.16 = (bf16[64,256]{1,0:T(8,128)(2,1)S(1)}, bf16[64,256]{1,0:T(8,128)(2,1)S(1)}, u32[]{:S(2)}, u32[]{:S(2)}) collective-permute-start(bf16[64,256]{1,0:T(8,128)(2,1)S(1)} %get-tuple-element.20), channel_id=1, source_target_pairs={{0,4},{1,5},{2,6},{3,7},{4,0},{5,1},{6,2},{7,3},{8,12},{9,13},{10,... | collective-permute-start | bytes 98312 | tf_op jit(solution)/shard_map/ppermute | solution.py:435
  118.0 15.2 %collective-permute-start.15 = (bf16[64,256]{1,0:T(8,128)(2,1)S(1)}, bf16[64,256]{1,0:T(8,128)(2,1)S(1)}, u32[]{:S(2)}, u32[]{:S(2)}) collective-permute-start(bf16[64,256]{1,0:T(8,128)(2,1)S(1)} %get-tuple-element.18), channel_id=1, source_target_pairs={{0,2},{1,3},{2,0},{3,1},{4,6},{5,7},{6,4},{7,5},{8,10},{9,11},{10,... | collective-permute-start | bytes 98312 | tf_op jit(solution)/shard_map/ppermute | solution.py:435

commit v17 on v16

--- a/solution.py
+++ b/solution.py
@@ -143,7 +143,7 @@
     )(base, rep, labels.reshape(batch, 1), weights, mixed)
 
 
-def weight_kernel(base_ref, emb_ref, lab_ref, st_ref, tot_ref, w_ref, g_ref, xhat_ref, y_ref, v_ref):
+def weight_kernel(base_ref, emb_ref, lab_ref, st_ref, tot_ref, w_ref, _, g_ref, xhat_ref, y_ref, v_ref):
     step = pl.program_id(0)
     tile = w_ref.shape[0]
     batch = emb_ref.shape[0]
@@ -171,7 +171,7 @@
         g_ref[at, :] = off_axis(raw, wwide) * w_inv
 
 
-def weight_gradient(base, emb, labels, stats, totals, weights):
+def weight_gradient(base, emb, labels, stats, totals, weights, after):
     batch, width = emb.shape
     classes = weights.shape[0]
     tile = math.gcd(classes, 2048)
@@ -186,6 +186,7 @@
             pl.BlockSpec((8, batch), whole),
             pl.BlockSpec((1, batch), whole),
             pl.BlockSpec((tile, width), lambda i: (i, 0)),
+            pl.BlockSpec(memory_space=pl.ANY),
         ],
         out_specs=pl.BlockSpec((tile, width), lambda i: (i, 0)),
         out_shape=pltpu.HBM((classes, width), jnp.float32),
@@ -201,7 +202,7 @@
             flops=12 * batch * classes * width, bytes_accessed=classes * width * 6, transcendentals=0
         ),
         name="weight_gradient",
-    )(base, emb, labels.reshape(1, batch), stats, totals.reshape(1, batch), weights)
+    )(base, emb, labels.reshape(1, batch), stats, totals.reshape(1, batch), weights, after)
 
 
 def fetch_kernel(rows_ref, *refs, first):
@@ -316,19 +317,18 @@
 
 
 def place_kernel(
-    me_ref, slot_ref, row_ref, _, held_ref, token_ref, stage_ref, *, peers, run, first
+    me_ref, slot_ref, row_ref, held_ref, token_ref, stage_ref, *, peers, run, first
 ):
     token_ref[...] = jnp.zeros_like(token_ref)
     place_runs(me_ref, slot_ref, row_ref, held_ref, stage_ref, [], peers, run, first)
 
 
-def place_rows(me, slots, rows, after, peers, run, first):
+def place_rows(me, slots, rows, peers, run, first):
     smem = pl.BlockSpec(memory_space=pltpu.SMEM)
     vmem = pl.BlockSpec(memory_space=pltpu.VMEM)
-    anywhere = pl.BlockSpec(memory_space=pl.ANY)
     return pl.pallas_call(
         functools.partial(place_kernel, peers=peers, run=run, first=first),
-        in_specs=[smem, smem, vmem, anywhere],
+        in_specs=[smem, smem, vmem],
         out_specs=[vmem, vmem],
         out_shape=[
             jax.ShapeDtypeStruct((2 * peers * run, 128), jnp.float32),
@@ -340,7 +340,7 @@
             flops=0, bytes_accessed=32 * rows.shape[0] * rows.shape[1], transcendentals=0
         ),
         name="place_rows",
-    )(me, slots, rows, after)
+    )(me, slots, rows)
 
 
 def split_copies(source_ref, target_ref, sem):
@@ -354,14 +354,13 @@
 
 
 def blend_kernel(
-    me_ref, slot_ref, row_ref, w_ref, in_ref, o_ref, held_ref, stage_ref, what_ref, new_ref,
-    held_sem, what_sem, new_sem, *, peers, run, first,
+    me_ref, slot_ref, row_ref, w_ref, _, o_ref, held_ref, stage_ref, what_ref, new_ref,
+    what_sem, new_sem, *, peers, run, first,
 ):
-    copies = split_copies(in_ref, held_ref, held_sem)
     weights = split_copies(w_ref, what_ref, what_sem)
-    for copy in copies + weights:
+    for copy in weights:
         copy.start()
-    place_runs(me_ref, slot_ref, row_ref, held_ref, stage_ref, copies, peers, run, first)
+    place_runs(me_ref, slot_ref, row_ref, held_ref, stage_ref, [], peers, run, first)
     for copy in weights:
         copy.wait()
     classes = o_ref.shape[0]
@@ -397,26 +396,29 @@
     smem = pl.BlockSpec(memory_space=pltpu.SMEM)
     vmem = pl.BlockSpec(memory_space=pltpu.VMEM)
     anywhere = pl.BlockSpec(memory_space=pl.ANY)
-    return pl.pallas_call(
+    refreshed, _ = pl.pallas_call(
         functools.partial(blend_kernel, peers=peers, run=run, first=first),
-        in_specs=[smem, smem, vmem, anywhere, anywhere],
-        out_specs=anywhere,
-        out_shape=pltpu.HBM((classes, width), jnp.bfloat16),
+        in_specs=[smem, smem, vmem, anywhere, vmem],
+        out_specs=[anywhere, vmem],
+        out_shape=[
+            pltpu.HBM((classes, width), jnp.bfloat16),
+            jax.ShapeDtypeStruct(held.shape, held.dtype),
+        ],
+        input_output_aliases={4: 1},
         scratch_shapes=[
-            pltpu.VMEM(held.shape, jnp.float32),
             pltpu.VMEM((2 * rows.shape[0], 128), jnp.float32),
             pltpu.VMEM((classes, width), jnp.bfloat16),
             pltpu.VMEM((classes, width), jnp.bfloat16),
-            pltpu.SemaphoreType.DMA((4,)),
             pltpu.SemaphoreType.DMA((2,)),
             pltpu.SemaphoreType.DMA((8,)),
         ],
-        compiler_params=pltpu.CompilerParams(vmem_limit_bytes=32 * MIB),
+        compiler_params=pltpu.CompilerParams(vmem_limit_bytes=20 * MIB),
         cost_estimate=pl.CostEstimate(
             flops=0, bytes_accessed=12 * classes * width, transcendentals=0
         ),
         name="place_and_blend",
     )(me, slots, rows, weights, held)
+    return refreshed
 
 
 def shards(embeddings, labels, class_weights, centroids, centroid_class):
@@ -450,44 +452,44 @@
     index = lax.dynamic_index_in_dim
 
     def share_out(sums, wanted, axis, flips):
-        got = []
+        raw, got = [], []
         for flip, asked in zip(flips, wanted):
             sent = jnp.concatenate([sums, asked.reshape(-1)]).reshape(-1, 128)
-            got.append(swap(sent, axis, flip).reshape(-1))
+            raw.append(swap(sent, axis, flip))
+            got.append(raw[-1].reshape(-1))
         got = jnp.stack(got)
-        return jnp.sum(got[:, : 2 * batch], axis=0), got[:, 2 * batch :]
+        return jnp.sum(got[:, : 2 * batch], axis=0), got[:, 2 * batch :], raw
 
     wanted = centroid_class.reshape(half, 2, groups, run).astype(jnp.float32)
     wanted = [index(wanted, grp ^ j, 2, False) for j in range(groups)]
-    sums, wanted = share_out(stats[:2].reshape(-1), wanted, "grp", range(groups))
+    sums, wanted, _ = share_out(stats[:2].reshape(-1), wanted, "grp", range(groups))
     wanted = wanted.reshape(groups, half, 2, run)
     wanted = [index(wanted, core ^ c, 2, False) for c in range(2)]
-    sums, wanted = share_out(sums, wanted, "rep", range(2))
+    sums, wanted, _ = share_out(sums, wanted, "rep", range(2))
     sent_b = in_hbm(fetch(runs, cut, run - cut, [stats]))
     sums = join([sums.reshape(-1, 128)], [sent_b]).reshape(-1)
     wanted = wanted.reshape(2, groups, half, run)
     wanted = [index(wanted, deep ^ z, 2, False) for z in range(half)]
-    sums, slots = share_out(sums, wanted, "rep", range(0, reps, 2))
+    sums, slots, raw = share_out(sums, wanted, "rep", range(0, reps, 2))
     slots = slots.reshape(-1).astype(jnp.int32) * 2
     total, target = sums[:batch], sums[batch:]
     losses = jnp.log(total) - target
     loss = lax.dynamic_slice_in_dim(losses, rep * rows_local, rows_local, 0)
 
-    rows_b = relay(released(sent_b, [total]))
-    weight_grad = weight_gradient(base, emb, labels, stats, total, weights)
-    done = in_hbm(weight_grad)
-    held, token = place_rows(me, slots, rows_a, done, peers, run, 0)
+    rows_b = relay(released(sent_b, raw[1:]))
+    held, token = place_rows(me, slots, rows_a, peers, run, 0)
+    weight_grad = weight_gradient(base, emb, labels, stats, total, weights, token)
 
     grad = (a / total[:, None] - b).reshape(half, 2, rows_local, width)
     grad = sum(swap(index(grad, core ^ c, 1, False), "rep", c) for c in range(2))
-    grad = join([swap(grad, "grp", j) for j in range(groups)], [token, loss])
+    grad = join([swap(grad, "grp", j) for j in range(groups)], [in_hbm(weight_grad), loss])
     sent = grad.astype(jnp.bfloat16)
     parts = [swap(index(sent, deep ^ z, 0, False), "rep", 2 * z) for z in range(1, half)]
     embedding_gradient = index(grad, deep, 0, False)
     for part in parts:
         embedding_gradient = embedding_gradient + part.astype(jnp.float32)
 
-    refreshed = place_and_blend(me, slots, rows_b, in_hbm(held), in_hbm(what), peers, run, cut)
+    refreshed = place_and_blend(me, slots, rows_b, held, in_hbm(what), peers, run, cut)
     return (loss, embedding_gradient, weight_grad, refreshed)
 
 

time: 135 us -> 137 us (1.015)
  local copies, waits for them, and re-layouts: 10.2 us -> 11.7 us
    unnamed x32 -> x44, local copies, waits for them, and re-layouts: 9.68 us -> 11.2 us
  transfers between devices with their start and end apart: 20 -> 20, of which waited for: 9 -> 10; matrix products, arithmetic and copies ran while one was open for 3% -> 3% of each run, Pallas kernels for 36% -> 35%
where the time goes in v17:
time: 137 us
  Pallas kernels  48.4 us (35%)
  waiting for transfers between devices  40 us (29%)
  starting transfers between devices  31.6 us (23%)
  local copies, waits for them, and re-layouts  11.7 us (9%)
  other arithmetic  3.76 us (3%)
    ppermute x18, waiting for transfers between devices, swap(): lax.ppermute(value, axis, [(i, i ^ k) for i in range(size)])  36.5 us
    ppermute x18, starting transfers between devices, swap(): lax.ppermute(value, axis, [(i, i ^ k) for i in range(size)])  23.4 us
    pallas_call x1, Pallas kernels, forward(): pl.pallas_call(functools.partial(forward_kernel, classes=classes, reps=re...  13.6 us
    unnamed x44, local copies, waits for them, and re-layouts  11.2 us
    pallas_call x1, Pallas kernels, weight_gradient(): pl.pallas_call(weight_kernel, grid=(classes // tile,), in_specs=[pl.Block...  10.9 us
    pallas_call x1, Pallas kernels, place_and_blend(): pl.pallas_call(functools.partial(blend_kernel, peers=peers, run=run, firs...  10.2 us
    pallas_call x1, Pallas kernels, place_rows(): pl.pallas_call(functools.partial(place_kernel, peers=peers, run=run, firs...  8.73 us
    all_to_all x2, starting transfers between devices, relay(): return lax.all_to_all(sent, ALL, 0, 0, tiled=True).reshape(-1, width)  8.23 us
  transfers between devices with their start and end apart: 20, of which 10 were waited for; matrix products, arithmetic and copies ran while one was open for 3% of the time, Pallas kernels for 35%

profile of v17, /device:TPU:0, one launch (start us, length us, event | category | flops | bytes accessed | tf_op | source)
XLA Modules:
  0.0 136.5 jit_solution(12562884842130295096)
XLA Ops:
  0.6 4.1 %collective-permute-start.1 = (bf16[64,256]{1,0:T(8,128)(2,1)}, bf16[64,256]{1,0:T(8,128)(2,1)S(1)}, u32[]{:S(2)}, u32[]{:S(2)}) collective-permute-start(bf16[64,256]{1,0:T(8,128)(2,1)} %param.5), channel_id=1, source_target_pairs={{0,4},{1,5},{2,6},{3,7},{4,0},{5,1},{6,2},{7,3},{8,12},{9,13},{10,... | collective-permute-start | bytes 98312 | tf_op jit(solution)/shard_map/ppermute | solution.py:437
  4.7 1.6 %collective-permute-start = (bf16[64,256]{1,0:T(8,128)(2,1)}, bf16[64,256]{1,0:T(8,128)(2,1)S(1)}, u32[]{:S(2)}, u32[]{:S(2)}) collective-permute-start(bf16[64,256]{1,0:T(8,128)(2,1)} %param.5), channel_id=1, source_target_pairs={{0,2},{1,3},{2,0},{3,1},{4,6},{5,7},{6,4},{7,5},{8,10},{9,11},{10,... | collective-permute-start | bytes 98312 | tf_op jit(solution)/shard_map/ppermute | solution.py:437
  6.3 0.0 collective-permute-start.2
  6.3 0.8 constant_dynamic-update-slice_fusion.3
  7.1 2.6 %fetch.3.refs_0_ = bf16[32,160,256]{2,1,0:T(8,128)(2,1)} custom-call(bf16[32,256,256]{2,1,0:T(8,128)(2,1)} %bitcast.79), custom_call_target="tpu_custom_call" | custom-call | bytes 10485760 | tf_op jit(solution)/shard_map/fetch/pallas_call | solution.py:234
  9.7 0.0 collective-permute-done
  9.8 0.0 collective-permute-done.1
  9.8 2.4 %collective-permute-done.2 = bf16[64,256]{1,0:T(8,128)(2,1)S(1)} collective-permute-done((bf16[64,256]{1,0:T(8,128)(2,1)}, bf16[64,256]{1,0:T(8,128)(2,1)S(1)}, u32[]{:S(2)}, u32[]{:S(2)}) %collective-permute-start.2) | collective-permute-done | bytes 32800 | tf_op jit(solution)/shard_map/ppermute | solution.py:437
  12.2 0.7 copy-done.10
  12.9 3.6 %all-to-all-start = ((bf16[32,160,256]{2,1,0:T(8,128)(2,1)}), bf16[32,160,256]{2,1,0:T(8,128)(2,1)S(1)}, u32[]{:S(2)}, u32[]{:S(2)}) async-start(bf16[32,160,256]{2,1,0:T(8,128)(2,1)} %release.2), calls=%async_computation | async-start | bytes 5242880 | tf_op jit(solution)/shard_map/all_to_all | solution.py:440
  16.5 0.3 collective-permute-start.3
  16.9 0.1 copy.17.lab_ref
  17.1 0.8 collective-permute-done.3
  18.0 0.0 copy-start.3
  18.0 0.7 copy-done.3
  18.7 0.9 copy-done.4
  19.6 13.6 %forward_sums.1 = (bf16[512,256]{1,0:T(8,128)(2,1)S(1)}, f32[512,256]{1,0:T(8,128)S(1)}, f32[512,256]{1,0:T(8,128)S(1)}, f32[8,512]{1,0:T(8,128)S(1)}, bf16[8192,256]{1,0:T(8,128)(2,1)}) custom-call(s32[1]{0:T(128)S(6)} %mul.18.base_ref, s32[1]{0:T(128)} %bitcast.1.rep_ref, s32[512,1]{1,0:T(8,128)S(1)} %copy.17.lab_ref, bf16[8192,256]{1,0:T(8,128)(2,1)} %w_ref.3, ...), custom_call_target="tpu_custom_call" | custom-call | flops 12884901888 | bytes 4194304 | tf_op jit(solution)/shard_map/forward_sums/pallas_call | solution.py:111
  33.2 0.8 copy-done.2
  34.0 0.7 copy-done.7
  34.7 1.8 %collective-permute-start.4 = (f32[24,128]{1,0:T(8,128)S(1)}, f32[24,128]{1,0:T(8,128)S(1)}, u32[]{:S(2)}, u32[]{:S(2)}) collective-permute-start(f32[24,128]{1,0:T(8,128)S(1)} %get-tuple-element.50), channel_id=1, source_target_pairs={{0,8},{8,0},{16,24},{24,16},{1,9},{9,1},{17,25},{25,17},{2,10},{10... | collective-permute-start | bytes 36872 | tf_op jit(solution)/shard_map/ppermute | solution.py:437
  36.6 1.5 %collective-permute-start.5 = (f32[24,128]{1,0:T(8,128)S(1)}, f32[24,128]{1,0:T(8,128)S(1)}, u32[]{:S(2)}, u32[]{:S(2)}) collective-permute-start(f32[24,128]{1,0:T(8,128)S(1)} %get-tuple-element.51), channel_id=1, source_target_pairs={{0,16},{8,24},{16,0},{24,8},{1,17},{9,25},{17,1},{25,9},{2,18},{10... | collective-permute-start | bytes 36872 | tf_op jit(solution)/shard_map/ppermute | solution.py:437
  38.0 0.3 collective-permute-start.6
  38.3 0.2 collective-permute-done.4
  38.5 2.0 %collective-permute-done.5 = f32[24,128]{1,0:T(8,128)S(1)} collective-permute-done((f32[24,128]{1,0:T(8,128)S(1)}, f32[24,128]{1,0:T(8,128)S(1)}, u32[]{:S(2)}, u32[]{:S(2)}) %collective-permute-start.5) | collective-permute-done | bytes 12320 | tf_op jit(solution)/shard_map/ppermute | solution.py:437
  40.5 3.7 %collective-permute-done.6 = f32[24,128]{1,0:T(8,128)S(1)} collective-permute-done((f32[24,128]{1,0:T(8,128)S(1)}, f32[24,128]{1,0:T(8,128)S(1)}, u32[]{:S(2)}, u32[]{:S(2)}) %collective-permute-start.6) | collective-permute-done | bytes 12320 | tf_op jit(solution)/shard_map/ppermute | solution.py:437
  44.3 0.1 collective-permute-start.7
  44.5 2.3 %fetch.2.refs_1_.refs_0_ = bf16[32,96,256]{2,1,0:T(8,128)(2,1)} custom-call(bf16[32,256,256]{2,1,0:T(8,128)(2,1)} %bitcast.80, f32[8,512]{1,0:T(8,128)S(1)} %get-tuple-element.12.refs_0_.st_ref), custom_call_target="tpu_custom_call" | custom-call | bytes 6291456 | tf_op jit(solution)/shard_map/fetch/pallas_call | solution.py:234
  46.8 0.0 collective-permute-done.7
  47.0 0.1 collective-permute-start.8
  47.1 2.4 %collective-permute-start.9 = (f32[24,128]{1,0:T(8,128)S(1)}, f32[24,128]{1,0:T(8,128)S(1)}, u32[]{:S(2)}, u32[]{:S(2)}) collective-permute-start(f32[24,128]{1,0:T(8,128)S(1)} %get-tuple-element.45), channel_id=1, source_target_pairs={{0,4},{1,5},{2,6},{3,7},{4,0},{5,1},{6,2},{7,3},{8,12},{9,13},{10,... | collective-permute-start | bytes 36872 | tf_op jit(solution)/shard_map/ppermute | solution.py:437
  49.6 1.9 %collective-permute-start.10 = (f32[24,128]{1,0:T(8,128)S(1)}, f32[24,128]{1,0:T(8,128)S(1)}, u32[]{:S(2)}, u32[]{:S(2)}) collective-permute-start(f32[24,128]{1,0:T(8,128)S(1)} %get-tuple-element.46), channel_id=1, source_target_pairs={{0,6},{1,7},{2,4},{3,5},{4,2},{5,3},{6,0},{7,1},{8,14},{9,15},{10,... | collective-permute-start | bytes 36872 | tf_op jit(solution)/shard_map/ppermute | solution.py:437
  51.5 8.7 %collective-permute-done.8.refs_1_ = f32[24,128]{1,0:T(8,128)S(1)} collective-permute-done((f32[24,128]{1,0:T(8,128)S(1)}, f32[24,128]{1,0:T(8,128)S(1)}, u32[]{:S(2)}, u32[]{:S(2)}) %collective-permute-start.8) | collective-permute-done | bytes 12320 | tf_op jit(solution)/shard_map/ppermute | solution.py:437
  60.1 17.3 %collective-permute-done.9.refs_2_ = f32[24,128]{1,0:T(8,128)S(1)} collective-permute-done((f32[24,128]{1,0:T(8,128)S(1)}, f32[24,128]{1,0:T(8,128)S(1)}, u32[]{:S(2)}, u32[]{:S(2)}) %collective-permute-start.9) | collective-permute-done | bytes 12320 | tf_op jit(solution)/shard_map/ppermute | solution.py:437
  77.4 0.0 collective-permute-done.10.refs_3_
  77.4 0.6 copy-done.14
  78.0 0.6 copy-done.16
  78.6 0.0 all-to-all-done
  78.6 4.6 %all-to-all-start.1 = ((bf16[32,96,256]{2,1,0:T(8,128)(2,1)}), bf16[32,96,256]{2,1,0:T(8,128)(2,1)}, u32[]{:S(2)}, u32[]{:S(2)}) async-start(bf16[32,96,256]{2,1,0:T(8,128)(2,1)} %release.3), calls=%async_computation.1 | async-start | bytes 3145728 | tf_op jit(solution)/shard_map/all_to_all | solution.py:440
  83.2 0.7 maximum_reduce_fusion
  84.0 1.2 divide_subtract_fusion
  85.2 0.0 copy-start.9
  85.2 0.8 copy-done.9
  86.0 0.3 collective-permute-start.11
  86.3 0.1 dynamic_slice.67.refs_5_
  86.4 1.2 collective-permute-done.11
  87.6 1.0 bitcast_add_fusion.refs_0_
  88.6 2.7 %collective-permute-start.14 = (f32[4,64,256]{2,1,0:T(8,128)S(1)}, f32[4,64,256]{2,1,0:T(8,128)S(1)}, u32[]{:S(2)}, u32[]{:S(2)}) collective-permute-start(f32[4,64,256]{2,1,0:T(8,128)S(1)} %bitcast_add_fusion.refs_0_), channel_id=1, source_target_pairs={{0,24},{8,16},{16,8},{24,0},{1,25},{9,17},{17,9},{25,1},{2,26},{10... | collective-permute-start | bytes 786440 | tf_op jit(solution)/shard_map/ppermute | solution.py:437
  91.2 0.6 collective-permute-start.13
  91.8 0.3 collective-permute-start.12
  92.1 8.7 %place_rows.1 = (f32[16384,128]{1,0:T(8,128)S(1)}, f32[8,128]{1,0:T(8,128)S(1)}) custom-call(s32[1]{0:T(128)} %bitcast.me_ref, s32[8192]{0:T(1024)S(1)} %bitcast.72, bf16[5120,256]{1,0:T(8,128)(2,1)S(1)} %bitcast.71), custom_call_target="tpu_custom_call" | custom-call | bytes 41943040 | tf_op jit(solution)/shard_map/place_rows/pallas_call | solution.py:329
  100.9 1.1 copy-done.8
  102.0 10.9 %weight_gradient.1.refs_4_ = f32[8192,256]{1,0:T(8,128)} custom-call(s32[1]{0:T(128)S(6)} %mul.18.base_ref, bf16[512,256]{1,0:T(8,128)(2,1)S(1)} %copy-done.8, s32[1,512]{1,0:T(1,128)S(1)} %bitcast.78, f32[8,512]{1,0:T(8,128)S(1)} %get-tuple-element.12.refs_0_.st_ref, f32[1,512]{1,0:T(1,128)S(1)} %bitcast.76, bf16[8192,256]{1,0:T(8,128)(2,1)} %w_ref.3, ...), custom_call_target="tpu_custom_call" | custom-call | flops 12884901888 | bytes 12582912 | tf_op jit(solution)/shard_map/weight_gradient/pallas_call | solution.py:179
  112.9 0.0 collective-permute-done.14.refs_3_
  113.0 0.2 collective-permute-done.13.refs_2_
  113.1 0.0 collective-permute-done.12.refs_1_
  113.2 1.6 %collective-permute-start.15 = (bf16[64,256]{1,0:T(8,128)(2,1)S(1)}, bf16[64,256]{1,0:T(8,128)(2,1)S(1)}, u32[]{:S(2)}, u32[]{:S(2)}) collective-permute-start(bf16[64,256]{1,0:T(8,128)(2,1)S(1)} %get-tuple-element.20), channel_id=1, source_target_pairs={{0,2},{1,3},{2,0},{3,1},{4,6},{5,7},{6,4},{7,5},{8,10},{9,11},{10,... | collective-permute-start | bytes 98312 | tf_op jit(solution)/shard_map/ppermute | solution.py:437
  114.9 3.9 %collective-permute-start.17 = (bf16[64,256]{1,0:T(8,128)(2,1)S(1)}, bf16[64,256]{1,0:T(8,128)(2,1)S(1)}, u32[]{:S(2)}, u32[]{:S(2)}) collective-permute-start(bf16[64,256]{1,0:T(8,128)(2,1)S(1)} %get-tuple-element.21), channel_id=1, source_target_pairs={{0,6},{1,7},{2,4},{3,5},{4,2},{5,3},{6,0},{7,1},{8,14},{9,15},{10,... | collective-permute-start | bytes 98312 | tf_op jit(solution)/shard_map/ppermute | solution.py:437
  118.7 0.0 collective-permute-start.16
  118.8 3.5 %all-to-all-done.1 = bf16[32,96,256]{2,1,0:T(8,128)(2,1)} async-done(((bf16[32,96,256]{2,1,0:T(8,128)(2,1)}), bf16[32,96,256]{2,1,0:T(8,128)(2,1)}, u32[]{:S(2)}, u32[]{:S(2)}) %all-to-all-start.1) | async-done | bytes 1572896 | tf_op jit(solution)/shard_map/all_to_all | solution.py:440
  122.3 3.4 %copy-done.1 = f32[16384,128]{1,0:T(8,128)S(1)} copy-done((f32[16384,128]{1,0:T(8,128)S(1)}, f32[16384,128]{1,0:T(8,128)}, u32[]{:S(2)}) %copy-start.1) | copy-done | bytes 8388632
  125.6 10.2 %place_and_blend.1 = (bf16[8192,256]{1,0:T(8,128)(2,1)}, f32[16384,128]{1,0:T(8,128)S(1)}) custom-call(s32[1]{0:T(128)} %bitcast.me_ref, s32[8192]{0:T(1024)S(1)} %bitcast.73, bf16[3072,256]{1,0:T(8,128)(2,1)} %bitcast.43.row_ref, bf16[8192,256]{1,0:T(8,128)(2,1)} %get-tuple-element.17.w_ref, f32[16384,128]{1,0:T(8,128)S(1)} %copy-done.1), custom_call_target="tpu_custom_call", output_to_operand_aliasing={{1}: (4, {})} | custom-call | bytes 25165824 | tf_op jit(solution)/shard_map/place_and_blend/pallas_call | solution.py:399
  135.8 0.0 collective-permute-done.15
  135.8 0.0 collective-permute-done.17
  135.9 0.7 fusion.1
  (57 shorter events, 0.6 us)
Async XLA Ops:
  0.6 9.1 %collective-permute-start.1 = (bf16[64,256]{1,0:T(8,128)(2,1)}, bf16[64,256]{1,0:T(8,128)(2,1)S(1)}, u32[]{:S(2)}, u32[]{:S(2)}) collective-permute-start(bf16[64,256]{1,0:T(8,128)(2,1)} %param.5), channel_id=1, source_target_pairs={{0,4},{1,5},{2,6},{3,7},{4,0},{5,1},{6,2},{7,3},{8,12},{9,13},{10,... | collective-permute-start | bytes 98312 | tf_op jit(solution)/shard_map/ppermute | solution.py:437
  4.7 5.0 %collective-permute-start = (bf16[64,256]{1,0:T(8,128)(2,1)}, bf16[64,256]{1,0:T(8,128)(2,1)S(1)}, u32[]{:S(2)}, u32[]{:S(2)}) collective-permute-start(bf16[64,256]{1,0:T(8,128)(2,1)} %param.5), channel_id=1, source_target_pairs={{0,2},{1,3},{2,0},{3,1},{4,6},{5,7},{6,4},{7,5},{8,10},{9,11},{10,... | collective-permute-start | bytes 98312 | tf_op jit(solution)/shard_map/ppermute | solution.py:437
  6.3 5.9 %collective-permute-start.2 = (bf16[64,256]{1,0:T(8,128)(2,1)}, bf16[64,256]{1,0:T(8,128)(2,1)S(1)}, u32[]{:S(2)}, u32[]{:S(2)}) collective-permute-start(bf16[64,256]{1,0:T(8,128)(2,1)} %param.5), channel_id=1, source_target_pairs={{0,6},{1,7},{2,4},{3,5},{4,2},{5,3},{6,0},{7,1},{8,14},{9,15},{10,... | collective-permute-start | bytes 98312 | tf_op jit(solution)/shard_map/ppermute | solution.py:437
  12.2 0.7 copy-start.10
  12.9 4.0 %copy-start.18 = (s32[8192]{0:T(1024)S(1)}, s32[8192]{0:T(1024)}, u32[]{:S(2)}) copy-start(s32[8192]{0:T(1024)} %param.9) | copy-start | bytes 98308
  12.9 4.0 %copy-start.5 = (s32[512]{0:T(512)S(1)}, s32[512]{0:T(512)}, u32[]{:S(2)}) copy-start(s32[512]{0:T(512)} %param.6) | copy-start | bytes 6148
  12.9 3.6 %copy-start.11 = (bf16[256,256]{1,0:T(8,128)(2,1)S(1)}, bf16[256,256]{1,0:T(8,128)(2,1)}, u32[]{:S(2)}) copy-start(bf16[256,256]{1,0:T(8,128)(2,1)} %copy-done.10) | copy-start | bytes 393220
  12.9 65.7 %all-to-all-start = ((bf16[32,160,256]{2,1,0:T(8,128)(2,1)}), bf16[32,160,256]{2,1,0:T(8,128)(2,1)S(1)}, u32[]{:S(2)}, u32[]{:S(2)}) async-start(bf16[32,160,256]{2,1,0:T(8,128)(2,1)} %release.2), calls=%async_computation | async-start | bytes 5242880 | tf_op jit(solution)/shard_map/all_to_all | solution.py:440
  16.5 1.4 %collective-permute-start.3 = (bf16[256,256]{1,0:T(8,128)(2,1)S(1)}, bf16[256,256]{1,0:T(8,128)(2,1)S(1)}, u32[]{:S(2)}, u32[]{:S(2)}) collective-permute-start(bf16[256,256]{1,0:T(8,128)(2,1)S(1)} %copy-done.11), channel_id=1, source_target_pairs={{0,1},{1,0},{2,3},{3,2},{4,5},{5,4},{6,7},{7,6},{8,9},{9,8},{10,11... | collective-permute-start | bytes 393224 | tf_op jit(solution)/shard_map/ppermute | solution.py:437
  18.0 0.7 copy-start.3
  18.7 0.9 copy-start.4
  33.2 0.8 copy-start.2
  34.0 0.7 copy-start.7
  34.7 3.8 %collective-permute-start.4 = (f32[24,128]{1,0:T(8,128)S(1)}, f32[24,128]{1,0:T(8,128)S(1)}, u32[]{:S(2)}, u32[]{:S(2)}) collective-permute-start(f32[24,128]{1,0:T(8,128)S(1)} %get-tuple-element.50), channel_id=1, source_target_pairs={{0,8},{8,0},{16,24},{24,16},{1,9},{9,1},{17,25},{25,17},{2,10},{10... | collective-permute-start | bytes 36872 | tf_op jit(solution)/shard_map/ppermute | solution.py:437
  36.6 3.9 %collective-permute-start.5 = (f32[24,128]{1,0:T(8,128)S(1)}, f32[24,128]{1,0:T(8,128)S(1)}, u32[]{:S(2)}, u32[]{:S(2)}) collective-permute-start(f32[24,128]{1,0:T(8,128)S(1)} %get-tuple-element.51), channel_id=1, source_target_pairs={{0,16},{8,24},{16,0},{24,8},{1,17},{9,25},{17,1},{25,9},{2,18},{10... | collective-permute-start | bytes 36872 | tf_op jit(solution)/shard_map/ppermute | solution.py:437
  38.0 6.1 %collective-permute-start.6 = (f32[24,128]{1,0:T(8,128)S(1)}, f32[24,128]{1,0:T(8,128)S(1)}, u32[]{:S(2)}, u32[]{:S(2)}) collective-permute-start(f32[24,128]{1,0:T(8,128)S(1)} %get-tuple-element.52), channel_id=1, source_target_pairs={{0,24},{8,16},{16,8},{24,0},{1,25},{9,17},{17,9},{25,1},{2,26},{10... | collective-permute-start | bytes 36872 | tf_op jit(solution)/shard_map/ppermute | solution.py:437
  44.3 2.5 %collective-permute-start.7 = (f32[40,128]{1,0:T(8,128)S(1)}, f32[40,128]{1,0:T(8,128)S(1)}, u32[]{:S(2)}, u32[]{:S(2)}) collective-permute-start(f32[40,128]{1,0:T(8,128)S(1)} %get-tuple-element.48), channel_id=1, source_target_pairs={{0,1},{1,0},{2,3},{3,2},{4,5},{5,4},{6,7},{7,6},{8,9},{9,8},{10,11... | collective-permute-start | bytes 61448 | tf_op jit(solution)/shard_map/ppermute | solution.py:437
  47.0 13.1 %collective-permute-start.8 = (f32[24,128]{1,0:T(8,128)S(1)}, f32[24,128]{1,0:T(8,128)S(1)}, u32[]{:S(2)}, u32[]{:S(2)}) collective-permute-start(f32[24,128]{1,0:T(8,128)S(1)} %get-tuple-element.44), channel_id=1, source_target_pairs={{0,2},{1,3},{2,0},{3,1},{4,6},{5,7},{6,4},{7,5},{8,10},{9,11},{10,... | collective-permute-start | bytes 36872 | tf_op jit(solution)/shard_map/ppermute | solution.py:437
  47.1 30.3 %collective-permute-start.9 = (f32[24,128]{1,0:T(8,128)S(1)}, f32[24,128]{1,0:T(8,128)S(1)}, u32[]{:S(2)}, u32[]{:S(2)}) collective-permute-start(f32[24,128]{1,0:T(8,128)S(1)} %get-tuple-element.45), channel_id=1, source_target_pairs={{0,4},{1,5},{2,6},{3,7},{4,0},{5,1},{6,2},{7,3},{8,12},{9,13},{10,... | collective-permute-start | bytes 36872 | tf_op jit(solution)/shard_map/ppermute | solution.py:437
  49.6 27.8 %collective-permute-start.10 = (f32[24,128]{1,0:T(8,128)S(1)}, f32[24,128]{1,0:T(8,128)S(1)}, u32[]{:S(2)}, u32[]{:S(2)}) collective-permute-start(f32[24,128]{1,0:T(8,128)S(1)} %get-tuple-element.46), channel_id=1, source_target_pairs={{0,6},{1,7},{2,4},{3,5},{4,2},{5,3},{6,0},{7,1},{8,14},{9,15},{10,... | collective-permute-start | bytes 36872 | tf_op jit(solution)/shard_map/ppermute | solution.py:437
  60.1 17.3 %copy-start.12 = (f32[24,128]{1,0:T(8,128)}, f32[24,128]{1,0:T(8,128)S(1)}, u32[]{:S(2)}) copy-start(f32[24,128]{1,0:T(8,128)S(1)} %collective-permute-done.8.refs_1_) | copy-start | bytes 36868
  77.4 0.6 copy-start.14
  78.0 0.6 copy-start.16
  78.6 7.6 %copy-start.13 = (f32[24,128]{1,0:T(8,128)S(1)}, f32[24,128]{1,0:T(8,128)}, u32[]{:S(2)}) copy-start(f32[24,128]{1,0:T(8,128)} %copy-done.12) | copy-start | bytes 36868
  78.6 7.6 %copy-start.15 = (f32[24,128]{1,0:T(8,128)S(1)}, f32[24,128]{1,0:T(8,128)}, u32[]{:S(2)}) copy-start(f32[24,128]{1,0:T(8,128)} %copy-done.14) | copy-start | bytes 36868
  78.6 7.6 %copy-start.17 = (f32[24,128]{1,0:T(8,128)S(1)}, f32[24,128]{1,0:T(8,128)}, u32[]{:S(2)}) copy-start(f32[24,128]{1,0:T(8,128)} %copy-done.16) | copy-start | bytes 36868
  78.6 43.6 %all-to-all-start.1 = ((bf16[32,96,256]{2,1,0:T(8,128)(2,1)}), bf16[32,96,256]{2,1,0:T(8,128)(2,1)}, u32[]{:S(2)}, u32[]{:S(2)}) async-start(bf16[32,96,256]{2,1,0:T(8,128)(2,1)} %release.3), calls=%async_computation.1 | async-start | bytes 3145728 | tf_op jit(solution)/shard_map/all_to_all | solution.py:440
  85.2 0.8 copy-start.9
  86.0 1.6 %collective-permute-start.11 = (f32[4,64,256]{2,1,0:T(8,128)S(1)}, f32[4,64,256]{2,1,0:T(8,128)S(1)}, u32[]{:S(2)}, u32[]{:S(2)}) collective-permute-start(f32[4,64,256]{2,1,0:T(8,128)S(1)} %dynamic-slice_bitcast_fusion), channel_id=1, source_target_pairs={{0,1},{1,0},{2,3},{3,2},{4,5},{5,4},{6,7},{7,6},{8,9},{9,8},{10,11... | collective-permute-start | bytes 786440 | tf_op jit(solution)/shard_map/ppermute | solution.py:437
  86.4 26.8 %copy-start.6 = (f32[64]{0:T(128)}, f32[64]{0:T(128)S(1)}, u32[]{:S(2)}) copy-start(f32[64]{0:T(128)S(1)} %dynamic_slice.67.refs_5_) | copy-start | bytes 772
  88.6 24.4 %collective-permute-start.14 = (f32[4,64,256]{2,1,0:T(8,128)S(1)}, f32[4,64,256]{2,1,0:T(8,128)S(1)}, u32[]{:S(2)}, u32[]{:S(2)}) collective-permute-start(f32[4,64,256]{2,1,0:T(8,128)S(1)} %bitcast_add_fusion.refs_0_), channel_id=1, source_target_pairs={{0,24},{8,16},{16,8},{24,0},{1,25},{9,17},{17,9},{25,1},{2,26},{10... | collective-permute-start | bytes 786440 | tf_op jit(solution)/shard_map/ppermute | solution.py:437
  91.2 21.9 %collective-permute-start.13 = (f32[4,64,256]{2,1,0:T(8,128)S(1)}, f32[4,64,256]{2,1,0:T(8,128)S(1)}, u32[]{:S(2)}, u32[]{:S(2)}) collective-permute-start(f32[4,64,256]{2,1,0:T(8,128)S(1)} %bitcast_add_fusion.refs_0_), channel_id=1, source_target_pairs={{0,16},{8,24},{16,0},{24,8},{1,17},{9,25},{17,1},{25,9},{2,18},{10... | collective-permute-start | bytes 786440 | tf_op jit(solution)/shard_map/ppermute | solution.py:437
  91.8 21.3 %collective-permute-start.12 = (f32[4,64,256]{2,1,0:T(8,128)S(1)}, f32[4,64,256]{2,1,0:T(8,128)S(1)}, u32[]{:S(2)}, u32[]{:S(2)}) collective-permute-start(f32[4,64,256]{2,1,0:T(8,128)S(1)} %bitcast_add_fusion.refs_0_), channel_id=1, source_target_pairs={{0,8},{8,0},{16,24},{24,16},{1,9},{9,1},{17,25},{25,17},{2,10},{10... | collective-permute-start | bytes 786440 | tf_op jit(solution)/shard_map/ppermute | solution.py:437
  100.9 12.1 %copy-start = (f32[16384,128]{1,0:T(8,128)}, f32[16384,128]{1,0:T(8,128)S(1)}, u32[]{:S(2)}) copy-start(f32[16384,128]{1,0:T(8,128)S(1)} %get-tuple-element.18._) | copy-start | bytes 25165828
  100.9 1.1 copy-start.8
  113.2 22.6 %collective-permute-start.15 = (bf16[64,256]{1,0:T(8,128)(2,1)S(1)}, bf16[64,256]{1,0:T(8,128)(2,1)S(1)}, u32[]{:S(2)}, u32[]{:S(2)}) collective-permute-start(bf16[64,256]{1,0:T(8,128)(2,1)S(1)} %get-tuple-element.20), channel_id=1, source_target_pairs={{0,2},{1,3},{2,0},{3,1},{4,6},{5,7},{6,4},{7,5},{8,10},{9,11},{10,... | collective-permute-start | bytes 98312 | tf_op jit(solution)/shard_map/ppermute | solution.py:437
  114.9 21.0 %collective-permute-start.17 = (bf16[64,256]{1,0:T(8,128)(2,1)S(1)}, bf16[64,256]{1,0:T(8,128)(2,1)S(1)}, u32[]{:S(2)}, u32[]{:S(2)}) collective-permute-start(bf16[64,256]{1,0:T(8,128)(2,1)S(1)} %get-tuple-element.21), channel_id=1, source_target_pairs={{0,6},{1,7},{2,4},{3,5},{4,2},{5,3},{6,0},{7,1},{8,14},{9,15},{10,... | collective-permute-start | bytes 98312 | tf_op jit(solution)/shard_map/ppermute | solution.py:437
  118.7 17.1 %collective-permute-start.16 = (bf16[64,256]{1,0:T(8,128)(2,1)S(1)}, bf16[64,256]{1,0:T(8,128)(2,1)S(1)}, u32[]{:S(2)}, u32[]{:S(2)}) collective-permute-start(bf16[64,256]{1,0:T(8,128)(2,1)S(1)} %get-tuple-element.22), channel_id=1, source_target_pairs={{0,4},{1,5},{2,6},{3,7},{4,0},{5,1},{6,2},{7,3},{8,12},{9,13},{10,... | collective-permute-start | bytes 98312 | tf_op jit(solution)/shard_map/ppermute | solution.py:437
  122.3 3.4 %copy-start.1 = (f32[16384,128]{1,0:T(8,128)S(1)}, f32[16384,128]{1,0:T(8,128)}, u32[]{:S(2)}) copy-start(f32[16384,128]{1,0:T(8,128)} %copy-done) | copy-start | bytes 25165828

commit v18 on v16

--- a/solution.py
+++ b/solution.py
@@ -143,7 +143,7 @@
     )(base, rep, labels.reshape(batch, 1), weights, mixed)
 
 
-def weight_kernel(base_ref, emb_ref, lab_ref, st_ref, tot_ref, w_ref, g_ref, xhat_ref, y_ref, v_ref):
+def weight_kernel(base_ref, emb_ref, lab_ref, st_ref, tot_ref, w_ref, _, g_ref, xhat_ref, y_ref, v_ref):
     step = pl.program_id(0)
     tile = w_ref.shape[0]
     batch = emb_ref.shape[0]
@@ -171,7 +171,7 @@
         g_ref[at, :] = off_axis(raw, wwide) * w_inv
 
 
-def weight_gradient(base, emb, labels, stats, totals, weights):
+def weight_gradient(base, emb, labels, stats, totals, weights, after):
     batch, width = emb.shape
     classes = weights.shape[0]
     tile = math.gcd(classes, 2048)
@@ -186,6 +186,7 @@
             pl.BlockSpec((8, batch), whole),
             pl.BlockSpec((1, batch), whole),
             pl.BlockSpec((tile, width), lambda i: (i, 0)),
+            pl.BlockSpec(memory_space=pl.ANY),
         ],
         out_specs=pl.BlockSpec((tile, width), lambda i: (i, 0)),
         out_shape=pltpu.HBM((classes, width), jnp.float32),
@@ -201,7 +202,7 @@
             flops=12 * batch * classes * width, bytes_accessed=classes * width * 6, transcendentals=0
         ),
         name="weight_gradient",
-    )(base, emb, labels.reshape(1, batch), stats, totals.reshape(1, batch), weights)
+    )(base, emb, labels.reshape(1, batch), stats, totals.reshape(1, batch), weights, after)
 
 
 def fetch_kernel(rows_ref, *refs, first):
@@ -250,7 +251,7 @@
 def join_kernel(*refs, count):
     total = refs[0][...]
     for ref in refs[1:count]:
-        total = total + ref[...]
+        total = total + ref[...].astype(total.dtype)
     refs[-1][...] = total
 
 
@@ -316,19 +317,18 @@
 
 
 def place_kernel(
-    me_ref, slot_ref, row_ref, _, held_ref, token_ref, stage_ref, *, peers, run, first
+    me_ref, slot_ref, row_ref, held_ref, token_ref, stage_ref, *, peers, run, first
 ):
     token_ref[...] = jnp.zeros_like(token_ref)
     place_runs(me_ref, slot_ref, row_ref, held_ref, stage_ref, [], peers, run, first)
 
 
-def place_rows(me, slots, rows, after, peers, run, first):
+def place_rows(me, slots, rows, peers, run, first):
     smem = pl.BlockSpec(memory_space=pltpu.SMEM)
     vmem = pl.BlockSpec(memory_space=pltpu.VMEM)
-    anywhere = pl.BlockSpec(memory_space=pl.ANY)
     return pl.pallas_call(
         functools.partial(place_kernel, peers=peers, run=run, first=first),
-        in_specs=[smem, smem, vmem, anywhere],
+        in_specs=[smem, smem, vmem],
         out_specs=[vmem, vmem],
         out_shape=[
             jax.ShapeDtypeStruct((2 * peers * run, 128), jnp.float32),
@@ -340,7 +340,7 @@
             flops=0, bytes_accessed=32 * rows.shape[0] * rows.shape[1], transcendentals=0
         ),
         name="place_rows",
-    )(me, slots, rows, after)
+    )(me, slots, rows)
 
 
 def split_copies(source_ref, target_ref, sem):
@@ -474,13 +474,14 @@
     loss = lax.dynamic_slice_in_dim(losses, rep * rows_local, rows_local, 0)
 
     rows_b = relay(released(sent_b, [total]))
-    weight_grad = weight_gradient(base, emb, labels, stats, total, weights)
-    done = in_hbm(weight_grad)
-    held, token = place_rows(me, slots, rows_a, done, peers, run, 0)
+    held, token = place_rows(me, slots, rows_a, peers, run, 0)
+    weight_grad = weight_gradient(base, emb, labels, stats, total, weights, token)
 
     grad = (a / total[:, None] - b).reshape(half, 2, rows_local, width)
     grad = sum(swap(index(grad, core ^ c, 1, False), "rep", c) for c in range(2))
-    grad = join([swap(grad, "grp", j) for j in range(groups)], [token, loss])
+    sent = grad.astype(jnp.bfloat16)
+    parts = [swap(sent, "grp", j) for j in range(1, groups)]
+    grad = join([grad, *parts], [in_hbm(weight_grad), loss])
     sent = grad.astype(jnp.bfloat16)
     parts = [swap(index(sent, deep ^ z, 0, False), "rep", 2 * z) for z in range(1, half)]
     embedding_gradient = index(grad, deep, 0, False)

time: 135 us -> 135 us (level)
  local copies, waits for them, and re-layouts: 10.2 us -> 7.06 us
  waiting for transfers between devices: 39.9 us -> 42.4 us
    unnamed x32, local copies, waits for them, and re-layouts: 9.68 us -> 6.58 us
    all_to_all x2, waiting for transfers between devices: 3.24 us -> 6.05 us  [relay(): return lax.all_to_all(sent, ALL, 0, 0, tiled=True).reshape(-1, width)]
  transfers between devices with their start and end apart: 20 -> 20, of which waited for: 9 -> 9; matrix products, arithmetic and copies ran while one was open for 3% -> 3% of each run, Pallas kernels for 36% -> 37%
where the time goes in v18:
time: 135 us; the launch traced here: 134 us
  Pallas kernels  49.4 us (37%)
  waiting for transfers between devices  42.4 us (31%)
  starting transfers between devices  30.3 us (22%)
  local copies, waits for them, and re-layouts  7.06 us (5%)
  other arithmetic  3.64 us (3%)
    ppermute x18, waiting for transfers between devices, swap(): lax.ppermute(value, axis, [(i, i ^ k) for i in range(size)])  36.4 us
    ppermute x18, starting transfers between devices, swap(): lax.ppermute(value, axis, [(i, i ^ k) for i in range(size)])  22.1 us
    pallas_call x1, Pallas kernels, forward(): pl.pallas_call(functools.partial(forward_kernel, classes=classes, reps=re...  13.6 us
    pallas_call x1, Pallas kernels, place_and_blend(): pl.pallas_call(functools.partial(blend_kernel, peers=peers, run=run, firs...  11.1 us
    pallas_call x1, Pallas kernels, weight_gradient(): pl.pallas_call(weight_kernel, grid=(classes // tile,), in_specs=[pl.Block...  10.9 us
    pallas_call x1, Pallas kernels, place_rows(): pl.pallas_call(functools.partial(place_kernel, peers=peers, run=run, firs...  8.73 us
    all_to_all x2, starting transfers between devices, relay(): return lax.all_to_all(sent, ALL, 0, 0, tiled=True).reshape(-1, width)  8.22 us
    unnamed x32, local copies, waits for them, and re-layouts  6.58 us
  transfers between devices with their start and end apart: 20, of which 9 were waited for; matrix products, arithmetic and copies ran while one was open for 3% of the time, Pallas kernels for 37%

profile of v18, /device:TPU:0, one launch (start us, length us, event | category | flops | bytes accessed | tf_op | source)
XLA Modules:
  0.0 133.8 jit_solution(15469190261277193941)
XLA Ops:
  0.6 4.1 %collective-permute-start.1 = (bf16[64,256]{1,0:T(8,128)(2,1)}, bf16[64,256]{1,0:T(8,128)(2,1)S(1)}, u32[]{:S(2)}, u32[]{:S(2)}) collective-permute-start(bf16[64,256]{1,0:T(8,128)(2,1)} %param.5), channel_id=1, source_target_pairs={{0,4},{1,5},{2,6},{3,7},{4,0},{5,1},{6,2},{7,3},{8,12},{9,13},{10,... | collective-permute-start | bytes 98312 | tf_op jit(solution)/shard_map/ppermute | solution.py:435
  4.7 1.6 %collective-permute-start = (bf16[64,256]{1,0:T(8,128)(2,1)}, bf16[64,256]{1,0:T(8,128)(2,1)S(1)}, u32[]{:S(2)}, u32[]{:S(2)}) collective-permute-start(bf16[64,256]{1,0:T(8,128)(2,1)} %param.5), channel_id=1, source_target_pairs={{0,2},{1,3},{2,0},{3,1},{4,6},{5,7},{6,4},{7,5},{8,10},{9,11},{10,... | collective-permute-start | bytes 98312 | tf_op jit(solution)/shard_map/ppermute | solution.py:435
  6.3 0.0 collective-permute-start.2
  6.3 0.8 constant_dynamic-update-slice_fusion.3
  7.1 2.6 %fetch.3.refs_0_ = bf16[32,160,256]{2,1,0:T(8,128)(2,1)} custom-call(bf16[32,256,256]{2,1,0:T(8,128)(2,1)} %bitcast.80), custom_call_target="tpu_custom_call" | custom-call | bytes 10485760 | tf_op jit(solution)/shard_map/fetch/pallas_call | solution.py:234
  9.7 0.0 collective-permute-done
  9.8 0.0 collective-permute-done.1
  9.8 2.4 %collective-permute-done.2 = bf16[64,256]{1,0:T(8,128)(2,1)S(1)} collective-permute-done((bf16[64,256]{1,0:T(8,128)(2,1)}, bf16[64,256]{1,0:T(8,128)(2,1)S(1)}, u32[]{:S(2)}, u32[]{:S(2)}) %collective-permute-start.2) | collective-permute-done | bytes 32800 | tf_op jit(solution)/shard_map/ppermute | solution.py:435
  12.2 0.7 copy-done.10
  12.9 3.6 %all-to-all-start = ((bf16[32,160,256]{2,1,0:T(8,128)(2,1)}), bf16[32,160,256]{2,1,0:T(8,128)(2,1)S(1)}, u32[]{:S(2)}, u32[]{:S(2)}) async-start(bf16[32,160,256]{2,1,0:T(8,128)(2,1)} %release.2), calls=%async_computation | async-start | bytes 5242880 | tf_op jit(solution)/shard_map/all_to_all | solution.py:438
  16.5 0.0 copy-done.11
  16.5 0.3 collective-permute-start.3
  16.9 0.1 copy.16.lab_ref
  17.1 0.8 collective-permute-done.3
  18.0 0.0 copy-start.3
  18.0 0.7 copy-done.3
  18.7 0.9 copy-done.4
  19.6 13.6 %forward_sums.1 = (bf16[512,256]{1,0:T(8,128)(2,1)S(1)}, f32[512,256]{1,0:T(8,128)S(1)}, f32[512,256]{1,0:T(8,128)S(1)}, f32[8,512]{1,0:T(8,128)S(1)}, bf16[8192,256]{1,0:T(8,128)(2,1)}) custom-call(s32[1]{0:T(128)S(6)} %mul.18.base_ref, s32[1]{0:T(128)} %bitcast.1.rep_ref, s32[512,1]{1,0:T(8,128)S(1)} %copy.16.lab_ref, bf16[8192,256]{1,0:T(8,128)(2,1)} %w_ref.3, ...), custom_call_target="tpu_custom_call" | custom-call | flops 12884901888 | bytes 4194304 | tf_op jit(solution)/shard_map/forward_sums/pallas_call | solution.py:111
  33.2 0.8 copy-done.1
  34.0 0.7 copy-done.7
  34.7 1.8 %collective-permute-start.4 = (f32[24,128]{1,0:T(8,128)S(1)}, f32[24,128]{1,0:T(8,128)S(1)}, u32[]{:S(2)}, u32[]{:S(2)}) collective-permute-start(f32[24,128]{1,0:T(8,128)S(1)} %get-tuple-element.50), channel_id=1, source_target_pairs={{0,8},{8,0},{16,24},{24,16},{1,9},{9,1},{17,25},{25,17},{2,10},{10... | collective-permute-start | bytes 36872 | tf_op jit(solution)/shard_map/ppermute | solution.py:435
  36.5 1.5 %collective-permute-start.5 = (f32[24,128]{1,0:T(8,128)S(1)}, f32[24,128]{1,0:T(8,128)S(1)}, u32[]{:S(2)}, u32[]{:S(2)}) collective-permute-start(f32[24,128]{1,0:T(8,128)S(1)} %get-tuple-element.51), channel_id=1, source_target_pairs={{0,16},{8,24},{16,0},{24,8},{1,17},{9,25},{17,1},{25,9},{2,18},{10... | collective-permute-start | bytes 36872 | tf_op jit(solution)/shard_map/ppermute | solution.py:435
  38.0 0.3 collective-permute-start.6
  38.3 0.2 collective-permute-done.4
  38.5 2.0 %collective-permute-done.5 = f32[24,128]{1,0:T(8,128)S(1)} collective-permute-done((f32[24,128]{1,0:T(8,128)S(1)}, f32[24,128]{1,0:T(8,128)S(1)}, u32[]{:S(2)}, u32[]{:S(2)}) %collective-permute-start.5) | collective-permute-done | bytes 12320 | tf_op jit(solution)/shard_map/ppermute | solution.py:435
  40.4 3.7 %collective-permute-done.6 = f32[24,128]{1,0:T(8,128)S(1)} collective-permute-done((f32[24,128]{1,0:T(8,128)S(1)}, f32[24,128]{1,0:T(8,128)S(1)}, u32[]{:S(2)}, u32[]{:S(2)}) %collective-permute-start.6) | collective-permute-done | bytes 12320 | tf_op jit(solution)/shard_map/ppermute | solution.py:435
  44.3 0.1 collective-permute-start.7
  44.4 2.3 %fetch.2.refs_1_.refs_0_ = bf16[32,96,256]{2,1,0:T(8,128)(2,1)} custom-call(bf16[32,256,256]{2,1,0:T(8,128)(2,1)} %bitcast.81, f32[8,512]{1,0:T(8,128)S(1)} %get-tuple-element.11.refs_0_.st_ref), custom_call_target="tpu_custom_call" | custom-call | bytes 6291456 | tf_op jit(solution)/shard_map/fetch/pallas_call | solution.py:234
  46.8 0.0 collective-permute-done.7
  47.0 0.1 collective-permute-start.8
  47.1 2.4 %collective-permute-start.9 = (f32[24,128]{1,0:T(8,128)S(1)}, f32[24,128]{1,0:T(8,128)S(1)}, u32[]{:S(2)}, u32[]{:S(2)}) collective-permute-start(f32[24,128]{1,0:T(8,128)S(1)} %get-tuple-element.45), channel_id=1, source_target_pairs={{0,4},{1,5},{2,6},{3,7},{4,0},{5,1},{6,2},{7,3},{8,12},{9,13},{10,... | collective-permute-start | bytes 36872 | tf_op jit(solution)/shard_map/ppermute | solution.py:435
  49.5 1.9 %collective-permute-start.10 = (f32[24,128]{1,0:T(8,128)S(1)}, f32[24,128]{1,0:T(8,128)S(1)}, u32[]{:S(2)}, u32[]{:S(2)}) collective-permute-start(f32[24,128]{1,0:T(8,128)S(1)} %get-tuple-element.46), channel_id=1, source_target_pairs={{0,6},{1,7},{2,4},{3,5},{4,2},{5,3},{6,0},{7,1},{8,14},{9,15},{10,... | collective-permute-start | bytes 36872 | tf_op jit(solution)/shard_map/ppermute | solution.py:435
  51.4 8.7 %collective-permute-done.8 = f32[24,128]{1,0:T(8,128)S(1)} collective-permute-done((f32[24,128]{1,0:T(8,128)S(1)}, f32[24,128]{1,0:T(8,128)S(1)}, u32[]{:S(2)}, u32[]{:S(2)}) %collective-permute-start.8) | collective-permute-done | bytes 12320 | tf_op jit(solution)/shard_map/ppermute | solution.py:435
  60.1 17.3 %collective-permute-done.9 = f32[24,128]{1,0:T(8,128)S(1)} collective-permute-done((f32[24,128]{1,0:T(8,128)S(1)}, f32[24,128]{1,0:T(8,128)S(1)}, u32[]{:S(2)}, u32[]{:S(2)}) %collective-permute-start.9) | collective-permute-done | bytes 12320 | tf_op jit(solution)/shard_map/ppermute | solution.py:435
  77.4 0.0 collective-permute-done.10
  77.4 0.6 fusion.13
  78.0 0.0 all-to-all-done
  78.0 4.6 %all-to-all-start.1 = ((bf16[32,96,256]{2,1,0:T(8,128)(2,1)}), bf16[32,96,256]{2,1,0:T(8,128)(2,1)}, u32[]{:S(2)}, u32[]{:S(2)}) async-start(bf16[32,96,256]{2,1,0:T(8,128)(2,1)} %release.3), calls=%async_computation.1 | async-start | bytes 3145728 | tf_op jit(solution)/shard_map/all_to_all | solution.py:438
  82.6 1.2 divide_subtract_fusion
  83.8 0.0 copy-start.9
  83.8 0.8 copy-done.9
  84.7 0.3 collective-permute-start.11
  85.0 0.1 dynamic_slice.67.refs_5_
  85.0 1.2 collective-permute-done.11
  86.3 1.0 fusion.12
  87.2 2.7 %collective-permute-start.14 = (bf16[4,64,256]{2,1,0:T(8,128)(2,1)S(1)}, bf16[4,64,256]{2,1,0:T(8,128)(2,1)S(1)}, u32[]{:S(2)}, u32[]{:S(2)}) collective-permute-start(bf16[4,64,256]{2,1,0:T(8,128)(2,1)S(1)} %get-tuple-element.18), channel_id=1, source_target_pairs={{0,24},{8,16},{16,8},{24,0},{1,25},{9,17},{17,9},{25,1},{2,26},{10... | collective-permute-start | bytes 393224 | tf_op jit(solution)/shard_map/ppermute | solution.py:435
  89.9 0.6 collective-permute-start.13
  90.5 0.3 collective-permute-start.12
  90.8 8.7 %place_rows.1 = (f32[16384,128]{1,0:T(8,128)S(1)}, f32[8,128]{1,0:T(8,128)S(1)}) custom-call(s32[1]{0:T(128)} %bitcast.me_ref, s32[8192]{0:T(1024)S(1)} %bitcast.73, bf16[5120,256]{1,0:T(8,128)(2,1)S(1)} %bitcast.72), custom_call_target="tpu_custom_call" | custom-call | bytes 41943040 | tf_op jit(solution)/shard_map/place_rows/pallas_call | solution.py:329
  99.6 1.1 copy-done.8
  100.7 10.9 %weight_gradient.1.refs_4_ = f32[8192,256]{1,0:T(8,128)} custom-call(s32[1]{0:T(128)S(6)} %mul.18.base_ref, bf16[512,256]{1,0:T(8,128)(2,1)S(1)} %copy-done.8, s32[1,512]{1,0:T(1,128)S(1)} %bitcast.79, f32[8,512]{1,0:T(8,128)S(1)} %get-tuple-element.11.refs_0_.st_ref, f32[1,512]{1,0:T(1,128)S(1)} %bitcast.75, bf16[8192,256]{1,0:T(8,128)(2,1)} %w_ref.3, ...), custom_call_target="tpu_custom_call" | custom-call | flops 12884901888 | bytes 12582912 | tf_op jit(solution)/shard_map/weight_gradient/pallas_call | solution.py:179
  111.6 0.0 collective-permute-done.14.refs_3_
  111.6 0.0 collective-permute-done.13.refs_2_
  111.6 0.0 collective-permute-done.12.refs_1_
  111.7 0.1 join.3
  111.8 1.8 %collective-permute-start.15 = (bf16[64,256]{1,0:T(8,128)(2,1)S(1)}, bf16[64,256]{1,0:T(8,128)(2,1)S(1)}, u32[]{:S(2)}, u32[]{:S(2)}) collective-permute-start(bf16[64,256]{1,0:T(8,128)(2,1)S(1)} %get-tuple-element.20), channel_id=1, source_target_pairs={{0,2},{1,3},{2,0},{3,1},{4,6},{5,7},{6,4},{7,5},{8,10},{9,11},{10,... | collective-permute-start | bytes 98312 | tf_op jit(solution)/shard_map/ppermute | solution.py:435
  113.5 2.4 %collective-permute-start.17 = (bf16[64,256]{1,0:T(8,128)(2,1)S(1)}, bf16[64,256]{1,0:T(8,128)(2,1)S(1)}, u32[]{:S(2)}, u32[]{:S(2)}) collective-permute-start(bf16[64,256]{1,0:T(8,128)(2,1)S(1)} %get-tuple-element.21), channel_id=1, source_target_pairs={{0,6},{1,7},{2,4},{3,5},{4,2},{5,3},{6,0},{7,1},{8,14},{9,15},{10,... | collective-permute-start | bytes 98312 | tf_op jit(solution)/shard_map/ppermute | solution.py:435
  115.9 0.0 collective-permute-start.16
  116.0 6.0 %all-to-all-done.1 = bf16[32,96,256]{2,1,0:T(8,128)(2,1)} async-done(((bf16[32,96,256]{2,1,0:T(8,128)(2,1)}), bf16[32,96,256]{2,1,0:T(8,128)(2,1)}, u32[]{:S(2)}, u32[]{:S(2)}) %all-to-all-start.1) | async-done | bytes 1572896 | tf_op jit(solution)/shard_map/all_to_all | solution.py:438
  122.0 11.1 %place_and_blend.1 = bf16[8192,256]{1,0:T(8,128)(2,1)} custom-call(s32[1]{0:T(128)} %bitcast.me_ref, s32[8192]{0:T(1024)S(1)} %bitcast.74, bf16[3072,256]{1,0:T(8,128)(2,1)} %bitcast.43.row_ref, bf16[8192,256]{1,0:T(8,128)(2,1)} %get-tuple-element.16.w_ref, f32[16384,128]{1,0:T(8,128)} %copy-done), custom_call_target="tpu_custom_call" | custom-call | bytes 25165824 | tf_op jit(solution)/shard_map/place_and_blend/pallas_call | solution.py:400
  133.2 0.0 collective-permute-done.15
  133.2 0.0 collective-permute-done.17
  133.2 0.0 collective-permute-done.16
  133.2 0.7 fusion.1
  (45 shorter events, 0.6 us)
Async XLA Ops:
  0.6 9.1 %collective-permute-start.1 = (bf16[64,256]{1,0:T(8,128)(2,1)}, bf16[64,256]{1,0:T(8,128)(2,1)S(1)}, u32[]{:S(2)}, u32[]{:S(2)}) collective-permute-start(bf16[64,256]{1,0:T(8,128)(2,1)} %param.5), channel_id=1, source_target_pairs={{0,4},{1,5},{2,6},{3,7},{4,0},{5,1},{6,2},{7,3},{8,12},{9,13},{10,... | collective-permute-start | bytes 98312 | tf_op jit(solution)/shard_map/ppermute | solution.py:435
  4.7 5.0 %collective-permute-start = (bf16[64,256]{1,0:T(8,128)(2,1)}, bf16[64,256]{1,0:T(8,128)(2,1)S(1)}, u32[]{:S(2)}, u32[]{:S(2)}) collective-permute-start(bf16[64,256]{1,0:T(8,128)(2,1)} %param.5), channel_id=1, source_target_pairs={{0,2},{1,3},{2,0},{3,1},{4,6},{5,7},{6,4},{7,5},{8,10},{9,11},{10,... | collective-permute-start | bytes 98312 | tf_op jit(solution)/shard_map/ppermute | solution.py:435
  6.3 5.9 %collective-permute-start.2 = (bf16[64,256]{1,0:T(8,128)(2,1)}, bf16[64,256]{1,0:T(8,128)(2,1)S(1)}, u32[]{:S(2)}, u32[]{:S(2)}) collective-permute-start(bf16[64,256]{1,0:T(8,128)(2,1)} %param.5), channel_id=1, source_target_pairs={{0,6},{1,7},{2,4},{3,5},{4,2},{5,3},{6,0},{7,1},{8,14},{9,15},{10,... | collective-permute-start | bytes 98312 | tf_op jit(solution)/shard_map/ppermute | solution.py:435
  12.2 0.7 copy-start.10
  12.9 4.0 %copy-start.12 = (s32[8192]{0:T(1024)S(1)}, s32[8192]{0:T(1024)}, u32[]{:S(2)}) copy-start(s32[8192]{0:T(1024)} %param.9) | copy-start | bytes 98308
  12.9 4.0 %copy-start.5 = (s32[512]{0:T(512)S(1)}, s32[512]{0:T(512)}, u32[]{:S(2)}) copy-start(s32[512]{0:T(512)} %param.6) | copy-start | bytes 6148
  12.9 3.6 %copy-start.11 = (bf16[256,256]{1,0:T(8,128)(2,1)S(1)}, bf16[256,256]{1,0:T(8,128)(2,1)}, u32[]{:S(2)}) copy-start(bf16[256,256]{1,0:T(8,128)(2,1)} %copy-done.10) | copy-start | bytes 393220
  12.9 65.1 %all-to-all-start = ((bf16[32,160,256]{2,1,0:T(8,128)(2,1)}), bf16[32,160,256]{2,1,0:T(8,128)(2,1)S(1)}, u32[]{:S(2)}, u32[]{:S(2)}) async-start(bf16[32,160,256]{2,1,0:T(8,128)(2,1)} %release.2), calls=%async_computation | async-start | bytes 5242880 | tf_op jit(solution)/shard_map/all_to_all | solution.py:438
  16.5 1.4 %collective-permute-start.3 = (bf16[256,256]{1,0:T(8,128)(2,1)S(1)}, bf16[256,256]{1,0:T(8,128)(2,1)S(1)}, u32[]{:S(2)}, u32[]{:S(2)}) collective-permute-start(bf16[256,256]{1,0:T(8,128)(2,1)S(1)} %copy-done.11), channel_id=1, source_target_pairs={{0,1},{1,0},{2,3},{3,2},{4,5},{5,4},{6,7},{7,6},{8,9},{9,8},{10,11... | collective-permute-start | bytes 393224 | tf_op jit(solution)/shard_map/ppermute | solution.py:435
  18.0 0.7 copy-start.3
  18.7 0.9 copy-start.4
  33.2 0.8 copy-start.1
  34.0 0.7 copy-start.7
  34.7 3.8 %collective-permute-start.4 = (f32[24,128]{1,0:T(8,128)S(1)}, f32[24,128]{1,0:T(8,128)S(1)}, u32[]{:S(2)}, u32[]{:S(2)}) collective-permute-start(f32[24,128]{1,0:T(8,128)S(1)} %get-tuple-element.50), channel_id=1, source_target_pairs={{0,8},{8,0},{16,24},{24,16},{1,9},{9,1},{17,25},{25,17},{2,10},{10... | collective-permute-start | bytes 36872 | tf_op jit(solution)/shard_map/ppermute | solution.py:435
  36.5 3.9 %collective-permute-start.5 = (f32[24,128]{1,0:T(8,128)S(1)}, f32[24,128]{1,0:T(8,128)S(1)}, u32[]{:S(2)}, u32[]{:S(2)}) collective-permute-start(f32[24,128]{1,0:T(8,128)S(1)} %get-tuple-element.51), channel_id=1, source_target_pairs={{0,16},{8,24},{16,0},{24,8},{1,17},{9,25},{17,1},{25,9},{2,18},{10... | collective-permute-start | bytes 36872 | tf_op jit(solution)/shard_map/ppermute | solution.py:435
  38.0 6.2 %collective-permute-start.6 = (f32[24,128]{1,0:T(8,128)S(1)}, f32[24,128]{1,0:T(8,128)S(1)}, u32[]{:S(2)}, u32[]{:S(2)}) collective-permute-start(f32[24,128]{1,0:T(8,128)S(1)} %get-tuple-element.52), channel_id=1, source_target_pairs={{0,24},{8,16},{16,8},{24,0},{1,25},{9,17},{17,9},{25,1},{2,26},{10... | collective-permute-start | bytes 36872 | tf_op jit(solution)/shard_map/ppermute | solution.py:435
  44.3 2.4 %collective-permute-start.7 = (f32[40,128]{1,0:T(8,128)S(1)}, f32[40,128]{1,0:T(8,128)S(1)}, u32[]{:S(2)}, u32[]{:S(2)}) collective-permute-start(f32[40,128]{1,0:T(8,128)S(1)} %get-tuple-element.48), channel_id=1, source_target_pairs={{0,1},{1,0},{2,3},{3,2},{4,5},{5,4},{6,7},{7,6},{8,9},{9,8},{10,11... | collective-permute-start | bytes 61448 | tf_op jit(solution)/shard_map/ppermute | solution.py:435
  47.0 13.1 %collective-permute-start.8 = (f32[24,128]{1,0:T(8,128)S(1)}, f32[24,128]{1,0:T(8,128)S(1)}, u32[]{:S(2)}, u32[]{:S(2)}) collective-permute-start(f32[24,128]{1,0:T(8,128)S(1)} %get-tuple-element.44), channel_id=1, source_target_pairs={{0,2},{1,3},{2,0},{3,1},{4,6},{5,7},{6,4},{7,5},{8,10},{9,11},{10,... | collective-permute-start | bytes 36872 | tf_op jit(solution)/shard_map/ppermute | solution.py:435
  47.1 30.3 %collective-permute-start.9 = (f32[24,128]{1,0:T(8,128)S(1)}, f32[24,128]{1,0:T(8,128)S(1)}, u32[]{:S(2)}, u32[]{:S(2)}) collective-permute-start(f32[24,128]{1,0:T(8,128)S(1)} %get-tuple-element.45), channel_id=1, source_target_pairs={{0,4},{1,5},{2,6},{3,7},{4,0},{5,1},{6,2},{7,3},{8,12},{9,13},{10,... | collective-permute-start | bytes 36872 | tf_op jit(solution)/shard_map/ppermute | solution.py:435
  49.5 27.9 %collective-permute-start.10 = (f32[24,128]{1,0:T(8,128)S(1)}, f32[24,128]{1,0:T(8,128)S(1)}, u32[]{:S(2)}, u32[]{:S(2)}) collective-permute-start(f32[24,128]{1,0:T(8,128)S(1)} %get-tuple-element.46), channel_id=1, source_target_pairs={{0,6},{1,7},{2,4},{3,5},{4,2},{5,3},{6,0},{7,1},{8,14},{9,15},{10,... | collective-permute-start | bytes 36872 | tf_op jit(solution)/shard_map/ppermute | solution.py:435
  78.0 4.6 %copy-start.2 = (f32[512]{0:T(512)S(1)}, f32[512]{0:T(512)}, u32[]{:S(2)}) copy-start(f32[512]{0:T(512)} %get-tuple-element.41.refs_1_) | copy-start | bytes 6148
  78.0 44.0 %all-to-all-start.1 = ((bf16[32,96,256]{2,1,0:T(8,128)(2,1)}), bf16[32,96,256]{2,1,0:T(8,128)(2,1)}, u32[]{:S(2)}, u32[]{:S(2)}) async-start(bf16[32,96,256]{2,1,0:T(8,128)(2,1)} %release.3), calls=%async_computation.1 | async-start | bytes 3145728 | tf_op jit(solution)/shard_map/all_to_all | solution.py:438
  83.8 0.8 copy-start.9
  84.7 1.6 %collective-permute-start.11 = (f32[4,64,256]{2,1,0:T(8,128)S(1)}, f32[4,64,256]{2,1,0:T(8,128)S(1)}, u32[]{:S(2)}, u32[]{:S(2)}) collective-permute-start(f32[4,64,256]{2,1,0:T(8,128)S(1)} %dynamic-slice_bitcast_fusion), channel_id=1, source_target_pairs={{0,1},{1,0},{2,3},{3,2},{4,5},{5,4},{6,7},{7,6},{8,9},{9,8},{10,11... | collective-permute-start | bytes 786440 | tf_op jit(solution)/shard_map/ppermute | solution.py:435
  85.0 26.6 %copy-start.6 = (f32[64]{0:T(128)}, f32[64]{0:T(128)S(1)}, u32[]{:S(2)}) copy-start(f32[64]{0:T(128)S(1)} %dynamic_slice.67.refs_5_) | copy-start | bytes 772
  87.2 24.4 %collective-permute-start.14 = (bf16[4,64,256]{2,1,0:T(8,128)(2,1)S(1)}, bf16[4,64,256]{2,1,0:T(8,128)(2,1)S(1)}, u32[]{:S(2)}, u32[]{:S(2)}) collective-permute-start(bf16[4,64,256]{2,1,0:T(8,128)(2,1)S(1)} %get-tuple-element.18), channel_id=1, source_target_pairs={{0,24},{8,16},{16,8},{24,0},{1,25},{9,17},{17,9},{25,1},{2,26},{10... | collective-permute-start | bytes 393224 | tf_op jit(solution)/shard_map/ppermute | solution.py:435
  89.9 21.7 %collective-permute-start.13 = (bf16[4,64,256]{2,1,0:T(8,128)(2,1)S(1)}, bf16[4,64,256]{2,1,0:T(8,128)(2,1)S(1)}, u32[]{:S(2)}, u32[]{:S(2)}) collective-permute-start(bf16[4,64,256]{2,1,0:T(8,128)(2,1)S(1)} %get-tuple-element.18), channel_id=1, source_target_pairs={{0,16},{8,24},{16,0},{24,8},{1,17},{9,25},{17,1},{25,9},{2,18},{10... | collective-permute-start | bytes 393224 | tf_op jit(solution)/shard_map/ppermute | solution.py:435
  90.5 21.2 %collective-permute-start.12 = (bf16[4,64,256]{2,1,0:T(8,128)(2,1)S(1)}, bf16[4,64,256]{2,1,0:T(8,128)(2,1)S(1)}, u32[]{:S(2)}, u32[]{:S(2)}) collective-permute-start(bf16[4,64,256]{2,1,0:T(8,128)(2,1)S(1)} %get-tuple-element.18), channel_id=1, source_target_pairs={{0,8},{8,0},{16,24},{24,16},{1,9},{9,1},{17,25},{25,17},{2,10},{10... | collective-permute-start | bytes 393224 | tf_op jit(solution)/shard_map/ppermute | solution.py:435
  99.5 12.1 %copy-start = (f32[16384,128]{1,0:T(8,128)}, f32[16384,128]{1,0:T(8,128)S(1)}, u32[]{:S(2)}) copy-start(f32[16384,128]{1,0:T(8,128)S(1)} %get-tuple-element.17.in_ref) | copy-start | bytes 25165828
  99.5 1.1 copy-start.8
  111.8 21.4 %collective-permute-start.15 = (bf16[64,256]{1,0:T(8,128)(2,1)S(1)}, bf16[64,256]{1,0:T(8,128)(2,1)S(1)}, u32[]{:S(2)}, u32[]{:S(2)}) collective-permute-start(bf16[64,256]{1,0:T(8,128)(2,1)S(1)} %get-tuple-element.20), channel_id=1, source_target_pairs={{0,2},{1,3},{2,0},{3,1},{4,6},{5,7},{6,4},{7,5},{8,10},{9,11},{10,... | collective-permute-start | bytes 98312 | tf_op jit(solution)/shard_map/ppermute | solution.py:435
  113.5 19.6 %collective-permute-start.17 = (bf16[64,256]{1,0:T(8,128)(2,1)S(1)}, bf16[64,256]{1,0:T(8,128)(2,1)S(1)}, u32[]{:S(2)}, u32[]{:S(2)}) collective-permute-start(bf16[64,256]{1,0:T(8,128)(2,1)S(1)} %get-tuple-element.21), channel_id=1, source_target_pairs={{0,6},{1,7},{2,4},{3,5},{4,2},{5,3},{6,0},{7,1},{8,14},{9,15},{10,... | collective-permute-start | bytes 98312 | tf_op jit(solution)/shard_map/ppermute | solution.py:435
  115.9 17.3 %collective-permute-start.16 = (bf16[64,256]{1,0:T(8,128)(2,1)S(1)}, bf16[64,256]{1,0:T(8,128)(2,1)S(1)}, u32[]{:S(2)}, u32[]{:S(2)}) collective-permute-start(bf16[64,256]{1,0:T(8,128)(2,1)S(1)} %get-tuple-element.22), channel_id=1, source_target_pairs={{0,4},{1,5},{2,6},{3,7},{4,0},{5,1},{6,2},{7,3},{8,12},{9,13},{10,... | collective-permute-start | bytes 98312 | tf_op jit(solution)/shard_map/ppermute | solution.py:435

commit v19 on v18

--- a/solution.py
+++ b/solution.py
@@ -407,7 +407,7 @@
             pltpu.VMEM((2 * rows.shape[0], 128), jnp.float32),
             pltpu.VMEM((classes, width), jnp.bfloat16),
             pltpu.VMEM((classes, width), jnp.bfloat16),
-            pltpu.SemaphoreType.DMA((4,)),
+            pltpu.SemaphoreType.DMA((8,)),
             pltpu.SemaphoreType.DMA((2,)),
             pltpu.SemaphoreType.DMA((8,)),
         ],
@@ -439,7 +439,7 @@
 
     weights = in_hbm(class_weights)
     runs = in_hbm(centroids.reshape(peers, run, width))
-    cut = run * 5 // 8 // 16 * 16
+    cut = run * 11 // 16 // 16 * 16
     mixed = jnp.concatenate([swap(embeddings, "rep", 2 * z) for z in range(reps // 2)])
     rows_a = relay(released(in_hbm(fetch(runs, 0, cut, [])), [mixed]))
     mixed = jnp.concatenate([swap(mixed, "rep", c) for c in range(2)])

time: 135 us -> 134 us (level)
  waiting for transfers between devices: 42.4 us -> 40.2 us
    all_to_all x2, waiting for transfers between devices: 6.05 us -> 0.01 us  [relay(): return lax.all_to_all(sent, ALL, 0, 0, tiled=True).reshape(-1, width)]
    ppermute x18, waiting for transfers between devices: 36.4 us -> 40.2 us  [swap(): lax.ppermute(value, axis, [(i, i ^ k) for i in range(size)])]
    unnamed x32 -> x34, local copies, waits for them, and re-layouts: 6.58 us -> 6.41 us
  transfers between devices with their start and end apart: 20 -> 20, of which waited for: 9 -> 8; matrix products, arithmetic and copies ran while one was open for 3% -> 5% of each run, Pallas kernels for 37% -> 37%
where the time goes in v19:
time: 134 us; the launch traced here: 133 us
  Pallas kernels  49.3 us (37%)
  waiting for transfers between devices  40.2 us (30%)
  starting transfers between devices  29.9 us (22%)
  local copies, waits for them, and re-layouts  8.3 us (6%)
  other arithmetic  4.32 us (3%)
    ppermute x18, waiting for transfers between devices, swap(): lax.ppermute(value, axis, [(i, i ^ k) for i in range(size)])  40.2 us
    ppermute x18, starting transfers between devices, swap(): lax.ppermute(value, axis, [(i, i ^ k) for i in range(size)])  21.9 us
    pallas_call x1, Pallas kernels, forward(): pl.pallas_call(functools.partial(forward_kernel, classes=classes, reps=re...  13.6 us
    pallas_call x1, Pallas kernels, weight_gradient(): pl.pallas_call(weight_kernel, grid=(classes // tile,), in_specs=[pl.Block...  10.9 us
    pallas_call x1, Pallas kernels, place_and_blend(): pl.pallas_call(functools.partial(blend_kernel, peers=peers, run=run, firs...  10.6 us
    pallas_call x1, Pallas kernels, place_rows(): pl.pallas_call(functools.partial(place_kernel, peers=peers, run=run, firs...  9.22 us
    all_to_all x2, starting transfers between devices, relay(): return lax.all_to_all(sent, ALL, 0, 0, tiled=True).reshape(-1, width)  7.96 us
    unnamed x34, local copies, waits for them, and re-layouts  6.41 us
  transfers between devices with their start and end apart: 20, of which 8 were waited for; matrix products, arithmetic and copies ran while one was open for 5% of the time, Pallas kernels for 37%

profile of v19, /device:TPU:0, one launch (start us, length us, event | category | flops | bytes accessed | tf_op | source)
XLA Modules:
  0.0 133.0 jit_solution(14574414066671970541)
XLA Ops:
  0.6 4.1 %collective-permute-start.1 = (bf16[64,256]{1,0:T(8,128)(2,1)}, bf16[64,256]{1,0:T(8,128)(2,1)S(1)}, u32[]{:S(2)}, u32[]{:S(2)}) collective-permute-start(bf16[64,256]{1,0:T(8,128)(2,1)} %param.5), channel_id=1, source_target_pairs={{0,4},{1,5},{2,6},{3,7},{4,0},{5,1},{6,2},{7,3},{8,12},{9,13},{10,... | collective-permute-start | bytes 98312 | tf_op jit(solution)/shard_map/ppermute | solution.py:435
  4.7 1.6 %collective-permute-start = (bf16[64,256]{1,0:T(8,128)(2,1)}, bf16[64,256]{1,0:T(8,128)(2,1)S(1)}, u32[]{:S(2)}, u32[]{:S(2)}) collective-permute-start(bf16[64,256]{1,0:T(8,128)(2,1)} %param.5), channel_id=1, source_target_pairs={{0,2},{1,3},{2,0},{3,1},{4,6},{5,7},{6,4},{7,5},{8,10},{9,11},{10,... | collective-permute-start | bytes 98312 | tf_op jit(solution)/shard_map/ppermute | solution.py:435
  6.3 0.0 collective-permute-start.2
  6.3 0.8 constant_dynamic-update-slice_fusion.3
  7.1 2.7 %fetch.3.refs_0_ = bf16[32,176,256]{2,1,0:T(8,128)(2,1)} custom-call(bf16[32,256,256]{2,1,0:T(8,128)(2,1)} %bitcast.80), custom_call_target="tpu_custom_call" | custom-call | bytes 11534336 | tf_op jit(solution)/shard_map/fetch/pallas_call | solution.py:234
  9.8 0.0 collective-permute-done
  9.9 0.0 collective-permute-done.1
  9.9 2.3 %collective-permute-done.2 = bf16[64,256]{1,0:T(8,128)(2,1)S(1)} collective-permute-done((bf16[64,256]{1,0:T(8,128)(2,1)}, bf16[64,256]{1,0:T(8,128)(2,1)S(1)}, u32[]{:S(2)}, u32[]{:S(2)}) %collective-permute-start.2) | collective-permute-done | bytes 32800 | tf_op jit(solution)/shard_map/ppermute | solution.py:435
  12.2 0.7 copy-done.11
  12.9 3.7 %all-to-all-start = ((bf16[32,176,256]{2,1,0:T(8,128)(2,1)}), bf16[32,176,256]{2,1,0:T(8,128)(2,1)S(1)}, u32[]{:S(2)}, u32[]{:S(2)}) async-start(bf16[32,176,256]{2,1,0:T(8,128)(2,1)} %release.2), calls=%async_computation | async-start | bytes 5767168 | tf_op jit(solution)/shard_map/all_to_all | solution.py:438
  16.6 0.3 collective-permute-start.3
  17.0 0.9 copy.16.lab_ref
  17.9 0.2 collective-permute-done.3
  18.1 0.7 copy-done.4
  18.8 0.9 copy-done.2
  19.7 0.9 copy-done.5
  20.7 13.6 %forward_sums.1 = (bf16[512,256]{1,0:T(8,128)(2,1)S(1)}, f32[512,256]{1,0:T(8,128)S(1)}, f32[512,256]{1,0:T(8,128)S(1)}, f32[8,512]{1,0:T(8,128)S(1)}, bf16[8192,256]{1,0:T(8,128)(2,1)}) custom-call(s32[1]{0:T(128)S(6)} %mul.18.base_ref, s32[1]{0:T(128)} %bitcast.1.rep_ref, s32[512,1]{1,0:T(8,128)S(1)} %copy-done.2, bf16[8192,256]{1,0:T(8,128)(2,1)} %w_ref.3, ...), custom_call_target="tpu_custom_call" | custom-call | flops 12884901888 | bytes 4194304 | tf_op jit(solution)/shard_map/forward_sums/pallas_call | solution.py:111
  34.2 0.8 copy-done.1
  35.0 0.7 copy-done.8
  35.8 0.6 pad_maximum_fusion.12
  36.4 1.8 %collective-permute-start.4 = (f32[24,128]{1,0:T(8,128)}, f32[24,128]{1,0:T(8,128)S(1)}, u32[]{:S(2)}, u32[]{:S(2)}) collective-permute-start(f32[24,128]{1,0:T(8,128)} %get-tuple-element.50), channel_id=1, source_target_pairs={{0,8},{8,0},{16,24},{24,16},{1,9},{9,1},{17,25},{25,17},{2,10},{10... | collective-permute-start | bytes 36872 | tf_op jit(solution)/shard_map/ppermute | solution.py:435
  38.1 1.5 %collective-permute-start.5 = (f32[24,128]{1,0:T(8,128)S(1)}, f32[24,128]{1,0:T(8,128)S(1)}, u32[]{:S(2)}, u32[]{:S(2)}) collective-permute-start(f32[24,128]{1,0:T(8,128)S(1)} %get-tuple-element.51), channel_id=1, source_target_pairs={{0,16},{8,24},{16,0},{24,8},{1,17},{9,25},{17,1},{25,9},{2,18},{10... | collective-permute-start | bytes 36872 | tf_op jit(solution)/shard_map/ppermute | solution.py:435
  39.6 0.3 collective-permute-start.6
  39.9 0.4 collective-permute-done.4
  40.3 2.0 %collective-permute-done.5 = f32[24,128]{1,0:T(8,128)S(1)} collective-permute-done((f32[24,128]{1,0:T(8,128)S(1)}, f32[24,128]{1,0:T(8,128)S(1)}, u32[]{:S(2)}, u32[]{:S(2)}) %collective-permute-start.5) | collective-permute-done | bytes 12320 | tf_op jit(solution)/shard_map/ppermute | solution.py:435
  42.3 2.1 %collective-permute-done.6 = f32[24,128]{1,0:T(8,128)S(1)} collective-permute-done((f32[24,128]{1,0:T(8,128)S(1)}, f32[24,128]{1,0:T(8,128)S(1)}, u32[]{:S(2)}, u32[]{:S(2)}) %collective-permute-start.6) | collective-permute-done | bytes 12320 | tf_op jit(solution)/shard_map/ppermute | solution.py:435
  44.6 0.1 collective-permute-start.7
  44.7 2.2 %fetch.2.refs_1_.refs_0_ = bf16[32,80,256]{2,1,0:T(8,128)(2,1)} custom-call(bf16[32,256,256]{2,1,0:T(8,128)(2,1)} %bitcast.81, f32[8,512]{1,0:T(8,128)S(1)} %get-tuple-element.11.refs_0_.st_ref), custom_call_target="tpu_custom_call" | custom-call | bytes 5242880 | tf_op jit(solution)/shard_map/fetch/pallas_call | solution.py:234
  46.9 0.0 collective-permute-done.7
  47.1 1.5 %collective-permute-start.8 = (f32[24,128]{1,0:T(8,128)S(1)}, f32[24,128]{1,0:T(8,128)S(1)}, u32[]{:S(2)}, u32[]{:S(2)}) collective-permute-start(f32[24,128]{1,0:T(8,128)S(1)} %get-tuple-element.44), channel_id=1, source_target_pairs={{0,2},{1,3},{2,0},{3,1},{4,6},{5,7},{6,4},{7,5},{8,10},{9,11},{10,... | collective-permute-start | bytes 36872 | tf_op jit(solution)/shard_map/ppermute | solution.py:435
  48.7 2.4 %collective-permute-start.9 = (f32[24,128]{1,0:T(8,128)S(1)}, f32[24,128]{1,0:T(8,128)S(1)}, u32[]{:S(2)}, u32[]{:S(2)}) collective-permute-start(f32[24,128]{1,0:T(8,128)S(1)} %get-tuple-element.45), channel_id=1, source_target_pairs={{0,4},{1,5},{2,6},{3,7},{4,0},{5,1},{6,2},{7,3},{8,12},{9,13},{10,... | collective-permute-start | bytes 36872 | tf_op jit(solution)/shard_map/ppermute | solution.py:435
  51.1 0.5 collective-permute-start.10
  51.6 12.9 %collective-permute-done.8 = f32[24,128]{1,0:T(8,128)S(1)} collective-permute-done((f32[24,128]{1,0:T(8,128)S(1)}, f32[24,128]{1,0:T(8,128)S(1)}, u32[]{:S(2)}, u32[]{:S(2)}) %collective-permute-start.8) | collective-permute-done | bytes 12320 | tf_op jit(solution)/shard_map/ppermute | solution.py:435
  64.5 18.6 %collective-permute-done.9 = f32[24,128]{1,0:T(8,128)S(1)} collective-permute-done((f32[24,128]{1,0:T(8,128)S(1)}, f32[24,128]{1,0:T(8,128)S(1)}, u32[]{:S(2)}, u32[]{:S(2)}) %collective-permute-start.9) | collective-permute-done | bytes 12320 | tf_op jit(solution)/shard_map/ppermute | solution.py:435
  83.1 0.0 collective-permute-done.10
  83.1 0.6 fusion.13
  83.7 0.0 all-to-all-done
  83.7 4.2 %all-to-all-start.1 = ((bf16[32,80,256]{2,1,0:T(8,128)(2,1)}), bf16[32,80,256]{2,1,0:T(8,128)(2,1)}, u32[]{:S(2)}, u32[]{:S(2)}) async-start(bf16[32,80,256]{2,1,0:T(8,128)(2,1)} %release.3), calls=%async_computation.1 | async-start | bytes 2621440 | tf_op jit(solution)/shard_map/all_to_all | solution.py:438
  88.0 1.2 divide_subtract_fusion
  89.2 0.0 copy-start.10
  89.2 0.8 copy-done.10
  90.0 0.7 dynamic-slice_bitcast_fusion
  90.7 0.2 collective-permute-start.11
  91.0 0.1 dynamic_slice.67.refs_5_
  91.0 1.6 %collective-permute-done.11 = f32[4,64,256]{2,1,0:T(8,128)} collective-permute-done((f32[4,64,256]{2,1,0:T(8,128)}, f32[4,64,256]{2,1,0:T(8,128)}, u32[]{:S(2)}, u32[]{:S(2)}) %collective-permute-start.11) | collective-permute-done | bytes 262176 | tf_op jit(solution)/shard_map/ppermute | solution.py:435
  92.6 1.1 fusion.12
  93.7 2.7 %collective-permute-start.14 = (bf16[4,64,256]{2,1,0:T(8,128)(2,1)S(1)}, bf16[4,64,256]{2,1,0:T(8,128)(2,1)S(1)}, u32[]{:S(2)}, u32[]{:S(2)}) collective-permute-start(bf16[4,64,256]{2,1,0:T(8,128)(2,1)S(1)} %get-tuple-element.18), channel_id=1, source_target_pairs={{0,24},{8,16},{16,8},{24,0},{1,25},{9,17},{17,9},{25,1},{2,26},{10... | collective-permute-start | bytes 393224 | tf_op jit(solution)/shard_map/ppermute | solution.py:435
  96.3 0.6 collective-permute-start.13
  96.9 0.3 collective-permute-start.12
  97.2 9.2 %place_rows.1 = (f32[16384,128]{1,0:T(8,128)S(1)}, f32[8,128]{1,0:T(8,128)S(1)}) custom-call(s32[1]{0:T(128)} %bitcast.me_ref, s32[8192]{0:T(1024)S(1)} %bitcast.73, bf16[5632,256]{1,0:T(8,128)(2,1)S(1)} %bitcast.72), custom_call_target="tpu_custom_call" | custom-call | bytes 46137344 | tf_op jit(solution)/shard_map/place_rows/pallas_call | solution.py:329
  106.5 10.9 %weight_gradient.1.refs_4_ = f32[8192,256]{1,0:T(8,128)} custom-call(s32[1]{0:T(128)S(6)} %mul.18.base_ref, bf16[512,256]{1,0:T(8,128)(2,1)S(1)} %copy-done.9, s32[1,512]{1,0:T(1,128)S(1)} %bitcast.79, f32[8,512]{1,0:T(8,128)S(1)} %get-tuple-element.11.refs_0_.st_ref, f32[1,512]{1,0:T(1,128)S(1)} %bitcast.75, bf16[8192,256]{1,0:T(8,128)(2,1)} %w_ref.3, ...), custom_call_target="tpu_custom_call" | custom-call | flops 12884901888 | bytes 12582912 | tf_op jit(solution)/shard_map/weight_gradient/pallas_call | solution.py:179
  117.4 0.0 collective-permute-done.14.refs_3_
  117.4 0.0 collective-permute-done.13.refs_2_
  117.4 0.0 collective-permute-done.12.refs_1_
  117.4 0.1 join.3
  117.6 1.8 %collective-permute-start.15 = (bf16[64,256]{1,0:T(8,128)(2,1)S(1)}, bf16[64,256]{1,0:T(8,128)(2,1)S(1)}, u32[]{:S(2)}, u32[]{:S(2)}) collective-permute-start(bf16[64,256]{1,0:T(8,128)(2,1)S(1)} %get-tuple-element.20), channel_id=1, source_target_pairs={{0,2},{1,3},{2,0},{3,1},{4,6},{5,7},{6,4},{7,5},{8,10},{9,11},{10,... | collective-permute-start | bytes 98312 | tf_op jit(solution)/shard_map/ppermute | solution.py:435
  119.3 2.4 %collective-permute-start.17 = (bf16[64,256]{1,0:T(8,128)(2,1)S(1)}, bf16[64,256]{1,0:T(8,128)(2,1)S(1)}, u32[]{:S(2)}, u32[]{:S(2)}) collective-permute-start(bf16[64,256]{1,0:T(8,128)(2,1)S(1)} %get-tuple-element.21), channel_id=1, source_target_pairs={{0,6},{1,7},{2,4},{3,5},{4,2},{5,3},{6,0},{7,1},{8,14},{9,15},{10,... | collective-permute-start | bytes 98312 | tf_op jit(solution)/shard_map/ppermute | solution.py:435
  121.7 0.1 collective-permute-start.16
  121.7 0.0 all-to-all-done.1
  121.7 10.6 %place_and_blend.1 = bf16[8192,256]{1,0:T(8,128)(2,1)} custom-call(s32[1]{0:T(128)} %bitcast.me_ref, s32[8192]{0:T(1024)S(1)} %bitcast.74, bf16[2560,256]{1,0:T(8,128)(2,1)} %bitcast.43.row_ref, bf16[8192,256]{1,0:T(8,128)(2,1)} %get-tuple-element.16.w_ref, f32[16384,128]{1,0:T(8,128)} %copy-done), custom_call_target="tpu_custom_call" | custom-call | bytes 25165824 | tf_op jit(solution)/shard_map/place_and_blend/pallas_call | solution.py:400
  132.4 0.0 collective-permute-done.15
  132.4 0.0 collective-permute-done.17
  132.4 0.0 collective-permute-done.16
  132.4 0.7 fusion.1
  (47 shorter events, 0.5 us)
Async XLA Ops:
  0.6 9.2 %collective-permute-start.1 = (bf16[64,256]{1,0:T(8,128)(2,1)}, bf16[64,256]{1,0:T(8,128)(2,1)S(1)}, u32[]{:S(2)}, u32[]{:S(2)}) collective-permute-start(bf16[64,256]{1,0:T(8,128)(2,1)} %param.5), channel_id=1, source_target_pairs={{0,4},{1,5},{2,6},{3,7},{4,0},{5,1},{6,2},{7,3},{8,12},{9,13},{10,... | collective-permute-start | bytes 98312 | tf_op jit(solution)/shard_map/ppermute | solution.py:435
  4.7 5.1 %collective-permute-start = (bf16[64,256]{1,0:T(8,128)(2,1)}, bf16[64,256]{1,0:T(8,128)(2,1)S(1)}, u32[]{:S(2)}, u32[]{:S(2)}) collective-permute-start(bf16[64,256]{1,0:T(8,128)(2,1)} %param.5), channel_id=1, source_target_pairs={{0,2},{1,3},{2,0},{3,1},{4,6},{5,7},{6,4},{7,5},{8,10},{9,11},{10,... | collective-permute-start | bytes 98312 | tf_op jit(solution)/shard_map/ppermute | solution.py:435
  6.3 5.9 %collective-permute-start.2 = (bf16[64,256]{1,0:T(8,128)(2,1)}, bf16[64,256]{1,0:T(8,128)(2,1)S(1)}, u32[]{:S(2)}, u32[]{:S(2)}) collective-permute-start(bf16[64,256]{1,0:T(8,128)(2,1)} %param.5), channel_id=1, source_target_pairs={{0,6},{1,7},{2,4},{3,5},{4,2},{5,3},{6,0},{7,1},{8,14},{9,15},{10,... | collective-permute-start | bytes 98312 | tf_op jit(solution)/shard_map/ppermute | solution.py:435
  12.2 0.7 copy-start.11
  12.9 3.7 %copy-start.12 = (bf16[256,256]{1,0:T(8,128)(2,1)S(1)}, bf16[256,256]{1,0:T(8,128)(2,1)}, u32[]{:S(2)}) copy-start(bf16[256,256]{1,0:T(8,128)(2,1)} %copy-done.11) | copy-start | bytes 393220
  12.9 4.1 %copy-start.13 = (s32[8192]{0:T(1024)S(1)}, s32[8192]{0:T(1024)}, u32[]{:S(2)}) copy-start(s32[8192]{0:T(1024)} %param.9) | copy-start | bytes 98308
  12.9 4.1 %copy-start.6 = (s32[512]{0:T(512)S(1)}, s32[512]{0:T(512)}, u32[]{:S(2)}) copy-start(s32[512]{0:T(512)} %param.6) | copy-start | bytes 6148
  12.9 70.8 %all-to-all-start = ((bf16[32,176,256]{2,1,0:T(8,128)(2,1)}), bf16[32,176,256]{2,1,0:T(8,128)(2,1)S(1)}, u32[]{:S(2)}, u32[]{:S(2)}) async-start(bf16[32,176,256]{2,1,0:T(8,128)(2,1)} %release.2), calls=%async_computation | async-start | bytes 5767168 | tf_op jit(solution)/shard_map/all_to_all | solution.py:438
  16.6 1.4 %collective-permute-start.3 = (bf16[256,256]{1,0:T(8,128)(2,1)S(1)}, bf16[256,256]{1,0:T(8,128)(2,1)S(1)}, u32[]{:S(2)}, u32[]{:S(2)}) collective-permute-start(bf16[256,256]{1,0:T(8,128)(2,1)S(1)} %copy-done.12), channel_id=1, source_target_pairs={{0,1},{1,0},{2,3},{3,2},{4,5},{5,4},{6,7},{7,6},{8,9},{9,8},{10,11... | collective-permute-start | bytes 393224 | tf_op jit(solution)/shard_map/ppermute | solution.py:435
  18.1 0.7 copy-start.4
  18.8 0.9 copy-start.2
  19.7 0.9 copy-start.5
  34.2 0.8 copy-start.1
  35.0 0.7 copy-start.8
  36.4 3.9 %collective-permute-start.4 = (f32[24,128]{1,0:T(8,128)}, f32[24,128]{1,0:T(8,128)S(1)}, u32[]{:S(2)}, u32[]{:S(2)}) collective-permute-start(f32[24,128]{1,0:T(8,128)} %get-tuple-element.50), channel_id=1, source_target_pairs={{0,8},{8,0},{16,24},{24,16},{1,9},{9,1},{17,25},{25,17},{2,10},{10... | collective-permute-start | bytes 36872 | tf_op jit(solution)/shard_map/ppermute | solution.py:435
  38.1 4.2 %collective-permute-start.5 = (f32[24,128]{1,0:T(8,128)S(1)}, f32[24,128]{1,0:T(8,128)S(1)}, u32[]{:S(2)}, u32[]{:S(2)}) collective-permute-start(f32[24,128]{1,0:T(8,128)S(1)} %get-tuple-element.51), channel_id=1, source_target_pairs={{0,16},{8,24},{16,0},{24,8},{1,17},{9,25},{17,1},{25,9},{2,18},{10... | collective-permute-start | bytes 36872 | tf_op jit(solution)/shard_map/ppermute | solution.py:435
  39.6 4.8 %collective-permute-start.6 = (f32[24,128]{1,0:T(8,128)S(1)}, f32[24,128]{1,0:T(8,128)S(1)}, u32[]{:S(2)}, u32[]{:S(2)}) collective-permute-start(f32[24,128]{1,0:T(8,128)S(1)} %get-tuple-element.52), channel_id=1, source_target_pairs={{0,24},{8,16},{16,8},{24,0},{1,25},{9,17},{17,9},{25,1},{2,26},{10... | collective-permute-start | bytes 36872 | tf_op jit(solution)/shard_map/ppermute | solution.py:435
  44.6 2.3 %collective-permute-start.7 = (f32[40,128]{1,0:T(8,128)S(1)}, f32[40,128]{1,0:T(8,128)S(1)}, u32[]{:S(2)}, u32[]{:S(2)}) collective-permute-start(f32[40,128]{1,0:T(8,128)S(1)} %get-tuple-element.48), channel_id=1, source_target_pairs={{0,1},{1,0},{2,3},{3,2},{4,5},{5,4},{6,7},{7,6},{8,9},{9,8},{10,11... | collective-permute-start | bytes 61448 | tf_op jit(solution)/shard_map/ppermute | solution.py:435
  47.1 17.4 %collective-permute-start.8 = (f32[24,128]{1,0:T(8,128)S(1)}, f32[24,128]{1,0:T(8,128)S(1)}, u32[]{:S(2)}, u32[]{:S(2)}) collective-permute-start(f32[24,128]{1,0:T(8,128)S(1)} %get-tuple-element.44), channel_id=1, source_target_pairs={{0,2},{1,3},{2,0},{3,1},{4,6},{5,7},{6,4},{7,5},{8,10},{9,11},{10,... | collective-permute-start | bytes 36872 | tf_op jit(solution)/shard_map/ppermute | solution.py:435
  48.7 34.4 %collective-permute-start.9 = (f32[24,128]{1,0:T(8,128)S(1)}, f32[24,128]{1,0:T(8,128)S(1)}, u32[]{:S(2)}, u32[]{:S(2)}) collective-permute-start(f32[24,128]{1,0:T(8,128)S(1)} %get-tuple-element.45), channel_id=1, source_target_pairs={{0,4},{1,5},{2,6},{3,7},{4,0},{5,1},{6,2},{7,3},{8,12},{9,13},{10,... | collective-permute-start | bytes 36872 | tf_op jit(solution)/shard_map/ppermute | solution.py:435
  51.1 32.0 %collective-permute-start.10 = (f32[24,128]{1,0:T(8,128)S(1)}, f32[24,128]{1,0:T(8,128)S(1)}, u32[]{:S(2)}, u32[]{:S(2)}) collective-permute-start(f32[24,128]{1,0:T(8,128)S(1)} %get-tuple-element.46), channel_id=1, source_target_pairs={{0,6},{1,7},{2,4},{3,5},{4,2},{5,3},{6,0},{7,1},{8,14},{9,15},{10,... | collective-permute-start | bytes 36872 | tf_op jit(solution)/shard_map/ppermute | solution.py:435
  83.7 4.3 %copy-start.3 = (f32[512]{0:T(512)S(1)}, f32[512]{0:T(512)}, u32[]{:S(2)}) copy-start(f32[512]{0:T(512)} %get-tuple-element.41.refs_1_) | copy-start | bytes 6148
  83.7 38.0 %all-to-all-start.1 = ((bf16[32,80,256]{2,1,0:T(8,128)(2,1)}), bf16[32,80,256]{2,1,0:T(8,128)(2,1)}, u32[]{:S(2)}, u32[]{:S(2)}) async-start(bf16[32,80,256]{2,1,0:T(8,128)(2,1)} %release.3), calls=%async_computation.1 | async-start | bytes 2621440 | tf_op jit(solution)/shard_map/all_to_all | solution.py:438
  89.2 0.8 copy-start.10
  89.2 17.3 %copy-start.9 = (bf16[512,256]{1,0:T(8,128)(2,1)S(1)}, bf16[512,256]{1,0:T(8,128)(2,1)}, u32[]{:S(2)}) copy-start(bf16[512,256]{1,0:T(8,128)(2,1)} %copy-done.8) | copy-start | bytes 786436
  90.7 1.9 %collective-permute-start.11 = (f32[4,64,256]{2,1,0:T(8,128)}, f32[4,64,256]{2,1,0:T(8,128)}, u32[]{:S(2)}, u32[]{:S(2)}) collective-permute-start(f32[4,64,256]{2,1,0:T(8,128)} %dynamic-slice_bitcast_fusion), channel_id=1, source_target_pairs={{0,1},{1,0},{2,3},{3,2},{4,5},{5,4},{6,7},{7,6},{8,9},{9,8},{10,11... | collective-permute-start | bytes 786440 | tf_op jit(solution)/shard_map/ppermute | solution.py:435
  91.0 26.4 %copy-start.7 = (f32[64]{0:T(128)}, f32[64]{0:T(128)S(1)}, u32[]{:S(2)}) copy-start(f32[64]{0:T(128)S(1)} %dynamic_slice.67.refs_5_) | copy-start | bytes 772
  93.7 23.8 %collective-permute-start.14 = (bf16[4,64,256]{2,1,0:T(8,128)(2,1)S(1)}, bf16[4,64,256]{2,1,0:T(8,128)(2,1)S(1)}, u32[]{:S(2)}, u32[]{:S(2)}) collective-permute-start(bf16[4,64,256]{2,1,0:T(8,128)(2,1)S(1)} %get-tuple-element.18), channel_id=1, source_target_pairs={{0,24},{8,16},{16,8},{24,0},{1,25},{9,17},{17,9},{25,1},{2,26},{10... | collective-permute-start | bytes 393224 | tf_op jit(solution)/shard_map/ppermute | solution.py:435
  96.3 21.1 %collective-permute-start.13 = (bf16[4,64,256]{2,1,0:T(8,128)(2,1)S(1)}, bf16[4,64,256]{2,1,0:T(8,128)(2,1)S(1)}, u32[]{:S(2)}, u32[]{:S(2)}) collective-permute-start(bf16[4,64,256]{2,1,0:T(8,128)(2,1)S(1)} %get-tuple-element.18), channel_id=1, source_target_pairs={{0,16},{8,24},{16,0},{24,8},{1,17},{9,25},{17,1},{25,9},{2,18},{10... | collective-permute-start | bytes 393224 | tf_op jit(solution)/shard_map/ppermute | solution.py:435
  96.9 20.5 %collective-permute-start.12 = (bf16[4,64,256]{2,1,0:T(8,128)(2,1)S(1)}, bf16[4,64,256]{2,1,0:T(8,128)(2,1)S(1)}, u32[]{:S(2)}, u32[]{:S(2)}) collective-permute-start(bf16[4,64,256]{2,1,0:T(8,128)(2,1)S(1)} %get-tuple-element.18), channel_id=1, source_target_pairs={{0,8},{8,0},{16,24},{24,16},{1,9},{9,1},{17,25},{25,17},{2,10},{10... | collective-permute-start | bytes 393224 | tf_op jit(solution)/shard_map/ppermute | solution.py:435
  106.4 11.0 %copy-start = (f32[16384,128]{1,0:T(8,128)}, f32[16384,128]{1,0:T(8,128)S(1)}, u32[]{:S(2)}) copy-start(f32[16384,128]{1,0:T(8,128)S(1)} %get-tuple-element.17.in_ref) | copy-start | bytes 25165828
  117.6 14.8 %collective-permute-start.15 = (bf16[64,256]{1,0:T(8,128)(2,1)S(1)}, bf16[64,256]{1,0:T(8,128)(2,1)S(1)}, u32[]{:S(2)}, u32[]{:S(2)}) collective-permute-start(bf16[64,256]{1,0:T(8,128)(2,1)S(1)} %get-tuple-element.20), channel_id=1, source_target_pairs={{0,2},{1,3},{2,0},{3,1},{4,6},{5,7},{6,4},{7,5},{8,10},{9,11},{10,... | collective-permute-start | bytes 98312 | tf_op jit(solution)/shard_map/ppermute | solution.py:435
  119.3 13.1 %collective-permute-start.17 = (bf16[64,256]{1,0:T(8,128)(2,1)S(1)}, bf16[64,256]{1,0:T(8,128)(2,1)S(1)}, u32[]{:S(2)}, u32[]{:S(2)}) collective-permute-start(bf16[64,256]{1,0:T(8,128)(2,1)S(1)} %get-tuple-element.21), channel_id=1, source_target_pairs={{0,6},{1,7},{2,4},{3,5},{4,2},{5,3},{6,0},{7,1},{8,14},{9,15},{10,... | collective-permute-start | bytes 98312 | tf_op jit(solution)/shard_map/ppermute | solution.py:435
  121.7 10.7 %collective-permute-start.16 = (bf16[64,256]{1,0:T(8,128)(2,1)S(1)}, bf16[64,256]{1,0:T(8,128)(2,1)S(1)}, u32[]{:S(2)}, u32[]{:S(2)}) collective-permute-start(bf16[64,256]{1,0:T(8,128)(2,1)S(1)} %get-tuple-element.22), channel_id=1, source_target_pairs={{0,4},{1,5},{2,6},{3,7},{4,0},{5,1},{6,2},{7,3},{8,12},{9,13},{10,... | collective-permute-start | bytes 98312 | tf_op jit(solution)/shard_map/ppermute | solution.py:435

commit v20 on v19

--- a/solution.py
+++ b/solution.py
@@ -289,7 +289,7 @@
 def place_runs(me_ref, slot_ref, row_ref, held_ref, stage_ref, copies, peers, run, first):
     size = row_ref.shape[0] // peers
     batch = max(n for n in range(1, 49) if size % n == 0)
-    chunk = max(n for n in range(16, 49, 16) if size % n == 0)
+    chunk = max(n for n in range(16, 193, 16) if size % n == 0)
 
     def prepare(source, carry):
         for block in range(0, size, chunk):

time: 134 us -> 134 us (level)
  no operation moved by 1% of the time
where the time goes in v20:
time: 134 us; the launch traced here: 133 us
  Pallas kernels  49.3 us (37%)
  waiting for transfers between devices  40.2 us (30%)
  starting transfers between devices  29.9 us (22%)
  local copies, waits for them, and re-layouts  8.3 us (6%)
  other arithmetic  4.32 us (3%)
    ppermute x18, waiting for transfers between devices, swap(): lax.ppermute(value, axis, [(i, i ^ k) for i in range(size)])  40.2 us
    ppermute x18, starting transfers between devices, swap(): lax.ppermute(value, axis, [(i, i ^ k) for i in range(size)])  21.9 us
    pallas_call x1, Pallas kernels, forward(): pl.pallas_call(functools.partial(forward_kernel, classes=classes, reps=re...  13.6 us
    pallas_call x1, Pallas kernels, weight_gradient(): pl.pallas_call(weight_kernel, grid=(classes // tile,), in_specs=[pl.Block...  10.9 us
    pallas_call x1, Pallas kernels, place_and_blend(): pl.pallas_call(functools.partial(blend_kernel, peers=peers, run=run, firs...  10.6 us
    pallas_call x1, Pallas kernels, place_rows(): pl.pallas_call(functools.partial(place_kernel, peers=peers, run=run, firs...  9.2 us
    all_to_all x2, starting transfers between devices, relay(): return lax.all_to_all(sent, ALL, 0, 0, tiled=True).reshape(-1, width)  7.96 us
    unnamed x34, local copies, waits for them, and re-layouts  6.41 us
  transfers between devices with their start and end apart: 20, of which 8 were waited for; matrix products, arithmetic and copies ran while one was open for 5% of the time, Pallas kernels for 37%

profile of v20, /device:TPU:0, one launch (start us, length us, event | category | flops | bytes accessed | tf_op | source)
XLA Modules:
  0.0 133.0 jit_solution(9727849010748547136)
XLA Ops:
  0.6 4.1 %collective-permute-start.1 = (bf16[64,256]{1,0:T(8,128)(2,1)}, bf16[64,256]{1,0:T(8,128)(2,1)S(1)}, u32[]{:S(2)}, u32[]{:S(2)}) collective-permute-start(bf16[64,256]{1,0:T(8,128)(2,1)} %param.5), channel_id=1, source_target_pairs={{0,4},{1,5},{2,6},{3,7},{4,0},{5,1},{6,2},{7,3},{8,12},{9,13},{10,... | collective-permute-start | bytes 98312 | tf_op jit(solution)/shard_map/ppermute | solution.py:435
  4.7 1.6 %collective-permute-start = (bf16[64,256]{1,0:T(8,128)(2,1)}, bf16[64,256]{1,0:T(8,128)(2,1)S(1)}, u32[]{:S(2)}, u32[]{:S(2)}) collective-permute-start(bf16[64,256]{1,0:T(8,128)(2,1)} %param.5), channel_id=1, source_target_pairs={{0,2},{1,3},{2,0},{3,1},{4,6},{5,7},{6,4},{7,5},{8,10},{9,11},{10,... | collective-permute-start | bytes 98312 | tf_op jit(solution)/shard_map/ppermute | solution.py:435
  6.3 0.0 collective-permute-start.2
  6.3 0.8 constant_dynamic-update-slice_fusion.3
  7.1 2.7 %fetch.3.refs_0_ = bf16[32,176,256]{2,1,0:T(8,128)(2,1)} custom-call(bf16[32,256,256]{2,1,0:T(8,128)(2,1)} %bitcast.80), custom_call_target="tpu_custom_call" | custom-call | bytes 11534336 | tf_op jit(solution)/shard_map/fetch/pallas_call | solution.py:234
  9.8 0.0 collective-permute-done
  9.9 0.0 collective-permute-done.1
  9.9 2.3 %collective-permute-done.2 = bf16[64,256]{1,0:T(8,128)(2,1)S(1)} collective-permute-done((bf16[64,256]{1,0:T(8,128)(2,1)}, bf16[64,256]{1,0:T(8,128)(2,1)S(1)}, u32[]{:S(2)}, u32[]{:S(2)}) %collective-permute-start.2) | collective-permute-done | bytes 32800 | tf_op jit(solution)/shard_map/ppermute | solution.py:435
  12.2 0.7 copy-done.11
  12.9 3.7 %all-to-all-start = ((bf16[32,176,256]{2,1,0:T(8,128)(2,1)}), bf16[32,176,256]{2,1,0:T(8,128)(2,1)S(1)}, u32[]{:S(2)}, u32[]{:S(2)}) async-start(bf16[32,176,256]{2,1,0:T(8,128)(2,1)} %release.2), calls=%async_computation | async-start | bytes 5767168 | tf_op jit(solution)/shard_map/all_to_all | solution.py:438
  16.6 0.3 collective-permute-start.3
  17.0 0.9 copy.16.lab_ref
  17.9 0.2 collective-permute-done.3
  18.1 0.7 copy-done.4
  18.8 0.9 copy-done.2
  19.7 0.9 copy-done.5
  20.7 13.6 %forward_sums.1 = (bf16[512,256]{1,0:T(8,128)(2,1)S(1)}, f32[512,256]{1,0:T(8,128)S(1)}, f32[512,256]{1,0:T(8,128)S(1)}, f32[8,512]{1,0:T(8,128)S(1)}, bf16[8192,256]{1,0:T(8,128)(2,1)}) custom-call(s32[1]{0:T(128)S(6)} %mul.18.base_ref, s32[1]{0:T(128)} %bitcast.1.rep_ref, s32[512,1]{1,0:T(8,128)S(1)} %copy-done.2, bf16[8192,256]{1,0:T(8,128)(2,1)} %w_ref.3, ...), custom_call_target="tpu_custom_call" | custom-call | flops 12884901888 | bytes 4194304 | tf_op jit(solution)/shard_map/forward_sums/pallas_call | solution.py:111
  34.2 0.8 copy-done.1
  35.0 0.7 copy-done.8
  35.8 0.6 pad_maximum_fusion.12
  36.4 1.8 %collective-permute-start.4 = (f32[24,128]{1,0:T(8,128)}, f32[24,128]{1,0:T(8,128)S(1)}, u32[]{:S(2)}, u32[]{:S(2)}) collective-permute-start(f32[24,128]{1,0:T(8,128)} %get-tuple-element.50), channel_id=1, source_target_pairs={{0,8},{8,0},{16,24},{24,16},{1,9},{9,1},{17,25},{25,17},{2,10},{10... | collective-permute-start | bytes 36872 | tf_op jit(solution)/shard_map/ppermute | solution.py:435
  38.1 1.5 %collective-permute-start.5 = (f32[24,128]{1,0:T(8,128)S(1)}, f32[24,128]{1,0:T(8,128)S(1)}, u32[]{:S(2)}, u32[]{:S(2)}) collective-permute-start(f32[24,128]{1,0:T(8,128)S(1)} %get-tuple-element.51), channel_id=1, source_target_pairs={{0,16},{8,24},{16,0},{24,8},{1,17},{9,25},{17,1},{25,9},{2,18},{10... | collective-permute-start | bytes 36872 | tf_op jit(solution)/shard_map/ppermute | solution.py:435
  39.6 0.3 collective-permute-start.6
  39.9 0.4 collective-permute-done.4
  40.3 2.0 %collective-permute-done.5 = f32[24,128]{1,0:T(8,128)S(1)} collective-permute-done((f32[24,128]{1,0:T(8,128)S(1)}, f32[24,128]{1,0:T(8,128)S(1)}, u32[]{:S(2)}, u32[]{:S(2)}) %collective-permute-start.5) | collective-permute-done | bytes 12320 | tf_op jit(solution)/shard_map/ppermute | solution.py:435
  42.3 2.1 %collective-permute-done.6 = f32[24,128]{1,0:T(8,128)S(1)} collective-permute-done((f32[24,128]{1,0:T(8,128)S(1)}, f32[24,128]{1,0:T(8,128)S(1)}, u32[]{:S(2)}, u32[]{:S(2)}) %collective-permute-start.6) | collective-permute-done | bytes 12320 | tf_op jit(solution)/shard_map/ppermute | solution.py:435
  44.6 0.1 collective-permute-start.7
  44.7 2.2 %fetch.2.refs_1_.refs_0_ = bf16[32,80,256]{2,1,0:T(8,128)(2,1)} custom-call(bf16[32,256,256]{2,1,0:T(8,128)(2,1)} %bitcast.81, f32[8,512]{1,0:T(8,128)S(1)} %get-tuple-element.11.refs_0_.st_ref), custom_call_target="tpu_custom_call" | custom-call | bytes 5242880 | tf_op jit(solution)/shard_map/fetch/pallas_call | solution.py:234
  46.9 0.0 collective-permute-done.7
  47.1 1.5 %collective-permute-start.8 = (f32[24,128]{1,0:T(8,128)S(1)}, f32[24,128]{1,0:T(8,128)S(1)}, u32[]{:S(2)}, u32[]{:S(2)}) collective-permute-start(f32[24,128]{1,0:T(8,128)S(1)} %get-tuple-element.44), channel_id=1, source_target_pairs={{0,2},{1,3},{2,0},{3,1},{4,6},{5,7},{6,4},{7,5},{8,10},{9,11},{10,... | collective-permute-start | bytes 36872 | tf_op jit(solution)/shard_map/ppermute | solution.py:435
  48.7 2.4 %collective-permute-start.9 = (f32[24,128]{1,0:T(8,128)S(1)}, f32[24,128]{1,0:T(8,128)S(1)}, u32[]{:S(2)}, u32[]{:S(2)}) collective-permute-start(f32[24,128]{1,0:T(8,128)S(1)} %get-tuple-element.45), channel_id=1, source_target_pairs={{0,4},{1,5},{2,6},{3,7},{4,0},{5,1},{6,2},{7,3},{8,12},{9,13},{10,... | collective-permute-start | bytes 36872 | tf_op jit(solution)/shard_map/ppermute | solution.py:435
  51.1 0.5 collective-permute-start.10
  51.6 12.9 %collective-permute-done.8 = f32[24,128]{1,0:T(8,128)S(1)} collective-permute-done((f32[24,128]{1,0:T(8,128)S(1)}, f32[24,128]{1,0:T(8,128)S(1)}, u32[]{:S(2)}, u32[]{:S(2)}) %collective-permute-start.8) | collective-permute-done | bytes 12320 | tf_op jit(solution)/shard_map/ppermute | solution.py:435
  64.5 18.6 %collective-permute-done.9 = f32[24,128]{1,0:T(8,128)S(1)} collective-permute-done((f32[24,128]{1,0:T(8,128)S(1)}, f32[24,128]{1,0:T(8,128)S(1)}, u32[]{:S(2)}, u32[]{:S(2)}) %collective-permute-start.9) | collective-permute-done | bytes 12320 | tf_op jit(solution)/shard_map/ppermute | solution.py:435
  83.1 0.0 collective-permute-done.10
  83.1 0.6 fusion.13
  83.7 0.0 all-to-all-done
  83.7 4.2 %all-to-all-start.1 = ((bf16[32,80,256]{2,1,0:T(8,128)(2,1)}), bf16[32,80,256]{2,1,0:T(8,128)(2,1)}, u32[]{:S(2)}, u32[]{:S(2)}) async-start(bf16[32,80,256]{2,1,0:T(8,128)(2,1)} %release.3), calls=%async_computation.1 | async-start | bytes 2621440 | tf_op jit(solution)/shard_map/all_to_all | solution.py:438
  88.0 1.2 divide_subtract_fusion
  89.2 0.0 copy-start.10
  89.2 0.8 copy-done.10
  90.0 0.7 dynamic-slice_bitcast_fusion
  90.7 0.2 collective-permute-start.11
  91.0 0.1 dynamic_slice.67.refs_5_
  91.0 1.6 %collective-permute-done.11 = f32[4,64,256]{2,1,0:T(8,128)} collective-permute-done((f32[4,64,256]{2,1,0:T(8,128)}, f32[4,64,256]{2,1,0:T(8,128)}, u32[]{:S(2)}, u32[]{:S(2)}) %collective-permute-start.11) | collective-permute-done | bytes 262176 | tf_op jit(solution)/shard_map/ppermute | solution.py:435
  92.6 1.1 fusion.12
  93.7 2.7 %collective-permute-start.14 = (bf16[4,64,256]{2,1,0:T(8,128)(2,1)S(1)}, bf16[4,64,256]{2,1,0:T(8,128)(2,1)S(1)}, u32[]{:S(2)}, u32[]{:S(2)}) collective-permute-start(bf16[4,64,256]{2,1,0:T(8,128)(2,1)S(1)} %get-tuple-element.18), channel_id=1, source_target_pairs={{0,24},{8,16},{16,8},{24,0},{1,25},{9,17},{17,9},{25,1},{2,26},{10... | collective-permute-start | bytes 393224 | tf_op jit(solution)/shard_map/ppermute | solution.py:435
  96.3 0.6 collective-permute-start.13
  96.9 0.3 collective-permute-start.12
  97.2 9.2 %place_rows.1 = (f32[16384,128]{1,0:T(8,128)S(1)}, f32[8,128]{1,0:T(8,128)S(1)}) custom-call(s32[1]{0:T(128)} %bitcast.me_ref, s32[8192]{0:T(1024)S(1)} %bitcast.73, bf16[5632,256]{1,0:T(8,128)(2,1)S(1)} %bitcast.72), custom_call_target="tpu_custom_call" | custom-call | bytes 46137344 | tf_op jit(solution)/shard_map/place_rows/pallas_call | solution.py:329
  106.4 10.9 %weight_gradient.1.refs_4_ = f32[8192,256]{1,0:T(8,128)} custom-call(s32[1]{0:T(128)S(6)} %mul.18.base_ref, bf16[512,256]{1,0:T(8,128)(2,1)S(1)} %copy-done.9, s32[1,512]{1,0:T(1,128)S(1)} %bitcast.79, f32[8,512]{1,0:T(8,128)S(1)} %get-tuple-element.11.refs_0_.st_ref, f32[1,512]{1,0:T(1,128)S(1)} %bitcast.75, bf16[8192,256]{1,0:T(8,128)(2,1)} %w_ref.3, ...), custom_call_target="tpu_custom_call" | custom-call | flops 12884901888 | bytes 12582912 | tf_op jit(solution)/shard_map/weight_gradient/pallas_call | solution.py:179
  117.4 0.0 collective-permute-done.14.refs_3_
  117.4 0.0 collective-permute-done.13.refs_2_
  117.4 0.0 collective-permute-done.12.refs_1_
  117.4 0.1 join.3
  117.5 1.8 %collective-permute-start.15 = (bf16[64,256]{1,0:T(8,128)(2,1)S(1)}, bf16[64,256]{1,0:T(8,128)(2,1)S(1)}, u32[]{:S(2)}, u32[]{:S(2)}) collective-permute-start(bf16[64,256]{1,0:T(8,128)(2,1)S(1)} %get-tuple-element.20), channel_id=1, source_target_pairs={{0,2},{1,3},{2,0},{3,1},{4,6},{5,7},{6,4},{7,5},{8,10},{9,11},{10,... | collective-permute-start | bytes 98312 | tf_op jit(solution)/shard_map/ppermute | solution.py:435
  119.3 2.4 %collective-permute-start.17 = (bf16[64,256]{1,0:T(8,128)(2,1)S(1)}, bf16[64,256]{1,0:T(8,128)(2,1)S(1)}, u32[]{:S(2)}, u32[]{:S(2)}) collective-permute-start(bf16[64,256]{1,0:T(8,128)(2,1)S(1)} %get-tuple-element.21), channel_id=1, source_target_pairs={{0,6},{1,7},{2,4},{3,5},{4,2},{5,3},{6,0},{7,1},{8,14},{9,15},{10,... | collective-permute-start | bytes 98312 | tf_op jit(solution)/shard_map/ppermute | solution.py:435
  121.7 0.0 collective-permute-start.16
  121.7 0.0 all-to-all-done.1
  121.7 10.6 %place_and_blend.1 = bf16[8192,256]{1,0:T(8,128)(2,1)} custom-call(s32[1]{0:T(128)} %bitcast.me_ref, s32[8192]{0:T(1024)S(1)} %bitcast.74, bf16[2560,256]{1,0:T(8,128)(2,1)} %bitcast.43.row_ref, bf16[8192,256]{1,0:T(8,128)(2,1)} %get-tuple-element.16.w_ref, f32[16384,128]{1,0:T(8,128)} %copy-done), custom_call_target="tpu_custom_call" | custom-call | bytes 25165824 | tf_op jit(solution)/shard_map/place_and_blend/pallas_call | solution.py:400
  132.3 0.0 collective-permute-done.15
  132.4 0.0 collective-permute-done.17
  132.4 0.0 collective-permute-done.16
  132.4 0.7 fusion.1
  (47 shorter events, 0.5 us)
Async XLA Ops:
  0.6 9.2 %collective-permute-start.1 = (bf16[64,256]{1,0:T(8,128)(2,1)}, bf16[64,256]{1,0:T(8,128)(2,1)S(1)}, u32[]{:S(2)}, u32[]{:S(2)}) collective-permute-start(bf16[64,256]{1,0:T(8,128)(2,1)} %param.5), channel_id=1, source_target_pairs={{0,4},{1,5},{2,6},{3,7},{4,0},{5,1},{6,2},{7,3},{8,12},{9,13},{10,... | collective-permute-start | bytes 98312 | tf_op jit(solution)/shard_map/ppermute | solution.py:435
  4.7 5.1 %collective-permute-start = (bf16[64,256]{1,0:T(8,128)(2,1)}, bf16[64,256]{1,0:T(8,128)(2,1)S(1)}, u32[]{:S(2)}, u32[]{:S(2)}) collective-permute-start(bf16[64,256]{1,0:T(8,128)(2,1)} %param.5), channel_id=1, source_target_pairs={{0,2},{1,3},{2,0},{3,1},{4,6},{5,7},{6,4},{7,5},{8,10},{9,11},{10,... | collective-permute-start | bytes 98312 | tf_op jit(solution)/shard_map/ppermute | solution.py:435
  6.3 5.9 %collective-permute-start.2 = (bf16[64,256]{1,0:T(8,128)(2,1)}, bf16[64,256]{1,0:T(8,128)(2,1)S(1)}, u32[]{:S(2)}, u32[]{:S(2)}) collective-permute-start(bf16[64,256]{1,0:T(8,128)(2,1)} %param.5), channel_id=1, source_target_pairs={{0,6},{1,7},{2,4},{3,5},{4,2},{5,3},{6,0},{7,1},{8,14},{9,15},{10,... | collective-permute-start | bytes 98312 | tf_op jit(solution)/shard_map/ppermute | solution.py:435
  12.2 0.7 copy-start.11
  12.9 3.7 %copy-start.12 = (bf16[256,256]{1,0:T(8,128)(2,1)S(1)}, bf16[256,256]{1,0:T(8,128)(2,1)}, u32[]{:S(2)}) copy-start(bf16[256,256]{1,0:T(8,128)(2,1)} %copy-done.11) | copy-start | bytes 393220
  12.9 4.1 %copy-start.13 = (s32[8192]{0:T(1024)S(1)}, s32[8192]{0:T(1024)}, u32[]{:S(2)}) copy-start(s32[8192]{0:T(1024)} %param.9) | copy-start | bytes 98308
  12.9 4.1 %copy-start.6 = (s32[512]{0:T(512)S(1)}, s32[512]{0:T(512)}, u32[]{:S(2)}) copy-start(s32[512]{0:T(512)} %param.6) | copy-start | bytes 6148
  12.9 70.8 %all-to-all-start = ((bf16[32,176,256]{2,1,0:T(8,128)(2,1)}), bf16[32,176,256]{2,1,0:T(8,128)(2,1)S(1)}, u32[]{:S(2)}, u32[]{:S(2)}) async-start(bf16[32,176,256]{2,1,0:T(8,128)(2,1)} %release.2), calls=%async_computation | async-start | bytes 5767168 | tf_op jit(solution)/shard_map/all_to_all | solution.py:438
  16.6 1.4 %collective-permute-start.3 = (bf16[256,256]{1,0:T(8,128)(2,1)S(1)}, bf16[256,256]{1,0:T(8,128)(2,1)S(1)}, u32[]{:S(2)}, u32[]{:S(2)}) collective-permute-start(bf16[256,256]{1,0:T(8,128)(2,1)S(1)} %copy-done.12), channel_id=1, source_target_pairs={{0,1},{1,0},{2,3},{3,2},{4,5},{5,4},{6,7},{7,6},{8,9},{9,8},{10,11... | collective-permute-start | bytes 393224 | tf_op jit(solution)/shard_map/ppermute | solution.py:435
  18.1 0.7 copy-start.4
  18.8 0.9 copy-start.2
  19.7 0.9 copy-start.5
  34.2 0.8 copy-start.1
  35.0 0.7 copy-start.8
  36.4 3.9 %collective-permute-start.4 = (f32[24,128]{1,0:T(8,128)}, f32[24,128]{1,0:T(8,128)S(1)}, u32[]{:S(2)}, u32[]{:S(2)}) collective-permute-start(f32[24,128]{1,0:T(8,128)} %get-tuple-element.50), channel_id=1, source_target_pairs={{0,8},{8,0},{16,24},{24,16},{1,9},{9,1},{17,25},{25,17},{2,10},{10... | collective-permute-start | bytes 36872 | tf_op jit(solution)/shard_map/ppermute | solution.py:435
  38.1 4.2 %collective-permute-start.5 = (f32[24,128]{1,0:T(8,128)S(1)}, f32[24,128]{1,0:T(8,128)S(1)}, u32[]{:S(2)}, u32[]{:S(2)}) collective-permute-start(f32[24,128]{1,0:T(8,128)S(1)} %get-tuple-element.51), channel_id=1, source_target_pairs={{0,16},{8,24},{16,0},{24,8},{1,17},{9,25},{17,1},{25,9},{2,18},{10... | collective-permute-start | bytes 36872 | tf_op jit(solution)/shard_map/ppermute | solution.py:435
  39.6 4.8 %collective-permute-start.6 = (f32[24,128]{1,0:T(8,128)S(1)}, f32[24,128]{1,0:T(8,128)S(1)}, u32[]{:S(2)}, u32[]{:S(2)}) collective-permute-start(f32[24,128]{1,0:T(8,128)S(1)} %get-tuple-element.52), channel_id=1, source_target_pairs={{0,24},{8,16},{16,8},{24,0},{1,25},{9,17},{17,9},{25,1},{2,26},{10... | collective-permute-start | bytes 36872 | tf_op jit(solution)/shard_map/ppermute | solution.py:435
  44.6 2.3 %collective-permute-start.7 = (f32[40,128]{1,0:T(8,128)S(1)}, f32[40,128]{1,0:T(8,128)S(1)}, u32[]{:S(2)}, u32[]{:S(2)}) collective-permute-start(f32[40,128]{1,0:T(8,128)S(1)} %get-tuple-element.48), channel_id=1, source_target_pairs={{0,1},{1,0},{2,3},{3,2},{4,5},{5,4},{6,7},{7,6},{8,9},{9,8},{10,11... | collective-permute-start | bytes 61448 | tf_op jit(solution)/shard_map/ppermute | solution.py:435
  47.1 17.4 %collective-permute-start.8 = (f32[24,128]{1,0:T(8,128)S(1)}, f32[24,128]{1,0:T(8,128)S(1)}, u32[]{:S(2)}, u32[]{:S(2)}) collective-permute-start(f32[24,128]{1,0:T(8,128)S(1)} %get-tuple-element.44), channel_id=1, source_target_pairs={{0,2},{1,3},{2,0},{3,1},{4,6},{5,7},{6,4},{7,5},{8,10},{9,11},{10,... | collective-permute-start | bytes 36872 | tf_op jit(solution)/shard_map/ppermute | solution.py:435
  48.7 34.4 %collective-permute-start.9 = (f32[24,128]{1,0:T(8,128)S(1)}, f32[24,128]{1,0:T(8,128)S(1)}, u32[]{:S(2)}, u32[]{:S(2)}) collective-permute-start(f32[24,128]{1,0:T(8,128)S(1)} %get-tuple-element.45), channel_id=1, source_target_pairs={{0,4},{1,5},{2,6},{3,7},{4,0},{5,1},{6,2},{7,3},{8,12},{9,13},{10,... | collective-permute-start | bytes 36872 | tf_op jit(solution)/shard_map/ppermute | solution.py:435
  51.1 32.0 %collective-permute-start.10 = (f32[24,128]{1,0:T(8,128)S(1)}, f32[24,128]{1,0:T(8,128)S(1)}, u32[]{:S(2)}, u32[]{:S(2)}) collective-permute-start(f32[24,128]{1,0:T(8,128)S(1)} %get-tuple-element.46), channel_id=1, source_target_pairs={{0,6},{1,7},{2,4},{3,5},{4,2},{5,3},{6,0},{7,1},{8,14},{9,15},{10,... | collective-permute-start | bytes 36872 | tf_op jit(solution)/shard_map/ppermute | solution.py:435
  83.7 4.3 %copy-start.3 = (f32[512]{0:T(512)S(1)}, f32[512]{0:T(512)}, u32[]{:S(2)}) copy-start(f32[512]{0:T(512)} %get-tuple-element.41.refs_1_) | copy-start | bytes 6148
  83.7 38.0 %all-to-all-start.1 = ((bf16[32,80,256]{2,1,0:T(8,128)(2,1)}), bf16[32,80,256]{2,1,0:T(8,128)(2,1)}, u32[]{:S(2)}, u32[]{:S(2)}) async-start(bf16[32,80,256]{2,1,0:T(8,128)(2,1)} %release.3), calls=%async_computation.1 | async-start | bytes 2621440 | tf_op jit(solution)/shard_map/all_to_all | solution.py:438
  89.2 0.8 copy-start.10
  89.2 17.2 %copy-start.9 = (bf16[512,256]{1,0:T(8,128)(2,1)S(1)}, bf16[512,256]{1,0:T(8,128)(2,1)}, u32[]{:S(2)}) copy-start(bf16[512,256]{1,0:T(8,128)(2,1)} %copy-done.8) | copy-start | bytes 786436
  90.7 1.9 %collective-permute-start.11 = (f32[4,64,256]{2,1,0:T(8,128)}, f32[4,64,256]{2,1,0:T(8,128)}, u32[]{:S(2)}, u32[]{:S(2)}) collective-permute-start(f32[4,64,256]{2,1,0:T(8,128)} %dynamic-slice_bitcast_fusion), channel_id=1, source_target_pairs={{0,1},{1,0},{2,3},{3,2},{4,5},{5,4},{6,7},{7,6},{8,9},{9,8},{10,11... | collective-permute-start | bytes 786440 | tf_op jit(solution)/shard_map/ppermute | solution.py:435
  91.0 26.4 %copy-start.7 = (f32[64]{0:T(128)}, f32[64]{0:T(128)S(1)}, u32[]{:S(2)}) copy-start(f32[64]{0:T(128)S(1)} %dynamic_slice.67.refs_5_) | copy-start | bytes 772
  93.7 23.7 %collective-permute-start.14 = (bf16[4,64,256]{2,1,0:T(8,128)(2,1)S(1)}, bf16[4,64,256]{2,1,0:T(8,128)(2,1)S(1)}, u32[]{:S(2)}, u32[]{:S(2)}) collective-permute-start(bf16[4,64,256]{2,1,0:T(8,128)(2,1)S(1)} %get-tuple-element.18), channel_id=1, source_target_pairs={{0,24},{8,16},{16,8},{24,0},{1,25},{9,17},{17,9},{25,1},{2,26},{10... | collective-permute-start | bytes 393224 | tf_op jit(solution)/shard_map/ppermute | solution.py:435
  96.3 21.1 %collective-permute-start.13 = (bf16[4,64,256]{2,1,0:T(8,128)(2,1)S(1)}, bf16[4,64,256]{2,1,0:T(8,128)(2,1)S(1)}, u32[]{:S(2)}, u32[]{:S(2)}) collective-permute-start(bf16[4,64,256]{2,1,0:T(8,128)(2,1)S(1)} %get-tuple-element.18), channel_id=1, source_target_pairs={{0,16},{8,24},{16,0},{24,8},{1,17},{9,25},{17,1},{25,9},{2,18},{10... | collective-permute-start | bytes 393224 | tf_op jit(solution)/shard_map/ppermute | solution.py:435
  96.9 20.5 %collective-permute-start.12 = (bf16[4,64,256]{2,1,0:T(8,128)(2,1)S(1)}, bf16[4,64,256]{2,1,0:T(8,128)(2,1)S(1)}, u32[]{:S(2)}, u32[]{:S(2)}) collective-permute-start(bf16[4,64,256]{2,1,0:T(8,128)(2,1)S(1)} %get-tuple-element.18), channel_id=1, source_target_pairs={{0,8},{8,0},{16,24},{24,16},{1,9},{9,1},{17,25},{25,17},{2,10},{10... | collective-permute-start | bytes 393224 | tf_op jit(solution)/shard_map/ppermute | solution.py:435
  106.4 11.0 %copy-start = (f32[16384,128]{1,0:T(8,128)}, f32[16384,128]{1,0:T(8,128)S(1)}, u32[]{:S(2)}) copy-start(f32[16384,128]{1,0:T(8,128)S(1)} %get-tuple-element.17.in_ref) | copy-start | bytes 25165828
  117.5 14.8 %collective-permute-start.15 = (bf16[64,256]{1,0:T(8,128)(2,1)S(1)}, bf16[64,256]{1,0:T(8,128)(2,1)S(1)}, u32[]{:S(2)}, u32[]{:S(2)}) collective-permute-start(bf16[64,256]{1,0:T(8,128)(2,1)S(1)} %get-tuple-element.20), channel_id=1, source_target_pairs={{0,2},{1,3},{2,0},{3,1},{4,6},{5,7},{6,4},{7,5},{8,10},{9,11},{10,... | collective-permute-start | bytes 98312 | tf_op jit(solution)/shard_map/ppermute | solution.py:435
  119.3 13.1 %collective-permute-start.17 = (bf16[64,256]{1,0:T(8,128)(2,1)S(1)}, bf16[64,256]{1,0:T(8,128)(2,1)S(1)}, u32[]{:S(2)}, u32[]{:S(2)}) collective-permute-start(bf16[64,256]{1,0:T(8,128)(2,1)S(1)} %get-tuple-element.21), channel_id=1, source_target_pairs={{0,6},{1,7},{2,4},{3,5},{4,2},{5,3},{6,0},{7,1},{8,14},{9,15},{10,... | collective-permute-start | bytes 98312 | tf_op jit(solution)/shard_map/ppermute | solution.py:435
  121.7 10.7 %collective-permute-start.16 = (bf16[64,256]{1,0:T(8,128)(2,1)S(1)}, bf16[64,256]{1,0:T(8,128)(2,1)S(1)}, u32[]{:S(2)}, u32[]{:S(2)}) collective-permute-start(bf16[64,256]{1,0:T(8,128)(2,1)S(1)} %get-tuple-element.22), channel_id=1, source_target_pairs={{0,4},{1,5},{2,6},{3,7},{4,0},{5,1},{6,2},{7,3},{8,12},{9,13},{10,... | collective-permute-start | bytes 98312 | tf_op jit(solution)/shard_map/ppermute | solution.py:435
